TPU v7x, 32 devices: a whole 2x2x4 slice. The times are simulated.
32 devices in a mesh: rows: 8 (over z, y), cols: 4 (over x, core).
Axes of the slice: x: 2, y: 2, z: 4, core: 2. Of those that a mesh axis runs over, the one named last changes fastest.
Arguments:
- kernel: bfloat16 [128, 64, 128, 128], P('rows', 'cols'), may hold values from -0.0625 to 0.0625
- pattern: int32 [128, 64], P('rows', 'cols'), may hold values from 0 to 23, as said below
- counts: int32 [128, 4], P('rows', 'cols'), may hold values from 1 to 16, as said below
- delays: float32 [16384, 128], P('rows'), may hold values from -6 to 6
Outputs:
- model: float32 [12288, 128], P('cols')
- gradient: float32 [12288, 128], P('cols')
- misfit: float32 [128], replicated
Inputs may be any that keep to these rules, and one draw needn't show every extreme that they name: `pattern`: within one row block and one column shard the 16 slots name different column blocks; slots at or beyond the count hold valid indices that take no part. `counts`: some row block uses all 16 slots of some column shard.
All inputs are finite; a program needn't handle non-finite values.
Results may differ from a plain program's by a relative error of at most 0.0087.
Values sent between devices are 32-bit elements; how exact they have to be, the bound alone decides.
No kernel may reach another device: no remote copies, remote signals or barrier semaphores. Data moves between devices by JAX's collectives and lax.ppermute only.
A program may use at most 128 MiB of HBM per device.

v0:
```python
import jax
import jax.numpy as jnp
from jax import lax
from jax.sharding import PartitionSpec as P

CB_DEV = 24
ITERS = 2


tiny_eps = 1e-06


def column_norm(values):
    return jnp.sum(values * values, axis=0)


def build_dense(kernel, pattern, counts):
    row_blocks = kernel.shape[0]
    slot_count = kernel.shape[1]
    alive_bool = jnp.arange(slot_count)[None, :] < counts
    selector = (
        (pattern[:, :, None] == jnp.arange(CB_DEV)[None, None, :]) & alive_bool[:, :, None]
    ).astype(jnp.bfloat16)
    placed = jnp.einsum("bkc,bkij->bicj", selector, kernel, preferred_element_type=jnp.float32)
    return placed.astype(jnp.bfloat16).reshape(row_blocks * 128, CB_DEV * 128)


def local_forward(dense_kernel, vec_bf):
    return jnp.dot(dense_kernel, vec_bf, preferred_element_type=jnp.float32)


def local_backward(dense_kernel, vec_bf):
    return lax.dot_general(
        dense_kernel, vec_bf, (((0,), (0,)), ((), ())), preferred_element_type=jnp.float32
    )


def on_device(kernel, pattern, counts, delays):
    width = delays.shape[1]
    dense_kernel = build_dense(kernel, pattern, counts)

    def back_step(left_raw, right_prev):
        left_bf = left_raw.astype(jnp.bfloat16)
        squares = lax.psum(column_norm(left_raw), "rows")
        beta_norm = jnp.sqrt(squares + tiny_eps)
        partial_sum = local_backward(dense_kernel, left_bf)
        summed = lax.psum(partial_sum, "rows")
        right_raw = summed / beta_norm - beta_norm * right_prev
        return (beta_norm, left_raw / beta_norm, right_raw)

    right_zero = jnp.zeros((CB_DEV * 128, width), jnp.float32)
    beta_first, left_vec, right_raw = back_step(delays, right_zero)
    resid_bar = beta_first
    model = right_zero
    search = right_zero
    diag_bar = beta_first
    rotate_cos = beta_first
    rotate_sin = beta_first
    radius = beta_first
    for iteration in range(ITERS):
        right_bf = right_raw.astype(jnp.bfloat16)
        fore_squares = lax.psum(column_norm(right_raw), "cols")
        fore_partial_sum = local_forward(dense_kernel, right_bf)
        fore_summed = lax.psum(fore_partial_sum, "cols")
        alpha_norm = jnp.sqrt(fore_squares + tiny_eps)
        fore_left_raw = fore_summed / alpha_norm - alpha_norm * left_vec
        alpha_norm, right_vec, left_raw = (alpha_norm, right_raw / alpha_norm, fore_left_raw)
        if iteration == 0:
            diag_bar = alpha_norm
            search = right_vec
        else:
            coupling = rotate_sin * alpha_norm
            diag_bar = -rotate_cos * alpha_norm
            search = right_vec - coupling / radius * search
        beta_norm, left_vec, right_raw = back_step(left_raw, right_vec)
        radius = jnp.sqrt(diag_bar * diag_bar + beta_norm * beta_norm)
        rotate_cos = diag_bar / radius
        rotate_sin = beta_norm / radius
        step_size = rotate_cos * resid_bar
        resid_bar = rotate_sin * resid_bar
        model = model + step_size / radius * search
    misfit = resid_bar / beta_first
    gradient = misfit * rotate_cos * right_raw
    return (model, gradient, misfit)


def solution(mesh):
    placed = (P("rows", "cols", None, None), P("rows", "cols"), P("rows", "cols"), P("rows", None))
    return jax.shard_map(
        on_device,
        mesh=mesh,
        in_specs=placed,
        out_specs=(P("cols", None), P("cols", None), P()),
        check_vma=False,
    )
```

profile of v0, /device:TPU:0, one launch (start us, length us, event | category | flops | bytes accessed | tf_op | source)
XLA Modules:
  0.0 423.4 jit_solution(8529983476030962423)
XLA Ops:
  7.2 0.0 all-reduce.6.cloned.1.call-start
  7.2 0.7 iota_compare_fusion.1
  7.9 0.0 copy-start.2
  7.9 9.3 %fusion.12 = bf16[16,24,128,128]{3,1,2,0:T(8,128)(2,1)S(1)} fusion(bf16[16,16,128,128]{3,2,1,0:T(8,128)(2,1)} %param.4, s32[16,16]{1,0:T(8,128)} %param.5, pred[16,16]{1,0:T(8,128)(4,1)S(1)} %iota_compare_fusion.1), kind=kOutput, calls=%fused_computation.12 | convolution fusion | flops 207630336 | bytes 20972800 | tf_op jit(solution)/shard_map/bkc,bkij->bicj/dot_general | solution.py:24
  17.3 0.0 copy-start
  17.3 4.6 %copy-done = bf16[16,24,128,128]{3,1,2,0:T(8,128)(2,1)} copy-done((bf16[16,24,128,128]{3,1,2,0:T(8,128)(2,1)}, bf16[16,24,128,128]{3,1,2,0:T(8,128)(2,1)S(1)}, u32[]{:S(2)}) %copy-start) | copy-done | bytes 12582936
  21.8 0.0 copy-done.2
  21.8 4.9 %fusion.8 = f32[3072,128]{1,0:T(8,128)} fusion(bf16[256,8,24,128]{3,2,1,0:T(8,128)(2,1)S(1)} %bitcast.21, f32[2048,128]{1,0:T(8,128)S(1)} %copy-done.2), kind=kOutput, calls=%fused_computation.8 | convolution fusion | flops 1610874880 | bytes 15204352 | tf_op jit(solution)/shard_map/dot_general | solution.py:33
  26.7 0.0 all-reduce.6.cloned.1.call-update
  26.8 0.0 all-reduce.8.cloned.1.call-start
  26.8 0.3 multiply_reduce_fusion.4
  27.1 23.8 %psum.71 = f32[128]{0:T(128)S(1)} all-reduce(f32[128]{0:T(128)S(1)} %multiply_reduce_fusion.4), channel_id=1, replica_groups=mesh['rows'=8,'cols'=4] {'rows'}, use_global_device_ids=true, to_apply=%region_2.0 | all-reduce | flops 128 | bytes 1024 | tf_op jit(solution)/shard_map/psum | solution.py:44
  50.9 67.9 %all-reduce.6.cloned.1.call-done = f32[3072,128]{1,0:T(8,128)} async-done(((f32[3072,128]{1,0:T(8,128)}), f32[3072,128]{1,0:T(8,128)}) %all-reduce.6.cloned.1.call-update) | async-done | bytes 1572880 | tf_op jit(solution)/shard_map/psum | solution.py:47
  118.8 0.0 copy-start.1
  118.8 9.5 %fusion.6 = f32[2048,128]{1,0:T(8,128)} fusion(bf16[256,8,24,128]{3,2,1,0:T(8,128)(2,1)} %bitcast.22, f32[3072,128]{1,0:T(8,128)} %all-reduce.6.cloned.1.call-done, f32[128]{0:T(128)S(1)} %get-tuple-element.22, f32[128]{0:T(128)S(1)} %get-tuple-element.23), kind=kOutput, calls=%fused_computation.6 | convolution fusion | flops 1611792384 | bytes 15205376 | tf_op jit(solution)/shard_map/dot_general | solution.py:29
  128.3 0.0 all-reduce.8.cloned.1.call-update
  128.3 0.0 all-reduce.10.cloned.1.call-start
  128.4 0.0 copy-done.1
  128.4 0.4 multiply_reduce_fusion.1
  128.8 7.0 %psum.72 = f32[128]{0:T(128)S(1)} all-reduce(f32[128]{0:T(128)S(1)} %multiply_reduce_fusion.1), channel_id=1, replica_groups=mesh['rows'=8,'cols'=4] {'cols'}, use_global_device_ids=true, to_apply=%region_4.0 | all-reduce | flops 128 | bytes 1024 | tf_op jit(solution)/shard_map/psum | solution.py:62
  135.9 28.1 %all-reduce.8.cloned.1.call-done = f32[2048,128]{1,0:T(8,128)} async-done(((f32[2048,128]{1,0:T(8,128)}), f32[2048,128]{1,0:T(8,128)}) %all-reduce.8.cloned.1.call-update) | async-done | bytes 1048592 | tf_op jit(solution)/shard_map/psum | solution.py:64
  164.0 1.5 multiply_reduce_fusion.3
  165.5 0.0 copy-start.3
  165.5 1.0 copy-done.3
  166.5 9.4 %fusion.4 = f32[3072,128]{1,0:T(8,128)} fusion(bf16[256,8,24,128]{3,2,1,0:T(8,128)(2,1)} %bitcast.23, f32[2048,128]{1,0:T(8,128)S(1)} %get-tuple-element.15), kind=kOutput, calls=%fused_computation.4 | convolution fusion | flops 1610874880 | bytes 15204352 | tf_op jit(solution)/shard_map/dot_general | solution.py:33
  175.9 0.0 all-reduce.10.cloned.1.call-update
  175.9 0.0 all-reduce.12.cloned.1.call-start
  176.0 22.0 %psum.74 = f32[128]{0:T(128)S(1)} all-reduce(f32[128]{0:T(128)S(1)} %get-tuple-element.14), channel_id=1, replica_groups=mesh['rows'=8,'cols'=4] {'rows'}, use_global_device_ids=true, to_apply=%region_7.0 | all-reduce | flops 128 | bytes 1024 | tf_op jit(solution)/shard_map/psum | solution.py:44
  198.0 67.6 %all-reduce.10.cloned.1.call-done = f32[3072,128]{1,0:T(8,128)} async-done(((f32[3072,128]{1,0:T(8,128)}), f32[3072,128]{1,0:T(8,128)}) %all-reduce.10.cloned.1.call-update) | async-done | bytes 1572880 | tf_op jit(solution)/shard_map/psum | solution.py:47
  265.6 1.8 multiply_reduce_fusion
  267.4 9.0 %fusion.2 = f32[2048,128]{1,0:T(8,128)} fusion(bf16[256,8,24,128]{3,2,1,0:T(8,128)(2,1)} %bitcast.24, f32[3072,128]{1,0:T(8,128)S(1)} %get-tuple-element.13), kind=kOutput, calls=%fused_computation.2 | convolution fusion | flops 1611005952 | bytes 15204352 | tf_op jit(solution)/shard_map/dot_general | solution.py:29
  276.4 0.0 all-reduce.12.cloned.1.call-update
  276.4 0.0 all-reduce.14.cloned.1.call-start
  276.5 7.1 %psum.76 = f32[128]{0:T(128)S(1)} all-reduce(f32[128]{0:T(128)S(1)} %get-tuple-element.12), channel_id=1, replica_groups=mesh['rows'=8,'cols'=4] {'cols'}, use_global_device_ids=true, to_apply=%region_10.0 | all-reduce | flops 128 | bytes 1024 | tf_op jit(solution)/shard_map/psum | solution.py:62
  283.6 28.5 %all-reduce.12.cloned.1.call-done = f32[2048,128]{1,0:T(8,128)} async-done(((f32[2048,128]{1,0:T(8,128)}), f32[2048,128]{1,0:T(8,128)}) %all-reduce.12.cloned.1.call-update) | async-done | bytes 1048592 | tf_op jit(solution)/shard_map/psum | solution.py:64
  312.0 1.8 multiply_reduce_fusion.2
  313.9 9.4 %fusion = f32[3072,128]{1,0:T(8,128)} fusion(bf16[256,8,24,128]{3,2,1,0:T(8,128)(2,1)} %bitcast.25, bf16[2048,128]{1,0:T(8,128)(2,1)S(1)} %get-tuple-element.11), kind=kOutput, calls=%fused_computation | convolution fusion | flops 1610612736 | bytes 14680064 | tf_op jit(solution)/shard_map/dot_general | solution.py:33
  323.3 0.0 all-reduce.14.cloned.1.call-update
  323.3 22.0 %psum.78 = f32[128]{0:T(128)S(1)} all-reduce(f32[128]{0:T(128)S(1)} %get-tuple-element.10), channel_id=1, replica_groups=mesh['rows'=8,'cols'=4] {'rows'}, use_global_device_ids=true, to_apply=%region_13.0 | all-reduce | flops 128 | bytes 1024 | tf_op jit(solution)/shard_map/psum | solution.py:44
  345.3 0.6 fusion.33
  345.9 67.2 %all-reduce.14.cloned.1.call-done = f32[3072,128]{1,0:T(8,128)} async-done(((f32[3072,128]{1,0:T(8,128)}), f32[3072,128]{1,0:T(8,128)}) %all-reduce.14.cloned.1.call-update) | async-done | bytes 1572880 | tf_op jit(solution)/shard_map/psum | solution.py:47
  413.1 3.7 subtract_multiply_fusion
  (5 shorter events, 0.0 us)
Async XLA Ops:
  7.2 111.6 %all-reduce.6.cloned.1.call-start = ((), (), s32[]{:S(2)}) async-start(), calls=%async_computation | async-start | bytes 3145728 | tf_op jit(solution)/shard_map/psum | solution.py:47
  7.9 13.9 %copy-start.2 = (f32[2048,128]{1,0:T(8,128)S(1)}, f32[2048,128]{1,0:T(8,128)}, u32[]{:S(2)}) copy-start(f32[2048,128]{1,0:T(8,128)} %param.7) | copy-start | bytes 3145732
  17.3 4.6 %copy-start = (bf16[16,24,128,128]{3,1,2,0:T(8,128)(2,1)}, bf16[16,24,128,128]{3,1,2,0:T(8,128)(2,1)S(1)}, u32[]{:S(2)}) copy-start(bf16[16,24,128,128]{3,1,2,0:T(8,128)(2,1)S(1)} %fusion.12) | copy-start | bytes 37748740
  26.8 137.3 %all-reduce.8.cloned.1.call-start = ((), (), s32[]{:S(2)}) async-start(), calls=%async_computation.1 | async-start | bytes 2097152 | tf_op jit(solution)/shard_map/psum | solution.py:64
  118.8 9.6 %copy-start.1 = (f32[3072,128]{1,0:T(8,128)S(1)}, f32[3072,128]{1,0:T(8,128)}, u32[]{:S(2)}) copy-start(f32[3072,128]{1,0:T(8,128)} %all-reduce.6.cloned.1.call-done) | copy-start | bytes 4718596
  128.3 137.3 %all-reduce.10.cloned.1.call-start = ((), (), s32[]{:S(2)}) async-start(), calls=%async_computation.2 | async-start | bytes 3145728 | tf_op jit(solution)/shard_map/psum | solution.py:47
  165.5 1.0 copy-start.3
  175.9 136.1 %all-reduce.12.cloned.1.call-start = ((), (), s32[]{:S(2)}) async-start(), calls=%async_computation.3 | async-start | bytes 2097152 | tf_op jit(solution)/shard_map/psum | solution.py:64
  276.4 136.7 %all-reduce.14.cloned.1.call-start = ((), (), s32[]{:S(2)}) async-start(), calls=%async_computation.4 | async-start | bytes 3145728 | tf_op jit(solution)/shard_map/psum | solution.py:47
Sparse Core Ops, SparseCore 0:
  26.9 91.8 all-reduce.5
  128.5 35.5 all-reduce.7
  176.1 89.4 all-reduce.9
  276.6 35.4 all-reduce.11
  323.4 89.6 all-reduce.13
where the time goes:
time: 424 us; the launch traced here: 423 us
  waiting for transfers between devices  259 us (61%)
  blocking collectives  81.9 us (19%)
  matrix products  51.5 us (12%)
  between operations  13.8 us (3%)
  other arithmetic  11 us (3%)
  local copies, waits for them, and re-layouts  5.54 us (1%)
    psum x3, waiting for transfers between devices, back_step(): summed = lax.psum(partial_sum, 'rows')  203 us
    psum x3, blocking collectives, back_step(): squares = lax.psum(column_norm(left_raw), 'rows')  67.8 us
    psum x2, waiting for transfers between devices, on_device(): fore_summed = lax.psum(fore_partial_sum, 'cols')  56.6 us
    dot_general x3, matrix products, local_backward(): lax.dot_general(dense_kernel, vec_bf, (((0,), (0,)), ((), ())), preferred...  23.7 us
    dot_general x2, matrix products, local_forward(): return jnp.dot(dense_kernel, vec_bf, preferred_element_type=jnp.float32)  18.5 us
    psum x2, blocking collectives, on_device(): fore_squares = lax.psum(column_norm(right_raw), 'cols')  14.1 us
    dot_general x1, matrix products, build_dense(): jnp.einsum('bkc,bkij->bicj', selector, kernel, preferred_element_type=jnp...  9.31 us
  transfers between devices with their start and end apart: 5, of which 5 were waited for; matrix products, arithmetic and copies ran while one was open for 0% of the time, Pallas kernels for 0%

commit v1 on v0

--- a/solution.py
+++ b/solution.py
@@ -35,16 +35,64 @@
     )
 
 
-def on_device(kernel, pattern, counts, delays):
+def swap(value, axis, count, bit):
+    return lax.ppermute(value, axis, [(i, i ^ (1 << bit)) for i in range(count)])
+
+
+def reduce_streams(streams, norm, axis, count, orders):
+    index = lax.axis_index(axis)
+    levels = len(orders[0])
+    streams = list(streams)
+    for level in range(levels):
+        for s, order in enumerate(orders):
+            bit = order[level]
+            side = (index >> bit) & 1
+            if level < levels - 1:
+                half = streams[s].shape[0] // 2
+                keep = lax.dynamic_slice_in_dim(streams[s], side * half, half)
+                send = lax.dynamic_slice_in_dim(streams[s], (1 - side) * half, half)
+            else:
+                keep = send = streams[s]
+            if s == 0:
+                send = jnp.concatenate([send, norm])
+            got = swap(send, axis, count, bit)
+            streams[s] = keep + got[: keep.shape[0]]
+            if s == 0:
+                norm = norm + got[keep.shape[0] :]
+    for level in reversed(range(levels - 1)):
+        for s, order in enumerate(orders):
+            bit = order[level]
+            side = (index >> bit) & 1
+            got = swap(streams[s], axis, count, bit)
+            low = jnp.where(side == 0, streams[s], got)
+            high = jnp.where(side == 0, got, streams[s])
+            streams[s] = jnp.concatenate([low, high])
+    return streams, norm
+
+
+def bit_orders(count):
+    bits = list(range(count.bit_length() - 1))
+    other = [bits[1], bits[0], *bits[2:]] if len(bits) > 2 else bits
+    return [bits, other]
+
+
+def on_device(row_count, col_count, kernel, pattern, counts, delays):
     width = delays.shape[1]
     dense_kernel = build_dense(kernel, pattern, counts)
 
+    def summed_with_norm(partial, values, axis, count):
+        norm = jnp.broadcast_to(column_norm(values)[None, :], (8, width))
+        half = partial.shape[0] // 2
+        pieces, norm = reduce_streams(
+            [partial[:half], partial[half:]], norm, axis, count, bit_orders(count)
+        )
+        return jnp.concatenate(pieces), norm[0]
+
     def back_step(left_raw, right_prev):
         left_bf = left_raw.astype(jnp.bfloat16)
-        squares = lax.psum(column_norm(left_raw), "rows")
+        partial_sum = local_backward(dense_kernel, left_bf)
+        summed, squares = summed_with_norm(partial_sum, left_raw, "rows", row_count)
         beta_norm = jnp.sqrt(squares + tiny_eps)
-        partial_sum = local_backward(dense_kernel, left_bf)
-        summed = lax.psum(partial_sum, "rows")
         right_raw = summed / beta_norm - beta_norm * right_prev
         return (beta_norm, left_raw / beta_norm, right_raw)
 
@@ -59,9 +107,8 @@
     radius = beta_first
     for iteration in range(ITERS):
         right_bf = right_raw.astype(jnp.bfloat16)
-        fore_squares = lax.psum(column_norm(right_raw), "cols")
         fore_partial_sum = local_forward(dense_kernel, right_bf)
-        fore_summed = lax.psum(fore_partial_sum, "cols")
+        fore_summed, fore_squares = summed_with_norm(fore_partial_sum, right_raw, "cols", col_count)
         alpha_norm = jnp.sqrt(fore_squares + tiny_eps)
         fore_left_raw = fore_summed / alpha_norm - alpha_norm * left_vec
         alpha_norm, right_vec, left_raw = (alpha_norm, right_raw / alpha_norm, fore_left_raw)
@@ -86,8 +133,14 @@
 
 def solution(mesh):
     placed = (P("rows", "cols", None, None), P("rows", "cols"), P("rows", "cols"), P("rows", None))
+
+    def local(kernel, pattern, counts, delays):
+        return on_device(
+            mesh.shape["rows"], mesh.shape["cols"], kernel, pattern, counts, delays
+        )
+
     return jax.shard_map(
-        on_device,
+        local,
         mesh=mesh,
         in_specs=placed,
         out_specs=(P("cols", None), P("cols", None), P()),

time: 424 us -> 253 us (0.60)
  waiting for transfers between devices: 259 us -> 153 us
  blocking collectives: 81.9 us -> 0 us
  starting transfers between devices: 0.21 us -> 42.2 us
  matrix products: 51.5 us -> 37.7 us
  between operations: 13.8 us -> 1.41 us
  other arithmetic: 11 us -> 15.4 us
    psum x5 -> x0, waiting for transfers between devices: 259 us -> none  [the longest x3 203 us: back_step(): summed = lax.psum(partial_sum, 'rows')]
    ppermute x0 -> x42, waiting for transfers between devices: none -> 153 us  [swap(): return lax.ppermute(value, axis, [(i, i ^ 1 << bit) for i in range(count)])]
    psum x5 -> x0, blocking collectives: 81.9 us -> none  [the longest x3 67.8 us: back_step(): squares = lax.psum(column_norm(left_raw), 'rows')]
    ppermute x0 -> x42, starting transfers between devices: none -> 42.2 us  [swap(): return lax.ppermute(value, axis, [(i, i ^ 1 << bit) for i in range(count)])]
    dot_general x3, matrix products: 23.7 us -> 16.3 us  [local_backward(): lax.dot_general(dense_kernel, vec_bf, (((0,), (0,)), ((), ())), preferred...]
    add x0 -> x39, other arithmetic: none -> 6.85 us  [the longest x26 5.44 us: reduce_streams(): streams[s] = keep + got[:keep.shape[0]]]
    dot_general x2, matrix products: 18.5 us -> 12.1 us  [local_forward(): return jnp.dot(dense_kernel, vec_bf, preferred_element_type=jnp.float32)]
  transfers between devices with their start and end apart: 5 -> 42, of which waited for: 5 -> 29; matrix products, arithmetic and copies ran while one was open for 0% -> 4% of each run, Pallas kernels for 0% -> 0%
where the time goes in v1:
time: 253 us
  waiting for transfers between devices  153 us (60%)
  starting transfers between devices  42.2 us (17%)
  matrix products  37.7 us (15%)
  other arithmetic  15.4 us (6%)
  local copies, waits for them, and re-layouts  3.15 us (1%)
    ppermute x42, waiting for transfers between devices, swap(): return lax.ppermute(value, axis, [(i, i ^ 1 << bit) for i in range(count)])  153 us
    ppermute x42, starting transfers between devices, swap(): return lax.ppermute(value, axis, [(i, i ^ 1 << bit) for i in range(count)])  42.2 us
    dot_general x3, matrix products, local_backward(): lax.dot_general(dense_kernel, vec_bf, (((0,), (0,)), ((), ())), preferred...  16.3 us
    dot_general x2, matrix products, local_forward(): return jnp.dot(dense_kernel, vec_bf, preferred_element_type=jnp.float32)  12.1 us
    dot_general x1, matrix products, build_dense(): jnp.einsum('bkc,bkij->bicj', selector, kernel, preferred_element_type=jnp...  9.31 us
    add x26, other arithmetic, reduce_streams(): streams[s] = keep + got[:keep.shape[0]]  5.44 us
  transfers between devices with their start and end apart: 42, of which 29 were waited for; matrix products, arithmetic and copies ran while one was open for 4% of the time, Pallas kernels for 0%

profile of v1, /device:TPU:0, one launch (start us, length us, event | category | flops | bytes accessed | tf_op | source)
XLA Modules:
  0.0 252.7 jit_solution(11309500972846894188)
XLA Ops:
  0.6 1.5 multiply_reduce_fusion.4
  2.9 9.3 %fusion.12 = bf16[16,24,128,128]{3,1,2,0:T(8,128)(2,1)S(1)} fusion(bf16[16,16,128,128]{3,2,1,0:T(8,128)(2,1)} %param.4, s32[16,16]{1,0:T(8,128)} %param.5, pred[16,16]{1,0:T(8,128)(4,1)S(1)} %iota_compare_fusion.1), kind=kOutput, calls=%fused_computation.12 | convolution fusion | flops 207630336 | bytes 20972800 | tf_op jit(solution)/shard_map/bkc,bkij->bicj/dot_general | solution.py:24
  12.2 3.8 %fusion.8 = f32[3072,128]{1,0:T(8,128)S(1)} fusion(bf16[256,8,24,128]{3,2,1,0:T(8,128)(2,1)S(1)} %bitcast.45, f32[2048,128]{1,0:T(8,128)S(1)} %copy-done.1), kind=kOutput, calls=%fused_computation.8 | convolution fusion | flops 1610874880 | bytes 15204352 | tf_op jit(solution)/shard_map/dot_general | solution.py:33
  17.0 3.0 %collective-permute-start = (f32[776,128]{1,0:T(8,128)S(1)}, f32[776,128]{1,0:T(8,128)S(1)}, u32[]{:S(2)}, u32[]{:S(2)}) collective-permute-start(f32[776,128]{1,0:T(8,128)S(1)} %pad_maximum_fusion), channel_id=1, source_target_pairs={{0,4},{4,0},{8,12},{12,8},{16,20},{20,16},{24,28},{28,24},{1,5},{5... | collective-permute-start | bytes 1191944 | tf_op jit(solution)/shard_map/ppermute | solution.py:39
  20.8 1.6 collective-permute-start.5
  22.3 6.9 %collective-permute-done = f32[776,128]{1,0:T(8,128)S(1)} collective-permute-done((f32[776,128]{1,0:T(8,128)S(1)}, f32[776,128]{1,0:T(8,128)S(1)}, u32[]{:S(2)}, u32[]{:S(2)}) %collective-permute-start) | collective-permute-done | bytes 397344 | tf_op jit(solution)/shard_map/ppermute | solution.py:39
  29.3 1.9 collective-permute-start.1
  31.8 1.0 dynamic-slice_add_fusion.2
  33.8 2.0 collective-permute-done.1
  35.9 2.7 %collective-permute-start.2 = (f32[392,128]{1,0:T(8,128)S(1)}, f32[392,128]{1,0:T(8,128)S(1)}, u32[]{:S(2)}, u32[]{:S(2)}) collective-permute-start(f32[392,128]{1,0:T(8,128)S(1)} %pad_maximum_fusion.14), channel_id=1, source_target_pairs={{0,16},{4,20},{8,24},{12,28},{16,0},{20,4},{24,8},{28,12},{1,17},{... | collective-permute-start | bytes 602120 | tf_op jit(solution)/shard_map/ppermute | solution.py:39
  38.6 2.8 %collective-permute-start.7 = (f32[384,128]{1,0:T(8,128)S(1)}, f32[384,128]{1,0:T(8,128)S(1)}, u32[]{:S(2)}, u32[]{:S(2)}) collective-permute-start(f32[384,128]{1,0:T(8,128)S(1)} %dynamic-slice_add_fusion.7), channel_id=1, source_target_pairs={{0,16},{4,20},{8,24},{12,28},{16,0},{20,4},{24,8},{28,12},{1,17},{... | collective-permute-start | bytes 589832 | tf_op jit(solution)/shard_map/ppermute | solution.py:39
  41.4 13.8 %collective-permute-done.7 = f32[384,128]{1,0:T(8,128)S(1)} collective-permute-done((f32[384,128]{1,0:T(8,128)S(1)}, f32[384,128]{1,0:T(8,128)S(1)}, u32[]{:S(2)}, u32[]{:S(2)}) %collective-permute-start.7) | collective-permute-done | bytes 196640 | tf_op jit(solution)/shard_map/ppermute | solution.py:39
  56.8 4.5 %collective-permute-done.8 = f32[384,128]{1,0:T(8,128)S(1)} collective-permute-done((f32[384,128]{1,0:T(8,128)S(1)}, f32[384,128]{1,0:T(8,128)S(1)}, u32[]{:S(2)}, u32[]{:S(2)}) %collective-permute-start.8) | collective-permute-done | bytes 196640 | tf_op jit(solution)/shard_map/ppermute | solution.py:39
  61.3 1.4 collective-permute-start.9
  63.8 7.4 %collective-permute-done.9 = f32[768,128]{1,0:T(8,128)S(1)} collective-permute-done((f32[768,128]{1,0:T(8,128)S(1)}, f32[768,128]{1,0:T(8,128)S(1)}, u32[]{:S(2)}, u32[]{:S(2)}) %collective-permute-start.9) | collective-permute-done | bytes 393248 | tf_op jit(solution)/shard_map/ppermute | solution.py:39
  71.2 1.6 collective-permute-done.4
  73.2 8.7 %fusion.6 = f32[2048,128]{1,0:T(8,128)S(1)} fusion(bf16[256,8,24,128]{3,2,1,0:T(8,128)(2,1)} %bitcast.46, f32[768,128]{1,0:T(8,128)S(1)} %get-tuple-element.38, f32[768,128]{1,0:T(8,128)S(1)} %get-tuple-element.37, f32[768,128]{1,0:T(8,128)S(1)} %get-tuple-element.36, f32[768,128]{1,0:T(8,128)S(1)} %get-tuple-element.35, f32[128]{0:T(128)S(1)} %broadcast_multiply_fusion, ...), kind=kOutput, calls=%fused_computation.6 | convolution fusion | flops 1612972032 | bytes 15205376 | tf_op jit(solution)/shard_map/dot_general | solution.py:29
  83.5 1.1 collective-permute-done.10
  84.6 1.1 slice_add_fusion.6
  87.1 1.5 collective-permute-start.11
  89.8 11.5 %collective-permute-done.14 = f32[512,128]{1,0:T(8,128)S(1)} collective-permute-done((f32[512,128]{1,0:T(8,128)}, f32[512,128]{1,0:T(8,128)S(1)}, u32[]{:S(2)}, u32[]{:S(2)}) %collective-permute-start.14) | collective-permute-done | bytes 262176 | tf_op jit(solution)/shard_map/ppermute | solution.py:39
  105.4 8.4 %fusion.4 = f32[3072,128]{1,0:T(8,128)S(1)} fusion(bf16[256,8,24,128]{3,2,1,0:T(8,128)(2,1)} %bitcast.47, f32[2048,128]{1,0:T(8,128)S(1)} %get-tuple-element.14), kind=kOutput, calls=%fused_computation.4 | convolution fusion | flops 1610874880 | bytes 15204352 | tf_op jit(solution)/shard_map/dot_general | solution.py:33
  114.0 1.0 collective-permute-start.16
  115.8 9.7 %collective-permute-done.16 = f32[776,128]{1,0:T(8,128)S(1)} collective-permute-done((f32[776,128]{1,0:T(8,128)S(1)}, f32[776,128]{1,0:T(8,128)S(1)}, u32[]{:S(2)}, u32[]{:S(2)}) %collective-permute-start.16) | collective-permute-done | bytes 397344 | tf_op jit(solution)/shard_map/ppermute | solution.py:39
  126.4 1.2 collective-permute-start.22
  127.5 4.7 %collective-permute-done.17 = f32[392,128]{1,0:T(8,128)S(1)} collective-permute-done((f32[392,128]{1,0:T(8,128)S(1)}, f32[392,128]{1,0:T(8,128)S(1)}, u32[]{:S(2)}, u32[]{:S(2)}) %collective-permute-start.17) | collective-permute-done | bytes 200736 | tf_op jit(solution)/shard_map/ppermute | solution.py:39
  132.3 3.4 %collective-permute-start.18 = (f32[392,128]{1,0:T(8,128)S(1)}, f32[392,128]{1,0:T(8,128)S(1)}, u32[]{:S(2)}, u32[]{:S(2)}) collective-permute-start(f32[392,128]{1,0:T(8,128)S(1)} %pad_maximum_fusion.16), channel_id=1, source_target_pairs={{0,16},{4,20},{8,24},{12,28},{16,0},{20,4},{24,8},{28,12},{1,17},{... | collective-permute-start | bytes 602120 | tf_op jit(solution)/shard_map/ppermute | solution.py:39
  136.0 16.2 %collective-permute-done.23 = f32[384,128]{1,0:T(8,128)S(1)} collective-permute-done((f32[384,128]{1,0:T(8,128)S(1)}, f32[384,128]{1,0:T(8,128)S(1)}, u32[]{:S(2)}, u32[]{:S(2)}) %collective-permute-start.23) | collective-permute-done | bytes 196640 | tf_op jit(solution)/shard_map/ppermute | solution.py:39
  152.2 1.0 collective-permute-start.24
  153.4 5.7 %collective-permute-done.24 = f32[384,128]{1,0:T(8,128)S(1)} collective-permute-done((f32[384,128]{1,0:T(8,128)S(1)}, f32[384,128]{1,0:T(8,128)S(1)}, u32[]{:S(2)}, u32[]{:S(2)}) %collective-permute-start.24) | collective-permute-done | bytes 196640 | tf_op jit(solution)/shard_map/ppermute | solution.py:39
  159.8 1.3 collective-permute-start.20
  161.1 8.3 %collective-permute-done.25 = f32[768,128]{1,0:T(8,128)S(1)} collective-permute-done((f32[768,128]{1,0:T(8,128)S(1)}, f32[768,128]{1,0:T(8,128)S(1)}, u32[]{:S(2)}, u32[]{:S(2)}) %collective-permute-start.25) | collective-permute-done | bytes 393248 | tf_op jit(solution)/shard_map/ppermute | solution.py:39
  170.1 3.4 %fusion.2 = f32[2048,128]{1,0:T(8,128)S(1)} fusion(bf16[256,8,24,128]{3,2,1,0:T(8,128)(2,1)S(1)} %bitcast.50, f32[3072,128]{1,0:T(8,128)S(1)} %get-tuple-element.12), kind=kOutput, calls=%fused_computation.2 | convolution fusion | flops 1611005952 | bytes 15204352 | tf_op jit(solution)/shard_map/dot_general | solution.py:29
  175.4 1.6 collective-permute-start.27
  177.6 11.9 %collective-permute-done.30 = f32[512,128]{1,0:T(8,128)S(1)} collective-permute-done((f32[512,128]{1,0:T(8,128)S(1)}, f32[512,128]{1,0:T(8,128)S(1)}, u32[]{:S(2)}, u32[]{:S(2)}) %collective-permute-start.30) | collective-permute-done | bytes 262176 | tf_op jit(solution)/shard_map/ppermute | solution.py:39
  191.9 4.1 %fusion = f32[3072,128]{1,0:T(8,128)S(1)} fusion(bf16[256,8,24,128]{3,2,1,0:T(8,128)(2,1)S(1)} %bitcast.51, bf16[2048,128]{1,0:T(8,128)(2,1)S(1)} %get-tuple-element.10), kind=kOutput, calls=%fused_computation | convolution fusion | flops 1610612736 | bytes 14680064 | tf_op jit(solution)/shard_map/dot_general | solution.py:33
  196.1 1.4 collective-permute-start.32
  197.6 1.1 collective-permute-start.37
  198.7 8.9 %collective-permute-done.32 = f32[776,128]{1,0:T(8,128)S(1)} collective-permute-done((f32[776,128]{1,0:T(8,128)S(1)}, f32[776,128]{1,0:T(8,128)S(1)}, u32[]{:S(2)}, u32[]{:S(2)}) %collective-permute-start.32) | collective-permute-done | bytes 397344 | tf_op jit(solution)/shard_map/ppermute | solution.py:39
  207.7 1.8 collective-permute-start.33
  210.2 3.8 %collective-permute-done.33 = f32[392,128]{1,0:T(8,128)S(1)} collective-permute-done((f32[392,128]{1,0:T(8,128)S(1)}, f32[392,128]{1,0:T(8,128)S(1)}, u32[]{:S(2)}, u32[]{:S(2)}) %collective-permute-start.33) | collective-permute-done | bytes 200736 | tf_op jit(solution)/shard_map/ppermute | solution.py:39
  215.6 1.6 collective-permute-start.39
  217.2 16.0 %collective-permute-done.39 = f32[384,128]{1,0:T(8,128)S(1)} collective-permute-done((f32[384,128]{1,0:T(8,128)S(1)}, f32[384,128]{1,0:T(8,128)S(1)}, u32[]{:S(2)}, u32[]{:S(2)}) %collective-permute-start.39) | collective-permute-done | bytes 196640 | tf_op jit(solution)/shard_map/ppermute | solution.py:39
  233.2 1.4 collective-permute-start.40
  235.4 3.8 %collective-permute-done.40 = f32[384,128]{1,0:T(8,128)S(1)} collective-permute-done((f32[384,128]{1,0:T(8,128)S(1)}, f32[384,128]{1,0:T(8,128)S(1)}, u32[]{:S(2)}, u32[]{:S(2)}) %collective-permute-start.40) | collective-permute-done | bytes 196640 | tf_op jit(solution)/shard_map/ppermute | solution.py:39
  239.4 2.1 collective-permute-done.35
  241.6 7.6 %collective-permute-done.41 = f32[768,128]{1,0:T(8,128)S(1)} collective-permute-done((f32[768,128]{1,0:T(8,128)S(1)}, f32[768,128]{1,0:T(8,128)S(1)}, u32[]{:S(2)}, u32[]{:S(2)}) %collective-permute-start.41) | collective-permute-done | bytes 393248 | tf_op jit(solution)/shard_map/ppermute | solution.py:39
  250.3 2.4 fusion.23
  (170 shorter events, 28.6 us)
Async XLA Ops:
  2.9 9.3 %copy-start.1 = (f32[2048,128]{1,0:T(8,128)S(1)}, f32[2048,128]{1,0:T(8,128)}, u32[]{:S(2)}) copy-start(f32[2048,128]{1,0:T(8,128)} %param.7) | copy-start | bytes 3145732
  12.2 4.6 %copy-start = (bf16[16,24,128,128]{3,1,2,0:T(8,128)(2,1)}, bf16[16,24,128,128]{3,1,2,0:T(8,128)(2,1)S(1)}, u32[]{:S(2)}) copy-start(bf16[16,24,128,128]{3,1,2,0:T(8,128)(2,1)S(1)} %fusion.12) | copy-start | bytes 37748740
  17.0 12.2 %collective-permute-start = (f32[776,128]{1,0:T(8,128)S(1)}, f32[776,128]{1,0:T(8,128)S(1)}, u32[]{:S(2)}, u32[]{:S(2)}) collective-permute-start(f32[776,128]{1,0:T(8,128)S(1)} %pad_maximum_fusion), channel_id=1, source_target_pairs={{0,4},{4,0},{8,12},{12,8},{16,20},{20,16},{24,28},{28,24},{1,5},{5... | collective-permute-start | bytes 1191944 | tf_op jit(solution)/shard_map/ppermute | solution.py:39
  20.8 11.0 %collective-permute-start.5 = (f32[768,128]{1,0:T(8,128)}, f32[768,128]{1,0:T(8,128)}, u32[]{:S(2)}, u32[]{:S(2)}) collective-permute-start(f32[768,128]{1,0:T(8,128)} %constant_dynamic-slice_fusion.13), channel_id=1, source_target_pairs={{0,8},{4,12},{8,0},{12,4},{16,24},{20,28},{24,16},{28,20},{1,9},{5... | collective-permute-start | bytes 1179656 | tf_op jit(solution)/shard_map/ppermute | solution.py:39
  29.3 6.5 %collective-permute-start.1 = (f32[392,128]{1,0:T(8,128)S(1)}, f32[392,128]{1,0:T(8,128)S(1)}, u32[]{:S(2)}, u32[]{:S(2)}) collective-permute-start(f32[392,128]{1,0:T(8,128)S(1)} %pad_maximum_fusion.13), channel_id=1, source_target_pairs={{0,8},{4,12},{8,0},{12,4},{16,24},{20,28},{24,16},{28,20},{1,9},{5... | collective-permute-start | bytes 602120 | tf_op jit(solution)/shard_map/ppermute | solution.py:39
  32.9 5.7 %collective-permute-start.6 = (f32[384,128]{1,0:T(8,128)S(1)}, f32[384,128]{1,0:T(8,128)S(1)}, u32[]{:S(2)}, u32[]{:S(2)}) collective-permute-start(f32[384,128]{1,0:T(8,128)S(1)} %constant_dynamic-slice_fusion.12), channel_id=1, source_target_pairs={{0,4},{4,0},{8,12},{12,8},{16,20},{20,16},{24,28},{28,24},{1,5},{5... | collective-permute-start | bytes 589832 | tf_op jit(solution)/shard_map/ppermute | solution.py:39
  35.9 20.1 %collective-permute-start.2 = (f32[392,128]{1,0:T(8,128)S(1)}, f32[392,128]{1,0:T(8,128)S(1)}, u32[]{:S(2)}, u32[]{:S(2)}) collective-permute-start(f32[392,128]{1,0:T(8,128)S(1)} %pad_maximum_fusion.14), channel_id=1, source_target_pairs={{0,16},{4,20},{8,24},{12,28},{16,0},{20,4},{24,8},{28,12},{1,17},{... | collective-permute-start | bytes 602120 | tf_op jit(solution)/shard_map/ppermute | solution.py:39
  38.6 16.5 %collective-permute-start.7 = (f32[384,128]{1,0:T(8,128)S(1)}, f32[384,128]{1,0:T(8,128)S(1)}, u32[]{:S(2)}, u32[]{:S(2)}) collective-permute-start(f32[384,128]{1,0:T(8,128)S(1)} %dynamic-slice_add_fusion.7), channel_id=1, source_target_pairs={{0,16},{4,20},{8,24},{12,28},{16,0},{20,4},{24,8},{28,12},{1,17},{... | collective-permute-start | bytes 589832 | tf_op jit(solution)/shard_map/ppermute | solution.py:39
  55.2 6.0 %collective-permute-start.8 = (f32[384,128]{1,0:T(8,128)S(1)}, f32[384,128]{1,0:T(8,128)S(1)}, u32[]{:S(2)}, u32[]{:S(2)}) collective-permute-start(f32[384,128]{1,0:T(8,128)S(1)} %add.244), channel_id=1, source_target_pairs={{0,4},{4,0},{8,12},{12,8},{16,20},{20,16},{24,28},{28,24},{1,5},{5... | collective-permute-start | bytes 589832 | tf_op jit(solution)/shard_map/ppermute | solution.py:39
  56.0 6.7 %collective-permute-start.3 = (f32[384,128]{1,0:T(8,128)S(1)}, f32[384,128]{1,0:T(8,128)S(1)}, u32[]{:S(2)}, u32[]{:S(2)}) collective-permute-start(f32[384,128]{1,0:T(8,128)S(1)} %slice_add_fusion.11), channel_id=1, source_target_pairs={{0,8},{4,12},{8,0},{12,4},{16,24},{20,28},{24,16},{28,20},{1,9},{5... | collective-permute-start | bytes 589832 | tf_op jit(solution)/shard_map/ppermute | solution.py:39
  61.3 9.8 %collective-permute-start.9 = (f32[768,128]{1,0:T(8,128)S(1)}, f32[768,128]{1,0:T(8,128)S(1)}, u32[]{:S(2)}, u32[]{:S(2)}) collective-permute-start(f32[768,128]{1,0:T(8,128)S(1)} %pad_maximum_fusion.4), channel_id=1, source_target_pairs={{0,8},{4,12},{8,0},{12,4},{16,24},{20,28},{24,16},{28,20},{1,9},{5... | collective-permute-start | bytes 1179656 | tf_op jit(solution)/shard_map/ppermute | solution.py:39
  62.8 10.0 %collective-permute-start.4 = (f32[768,128]{1,0:T(8,128)S(1)}, f32[768,128]{1,0:T(8,128)S(1)}, u32[]{:S(2)}, u32[]{:S(2)}) collective-permute-start(f32[768,128]{1,0:T(8,128)S(1)} %pad_maximum_fusion.3), channel_id=1, source_target_pairs={{0,4},{4,0},{8,12},{12,8},{16,20},{20,16},{24,28},{28,24},{1,5},{5... | collective-permute-start | bytes 1179656 | tf_op jit(solution)/shard_map/ppermute | solution.py:39
  82.0 0.8 copy-start.2
  82.8 1.7 collective-permute-start.10
  83.0 5.6 %collective-permute-start.13 = (f32[512,128]{1,0:T(8,128)S(1)}, f32[512,128]{1,0:T(8,128)S(1)}, u32[]{:S(2)}, u32[]{:S(2)}) collective-permute-start(f32[512,128]{1,0:T(8,128)S(1)} %constant_dynamic-slice_fusion.10), channel_id=1, source_target_pairs={{0,1},{1,0},{2,3},{3,2},{4,5},{5,4},{6,7},{7,6},{8,9},{9,8},{10,11... | collective-permute-start | bytes 786440 | tf_op jit(solution)/shard_map/ppermute | solution.py:39
  87.1 15.3 %collective-permute-start.11 = (f32[520,128]{1,0:T(8,128)}, f32[520,128]{1,0:T(8,128)}, u32[]{:S(2)}, u32[]{:S(2)}) collective-permute-start(f32[520,128]{1,0:T(8,128)} %pad_maximum_fusion.10), channel_id=1, source_target_pairs={{0,2},{1,3},{2,0},{3,1},{4,6},{5,7},{6,4},{7,5},{8,10},{9,11},{10,... | collective-permute-start | bytes 798728 | tf_op jit(solution)/shard_map/ppermute | solution.py:39
  89.3 12.0 %collective-permute-start.14 = (f32[512,128]{1,0:T(8,128)}, f32[512,128]{1,0:T(8,128)S(1)}, u32[]{:S(2)}, u32[]{:S(2)}) collective-permute-start(f32[512,128]{1,0:T(8,128)} %dynamic-slice_add_fusion.4), channel_id=1, source_target_pairs={{0,2},{1,3},{2,0},{3,1},{4,6},{5,7},{6,4},{7,5},{8,10},{9,11},{10,... | collective-permute-start | bytes 786440 | tf_op jit(solution)/shard_map/ppermute | solution.py:39
  102.3 2.3 collective-permute-start.15
  103.4 1.7 collective-permute-start.12
  113.8 56.3 %slice-start = ((s8[12582912]{0:T(1024)(128)(4,1)}), s8[4194304]{0:T(1024)(128)(4,1)S(1)}, s32[]{:S(2)}) async-start(s8[12582912]{0:T(1024)(128)(4,1)} %bitcast.48), calls=%async_computation | async-start | bytes 8388608
  114.0 11.6 %collective-permute-start.16 = (f32[776,128]{1,0:T(8,128)S(1)}, f32[776,128]{1,0:T(8,128)S(1)}, u32[]{:S(2)}, u32[]{:S(2)}) collective-permute-start(f32[776,128]{1,0:T(8,128)S(1)} %pad_maximum_fusion.1), channel_id=1, source_target_pairs={{0,4},{4,0},{8,12},{12,8},{16,20},{20,16},{24,28},{28,24},{1,5},{5... | collective-permute-start | bytes 1191944 | tf_op jit(solution)/shard_map/ppermute | solution.py:39
  115.0 11.2 %collective-permute-start.21 = (f32[768,128]{1,0:T(8,128)S(1)}, f32[768,128]{1,0:T(8,128)S(1)}, u32[]{:S(2)}, u32[]{:S(2)}) collective-permute-start(f32[768,128]{1,0:T(8,128)S(1)} %constant_dynamic-slice_fusion.7), channel_id=1, source_target_pairs={{0,8},{4,12},{8,0},{12,4},{16,24},{20,28},{24,16},{28,20},{1,9},{5... | collective-permute-start | bytes 1179656 | tf_op jit(solution)/shard_map/ppermute | solution.py:39
  125.7 44.4 %slice-start.1 = ((s8[12582912]{0:T(1024)(128)(4,1)}), s8[4194304]{0:T(1024)(128)(4,1)S(1)}, s32[]{:S(2)}) async-start(s8[12582912]{0:T(1024)(128)(4,1)} %bitcast.48), calls=%async_computation.1 | async-start | bytes 8388608
  125.7 6.5 %collective-permute-start.17 = (f32[392,128]{1,0:T(8,128)S(1)}, f32[392,128]{1,0:T(8,128)S(1)}, u32[]{:S(2)}, u32[]{:S(2)}) collective-permute-start(f32[392,128]{1,0:T(8,128)S(1)} %pad_maximum_fusion.15), channel_id=1, source_target_pairs={{0,8},{4,12},{8,0},{12,4},{16,24},{20,28},{24,16},{28,20},{1,9},{5... | collective-permute-start | bytes 602120 | tf_op jit(solution)/shard_map/ppermute | solution.py:39
  126.4 9.3 %collective-permute-start.22 = (f32[384,128]{1,0:T(8,128)S(1)}, f32[384,128]{1,0:T(8,128)S(1)}, u32[]{:S(2)}, u32[]{:S(2)}) collective-permute-start(f32[384,128]{1,0:T(8,128)S(1)} %constant_dynamic-slice_fusion.6), channel_id=1, source_target_pairs={{0,4},{4,0},{8,12},{12,8},{16,20},{20,16},{24,28},{28,24},{1,5},{5... | collective-permute-start | bytes 589832 | tf_op jit(solution)/shard_map/ppermute | solution.py:39
  132.3 21.0 %collective-permute-start.18 = (f32[392,128]{1,0:T(8,128)S(1)}, f32[392,128]{1,0:T(8,128)S(1)}, u32[]{:S(2)}, u32[]{:S(2)}) collective-permute-start(f32[392,128]{1,0:T(8,128)S(1)} %pad_maximum_fusion.16), channel_id=1, source_target_pairs={{0,16},{4,20},{8,24},{12,28},{16,0},{20,4},{24,8},{28,12},{1,17},{... | collective-permute-start | bytes 602120 | tf_op jit(solution)/shard_map/ppermute | solution.py:39
  135.7 16.5 %collective-permute-start.23 = (f32[384,128]{1,0:T(8,128)S(1)}, f32[384,128]{1,0:T(8,128)S(1)}, u32[]{:S(2)}, u32[]{:S(2)}) collective-permute-start(f32[384,128]{1,0:T(8,128)S(1)} %dynamic-slice_add_fusion.6), channel_id=1, source_target_pairs={{0,16},{4,20},{8,24},{12,28},{16,0},{20,4},{24,8},{28,12},{1,17},{... | collective-permute-start | bytes 589832 | tf_op jit(solution)/shard_map/ppermute | solution.py:39
  152.2 6.9 %collective-permute-start.24 = (f32[384,128]{1,0:T(8,128)S(1)}, f32[384,128]{1,0:T(8,128)S(1)}, u32[]{:S(2)}, u32[]{:S(2)}) collective-permute-start(f32[384,128]{1,0:T(8,128)S(1)} %add.266), channel_id=1, source_target_pairs={{0,4},{4,0},{8,12},{12,8},{16,20},{20,16},{24,28},{28,24},{1,5},{5... | collective-permute-start | bytes 589832 | tf_op jit(solution)/shard_map/ppermute | solution.py:39
  153.3 6.5 %collective-permute-start.19 = (f32[384,128]{1,0:T(8,128)S(1)}, f32[384,128]{1,0:T(8,128)S(1)}, u32[]{:S(2)}, u32[]{:S(2)}) collective-permute-start(f32[384,128]{1,0:T(8,128)S(1)} %slice_add_fusion.9), channel_id=1, source_target_pairs={{0,8},{4,12},{8,0},{12,4},{16,24},{20,28},{24,16},{28,20},{1,9},{5... | collective-permute-start | bytes 589832 | tf_op jit(solution)/shard_map/ppermute | solution.py:39
  159.2 10.3 %collective-permute-start.25 = (f32[768,128]{1,0:T(8,128)S(1)}, f32[768,128]{1,0:T(8,128)S(1)}, u32[]{:S(2)}, u32[]{:S(2)}) collective-permute-start(f32[768,128]{1,0:T(8,128)S(1)} %pad_maximum_fusion.6), channel_id=1, source_target_pairs={{0,8},{4,12},{8,0},{12,4},{16,24},{20,28},{24,16},{28,20},{1,9},{5... | collective-permute-start | bytes 1179656 | tf_op jit(solution)/shard_map/ppermute | solution.py:39
  159.8 9.8 %collective-permute-start.20 = (f32[768,128]{1,0:T(8,128)S(1)}, f32[768,128]{1,0:T(8,128)S(1)}, u32[]{:S(2)}, u32[]{:S(2)}) collective-permute-start(f32[768,128]{1,0:T(8,128)S(1)} %pad_maximum_fusion.5), channel_id=1, source_target_pairs={{0,4},{4,0},{8,12},{12,8},{16,20},{20,16},{24,28},{28,24},{1,5},{5... | collective-permute-start | bytes 1179656 | tf_op jit(solution)/shard_map/ppermute | solution.py:39
  161.1 9.0 %slice-start.2 = ((s8[12582912]{0:T(1024)(128)(4,1)}), s8[4194304]{0:T(1024)(128)(4,1)S(1)}, s32[]{:S(2)}) async-start(s8[12582912]{0:T(1024)(128)(4,1)} %bitcast.48), calls=%async_computation.2 | async-start | bytes 8388608
  173.7 1.6 collective-permute-start.26
  173.8 3.1 %collective-permute-start.29 = (f32[512,128]{1,0:T(8,128)S(1)}, f32[512,128]{1,0:T(8,128)S(1)}, u32[]{:S(2)}, u32[]{:S(2)}) collective-permute-start(f32[512,128]{1,0:T(8,128)S(1)} %constant_dynamic-slice_fusion.4), channel_id=1, source_target_pairs={{0,1},{1,0},{2,3},{3,2},{4,5},{5,4},{6,7},{7,6},{8,9},{9,8},{10,11... | collective-permute-start | bytes 786440 | tf_op jit(solution)/shard_map/ppermute | solution.py:39
  175.4 14.2 %collective-permute-start.27 = (f32[520,128]{1,0:T(8,128)S(1)}, f32[520,128]{1,0:T(8,128)S(1)}, u32[]{:S(2)}, u32[]{:S(2)}) collective-permute-start(f32[520,128]{1,0:T(8,128)S(1)} %pad_maximum_fusion.12), channel_id=1, source_target_pairs={{0,2},{1,3},{2,0},{3,1},{4,6},{5,7},{6,4},{7,5},{8,10},{9,11},{10,... | collective-permute-start | bytes 798728 | tf_op jit(solution)/shard_map/ppermute | solution.py:39
  177.0 12.5 %collective-permute-start.30 = (f32[512,128]{1,0:T(8,128)S(1)}, f32[512,128]{1,0:T(8,128)S(1)}, u32[]{:S(2)}, u32[]{:S(2)}) collective-permute-start(f32[512,128]{1,0:T(8,128)S(1)} %dynamic-slice_add_fusion.3), channel_id=1, source_target_pairs={{0,2},{1,3},{2,0},{3,1},{4,6},{5,7},{6,4},{7,5},{8,10},{9,11},{10,... | collective-permute-start | bytes 786440 | tf_op jit(solution)/shard_map/ppermute | solution.py:39
  189.5 1.6 collective-permute-start.31
  189.7 1.8 collective-permute-start.28
  196.1 11.4 %collective-permute-start.32 = (f32[776,128]{1,0:T(8,128)S(1)}, f32[776,128]{1,0:T(8,128)S(1)}, u32[]{:S(2)}, u32[]{:S(2)}) collective-permute-start(f32[776,128]{1,0:T(8,128)S(1)} %pad_maximum_fusion.2), channel_id=1, source_target_pairs={{0,4},{4,0},{8,12},{12,8},{16,20},{20,16},{24,28},{28,24},{1,5},{5... | collective-permute-start | bytes 1191944 | tf_op jit(solution)/shard_map/ppermute | solution.py:39
  197.6 11.9 %collective-permute-start.37 = (f32[768,128]{1,0:T(8,128)S(1)}, f32[768,128]{1,0:T(8,128)S(1)}, u32[]{:S(2)}, u32[]{:S(2)}) collective-permute-start(f32[768,128]{1,0:T(8,128)S(1)} %constant_dynamic-slice_fusion.1), channel_id=1, source_target_pairs={{0,8},{4,12},{8,0},{12,4},{16,24},{20,28},{24,16},{28,20},{1,9},{5... | collective-permute-start | bytes 1179656 | tf_op jit(solution)/shard_map/ppermute | solution.py:39
  207.7 6.4 %collective-permute-start.33 = (f32[392,128]{1,0:T(8,128)S(1)}, f32[392,128]{1,0:T(8,128)S(1)}, u32[]{:S(2)}, u32[]{:S(2)}) collective-permute-start(f32[392,128]{1,0:T(8,128)S(1)} %pad_maximum_fusion.17), channel_id=1, source_target_pairs={{0,8},{4,12},{8,0},{12,4},{16,24},{20,28},{24,16},{28,20},{1,9},{5... | collective-permute-start | bytes 602120 | tf_op jit(solution)/shard_map/ppermute | solution.py:39
  209.5 6.0 %collective-permute-start.38 = (f32[384,128]{1,0:T(8,128)S(1)}, f32[384,128]{1,0:T(8,128)S(1)}, u32[]{:S(2)}, u32[]{:S(2)}) collective-permute-start(f32[384,128]{1,0:T(8,128)S(1)} %constant_dynamic-slice_fusion), channel_id=1, source_target_pairs={{0,4},{4,0},{8,12},{12,8},{16,20},{20,16},{24,28},{28,24},{1,5},{5... | collective-permute-start | bytes 589832 | tf_op jit(solution)/shard_map/ppermute | solution.py:39
  214.1 20.5 %collective-permute-start.34 = (f32[392,128]{1,0:T(8,128)S(1)}, f32[392,128]{1,0:T(8,128)S(1)}, u32[]{:S(2)}, u32[]{:S(2)}) collective-permute-start(f32[392,128]{1,0:T(8,128)S(1)} %pad_maximum_fusion.18), channel_id=1, source_target_pairs={{0,16},{4,20},{8,24},{12,28},{16,0},{20,4},{24,8},{28,12},{1,17},{... | collective-permute-start | bytes 602120 | tf_op jit(solution)/shard_map/ppermute | solution.py:39
  215.6 17.6 %collective-permute-start.39 = (f32[384,128]{1,0:T(8,128)S(1)}, f32[384,128]{1,0:T(8,128)S(1)}, u32[]{:S(2)}, u32[]{:S(2)}) collective-permute-start(f32[384,128]{1,0:T(8,128)S(1)} %dynamic-slice_add_fusion.5), channel_id=1, source_target_pairs={{0,16},{4,20},{8,24},{12,28},{16,0},{20,4},{24,8},{28,12},{1,17},{... | collective-permute-start | bytes 589832 | tf_op jit(solution)/shard_map/ppermute | solution.py:39
  233.2 6.0 %collective-permute-start.40 = (f32[384,128]{1,0:T(8,128)S(1)}, f32[384,128]{1,0:T(8,128)S(1)}, u32[]{:S(2)}, u32[]{:S(2)}) collective-permute-start(f32[384,128]{1,0:T(8,128)S(1)} %add.285), channel_id=1, source_target_pairs={{0,4},{4,0},{8,12},{12,8},{16,20},{20,16},{24,28},{28,24},{1,5},{5... | collective-permute-start | bytes 589832 | tf_op jit(solution)/shard_map/ppermute | solution.py:39
  234.7 6.7 %collective-permute-start.35 = (f32[384,128]{1,0:T(8,128)S(1)}, f32[384,128]{1,0:T(8,128)S(1)}, u32[]{:S(2)}, u32[]{:S(2)}) collective-permute-start(f32[384,128]{1,0:T(8,128)S(1)} %slice_add_fusion.7), channel_id=1, source_target_pairs={{0,8},{4,12},{8,0},{12,4},{16,24},{20,28},{24,16},{28,20},{1,9},{5... | collective-permute-start | bytes 589832 | tf_op jit(solution)/shard_map/ppermute | solution.py:39
  239.3 10.0 %collective-permute-start.41 = (f32[768,128]{1,0:T(8,128)S(1)}, f32[768,128]{1,0:T(8,128)S(1)}, u32[]{:S(2)}, u32[]{:S(2)}) collective-permute-start(f32[768,128]{1,0:T(8,128)S(1)} %pad_maximum_fusion.8), channel_id=1, source_target_pairs={{0,8},{4,12},{8,0},{12,4},{16,24},{20,28},{24,16},{28,20},{1,9},{5... | collective-permute-start | bytes 1179656 | tf_op jit(solution)/shard_map/ppermute | solution.py:39
  241.5 8.8 %collective-permute-start.36 = (f32[768,128]{1,0:T(8,128)S(1)}, f32[768,128]{1,0:T(8,128)S(1)}, u32[]{:S(2)}, u32[]{:S(2)}) collective-permute-start(f32[768,128]{1,0:T(8,128)S(1)} %pad_maximum_fusion.7), channel_id=1, source_target_pairs={{0,4},{4,0},{8,12},{12,8},{16,20},{20,16},{24,28},{28,24},{1,5},{5... | collective-permute-start | bytes 1179656 | tf_op jit(solution)/shard_map/ppermute | solution.py:39

commit v2 on v0

v2 whole, which is shorter than its diff:
```python
import jax
import jax.numpy as jnp
from jax import lax
from jax.experimental import pallas as pl
from jax.experimental.pallas import tpu as pltpu
from jax.sharding import PartitionSpec as P

CB_DEV = 24
ITERS = 2
TILE = 128
ROW_STREAMS = ((8, False), (8, True), (8, False))
COL_STREAMS = (8, 8)

tiny_eps = 1e-06


def fill_kernel(slot_ref, flip_ref, tile_ref, *out_refs):
    block = pl.program_id(0) ^ flip_ref[0]
    position = 0
    for out_ref in out_refs:
        for place in range(out_ref.shape[1] // TILE):
            slot = slot_ref[block * CB_DEV + position]
            lanes = slice(place * TILE, (place + 1) * TILE)

            @pl.when(slot >= 0)
            def _():
                out_ref[:, lanes] = tile_ref[0, jnp.maximum(slot, 0)]

            @pl.when(slot < 0)
            def _():
                out_ref[:, lanes] = jnp.zeros((TILE, TILE), out_ref.dtype)

            position += 1


def fill_dense(kernel, slots, flip, widths):
    row_blocks, slot_count = kernel.shape[:2]
    return pl.pallas_call(
        fill_kernel,
        grid_spec=pltpu.PrefetchScalarGridSpec(
            num_scalar_prefetch=2,
            grid=(row_blocks,),
            in_specs=[
                pl.BlockSpec(
                    (1, slot_count, TILE, TILE), lambda i, slots, flip: (i ^ flip[0], 0, 0, 0)
                )
            ],
            out_specs=[
                pl.BlockSpec((TILE, width * TILE), lambda i, slots, flip: (i, 0))
                for width in widths
            ],
        ),
        out_shape=[
            jax.ShapeDtypeStruct((row_blocks * TILE, width * TILE), kernel.dtype)
            for width in widths
        ],
        compiler_params=pltpu.CompilerParams(vmem_limit_bytes=16 * 1024 * 1024),
    )(slots, flip, kernel)


def swap(value, axis, count, bit):
    return lax.ppermute(value, axis, [(i, i ^ (1 << bit)) for i in range(count)])


def swap_with(value, extra, axis, count, bit):
    got = swap(jnp.concatenate([value, extra]), axis, count, bit)
    return got[: value.shape[0]], got[value.shape[0] :]


def after(value, other):
    return lax.optimization_barrier((value, other))[0]


def column_norm(pieces):
    sums = []
    for piece in pieces:
        blocks = piece.reshape(-1, TILE, piece.shape[-1])
        sums.append(jnp.sum(blocks * blocks, axis=1))
    sums = jnp.concatenate(sums)
    parts = [sums[i] for i in range(sums.shape[0])]
    while len(parts) > 1:
        paired = [parts[i] + parts[i + 1] for i in range(0, len(parts) - 1, 2)]
        parts = paired + parts[len(parts) - len(parts) % 2 :]
    return parts[0]


def on_device(row_count, col_count, kernel, pattern, counts, delays):
    width = delays.shape[1]
    row_blocks, slot_count = pattern.shape
    row_bits = list(range(row_count.bit_length() - 1))
    col_bits = list(range(col_count.bit_length() - 1))
    row_index = lax.axis_index("rows")
    col_index = lax.axis_index("cols")

    def side(index, bit):
        return (index >> bit) & 1

    orders = [
        [row_bits[1], row_bits[0], *row_bits[2:]] if turned else row_bits
        for _, turned in ROW_STREAMS
    ]

    position_of = []
    start = 0
    for (blocks, _), order in zip(ROW_STREAMS, orders):
        mask = (1 - side(row_index, order[0])) * (blocks // 2) + (
            1 - side(row_index, order[1])
        ) * (blocks // 4)
        quarter = jnp.arange(blocks) // (blocks // 4)
        rest = jnp.arange(blocks) % (blocks // 4)
        quarter_mask = (1 - side(row_index, order[0])) * 2 + (1 - side(row_index, order[1]))
        position_of.append(start + (quarter ^ quarter_mask) * (blocks // 4) + rest)
        start += blocks
    block_at = jnp.concatenate(position_of)
    flip = (1 - side(col_index, 0)) * (COL_STREAMS[0] // 2)

    alive = jnp.arange(slot_count)[None, :] < counts
    hits = (pattern[:, :, None] == block_at[None, None, :]) & alive[:, :, None]
    slots = jnp.sum(hits * (jnp.arange(slot_count) + 1)[None, :, None], axis=1) - 1
    widths = [half for blocks, _ in ROW_STREAMS for half in (blocks // 2, blocks // 2)]
    dense = fill_dense(
        kernel,
        slots.reshape(-1).astype(jnp.int32),
        flip.reshape(1).astype(jnp.int32),
        widths,
    )

    kept_first = side(col_index, 0) == 0
    left_pieces = []
    start = 0
    for blocks in COL_STREAMS:
        half = blocks // 2 * TILE
        low = delays[start : start + half]
        high = delays[start + half : start + 2 * half]
        left_pieces += [jnp.where(kept_first, high, low), jnp.where(kept_first, low, high)]
        start += 2 * half

    def reduce_rows(partials, norm):
        keeps = []
        first_got = []
        for s, order in enumerate(orders):
            send, keep = partials[s]
            if s >= 2:
                send = after(send, first_got[s - 2])
            if s == 1:
                got, other = swap_with(send, norm, "rows", row_count, order[0])
                norm = norm + other
            else:
                got = swap(send, "rows", row_count, order[0])
            first_got.append(got)
            keeps.append(keep + got)
        for level in range(1, len(row_bits)):
            for s, order in enumerate(orders):
                mine = keeps[s]
                if level == 1:
                    half = mine.shape[0] // 2
                    send, mine = mine[:half], mine[half:]
                else:
                    send = mine
                if s == 1:
                    got, other = swap_with(send, norm, "rows", row_count, order[level])
                    norm = norm + other
                else:
                    got = swap(send, "rows", row_count, order[level])
                keeps[s] = mine + got
        pieces = []
        for s, order in enumerate(orders):
            inner = swap(keeps[s], "rows", row_count, order[1])
            own = jnp.concatenate([inner, keeps[s]])
            outer = swap(own, "rows", row_count, order[0])
            pieces += [outer, own]
        return pieces, norm[0]

    def reduce_cols(partials, norm):
        keeps = []
        for s in range(len(COL_STREAMS)):
            send, keep = partials[2 * s], partials[2 * s + 1]
            if s == 0:
                got, other = swap_with(send, norm, "cols", col_count, 0)
                norm = norm + other
            else:
                got = swap(send, "cols", col_count, 0)
            keeps.append(keep + got)
        for bit in col_bits[1:]:
            for s in range(len(COL_STREAMS)):
                if s == 0:
                    got, other = swap_with(keeps[s], norm, "cols", col_count, bit)
                    norm = norm + other
                else:
                    got = swap(keeps[s], "cols", col_count, bit)
                keeps[s] = keeps[s] + got
        pieces = []
        for s in range(len(COL_STREAMS)):
            pieces += [swap(keeps[s], "cols", col_count, 0), keeps[s]]
        return pieces, norm[0]

    def spread(norm):
        return jnp.broadcast_to(norm[None, :], (8, width))

    def back_step(left_raw, right_prev):
        left_bf = jnp.concatenate([piece.astype(jnp.bfloat16) for piece in left_raw])
        products = [
            lax.dot_general(
                chunk, left_bf, (((0,), (0,)), ((), ())), preferred_element_type=jnp.float32
            )
            for chunk in dense
        ]
        partials = list(zip(products[0::2], products[1::2]))
        summed, squares = reduce_rows(partials, spread(column_norm(left_raw)))
        beta_norm = jnp.sqrt(squares + tiny_eps)
        right_raw = [
            total / beta_norm - beta_norm * prev for total, prev in zip(summed, right_prev)
        ]
        return (beta_norm, [piece / beta_norm for piece in left_raw], right_raw)

    def fore_products(right_raw):
        totals = None
        for chunk, piece in zip(dense, right_raw):
            part = jnp.dot(chunk, piece.astype(jnp.bfloat16), preferred_element_type=jnp.float32)
            totals = part if totals is None else totals + part
        pieces = []
        start = 0
        for blocks in COL_STREAMS:
            half = blocks // 2 * TILE
            pieces += [totals[start : start + half], totals[start + half : start + 2 * half]]
            start += 2 * half
        return pieces

    right_zero = [jnp.zeros((chunk.shape[1], width), jnp.float32) for chunk in dense]
    beta_first, left_vec, right_raw = back_step(left_pieces, right_zero)
    resid_bar = beta_first
    model = right_zero
    search = right_zero
    diag_bar = beta_first
    rotate_cos = beta_first
    rotate_sin = beta_first
    radius = beta_first
    for iteration in range(ITERS):
        fore_summed, fore_squares = reduce_cols(
            fore_products(right_raw), spread(column_norm(right_raw))
        )
        alpha_norm = jnp.sqrt(fore_squares + tiny_eps)
        left_raw = [
            total / alpha_norm - alpha_norm * prev for total, prev in zip(fore_summed, left_vec)
        ]
        right_vec = [piece / alpha_norm for piece in right_raw]
        if iteration == 0:
            diag_bar = alpha_norm
            search = right_vec
        else:
            coupling = rotate_sin * alpha_norm
            diag_bar = -rotate_cos * alpha_norm
            search = [now - coupling / radius * old for now, old in zip(right_vec, search)]
        beta_norm, left_vec, right_raw = back_step(left_raw, right_vec)
        radius = jnp.sqrt(diag_bar * diag_bar + beta_norm * beta_norm)
        rotate_cos = diag_bar / radius
        rotate_sin = beta_norm / radius
        step_size = rotate_cos * resid_bar
        resid_bar = rotate_sin * resid_bar
        model = [old + step_size / radius * way for old, way in zip(model, search)]
    misfit = resid_bar / beta_first
    gradient = [misfit * rotate_cos * piece for piece in right_raw]

    def in_block_order(pieces):
        out = []
        for s, order in enumerate(orders):
            outer, own = pieces[2 * s], pieces[2 * s + 1]
            half = outer.shape[0] // 2
            straight = side(row_index, order[1]) == 1
            outer, own = (
                jnp.where(straight, v, jnp.concatenate([v[half:], v[:half]]))
                for v in (outer, own)
            )
            straight = side(row_index, order[0]) == 1
            out += [jnp.where(straight, outer, own), jnp.where(straight, own, outer)]
        return jnp.concatenate(out)

    return (in_block_order(model), in_block_order(gradient), misfit)


def solution(mesh):
    placed = (P("rows", "cols", None, None), P("rows", "cols"), P("rows", "cols"), P("rows", None))

    def local(kernel, pattern, counts, delays):
        return on_device(
            mesh.shape["rows"], mesh.shape["cols"], kernel, pattern, counts, delays
        )

    return jax.shard_map(
        local,
        mesh=mesh,
        in_specs=placed,
        out_specs=(P("cols", None), P("cols", None), P()),
        check_vma=False,
    )
```

time: 424 us -> 232 us (0.55)
  waiting for transfers between devices: 259 us -> 117 us
  blocking collectives: 81.9 us -> 0 us
  starting transfers between devices: 0.21 us -> 61.9 us
  matrix products: 51.5 us -> 22.6 us
  between operations: 13.8 us -> 1.93 us
  Pallas kernels: 0 us -> 6.65 us
    psum x5 -> x0, waiting for transfers between devices: 259 us -> none  [the longest x3 203 us: back_step(): summed = lax.psum(partial_sum, 'rows')]
    ppermute x0 -> x57, waiting for transfers between devices: none -> 117 us  [swap(): return lax.ppermute(value, axis, [(i, i ^ 1 << bit) for i in range(count)])]
    psum x5 -> x0, blocking collectives: 81.9 us -> none  [the longest x3 67.8 us: back_step(): squares = lax.psum(column_norm(left_raw), 'rows')]
    ppermute x0 -> x57, starting transfers between devices: none -> 61.9 us  [swap(): return lax.ppermute(value, axis, [(i, i ^ 1 << bit) for i in range(count)])]
    dot_general x6 -> x30, matrix products: 51.5 us -> 22.6 us  [the longest x18 14 us: back_step(): lax.dot_general(chunk, left_bf, (((0,), (0,)), ((), ())), preferred_eleme...]
    pallas_call x0 -> x1, Pallas kernels: none -> 6.65 us  [fill_dense(): pl.pallas_call(fill_kernel, grid_spec=pltpu.PrefetchScalarGridSpec(num_sc...]
  transfers between devices with their start and end apart: 5 -> 57, of which waited for: 5 -> 40; matrix products, arithmetic and copies ran while one was open for 0% -> 10% of each run, Pallas kernels for 0% -> 0%
where the time goes in v2:
time: 232 us; the launch traced here: 231 us
  waiting for transfers between devices  117 us (50%)
  starting transfers between devices  61.9 us (27%)
  matrix products  22.6 us (10%)
  other arithmetic  13.9 us (6%)
  local copies, waits for them, and re-layouts  7.05 us (3%)
  Pallas kernels  6.65 us (3%)
    ppermute x57, waiting for transfers between devices, swap(): return lax.ppermute(value, axis, [(i, i ^ 1 << bit) for i in range(count)])  117 us
    ppermute x57, starting transfers between devices, swap(): return lax.ppermute(value, axis, [(i, i ^ 1 << bit) for i in range(count)])  61.9 us
    dot_general x18, matrix products, back_step(): lax.dot_general(chunk, left_bf, (((0,), (0,)), ((), ())), preferred_eleme...  14 us
    dot_general x12, matrix products, fore_products(): jnp.dot(chunk, piece.astype(jnp.bfloat16), preferred_element_type=jnp.flo...  8.63 us
    pallas_call x1, Pallas kernels, fill_dense(): pl.pallas_call(fill_kernel, grid_spec=pltpu.PrefetchScalarGridSpec(num_sc...  6.65 us
    unnamed x70, local copies, waits for them, and re-layouts  6.56 us
  transfers between devices with their start and end apart: 57, of which 40 were waited for; matrix products, arithmetic and copies ran while one was open for 10% of the time, Pallas kernels for 0%

profile of v2, /device:TPU:0, one launch (start us, length us, event | category | flops | bytes accessed | tf_op | source)
XLA Modules:
  0.0 230.9 jit_solution(14376909404662362768)
XLA Ops:
  2.5 1.3 fusion.66
  3.8 3.4 %copy-done = bf16[16,16,128,128]{3,2,1,0:T(8,128)(2,1)S(1)} copy-done((bf16[16,16,128,128]{3,2,1,0:T(8,128)(2,1)S(1)}, bf16[16,16,128,128]{3,2,1,0:T(8,128)(2,1)}, u32[]{:S(2)}) %copy-start) | copy-done | bytes 8388632
  7.2 6.7 %shard_map.70 = (bf16[2048,512]{1,0:T(8,128)(2,1)S(1)}, bf16[2048,512]{1,0:T(8,128)(2,1)S(1)}, bf16[2048,512]{1,0:T(8,128)(2,1)S(1)}, bf16[2048,512]{1,0:T(8,128...) custom-call(s32[384]{0:T(512)S(1)} %sub.148.slot_ref, s32[1]{0:T(128)} %bitcast.1.flip_ref, ...), custom_call_target="tpu_custom_call" | custom-call | tf_op jit(solution)/shard_map/pallas_call | solution.py:38
  14.6 2.8 %collective-permute-start = (f32[512,128]{1,0:T(8,128)S(1)}, f32[512,128]{1,0:T(8,128)S(1)}, u32[]{:S(2)}, u32[]{:S(2)}) collective-permute-start(f32[512,128]{1,0:T(8,128)S(1)} %fusion.54), channel_id=1, source_target_pairs={{0,4},{4,0},{8,12},{12,8},{16,20},{20,16},{24,28},{28,24},{1,5},{5... | collective-permute-start | bytes 786440 | tf_op jit(solution)/shard_map/ppermute | solution.py:62
  18.4 1.6 collective-permute-start.5
  20.8 2.9 %collective-permute-done = f32[512,128]{1,0:T(8,128)S(1)} collective-permute-done((f32[512,128]{1,0:T(8,128)S(1)}, f32[512,128]{1,0:T(8,128)S(1)}, u32[]{:S(2)}, u32[]{:S(2)}) %collective-permute-start) | collective-permute-done | bytes 262176 | tf_op jit(solution)/shard_map/ppermute | solution.py:62
  24.5 2.0 collective-permute-start.1
  26.5 1.4 collective-permute-start.10
  29.5 2.9 %collective-permute-start.2 = (f32[256,128]{1,0:T(8,128)S(1)}, f32[256,128]{1,0:T(8,128)S(1)}, u32[]{:S(2)}, u32[]{:S(2)}) collective-permute-start(f32[256,128]{1,0:T(8,128)S(1)} %slice_add_fusion.20), channel_id=1, source_target_pairs={{0,16},{4,20},{8,24},{12,28},{16,0},{20,4},{24,8},{28,12},{1,17},{... | collective-permute-start | bytes 393224 | tf_op jit(solution)/shard_map/ppermute | solution.py:62
  32.4 3.8 %collective-permute-done.6 = f32[264,128]{1,0:T(8,128)S(1)} collective-permute-done((f32[264,128]{1,0:T(8,128)S(1)}, f32[264,128]{1,0:T(8,128)S(1)}, u32[]{:S(2)}, u32[]{:S(2)}) %collective-permute-start.6) | collective-permute-done | bytes 135200 | tf_op jit(solution)/shard_map/ppermute | solution.py:62
  36.3 2.8 %collective-permute-start.7 = (f32[264,128]{1,0:T(8,128)S(1)}, f32[264,128]{1,0:T(8,128)S(1)}, u32[]{:S(2)}, u32[]{:S(2)}) collective-permute-start(f32[264,128]{1,0:T(8,128)S(1)} %pad_maximum_fusion.20), channel_id=1, source_target_pairs={{0,16},{4,20},{8,24},{12,28},{16,0},{20,4},{24,8},{28,12},{1,17},{... | collective-permute-start | bytes 405512 | tf_op jit(solution)/shard_map/ppermute | solution.py:62
  40.4 1.7 collective-permute-start.11
  42.1 1.6 collective-permute-done.7
  43.7 1.6 collective-permute-start.8
  46.2 1.3 collective-permute-start.4
  50.8 4.2 %collective-permute-done.12 = f32[256,128]{1,0:T(8,128)S(1)} collective-permute-done((f32[256,128]{1,0:T(8,128)S(1)}, f32[256,128]{1,0:T(8,128)S(1)}, u32[]{:S(2)}, u32[]{:S(2)}) %collective-permute-start.12) | collective-permute-done | bytes 131104 | tf_op jit(solution)/shard_map/ppermute | solution.py:62
  56.1 4.8 %collective-permute-done.13 = f32[256,128]{1,0:T(8,128)S(1)} collective-permute-done((f32[256,128]{1,0:T(8,128)S(1)}, f32[256,128]{1,0:T(8,128)S(1)}, u32[]{:S(2)}, u32[]{:S(2)}) %collective-permute-start.13) | collective-permute-done | bytes 131104 | tf_op jit(solution)/shard_map/ppermute | solution.py:62
  60.9 1.3 collective-permute-start.14
  64.5 2.9 %collective-permute-done.14 = f32[512,128]{1,0:T(8,128)S(1)} collective-permute-done((f32[512,128]{1,0:T(8,128)S(1)}, f32[512,128]{1,0:T(8,128)S(1)}, u32[]{:S(2)}, u32[]{:S(2)}) %collective-permute-start.14) | collective-permute-done | bytes 262176 | tf_op jit(solution)/shard_map/ppermute | solution.py:62
  70.6 1.9 collective-permute-start.16
  72.7 7.2 %collective-permute-done.16 = f32[520,128]{1,0:T(8,128)S(1)} collective-permute-done((f32[520,128]{1,0:T(8,128)S(1)}, f32[520,128]{1,0:T(8,128)S(1)}, u32[]{:S(2)}, u32[]{:S(2)}) %collective-permute-start.16) | collective-permute-done | bytes 266272 | tf_op jit(solution)/shard_map/ppermute | solution.py:62
  79.9 4.9 %collective-permute-done.19 = f32[512,128]{1,0:T(8,128)S(1)} collective-permute-done((f32[512,128]{1,0:T(8,128)S(1)}, f32[512,128]{1,0:T(8,128)S(1)}, u32[]{:S(2)}, u32[]{:S(2)}) %collective-permute-start.19) | collective-permute-done | bytes 262176 | tf_op jit(solution)/shard_map/ppermute | solution.py:62
  91.2 6.0 %collective-permute-done.24 = f32[512,128]{1,0:T(8,128)S(1)} collective-permute-done((f32[512,128]{1,0:T(8,128)S(1)}, f32[512,128]{1,0:T(8,128)S(1)}, u32[]{:S(2)}, u32[]{:S(2)}) %collective-permute-start.24) | collective-permute-done | bytes 262176 | tf_op jit(solution)/shard_map/ppermute | solution.py:62
  101.4 1.7 collective-permute-done.25
  103.1 1.6 collective-permute-start.26
  104.7 3.9 %collective-permute-done.22 = f32[264,128]{1,0:T(8,128)S(1)} collective-permute-done((f32[264,128]{1,0:T(8,128)S(1)}, f32[264,128]{1,0:T(8,128)S(1)}, u32[]{:S(2)}, u32[]{:S(2)}) %collective-permute-start.22) | collective-permute-done | bytes 135200 | tf_op jit(solution)/shard_map/ppermute | solution.py:62
  108.7 3.1 %collective-permute-start.23 = (f32[264,128]{1,0:T(8,128)S(1)}, f32[264,128]{1,0:T(8,128)S(1)}, u32[]{:S(2)}, u32[]{:S(2)}) collective-permute-start(f32[264,128]{1,0:T(8,128)S(1)} %pad_maximum_fusion.22), channel_id=1, source_target_pairs={{0,16},{4,20},{8,24},{12,28},{16,0},{20,4},{24,8},{28,12},{1,17},{... | collective-permute-start | bytes 405512 | tf_op jit(solution)/shard_map/ppermute | solution.py:62
  113.0 1.7 collective-permute-start.27
  116.6 2.5 %collective-permute-done.32 = f32[256,128]{1,0:T(8,128)S(1)} collective-permute-done((f32[256,128]{1,0:T(8,128)S(1)}, f32[256,128]{1,0:T(8,128)S(1)}, u32[]{:S(2)}, u32[]{:S(2)}) %collective-permute-start.32) | collective-permute-done | bytes 131104 | tf_op jit(solution)/shard_map/ppermute | solution.py:62
  121.7 3.8 %collective-permute-start.30 = (f32[512,128]{1,0:T(8,128)S(1)}, f32[512,128]{1,0:T(8,128)S(1)}, u32[]{:S(2)}, u32[]{:S(2)}) collective-permute-start(f32[512,128]{1,0:T(8,128)S(1)} %get-tuple-element.136), channel_id=1, source_target_pairs={{0,8},{4,12},{8,0},{12,4},{16,24},{20,28},{24,16},{28,20},{1,9},{5... | collective-permute-start | bytes 786440 | tf_op jit(solution)/shard_map/ppermute | solution.py:62
  127.8 4.6 %collective-permute-done.34 = f32[256,128]{1,0:T(8,128)S(1)} collective-permute-done((f32[256,128]{1,0:T(8,128)S(1)}, f32[256,128]{1,0:T(8,128)S(1)}, u32[]{:S(2)}, u32[]{:S(2)}) %collective-permute-start.34) | collective-permute-done | bytes 131104 | tf_op jit(solution)/shard_map/ppermute | solution.py:62
  132.5 1.4 collective-permute-start.35
  134.9 4.0 %collective-permute-done.35 = f32[512,128]{1,0:T(8,128)S(1)} collective-permute-done((f32[512,128]{1,0:T(8,128)S(1)}, f32[512,128]{1,0:T(8,128)S(1)}, u32[]{:S(2)}, u32[]{:S(2)}) %collective-permute-start.35) | collective-permute-done | bytes 262176 | tf_op jit(solution)/shard_map/ppermute | solution.py:62
  143.6 1.9 collective-permute-start.37
  145.7 7.2 %collective-permute-done.37 = f32[520,128]{1,0:T(8,128)S(1)} collective-permute-done((f32[520,128]{1,0:T(8,128)S(1)}, f32[520,128]{1,0:T(8,128)S(1)}, u32[]{:S(2)}, u32[]{:S(2)}) %collective-permute-start.37) | collective-permute-done | bytes 266272 | tf_op jit(solution)/shard_map/ppermute | solution.py:62
  153.5 4.4 %collective-permute-done.40 = f32[512,128]{1,0:T(8,128)S(1)} collective-permute-done((f32[512,128]{1,0:T(8,128)S(1)}, f32[512,128]{1,0:T(8,128)S(1)}, u32[]{:S(2)}, u32[]{:S(2)}) %collective-permute-start.40) | collective-permute-done | bytes 262176 | tf_op jit(solution)/shard_map/ppermute | solution.py:62
  161.5 1.3 fusion.58
  168.2 5.6 %collective-permute-done.45 = f32[512,128]{1,0:T(8,128)S(1)} collective-permute-done((f32[512,128]{1,0:T(8,128)S(1)}, f32[512,128]{1,0:T(8,128)S(1)}, u32[]{:S(2)}, u32[]{:S(2)}) %collective-permute-start.45) | collective-permute-done | bytes 262176 | tf_op jit(solution)/shard_map/ppermute | solution.py:62
  179.6 1.4 collective-permute-start.47
  181.0 4.5 %collective-permute-done.43 = f32[264,128]{1,0:T(8,128)S(1)} collective-permute-done((f32[264,128]{1,0:T(8,128)S(1)}, f32[264,128]{1,0:T(8,128)S(1)}, u32[]{:S(2)}, u32[]{:S(2)}) %collective-permute-start.43) | collective-permute-done | bytes 135200 | tf_op jit(solution)/shard_map/ppermute | solution.py:62
  190.0 2.2 collective-permute-done.44
  193.8 1.6 collective-permute-done.53
  195.5 1.4 collective-permute-start.54
  198.1 4.9 %collective-permute-done.54 = f32[256,128]{1,0:T(8,128)S(1)} collective-permute-done((f32[256,128]{1,0:T(8,128)S(1)}, f32[256,128]{1,0:T(8,128)S(1)}, u32[]{:S(2)}, u32[]{:S(2)}) %collective-permute-start.54) | collective-permute-done | bytes 131104 | tf_op jit(solution)/shard_map/ppermute | solution.py:62
  203.8 4.3 %collective-permute-done.55 = f32[256,128]{1,0:T(8,128)S(1)} collective-permute-done((f32[256,128]{1,0:T(8,128)S(1)}, f32[256,128]{1,0:T(8,128)S(1)}, u32[]{:S(2)}, u32[]{:S(2)}) %collective-permute-start.55) | collective-permute-done | bytes 131104 | tf_op jit(solution)/shard_map/ppermute | solution.py:62
  209.5 5.6 %collective-permute-done.56 = f32[512,128]{1,0:T(8,128)S(1)} collective-permute-done((f32[512,128]{1,0:T(8,128)S(1)}, f32[512,128]{1,0:T(8,128)S(1)}, u32[]{:S(2)}, u32[]{:S(2)}) %collective-permute-start.56) | collective-permute-done | bytes 262176 | tf_op jit(solution)/shard_map/ppermute | solution.py:62
  216.7 5.1 %collective-permute-done.49 = f32[512,128]{1,0:T(8,128)S(1)} collective-permute-done((f32[512,128]{1,0:T(8,128)S(1)}, f32[512,128]{1,0:T(8,128)S(1)}, u32[]{:S(2)}, u32[]{:S(2)}) %collective-permute-start.49) | collective-permute-done | bytes 262176 | tf_op jit(solution)/shard_map/ppermute | solution.py:62
  222.5 6.1 %collective-permute-done.51 = f32[512,128]{1,0:T(8,128)S(1)} collective-permute-done((f32[512,128]{1,0:T(8,128)S(1)}, f32[512,128]{1,0:T(8,128)S(1)}, u32[]{:S(2)}, u32[]{:S(2)}) %collective-permute-start.51) | collective-permute-done | bytes 262176 | tf_op jit(solution)/shard_map/ppermute | solution.py:62
  (304 shorter events, 72.1 us)
Async XLA Ops:
  14.6 9.1 %collective-permute-start = (f32[512,128]{1,0:T(8,128)S(1)}, f32[512,128]{1,0:T(8,128)S(1)}, u32[]{:S(2)}, u32[]{:S(2)}) collective-permute-start(f32[512,128]{1,0:T(8,128)S(1)} %fusion.54), channel_id=1, source_target_pairs={{0,4},{4,0},{8,12},{12,8},{16,20},{20,16},{24,28},{28,24},{1,5},{5... | collective-permute-start | bytes 786440 | tf_op jit(solution)/shard_map/ppermute | solution.py:62
  18.4 9.6 %collective-permute-start.5 = (f32[520,128]{1,0:T(8,128)S(1)}, f32[520,128]{1,0:T(8,128)S(1)}, u32[]{:S(2)}, u32[]{:S(2)}) collective-permute-start(f32[520,128]{1,0:T(8,128)S(1)} %pad_maximum_fusion.3), channel_id=1, source_target_pairs={{0,8},{4,12},{8,0},{12,4},{16,24},{20,28},{24,16},{28,20},{1,9},{5... | collective-permute-start | bytes 798728 | tf_op jit(solution)/shard_map/ppermute | solution.py:62
  24.5 5.0 %collective-permute-start.1 = (f32[256,128]{1,0:T(8,128)S(1)}, f32[256,128]{1,0:T(8,128)S(1)}, u32[]{:S(2)}, u32[]{:S(2)}) collective-permute-start(f32[256,128]{1,0:T(8,128)S(1)} %slice.725), channel_id=1, source_target_pairs={{0,8},{4,12},{8,0},{12,4},{16,24},{20,28},{24,16},{28,20},{1,9},{5... | collective-permute-start | bytes 393224 | tf_op jit(solution)/shard_map/ppermute | solution.py:62
  26.5 13.8 %collective-permute-start.10 = (f32[512,128]{1,0:T(8,128)S(1)}, f32[512,128]{1,0:T(8,128)S(1)}, u32[]{:S(2)}, u32[]{:S(2)}) collective-permute-start(f32[512,128]{1,0:T(8,128)S(1)} %fusion.50), channel_id=1, source_target_pairs={{0,4},{4,0},{8,12},{12,8},{16,20},{20,16},{24,28},{28,24},{1,5},{5... | collective-permute-start | bytes 786440 | tf_op jit(solution)/shard_map/ppermute | solution.py:62
  28.7 7.5 %collective-permute-start.6 = (f32[264,128]{1,0:T(8,128)S(1)}, f32[264,128]{1,0:T(8,128)S(1)}, u32[]{:S(2)}, u32[]{:S(2)}) collective-permute-start(f32[264,128]{1,0:T(8,128)S(1)} %pad_maximum_fusion.19), channel_id=1, source_target_pairs={{0,4},{4,0},{8,12},{12,8},{16,20},{20,16},{24,28},{28,24},{1,5},{5... | collective-permute-start | bytes 405512 | tf_op jit(solution)/shard_map/ppermute | solution.py:62
  29.5 10.3 %collective-permute-start.2 = (f32[256,128]{1,0:T(8,128)S(1)}, f32[256,128]{1,0:T(8,128)S(1)}, u32[]{:S(2)}, u32[]{:S(2)}) collective-permute-start(f32[256,128]{1,0:T(8,128)S(1)} %slice_add_fusion.20), channel_id=1, source_target_pairs={{0,16},{4,20},{8,24},{12,28},{16,0},{20,4},{24,8},{28,12},{1,17},{... | collective-permute-start | bytes 393224 | tf_op jit(solution)/shard_map/ppermute | solution.py:62
  36.3 7.4 %collective-permute-start.7 = (f32[264,128]{1,0:T(8,128)S(1)}, f32[264,128]{1,0:T(8,128)S(1)}, u32[]{:S(2)}, u32[]{:S(2)}) collective-permute-start(f32[264,128]{1,0:T(8,128)S(1)} %pad_maximum_fusion.20), channel_id=1, source_target_pairs={{0,16},{4,20},{8,24},{12,28},{16,0},{20,4},{24,8},{28,12},{1,17},{... | collective-permute-start | bytes 405512 | tf_op jit(solution)/shard_map/ppermute | solution.py:62
  39.9 6.3 %collective-permute-start.3 = (f32[256,128]{1,0:T(8,128)S(1)}, f32[256,128]{1,0:T(8,128)S(1)}, u32[]{:S(2)}, u32[]{:S(2)}) collective-permute-start(f32[256,128]{1,0:T(8,128)S(1)} %add.671), channel_id=1, source_target_pairs={{0,8},{4,12},{8,0},{12,4},{16,24},{20,28},{24,16},{28,20},{1,9},{5... | collective-permute-start | bytes 393224 | tf_op jit(solution)/shard_map/ppermute | solution.py:62
  40.4 7.2 %collective-permute-start.11 = (f32[256,128]{1,0:T(8,128)S(1)}, f32[256,128]{1,0:T(8,128)S(1)}, u32[]{:S(2)}, u32[]{:S(2)}) collective-permute-start(f32[256,128]{1,0:T(8,128)S(1)} %slice.735), channel_id=1, source_target_pairs={{0,8},{4,12},{8,0},{12,4},{16,24},{20,28},{24,16},{28,20},{1,9},{5... | collective-permute-start | bytes 393224 | tf_op jit(solution)/shard_map/ppermute | solution.py:62
  43.7 6.3 %collective-permute-start.8 = (f32[256,128]{1,0:T(8,128)S(1)}, f32[256,128]{1,0:T(8,128)S(1)}, u32[]{:S(2)}, u32[]{:S(2)}) collective-permute-start(f32[256,128]{1,0:T(8,128)S(1)} %slice_add_fusion.18), channel_id=1, source_target_pairs={{0,4},{4,0},{8,12},{12,8},{16,20},{20,16},{24,28},{28,24},{1,5},{5... | collective-permute-start | bytes 393224 | tf_op jit(solution)/shard_map/ppermute | solution.py:62
  46.2 17.5 %collective-permute-start.4 = (f32[512,128]{1,0:T(8,128)S(1)}, f32[512,128]{1,0:T(8,128)S(1)}, u32[]{:S(2)}, u32[]{:S(2)}) collective-permute-start(f32[512,128]{1,0:T(8,128)S(1)} %pad_maximum_fusion.10), channel_id=1, source_target_pairs={{0,4},{4,0},{8,12},{12,8},{16,20},{20,16},{24,28},{28,24},{1,5},{5... | collective-permute-start | bytes 786440 | tf_op jit(solution)/shard_map/ppermute | solution.py:62
  47.6 7.3 %collective-permute-start.12 = (f32[256,128]{1,0:T(8,128)S(1)}, f32[256,128]{1,0:T(8,128)S(1)}, u32[]{:S(2)}, u32[]{:S(2)}) collective-permute-start(f32[256,128]{1,0:T(8,128)S(1)} %slice_add_fusion.17), channel_id=1, source_target_pairs={{0,16},{4,20},{8,24},{12,28},{16,0},{20,4},{24,8},{28,12},{1,17},{... | collective-permute-start | bytes 393224 | tf_op jit(solution)/shard_map/ppermute | solution.py:62
  50.1 12.9 %collective-permute-start.9 = (f32[512,128]{1,0:T(8,128)S(1)}, f32[512,128]{1,0:T(8,128)S(1)}, u32[]{:S(2)}, u32[]{:S(2)}) collective-permute-start(f32[512,128]{1,0:T(8,128)S(1)} %pad_maximum_fusion.11), channel_id=1, source_target_pairs={{0,8},{4,12},{8,0},{12,4},{16,24},{20,28},{24,16},{28,20},{1,9},{5... | collective-permute-start | bytes 786440 | tf_op jit(solution)/shard_map/ppermute | solution.py:62
  55.0 5.9 %collective-permute-start.13 = (f32[256,128]{1,0:T(8,128)S(1)}, f32[256,128]{1,0:T(8,128)S(1)}, u32[]{:S(2)}, u32[]{:S(2)}) collective-permute-start(f32[256,128]{1,0:T(8,128)S(1)} %add.711), channel_id=1, source_target_pairs={{0,8},{4,12},{8,0},{12,4},{16,24},{20,28},{24,16},{28,20},{1,9},{5... | collective-permute-start | bytes 393224 | tf_op jit(solution)/shard_map/ppermute | solution.py:62
  60.9 6.5 %collective-permute-start.14 = (f32[512,128]{1,0:T(8,128)S(1)}, f32[512,128]{1,0:T(8,128)S(1)}, u32[]{:S(2)}, u32[]{:S(2)}) collective-permute-start(f32[512,128]{1,0:T(8,128)S(1)} %pad_maximum_fusion.12), channel_id=1, source_target_pairs={{0,4},{4,0},{8,12},{12,8},{16,20},{20,16},{24,28},{28,24},{1,5},{5... | collective-permute-start | bytes 786440 | tf_op jit(solution)/shard_map/ppermute | solution.py:62
  70.6 9.3 %collective-permute-start.16 = (f32[520,128]{1,0:T(8,128)S(1)}, f32[520,128]{1,0:T(8,128)S(1)}, u32[]{:S(2)}, u32[]{:S(2)}) collective-permute-start(f32[520,128]{1,0:T(8,128)S(1)} %pad_maximum_fusion.5), channel_id=1, source_target_pairs={{0,2},{1,3},{2,0},{3,1},{4,6},{5,7},{6,4},{7,5},{8,10},{9,11},{10,... | collective-permute-start | bytes 798728 | tf_op jit(solution)/shard_map/ppermute | solution.py:62
  72.5 12.3 %collective-permute-start.19 = (f32[512,128]{1,0:T(8,128)S(1)}, f32[512,128]{1,0:T(8,128)S(1)}, u32[]{:S(2)}, u32[]{:S(2)}) collective-permute-start(f32[512,128]{1,0:T(8,128)S(1)} %get-tuple-element.74), channel_id=1, source_target_pairs={{0,2},{1,3},{2,0},{3,1},{4,6},{5,7},{6,4},{7,5},{8,10},{9,11},{10,... | collective-permute-start | bytes 786440 | tf_op jit(solution)/shard_map/ppermute | solution.py:62
  88.8 8.4 %collective-permute-start.24 = (f32[512,128]{1,0:T(8,128)S(1)}, f32[512,128]{1,0:T(8,128)S(1)}, u32[]{:S(2)}, u32[]{:S(2)}) collective-permute-start(f32[512,128]{1,0:T(8,128)S(1)} %fusion.46), channel_id=1, source_target_pairs={{0,4},{4,0},{8,12},{12,8},{16,20},{20,16},{24,28},{28,24},{1,5},{5... | collective-permute-start | bytes 786440 | tf_op jit(solution)/shard_map/ppermute | solution.py:62
  90.2 9.4 %collective-permute-start.21 = (f32[520,128]{1,0:T(8,128)S(1)}, f32[520,128]{1,0:T(8,128)S(1)}, u32[]{:S(2)}, u32[]{:S(2)}) collective-permute-start(f32[520,128]{1,0:T(8,128)S(1)} %pad_maximum_fusion.6), channel_id=1, source_target_pairs={{0,8},{4,12},{8,0},{12,4},{16,24},{20,28},{24,16},{28,20},{1,9},{5... | collective-permute-start | bytes 798728 | tf_op jit(solution)/shard_map/ppermute | solution.py:62
  98.0 5.0 %collective-permute-start.25 = (f32[256,128]{1,0:T(8,128)S(1)}, f32[256,128]{1,0:T(8,128)S(1)}, u32[]{:S(2)}, u32[]{:S(2)}) collective-permute-start(f32[256,128]{1,0:T(8,128)S(1)} %slice.752), channel_id=1, source_target_pairs={{0,8},{4,12},{8,0},{12,4},{16,24},{20,28},{24,16},{28,20},{1,9},{5... | collective-permute-start | bytes 393224 | tf_op jit(solution)/shard_map/ppermute | solution.py:62
  98.4 13.3 %collective-permute-start.31 = (f32[512,128]{1,0:T(8,128)S(1)}, f32[512,128]{1,0:T(8,128)S(1)}, u32[]{:S(2)}, u32[]{:S(2)}) collective-permute-start(f32[512,128]{1,0:T(8,128)S(1)} %fusion.44), channel_id=1, source_target_pairs={{0,4},{4,0},{8,12},{12,8},{16,20},{20,16},{24,28},{28,24},{1,5},{5... | collective-permute-start | bytes 786440 | tf_op jit(solution)/shard_map/ppermute | solution.py:62
  100.4 8.2 %collective-permute-start.22 = (f32[264,128]{1,0:T(8,128)S(1)}, f32[264,128]{1,0:T(8,128)S(1)}, u32[]{:S(2)}, u32[]{:S(2)}) collective-permute-start(f32[264,128]{1,0:T(8,128)S(1)} %pad_maximum_fusion.21), channel_id=1, source_target_pairs={{0,4},{4,0},{8,12},{12,8},{16,20},{20,16},{24,28},{28,24},{1,5},{5... | collective-permute-start | bytes 405512 | tf_op jit(solution)/shard_map/ppermute | solution.py:62
  103.1 9.9 %collective-permute-start.26 = (f32[256,128]{1,0:T(8,128)S(1)}, f32[256,128]{1,0:T(8,128)S(1)}, u32[]{:S(2)}, u32[]{:S(2)}) collective-permute-start(f32[256,128]{1,0:T(8,128)S(1)} %slice_add_fusion.15), channel_id=1, source_target_pairs={{0,16},{4,20},{8,24},{12,28},{16,0},{20,4},{24,8},{28,12},{1,17},{... | collective-permute-start | bytes 393224 | tf_op jit(solution)/shard_map/ppermute | solution.py:62
  108.7 7.1 %collective-permute-start.23 = (f32[264,128]{1,0:T(8,128)S(1)}, f32[264,128]{1,0:T(8,128)S(1)}, u32[]{:S(2)}, u32[]{:S(2)}) collective-permute-start(f32[264,128]{1,0:T(8,128)S(1)} %pad_maximum_fusion.22), channel_id=1, source_target_pairs={{0,16},{4,20},{8,24},{12,28},{16,0},{20,4},{24,8},{28,12},{1,17},{... | collective-permute-start | bytes 405512 | tf_op jit(solution)/shard_map/ppermute | solution.py:62
  112.6 6.5 %collective-permute-start.32 = (f32[256,128]{1,0:T(8,128)S(1)}, f32[256,128]{1,0:T(8,128)S(1)}, u32[]{:S(2)}, u32[]{:S(2)}) collective-permute-start(f32[256,128]{1,0:T(8,128)S(1)} %slice.755), channel_id=1, source_target_pairs={{0,8},{4,12},{8,0},{12,4},{16,24},{20,28},{24,16},{28,20},{1,9},{5... | collective-permute-start | bytes 393224 | tf_op jit(solution)/shard_map/ppermute | solution.py:62
  113.0 7.9 %collective-permute-start.27 = (f32[256,128]{1,0:T(8,128)S(1)}, f32[256,128]{1,0:T(8,128)S(1)}, u32[]{:S(2)}, u32[]{:S(2)}) collective-permute-start(f32[256,128]{1,0:T(8,128)S(1)} %add.756), channel_id=1, source_target_pairs={{0,8},{4,12},{8,0},{12,4},{16,24},{20,28},{24,16},{28,20},{1,9},{5... | collective-permute-start | bytes 393224 | tf_op jit(solution)/shard_map/ppermute | solution.py:62
  115.8 5.2 %collective-permute-start.29 = (f32[256,128]{1,0:T(8,128)S(1)}, f32[256,128]{1,0:T(8,128)S(1)}, u32[]{:S(2)}, u32[]{:S(2)}) collective-permute-start(f32[256,128]{1,0:T(8,128)S(1)} %slice_add_fusion.14), channel_id=1, source_target_pairs={{0,4},{4,0},{8,12},{12,8},{16,20},{20,16},{24,28},{28,24},{1,5},{5... | collective-permute-start | bytes 393224 | tf_op jit(solution)/shard_map/ppermute | solution.py:62
  119.1 7.3 %collective-permute-start.33 = (f32[256,128]{1,0:T(8,128)S(1)}, f32[256,128]{1,0:T(8,128)S(1)}, u32[]{:S(2)}, u32[]{:S(2)}) collective-permute-start(f32[256,128]{1,0:T(8,128)S(1)} %slice_add_fusion.13), channel_id=1, source_target_pairs={{0,16},{4,20},{8,24},{12,28},{16,0},{20,4},{24,8},{28,12},{1,17},{... | collective-permute-start | bytes 393224 | tf_op jit(solution)/shard_map/ppermute | solution.py:62
  121.1 13.8 %collective-permute-start.28 = (f32[512,128]{1,0:T(8,128)S(1)}, f32[512,128]{1,0:T(8,128)S(1)}, u32[]{:S(2)}, u32[]{:S(2)}) collective-permute-start(f32[512,128]{1,0:T(8,128)S(1)} %get-tuple-element.124), channel_id=1, source_target_pairs={{0,4},{4,0},{8,12},{12,8},{16,20},{20,16},{24,28},{28,24},{1,5},{5... | collective-permute-start | bytes 786440 | tf_op jit(solution)/shard_map/ppermute | solution.py:62
  121.7 13.2 %collective-permute-start.30 = (f32[512,128]{1,0:T(8,128)S(1)}, f32[512,128]{1,0:T(8,128)S(1)}, u32[]{:S(2)}, u32[]{:S(2)}) collective-permute-start(f32[512,128]{1,0:T(8,128)S(1)} %get-tuple-element.136), channel_id=1, source_target_pairs={{0,8},{4,12},{8,0},{12,4},{16,24},{20,28},{24,16},{28,20},{1,9},{5... | collective-permute-start | bytes 786440 | tf_op jit(solution)/shard_map/ppermute | solution.py:62
  126.4 6.0 %collective-permute-start.34 = (f32[256,128]{1,0:T(8,128)S(1)}, f32[256,128]{1,0:T(8,128)S(1)}, u32[]{:S(2)}, u32[]{:S(2)}) collective-permute-start(f32[256,128]{1,0:T(8,128)S(1)} %add.775), channel_id=1, source_target_pairs={{0,8},{4,12},{8,0},{12,4},{16,24},{20,28},{24,16},{28,20},{1,9},{5... | collective-permute-start | bytes 393224 | tf_op jit(solution)/shard_map/ppermute | solution.py:62
  132.5 6.4 %collective-permute-start.35 = (f32[512,128]{1,0:T(8,128)S(1)}, f32[512,128]{1,0:T(8,128)S(1)}, u32[]{:S(2)}, u32[]{:S(2)}) collective-permute-start(f32[512,128]{1,0:T(8,128)S(1)} %get-tuple-element.128), channel_id=1, source_target_pairs={{0,4},{4,0},{8,12},{12,8},{16,20},{20,16},{24,28},{28,24},{1,5},{5... | collective-permute-start | bytes 786440 | tf_op jit(solution)/shard_map/ppermute | solution.py:62
  143.6 9.3 %collective-permute-start.37 = (f32[520,128]{1,0:T(8,128)S(1)}, f32[520,128]{1,0:T(8,128)S(1)}, u32[]{:S(2)}, u32[]{:S(2)}) collective-permute-start(f32[520,128]{1,0:T(8,128)S(1)} %pad_maximum_fusion.8), channel_id=1, source_target_pairs={{0,2},{1,3},{2,0},{3,1},{4,6},{5,7},{6,4},{7,5},{8,10},{9,11},{10,... | collective-permute-start | bytes 798728 | tf_op jit(solution)/shard_map/ppermute | solution.py:62
  145.6 12.3 %collective-permute-start.40 = (f32[512,128]{1,0:T(8,128)S(1)}, f32[512,128]{1,0:T(8,128)S(1)}, u32[]{:S(2)}, u32[]{:S(2)}) collective-permute-start(f32[512,128]{1,0:T(8,128)S(1)} %get-tuple-element.70), channel_id=1, source_target_pairs={{0,2},{1,3},{2,0},{3,1},{4,6},{5,7},{6,4},{7,5},{8,10},{9,11},{10,... | collective-permute-start | bytes 786440 | tf_op jit(solution)/shard_map/ppermute | solution.py:62
  165.5 8.3 %collective-permute-start.45 = (f32[512,128]{1,0:T(8,128)S(1)}, f32[512,128]{1,0:T(8,128)S(1)}, u32[]{:S(2)}, u32[]{:S(2)}) collective-permute-start(f32[512,128]{1,0:T(8,128)S(1)} %fusion.40), channel_id=1, source_target_pairs={{0,4},{4,0},{8,12},{12,8},{16,20},{20,16},{24,28},{28,24},{1,5},{5... | collective-permute-start | bytes 786440 | tf_op jit(solution)/shard_map/ppermute | solution.py:62
  166.8 9.6 %collective-permute-start.42 = (f32[520,128]{1,0:T(8,128)S(1)}, f32[520,128]{1,0:T(8,128)S(1)}, u32[]{:S(2)}, u32[]{:S(2)}) collective-permute-start(f32[520,128]{1,0:T(8,128)S(1)} %pad_maximum_fusion.9), channel_id=1, source_target_pairs={{0,8},{4,12},{8,0},{12,4},{16,24},{20,28},{24,16},{28,20},{1,9},{5... | collective-permute-start | bytes 798728 | tf_op jit(solution)/shard_map/ppermute | solution.py:62
  174.6 5.0 %collective-permute-start.46 = (f32[256,128]{1,0:T(8,128)S(1)}, f32[256,128]{1,0:T(8,128)S(1)}, u32[]{:S(2)}, u32[]{:S(2)}) collective-permute-start(f32[256,128]{1,0:T(8,128)S(1)} %slice.784), channel_id=1, source_target_pairs={{0,8},{4,12},{8,0},{12,4},{16,24},{20,28},{24,16},{28,20},{1,9},{5... | collective-permute-start | bytes 393224 | tf_op jit(solution)/shard_map/ppermute | solution.py:62
  175.4 12.7 %collective-permute-start.52 = (f32[512,128]{1,0:T(8,128)S(1)}, f32[512,128]{1,0:T(8,128)S(1)}, u32[]{:S(2)}, u32[]{:S(2)}) collective-permute-start(f32[512,128]{1,0:T(8,128)S(1)} %fusion.38), channel_id=1, source_target_pairs={{0,4},{4,0},{8,12},{12,8},{16,20},{20,16},{24,28},{28,24},{1,5},{5... | collective-permute-start | bytes 786440 | tf_op jit(solution)/shard_map/ppermute | solution.py:62
  177.2 8.2 %collective-permute-start.43 = (f32[264,128]{1,0:T(8,128)S(1)}, f32[264,128]{1,0:T(8,128)S(1)}, u32[]{:S(2)}, u32[]{:S(2)}) collective-permute-start(f32[264,128]{1,0:T(8,128)S(1)} %pad_maximum_fusion.23), channel_id=1, source_target_pairs={{0,4},{4,0},{8,12},{12,8},{16,20},{20,16},{24,28},{28,24},{1,5},{5... | collective-permute-start | bytes 405512 | tf_op jit(solution)/shard_map/ppermute | solution.py:62
  179.6 7.4 %collective-permute-start.47 = (f32[256,128]{1,0:T(8,128)S(1)}, f32[256,128]{1,0:T(8,128)S(1)}, u32[]{:S(2)}, u32[]{:S(2)}) collective-permute-start(f32[256,128]{1,0:T(8,128)S(1)} %slice_add_fusion.11), channel_id=1, source_target_pairs={{0,16},{4,20},{8,24},{12,28},{16,0},{20,4},{24,8},{28,12},{1,17},{... | collective-permute-start | bytes 393224 | tf_op jit(solution)/shard_map/ppermute | solution.py:62
  185.5 6.7 %collective-permute-start.44 = (f32[264,128]{1,0:T(8,128)S(1)}, f32[264,128]{1,0:T(8,128)S(1)}, u32[]{:S(2)}, u32[]{:S(2)}) collective-permute-start(f32[264,128]{1,0:T(8,128)S(1)} %pad_maximum_fusion.24), channel_id=1, source_target_pairs={{0,16},{4,20},{8,24},{12,28},{16,0},{20,4},{24,8},{28,12},{1,17},{... | collective-permute-start | bytes 405512 | tf_op jit(solution)/shard_map/ppermute | solution.py:62
  187.0 22.5 %collective-permute-start.48 = (f32[256,128]{1,0:T(8,128)S(1)}, f32[256,128]{1,0:T(8,128)S(1)}, u32[]{:S(2)}, u32[]{:S(2)}) collective-permute-start(f32[256,128]{1,0:T(8,128)S(1)} %add.826), channel_id=1, source_target_pairs={{0,8},{4,12},{8,0},{12,4},{16,24},{20,28},{24,16},{28,20},{1,9},{5... | collective-permute-start | bytes 393224 | tf_op jit(solution)/shard_map/ppermute | solution.py:62
  188.9 6.5 %collective-permute-start.53 = (f32[256,128]{1,0:T(8,128)S(1)}, f32[256,128]{1,0:T(8,128)S(1)}, u32[]{:S(2)}, u32[]{:S(2)}) collective-permute-start(f32[256,128]{1,0:T(8,128)S(1)} %slice.795), channel_id=1, source_target_pairs={{0,8},{4,12},{8,0},{12,4},{16,24},{20,28},{24,16},{28,20},{1,9},{5... | collective-permute-start | bytes 393224 | tf_op jit(solution)/shard_map/ppermute | solution.py:62
  192.2 24.5 %collective-permute-start.50 = (f32[256,128]{1,0:T(8,128)S(1)}, f32[256,128]{1,0:T(8,128)S(1)}, u32[]{:S(2)}, u32[]{:S(2)}) collective-permute-start(f32[256,128]{1,0:T(8,128)S(1)} %slice_add_fusion.10), channel_id=1, source_target_pairs={{0,4},{4,0},{8,12},{12,8},{16,20},{20,16},{24,28},{28,24},{1,5},{5... | collective-permute-start | bytes 393224 | tf_op jit(solution)/shard_map/ppermute | solution.py:62
  195.5 7.6 %collective-permute-start.54 = (f32[256,128]{1,0:T(8,128)S(1)}, f32[256,128]{1,0:T(8,128)S(1)}, u32[]{:S(2)}, u32[]{:S(2)}) collective-permute-start(f32[256,128]{1,0:T(8,128)S(1)} %slice_add_fusion.9), channel_id=1, source_target_pairs={{0,16},{4,20},{8,24},{12,28},{16,0},{20,4},{24,8},{28,12},{1,17},{... | collective-permute-start | bytes 393224 | tf_op jit(solution)/shard_map/ppermute | solution.py:62
  208.2 6.8 %collective-permute-start.56 = (f32[512,128]{1,0:T(8,128)S(1)}, f32[512,128]{1,0:T(8,128)S(1)}, u32[]{:S(2)}, u32[]{:S(2)}) collective-permute-start(f32[512,128]{1,0:T(8,128)S(1)} %get-tuple-element.98), channel_id=1, source_target_pairs={{0,4},{4,0},{8,12},{12,8},{16,20},{20,16},{24,28},{28,24},{1,5},{5... | collective-permute-start | bytes 786440 | tf_op jit(solution)/shard_map/ppermute | solution.py:62
  215.4 6.4 %collective-permute-start.49 = (f32[512,128]{1,0:T(8,128)S(1)}, f32[512,128]{1,0:T(8,128)S(1)}, u32[]{:S(2)}, u32[]{:S(2)}) collective-permute-start(f32[512,128]{1,0:T(8,128)S(1)} %get-tuple-element.108), channel_id=1, source_target_pairs={{0,4},{4,0},{8,12},{12,8},{16,20},{20,16},{24,28},{28,24},{1,5},{5... | collective-permute-start | bytes 786440 | tf_op jit(solution)/shard_map/ppermute | solution.py:62
  222.1 6.4 %collective-permute-start.51 = (f32[512,128]{1,0:T(8,128)S(1)}, f32[512,128]{1,0:T(8,128)S(1)}, u32[]{:S(2)}, u32[]{:S(2)}) collective-permute-start(f32[512,128]{1,0:T(8,128)S(1)} %get-tuple-element.103), channel_id=1, source_target_pairs={{0,8},{4,12},{8,0},{12,4},{16,24},{20,28},{24,16},{28,20},{1,9},{5... | collective-permute-start | bytes 786440 | tf_op jit(solution)/shard_map/ppermute | solution.py:62
  (44 other events, 950.4 us)

commit v3 on v2

--- a/solution.py
+++ b/solution.py
@@ -8,8 +8,8 @@
 CB_DEV = 24
 ITERS = 2
 TILE = 128
-ROW_STREAMS = ((8, False), (8, True), (8, False))
-COL_STREAMS = (8, 8)
+ROW_STREAMS = (12, 12)
+COL_STREAMS = (16,)
 
 tiny_eps = 1e-06
 
@@ -58,26 +58,16 @@
     )(slots, flip, kernel)
 
 
-def swap(value, axis, count, bit):
-    return lax.ppermute(value, axis, [(i, i ^ (1 << bit)) for i in range(count)])
-
-
-def swap_with(value, extra, axis, count, bit):
-    got = swap(jnp.concatenate([value, extra]), axis, count, bit)
-    return got[: value.shape[0]], got[value.shape[0] :]
-
-
 def after(value, other):
     return lax.optimization_barrier((value, other))[0]
 
 
-def column_norm(pieces):
-    sums = []
+def column_norm(pieces, unit):
+    parts = []
     for piece in pieces:
-        blocks = piece.reshape(-1, TILE, piece.shape[-1])
-        sums.append(jnp.sum(blocks * blocks, axis=1))
-    sums = jnp.concatenate(sums)
-    parts = [sums[i] for i in range(sums.shape[0])]
+        squares = (piece * piece).reshape(-1, unit, piece.shape[-1])
+        sums = jnp.sum(squares, axis=1)
+        parts += [sums[i] for i in range(sums.shape[0])]
     while len(parts) > 1:
         paired = [parts[i] + parts[i + 1] for i in range(0, len(parts) - 1, 2)]
         parts = paired + parts[len(parts) - len(parts) % 2 :]
@@ -95,29 +85,39 @@
     def side(index, bit):
         return (index >> bit) & 1
 
-    orders = [
-        [row_bits[1], row_bits[0], *row_bits[2:]] if turned else row_bits
-        for _, turned in ROW_STREAMS
-    ]
+    core = side(col_index, 0)
+    orders = [row_bits, [row_bits[1], row_bits[0], *row_bits[2:]]]
+    outer_side, inner_side = (
+        jnp.where(core == 0, side(row_index, orders[0][level]), side(row_index, orders[1][level]))
+        for level in range(2)
+    )
+
+    def swap_rows(value, level):
+        pairs = []
+        for row in range(row_count):
+            for col in range(col_count):
+                partner = row ^ (1 << orders[col & 1][level])
+                pairs.append((row * col_count + col, partner * col_count + col))
+        return lax.ppermute(value, ("rows", "cols"), pairs)
+
+    def swap_cols(value, level):
+        return lax.ppermute(value, "cols", [(i, i ^ (1 << level)) for i in range(col_count)])
 
     position_of = []
     start = 0
-    for (blocks, _), order in zip(ROW_STREAMS, orders):
-        mask = (1 - side(row_index, order[0])) * (blocks // 2) + (
-            1 - side(row_index, order[1])
-        ) * (blocks // 4)
+    for blocks in ROW_STREAMS:
         quarter = jnp.arange(blocks) // (blocks // 4)
         rest = jnp.arange(blocks) % (blocks // 4)
-        quarter_mask = (1 - side(row_index, order[0])) * 2 + (1 - side(row_index, order[1]))
-        position_of.append(start + (quarter ^ quarter_mask) * (blocks // 4) + rest)
+        mask = (1 - outer_side) * 2 + (1 - inner_side)
+        position_of.append(start + (quarter ^ mask) * (blocks // 4) + rest)
         start += blocks
     block_at = jnp.concatenate(position_of)
-    flip = (1 - side(col_index, 0)) * (COL_STREAMS[0] // 2)
+    flip = (1 - core) * (COL_STREAMS[0] // 2)
 
     alive = jnp.arange(slot_count)[None, :] < counts
     hits = (pattern[:, :, None] == block_at[None, None, :]) & alive[:, :, None]
     slots = jnp.sum(hits * (jnp.arange(slot_count) + 1)[None, :, None], axis=1) - 1
-    widths = [half for blocks, _ in ROW_STREAMS for half in (blocks // 2, blocks // 2)]
+    widths = [half for blocks in ROW_STREAMS for half in (blocks // 2, blocks // 2)]
     dense = fill_dense(
         kernel,
         slots.reshape(-1).astype(jnp.int32),
@@ -125,7 +125,7 @@
         widths,
     )
 
-    kept_first = side(col_index, 0) == 0
+    kept_first = core == 0
     left_pieces = []
     start = 0
     for blocks in COL_STREAMS:
@@ -135,64 +135,43 @@
         left_pieces += [jnp.where(kept_first, high, low), jnp.where(kept_first, low, high)]
         start += 2 * half
 
+    def staggered(sends, norm, swap):
+        got = []
+        for s, send in enumerate(sends):
+            if s > 0:
+                send = after(send, got[s - 1])
+            elif norm is not None:
+                send = jnp.concatenate([send, norm])
+            got.append(swap(send))
+        if norm is not None:
+            split = sends[0].shape[0]
+            norm = norm + got[0][split:]
+            got[0] = got[0][:split]
+        return got, norm
+
     def reduce_rows(partials, norm):
-        keeps = []
-        first_got = []
-        for s, order in enumerate(orders):
-            send, keep = partials[s]
-            if s >= 2:
-                send = after(send, first_got[s - 2])
-            if s == 1:
-                got, other = swap_with(send, norm, "rows", row_count, order[0])
-                norm = norm + other
+        sends, keeps = [list(part) for part in zip(*partials)]
+        for level in range(len(row_bits)):
+            got, norm = staggered(sends, norm, lambda value: swap_rows(value, level))
+            keeps = [keep + other for keep, other in zip(keeps, got)]
+            if level == 0:
+                halves = [keep.shape[0] // 2 for keep in keeps]
+                sends = [keep[:half] for keep, half in zip(keeps, halves)]
+                keeps = [keep[half:] for keep, half in zip(keeps, halves)]
             else:
-                got = swap(send, "rows", row_count, order[0])
-            first_got.append(got)
-            keeps.append(keep + got)
-        for level in range(1, len(row_bits)):
-            for s, order in enumerate(orders):
-                mine = keeps[s]
-                if level == 1:
-                    half = mine.shape[0] // 2
-                    send, mine = mine[:half], mine[half:]
-                else:
-                    send = mine
-                if s == 1:
-                    got, other = swap_with(send, norm, "rows", row_count, order[level])
-                    norm = norm + other
-                else:
-                    got = swap(send, "rows", row_count, order[level])
-                keeps[s] = mine + got
-        pieces = []
-        for s, order in enumerate(orders):
-            inner = swap(keeps[s], "rows", row_count, order[1])
-            own = jnp.concatenate([inner, keeps[s]])
-            outer = swap(own, "rows", row_count, order[0])
-            pieces += [outer, own]
-        return pieces, norm[0]
+                sends = keeps
+        inner, _ = staggered(keeps, None, lambda value: swap_rows(value, 1))
+        own = [jnp.concatenate(pair) for pair in zip(inner, keeps)]
+        outer, _ = staggered(own, None, lambda value: swap_rows(value, 0))
+        return [piece for pair in zip(outer, own) for piece in pair], norm[0]
 
     def reduce_cols(partials, norm):
-        keeps = []
-        for s in range(len(COL_STREAMS)):
-            send, keep = partials[2 * s], partials[2 * s + 1]
-            if s == 0:
-                got, other = swap_with(send, norm, "cols", col_count, 0)
-                norm = norm + other
-            else:
-                got = swap(send, "cols", col_count, 0)
-            keeps.append(keep + got)
-        for bit in col_bits[1:]:
-            for s in range(len(COL_STREAMS)):
-                if s == 0:
-                    got, other = swap_with(keeps[s], norm, "cols", col_count, bit)
-                    norm = norm + other
-                else:
-                    got = swap(keeps[s], "cols", col_count, bit)
-                keeps[s] = keeps[s] + got
-        pieces = []
-        for s in range(len(COL_STREAMS)):
-            pieces += [swap(keeps[s], "cols", col_count, 0), keeps[s]]
-        return pieces, norm[0]
+        sends, keeps = partials[0::2], partials[1::2]
+        for level in range(len(col_bits)):
+            got, norm = staggered(sends, norm, lambda value: swap_cols(value, level))
+            sends = keeps = [keep + other for keep, other in zip(keeps, got)]
+        other, _ = staggered(keeps, None, lambda value: swap_cols(value, 0))
+        return [piece for pair in zip(other, keeps) for piece in pair], norm[0]
 
     def spread(norm):
         return jnp.broadcast_to(norm[None, :], (8, width))
@@ -206,7 +185,7 @@
             for chunk in dense
         ]
         partials = list(zip(products[0::2], products[1::2]))
-        summed, squares = reduce_rows(partials, spread(column_norm(left_raw)))
+        summed, squares = reduce_rows(partials, spread(column_norm(left_raw, left_raw[0].shape[0])))
         beta_norm = jnp.sqrt(squares + tiny_eps)
         right_raw = [
             total / beta_norm - beta_norm * prev for total, prev in zip(summed, right_prev)
@@ -237,7 +216,7 @@
     radius = beta_first
     for iteration in range(ITERS):
         fore_summed, fore_squares = reduce_cols(
-            fore_products(right_raw), spread(column_norm(right_raw))
+            fore_products(right_raw), spread(column_norm(right_raw, right_raw[0].shape[0] // 2))
         )
         alpha_norm = jnp.sqrt(fore_squares + tiny_eps)
         left_raw = [
@@ -263,16 +242,13 @@
 
     def in_block_order(pieces):
         out = []
-        for s, order in enumerate(orders):
-            outer, own = pieces[2 * s], pieces[2 * s + 1]
+        for outer, own in zip(pieces[0::2], pieces[1::2]):
             half = outer.shape[0] // 2
-            straight = side(row_index, order[1]) == 1
             outer, own = (
-                jnp.where(straight, v, jnp.concatenate([v[half:], v[:half]]))
+                jnp.where(inner_side == 1, v, jnp.concatenate([v[half:], v[:half]]))
                 for v in (outer, own)
             )
-            straight = side(row_index, order[0]) == 1
-            out += [jnp.where(straight, outer, own), jnp.where(straight, own, outer)]
+            out += [jnp.where(outer_side == 1, outer, own), jnp.where(outer_side == 1, own, outer)]
         return jnp.concatenate(out)
 
     return (in_block_order(model), in_block_order(gradient), misfit)

time: 232 us -> 257 us (1.11)
  waiting for transfers between devices: 117 us -> 142 us
  starting transfers between devices: 61.9 us -> 43.3 us
  other arithmetic: 13.9 us -> 24.5 us
  matrix products: 22.6 us -> 30.6 us
    ppermute x57 -> x36, waiting for transfers between devices: 117 us -> 142 us  [the longest x30 109 us: swap_rows(): return lax.ppermute(value, ('rows', 'cols'), pairs)]
    ppermute x57 -> x36, starting transfers between devices: 61.9 us -> 43.3 us  [the longest x30 38.7 us: swap_rows(): return lax.ppermute(value, ('rows', 'cols'), pairs)]
    dot_general x12 -> x8, matrix products: 8.63 us -> 16.1 us  [fore_products(): jnp.dot(chunk, piece.astype(jnp.bfloat16), preferred_element_type=jnp.flo...]
    reduce_sum x15 -> x11, other arithmetic: 3.05 us -> 8.19 us  [column_norm(): sums = jnp.sum(squares, axis=1)]
    unnamed x70 -> x130, local copies, waits for them, and re-layouts: 6.56 us -> 7.16 us
    dot_general x18 -> x12, matrix products: 14 us -> 14.5 us  [back_step(): lax.dot_general(chunk, left_bf, (((0,), (0,)), ((), ())), preferred_eleme...]
  transfers between devices with their start and end apart: 57 -> 36, of which waited for: 40 -> 30; matrix products, arithmetic and copies ran while one was open for 10% -> 8% of each run, Pallas kernels for 0% -> 0%
where the time goes in v3:
time: 257 us
  waiting for transfers between devices  142 us (55%)
  starting transfers between devices  43.3 us (17%)
  matrix products  30.6 us (12%)
  other arithmetic  24.5 us (10%)
  local copies, waits for them, and re-layouts  7.64 us (3%)
  Pallas kernels  6.73 us (3%)
    ppermute x30, waiting for transfers between devices, swap_rows(): return lax.ppermute(value, ('rows', 'cols'), pairs)  109 us
    ppermute x30, starting transfers between devices, swap_rows(): return lax.ppermute(value, ('rows', 'cols'), pairs)  38.7 us
    ppermute x6, waiting for transfers between devices, swap_cols(): lax.ppermute(value, 'cols', [(i, i ^ 1 << level) for i in range(col_count)])  32.6 us
    dot_general x8, matrix products, fore_products(): jnp.dot(chunk, piece.astype(jnp.bfloat16), preferred_element_type=jnp.flo...  16.1 us
    dot_general x12, matrix products, back_step(): lax.dot_general(chunk, left_bf, (((0,), (0,)), ((), ())), preferred_eleme...  14.5 us
    reduce_sum x11, other arithmetic, column_norm(): sums = jnp.sum(squares, axis=1)  8.19 us
    unnamed x130, local copies, waits for them, and re-layouts  7.16 us
    pallas_call x1, Pallas kernels, fill_dense(): pl.pallas_call(fill_kernel, grid_spec=pltpu.PrefetchScalarGridSpec(num_sc...  6.73 us
  transfers between devices with their start and end apart: 36, of which 30 were waited for; matrix products, arithmetic and copies ran while one was open for 8% of the time, Pallas kernels for 0%

profile of v3, /device:TPU:0, one launch (start us, length us, event | category | flops | bytes accessed | tf_op | source)
XLA Modules:
  0.0 256.6 jit_solution(14252983515616976357)
XLA Ops:
  2.4 2.1 fusion.58
  5.6 3.4 %copy-done.3 = bf16[16,16,128,128]{3,2,1,0:T(8,128)(2,1)S(1)} copy-done((bf16[16,16,128,128]{3,2,1,0:T(8,128)(2,1)S(1)}, bf16[16,16,128,128]{3,2,1,0:T(8,128)(2,1)}, u32[]{:S(2)}) %copy-start.3) | copy-done | bytes 8388632
  8.9 6.7 %shard_map.70 = (bf16[2048,768]{1,0:T(8,128)(2,1)S(1)}, bf16[2048,768]{1,0:T(8,128)(2,1)S(1)}, bf16[2048,768]{1,0:T(8,128)(2,1)S(1)}, bf16[2048,768]{1,0:T(8,128)(2,1)S(1)}) custom-call(s32[384]{0:T(512)S(1)} %sub.100.slot_ref, s32[1]{0:T(128)} %bitcast.1.flip_ref, bf16[16,16,128,128]{3,2,1,0:T(8,128)(2,1)S(1)} %copy-done.3), custom_call_target="tpu_custom_call" | custom-call | tf_op jit(solution)/shard_map/pallas_call | solution.py:38
  16.8 2.7 %collective-permute-start = (f32[776,128]{1,0:T(8,128)S(1)}, f32[776,128]{1,0:T(8,128)S(1)}, u32[]{:S(2)}, u32[]{:S(2)}) collective-permute-start(f32[776,128]{1,0:T(8,128)S(1)} %pad_maximum_fusion.9), channel_id=1, source_target_pairs={{0,4},{1,9},{2,6},{3,11},{4,0},{5,13},{6,2},{7,15},{8,12},{9,1},{1... | collective-permute-start | bytes 1191944 | tf_op jit(solution)/shard_map/ppermute | solution.py:101
  19.5 5.8 %collective-permute-done = f32[776,128]{1,0:T(8,128)S(1)} collective-permute-done((f32[776,128]{1,0:T(8,128)S(1)}, f32[776,128]{1,0:T(8,128)S(1)}, u32[]{:S(2)}, u32[]{:S(2)}) %collective-permute-start) | collective-permute-done | bytes 397344 | tf_op jit(solution)/shard_map/ppermute | solution.py:101
  26.4 2.2 collective-permute-start.1
  29.7 1.7 collective-permute-start.5
  31.3 2.3 collective-permute-done.1
  33.7 3.5 %collective-permute-start.2 = (f32[392,128]{1,0:T(8,128)S(1)}, f32[392,128]{1,0:T(8,128)S(1)}, u32[]{:S(2)}, u32[]{:S(2)}) collective-permute-start(f32[392,128]{1,0:T(8,128)S(1)} %pad_maximum_fusion.19), channel_id=1, source_target_pairs={{0,16},{1,17},{2,18},{3,19},{4,20},{5,21},{6,22},{7,23},{8,24},{9,... | collective-permute-start | bytes 602120 | tf_op jit(solution)/shard_map/ppermute | solution.py:101
  38.3 4.1 %collective-permute-start.6 = (f32[384,128]{1,0:T(8,128)S(1)}, f32[384,128]{1,0:T(8,128)S(1)}, u32[]{:S(2)}, u32[]{:S(2)}) collective-permute-start(f32[384,128]{1,0:T(8,128)S(1)} %slice.333), channel_id=1, source_target_pairs={{0,8},{1,5},{2,10},{3,7},{4,12},{5,1},{6,14},{7,3},{8,0},{9,13},{1... | collective-permute-start | bytes 589832 | tf_op jit(solution)/shard_map/ppermute | solution.py:101
  42.4 2.9 %collective-permute-done.2 = f32[392,128]{1,0:T(8,128)S(1)} collective-permute-done((f32[392,128]{1,0:T(8,128)S(1)}, f32[392,128]{1,0:T(8,128)S(1)}, u32[]{:S(2)}, u32[]{:S(2)}) %collective-permute-start.2) | collective-permute-done | bytes 200736 | tf_op jit(solution)/shard_map/ppermute | solution.py:101
  48.2 7.8 %collective-permute-done.3 = f32[384,128]{1,0:T(8,128)S(1)} collective-permute-done((f32[384,128]{1,0:T(8,128)S(1)}, f32[384,128]{1,0:T(8,128)S(1)}, u32[]{:S(2)}, u32[]{:S(2)}) %collective-permute-start.3) | collective-permute-done | bytes 196640 | tf_op jit(solution)/shard_map/ppermute | solution.py:101
  56.3 1.8 collective-permute-start.8
  58.1 2.0 fusion.15
  60.1 3.7 %collective-permute-done.8 = f32[384,128]{1,0:T(8,128)S(1)} collective-permute-done((f32[384,128]{1,0:T(8,128)S(1)}, f32[384,128]{1,0:T(8,128)S(1)}, u32[]{:S(2)}, u32[]{:S(2)}) %collective-permute-start.8) | collective-permute-done | bytes 196640 | tf_op jit(solution)/shard_map/ppermute | solution.py:101
  63.9 3.6 %collective-permute-start.9 = (f32[768,128]{1,0:T(8,128)S(1)}, f32[768,128]{1,0:T(8,128)S(1)}, u32[]{:S(2)}, u32[]{:S(2)}) collective-permute-start(f32[768,128]{1,0:T(8,128)S(1)} %pad_maximum_fusion.13), channel_id=1, source_target_pairs={{0,4},{1,9},{2,6},{3,11},{4,0},{5,13},{6,2},{7,15},{8,12},{9,1},{1... | collective-permute-start | bytes 1179656 | tf_op jit(solution)/shard_map/ppermute | solution.py:101
  67.6 2.0 fusion.11
  69.6 3.6 %collective-permute-done.9 = f32[768,128]{1,0:T(8,128)S(1)} collective-permute-done((f32[768,128]{1,0:T(8,128)S(1)}, f32[768,128]{1,0:T(8,128)S(1)}, u32[]{:S(2)}, u32[]{:S(2)}) %collective-permute-start.9) | collective-permute-done | bytes 393248 | tf_op jit(solution)/shard_map/ppermute | solution.py:101
  75.1 1.6 reduce_sum.138
  78.3 3.1 %fusion.13 = f32[2048,128]{1,0:T(8,128)S(1)} fusion(bf16[2048,768]{1,0:T(8,128)(2,1)} %copy-done, f32[768,128]{1,0:T(8,128)} %copy-done.11, f32[128]{0:T(128)S(1)} %broadcast_multiply_fusion, f32[128]{0:T(128)S(1)} %fusion.31), kind=kOutput, calls=%fused_computation.105 | convolution fusion | flops 402948096 | bytes 4588544 | tf_op jit(solution)/shard_map/dot_general | solution.py:198
  82.7 1.9 collective-permute-done.10
  84.8 3.1 %collective-permute-start.11 = (f32[1032,128]{1,0:T(8,128)S(1)}, f32[1032,128]{1,0:T(8,128)S(1)}, u32[]{:S(2)}, u32[]{:S(2)}) collective-permute-start(f32[1032,128]{1,0:T(8,128)S(1)} %pad_maximum_fusion.3), channel_id=1, source_target_pairs={{0,2},{1,3},{2,0},{3,1},{4,6},{5,7},{6,4},{7,5},{8,10},{9,11},{10,... | collective-permute-start | bytes 1585160 | tf_op jit(solution)/shard_map/ppermute | solution.py:104
  87.9 12.3 %collective-permute-done.11 = f32[1032,128]{1,0:T(8,128)S(1)} collective-permute-done((f32[1032,128]{1,0:T(8,128)S(1)}, f32[1032,128]{1,0:T(8,128)S(1)}, u32[]{:S(2)}, u32[]{:S(2)}) %collective-permute-start.11) | collective-permute-done | bytes 528416 | tf_op jit(solution)/shard_map/ppermute | solution.py:104
  101.2 1.7 collective-permute-done.12
  105.9 7.1 %collective-permute-done.13 = f32[776,128]{1,0:T(8,128)S(1)} collective-permute-done((f32[776,128]{1,0:T(8,128)S(1)}, f32[776,128]{1,0:T(8,128)S(1)}, u32[]{:S(2)}, u32[]{:S(2)}) %collective-permute-start.13) | collective-permute-done | bytes 397344 | tf_op jit(solution)/shard_map/ppermute | solution.py:101
  116.4 5.8 %collective-permute-done.14 = f32[392,128]{1,0:T(8,128)S(1)} collective-permute-done((f32[392,128]{1,0:T(8,128)S(1)}, f32[392,128]{1,0:T(8,128)S(1)}, u32[]{:S(2)}, u32[]{:S(2)}) %collective-permute-start.14) | collective-permute-done | bytes 200736 | tf_op jit(solution)/shard_map/ppermute | solution.py:101
  124.3 2.1 collective-permute-start.19
  126.4 4.6 %collective-permute-done.15 = f32[392,128]{1,0:T(8,128)S(1)} collective-permute-done((f32[392,128]{1,0:T(8,128)S(1)}, f32[392,128]{1,0:T(8,128)S(1)}, u32[]{:S(2)}, u32[]{:S(2)}) %collective-permute-start.15) | collective-permute-done | bytes 200736 | tf_op jit(solution)/shard_map/ppermute | solution.py:101
  132.2 1.7 collective-permute-start.20
  133.8 9.8 %collective-permute-done.20 = f32[384,128]{1,0:T(8,128)S(1)} collective-permute-done((f32[384,128]{1,0:T(8,128)S(1)}, f32[384,128]{1,0:T(8,128)S(1)}, u32[]{:S(2)}, u32[]{:S(2)}) %collective-permute-start.20) | collective-permute-done | bytes 196640 | tf_op jit(solution)/shard_map/ppermute | solution.py:101
  143.8 5.6 %collective-permute-done.21 = f32[384,128]{1,0:T(8,128)S(1)} collective-permute-done((f32[384,128]{1,0:T(8,128)S(1)}, f32[384,128]{1,0:T(8,128)S(1)}, u32[]{:S(2)}, u32[]{:S(2)}) %collective-permute-start.21) | collective-permute-done | bytes 196640 | tf_op jit(solution)/shard_map/ppermute | solution.py:101
  150.6 2.0 fusion.8
  152.5 5.0 %collective-permute-done.17 = f32[768,128]{1,0:T(8,128)S(1)} collective-permute-done((f32[768,128]{1,0:T(8,128)S(1)}, f32[768,128]{1,0:T(8,128)S(1)}, u32[]{:S(2)}, u32[]{:S(2)}) %collective-permute-start.17) | collective-permute-done | bytes 393248 | tf_op jit(solution)/shard_map/ppermute | solution.py:101
  158.3 2.0 fusion.4
  161.1 4.1 %collective-permute-done.22 = f32[768,128]{1,0:T(8,128)S(1)} collective-permute-done((f32[768,128]{1,0:T(8,128)S(1)}, f32[768,128]{1,0:T(8,128)S(1)}, u32[]{:S(2)}, u32[]{:S(2)}) %collective-permute-start.22) | collective-permute-done | bytes 393248 | tf_op jit(solution)/shard_map/ppermute | solution.py:101
  169.8 3.1 %fusion.6 = f32[2048,128]{1,0:T(8,128)S(1)} fusion(bf16[2048,768]{1,0:T(8,128)(2,1)} %copy-done, f32[768,128]{1,0:T(8,128)} %get-tuple-element.117), kind=kOutput, calls=%fused_computation.94 | convolution fusion | flops 402751488 | bytes 4587520 | tf_op jit(solution)/shard_map/dot_general | solution.py:198
  174.2 1.9 collective-permute-done.23
  177.4 13.0 %collective-permute-done.24 = f32[1032,128]{1,0:T(8,128)S(1)} collective-permute-done((f32[1032,128]{1,0:T(8,128)S(1)}, f32[1032,128]{1,0:T(8,128)S(1)}, u32[]{:S(2)}, u32[]{:S(2)}) %collective-permute-start.24) | collective-permute-done | bytes 528416 | tf_op jit(solution)/shard_map/ppermute | solution.py:104
  191.4 1.7 collective-permute-done.25
  196.1 7.3 %collective-permute-done.26 = f32[776,128]{1,0:T(8,128)} collective-permute-done((f32[776,128]{1,0:T(8,128)}, f32[776,128]{1,0:T(8,128)}, u32[]{:S(2)}, u32[]{:S(2)}) %collective-permute-start.26) | collective-permute-done | bytes 397344 | tf_op jit(solution)/shard_map/ppermute | solution.py:101
  203.4 3.1 %slice_add_fusion.4 = f32[768,128]{1,0:T(8,128)S(1)} fusion(f32[776,128]{1,0:T(8,128)} %collective-permute-done.26, bf16[2048,768]{1,0:T(8,128)(2,1)} %copy-done.7, bf16[1024,128]{1,0:T(8,128)(2,1)} %copy-done.49, bf16[1024,128]{1,0:T(8,128)(2,1)} %copy-done.47), kind=kOutput, calls=%fused_computation.34 | convolution fusion | flops 403800064 | bytes 4456448 | tf_op jit(solution)/shard_map/dot_general | solution.py:182
  209.6 5.5 %collective-permute-done.27 = f32[392,128]{1,0:T(8,128)S(1)} collective-permute-done((f32[392,128]{1,0:T(8,128)S(1)}, f32[392,128]{1,0:T(8,128)S(1)}, u32[]{:S(2)}, u32[]{:S(2)}) %collective-permute-start.27) | collective-permute-done | bytes 200736 | tf_op jit(solution)/shard_map/ppermute | solution.py:101
  217.7 2.1 collective-permute-start.32
  219.7 5.0 %collective-permute-done.28 = f32[392,128]{1,0:T(8,128)S(1)} collective-permute-done((f32[392,128]{1,0:T(8,128)S(1)}, f32[392,128]{1,0:T(8,128)S(1)}, u32[]{:S(2)}, u32[]{:S(2)}) %collective-permute-start.28) | collective-permute-done | bytes 200736 | tf_op jit(solution)/shard_map/ppermute | solution.py:101
  227.5 2.2 collective-permute-start.33
  229.8 7.5 %collective-permute-done.29 = f32[384,128]{1,0:T(8,128)S(1)} collective-permute-done((f32[384,128]{1,0:T(8,128)S(1)}, f32[384,128]{1,0:T(8,128)S(1)}, u32[]{:S(2)}, u32[]{:S(2)}) %collective-permute-start.29) | collective-permute-done | bytes 196640 | tf_op jit(solution)/shard_map/ppermute | solution.py:101
  239.0 6.0 %collective-permute-done.34 = f32[384,128]{1,0:T(8,128)S(1)} collective-permute-done((f32[384,128]{1,0:T(8,128)S(1)}, f32[384,128]{1,0:T(8,128)S(1)}, u32[]{:S(2)}, u32[]{:S(2)}) %collective-permute-start.34) | collective-permute-done | bytes 196640 | tf_op jit(solution)/shard_map/ppermute | solution.py:101
  247.2 6.4 %collective-permute-done.35 = f32[768,128]{1,0:T(8,128)S(1)} collective-permute-done((f32[768,128]{1,0:T(8,128)S(1)}, f32[768,128]{1,0:T(8,128)S(1)}, u32[]{:S(2)}, u32[]{:S(2)}) %collective-permute-start.35) | collective-permute-done | bytes 393248 | tf_op jit(solution)/shard_map/ppermute | solution.py:101
  (287 shorter events, 54.4 us)
Async XLA Ops:
  15.7 42.4 %copy-start.7 = (bf16[2048,768]{1,0:T(8,128)(2,1)}, bf16[2048,768]{1,0:T(8,128)(2,1)S(1)}, u32[]{:S(2)}) copy-start(bf16[2048,768]{1,0:T(8,128)(2,1)S(1)} %get-tuple-element.22) | copy-start | bytes 9437188
  15.7 51.9 %copy-start.4 = (bf16[2048,768]{1,0:T(8,128)(2,1)}, bf16[2048,768]{1,0:T(8,128)(2,1)S(1)}, u32[]{:S(2)}) copy-start(bf16[2048,768]{1,0:T(8,128)(2,1)S(1)} %get-tuple-element.24) | copy-start | bytes 9437188
  16.8 8.5 %collective-permute-start = (f32[776,128]{1,0:T(8,128)S(1)}, f32[776,128]{1,0:T(8,128)S(1)}, u32[]{:S(2)}, u32[]{:S(2)}) collective-permute-start(f32[776,128]{1,0:T(8,128)S(1)} %pad_maximum_fusion.9), channel_id=1, source_target_pairs={{0,4},{1,9},{2,6},{3,11},{4,0},{5,13},{6,2},{7,15},{8,12},{9,1},{1... | collective-permute-start | bytes 1191944 | tf_op jit(solution)/shard_map/ppermute | solution.py:101
  26.4 7.2 %collective-permute-start.1 = (f32[392,128]{1,0:T(8,128)S(1)}, f32[392,128]{1,0:T(8,128)S(1)}, u32[]{:S(2)}, u32[]{:S(2)}) collective-permute-start(f32[392,128]{1,0:T(8,128)S(1)} %pad_maximum_fusion.18), channel_id=1, source_target_pairs={{0,8},{1,5},{2,10},{3,7},{4,12},{5,1},{6,14},{7,3},{8,0},{9,13},{1... | collective-permute-start | bytes 602120 | tf_op jit(solution)/shard_map/ppermute | solution.py:101
  29.7 8.6 %collective-permute-start.5 = (f32[768,128]{1,0:T(8,128)S(1)}, f32[768,128]{1,0:T(8,128)S(1)}, u32[]{:S(2)}, u32[]{:S(2)}) collective-permute-start(f32[768,128]{1,0:T(8,128)S(1)} %fusion.42), channel_id=1, source_target_pairs={{0,4},{1,9},{2,6},{3,11},{4,0},{5,13},{6,2},{7,15},{8,12},{9,1},{1... | collective-permute-start | bytes 1179656 | tf_op jit(solution)/shard_map/ppermute | solution.py:101
  33.7 11.6 %collective-permute-start.2 = (f32[392,128]{1,0:T(8,128)S(1)}, f32[392,128]{1,0:T(8,128)S(1)}, u32[]{:S(2)}, u32[]{:S(2)}) collective-permute-start(f32[392,128]{1,0:T(8,128)S(1)} %pad_maximum_fusion.19), channel_id=1, source_target_pairs={{0,16},{1,17},{2,18},{3,19},{4,20},{5,21},{6,22},{7,23},{8,24},{9,... | collective-permute-start | bytes 602120 | tf_op jit(solution)/shard_map/ppermute | solution.py:101
  38.3 8.5 %collective-permute-start.6 = (f32[384,128]{1,0:T(8,128)S(1)}, f32[384,128]{1,0:T(8,128)S(1)}, u32[]{:S(2)}, u32[]{:S(2)}) collective-permute-start(f32[384,128]{1,0:T(8,128)S(1)} %slice.333), channel_id=1, source_target_pairs={{0,8},{1,5},{2,10},{3,7},{4,12},{5,1},{6,14},{7,3},{8,0},{9,13},{1... | collective-permute-start | bytes 589832 | tf_op jit(solution)/shard_map/ppermute | solution.py:101
  45.4 10.6 %collective-permute-start.3 = (f32[384,128]{1,0:T(8,128)S(1)}, f32[384,128]{1,0:T(8,128)S(1)}, u32[]{:S(2)}, u32[]{:S(2)}) collective-permute-start(f32[384,128]{1,0:T(8,128)S(1)} %slice_add_fusion.14), channel_id=1, source_target_pairs={{0,8},{1,5},{2,10},{3,7},{4,12},{5,1},{6,14},{7,3},{8,0},{9,13},{1... | collective-permute-start | bytes 589832 | tf_op jit(solution)/shard_map/ppermute | solution.py:101
  46.8 9.4 %collective-permute-start.7 = (f32[384,128]{1,0:T(8,128)S(1)}, f32[384,128]{1,0:T(8,128)S(1)}, u32[]{:S(2)}, u32[]{:S(2)}) collective-permute-start(f32[384,128]{1,0:T(8,128)S(1)} %slice_add_fusion.13), channel_id=1, source_target_pairs={{0,16},{1,17},{2,18},{3,19},{4,20},{5,21},{6,22},{7,23},{8,24},{9,... | collective-permute-start | bytes 589832 | tf_op jit(solution)/shard_map/ppermute | solution.py:101
  56.0 7.8 %collective-permute-start.4 = (f32[768,128]{1,0:T(8,128)S(1)}, f32[768,128]{1,0:T(8,128)S(1)}, u32[]{:S(2)}, u32[]{:S(2)}) collective-permute-start(f32[768,128]{1,0:T(8,128)S(1)} %pad_maximum_fusion.12), channel_id=1, source_target_pairs={{0,4},{1,9},{2,6},{3,11},{4,0},{5,13},{6,2},{7,15},{8,12},{9,1},{1... | collective-permute-start | bytes 1179656 | tf_op jit(solution)/shard_map/ppermute | solution.py:101
  56.3 7.5 %collective-permute-start.8 = (f32[384,128]{1,0:T(8,128)S(1)}, f32[384,128]{1,0:T(8,128)S(1)}, u32[]{:S(2)}, u32[]{:S(2)}) collective-permute-start(f32[384,128]{1,0:T(8,128)S(1)} %add.322), channel_id=1, source_target_pairs={{0,8},{1,5},{2,10},{3,7},{4,12},{5,1},{6,14},{7,3},{8,0},{9,13},{1... | collective-permute-start | bytes 589832 | tf_op jit(solution)/shard_map/ppermute | solution.py:101
  63.9 9.4 %collective-permute-start.9 = (f32[768,128]{1,0:T(8,128)S(1)}, f32[768,128]{1,0:T(8,128)S(1)}, u32[]{:S(2)}, u32[]{:S(2)}) collective-permute-start(f32[768,128]{1,0:T(8,128)S(1)} %pad_maximum_fusion.13), channel_id=1, source_target_pairs={{0,4},{1,9},{2,6},{3,11},{4,0},{5,13},{6,2},{7,15},{8,12},{9,1},{1... | collective-permute-start | bytes 1179656 | tf_op jit(solution)/shard_map/ppermute | solution.py:101
  82.7 2.0 collective-permute-start.10
  84.8 15.4 %collective-permute-start.11 = (f32[1032,128]{1,0:T(8,128)S(1)}, f32[1032,128]{1,0:T(8,128)S(1)}, u32[]{:S(2)}, u32[]{:S(2)}) collective-permute-start(f32[1032,128]{1,0:T(8,128)S(1)} %pad_maximum_fusion.3), channel_id=1, source_target_pairs={{0,2},{1,3},{2,0},{3,1},{4,6},{5,7},{6,4},{7,5},{8,10},{9,11},{10,... | collective-permute-start | bytes 1585160 | tf_op jit(solution)/shard_map/ppermute | solution.py:104
  101.0 2.0 collective-permute-start.12
  105.1 7.9 %collective-permute-start.13 = (f32[776,128]{1,0:T(8,128)S(1)}, f32[776,128]{1,0:T(8,128)S(1)}, u32[]{:S(2)}, u32[]{:S(2)}) collective-permute-start(f32[776,128]{1,0:T(8,128)S(1)} %pad_maximum_fusion.10), channel_id=1, source_target_pairs={{0,4},{1,9},{2,6},{3,11},{4,0},{5,13},{6,2},{7,15},{8,12},{9,1},{1... | collective-permute-start | bytes 1191944 | tf_op jit(solution)/shard_map/ppermute | solution.py:101
  114.3 7.9 %collective-permute-start.14 = (f32[392,128]{1,0:T(8,128)S(1)}, f32[392,128]{1,0:T(8,128)S(1)}, u32[]{:S(2)}, u32[]{:S(2)}) collective-permute-start(f32[392,128]{1,0:T(8,128)S(1)} %pad_maximum_fusion.20), channel_id=1, source_target_pairs={{0,8},{1,5},{2,10},{3,7},{4,12},{5,1},{6,14},{7,3},{8,0},{9,13},{1... | collective-permute-start | bytes 602120 | tf_op jit(solution)/shard_map/ppermute | solution.py:101
  115.4 7.8 %collective-permute-start.18 = (f32[768,128]{1,0:T(8,128)S(1)}, f32[768,128]{1,0:T(8,128)S(1)}, u32[]{:S(2)}, u32[]{:S(2)}) collective-permute-start(f32[768,128]{1,0:T(8,128)S(1)} %fusion.37), channel_id=1, source_target_pairs={{0,4},{1,9},{2,6},{3,11},{4,0},{5,13},{6,2},{7,15},{8,12},{9,1},{1... | collective-permute-start | bytes 1179656 | tf_op jit(solution)/shard_map/ppermute | solution.py:101
  122.3 27.1 %copy-start.36 = (f32[384,128]{1,0:T(8,128)S(1)}, f32[384,128]{1,0:T(8,128)}, u32[]{:S(2)}) copy-start(f32[384,128]{1,0:T(8,128)} %copy-done.35) | copy-start | bytes 589828
  122.3 27.1 %copy-start.39 = (f32[384,128]{1,0:T(8,128)S(1)}, f32[384,128]{1,0:T(8,128)}, u32[]{:S(2)}) copy-start(f32[384,128]{1,0:T(8,128)} %copy-done.38) | copy-start | bytes 589828
  122.3 27.1 %copy-start.42 = (f32[384,128]{1,0:T(8,128)S(1)}, f32[384,128]{1,0:T(8,128)}, u32[]{:S(2)}) copy-start(f32[384,128]{1,0:T(8,128)} %copy-done.41) | copy-start | bytes 589828
  122.3 27.1 %copy-start.45 = (f32[384,128]{1,0:T(8,128)S(1)}, f32[384,128]{1,0:T(8,128)}, u32[]{:S(2)}) copy-start(f32[384,128]{1,0:T(8,128)} %copy-done.44) | copy-start | bytes 589828
  122.3 8.6 %collective-permute-start.15 = (f32[392,128]{1,0:T(8,128)S(1)}, f32[392,128]{1,0:T(8,128)S(1)}, u32[]{:S(2)}, u32[]{:S(2)}) collective-permute-start(f32[392,128]{1,0:T(8,128)S(1)} %pad_maximum_fusion.21), channel_id=1, source_target_pairs={{0,16},{1,17},{2,18},{3,19},{4,20},{5,21},{6,22},{7,23},{8,24},{9,... | collective-permute-start | bytes 602120 | tf_op jit(solution)/shard_map/ppermute | solution.py:101
  124.3 7.8 %collective-permute-start.19 = (f32[384,128]{1,0:T(8,128)S(1)}, f32[384,128]{1,0:T(8,128)S(1)}, u32[]{:S(2)}, u32[]{:S(2)}) collective-permute-start(f32[384,128]{1,0:T(8,128)S(1)} %slice.349), channel_id=1, source_target_pairs={{0,8},{1,5},{2,10},{3,7},{4,12},{5,1},{6,14},{7,3},{8,0},{9,13},{1... | collective-permute-start | bytes 589832 | tf_op jit(solution)/shard_map/ppermute | solution.py:101
  130.9 12.7 %collective-permute-start.16 = (f32[384,128]{1,0:T(8,128)S(1)}, f32[384,128]{1,0:T(8,128)S(1)}, u32[]{:S(2)}, u32[]{:S(2)}) collective-permute-start(f32[384,128]{1,0:T(8,128)S(1)} %slice_add_fusion.11), channel_id=1, source_target_pairs={{0,8},{1,5},{2,10},{3,7},{4,12},{5,1},{6,14},{7,3},{8,0},{9,13},{1... | collective-permute-start | bytes 589832 | tf_op jit(solution)/shard_map/ppermute | solution.py:101
  132.2 11.5 %collective-permute-start.20 = (f32[384,128]{1,0:T(8,128)S(1)}, f32[384,128]{1,0:T(8,128)S(1)}, u32[]{:S(2)}, u32[]{:S(2)}) collective-permute-start(f32[384,128]{1,0:T(8,128)S(1)} %slice_add_fusion.10), channel_id=1, source_target_pairs={{0,16},{1,17},{2,18},{3,19},{4,20},{5,21},{6,22},{7,23},{8,24},{9,... | collective-permute-start | bytes 589832 | tf_op jit(solution)/shard_map/ppermute | solution.py:101
  143.7 5.7 %collective-permute-start.21 = (f32[384,128]{1,0:T(8,128)S(1)}, f32[384,128]{1,0:T(8,128)S(1)}, u32[]{:S(2)}, u32[]{:S(2)}) collective-permute-start(f32[384,128]{1,0:T(8,128)S(1)} %add.349), channel_id=1, source_target_pairs={{0,8},{1,5},{2,10},{3,7},{4,12},{5,1},{6,14},{7,3},{8,0},{9,13},{1... | collective-permute-start | bytes 589832 | tf_op jit(solution)/shard_map/ppermute | solution.py:101
  149.6 7.8 %collective-permute-start.17 = (f32[768,128]{1,0:T(8,128)S(1)}, f32[768,128]{1,0:T(8,128)S(1)}, u32[]{:S(2)}, u32[]{:S(2)}) collective-permute-start(f32[768,128]{1,0:T(8,128)S(1)} %get-tuple-element.106), channel_id=1, source_target_pairs={{0,4},{1,9},{2,6},{3,11},{4,0},{5,13},{6,2},{7,15},{8,12},{9,1},{1... | collective-permute-start | bytes 1179656 | tf_op jit(solution)/shard_map/ppermute | solution.py:101
  157.5 7.8 %collective-permute-start.22 = (f32[768,128]{1,0:T(8,128)S(1)}, f32[768,128]{1,0:T(8,128)S(1)}, u32[]{:S(2)}, u32[]{:S(2)}) collective-permute-start(f32[768,128]{1,0:T(8,128)S(1)} %get-tuple-element.35), channel_id=1, source_target_pairs={{0,4},{1,9},{2,6},{3,11},{4,0},{5,13},{6,2},{7,15},{8,12},{9,1},{1... | collective-permute-start | bytes 1179656 | tf_op jit(solution)/shard_map/ppermute | solution.py:101
  174.1 2.0 collective-permute-start.23
  176.3 14.1 %collective-permute-start.24 = (f32[1032,128]{1,0:T(8,128)S(1)}, f32[1032,128]{1,0:T(8,128)S(1)}, u32[]{:S(2)}, u32[]{:S(2)}) collective-permute-start(f32[1032,128]{1,0:T(8,128)S(1)} %pad_maximum_fusion.5), channel_id=1, source_target_pairs={{0,2},{1,3},{2,0},{3,1},{4,6},{5,7},{6,4},{7,5},{8,10},{9,11},{10,... | collective-permute-start | bytes 1585160 | tf_op jit(solution)/shard_map/ppermute | solution.py:104
  191.1 2.0 collective-permute-start.25
  195.2 8.1 %collective-permute-start.26 = (f32[776,128]{1,0:T(8,128)}, f32[776,128]{1,0:T(8,128)}, u32[]{:S(2)}, u32[]{:S(2)}) collective-permute-start(f32[776,128]{1,0:T(8,128)} %pad_maximum_fusion.11), channel_id=1, source_target_pairs={{0,4},{1,9},{2,6},{3,11},{4,0},{5,13},{6,2},{7,15},{8,12},{9,1},{1... | collective-permute-start | bytes 1191944 | tf_op jit(solution)/shard_map/ppermute | solution.py:101
  207.4 7.7 %collective-permute-start.27 = (f32[392,128]{1,0:T(8,128)S(1)}, f32[392,128]{1,0:T(8,128)S(1)}, u32[]{:S(2)}, u32[]{:S(2)}) collective-permute-start(f32[392,128]{1,0:T(8,128)S(1)} %pad_maximum_fusion.22), channel_id=1, source_target_pairs={{0,8},{1,5},{2,10},{3,7},{4,12},{5,1},{6,14},{7,3},{8,0},{9,13},{1... | collective-permute-start | bytes 602120 | tf_op jit(solution)/shard_map/ppermute | solution.py:101
  208.5 8.1 %collective-permute-start.31 = (f32[768,128]{1,0:T(8,128)S(1)}, f32[768,128]{1,0:T(8,128)S(1)}, u32[]{:S(2)}, u32[]{:S(2)}) collective-permute-start(f32[768,128]{1,0:T(8,128)S(1)} %fusion.32), channel_id=1, source_target_pairs={{0,4},{1,9},{2,6},{3,11},{4,0},{5,13},{6,2},{7,15},{8,12},{9,1},{1... | collective-permute-start | bytes 1179656 | tf_op jit(solution)/shard_map/ppermute | solution.py:101
  215.8 21.4 %copy-start.32 = (f32[768,128]{1,0:T(8,128)S(1)}, f32[768,128]{1,0:T(8,128)}, u32[]{:S(2)}) copy-start(f32[768,128]{1,0:T(8,128)} %copy-done.31) | copy-start | bytes 1179652
  215.8 21.4 %copy-start.40 = (f32[384,128]{1,0:T(8,128)S(1)}, f32[384,128]{1,0:T(8,128)}, u32[]{:S(2)}) copy-start(f32[384,128]{1,0:T(8,128)} %copy-done.38) | copy-start | bytes 589828
  215.9 8.8 %collective-permute-start.28 = (f32[392,128]{1,0:T(8,128)S(1)}, f32[392,128]{1,0:T(8,128)S(1)}, u32[]{:S(2)}, u32[]{:S(2)}) collective-permute-start(f32[392,128]{1,0:T(8,128)S(1)} %pad_maximum_fusion.23), channel_id=1, source_target_pairs={{0,16},{1,17},{2,18},{3,19},{4,20},{5,21},{6,22},{7,23},{8,24},{9,... | collective-permute-start | bytes 602120 | tf_op jit(solution)/shard_map/ppermute | solution.py:101
  217.6 27.7 %copy-start.25 = (f32[768,128]{1,0:T(8,128)S(1)}, f32[768,128]{1,0:T(8,128)}, u32[]{:S(2)}) copy-start(f32[768,128]{1,0:T(8,128)} %get-tuple-element.57) | copy-start | bytes 1179652
  217.6 27.7 %copy-start.34 = (f32[768,128]{1,0:T(8,128)S(1)}, f32[768,128]{1,0:T(8,128)}, u32[]{:S(2)}) copy-start(f32[768,128]{1,0:T(8,128)} %copy-done.33) | copy-start | bytes 1179652
  217.6 27.7 %copy-start.37 = (f32[384,128]{1,0:T(8,128)S(1)}, f32[384,128]{1,0:T(8,128)}, u32[]{:S(2)}) copy-start(f32[384,128]{1,0:T(8,128)} %copy-done.35) | copy-start | bytes 589828
  217.6 27.7 %copy-start.43 = (f32[384,128]{1,0:T(8,128)S(1)}, f32[384,128]{1,0:T(8,128)}, u32[]{:S(2)}) copy-start(f32[384,128]{1,0:T(8,128)} %copy-done.41) | copy-start | bytes 589828
  217.7 9.8 %collective-permute-start.32 = (f32[384,128]{1,0:T(8,128)S(1)}, f32[384,128]{1,0:T(8,128)S(1)}, u32[]{:S(2)}, u32[]{:S(2)}) collective-permute-start(f32[384,128]{1,0:T(8,128)S(1)} %slice.377), channel_id=1, source_target_pairs={{0,8},{1,5},{2,10},{3,7},{4,12},{5,1},{6,14},{7,3},{8,0},{9,13},{1... | collective-permute-start | bytes 589832 | tf_op jit(solution)/shard_map/ppermute | solution.py:101
  226.7 10.6 %collective-permute-start.29 = (f32[384,128]{1,0:T(8,128)S(1)}, f32[384,128]{1,0:T(8,128)S(1)}, u32[]{:S(2)}, u32[]{:S(2)}) collective-permute-start(f32[384,128]{1,0:T(8,128)S(1)} %slice_add_fusion.8), channel_id=1, source_target_pairs={{0,8},{1,5},{2,10},{3,7},{4,12},{5,1},{6,14},{7,3},{8,0},{9,13},{1... | collective-permute-start | bytes 589832 | tf_op jit(solution)/shard_map/ppermute | solution.py:101
  227.5 11.1 %collective-permute-start.33 = (f32[384,128]{1,0:T(8,128)S(1)}, f32[384,128]{1,0:T(8,128)S(1)}, u32[]{:S(2)}, u32[]{:S(2)}) collective-permute-start(f32[384,128]{1,0:T(8,128)S(1)} %slice_add_fusion.7), channel_id=1, source_target_pairs={{0,16},{1,17},{2,18},{3,19},{4,20},{5,21},{6,22},{7,23},{8,24},{9,... | collective-permute-start | bytes 589832 | tf_op jit(solution)/shard_map/ppermute | solution.py:101
  237.5 7.8 %collective-permute-start.30 = (f32[768,128]{1,0:T(8,128)S(1)}, f32[768,128]{1,0:T(8,128)S(1)}, u32[]{:S(2)}, u32[]{:S(2)}) collective-permute-start(f32[768,128]{1,0:T(8,128)S(1)} %get-tuple-element.91), channel_id=1, source_target_pairs={{0,4},{1,9},{2,6},{3,11},{4,0},{5,13},{6,2},{7,15},{8,12},{9,1},{1... | collective-permute-start | bytes 1179656 | tf_op jit(solution)/shard_map/ppermute | solution.py:101
  238.7 6.3 %collective-permute-start.34 = (f32[384,128]{1,0:T(8,128)S(1)}, f32[384,128]{1,0:T(8,128)S(1)}, u32[]{:S(2)}, u32[]{:S(2)}) collective-permute-start(f32[384,128]{1,0:T(8,128)S(1)} %add.377), channel_id=1, source_target_pairs={{0,8},{1,5},{2,10},{3,7},{4,12},{5,1},{6,14},{7,3},{8,0},{9,13},{1... | collective-permute-start | bytes 589832 | tf_op jit(solution)/shard_map/ppermute | solution.py:101
  245.8 7.8 %collective-permute-start.35 = (f32[768,128]{1,0:T(8,128)S(1)}, f32[768,128]{1,0:T(8,128)S(1)}, u32[]{:S(2)}, u32[]{:S(2)}) collective-permute-start(f32[768,128]{1,0:T(8,128)S(1)} %get-tuple-element.40), channel_id=1, source_target_pairs={{0,4},{1,9},{2,6},{3,11},{4,0},{5,13},{6,2},{7,15},{8,12},{9,1},{1... | collective-permute-start | bytes 1179656 | tf_op jit(solution)/shard_map/ppermute | solution.py:101
  (53 other events, 375.1 us)

commit v4 on v3

--- a/solution.py
+++ b/solution.py
@@ -8,7 +8,8 @@
 CB_DEV = 24
 ITERS = 2
 TILE = 128
-ROW_STREAMS = (12, 12)
+PIECE = 4
+ROW_STREAMS = (4, 2)
 COL_STREAMS = (16,)
 
 tiny_eps = 1e-06
@@ -58,16 +59,13 @@
     )(slots, flip, kernel)
 
 
-def after(value, other):
-    return lax.optimization_barrier((value, other))[0]
-
-
 def column_norm(pieces, unit):
     parts = []
     for piece in pieces:
-        squares = (piece * piece).reshape(-1, unit, piece.shape[-1])
-        sums = jnp.sum(squares, axis=1)
+        blocks = piece.reshape(-1, TILE, piece.shape[-1])
+        sums = jnp.sum(blocks * blocks, axis=1)
         parts += [sums[i] for i in range(sums.shape[0])]
+    parts = [sum(parts[i + 1 : i + unit], parts[i]) for i in range(0, len(parts), unit)]
     while len(parts) > 1:
         paired = [parts[i] + parts[i + 1] for i in range(0, len(parts) - 1, 2)]
         parts = paired + parts[len(parts) - len(parts) % 2 :]
@@ -86,17 +84,24 @@
         return (index >> bit) & 1
 
     core = side(col_index, 0)
-    orders = [row_bits, [row_bits[1], row_bits[0], *row_bits[2:]]]
-    outer_side, inner_side = (
-        jnp.where(core == 0, side(row_index, orders[0][level]), side(row_index, orders[1][level]))
-        for level in range(2)
-    )
-
-    def swap_rows(value, level):
+    first, second, third, *more = row_bits
+    orders = [
+        [[first, second, third, *more], [second, first, third, *more]],
+        [[first, third, second, *more], [third, first, second, *more]],
+    ]
+    sides = [
+        [
+            jnp.where(core == 0, side(row_index, by_core[0][level]), side(row_index, by_core[1][level]))
+            for level in range(2)
+        ]
+        for by_core in orders
+    ]
+
+    def swap_rows(value, stream, level):
         pairs = []
         for row in range(row_count):
             for col in range(col_count):
-                partner = row ^ (1 << orders[col & 1][level])
+                partner = row ^ (1 << orders[stream][col & 1][level])
                 pairs.append((row * col_count + col, partner * col_count + col))
         return lax.ppermute(value, ("rows", "cols"), pairs)
 
@@ -105,7 +110,8 @@
 
     position_of = []
     start = 0
-    for blocks in ROW_STREAMS:
+    for pieces, (outer_side, inner_side) in zip(ROW_STREAMS, sides):
+        blocks = pieces * PIECE
         quarter = jnp.arange(blocks) // (blocks // 4)
         rest = jnp.arange(blocks) % (blocks // 4)
         mask = (1 - outer_side) * 2 + (1 - inner_side)
@@ -117,7 +123,7 @@
     alive = jnp.arange(slot_count)[None, :] < counts
     hits = (pattern[:, :, None] == block_at[None, None, :]) & alive[:, :, None]
     slots = jnp.sum(hits * (jnp.arange(slot_count) + 1)[None, :, None], axis=1) - 1
-    widths = [half for blocks in ROW_STREAMS for half in (blocks // 2, blocks // 2)]
+    widths = [PIECE] * sum(ROW_STREAMS)
     dense = fill_dense(
         kernel,
         slots.reshape(-1).astype(jnp.int32),
@@ -135,42 +141,58 @@
         left_pieces += [jnp.where(kept_first, high, low), jnp.where(kept_first, low, high)]
         start += 2 * half
 
-    def staggered(sends, norm, swap):
-        got = []
-        for s, send in enumerate(sends):
-            if s > 0:
-                send = after(send, got[s - 1])
-            elif norm is not None:
-                send = jnp.concatenate([send, norm])
-            got.append(swap(send))
-        if norm is not None:
-            split = sends[0].shape[0]
-            norm = norm + got[0][split:]
-            got[0] = got[0][:split]
-        return got, norm
-
-    def reduce_rows(partials, norm):
-        sends, keeps = [list(part) for part in zip(*partials)]
-        for level in range(len(row_bits)):
-            got, norm = staggered(sends, norm, lambda value: swap_rows(value, level))
-            keeps = [keep + other for keep, other in zip(keeps, got)]
-            if level == 0:
-                halves = [keep.shape[0] // 2 for keep in keeps]
-                sends = [keep[:half] for keep, half in zip(keeps, halves)]
-                keeps = [keep[half:] for keep, half in zip(keeps, halves)]
+    def swap_normed(value, norm, swap):
+        got = swap(jnp.concatenate([value, norm]))
+        return got[: value.shape[0]], norm + got[value.shape[0] :]
+
+    def reduce_rows(products, norm):
+        streams = []
+        start = 0
+        for pieces in ROW_STREAMS:
+            half = pieces // 2
+            streams.append(
+                [jnp.concatenate(products[start : start + half]), products[start + half : start + pieces]]
+            )
+            start += pieces
+        keeps = []
+        for s, (send, keep) in enumerate(streams):
+            if s == 0:
+                got, norm = swap_normed(send, norm, lambda value: swap_rows(value, 0, 0))
             else:
-                sends = keeps
-        inner, _ = staggered(keeps, None, lambda value: swap_rows(value, 1))
-        own = [jnp.concatenate(pair) for pair in zip(inner, keeps)]
-        outer, _ = staggered(own, None, lambda value: swap_rows(value, 0))
-        return [piece for pair in zip(outer, own) for piece in pair], norm[0]
+                got = swap_rows(send, s, 0)
+            keep = jnp.concatenate(keep) + got
+            half = keep.shape[0] // 2
+            keeps.append((keep[:half], keep[half:]))
+        for level in range(1, len(row_bits)):
+            for s, (send, keep) in enumerate(keeps):
+                if s == 0:
+                    got, norm = swap_normed(send, norm, lambda value: swap_rows(value, 0, level))
+                else:
+                    got = swap_rows(send, s, level)
+                keeps[s] = (keep + got, keep + got)
+        own = []
+        for s, (keep, _) in enumerate(keeps):
+            own.append([swap_rows(keep, s, 1), keep])
+        pieces = []
+        for s, pair in enumerate(own):
+            own_all = jnp.concatenate(pair)
+            both = jnp.concatenate([swap_rows(own_all, s, 0), own_all])
+            step = both.shape[0] // ROW_STREAMS[s]
+            pieces += [both[i * step : (i + 1) * step] for i in range(ROW_STREAMS[s])]
+        return pieces, norm[0]
 
     def reduce_cols(partials, norm):
         sends, keeps = partials[0::2], partials[1::2]
         for level in range(len(col_bits)):
-            got, norm = staggered(sends, norm, lambda value: swap_cols(value, level))
+            got = []
+            for s, send in enumerate(sends):
+                if s == 0:
+                    other, norm = swap_normed(send, norm, lambda value: swap_cols(value, level))
+                else:
+                    other = swap_cols(send, level)
+                got.append(other)
             sends = keeps = [keep + other for keep, other in zip(keeps, got)]
-        other, _ = staggered(keeps, None, lambda value: swap_cols(value, 0))
+        other = [swap_cols(keep, 0) for keep in keeps]
         return [piece for pair in zip(other, keeps) for piece in pair], norm[0]
 
     def spread(norm):
@@ -184,8 +206,8 @@
             )
             for chunk in dense
         ]
-        partials = list(zip(products[0::2], products[1::2]))
-        summed, squares = reduce_rows(partials, spread(column_norm(left_raw, left_raw[0].shape[0])))
+        squares = column_norm(left_raw, left_raw[0].shape[0] // TILE)
+        summed, squares = reduce_rows(products, spread(squares))
         beta_norm = jnp.sqrt(squares + tiny_eps)
         right_raw = [
             total / beta_norm - beta_norm * prev for total, prev in zip(summed, right_prev)
@@ -216,7 +238,7 @@
     radius = beta_first
     for iteration in range(ITERS):
         fore_summed, fore_squares = reduce_cols(
-            fore_products(right_raw), spread(column_norm(right_raw, right_raw[0].shape[0] // 2))
+            fore_products(right_raw), spread(column_norm(right_raw, ROW_STREAMS[1] * PIECE // 4))
         )
         alpha_norm = jnp.sqrt(fore_squares + tiny_eps)
         left_raw = [
@@ -242,13 +264,16 @@
 
     def in_block_order(pieces):
         out = []
-        for outer, own in zip(pieces[0::2], pieces[1::2]):
-            half = outer.shape[0] // 2
-            outer, own = (
-                jnp.where(inner_side == 1, v, jnp.concatenate([v[half:], v[:half]]))
-                for v in (outer, own)
-            )
-            out += [jnp.where(outer_side == 1, outer, own), jnp.where(outer_side == 1, own, outer)]
+        start = 0
+        for count, (outer_side, inner_side) in zip(ROW_STREAMS, sides):
+            whole = jnp.concatenate(pieces[start : start + count])
+            quarter = whole.shape[0] // 4
+            parts = [whole[i * quarter : (i + 1) * quarter] for i in range(4)]
+            straight = inner_side == 1
+            parts = [jnp.where(straight, parts[i], parts[i ^ 1]) for i in range(4)]
+            straight = outer_side == 1
+            out += [jnp.where(straight, parts[i], parts[i ^ 2]) for i in range(4)]
+            start += count
         return jnp.concatenate(out)
 
     return (in_block_order(model), in_block_order(gradient), misfit)

time: 257 us -> 231 us (0.90)
  other arithmetic: 24.5 us -> 11 us
  matrix products: 30.6 us -> 22.4 us
  starting transfers between devices: 43.3 us -> 38.1 us
  waiting for transfers between devices: 142 us -> 146 us
  local copies, waits for them, and re-layouts: 7.64 us -> 4.79 us
    dot_general x8 -> x12, matrix products: 16.1 us -> 8.5 us  [fore_products(): jnp.dot(chunk, piece.astype(jnp.bfloat16), preferred_element_type=jnp.flo...]
    reduce_sum x11 -> x8, other arithmetic: 8.19 us -> 1 us  [column_norm(): sums = jnp.sum(blocks * blocks, axis=1)]
    ppermute x30, waiting for transfers between devices: 109 us -> 114 us  [swap_rows(): return lax.ppermute(value, ('rows', 'cols'), pairs)]
    ppermute x30, starting transfers between devices: 38.7 us -> 34.6 us  [swap_rows(): return lax.ppermute(value, ('rows', 'cols'), pairs)]
    unnamed x130 -> x10, local copies, waits for them, and re-layouts: 7.16 us -> 4.53 us
    dot_general x12 -> x18, matrix products: 14.5 us -> 13.9 us  [back_step(): lax.dot_general(chunk, left_bf, (((0,), (0,)), ((), ())), preferred_eleme...]
where the time goes in v4:
time: 231 us
  waiting for transfers between devices  146 us (63%)
  starting transfers between devices  38.1 us (16%)
  matrix products  22.4 us (10%)
  other arithmetic  11 us (5%)
  Pallas kernels  6.77 us (3%)
  local copies, waits for them, and re-layouts  4.79 us (2%)
    ppermute x30, waiting for transfers between devices, swap_rows(): return lax.ppermute(value, ('rows', 'cols'), pairs)  114 us
    ppermute x30, starting transfers between devices, swap_rows(): return lax.ppermute(value, ('rows', 'cols'), pairs)  34.6 us
    ppermute x6, waiting for transfers between devices, swap_cols(): lax.ppermute(value, 'cols', [(i, i ^ 1 << level) for i in range(col_count)])  32.5 us
    dot_general x18, matrix products, back_step(): lax.dot_general(chunk, left_bf, (((0,), (0,)), ((), ())), preferred_eleme...  13.9 us
    dot_general x12, matrix products, fore_products(): jnp.dot(chunk, piece.astype(jnp.bfloat16), preferred_element_type=jnp.flo...  8.5 us
    pallas_call x1, Pallas kernels, fill_dense(): pl.pallas_call(fill_kernel, grid_spec=pltpu.PrefetchScalarGridSpec(num_sc...  6.77 us
  transfers between devices with their start and end apart: 36, of which 30 were waited for; matrix products, arithmetic and copies ran while one was open for 8% of the time, Pallas kernels for 0%

profile of v4, /device:TPU:0, one launch (start us, length us, event | category | flops | bytes accessed | tf_op | source)
XLA Modules:
  0.0 230.9 jit_solution(5513456151140213839)
XLA Ops:
  2.5 1.3 fusion.76
  3.8 3.4 %copy-done = bf16[16,16,128,128]{3,2,1,0:T(8,128)(2,1)S(1)} copy-done((bf16[16,16,128,128]{3,2,1,0:T(8,128)(2,1)S(1)}, bf16[16,16,128,128]{3,2,1,0:T(8,128)(2,1)}, u32[]{:S(2)}) %copy-start) | copy-done | bytes 8388632
  7.2 6.8 %shard_map.70 = (bf16[2048,512]{1,0:T(8,128)(2,1)S(1)}, bf16[2048,512]{1,0:T(8,128)(2,1)S(1)}, bf16[2048,512]{1,0:T(8,128)(2,1)S(1)}, bf16[2048,512]{1,0:T(8,128...) custom-call(s32[384]{0:T(512)S(1)} %sub.127.slot_ref, s32[1]{0:T(128)} %bitcast.1.flip_ref, ...), custom_call_target="tpu_custom_call" | custom-call | tf_op jit(solution)/shard_map/pallas_call | solution.py:39
  15.7 2.7 %collective-permute-start = (f32[1032,128]{1,0:T(8,128)S(1)}, f32[1032,128]{1,0:T(8,128)S(1)}, u32[]{:S(2)}, u32[]{:S(2)}) collective-permute-start(f32[1032,128]{1,0:T(8,128)S(1)} %pad_maximum_fusion), channel_id=1, source_target_pairs={{0,4},{1,9},{2,6},{3,11},{4,0},{5,13},{6,2},{7,15},{8,12},{9,1},{1... | collective-permute-start | bytes 1585160 | tf_op jit(solution)/shard_map/ppermute | solution.py:106
  20.7 7.7 %collective-permute-done.5 = f32[512,128]{1,0:T(8,128)S(1)} collective-permute-done((f32[512,128]{1,0:T(8,128)S(1)}, f32[512,128]{1,0:T(8,128)S(1)}, u32[]{:S(2)}, u32[]{:S(2)}) %collective-permute-start.5) | collective-permute-done | bytes 262176 | tf_op jit(solution)/shard_map/ppermute | solution.py:106
  29.1 3.2 %collective-permute-start.6 = (f32[256,128]{1,0:T(8,128)S(1)}, f32[256,128]{1,0:T(8,128)S(1)}, u32[]{:S(2)}, u32[]{:S(2)}) collective-permute-start(f32[256,128]{1,0:T(8,128)S(1)} %slice.647), channel_id=1, source_target_pairs={{0,16},{1,5},{2,18},{3,7},{4,20},{5,1},{6,22},{7,3},{8,24},{9,13},... | collective-permute-start | bytes 393224 | tf_op jit(solution)/shard_map/ppermute | solution.py:106
  32.5 1.9 collective-permute-start.1
  35.3 2.5 %collective-permute-start.7 = (f32[256,128]{1,0:T(8,128)S(1)}, f32[256,128]{1,0:T(8,128)S(1)}, u32[]{:S(2)}, u32[]{:S(2)}) collective-permute-start(f32[256,128]{1,0:T(8,128)S(1)} %slice_add_fusion.15), channel_id=1, source_target_pairs={{0,8},{1,9},{2,10},{3,11},{4,12},{5,13},{6,14},{7,15},{8,0},{9,1},... | collective-permute-start | bytes 393224 | tf_op jit(solution)/shard_map/ppermute | solution.py:106
  37.8 4.7 %collective-permute-done.1 = f32[520,128]{1,0:T(8,128)S(1)} collective-permute-done((f32[520,128]{1,0:T(8,128)S(1)}, f32[520,128]{1,0:T(8,128)S(1)}, u32[]{:S(2)}, u32[]{:S(2)}) %collective-permute-start.1) | collective-permute-done | bytes 266272 | tf_op jit(solution)/shard_map/ppermute | solution.py:106
  42.6 1.3 collective-permute-start.2
  44.6 1.1 collective-permute-start.8
  45.7 15.3 %collective-permute-done.8 = f32[256,128]{1,0:T(8,128)S(1)} collective-permute-done((f32[256,128]{1,0:T(8,128)S(1)}, f32[256,128]{1,0:T(8,128)S(1)}, u32[]{:S(2)}, u32[]{:S(2)}) %collective-permute-start.8) | collective-permute-done | bytes 131104 | tf_op jit(solution)/shard_map/ppermute | solution.py:106
  61.0 1.1 collective-permute-start.9
  62.3 6.2 %collective-permute-done.3 = f32[512,128]{1,0:T(8,128)S(1)} collective-permute-done((f32[512,128]{1,0:T(8,128)S(1)}, f32[512,128]{1,0:T(8,128)S(1)}, u32[]{:S(2)}, u32[]{:S(2)}) %collective-permute-start.3) | collective-permute-done | bytes 262176 | tf_op jit(solution)/shard_map/ppermute | solution.py:106
  68.5 1.1 collective-permute-start.4
  71.1 6.7 %collective-permute-done.4 = f32[1024,128]{1,0:T(8,128)S(1)} collective-permute-done((f32[1024,128]{1,0:T(8,128)S(1)}, f32[1024,128]{1,0:T(8,128)S(1)}, u32[]{:S(2)}, u32[]{:S(2)}) %collective-permute-start.4) | collective-permute-done | bytes 524320 | tf_op jit(solution)/shard_map/ppermute | solution.py:106
  81.1 1.9 collective-permute-done.10
  83.1 1.6 collective-permute-start.11
  84.8 12.5 %collective-permute-done.11 = f32[1032,128]{1,0:T(8,128)S(1)} collective-permute-done((f32[1032,128]{1,0:T(8,128)S(1)}, f32[1032,128]{1,0:T(8,128)S(1)}, u32[]{:S(2)}, u32[]{:S(2)}) %collective-permute-start.11) | collective-permute-done | bytes 528416 | tf_op jit(solution)/shard_map/ppermute | solution.py:109
  97.6 1.8 collective-permute-done.12
  102.0 1.1 collective-permute-start.18
  103.2 1.0 collective-permute-start.13
  105.7 8.3 %collective-permute-done.13 = f32[1032,128]{1,0:T(8,128)S(1)} collective-permute-done((f32[1032,128]{1,0:T(8,128)S(1)}, f32[1032,128]{1,0:T(8,128)S(1)}, u32[]{:S(2)}, u32[]{:S(2)}) %collective-permute-start.13) | collective-permute-done | bytes 528416 | tf_op jit(solution)/shard_map/ppermute | solution.py:106
  115.2 3.5 %collective-permute-start.19 = (f32[256,128]{1,0:T(8,128)S(1)}, f32[256,128]{1,0:T(8,128)S(1)}, u32[]{:S(2)}, u32[]{:S(2)}) collective-permute-start(f32[256,128]{1,0:T(8,128)S(1)} %slice.665), channel_id=1, source_target_pairs={{0,16},{1,5},{2,18},{3,7},{4,20},{5,1},{6,22},{7,3},{8,24},{9,13},... | collective-permute-start | bytes 393224 | tf_op jit(solution)/shard_map/ppermute | solution.py:106
  118.7 3.3 %collective-permute-done.14 = f32[520,128]{1,0:T(8,128)S(1)} collective-permute-done((f32[520,128]{1,0:T(8,128)S(1)}, f32[520,128]{1,0:T(8,128)S(1)}, u32[]{:S(2)}, u32[]{:S(2)}) %collective-permute-start.14) | collective-permute-done | bytes 266272 | tf_op jit(solution)/shard_map/ppermute | solution.py:106
  122.1 1.2 collective-permute-start.15
  123.4 2.5 %collective-permute-start.20 = (f32[256,128]{1,0:T(8,128)S(1)}, f32[256,128]{1,0:T(8,128)S(1)}, u32[]{:S(2)}, u32[]{:S(2)}) collective-permute-start(f32[256,128]{1,0:T(8,128)S(1)} %slice_add_fusion.14), channel_id=1, source_target_pairs={{0,8},{1,9},{2,10},{3,11},{4,12},{5,13},{6,14},{7,15},{8,0},{9,1},... | collective-permute-start | bytes 393224 | tf_op jit(solution)/shard_map/ppermute | solution.py:106
  125.9 3.9 %collective-permute-done.20 = f32[256,128]{1,0:T(8,128)S(1)} collective-permute-done((f32[256,128]{1,0:T(8,128)S(1)}, f32[256,128]{1,0:T(8,128)S(1)}, u32[]{:S(2)}, u32[]{:S(2)}) %collective-permute-start.20) | collective-permute-done | bytes 131104 | tf_op jit(solution)/shard_map/ppermute | solution.py:106
  129.8 2.9 %collective-permute-start.21 = (f32[256,128]{1,0:T(8,128)S(1)}, f32[256,128]{1,0:T(8,128)S(1)}, u32[]{:S(2)}, u32[]{:S(2)}) collective-permute-start(f32[256,128]{1,0:T(8,128)S(1)} %add.725), channel_id=1, source_target_pairs={{0,16},{1,5},{2,18},{3,7},{4,20},{5,1},{6,22},{7,3},{8,24},{9,13},... | collective-permute-start | bytes 393224 | tf_op jit(solution)/shard_map/ppermute | solution.py:106
  132.7 2.2 collective-permute-done.15
  135.1 1.2 collective-permute-done.21
  137.0 8.0 %collective-permute-done.16 = f32[512,128]{1,0:T(8,128)S(1)} collective-permute-done((f32[512,128]{1,0:T(8,128)S(1)}, f32[512,128]{1,0:T(8,128)S(1)}, u32[]{:S(2)}, u32[]{:S(2)}) %collective-permute-start.16) | collective-permute-done | bytes 262176 | tf_op jit(solution)/shard_map/ppermute | solution.py:106
  146.6 7.7 %collective-permute-done.17 = f32[1024,128]{1,0:T(8,128)S(1)} collective-permute-done((f32[1024,128]{1,0:T(8,128)S(1)}, f32[1024,128]{1,0:T(8,128)S(1)}, u32[]{:S(2)}, u32[]{:S(2)}) %collective-permute-start.17) | collective-permute-done | bytes 524320 | tf_op jit(solution)/shard_map/ppermute | solution.py:106
  157.8 1.9 collective-permute-done.23
  159.8 1.6 collective-permute-start.24
  161.4 12.5 %collective-permute-done.24 = f32[1032,128]{1,0:T(8,128)S(1)} collective-permute-done((f32[1032,128]{1,0:T(8,128)S(1)}, f32[1032,128]{1,0:T(8,128)S(1)}, u32[]{:S(2)}, u32[]{:S(2)}) %collective-permute-start.24) | collective-permute-done | bytes 528416 | tf_op jit(solution)/shard_map/ppermute | solution.py:109
  174.2 1.8 collective-permute-done.25
  178.6 2.0 collective-permute-start.31
  182.4 5.5 %collective-permute-done.26 = f32[1032,128]{1,0:T(8,128)S(1)} collective-permute-done((f32[1032,128]{1,0:T(8,128)S(1)}, f32[1032,128]{1,0:T(8,128)S(1)}, u32[]{:S(2)}, u32[]{:S(2)}) %collective-permute-start.26) | collective-permute-done | bytes 528416 | tf_op jit(solution)/shard_map/ppermute | solution.py:106
  188.0 2.6 %collective-permute-done.31 = f32[512,128]{1,0:T(8,128)S(1)} collective-permute-done((f32[512,128]{1,0:T(8,128)S(1)}, f32[512,128]{1,0:T(8,128)S(1)}, u32[]{:S(2)}, u32[]{:S(2)}) %collective-permute-start.31) | collective-permute-done | bytes 262176 | tf_op jit(solution)/shard_map/ppermute | solution.py:106
  191.5 2.9 %collective-permute-done.27 = f32[520,128]{1,0:T(8,128)S(1)} collective-permute-done((f32[520,128]{1,0:T(8,128)S(1)}, f32[520,128]{1,0:T(8,128)S(1)}, u32[]{:S(2)}, u32[]{:S(2)}) %collective-permute-start.27) | collective-permute-done | bytes 266272 | tf_op jit(solution)/shard_map/ppermute | solution.py:106
  195.7 2.1 collective-permute-done.32
  197.9 7.4 %collective-permute-done.33 = f32[256,128]{1,0:T(8,128)S(1)} collective-permute-done((f32[256,128]{1,0:T(8,128)S(1)}, f32[256,128]{1,0:T(8,128)S(1)}, u32[]{:S(2)}, u32[]{:S(2)}) %collective-permute-start.33) | collective-permute-done | bytes 131104 | tf_op jit(solution)/shard_map/ppermute | solution.py:106
  205.3 3.1 %collective-permute-start.34 = (f32[256,128]{1,0:T(8,128)S(1)}, f32[256,128]{1,0:T(8,128)S(1)}, u32[]{:S(2)}, u32[]{:S(2)}) collective-permute-start(f32[256,128]{1,0:T(8,128)S(1)} %add.775), channel_id=1, source_target_pairs={{0,16},{1,5},{2,18},{3,7},{4,20},{5,1},{6,22},{7,3},{8,24},{9,13},... | collective-permute-start | bytes 393224 | tf_op jit(solution)/shard_map/ppermute | solution.py:106
  208.4 2.3 collective-permute-done.28
  215.6 4.3 %collective-permute-done.29 = f32[512,128]{1,0:T(8,128)S(1)} collective-permute-done((f32[512,128]{1,0:T(8,128)S(1)}, f32[512,128]{1,0:T(8,128)S(1)}, u32[]{:S(2)}, u32[]{:S(2)}) %collective-permute-start.29) | collective-permute-done | bytes 262176 | tf_op jit(solution)/shard_map/ppermute | solution.py:106
  220.4 8.8 %collective-permute-done.30 = f32[1024,128]{1,0:T(8,128)S(1)} collective-permute-done((f32[1024,128]{1,0:T(8,128)S(1)}, f32[1024,128]{1,0:T(8,128)S(1)}, u32[]{:S(2)}, u32[]{:S(2)}) %collective-permute-start.30) | collective-permute-done | bytes 524320 | tf_op jit(solution)/shard_map/ppermute | solution.py:106
  229.8 1.1 copy-done.3
  (177 shorter events, 37.6 us)
Async XLA Ops:
  3.8 3.4 %copy-start = (bf16[16,16,128,128]{3,2,1,0:T(8,128)(2,1)S(1)}, bf16[16,16,128,128]{3,2,1,0:T(8,128)(2,1)}, u32[]{:S(2)}) copy-start(bf16[16,16,128,128]{3,2,1,0:T(8,128)(2,1)} %tile_ref.1) | copy-start | bytes 25165828
  15.7 16.7 %collective-permute-start = (f32[1032,128]{1,0:T(8,128)S(1)}, f32[1032,128]{1,0:T(8,128)S(1)}, u32[]{:S(2)}, u32[]{:S(2)}) collective-permute-start(f32[1032,128]{1,0:T(8,128)S(1)} %pad_maximum_fusion), channel_id=1, source_target_pairs={{0,4},{1,9},{2,6},{3,11},{4,0},{5,13},{6,2},{7,15},{8,12},{9,1},{1... | collective-permute-start | bytes 1585160 | tf_op jit(solution)/shard_map/ppermute | solution.py:106
  19.1 9.3 %collective-permute-start.5 = (f32[512,128]{1,0:T(8,128)S(1)}, f32[512,128]{1,0:T(8,128)S(1)}, u32[]{:S(2)}, u32[]{:S(2)}) collective-permute-start(f32[512,128]{1,0:T(8,128)S(1)} %fusion.60), channel_id=1, source_target_pairs={{0,4},{1,17},{2,6},{3,19},{4,0},{5,21},{6,2},{7,23},{8,12},{9,25},... | collective-permute-start | bytes 786440 | tf_op jit(solution)/shard_map/ppermute | solution.py:106
  29.1 6.2 %collective-permute-start.6 = (f32[256,128]{1,0:T(8,128)S(1)}, f32[256,128]{1,0:T(8,128)S(1)}, u32[]{:S(2)}, u32[]{:S(2)}) collective-permute-start(f32[256,128]{1,0:T(8,128)S(1)} %slice.647), channel_id=1, source_target_pairs={{0,16},{1,5},{2,18},{3,7},{4,20},{5,1},{6,22},{7,3},{8,24},{9,13},... | collective-permute-start | bytes 393224 | tf_op jit(solution)/shard_map/ppermute | solution.py:106
  32.5 10.0 %collective-permute-start.1 = (f32[520,128]{1,0:T(8,128)S(1)}, f32[520,128]{1,0:T(8,128)S(1)}, u32[]{:S(2)}, u32[]{:S(2)}) collective-permute-start(f32[520,128]{1,0:T(8,128)S(1)} %pad_maximum_fusion.13), channel_id=1, source_target_pairs={{0,8},{1,5},{2,10},{3,7},{4,12},{5,1},{6,14},{7,3},{8,0},{9,13},{1... | collective-permute-start | bytes 798728 | tf_op jit(solution)/shard_map/ppermute | solution.py:106
  35.3 9.3 %collective-permute-start.7 = (f32[256,128]{1,0:T(8,128)S(1)}, f32[256,128]{1,0:T(8,128)S(1)}, u32[]{:S(2)}, u32[]{:S(2)}) collective-permute-start(f32[256,128]{1,0:T(8,128)S(1)} %slice_add_fusion.15), channel_id=1, source_target_pairs={{0,8},{1,9},{2,10},{3,11},{4,12},{5,13},{6,14},{7,15},{8,0},{9,1},... | collective-permute-start | bytes 393224 | tf_op jit(solution)/shard_map/ppermute | solution.py:106
  42.6 19.5 %collective-permute-start.2 = (f32[520,128]{1,0:T(8,128)S(1)}, f32[520,128]{1,0:T(8,128)S(1)}, u32[]{:S(2)}, u32[]{:S(2)}) collective-permute-start(f32[520,128]{1,0:T(8,128)S(1)} %pad_maximum_fusion.14), channel_id=1, source_target_pairs={{0,16},{1,17},{2,18},{3,19},{4,20},{5,21},{6,22},{7,23},{8,24},{9,... | collective-permute-start | bytes 798728 | tf_op jit(solution)/shard_map/ppermute | solution.py:106
  44.6 16.4 %collective-permute-start.8 = (f32[256,128]{1,0:T(8,128)S(1)}, f32[256,128]{1,0:T(8,128)S(1)}, u32[]{:S(2)}, u32[]{:S(2)}) collective-permute-start(f32[256,128]{1,0:T(8,128)S(1)} %add.666), channel_id=1, source_target_pairs={{0,16},{1,5},{2,18},{3,7},{4,20},{5,1},{6,22},{7,3},{8,24},{9,13},... | collective-permute-start | bytes 393224 | tf_op jit(solution)/shard_map/ppermute | solution.py:106
  61.0 19.0 %collective-permute-start.9 = (f32[512,128]{1,0:T(8,128)S(1)}, f32[512,128]{1,0:T(8,128)S(1)}, u32[]{:S(2)}, u32[]{:S(2)}) collective-permute-start(f32[512,128]{1,0:T(8,128)S(1)} %pad_maximum_fusion.19), channel_id=1, source_target_pairs={{0,4},{1,17},{2,6},{3,19},{4,0},{5,21},{6,2},{7,23},{8,12},{9,25},... | collective-permute-start | bytes 786440 | tf_op jit(solution)/shard_map/ppermute | solution.py:106
  62.1 6.4 %collective-permute-start.3 = (f32[512,128]{1,0:T(8,128)S(1)}, f32[512,128]{1,0:T(8,128)S(1)}, u32[]{:S(2)}, u32[]{:S(2)}) collective-permute-start(f32[512,128]{1,0:T(8,128)S(1)} %slice_add_fusion.11), channel_id=1, source_target_pairs={{0,8},{1,5},{2,10},{3,7},{4,12},{5,1},{6,14},{7,3},{8,0},{9,13},{1... | collective-permute-start | bytes 786440 | tf_op jit(solution)/shard_map/ppermute | solution.py:106
  68.5 9.2 %collective-permute-start.4 = (f32[1024,128]{1,0:T(8,128)S(1)}, f32[1024,128]{1,0:T(8,128)S(1)}, u32[]{:S(2)}, u32[]{:S(2)}) collective-permute-start(f32[1024,128]{1,0:T(8,128)S(1)} %pad_maximum_fusion.8), channel_id=1, source_target_pairs={{0,4},{1,9},{2,6},{3,11},{4,0},{5,13},{6,2},{7,15},{8,12},{9,1},{1... | collective-permute-start | bytes 1572872 | tf_op jit(solution)/shard_map/ppermute | solution.py:106
  81.0 2.0 collective-permute-start.10
  83.1 14.1 %collective-permute-start.11 = (f32[1032,128]{1,0:T(8,128)S(1)}, f32[1032,128]{1,0:T(8,128)S(1)}, u32[]{:S(2)}, u32[]{:S(2)}) collective-permute-start(f32[1032,128]{1,0:T(8,128)S(1)} %pad_maximum_fusion.2), channel_id=1, source_target_pairs={{0,2},{1,3},{2,0},{3,1},{4,6},{5,7},{6,4},{7,5},{8,10},{9,11},{10,... | collective-permute-start | bytes 1585160 | tf_op jit(solution)/shard_map/ppermute | solution.py:109
  97.4 2.0 collective-permute-start.12
  102.0 12.5 %collective-permute-start.18 = (f32[512,128]{1,0:T(8,128)S(1)}, f32[512,128]{1,0:T(8,128)S(1)}, u32[]{:S(2)}, u32[]{:S(2)}) collective-permute-start(f32[512,128]{1,0:T(8,128)S(1)} %fusion.55), channel_id=1, source_target_pairs={{0,4},{1,17},{2,6},{3,19},{4,0},{5,21},{6,2},{7,23},{8,12},{9,25},... | collective-permute-start | bytes 786440 | tf_op jit(solution)/shard_map/ppermute | solution.py:106
  103.2 10.9 %collective-permute-start.13 = (f32[1032,128]{1,0:T(8,128)S(1)}, f32[1032,128]{1,0:T(8,128)S(1)}, u32[]{:S(2)}, u32[]{:S(2)}) collective-permute-start(f32[1032,128]{1,0:T(8,128)S(1)} %pad_maximum_fusion.3), channel_id=1, source_target_pairs={{0,4},{1,9},{2,6},{3,11},{4,0},{5,13},{6,2},{7,15},{8,12},{9,1},{1... | collective-permute-start | bytes 1585160 | tf_op jit(solution)/shard_map/ppermute | solution.py:106
  114.2 7.9 %collective-permute-start.14 = (f32[520,128]{1,0:T(8,128)S(1)}, f32[520,128]{1,0:T(8,128)S(1)}, u32[]{:S(2)}, u32[]{:S(2)}) collective-permute-start(f32[520,128]{1,0:T(8,128)S(1)} %pad_maximum_fusion.15), channel_id=1, source_target_pairs={{0,8},{1,5},{2,10},{3,7},{4,12},{5,1},{6,14},{7,3},{8,0},{9,13},{1... | collective-permute-start | bytes 798728 | tf_op jit(solution)/shard_map/ppermute | solution.py:106
  115.2 8.1 %collective-permute-start.19 = (f32[256,128]{1,0:T(8,128)S(1)}, f32[256,128]{1,0:T(8,128)S(1)}, u32[]{:S(2)}, u32[]{:S(2)}) collective-permute-start(f32[256,128]{1,0:T(8,128)S(1)} %slice.665), channel_id=1, source_target_pairs={{0,16},{1,5},{2,18},{3,7},{4,20},{5,1},{6,22},{7,3},{8,24},{9,13},... | collective-permute-start | bytes 393224 | tf_op jit(solution)/shard_map/ppermute | solution.py:106
  122.1 12.8 %collective-permute-start.15 = (f32[520,128]{1,0:T(8,128)S(1)}, f32[520,128]{1,0:T(8,128)S(1)}, u32[]{:S(2)}, u32[]{:S(2)}) collective-permute-start(f32[520,128]{1,0:T(8,128)S(1)} %pad_maximum_fusion.16), channel_id=1, source_target_pairs={{0,16},{1,17},{2,18},{3,19},{4,20},{5,21},{6,22},{7,23},{8,24},{9,... | collective-permute-start | bytes 798728 | tf_op jit(solution)/shard_map/ppermute | solution.py:106
  123.4 6.4 %collective-permute-start.20 = (f32[256,128]{1,0:T(8,128)S(1)}, f32[256,128]{1,0:T(8,128)S(1)}, u32[]{:S(2)}, u32[]{:S(2)}) collective-permute-start(f32[256,128]{1,0:T(8,128)S(1)} %slice_add_fusion.14), channel_id=1, source_target_pairs={{0,8},{1,9},{2,10},{3,11},{4,12},{5,13},{6,14},{7,15},{8,0},{9,1},... | collective-permute-start | bytes 393224 | tf_op jit(solution)/shard_map/ppermute | solution.py:106
  129.8 6.5 %collective-permute-start.21 = (f32[256,128]{1,0:T(8,128)S(1)}, f32[256,128]{1,0:T(8,128)S(1)}, u32[]{:S(2)}, u32[]{:S(2)}) collective-permute-start(f32[256,128]{1,0:T(8,128)S(1)} %add.725), channel_id=1, source_target_pairs={{0,16},{1,5},{2,18},{3,7},{4,20},{5,1},{6,22},{7,3},{8,24},{9,13},... | collective-permute-start | bytes 393224 | tf_op jit(solution)/shard_map/ppermute | solution.py:106
  135.0 10.0 %collective-permute-start.16 = (f32[512,128]{1,0:T(8,128)S(1)}, f32[512,128]{1,0:T(8,128)S(1)}, u32[]{:S(2)}, u32[]{:S(2)}) collective-permute-start(f32[512,128]{1,0:T(8,128)S(1)} %get-tuple-element.45), channel_id=1, source_target_pairs={{0,8},{1,5},{2,10},{3,7},{4,12},{5,1},{6,14},{7,3},{8,0},{9,13},{1... | collective-permute-start | bytes 786440 | tf_op jit(solution)/shard_map/ppermute | solution.py:106
  136.4 10.2 %collective-permute-start.22 = (f32[512,128]{1,0:T(8,128)S(1)}, f32[512,128]{1,0:T(8,128)S(1)}, u32[]{:S(2)}, u32[]{:S(2)}) collective-permute-start(f32[512,128]{1,0:T(8,128)S(1)} %get-tuple-element.67), channel_id=1, source_target_pairs={{0,4},{1,17},{2,6},{3,19},{4,0},{5,21},{6,2},{7,23},{8,12},{9,25},... | collective-permute-start | bytes 786440 | tf_op jit(solution)/shard_map/ppermute | solution.py:106
  145.1 9.2 %collective-permute-start.17 = (f32[1024,128]{1,0:T(8,128)S(1)}, f32[1024,128]{1,0:T(8,128)S(1)}, u32[]{:S(2)}, u32[]{:S(2)}) collective-permute-start(f32[1024,128]{1,0:T(8,128)S(1)} %pad_maximum_fusion.10), channel_id=1, source_target_pairs={{0,4},{1,9},{2,6},{3,11},{4,0},{5,13},{6,2},{7,15},{8,12},{9,1},{1... | collective-permute-start | bytes 1572872 | tf_op jit(solution)/shard_map/ppermute | solution.py:106
  154.7 2.1 copy-start.1
  157.7 2.0 collective-permute-start.23
  159.8 14.1 %collective-permute-start.24 = (f32[1032,128]{1,0:T(8,128)S(1)}, f32[1032,128]{1,0:T(8,128)S(1)}, u32[]{:S(2)}, u32[]{:S(2)}) collective-permute-start(f32[1032,128]{1,0:T(8,128)S(1)} %pad_maximum_fusion.5), channel_id=1, source_target_pairs={{0,2},{1,3},{2,0},{3,1},{4,6},{5,7},{6,4},{7,5},{8,10},{9,11},{10,... | collective-permute-start | bytes 1585160 | tf_op jit(solution)/shard_map/ppermute | solution.py:109
  174.1 2.0 collective-permute-start.25
  178.5 9.3 %collective-permute-start.26 = (f32[1032,128]{1,0:T(8,128)S(1)}, f32[1032,128]{1,0:T(8,128)S(1)}, u32[]{:S(2)}, u32[]{:S(2)}) collective-permute-start(f32[1032,128]{1,0:T(8,128)S(1)} %pad_maximum_fusion.6), channel_id=1, source_target_pairs={{0,4},{1,9},{2,6},{3,11},{4,0},{5,13},{6,2},{7,15},{8,12},{9,1},{1... | collective-permute-start | bytes 1585160 | tf_op jit(solution)/shard_map/ppermute | solution.py:106
  178.6 12.0 %collective-permute-start.31 = (f32[512,128]{1,0:T(8,128)S(1)}, f32[512,128]{1,0:T(8,128)S(1)}, u32[]{:S(2)}, u32[]{:S(2)}) collective-permute-start(f32[512,128]{1,0:T(8,128)S(1)} %fusion.50), channel_id=1, source_target_pairs={{0,4},{1,17},{2,6},{3,19},{4,0},{5,21},{6,2},{7,23},{8,12},{9,25},... | collective-permute-start | bytes 786440 | tf_op jit(solution)/shard_map/ppermute | solution.py:106
  188.0 6.5 %collective-permute-start.27 = (f32[520,128]{1,0:T(8,128)S(1)}, f32[520,128]{1,0:T(8,128)S(1)}, u32[]{:S(2)}, u32[]{:S(2)}) collective-permute-start(f32[520,128]{1,0:T(8,128)S(1)} %pad_maximum_fusion.17), channel_id=1, source_target_pairs={{0,8},{1,5},{2,10},{3,7},{4,12},{5,1},{6,14},{7,3},{8,0},{9,13},{1... | collective-permute-start | bytes 798728 | tf_op jit(solution)/shard_map/ppermute | solution.py:106
  191.4 6.4 %collective-permute-start.32 = (f32[256,128]{1,0:T(8,128)S(1)}, f32[256,128]{1,0:T(8,128)S(1)}, u32[]{:S(2)}, u32[]{:S(2)}) collective-permute-start(f32[256,128]{1,0:T(8,128)S(1)} %slice.687), channel_id=1, source_target_pairs={{0,16},{1,5},{2,18},{3,7},{4,20},{5,1},{6,22},{7,3},{8,24},{9,13},... | collective-permute-start | bytes 393224 | tf_op jit(solution)/shard_map/ppermute | solution.py:106
  195.2 15.5 %collective-permute-start.28 = (f32[520,128]{1,0:T(8,128)}, f32[520,128]{1,0:T(8,128)}, u32[]{:S(2)}, u32[]{:S(2)}) collective-permute-start(f32[520,128]{1,0:T(8,128)} %pad_maximum_fusion.18), channel_id=1, source_target_pairs={{0,16},{1,17},{2,18},{3,19},{4,20},{5,21},{6,22},{7,23},{8,24},{9,... | collective-permute-start | bytes 798728 | tf_op jit(solution)/shard_map/ppermute | solution.py:106
  197.8 7.5 %collective-permute-start.33 = (f32[256,128]{1,0:T(8,128)S(1)}, f32[256,128]{1,0:T(8,128)S(1)}, u32[]{:S(2)}, u32[]{:S(2)}) collective-permute-start(f32[256,128]{1,0:T(8,128)S(1)} %slice_add_fusion.13), channel_id=1, source_target_pairs={{0,8},{1,9},{2,10},{3,11},{4,12},{5,13},{6,14},{7,15},{8,0},{9,1},... | collective-permute-start | bytes 393224 | tf_op jit(solution)/shard_map/ppermute | solution.py:106
  205.3 8.1 %collective-permute-start.34 = (f32[256,128]{1,0:T(8,128)S(1)}, f32[256,128]{1,0:T(8,128)S(1)}, u32[]{:S(2)}, u32[]{:S(2)}) collective-permute-start(f32[256,128]{1,0:T(8,128)S(1)} %add.775), channel_id=1, source_target_pairs={{0,16},{1,5},{2,18},{3,7},{4,20},{5,1},{6,22},{7,3},{8,24},{9,13},... | collective-permute-start | bytes 393224 | tf_op jit(solution)/shard_map/ppermute | solution.py:106
  211.7 8.2 %collective-permute-start.29 = (f32[512,128]{1,0:T(8,128)S(1)}, f32[512,128]{1,0:T(8,128)S(1)}, u32[]{:S(2)}, u32[]{:S(2)}) collective-permute-start(f32[512,128]{1,0:T(8,128)S(1)} %slice_add_fusion.7), channel_id=1, source_target_pairs={{0,8},{1,5},{2,10},{3,7},{4,12},{5,1},{6,14},{7,3},{8,0},{9,13},{1... | collective-permute-start | bytes 786440 | tf_op jit(solution)/shard_map/ppermute | solution.py:106
  213.5 6.5 %collective-permute-start.35 = (f32[512,128]{1,0:T(8,128)S(1)}, f32[512,128]{1,0:T(8,128)S(1)}, u32[]{:S(2)}, u32[]{:S(2)}) collective-permute-start(f32[512,128]{1,0:T(8,128)S(1)} %get-tuple-element.65), channel_id=1, source_target_pairs={{0,4},{1,17},{2,6},{3,19},{4,0},{5,21},{6,2},{7,23},{8,12},{9,25},... | collective-permute-start | bytes 786440 | tf_op jit(solution)/shard_map/ppermute | solution.py:106
  214.7 5.4 %copy-start.2 = (f32[512,128]{1,0:T(8,128)S(1)}, f32[512,128]{1,0:T(8,128)}, u32[]{:S(2)}) copy-start(f32[512,128]{1,0:T(8,128)} %copy-done.1) | copy-start | bytes 786436
  219.9 9.2 %collective-permute-start.30 = (f32[1024,128]{1,0:T(8,128)S(1)}, f32[1024,128]{1,0:T(8,128)S(1)}, u32[]{:S(2)}, u32[]{:S(2)}) collective-permute-start(f32[1024,128]{1,0:T(8,128)S(1)} %pad_maximum_fusion.12), channel_id=1, source_target_pairs={{0,4},{1,9},{2,6},{3,11},{4,0},{5,13},{6,2},{7,15},{8,12},{9,1},{1... | collective-permute-start | bytes 1572872 | tf_op jit(solution)/shard_map/ppermute | solution.py:106
  220.4 9.1 %copy-start.4 = (f32[3072,128]{1,0:T(8,128)}, f32[3072,128]{1,0:T(8,128)S(1)}, u32[]{:S(2)}) copy-start(f32[3072,128]{1,0:T(8,128)S(1)} %select_dynamic-update-slice_fusion.12) | copy-start | bytes 4718596
  229.8 1.1 copy-start.3

commit v5 on v0

v5 whole, which is shorter than its diff:
```python
import functools

import jax
import jax.numpy as jnp
from jax import lax
from jax.experimental import pallas as pl
from jax.experimental.pallas import tpu as pltpu
from jax.sharding import PartitionSpec as P

CB_DEV = 24
ITERS = 2
TILE = 128
PAIR = 2 * TILE
UNITS = 4
NORM_ROWS = 8
BUFFERS = 4

tiny_eps = 1e-06

WHOLE = pl.BlockSpec(memory_space=pltpu.VMEM)
SCALARS = pl.BlockSpec(memory_space=pltpu.SMEM)


def low_lanes(shape):
    return lax.broadcasted_iota(jnp.int32, shape, 1) < shape[1] // 2


def turned(value):
    return pltpu.roll(value, value.shape[1] // 2, 1)


def rows_of(pair, size=TILE):
    return slice(pair * size, (pair + 1) * size)


def fill_kernel(
    pattern_ref, count_ref, place_ref, flip_ref, delays_ref, tiles_ref,
    dense_ref, *rest,
):
    left_refs, (buffer_ref, arrived) = rest[:-2], rest[-2:]
    row_blocks = tiles_ref.shape[0]
    flip = flip_ref[0]

    def fetch(position, slot):
        return pltpu.make_async_copy(
            tiles_ref.at[position ^ flip], buffer_ref.at[slot], arrived.at[slot]
        )

    for position in range(BUFFERS):
        fetch(position, position).start()

    low = low_lanes((TILE, TILE))
    for pair in range(row_blocks // 2):
        source = (pair ^ (flip // 2)) * PAIR
        even = delays_ref[pl.ds(pl.multiple_of(source, TILE), TILE), :]
        odd = delays_ref[pl.ds(pl.multiple_of(source + TILE, TILE), TILE), :]
        left_refs[0][rows_of(pair), :] = jnp.where(low, even, turned(odd))
        left_refs[1][rows_of(pair), :] = jnp.where(low, turned(even), odd)

    @pl.loop(0, row_blocks)
    def _(position):
        slot = lax.rem(position, BUFFERS)
        rows = pl.ds(pl.multiple_of(position * TILE, TILE), TILE)
        dense_ref[rows, :] = jnp.zeros((TILE, dense_ref.shape[1]), dense_ref.dtype)
        fetch(position, slot).wait()
        block = position ^ flip

        @pl.loop(0, count_ref[block, 0])
        def _(tile):
            place = place_ref[pattern_ref[block, tile]]
            lanes = pl.ds(pl.multiple_of(place * TILE, TILE), TILE)
            dense_ref[rows, lanes] = buffer_ref[slot, tile]

        @pl.when(position + BUFFERS < row_blocks)
        def _():
            fetch(position + BUFFERS, slot).start()


def fill_dense(kernel, pattern, counts, places, flip, delays):
    row_blocks, slot_count = kernel.shape[:2]
    rows = row_blocks * TILE
    left = jax.ShapeDtypeStruct((rows // 2, TILE), jnp.float32)
    return pl.pallas_call(
        fill_kernel,
        in_specs=[SCALARS] * 4 + [WHOLE, pl.BlockSpec(memory_space=pl.ANY)],
        out_specs=[WHOLE] * 3,
        out_shape=[jax.ShapeDtypeStruct((rows, CB_DEV * TILE), kernel.dtype), left, left],
        scratch_shapes=[
            pltpu.VMEM((BUFFERS, slot_count, TILE, TILE), kernel.dtype),
            pltpu.SemaphoreType.DMA((BUFFERS,)),
        ],
        compiler_params=pltpu.CompilerParams(vmem_limit_bytes=46 * 1024 * 1024),
        cost_estimate=pl.CostEstimate(
            flops=0, bytes_accessed=2 * kernel.size, transcendentals=0
        ),
    )(pattern, counts, places, flip, delays, kernel)


def norm_of(ref):
    return jnp.sqrt(ref[0:1, :] + tiny_eps)


def squares_row(sums):
    while len(sums) > 1:
        sums = [sums[i] + sums[i + 1] for i in range(0, len(sums), 2)]
    row = jnp.sum(sums[0], axis=0, keepdims=True)
    return row + turned(row)


def next_vector(parts, raw_ref, scale_ref, past_ref, past_scale_ref):
    if scale_ref is not None:
        scale = norm_of(scale_ref)
    if past_ref is not None:
        past_scale = norm_of(past_scale_ref)
    position = 0
    for part, units in parts:
        pairs = part.shape[0] // TILE // units
        for unit in range(units):
            squares = jnp.zeros((NORM_ROWS, TILE), jnp.float32)
            for pair in range(pairs):
                value = part[rows_of(unit * pairs + pair), :]
                if scale_ref is not None:
                    value = value / scale
                if past_ref is not None:
                    value = value - scale * (past_ref[rows_of(position), :] / past_scale)
                if raw_ref is not None:
                    raw_ref[rows_of(position), :] = value
                squares += jnp.sum((value * value).reshape(-1, NORM_ROWS, TILE), axis=0)
                yield position, value, squares if pair == pairs - 1 else None
                position += 1


def store_message(pair, value, send_ref, keep_ref):
    half = keep_ref.shape[0] // TILE
    if pair < half:
        send_ref[rows_of(pair), :] = value
    else:
        keep_ref[rows_of(pair - half), :] = value


def back_kernel(first, *refs):
    if first:
        dense_ref, own_ref, send_ref, keep_ref, turned_ref = refs
        parts, raw_ref, scales = [(own_ref, 2)], None, (None, None, None)
    else:
        (dense_ref, other_ref, own_ref, scale_ref, past_ref, past_scale_ref,
         send_ref, keep_ref, raw_ref, turned_ref) = refs
        parts, scales = [(other_ref, 1), (own_ref, 1)], (scale_ref, past_ref, past_scale_ref)
    sums = []
    half = turned_ref.shape[0]
    for pair, value, squares in next_vector(parts, raw_ref, *scales):
        flat = value.T.astype(turned_ref.dtype)
        turned_ref[:, rows_of(2 * pair)] = flat[:half]
        turned_ref[:, rows_of(2 * pair + 1)] = flat[half:]
        if squares is not None:
            sums.append(squares)
    send_ref[keep_ref.shape[0] :, :] = jnp.broadcast_to(squares_row(sums), (NORM_ROWS, TILE))
    for pair in range(dense_ref.shape[1] // PAIR):
        product = jnp.dot(
            turned_ref[...], dense_ref[:, rows_of(pair, PAIR)], preferred_element_type=jnp.float32
        )
        stacked = jnp.concatenate([product[:, :TILE], product[:, TILE:]], axis=0)
        store_message(pair, stacked.T, send_ref, keep_ref)


def fore_kernel(first, *refs):
    if first:
        (dense_ref, outer_ref, inner_ref, mine_ref, scale_ref,
         send_ref, keep_ref, raw_ref, wide_ref) = refs
        scales = (scale_ref, None, None)
    else:
        (dense_ref, outer_ref, inner_ref, mine_ref, scale_ref, past_ref, past_scale_ref,
         send_ref, keep_ref, raw_ref, wide_ref) = refs
        scales = (scale_ref, past_ref, past_scale_ref)
    parts = [(outer_ref, 2), (inner_ref, 1), (mine_ref, 1)]
    low = low_lanes((TILE, TILE))
    sums = []
    for pair, value, squares in next_vector(parts, raw_ref, *scales):
        other = turned(value)
        wide_ref[rows_of(2 * pair), :] = jnp.where(low, value, other).astype(wide_ref.dtype)
        wide_ref[rows_of(2 * pair + 1), :] = jnp.where(low, other, value).astype(wide_ref.dtype)
        if squares is not None:
            sums.append(squares)
    send_ref[keep_ref.shape[0] :, :] = jnp.broadcast_to(squares_row(sums), (NORM_ROWS, TILE))
    step = 4
    for start in range(0, dense_ref.shape[0] // TILE, step):
        product = jnp.dot(
            dense_ref[start * TILE : (start + step) * TILE, :],
            wide_ref[...],
            preferred_element_type=jnp.float32,
        )
        for pair in range(step // 2):
            even, odd = product[rows_of(2 * pair), :], product[rows_of(2 * pair + 1), :]
            store_message(start // 2 + pair, jnp.where(low, even, odd), send_ref, keep_ref)


def product_call(body, dense, operands, half, raw_rows, scratch):
    message = jax.ShapeDtypeStruct((half + NORM_ROWS, TILE), jnp.float32)
    kept = jax.ShapeDtypeStruct((half, TILE), jnp.float32)
    shapes = [message, kept]
    if raw_rows:
        shapes.append(jax.ShapeDtypeStruct((raw_rows, TILE), jnp.float32))
    return pl.pallas_call(
        body,
        in_specs=[WHOLE] * (1 + len(operands)),
        out_specs=[WHOLE] * len(shapes),
        out_shape=shapes,
        scratch_shapes=[scratch],
        compiler_params=pltpu.CompilerParams(vmem_limit_bytes=12 * 1024 * 1024),
        cost_estimate=pl.CostEstimate(
            flops=4 * TILE * dense.size, bytes_accessed=2 * dense.size, transcendentals=0
        ),
    )(dense, *operands)


def back_product(dense, operands, first):
    scratch = pltpu.VMEM((TILE // 2, dense.shape[0]), dense.dtype)
    raw_rows = 0 if first else dense.shape[0] // 2
    return product_call(
        functools.partial(back_kernel, first), dense, operands, dense.shape[1] // 4, raw_rows, scratch
    )


def fore_product(dense, operands, first):
    scratch = pltpu.VMEM((dense.shape[1], TILE), dense.dtype)
    return product_call(
        functools.partial(fore_kernel, first),
        dense, operands, dense.shape[0] // 4, dense.shape[1] // 2, scratch,
    )


def rotation(norms):
    betas, alphas = [norm_of(ref) for ref in norms[0::2]], [norm_of(ref) for ref in norms[1::2]]
    resid_bar, diag_bar = betas[0], alphas[0]
    steps = []
    for j in range(len(alphas)):
        radius = jnp.sqrt(diag_bar * diag_bar + betas[j + 1] * betas[j + 1])
        rotate_cos = diag_bar / radius
        rotate_sin = betas[j + 1] / radius
        step_size = rotate_cos * resid_bar
        resid_bar = rotate_sin * resid_bar
        coupling = None
        if j + 1 < len(alphas):
            coupling = rotate_sin * alphas[j + 1] / radius
            diag_bar = -rotate_cos * alphas[j + 1]
        steps.append((step_size / radius, coupling))
    misfit = resid_bar / betas[0]
    return alphas, betas, steps, misfit, misfit * rotate_cos


def store_in_order(out_ref, mask, pair, low, values):
    pairs = out_ref.shape[0] // PAIR // UNITS
    start = (((pair // pairs) ^ mask) * pairs + pair % pairs) * PAIR
    ours, theirs = values
    even = pl.ds(pl.multiple_of(start, TILE), TILE)
    odd = pl.ds(pl.multiple_of(start + TILE, TILE), TILE)
    out_ref[even, :] = jnp.where(low, ours, turned(theirs))
    out_ref[odd, :] = jnp.where(low, turned(ours), theirs)


def model_kernel(count, mask_ref, *refs):
    ins, (model_ref, misfit_ref) = refs[:-2], refs[-2:]
    chains = [ins[: len(ins) // 2], ins[len(ins) // 2 :]]
    low = low_lanes((TILE, TILE))
    rotations = [rotation(refs_[count:]) for refs_ in chains]
    misfits = [jnp.broadcast_to(r[3], misfit_ref.shape) for r in rotations]
    misfit_ref[...] = jnp.where(low_lanes(misfit_ref.shape), misfits[0], misfits[1])
    for pair in range(model_ref.shape[0] // PAIR):
        values = []
        for refs_, (alphas, _, steps, _, _) in zip(chains, rotations):
            search = total = None
            for j in range(count):
                right = refs_[j][rows_of(pair), :] / alphas[j]
                search = right if j == 0 else right - steps[j - 1][1] * search
                total = steps[j][0] * search if j == 0 else total + steps[j][0] * search
            values.append(total)
        store_in_order(model_ref, mask_ref[0], pair, low, values)


def gradient_kernel(mask_ref, *refs):
    ins, gradient_ref = refs[:-1], refs[-1]
    chains = [ins[: len(ins) // 2], ins[len(ins) // 2 :]]
    low = low_lanes((TILE, TILE))
    vectors = []
    factors = []
    for outer_ref, inner_ref, mine_ref, past_ref, *norms in chains:
        alphas, betas, _, _, factor = rotation(norms)
        parts = [(outer_ref, 2), (inner_ref, 1), (mine_ref, 1)]
        vectors.append(next_vector(parts, None, norms[-1], past_ref, norms[-2]))
        factors.append(factor)
    for ours, theirs in zip(*vectors):
        values = [factors[0] * ours[1], factors[1] * theirs[1]]
        store_in_order(gradient_ref, mask_ref[0], ours[0], low, values)


def last_call(body, mask, operands, shapes):
    return pl.pallas_call(
        body,
        in_specs=[SCALARS] + [WHOLE] * len(operands),
        out_specs=[WHOLE] * len(shapes),
        out_shape=[jax.ShapeDtypeStruct(shape, jnp.float32) for shape in shapes],
        compiler_params=pltpu.CompilerParams(vmem_limit_bytes=12 * 1024 * 1024),
        cost_estimate=pl.CostEstimate(
            flops=0, bytes_accessed=8 * shapes[0][0] * TILE, transcendentals=0
        ),
    )(mask, *operands)


def on_device(row_count, col_count, kernel, pattern, counts, delays):
    row_bits = list(range(row_count.bit_length() - 1))
    col_bits = list(range(col_count.bit_length() - 1))
    row_index = lax.axis_index("rows")
    core = lax.axis_index("cols") & 1

    orders = [row_bits, [row_bits[1], row_bits[0], *row_bits[2:]]]

    def swap_rows(value, level):
        pairs = []
        for row in range(row_count):
            for col in range(col_count):
                partner = row ^ (1 << orders[col & 1][level])
                pairs.append((row * col_count + col, partner * col_count + col))
        return lax.ppermute(value, ("rows", "cols"), pairs)

    def swap_cols(value, level):
        return lax.ppermute(value, "cols", [(i, i ^ (1 << level)) for i in range(col_count)])

    bits = [(row_index >> bit) & 1 for bit in row_bits[:2]]
    outer_side = jnp.where(core == 0, bits[0], bits[1])
    inner_side = jnp.where(core == 0, bits[1], bits[0])
    mask = ((1 - outer_side) * 2 + (1 - inner_side)).astype(jnp.int32)
    blocks = jnp.arange(CB_DEV, dtype=jnp.int32)
    unit = CB_DEV // UNITS
    places = ((blocks // unit) ^ mask) * unit + blocks % unit
    flip = ((1 - core) * (kernel.shape[0] // 2)).astype(jnp.int32).reshape(1)
    mask = mask.reshape(1)

    dense, *lefts = fill_dense(kernel, pattern, counts, places, flip, delays)

    def swap_normed(value, norm, swap):
        got = swap(jnp.concatenate([value, norm]))
        return got[: value.shape[0]], norm + got[value.shape[0] :]

    def reduce_rows(send, keep):
        half = keep.shape[0]
        got = swap_rows(send, 0)
        keep = keep + got[:half]
        norm = send[half:] + got[half:]
        send, mine = keep[: half // 2], keep[half // 2 :]
        for level in range(1, len(row_bits)):
            got, norm = swap_normed(send, norm, lambda value: swap_rows(value, level))
            mine = mine + got
            send = mine
        inner = swap_rows(mine, 1)
        outer = swap_rows(jnp.concatenate([inner, mine]), 0)
        return [outer, inner, mine], norm

    def reduce_cols(send, keep):
        half = keep.shape[0]
        got = swap_cols(send, 0)
        own = keep + got[:half]
        norm = send[half:] + got[half:]
        for bit in col_bits[1:]:
            got, norm = swap_normed(own, norm, lambda value: swap_cols(value, bit))
            own = own + got
        return [swap_cols(own, 0), own], norm

    def chain(left):
        send, keep = back_product(dense, [left], True)
        totals, norm = reduce_rows(send, keep)
        norms = [norm]
        rights = []
        for iteration in range(ITERS):
            past = [rights[-1], norms[-2]] if rights else []
            send, keep, right = fore_product(dense, [*totals, norms[-1], *past], not rights)
            rights.append(right)
            halves, norm = reduce_cols(send, keep)
            norms.append(norm)
            send, keep, left = back_product(
                dense, [*halves, norms[-1], left, norms[-2]], False
            )
            totals, norm = reduce_rows(send, keep)
            norms.append(norm)
        return rights, norms, totals

    chains = [chain(left) for left in lefts]
    cells = dense.shape[1]
    model, misfit = last_call(
        functools.partial(model_kernel, ITERS),
        mask,
        [operand for rights, norms, _ in chains for operand in [*rights, *norms]],
        [(cells, TILE), (NORM_ROWS, TILE)],
    )
    (gradient,) = last_call(
        gradient_kernel,
        mask,
        [operand for rights, norms, totals in chains for operand in [*totals, rights[-1], *norms]],
        [(cells, TILE)],
    )
    return (model, gradient, misfit[0])


def solution(mesh):
    placed = (P("rows", "cols", None, None), P("rows", "cols"), P("rows", "cols"), P("rows", None))

    def local(kernel, pattern, counts, delays):
        return on_device(
            mesh.shape["rows"], mesh.shape["cols"], kernel, pattern, counts, delays
        )

    return jax.shard_map(
        local,
        mesh=mesh,
        in_specs=placed,
        out_specs=(P("cols", None), P("cols", None), P()),
        check_vma=False,
    )
```

time: 424 us -> 220 us (0.52)
  waiting for transfers between devices: 259 us -> 121 us
  blocking collectives: 81.9 us -> 0 us
  matrix products: 51.5 us -> 0 us
  Pallas kernels: 0 us -> 44.2 us
  starting transfers between devices: 0.21 us -> 43.8 us
  between operations: 13.8 us -> 1.33 us
  other arithmetic: 11 us -> 1.43 us
    psum x5 -> x0, waiting for transfers between devices: 259 us -> none  [the longest x3 203 us: back_step(): summed = lax.psum(partial_sum, 'rows')]
    ppermute x0 -> x42, waiting for transfers between devices: none -> 121 us  [the longest x30 98.5 us: swap_rows(): return lax.ppermute(value, ('rows', 'cols'), pairs)]
    psum x5 -> x0, blocking collectives: 81.9 us -> none  [the longest x3 67.8 us: back_step(): squares = lax.psum(column_norm(left_raw), 'rows')]
    dot_general x6 -> x0, matrix products: 51.5 us -> none  [the longest x3 23.7 us: local_backward(): lax.dot_general(dense_kernel, vec_bf, (((0,), (0,)), ((), ())), preferred...]
    pallas_call x0 -> x13, Pallas kernels: none -> 44.2 us  [the longest x10 29.6 us: product_call(): pl.pallas_call(body, in_specs=[WHOLE] * (1 + len(operands)), out_specs=[W...]
    ppermute x0 -> x42, starting transfers between devices: none -> 43.8 us  [the longest x30 37.1 us: swap_rows(): return lax.ppermute(value, ('rows', 'cols'), pairs)]
    reduce_sum x5 -> x0, other arithmetic: 5.9 us -> none  [column_norm(): return jnp.sum(values * values, axis=0)]
    mul x3 -> x0, other arithmetic: 4.32 us -> none  [the longest x2 4.31 us: on_device(): gradient = misfit * rotate_cos * right_raw]
  transfers between devices with their start and end apart: 5 -> 42, of which waited for: 5 -> 30; matrix products, arithmetic and copies ran while one was open for 0% -> 1% of each run, Pallas kernels for 0% -> 13%
where the time goes in v5:
time: 220 us
  waiting for transfers between devices  121 us (55%)
  Pallas kernels  44.2 us (20%)
  starting transfers between devices  43.8 us (20%)
  local copies, waits for them, and re-layouts  7.83 us (4%)
    ppermute x30, waiting for transfers between devices, swap_rows(): return lax.ppermute(value, ('rows', 'cols'), pairs)  98.5 us
    ppermute x30, starting transfers between devices, swap_rows(): return lax.ppermute(value, ('rows', 'cols'), pairs)  37.1 us
    pallas_call x10, Pallas kernels, product_call(): pl.pallas_call(body, in_specs=[WHOLE] * (1 + len(operands)), out_specs=[W...  29.6 us
    ppermute x12, waiting for transfers between devices, swap_cols(): lax.ppermute(value, 'cols', [(i, i ^ 1 << level) for i in range(col_count)])  22.6 us
    pallas_call x1, Pallas kernels, fill_dense(): pl.pallas_call(fill_kernel, in_specs=[SCALARS] * 4 + [WHOLE, pl.BlockSpec...  11.2 us
    unnamed x13, local copies, waits for them, and re-layouts  7.23 us
    ppermute x12, starting transfers between devices, swap_cols(): lax.ppermute(value, 'cols', [(i, i ^ 1 << level) for i in range(col_count)])  6.7 us
  transfers between devices with their start and end apart: 42, of which 30 were waited for; matrix products, arithmetic and copies ran while one was open for 1% of the time, Pallas kernels for 13%

profile of v5, /device:TPU:0, one launch (start us, length us, event | category | flops | bytes accessed | tf_op | source)
XLA Modules:
  0.0 219.7 jit_solution(6093372435784409087)
XLA Ops:
  3.3 11.2 %shard_map.67 = (bf16[2048,3072]{1,0:T(8,128)(2,1)}, f32[1024,128]{1,0:T(8,128)S(1)}, f32[1024,128]{1,0:T(8,128)S(1)}) custom-call(s32[16,16]{1,0:T(8,128)S(1)} %copy-done.2, s32[16,1]{1,0:T(8,128)S(1)} %copy.7.count_ref, s32[24]{0:T(128)S(1)} %fusion.place_ref, s32[1]{0:T(128)} %bitcast.1.flip_ref, f32[2048,128]{1,0:T(8,128)S(1)} %copy-done.1, ...), custom_call_target="tpu_custom_call" | custom-call | bytes 8388608 | tf_op jit(solution)/shard_map/pallas_call | solution.py:83
  14.5 4.6 %copy-done = bf16[2048,3072]{1,0:T(8,128)(2,1)S(1)} copy-done((bf16[2048,3072]{1,0:T(8,128)(2,1)S(1)}, bf16[2048,3072]{1,0:T(8,128)(2,1)}, u32[]{:S(2)}) %copy-start) | copy-done | bytes 12582936
  19.1 2.5 %shard_map.68 = (f32[776,128]{1,0:T(8,128)S(1)}, f32[768,128]{1,0:T(8,128)S(1)}) custom-call(bf16[2048,3072]{1,0:T(8,128)(2,1)S(1)} %copy-done, f32[1024,128]{1,0:T(8,128)S(1)} %get-tuple-element.35.refs_1_.refs_4_), custom_call_target="tpu_custom_call" | custom-call | flops 3221225472 | bytes 12582912 | tf_op jit(solution)/shard_map/pallas_call | solution.py:203
  21.6 2.7 %collective-permute-start = (f32[776,128]{1,0:T(8,128)S(1)}, f32[776,128]{1,0:T(8,128)S(1)}, u32[]{:S(2)}, u32[]{:S(2)}) collective-permute-start(f32[776,128]{1,0:T(8,128)S(1)} %get-tuple-element.37), channel_id=1, source_target_pairs={{0,4},{1,9},{2,6},{3,11},{4,0},{5,13},{6,2},{7,15},{8,12},{9,1},{1... | collective-permute-start | bytes 1191944 | tf_op jit(solution)/shard_map/ppermute | solution.py:323
  24.3 2.5 %shard_map.73 = (f32[776,128]{1,0:T(8,128)S(1)}, f32[768,128]{1,0:T(8,128)S(1)}) custom-call(bf16[2048,3072]{1,0:T(8,128)(2,1)S(1)} %copy-done, f32[1024,128]{1,0:T(8,128)S(1)} %get-tuple-element.49.refs_1_.refs_4_), custom_call_target="tpu_custom_call" | custom-call | flops 3221225472 | bytes 12582912 | tf_op jit(solution)/shard_map/pallas_call | solution.py:203
  26.9 3.2 %collective-permute-done = f32[776,128]{1,0:T(8,128)S(1)} collective-permute-done((f32[776,128]{1,0:T(8,128)S(1)}, f32[776,128]{1,0:T(8,128)S(1)}, u32[]{:S(2)}, u32[]{:S(2)}) %collective-permute-start) | collective-permute-done | bytes 397344 | tf_op jit(solution)/shard_map/ppermute | solution.py:323
  30.2 2.0 collective-permute-start.1
  32.3 4.9 %collective-permute-done.19 = f32[776,128]{1,0:T(8,128)S(1)} collective-permute-done((f32[776,128]{1,0:T(8,128)S(1)}, f32[776,128]{1,0:T(8,128)S(1)}, u32[]{:S(2)}, u32[]{:S(2)}) %collective-permute-start.19) | collective-permute-done | bytes 397344 | tf_op jit(solution)/shard_map/ppermute | solution.py:323
  39.0 3.4 %collective-permute-start.2 = (f32[392,128]{1,0:T(8,128)S(1)}, f32[392,128]{1,0:T(8,128)S(1)}, u32[]{:S(2)}, u32[]{:S(2)}) collective-permute-start(f32[392,128]{1,0:T(8,128)S(1)} %pad_maximum_fusion.11), channel_id=1, source_target_pairs={{0,16},{1,17},{2,18},{3,19},{4,20},{5,21},{6,22},{7,23},{8,24},{9,... | collective-permute-start | bytes 602120 | tf_op jit(solution)/shard_map/ppermute | solution.py:323
  42.4 3.2 %collective-permute-done.20 = f32[392,128]{1,0:T(8,128)S(1)} collective-permute-done((f32[392,128]{1,0:T(8,128)S(1)}, f32[392,128]{1,0:T(8,128)S(1)}, u32[]{:S(2)}, u32[]{:S(2)}) %collective-permute-start.20) | collective-permute-done | bytes 200736 | tf_op jit(solution)/shard_map/ppermute | solution.py:323
  45.6 2.6 %collective-permute-start.21 = (f32[392,128]{1,0:T(8,128)S(1)}, f32[392,128]{1,0:T(8,128)S(1)}, u32[]{:S(2)}, u32[]{:S(2)}) collective-permute-start(f32[392,128]{1,0:T(8,128)S(1)} %pad_maximum_fusion.17), channel_id=1, source_target_pairs={{0,16},{1,17},{2,18},{3,19},{4,20},{5,21},{6,22},{7,23},{8,24},{9,... | collective-permute-start | bytes 602120 | tf_op jit(solution)/shard_map/ppermute | solution.py:323
  48.2 7.3 %collective-permute-done.2 = f32[392,128]{1,0:T(8,128)S(1)} collective-permute-done((f32[392,128]{1,0:T(8,128)S(1)}, f32[392,128]{1,0:T(8,128)S(1)}, u32[]{:S(2)}, u32[]{:S(2)}) %collective-permute-start.2) | collective-permute-done | bytes 200736 | tf_op jit(solution)/shard_map/ppermute | solution.py:323
  55.7 2.3 %collective-permute-done.21 = f32[392,128]{1,0:T(8,128)S(1)} collective-permute-done((f32[392,128]{1,0:T(8,128)S(1)}, f32[392,128]{1,0:T(8,128)S(1)}, u32[]{:S(2)}, u32[]{:S(2)}) %collective-permute-start.21) | collective-permute-done | bytes 200736 | tf_op jit(solution)/shard_map/ppermute | solution.py:323
  59.1 3.0 %collective-permute-done.3.refs_2_ = f32[384,128]{1,0:T(8,128)S(1)} collective-permute-done((f32[384,128]{1,0:T(8,128)S(1)}, f32[384,128]{1,0:T(8,128)S(1)}, u32[]{:S(2)}, u32[]{:S(2)}) %collective-permute-start.3) | collective-permute-done | bytes 196640 | tf_op jit(solution)/shard_map/ppermute | solution.py:323
  63.3 2.9 %collective-permute-done.22.refs_2_ = f32[384,128]{1,0:T(8,128)S(1)} collective-permute-done((f32[384,128]{1,0:T(8,128)S(1)}, f32[384,128]{1,0:T(8,128)S(1)}, u32[]{:S(2)}, u32[]{:S(2)}) %collective-permute-start.22) | collective-permute-done | bytes 196640 | tf_op jit(solution)/shard_map/ppermute | solution.py:323
  67.5 2.4 %collective-permute-done.4.refs_1_ = f32[768,128]{1,0:T(8,128)S(1)} collective-permute-done((f32[768,128]{1,0:T(8,128)S(1)}, f32[768,128]{1,0:T(8,128)S(1)}, u32[]{:S(2)}, u32[]{:S(2)}) %collective-permute-start.4) | collective-permute-done | bytes 393248 | tf_op jit(solution)/shard_map/ppermute | solution.py:323
  69.9 3.5 %shard_map.69 = (f32[520,128]{1,0:T(8,128)S(1)}, f32[512,128]{1,0:T(8,128)S(1)}, f32[1536,128]{1,0:T(8,128)S(1)}) custom-call(bf16[2048,3072]{1,0:T(8,128)(2,1)S(1)} %bitcast.5, f32[768,128]{1,0:T(8,128)S(1)} %collective-permute-done.4.refs_1_, f32[384,128]{1,0:T(8,128)S(1)} %collective-permute-done.3.refs_2_, f32[384,128]{1,0:T(8,128)S(1)} %slice_add_fusion.24.refs_3_, ...), custom_call_target="tpu_custom_call" | custom-call | flops 3221225472 | bytes 12582912 | tf_op jit(solution)/shard_map/pallas_call | solution.py:203
  74.1 3.5 %shard_map.74 = (f32[520,128]{1,0:T(8,128)S(1)}, f32[512,128]{1,0:T(8,128)S(1)}, f32[1536,128]{1,0:T(8,128)S(1)}) custom-call(bf16[2048,3072]{1,0:T(8,128)(2,1)S(1)} %bitcast.5, f32[768,128]{1,0:T(8,128)S(1)} %collective-permute-done.23.refs_1_, f32[384,128]{1,0:T(8,128)S(1)} %collective-permute-done.22.refs_2_, f32[384,128]{1,0:T(8,128)S(1)} %slice_add_fusion.19.refs_3_, ...), custom_call_target="tpu_custom_call" | custom-call | flops 3221225472 | bytes 12582912 | tf_op jit(solution)/shard_map/pallas_call | solution.py:203
  80.9 6.2 %collective-permute-done.6 = f32[520,128]{1,0:T(8,128)S(1)} collective-permute-done((f32[520,128]{1,0:T(8,128)S(1)}, f32[520,128]{1,0:T(8,128)S(1)}, u32[]{:S(2)}, u32[]{:S(2)}) %collective-permute-start.6) | collective-permute-done | bytes 266272 | tf_op jit(solution)/shard_map/ppermute | solution.py:326
  87.2 5.2 %collective-permute-done.25 = f32[520,128]{1,0:T(8,128)S(1)} collective-permute-done((f32[520,128]{1,0:T(8,128)S(1)}, f32[520,128]{1,0:T(8,128)S(1)}, u32[]{:S(2)}, u32[]{:S(2)}) %collective-permute-start.25) | collective-permute-done | bytes 266272 | tf_op jit(solution)/shard_map/ppermute | solution.py:326
  92.5 2.7 %shard_map.70 = (f32[776,128]{1,0:T(8,128)S(1)}, f32[768,128]{1,0:T(8,128)S(1)}, f32[1024,128]{1,0:T(8,128)S(1)}) custom-call(bf16[2048,3072]{1,0:T(8,128)(2,1)S(1)} %bitcast.5, f32[512,128]{1,0:T(8,128)S(1)} %collective-permute-done.7.refs_1_, f32[512,128]{1,0:T(8,128)S(1)} %slice_add_fusion.12.refs_2_, ...), custom_call_target="tpu_custom_call" | custom-call | flops 3221225472 | bytes 12582912 | tf_op jit(solution)/shard_map/pallas_call | solution.py:203
  95.2 1.8 collective-permute-start.8
  97.1 2.5 %shard_map.75 = (f32[776,128]{1,0:T(8,128)S(1)}, f32[768,128]{1,0:T(8,128)S(1)}, f32[1024,128]{1,0:T(8,128)S(1)}) custom-call(bf16[2048,3072]{1,0:T(8,128)(2,1)S(1)} %bitcast.5, f32[512,128]{1,0:T(8,128)S(1)} %collective-permute-done.26.refs_1_, f32[512,128]{1,0:T(8,128)S(1)} %slice_add_fusion.8.refs_2_, ...), custom_call_target="tpu_custom_call" | custom-call | flops 3221225472 | bytes 12582912 | tf_op jit(solution)/shard_map/pallas_call | solution.py:203
  99.9 3.2 %collective-permute-done.8 = f32[776,128]{1,0:T(8,128)S(1)} collective-permute-done((f32[776,128]{1,0:T(8,128)S(1)}, f32[776,128]{1,0:T(8,128)S(1)}, u32[]{:S(2)}, u32[]{:S(2)}) %collective-permute-start.8) | collective-permute-done | bytes 397344 | tf_op jit(solution)/shard_map/ppermute | solution.py:323
  103.9 5.5 %collective-permute-done.27 = f32[776,128]{1,0:T(8,128)S(1)} collective-permute-done((f32[776,128]{1,0:T(8,128)S(1)}, f32[776,128]{1,0:T(8,128)S(1)}, u32[]{:S(2)}, u32[]{:S(2)}) %collective-permute-start.27) | collective-permute-done | bytes 397344 | tf_op jit(solution)/shard_map/ppermute | solution.py:323
  110.0 3.4 %collective-permute-start.10 = (f32[392,128]{1,0:T(8,128)S(1)}, f32[392,128]{1,0:T(8,128)S(1)}, u32[]{:S(2)}, u32[]{:S(2)}) collective-permute-start(f32[392,128]{1,0:T(8,128)S(1)} %pad_maximum_fusion.13), channel_id=1, source_target_pairs={{0,16},{1,17},{2,18},{3,19},{4,20},{5,21},{6,22},{7,23},{8,24},{9,... | collective-permute-start | bytes 602120 | tf_op jit(solution)/shard_map/ppermute | solution.py:323
  113.4 4.1 %collective-permute-done.28 = f32[392,128]{1,0:T(8,128)S(1)} collective-permute-done((f32[392,128]{1,0:T(8,128)S(1)}, f32[392,128]{1,0:T(8,128)S(1)}, u32[]{:S(2)}, u32[]{:S(2)}) %collective-permute-start.28) | collective-permute-done | bytes 200736 | tf_op jit(solution)/shard_map/ppermute | solution.py:323
  119.2 7.9 %collective-permute-done.10 = f32[392,128]{1,0:T(8,128)S(1)} collective-permute-done((f32[392,128]{1,0:T(8,128)S(1)}, f32[392,128]{1,0:T(8,128)S(1)}, u32[]{:S(2)}, u32[]{:S(2)}) %collective-permute-start.10) | collective-permute-done | bytes 200736 | tf_op jit(solution)/shard_map/ppermute | solution.py:323
  127.2 3.1 %collective-permute-done.29 = f32[392,128]{1,0:T(8,128)S(1)} collective-permute-done((f32[392,128]{1,0:T(8,128)S(1)}, f32[392,128]{1,0:T(8,128)S(1)}, u32[]{:S(2)}, u32[]{:S(2)}) %collective-permute-start.29) | collective-permute-done | bytes 200736 | tf_op jit(solution)/shard_map/ppermute | solution.py:323
  130.6 2.3 %collective-permute-done.11.refs_2_ = f32[384,128]{1,0:T(8,128)S(1)} collective-permute-done((f32[384,128]{1,0:T(8,128)S(1)}, f32[384,128]{1,0:T(8,128)S(1)}, u32[]{:S(2)}, u32[]{:S(2)}) %collective-permute-start.11) | collective-permute-done | bytes 196640 | tf_op jit(solution)/shard_map/ppermute | solution.py:323
  134.1 4.0 %collective-permute-done.30.refs_2_ = f32[384,128]{1,0:T(8,128)S(1)} collective-permute-done((f32[384,128]{1,0:T(8,128)S(1)}, f32[384,128]{1,0:T(8,128)S(1)}, u32[]{:S(2)}, u32[]{:S(2)}) %collective-permute-start.30) | collective-permute-done | bytes 196640 | tf_op jit(solution)/shard_map/ppermute | solution.py:323
  138.2 1.7 collective-permute-start.31
  140.7 3.5 %shard_map.71 = (f32[520,128]{1,0:T(8,128)S(1)}, f32[512,128]{1,0:T(8,128)S(1)}, f32[1536,128]{1,0:T(8,128)S(1)}) custom-call(bf16[2048,3072]{1,0:T(8,128)(2,1)S(1)} %bitcast.5, f32[768,128]{1,0:T(8,128)S(1)} %collective-permute-done.12.refs_1_, f32[384,128]{1,0:T(8,128)S(1)} %collective-permute-done.11.refs_2_, f32[384,128]{1,0:T(8,128)S(1)} %slice_add_fusion.22.refs_3_, ...), custom_call_target="tpu_custom_call" | custom-call | flops 3221225472 | bytes 12582912 | tf_op jit(solution)/shard_map/pallas_call | solution.py:203
  146.0 3.6 %shard_map.76 = (f32[520,128]{1,0:T(8,128)S(1)}, f32[512,128]{1,0:T(8,128)S(1)}, f32[1536,128]{1,0:T(8,128)S(1)}) custom-call(bf16[2048,3072]{1,0:T(8,128)(2,1)S(1)} %bitcast.5, f32[768,128]{1,0:T(8,128)S(1)} %collective-permute-done.31.refs_1_, f32[384,128]{1,0:T(8,128)S(1)} %collective-permute-done.30.refs_2_, f32[384,128]{1,0:T(8,128)S(1)} %slice_add_fusion.17.refs_3_, ...), custom_call_target="tpu_custom_call" | custom-call | flops 3221225472 | bytes 12582912 | tf_op jit(solution)/shard_map/pallas_call | solution.py:203
  149.7 1.7 collective-permute-start.14
  153.0 6.0 %collective-permute-done.14 = f32[520,128]{1,0:T(8,128)S(1)} collective-permute-done((f32[520,128]{1,0:T(8,128)S(1)}, f32[520,128]{1,0:T(8,128)S(1)}, u32[]{:S(2)}, u32[]{:S(2)}) %collective-permute-start.14) | collective-permute-done | bytes 266272 | tf_op jit(solution)/shard_map/ppermute | solution.py:326
  159.1 5.2 %collective-permute-done.33 = f32[520,128]{1,0:T(8,128)S(1)} collective-permute-done((f32[520,128]{1,0:T(8,128)S(1)}, f32[520,128]{1,0:T(8,128)S(1)}, u32[]{:S(2)}, u32[]{:S(2)}) %collective-permute-start.33) | collective-permute-done | bytes 266272 | tf_op jit(solution)/shard_map/ppermute | solution.py:326
  164.4 2.5 %shard_map.72 = (f32[776,128]{1,0:T(8,128)S(1)}, f32[768,128]{1,0:T(8,128)S(1)}, f32[1024,128]{1,0:T(8,128)}) custom-call(bf16[2048,3072]{1,0:T(8,128)(2,1)S(1)} %bitcast.5, f32[512,128]{1,0:T(8,128)S(1)} %collective-permute-done.15.refs_1_, f32[512,128]{1,0:T(8,128)S(1)} %slice_add_fusion.10.refs_2_, f32[8,128]{1,0:T(8,128)S(1)} %slice_add_fusion.42.refs_3_.refs_5_.refs_7_, ...), custom_call_target="tpu_custom_call" | custom-call | flops 3221225472 | bytes 12582912 | tf_op jit(solution)/shard_map/pallas_call | solution.py:203
  168.7 2.8 %shard_map.77 = (f32[776,128]{1,0:T(8,128)S(1)}, f32[768,128]{1,0:T(8,128)S(1)}, f32[1024,128]{1,0:T(8,128)}) custom-call(bf16[2048,3072]{1,0:T(8,128)(2,1)S(1)} %bitcast.5, f32[512,128]{1,0:T(8,128)S(1)} %collective-permute-done.34.refs_1_, f32[512,128]{1,0:T(8,128)S(1)} %slice_add_fusion.6.refs_2_, ...), custom_call_target="tpu_custom_call" | custom-call | flops 3221225472 | bytes 12582912 | tf_op jit(solution)/shard_map/pallas_call | solution.py:203
  171.9 3.0 %collective-permute-done.16 = f32[776,128]{1,0:T(8,128)S(1)} collective-permute-done((f32[776,128]{1,0:T(8,128)S(1)}, f32[776,128]{1,0:T(8,128)S(1)}, u32[]{:S(2)}, u32[]{:S(2)}) %collective-permute-start.16) | collective-permute-done | bytes 397344 | tf_op jit(solution)/shard_map/ppermute | solution.py:323
  175.1 6.3 %collective-permute-done.35 = f32[776,128]{1,0:T(8,128)S(1)} collective-permute-done((f32[776,128]{1,0:T(8,128)S(1)}, f32[776,128]{1,0:T(8,128)S(1)}, u32[]{:S(2)}, u32[]{:S(2)}) %collective-permute-start.35) | collective-permute-done | bytes 397344 | tf_op jit(solution)/shard_map/ppermute | solution.py:323
  181.6 3.1 %collective-permute-start.18 = (f32[392,128]{1,0:T(8,128)S(1)}, f32[392,128]{1,0:T(8,128)S(1)}, u32[]{:S(2)}, u32[]{:S(2)}) collective-permute-start(f32[392,128]{1,0:T(8,128)S(1)} %pad_maximum_fusion.15), channel_id=1, source_target_pairs={{0,16},{1,17},{2,18},{3,19},{4,20},{5,21},{6,22},{7,23},{8,24},{9,... | collective-permute-start | bytes 602120 | tf_op jit(solution)/shard_map/ppermute | solution.py:323
  184.7 4.2 %collective-permute-done.36 = f32[392,128]{1,0:T(8,128)S(1)} collective-permute-done((f32[392,128]{1,0:T(8,128)S(1)}, f32[392,128]{1,0:T(8,128)S(1)}, u32[]{:S(2)}, u32[]{:S(2)}) %collective-permute-start.36) | collective-permute-done | bytes 200736 | tf_op jit(solution)/shard_map/ppermute | solution.py:323
  190.5 7.8 %collective-permute-done.18 = f32[392,128]{1,0:T(8,128)S(1)} collective-permute-done((f32[392,128]{1,0:T(8,128)S(1)}, f32[392,128]{1,0:T(8,128)S(1)}, u32[]{:S(2)}, u32[]{:S(2)}) %collective-permute-start.18) | collective-permute-done | bytes 200736 | tf_op jit(solution)/shard_map/ppermute | solution.py:323
  198.4 3.8 %collective-permute-done.37 = f32[392,128]{1,0:T(8,128)S(1)} collective-permute-done((f32[392,128]{1,0:T(8,128)S(1)}, f32[392,128]{1,0:T(8,128)S(1)}, u32[]{:S(2)}, u32[]{:S(2)}) %collective-permute-start.37) | collective-permute-done | bytes 200736 | tf_op jit(solution)/shard_map/ppermute | solution.py:323
  202.4 2.0 collective-permute-done.38.refs_1_
  205.6 4.5 %collective-permute-done.40.refs_10_ = f32[384,128]{1,0:T(8,128)S(1)} collective-permute-done((f32[384,128]{1,0:T(8,128)S(1)}, f32[384,128]{1,0:T(8,128)S(1)}, u32[]{:S(2)}, u32[]{:S(2)}) %collective-permute-start.40) | collective-permute-done | bytes 196640 | tf_op jit(solution)/shard_map/ppermute | solution.py:323
  213.5 4.4 %collective-permute-done.41.refs_9_ = f32[768,128]{1,0:T(8,128)S(1)} collective-permute-done((f32[768,128]{1,0:T(8,128)S(1)}, f32[768,128]{1,0:T(8,128)S(1)}, u32[]{:S(2)}, u32[]{:S(2)}) %collective-permute-start.41) | collective-permute-done | bytes 393248 | tf_op jit(solution)/shard_map/ppermute | solution.py:323
  (145 shorter events, 32.4 us)
Async XLA Ops:
  1.4 1.2 copy-start.1
  2.6 0.7 copy-start.2
  14.5 4.6 %copy-start = (bf16[2048,3072]{1,0:T(8,128)(2,1)S(1)}, bf16[2048,3072]{1,0:T(8,128)(2,1)}, u32[]{:S(2)}) copy-start(bf16[2048,3072]{1,0:T(8,128)(2,1)} %get-tuple-element.34.refs_0_) | copy-start | bytes 37748740
  19.1 50.8 %slice-start = ((s8[12582912]{0:T(1024)(128)(4,1)}), s8[4194304]{0:T(1024)(128)(4,1)S(1)}, s32[]{:S(2)}) async-start(s8[12582912]{0:T(1024)(128)(4,1)} %bitcast.4), calls=%async_computation | async-start | bytes 8388608
  19.1 50.8 %slice-start.1 = ((s8[12582912]{0:T(1024)(128)(4,1)}), s8[4194304]{0:T(1024)(128)(4,1)S(1)}, s32[]{:S(2)}) async-start(s8[12582912]{0:T(1024)(128)(4,1)} %bitcast.4), calls=%async_computation.1 | async-start | bytes 8388608
  21.6 8.5 %collective-permute-start = (f32[776,128]{1,0:T(8,128)S(1)}, f32[776,128]{1,0:T(8,128)S(1)}, u32[]{:S(2)}, u32[]{:S(2)}) collective-permute-start(f32[776,128]{1,0:T(8,128)S(1)} %get-tuple-element.37), channel_id=1, source_target_pairs={{0,4},{1,9},{2,6},{3,11},{4,0},{5,13},{6,2},{7,15},{8,12},{9,1},{1... | collective-permute-start | bytes 1191944 | tf_op jit(solution)/shard_map/ppermute | solution.py:323
  24.3 45.6 %slice-start.2 = ((s8[12582912]{0:T(1024)(128)(4,1)}), s8[4194304]{0:T(1024)(128)(4,1)S(1)}, s32[]{:S(2)}) async-start(s8[12582912]{0:T(1024)(128)(4,1)} %bitcast.4), calls=%async_computation.2 | async-start | bytes 8388608
  26.8 10.4 %collective-permute-start.19 = (f32[776,128]{1,0:T(8,128)S(1)}, f32[776,128]{1,0:T(8,128)S(1)}, u32[]{:S(2)}, u32[]{:S(2)}) collective-permute-start(f32[776,128]{1,0:T(8,128)S(1)} %get-tuple-element.51), channel_id=1, source_target_pairs={{0,4},{1,9},{2,6},{3,11},{4,0},{5,13},{6,2},{7,15},{8,12},{9,1},{1... | collective-permute-start | bytes 1191944 | tf_op jit(solution)/shard_map/ppermute | solution.py:323
  30.2 8.7 %collective-permute-start.1 = (f32[392,128]{1,0:T(8,128)S(1)}, f32[392,128]{1,0:T(8,128)S(1)}, u32[]{:S(2)}, u32[]{:S(2)}) collective-permute-start(f32[392,128]{1,0:T(8,128)S(1)} %pad_maximum_fusion.10), channel_id=1, source_target_pairs={{0,8},{1,5},{2,10},{3,7},{4,12},{5,1},{6,14},{7,3},{8,0},{9,13},{1... | collective-permute-start | bytes 602120 | tf_op jit(solution)/shard_map/ppermute | solution.py:323
  37.3 8.2 %collective-permute-start.20 = (f32[392,128]{1,0:T(8,128)S(1)}, f32[392,128]{1,0:T(8,128)S(1)}, u32[]{:S(2)}, u32[]{:S(2)}) collective-permute-start(f32[392,128]{1,0:T(8,128)S(1)} %pad_maximum_fusion.16), channel_id=1, source_target_pairs={{0,8},{1,5},{2,10},{3,7},{4,12},{5,1},{6,14},{7,3},{8,0},{9,13},{1... | collective-permute-start | bytes 602120 | tf_op jit(solution)/shard_map/ppermute | solution.py:323
  39.0 16.6 %collective-permute-start.2 = (f32[392,128]{1,0:T(8,128)S(1)}, f32[392,128]{1,0:T(8,128)S(1)}, u32[]{:S(2)}, u32[]{:S(2)}) collective-permute-start(f32[392,128]{1,0:T(8,128)S(1)} %pad_maximum_fusion.11), channel_id=1, source_target_pairs={{0,16},{1,17},{2,18},{3,19},{4,20},{5,21},{6,22},{7,23},{8,24},{9,... | collective-permute-start | bytes 602120 | tf_op jit(solution)/shard_map/ppermute | solution.py:323
  45.6 12.4 %collective-permute-start.21 = (f32[392,128]{1,0:T(8,128)S(1)}, f32[392,128]{1,0:T(8,128)S(1)}, u32[]{:S(2)}, u32[]{:S(2)}) collective-permute-start(f32[392,128]{1,0:T(8,128)S(1)} %pad_maximum_fusion.17), channel_id=1, source_target_pairs={{0,16},{1,17},{2,18},{3,19},{4,20},{5,21},{6,22},{7,23},{8,24},{9,... | collective-permute-start | bytes 602120 | tf_op jit(solution)/shard_map/ppermute | solution.py:323
  55.6 6.5 %collective-permute-start.3 = (f32[384,128]{1,0:T(8,128)S(1)}, f32[384,128]{1,0:T(8,128)S(1)}, u32[]{:S(2)}, u32[]{:S(2)}) collective-permute-start(f32[384,128]{1,0:T(8,128)S(1)} %slice_add_fusion.24.refs_3_), channel_id=1, source_target_pairs={{0,8},{1,5},{2,10},{3,7},{4,12},{5,1},{6,14},{7,3},{8,0},{9,13},{1... | collective-permute-start | bytes 589832 | tf_op jit(solution)/shard_map/ppermute | solution.py:323
  58.0 8.2 %collective-permute-start.22 = (f32[384,128]{1,0:T(8,128)S(1)}, f32[384,128]{1,0:T(8,128)S(1)}, u32[]{:S(2)}, u32[]{:S(2)}) collective-permute-start(f32[384,128]{1,0:T(8,128)S(1)} %slice_add_fusion.19.refs_3_), channel_id=1, source_target_pairs={{0,8},{1,5},{2,10},{3,7},{4,12},{5,1},{6,14},{7,3},{8,0},{9,13},{1... | collective-permute-start | bytes 589832 | tf_op jit(solution)/shard_map/ppermute | solution.py:323
  62.1 7.8 %collective-permute-start.4 = (f32[768,128]{1,0:T(8,128)S(1)}, f32[768,128]{1,0:T(8,128)S(1)}, u32[]{:S(2)}, u32[]{:S(2)}) collective-permute-start(f32[768,128]{1,0:T(8,128)S(1)} %pad_maximum_fusion), channel_id=1, source_target_pairs={{0,4},{1,9},{2,6},{3,11},{4,0},{5,13},{6,2},{7,15},{8,12},{9,1},{1... | collective-permute-start | bytes 1179656 | tf_op jit(solution)/shard_map/ppermute | solution.py:323
  66.3 7.8 %collective-permute-start.23 = (f32[768,128]{1,0:T(8,128)S(1)}, f32[768,128]{1,0:T(8,128)S(1)}, u32[]{:S(2)}, u32[]{:S(2)}) collective-permute-start(f32[768,128]{1,0:T(8,128)S(1)} %pad_maximum_fusion.2), channel_id=1, source_target_pairs={{0,4},{1,9},{2,6},{3,11},{4,0},{5,13},{6,2},{7,15},{8,12},{9,1},{1... | collective-permute-start | bytes 1179656 | tf_op jit(solution)/shard_map/ppermute | solution.py:323
  73.5 4.3 %collective-permute-start.5 = (f32[520,128]{1,0:T(8,128)S(1)}, f32[520,128]{1,0:T(8,128)S(1)}, u32[]{:S(2)}, u32[]{:S(2)}) collective-permute-start(f32[520,128]{1,0:T(8,128)S(1)} %get-tuple-element.40), channel_id=1, source_target_pairs={{0,1},{1,0},{2,3},{3,2},{4,5},{5,4},{6,7},{7,6},{8,9},{9,8},{10,11... | collective-permute-start | bytes 798728 | tf_op jit(solution)/shard_map/ppermute | solution.py:326
  77.6 1.7 collective-permute-start.24
  77.8 9.3 %collective-permute-start.6 = (f32[520,128]{1,0:T(8,128)S(1)}, f32[520,128]{1,0:T(8,128)S(1)}, u32[]{:S(2)}, u32[]{:S(2)}) collective-permute-start(f32[520,128]{1,0:T(8,128)S(1)} %pad_maximum_fusion.6), channel_id=1, source_target_pairs={{0,2},{1,3},{2,0},{3,1},{4,6},{5,7},{6,4},{7,5},{8,10},{9,11},{10,... | collective-permute-start | bytes 798728 | tf_op jit(solution)/shard_map/ppermute | solution.py:326
  79.4 12.9 %collective-permute-start.25 = (f32[520,128]{1,0:T(8,128)S(1)}, f32[520,128]{1,0:T(8,128)S(1)}, u32[]{:S(2)}, u32[]{:S(2)}) collective-permute-start(f32[520,128]{1,0:T(8,128)S(1)} %pad_maximum_fusion.8), channel_id=1, source_target_pairs={{0,2},{1,3},{2,0},{3,1},{4,6},{5,7},{6,4},{7,5},{8,10},{9,11},{10,... | collective-permute-start | bytes 798728 | tf_op jit(solution)/shard_map/ppermute | solution.py:326
  87.1 5.4 %collective-permute-start.7 = (f32[512,128]{1,0:T(8,128)S(1)}, f32[512,128]{1,0:T(8,128)S(1)}, u32[]{:S(2)}, u32[]{:S(2)}) collective-permute-start(f32[512,128]{1,0:T(8,128)S(1)} %slice_add_fusion.12.refs_2_), channel_id=1, source_target_pairs={{0,1},{1,0},{2,3},{3,2},{4,5},{5,4},{6,7},{7,6},{8,9},{9,8},{10,11... | collective-permute-start | bytes 786440 | tf_op jit(solution)/shard_map/ppermute | solution.py:326
  92.4 4.7 %collective-permute-start.26 = (f32[512,128]{1,0:T(8,128)S(1)}, f32[512,128]{1,0:T(8,128)S(1)}, u32[]{:S(2)}, u32[]{:S(2)}) collective-permute-start(f32[512,128]{1,0:T(8,128)S(1)} %slice_add_fusion.8.refs_2_), channel_id=1, source_target_pairs={{0,1},{1,0},{2,3},{3,2},{4,5},{5,4},{6,7},{7,6},{8,9},{9,8},{10,11... | collective-permute-start | bytes 786440 | tf_op jit(solution)/shard_map/ppermute | solution.py:326
  95.2 7.9 %collective-permute-start.8 = (f32[776,128]{1,0:T(8,128)S(1)}, f32[776,128]{1,0:T(8,128)S(1)}, u32[]{:S(2)}, u32[]{:S(2)}) collective-permute-start(f32[776,128]{1,0:T(8,128)S(1)} %get-tuple-element.42), channel_id=1, source_target_pairs={{0,4},{1,9},{2,6},{3,11},{4,0},{5,13},{6,2},{7,15},{8,12},{9,1},{1... | collective-permute-start | bytes 1191944 | tf_op jit(solution)/shard_map/ppermute | solution.py:323
  99.6 9.8 %collective-permute-start.27 = (f32[776,128]{1,0:T(8,128)S(1)}, f32[776,128]{1,0:T(8,128)S(1)}, u32[]{:S(2)}, u32[]{:S(2)}) collective-permute-start(f32[776,128]{1,0:T(8,128)S(1)} %get-tuple-element.56), channel_id=1, source_target_pairs={{0,4},{1,9},{2,6},{3,11},{4,0},{5,13},{6,2},{7,15},{8,12},{9,1},{1... | collective-permute-start | bytes 1191944 | tf_op jit(solution)/shard_map/ppermute | solution.py:323
  103.2 6.7 %collective-permute-start.9 = (f32[392,128]{1,0:T(8,128)S(1)}, f32[392,128]{1,0:T(8,128)S(1)}, u32[]{:S(2)}, u32[]{:S(2)}) collective-permute-start(f32[392,128]{1,0:T(8,128)S(1)} %pad_maximum_fusion.12), channel_id=1, source_target_pairs={{0,8},{1,5},{2,10},{3,7},{4,12},{5,1},{6,14},{7,3},{8,0},{9,13},{1... | collective-permute-start | bytes 602120 | tf_op jit(solution)/shard_map/ppermute | solution.py:323
  109.5 8.0 %collective-permute-start.28 = (f32[392,128]{1,0:T(8,128)S(1)}, f32[392,128]{1,0:T(8,128)S(1)}, u32[]{:S(2)}, u32[]{:S(2)}) collective-permute-start(f32[392,128]{1,0:T(8,128)S(1)} %pad_maximum_fusion.18), channel_id=1, source_target_pairs={{0,8},{1,5},{2,10},{3,7},{4,12},{5,1},{6,14},{7,3},{8,0},{9,13},{1... | collective-permute-start | bytes 602120 | tf_op jit(solution)/shard_map/ppermute | solution.py:323
  110.0 17.1 %collective-permute-start.10 = (f32[392,128]{1,0:T(8,128)S(1)}, f32[392,128]{1,0:T(8,128)S(1)}, u32[]{:S(2)}, u32[]{:S(2)}) collective-permute-start(f32[392,128]{1,0:T(8,128)S(1)} %pad_maximum_fusion.13), channel_id=1, source_target_pairs={{0,16},{1,17},{2,18},{3,19},{4,20},{5,21},{6,22},{7,23},{8,24},{9,... | collective-permute-start | bytes 602120 | tf_op jit(solution)/shard_map/ppermute | solution.py:323
  117.6 12.7 %collective-permute-start.29 = (f32[392,128]{1,0:T(8,128)S(1)}, f32[392,128]{1,0:T(8,128)S(1)}, u32[]{:S(2)}, u32[]{:S(2)}) collective-permute-start(f32[392,128]{1,0:T(8,128)S(1)} %pad_maximum_fusion.19), channel_id=1, source_target_pairs={{0,16},{1,17},{2,18},{3,19},{4,20},{5,21},{6,22},{7,23},{8,24},{9,... | collective-permute-start | bytes 602120 | tf_op jit(solution)/shard_map/ppermute | solution.py:323
  127.1 5.7 %collective-permute-start.11 = (f32[384,128]{1,0:T(8,128)S(1)}, f32[384,128]{1,0:T(8,128)S(1)}, u32[]{:S(2)}, u32[]{:S(2)}) collective-permute-start(f32[384,128]{1,0:T(8,128)S(1)} %slice_add_fusion.22.refs_3_), channel_id=1, source_target_pairs={{0,8},{1,5},{2,10},{3,7},{4,12},{5,1},{6,14},{7,3},{8,0},{9,13},{1... | collective-permute-start | bytes 589832 | tf_op jit(solution)/shard_map/ppermute | solution.py:323
  130.3 7.8 %collective-permute-start.30 = (f32[384,128]{1,0:T(8,128)S(1)}, f32[384,128]{1,0:T(8,128)S(1)}, u32[]{:S(2)}, u32[]{:S(2)}) collective-permute-start(f32[384,128]{1,0:T(8,128)S(1)} %slice_add_fusion.17.refs_3_), channel_id=1, source_target_pairs={{0,8},{1,5},{2,10},{3,7},{4,12},{5,1},{6,14},{7,3},{8,0},{9,13},{1... | collective-permute-start | bytes 589832 | tf_op jit(solution)/shard_map/ppermute | solution.py:323
  132.9 7.8 %collective-permute-start.12 = (f32[768,128]{1,0:T(8,128)S(1)}, f32[768,128]{1,0:T(8,128)S(1)}, u32[]{:S(2)}, u32[]{:S(2)}) collective-permute-start(f32[768,128]{1,0:T(8,128)S(1)} %pad_maximum_fusion.1), channel_id=1, source_target_pairs={{0,4},{1,9},{2,6},{3,11},{4,0},{5,13},{6,2},{7,15},{8,12},{9,1},{1... | collective-permute-start | bytes 1179656 | tf_op jit(solution)/shard_map/ppermute | solution.py:323
  138.2 7.8 %collective-permute-start.31 = (f32[768,128]{1,0:T(8,128)S(1)}, f32[768,128]{1,0:T(8,128)S(1)}, u32[]{:S(2)}, u32[]{:S(2)}) collective-permute-start(f32[768,128]{1,0:T(8,128)S(1)} %pad_maximum_fusion.3), channel_id=1, source_target_pairs={{0,4},{1,9},{2,6},{3,11},{4,0},{5,13},{6,2},{7,15},{8,12},{9,1},{1... | collective-permute-start | bytes 1179656 | tf_op jit(solution)/shard_map/ppermute | solution.py:323
  144.3 5.4 %collective-permute-start.13 = (f32[520,128]{1,0:T(8,128)S(1)}, f32[520,128]{1,0:T(8,128)S(1)}, u32[]{:S(2)}, u32[]{:S(2)}) collective-permute-start(f32[520,128]{1,0:T(8,128)S(1)} %get-tuple-element.44), channel_id=1, source_target_pairs={{0,1},{1,0},{2,3},{3,2},{4,5},{5,4},{6,7},{7,6},{8,9},{9,8},{10,11... | collective-permute-start | bytes 798728 | tf_op jit(solution)/shard_map/ppermute | solution.py:326
  149.6 1.9 collective-permute-start.32
  149.7 9.3 %collective-permute-start.14 = (f32[520,128]{1,0:T(8,128)S(1)}, f32[520,128]{1,0:T(8,128)S(1)}, u32[]{:S(2)}, u32[]{:S(2)}) collective-permute-start(f32[520,128]{1,0:T(8,128)S(1)} %pad_maximum_fusion.7), channel_id=1, source_target_pairs={{0,2},{1,3},{2,0},{3,1},{4,6},{5,7},{6,4},{7,5},{8,10},{9,11},{10,... | collective-permute-start | bytes 798728 | tf_op jit(solution)/shard_map/ppermute | solution.py:326
  151.5 12.8 %collective-permute-start.33 = (f32[520,128]{1,0:T(8,128)S(1)}, f32[520,128]{1,0:T(8,128)S(1)}, u32[]{:S(2)}, u32[]{:S(2)}) collective-permute-start(f32[520,128]{1,0:T(8,128)S(1)} %pad_maximum_fusion.9), channel_id=1, source_target_pairs={{0,2},{1,3},{2,0},{3,1},{4,6},{5,7},{6,4},{7,5},{8,10},{9,11},{10,... | collective-permute-start | bytes 798728 | tf_op jit(solution)/shard_map/ppermute | solution.py:326
  159.0 5.4 %collective-permute-start.15 = (f32[512,128]{1,0:T(8,128)S(1)}, f32[512,128]{1,0:T(8,128)S(1)}, u32[]{:S(2)}, u32[]{:S(2)}) collective-permute-start(f32[512,128]{1,0:T(8,128)S(1)} %slice_add_fusion.10.refs_2_), channel_id=1, source_target_pairs={{0,1},{1,0},{2,3},{3,2},{4,5},{5,4},{6,7},{7,6},{8,9},{9,8},{10,11... | collective-permute-start | bytes 786440 | tf_op jit(solution)/shard_map/ppermute | solution.py:326
  164.3 4.4 %collective-permute-start.34 = (f32[512,128]{1,0:T(8,128)S(1)}, f32[512,128]{1,0:T(8,128)S(1)}, u32[]{:S(2)}, u32[]{:S(2)}) collective-permute-start(f32[512,128]{1,0:T(8,128)S(1)} %slice_add_fusion.6.refs_2_), channel_id=1, source_target_pairs={{0,1},{1,0},{2,3},{3,2},{4,5},{5,4},{6,7},{7,6},{8,9},{9,8},{10,11... | collective-permute-start | bytes 786440 | tf_op jit(solution)/shard_map/ppermute | solution.py:326
  167.0 7.9 %collective-permute-start.16 = (f32[776,128]{1,0:T(8,128)S(1)}, f32[776,128]{1,0:T(8,128)S(1)}, u32[]{:S(2)}, u32[]{:S(2)}) collective-permute-start(f32[776,128]{1,0:T(8,128)S(1)} %get-tuple-element.47), channel_id=1, source_target_pairs={{0,4},{1,9},{2,6},{3,11},{4,0},{5,13},{6,2},{7,15},{8,12},{9,1},{1... | collective-permute-start | bytes 1191944 | tf_op jit(solution)/shard_map/ppermute | solution.py:323
  171.4 9.9 %collective-permute-start.35 = (f32[776,128]{1,0:T(8,128)S(1)}, f32[776,128]{1,0:T(8,128)S(1)}, u32[]{:S(2)}, u32[]{:S(2)}) collective-permute-start(f32[776,128]{1,0:T(8,128)S(1)} %get-tuple-element.61), channel_id=1, source_target_pairs={{0,4},{1,9},{2,6},{3,11},{4,0},{5,13},{6,2},{7,15},{8,12},{9,1},{1... | collective-permute-start | bytes 1191944 | tf_op jit(solution)/shard_map/ppermute | solution.py:323
  175.0 6.6 %collective-permute-start.17 = (f32[392,128]{1,0:T(8,128)S(1)}, f32[392,128]{1,0:T(8,128)S(1)}, u32[]{:S(2)}, u32[]{:S(2)}) collective-permute-start(f32[392,128]{1,0:T(8,128)S(1)} %pad_maximum_fusion.14), channel_id=1, source_target_pairs={{0,8},{1,5},{2,10},{3,7},{4,12},{5,1},{6,14},{7,3},{8,0},{9,13},{1... | collective-permute-start | bytes 602120 | tf_op jit(solution)/shard_map/ppermute | solution.py:323
  181.5 7.5 %collective-permute-start.36 = (f32[392,128]{1,0:T(8,128)S(1)}, f32[392,128]{1,0:T(8,128)S(1)}, u32[]{:S(2)}, u32[]{:S(2)}) collective-permute-start(f32[392,128]{1,0:T(8,128)S(1)} %pad_maximum_fusion.20), channel_id=1, source_target_pairs={{0,8},{1,5},{2,10},{3,7},{4,12},{5,1},{6,14},{7,3},{8,0},{9,13},{1... | collective-permute-start | bytes 602120 | tf_op jit(solution)/shard_map/ppermute | solution.py:323
  181.6 16.7 %collective-permute-start.18 = (f32[392,128]{1,0:T(8,128)S(1)}, f32[392,128]{1,0:T(8,128)S(1)}, u32[]{:S(2)}, u32[]{:S(2)}) collective-permute-start(f32[392,128]{1,0:T(8,128)S(1)} %pad_maximum_fusion.15), channel_id=1, source_target_pairs={{0,16},{1,17},{2,18},{3,19},{4,20},{5,21},{6,22},{7,23},{8,24},{9,... | collective-permute-start | bytes 602120 | tf_op jit(solution)/shard_map/ppermute | solution.py:323
  189.0 13.2 %collective-permute-start.37 = (f32[392,128]{1,0:T(8,128)S(1)}, f32[392,128]{1,0:T(8,128)S(1)}, u32[]{:S(2)}, u32[]{:S(2)}) collective-permute-start(f32[392,128]{1,0:T(8,128)S(1)} %pad_maximum_fusion.21), channel_id=1, source_target_pairs={{0,16},{1,17},{2,18},{3,19},{4,20},{5,21},{6,22},{7,23},{8,24},{9,... | collective-permute-start | bytes 602120 | tf_op jit(solution)/shard_map/ppermute | solution.py:323
  198.3 6.0 %collective-permute-start.38 = (f32[384,128]{1,0:T(8,128)S(1)}, f32[384,128]{1,0:T(8,128)S(1)}, u32[]{:S(2)}, u32[]{:S(2)}) collective-permute-start(f32[384,128]{1,0:T(8,128)S(1)} %slice_add_fusion.15.refs_2_), channel_id=1, source_target_pairs={{0,8},{1,5},{2,10},{3,7},{4,12},{5,1},{6,14},{7,3},{8,0},{9,13},{1... | collective-permute-start | bytes 589832 | tf_op jit(solution)/shard_map/ppermute | solution.py:323
  202.3 7.8 %collective-permute-start.40 = (f32[384,128]{1,0:T(8,128)S(1)}, f32[384,128]{1,0:T(8,128)S(1)}, u32[]{:S(2)}, u32[]{:S(2)}) collective-permute-start(f32[384,128]{1,0:T(8,128)S(1)} %slice_add_fusion.14.refs_11_), channel_id=1, source_target_pairs={{0,8},{1,5},{2,10},{3,7},{4,12},{5,1},{6,14},{7,3},{8,0},{9,13},{1... | collective-permute-start | bytes 589832 | tf_op jit(solution)/shard_map/ppermute | solution.py:323
  204.4 9.2 %collective-permute-start.39 = (f32[768,128]{1,0:T(8,128)S(1)}, f32[768,128]{1,0:T(8,128)S(1)}, u32[]{:S(2)}, u32[]{:S(2)}) collective-permute-start(f32[768,128]{1,0:T(8,128)S(1)} %pad_maximum_fusion.4), channel_id=1, source_target_pairs={{0,4},{1,9},{2,6},{3,11},{4,0},{5,13},{6,2},{7,15},{8,12},{9,1},{1... | collective-permute-start | bytes 1179656 | tf_op jit(solution)/shard_map/ppermute | solution.py:323
  210.1 7.8 %collective-permute-start.41 = (f32[768,128]{1,0:T(8,128)S(1)}, f32[768,128]{1,0:T(8,128)S(1)}, u32[]{:S(2)}, u32[]{:S(2)}) collective-permute-start(f32[768,128]{1,0:T(8,128)S(1)} %pad_maximum_fusion.5), channel_id=1, source_target_pairs={{0,4},{1,9},{2,6},{3,11},{4,0},{5,13},{6,2},{7,15},{8,12},{9,1},{1... | collective-permute-start | bytes 1179656 | tf_op jit(solution)/shard_map/ppermute | solution.py:323

commit v6 on v5

--- a/solution.py
+++ b/solution.py
@@ -13,7 +13,7 @@
 PAIR = 2 * TILE
 UNITS = 4
 NORM_ROWS = 8
-BUFFERS = 4
+BEHIND = 2
 
 tiny_eps = 1e-06
 
@@ -34,66 +34,43 @@
 
 
 def fill_kernel(
-    pattern_ref, count_ref, place_ref, flip_ref, delays_ref, tiles_ref,
-    dense_ref, *rest,
+    pattern_ref, count_ref, place_ref, flip_ref, delays_ref, tiles_ref, dense_ref, *left_refs
 ):
-    left_refs, (buffer_ref, arrived) = rest[:-2], rest[-2:]
-    row_blocks = tiles_ref.shape[0]
     flip = flip_ref[0]
-
-    def fetch(position, slot):
-        return pltpu.make_async_copy(
-            tiles_ref.at[position ^ flip], buffer_ref.at[slot], arrived.at[slot]
-        )
-
-    for position in range(BUFFERS):
-        fetch(position, position).start()
-
     low = low_lanes((TILE, TILE))
-    for pair in range(row_blocks // 2):
+    for pair in range(delays_ref.shape[0] // PAIR):
         source = (pair ^ (flip // 2)) * PAIR
         even = delays_ref[pl.ds(pl.multiple_of(source, TILE), TILE), :]
         odd = delays_ref[pl.ds(pl.multiple_of(source + TILE, TILE), TILE), :]
         left_refs[0][rows_of(pair), :] = jnp.where(low, even, turned(odd))
         left_refs[1][rows_of(pair), :] = jnp.where(low, turned(even), odd)
 
-    @pl.loop(0, row_blocks)
+    @pl.loop(0, tiles_ref.shape[0])
     def _(position):
-        slot = lax.rem(position, BUFFERS)
         rows = pl.ds(pl.multiple_of(position * TILE, TILE), TILE)
         dense_ref[rows, :] = jnp.zeros((TILE, dense_ref.shape[1]), dense_ref.dtype)
-        fetch(position, slot).wait()
         block = position ^ flip
 
-        @pl.loop(0, count_ref[block, 0])
+        @pl.loop(0, count_ref[block])
         def _(tile):
             place = place_ref[pattern_ref[block, tile]]
             lanes = pl.ds(pl.multiple_of(place * TILE, TILE), TILE)
-            dense_ref[rows, lanes] = buffer_ref[slot, tile]
-
-        @pl.when(position + BUFFERS < row_blocks)
-        def _():
-            fetch(position + BUFFERS, slot).start()
+            dense_ref[rows, lanes] = tiles_ref[block, tile]
 
 
 def fill_dense(kernel, pattern, counts, places, flip, delays):
-    row_blocks, slot_count = kernel.shape[:2]
-    rows = row_blocks * TILE
+    rows = kernel.shape[0] * TILE
     left = jax.ShapeDtypeStruct((rows // 2, TILE), jnp.float32)
     return pl.pallas_call(
         fill_kernel,
-        in_specs=[SCALARS] * 4 + [WHOLE, pl.BlockSpec(memory_space=pl.ANY)],
+        in_specs=[SCALARS] * 4 + [WHOLE] * 2,
         out_specs=[WHOLE] * 3,
         out_shape=[jax.ShapeDtypeStruct((rows, CB_DEV * TILE), kernel.dtype), left, left],
-        scratch_shapes=[
-            pltpu.VMEM((BUFFERS, slot_count, TILE, TILE), kernel.dtype),
-            pltpu.SemaphoreType.DMA((BUFFERS,)),
-        ],
-        compiler_params=pltpu.CompilerParams(vmem_limit_bytes=46 * 1024 * 1024),
+        compiler_params=pltpu.CompilerParams(vmem_limit_bytes=12 * 1024 * 1024),
         cost_estimate=pl.CostEstimate(
             flops=0, bytes_accessed=2 * kernel.size, transcendentals=0
         ),
-    )(pattern, counts, places, flip, delays, kernel)
+    )(pattern, counts.reshape(-1), places, flip, delays, kernel)
 
 
 def norm_of(ref):
@@ -341,7 +318,7 @@
         got = swap(jnp.concatenate([value, norm]))
         return got[: value.shape[0]], norm + got[value.shape[0] :]
 
-    def reduce_rows(send, keep):
+    def reduce_rows(send, keep, swap_rows):
         half = keep.shape[0]
         got = swap_rows(send, 0)
         keep = keep + got[:half]
@@ -355,7 +332,7 @@
         outer = swap_rows(jnp.concatenate([inner, mine]), 0)
         return [outer, inner, mine], norm
 
-    def reduce_cols(send, keep):
+    def reduce_cols(send, keep, swap_cols):
         half = keep.shape[0]
         got = swap_cols(send, 0)
         own = keep + got[:half]
@@ -365,25 +342,40 @@
             own = own + got
         return [swap_cols(own, 0), own], norm
 
-    def chain(left):
+    def chain(left, leader):
+        gots = []
+
+        def follow(swap):
+            def one(value, level):
+                ahead = len(gots) + BEHIND - 1
+                if ahead < len(leader):
+                    value = lax.optimization_barrier((value, leader[ahead]))[0]
+                gots.append(swap(value, level))
+                return gots[-1]
+
+            return one
+
+        rows, cols = follow(swap_rows), follow(swap_cols)
         send, keep = back_product(dense, [left], True)
-        totals, norm = reduce_rows(send, keep)
+        totals, norm = reduce_rows(send, keep, rows)
         norms = [norm]
         rights = []
         for iteration in range(ITERS):
             past = [rights[-1], norms[-2]] if rights else []
             send, keep, right = fore_product(dense, [*totals, norms[-1], *past], not rights)
             rights.append(right)
-            halves, norm = reduce_cols(send, keep)
+            halves, norm = reduce_cols(send, keep, cols)
             norms.append(norm)
             send, keep, left = back_product(
                 dense, [*halves, norms[-1], left, norms[-2]], False
             )
-            totals, norm = reduce_rows(send, keep)
+            totals, norm = reduce_rows(send, keep, rows)
             norms.append(norm)
-        return rights, norms, totals
-
-    chains = [chain(left) for left in lefts]
+        return (rights, norms, totals), gots
+
+    ahead, gots = chain(lefts[0], [])
+    behind, _ = chain(lefts[1], gots)
+    chains = [ahead, behind]
     cells = dense.shape[1]
     model, misfit = last_call(
         functools.partial(model_kernel, ITERS),

time: 220 us -> 209 us (0.950)
  Pallas kernels: 44.2 us -> 36.8 us
  waiting for transfers between devices: 121 us -> 118 us
    ppermute x12, waiting for transfers between devices: 22.6 us -> 9.39 us  [swap_cols(): lax.ppermute(value, 'cols', [(i, i ^ 1 << level) for i in range(col_count)])]
    ppermute x30, waiting for transfers between devices: 98.5 us -> 109 us  [swap_rows(): return lax.ppermute(value, ('rows', 'cols'), pairs)]
    pallas_call x1, Pallas kernels: 11.2 us -> 3.8 us  [fill_dense(): pl.pallas_call(fill_kernel, in_specs=[SCALARS] * 4 + [WHOLE] * 2, out_spe...]
    ppermute x12, starting transfers between devices: 6.7 us -> 14 us  [swap_cols(): lax.ppermute(value, 'cols', [(i, i ^ 1 << level) for i in range(col_count)])]
    ppermute x30, starting transfers between devices: 37.1 us -> 31.8 us  [swap_rows(): return lax.ppermute(value, ('rows', 'cols'), pairs)]
    unnamed x13 -> x8, local copies, waits for them, and re-layouts: 7.23 us -> 5.95 us
  transfers between devices with their start and end apart: 42 -> 42, of which waited for: 30 -> 31; matrix products, arithmetic and copies ran while one was open for 1% -> 1% of each run, Pallas kernels for 13% -> 14%
where the time goes in v6:
time: 209 us; the launch traced here: 210 us
  waiting for transfers between devices  118 us (56%)
  starting transfers between devices  45.8 us (22%)
  Pallas kernels  36.8 us (18%)
  local copies, waits for them, and re-layouts  6.55 us (3%)
    ppermute x30, waiting for transfers between devices, swap_rows(): return lax.ppermute(value, ('rows', 'cols'), pairs)  109 us
    ppermute x30, starting transfers between devices, swap_rows(): return lax.ppermute(value, ('rows', 'cols'), pairs)  31.8 us
    pallas_call x10, Pallas kernels, product_call(): pl.pallas_call(body, in_specs=[WHOLE] * (1 + len(operands)), out_specs=[W...  29.6 us
    ppermute x12, starting transfers between devices, swap_cols(): lax.ppermute(value, 'cols', [(i, i ^ 1 << level) for i in range(col_count)])  14 us
    ppermute x12, waiting for transfers between devices, swap_cols(): lax.ppermute(value, 'cols', [(i, i ^ 1 << level) for i in range(col_count)])  9.39 us
    unnamed x8, local copies, waits for them, and re-layouts  5.95 us
  transfers between devices with their start and end apart: 42, of which 31 were waited for; matrix products, arithmetic and copies ran while one was open for 1% of the time, Pallas kernels for 14%

profile of v6, /device:TPU:0, one launch (start us, length us, event | category | flops | bytes accessed | tf_op | source)
XLA Modules:
  0.0 209.9 jit_solution(9745639821905618906)
XLA Ops:
  0.7 3.4 %copy-done = bf16[16,16,128,128]{3,2,1,0:T(8,128)(2,1)S(1)} copy-done((bf16[16,16,128,128]{3,2,1,0:T(8,128)(2,1)S(1)}, bf16[16,16,128,128]{3,2,1,0:T(8,128)(2,1)}, u32[]{:S(2)}) %copy-start) | copy-done | bytes 8388632
  6.6 3.8 %shard_map.67 = (bf16[2048,3072]{1,0:T(8,128)(2,1)S(1)}, f32[1024,128]{1,0:T(8,128)S(1)}, f32[1024,128]{1,0:T(8,128)S(1)}) custom-call(s32[16,16]{1,0:T(8,128)S(1)} %copy-done.2, s32[16]{0:T(128)S(1)} %bitcast.5, s32[24]{0:T(128)S(1)} %fusion.place_ref, s32[1]{0:T(128)} %bitcast.2.flip_ref, f32[2048,128]{1,0:T(8,128)S(1)} %copy-done.1, ...), custom_call_target="tpu_custom_call" | custom-call | bytes 8388608 | tf_op jit(solution)/shard_map/pallas_call | solution.py:64
  10.4 2.5 %shard_map.68 = (f32[776,128]{1,0:T(8,128)S(1)}, f32[768,128]{1,0:T(8,128)S(1)}) custom-call(bf16[2048,3072]{1,0:T(8,128)(2,1)S(1)} %get-tuple-element.54.refs_0_, f32[1024,128]{1,0:T(8,128)S(1)} %get-tuple-element.55.refs_1_.refs_4_), custom_call_target="tpu_custom_call" | custom-call | flops 3221225472 | bytes 12582912 | tf_op jit(solution)/shard_map/pallas_call | solution.py:180
  14.6 6.2 %collective-permute-done = f32[776,128]{1,0:T(8,128)S(1)} collective-permute-done((f32[776,128]{1,0:T(8,128)S(1)}, f32[776,128]{1,0:T(8,128)S(1)}, u32[]{:S(2)}, u32[]{:S(2)}) %collective-permute-start) | collective-permute-done | bytes 397344 | tf_op jit(solution)/shard_map/ppermute | solution.py:300
  20.9 3.1 %collective-permute-start.1 = (f32[392,128]{1,0:T(8,128)S(1)}, f32[392,128]{1,0:T(8,128)S(1)}, u32[]{:S(2)}, u32[]{:S(2)}) collective-permute-start(f32[392,128]{1,0:T(8,128)S(1)} %pad_maximum_fusion.10), channel_id=1, source_target_pairs={{0,8},{1,5},{2,10},{3,7},{4,12},{5,1},{6,14},{7,3},{8,0},{9,13},{1... | collective-permute-start | bytes 602120 | tf_op jit(solution)/shard_map/ppermute | solution.py:300
  24.0 3.7 %collective-permute-done.1 = f32[392,128]{1,0:T(8,128)S(1)} collective-permute-done((f32[392,128]{1,0:T(8,128)S(1)}, f32[392,128]{1,0:T(8,128)S(1)}, u32[]{:S(2)}, u32[]{:S(2)}) %collective-permute-start.1) | collective-permute-done | bytes 200736 | tf_op jit(solution)/shard_map/ppermute | solution.py:300
  27.8 2.8 %collective-permute-start.2 = (f32[392,128]{1,0:T(8,128)S(1)}, f32[392,128]{1,0:T(8,128)S(1)}, u32[]{:S(2)}, u32[]{:S(2)}) collective-permute-start(f32[392,128]{1,0:T(8,128)S(1)} %pad_maximum_fusion.11), channel_id=1, source_target_pairs={{0,16},{1,17},{2,18},{3,19},{4,20},{5,21},{6,22},{7,23},{8,24},{9,... | collective-permute-start | bytes 602120 | tf_op jit(solution)/shard_map/ppermute | solution.py:300
  30.6 2.5 %shard_map.73 = (f32[776,128]{1,0:T(8,128)S(1)}, f32[768,128]{1,0:T(8,128)S(1)}) custom-call(bf16[2048,3072]{1,0:T(8,128)(2,1)S(1)} %get-tuple-element.54.refs_0_, f32[1024,128]{1,0:T(8,128)S(1)} %get-tuple-element.69.refs_1_.refs_4_), custom_call_target="tpu_custom_call" | custom-call | flops 3221225472 | bytes 12582912 | tf_op jit(solution)/shard_map/pallas_call | solution.py:180
  34.8 3.9 %collective-permute-done.2 = f32[392,128]{1,0:T(8,128)S(1)} collective-permute-done((f32[392,128]{1,0:T(8,128)S(1)}, f32[392,128]{1,0:T(8,128)S(1)}, u32[]{:S(2)}, u32[]{:S(2)}) %collective-permute-start.2) | collective-permute-done | bytes 200736 | tf_op jit(solution)/shard_map/ppermute | solution.py:300
  39.4 3.7 %collective-permute-done.19 = f32[776,128]{1,0:T(8,128)S(1)} collective-permute-done((f32[776,128]{1,0:T(8,128)S(1)}, f32[776,128]{1,0:T(8,128)S(1)}, u32[]{:S(2)}, u32[]{:S(2)}) %collective-permute-start.19) | collective-permute-done | bytes 397344 | tf_op jit(solution)/shard_map/ppermute | solution.py:300
  46.2 7.1 %collective-permute-done.20 = f32[392,128]{1,0:T(8,128)S(1)} collective-permute-done((f32[392,128]{1,0:T(8,128)S(1)}, f32[392,128]{1,0:T(8,128)S(1)}, u32[]{:S(2)}, u32[]{:S(2)}) %collective-permute-start.20) | collective-permute-done | bytes 200736 | tf_op jit(solution)/shard_map/ppermute | solution.py:300
  53.4 3.5 %shard_map.69 = (f32[520,128]{1,0:T(8,128)S(1)}, f32[512,128]{1,0:T(8,128)S(1)}, f32[1536,128]{1,0:T(8,128)S(1)}) custom-call(bf16[2048,3072]{1,0:T(8,128)(2,1)S(1)} %get-tuple-element.54.refs_0_, f32[768,128]{1,0:T(8,128)S(1)} %collective-permute-done.4.refs_1_, f32[384,128]{1,0:T(8,128)S(1)} %collective-permute-done.3.refs_2_, ...), custom_call_target="tpu_custom_call" | custom-call | flops 3221225472 | bytes 12582912 | tf_op jit(solution)/shard_map/pallas_call | solution.py:180
  58.0 3.1 %collective-permute-done.21 = f32[392,128]{1,0:T(8,128)S(1)} collective-permute-done((f32[392,128]{1,0:T(8,128)S(1)}, f32[392,128]{1,0:T(8,128)S(1)}, u32[]{:S(2)}, u32[]{:S(2)}) %collective-permute-start.21) | collective-permute-done | bytes 200736 | tf_op jit(solution)/shard_map/ppermute | solution.py:300
  61.3 3.1 %collective-permute-start.6 = (f32[520,128]{1,0:T(8,128)S(1)}, f32[520,128]{1,0:T(8,128)S(1)}, u32[]{:S(2)}, u32[]{:S(2)}) collective-permute-start(f32[520,128]{1,0:T(8,128)S(1)} %pad_maximum_fusion.6), channel_id=1, source_target_pairs={{0,2},{1,3},{2,0},{3,1},{4,6},{5,7},{6,4},{7,5},{8,10},{9,11},{10,... | collective-permute-start | bytes 798728 | tf_op jit(solution)/shard_map/ppermute | solution.py:303
  64.5 4.0 %collective-permute-done.22.refs_2_ = f32[384,128]{1,0:T(8,128)S(1)} collective-permute-done((f32[384,128]{1,0:T(8,128)S(1)}, f32[384,128]{1,0:T(8,128)S(1)}, u32[]{:S(2)}, u32[]{:S(2)}) %collective-permute-start.22) | collective-permute-done | bytes 196640 | tf_op jit(solution)/shard_map/ppermute | solution.py:300
  70.2 6.1 %collective-permute-done.23.refs_1_ = f32[768,128]{1,0:T(8,128)S(1)} collective-permute-done((f32[768,128]{1,0:T(8,128)S(1)}, f32[768,128]{1,0:T(8,128)S(1)}, u32[]{:S(2)}, u32[]{:S(2)}) %collective-permute-start.23) | collective-permute-done | bytes 393248 | tf_op jit(solution)/shard_map/ppermute | solution.py:300
  76.3 3.5 %shard_map.74 = (f32[520,128]{1,0:T(8,128)S(1)}, f32[512,128]{1,0:T(8,128)S(1)}, f32[1536,128]{1,0:T(8,128)S(1)}) custom-call(bf16[2048,3072]{1,0:T(8,128)(2,1)S(1)} %get-tuple-element.54.refs_0_, f32[768,128]{1,0:T(8,128)S(1)} %collective-permute-done.23.refs_1_, f32[384,128]{1,0:T(8,128)S(1)} %collective-permute-done.22.refs_2_, ...), custom_call_target="tpu_custom_call" | custom-call | flops 3221225472 | bytes 12582912 | tf_op jit(solution)/shard_map/pallas_call | solution.py:180
  79.9 2.7 %shard_map.70 = (f32[776,128]{1,0:T(8,128)S(1)}, f32[768,128]{1,0:T(8,128)S(1)}, f32[1024,128]{1,0:T(8,128)S(1)}) custom-call(bf16[2048,3072]{1,0:T(8,128)(2,1)S(1)} %get-tuple-element.54.refs_0_, f32[512,128]{1,0:T(8,128)S(1)} %collective-permute-done.7.refs_1_, f32[512,128]{1,0:T(8,128)S(1)} %slice_add_fusion.12.refs_2_, ...), custom_call_target="tpu_custom_call" | custom-call | flops 3221225472 | bytes 12582912 | tf_op jit(solution)/shard_map/pallas_call | solution.py:180
  84.3 2.1 %collective-permute-start.25 = (f32[520,128]{1,0:T(8,128)S(1)}, f32[520,128]{1,0:T(8,128)S(1)}, u32[]{:S(2)}, u32[]{:S(2)}) collective-permute-start(f32[520,128]{1,0:T(8,128)S(1)} %pad_maximum_fusion.8), channel_id=1, source_target_pairs={{0,2},{1,3},{2,0},{3,1},{4,6},{5,7},{6,4},{7,5},{8,10},{9,11},{10,... | collective-permute-start | bytes 798728 | tf_op jit(solution)/shard_map/ppermute | solution.py:303
  86.5 4.0 %collective-permute-done.8 = f32[776,128]{1,0:T(8,128)S(1)} collective-permute-done((f32[776,128]{1,0:T(8,128)S(1)}, f32[776,128]{1,0:T(8,128)S(1)}, u32[]{:S(2)}, u32[]{:S(2)}) %collective-permute-start.8) | collective-permute-done | bytes 397344 | tf_op jit(solution)/shard_map/ppermute | solution.py:300
  90.7 2.8 %collective-permute-done.25 = f32[520,128]{1,0:T(8,128)S(1)} collective-permute-done((f32[520,128]{1,0:T(8,128)S(1)}, f32[520,128]{1,0:T(8,128)S(1)}, u32[]{:S(2)}, u32[]{:S(2)}) %collective-permute-start.25) | collective-permute-done | bytes 266272 | tf_op jit(solution)/shard_map/ppermute | solution.py:303
  93.6 2.8 %collective-permute-done.9 = f32[392,128]{1,0:T(8,128)S(1)} collective-permute-done((f32[392,128]{1,0:T(8,128)S(1)}, f32[392,128]{1,0:T(8,128)S(1)}, u32[]{:S(2)}, u32[]{:S(2)}) %collective-permute-start.9) | collective-permute-done | bytes 200736 | tf_op jit(solution)/shard_map/ppermute | solution.py:300
  96.5 2.5 %shard_map.75 = (f32[776,128]{1,0:T(8,128)S(1)}, f32[768,128]{1,0:T(8,128)S(1)}, f32[1024,128]{1,0:T(8,128)S(1)}) custom-call(bf16[2048,3072]{1,0:T(8,128)(2,1)S(1)} %get-tuple-element.54.refs_0_, f32[512,128]{1,0:T(8,128)S(1)} %collective-permute-done.26.refs_1_, f32[512,128]{1,0:T(8,128)S(1)} %slice_add_fusion.8.refs_2_, ...), custom_call_target="tpu_custom_call" | custom-call | flops 3221225472 | bytes 12582912 | tf_op jit(solution)/shard_map/pallas_call | solution.py:180
  100.7 6.5 %collective-permute-done.10 = f32[392,128]{1,0:T(8,128)S(1)} collective-permute-done((f32[392,128]{1,0:T(8,128)S(1)}, f32[392,128]{1,0:T(8,128)S(1)}, u32[]{:S(2)}, u32[]{:S(2)}) %collective-permute-start.10) | collective-permute-done | bytes 200736 | tf_op jit(solution)/shard_map/ppermute | solution.py:300
  107.5 2.1 collective-permute-start.28
  109.5 3.5 %collective-permute-done.11.refs_2_ = f32[384,128]{1,0:T(8,128)S(1)} collective-permute-done((f32[384,128]{1,0:T(8,128)S(1)}, f32[384,128]{1,0:T(8,128)S(1)}, u32[]{:S(2)}, u32[]{:S(2)}) %collective-permute-start.11) | collective-permute-done | bytes 196640 | tf_op jit(solution)/shard_map/ppermute | solution.py:300
  115.5 2.2 %collective-permute-start.29 = (f32[392,128]{1,0:T(8,128)S(1)}, f32[392,128]{1,0:T(8,128)S(1)}, u32[]{:S(2)}, u32[]{:S(2)}) collective-permute-start(f32[392,128]{1,0:T(8,128)S(1)} %pad_maximum_fusion.19), channel_id=1, source_target_pairs={{0,16},{1,17},{2,18},{3,19},{4,20},{5,21},{6,22},{7,23},{8,24},{9,... | collective-permute-start | bytes 602120 | tf_op jit(solution)/shard_map/ppermute | solution.py:300
  117.7 3.2 %collective-permute-done.12.refs_1_ = f32[768,128]{1,0:T(8,128)S(1)} collective-permute-done((f32[768,128]{1,0:T(8,128)S(1)}, f32[768,128]{1,0:T(8,128)S(1)}, u32[]{:S(2)}, u32[]{:S(2)}) %collective-permute-start.12) | collective-permute-done | bytes 393248 | tf_op jit(solution)/shard_map/ppermute | solution.py:300
  120.9 3.5 %shard_map.71 = (f32[520,128]{1,0:T(8,128)S(1)}, f32[512,128]{1,0:T(8,128)S(1)}, f32[1536,128]{1,0:T(8,128)S(1)}) custom-call(bf16[2048,3072]{1,0:T(8,128)(2,1)S(1)} %get-tuple-element.54.refs_0_, f32[768,128]{1,0:T(8,128)S(1)} %collective-permute-done.12.refs_1_, f32[384,128]{1,0:T(8,128)S(1)} %collective-permute-done.11.refs_2_, ...), custom_call_target="tpu_custom_call" | custom-call | flops 3221225472 | bytes 12582912 | tf_op jit(solution)/shard_map/pallas_call | solution.py:180
  126.6 5.6 %collective-permute-done.30.refs_2_ = f32[384,128]{1,0:T(8,128)S(1)} collective-permute-done((f32[384,128]{1,0:T(8,128)S(1)}, f32[384,128]{1,0:T(8,128)S(1)}, u32[]{:S(2)}, u32[]{:S(2)}) %collective-permute-start.30) | collective-permute-done | bytes 196640 | tf_op jit(solution)/shard_map/ppermute | solution.py:300
  134.0 2.4 %collective-permute-start.14 = (f32[520,128]{1,0:T(8,128)S(1)}, f32[520,128]{1,0:T(8,128)S(1)}, u32[]{:S(2)}, u32[]{:S(2)}) collective-permute-start(f32[520,128]{1,0:T(8,128)S(1)} %pad_maximum_fusion.7), channel_id=1, source_target_pairs={{0,2},{1,3},{2,0},{3,1},{4,6},{5,7},{6,4},{7,5},{8,10},{9,11},{10,... | collective-permute-start | bytes 798728 | tf_op jit(solution)/shard_map/ppermute | solution.py:303
  136.4 3.7 %collective-permute-done.31.refs_1_ = f32[768,128]{1,0:T(8,128)S(1)} collective-permute-done((f32[768,128]{1,0:T(8,128)S(1)}, f32[768,128]{1,0:T(8,128)S(1)}, u32[]{:S(2)}, u32[]{:S(2)}) %collective-permute-start.31) | collective-permute-done | bytes 393248 | tf_op jit(solution)/shard_map/ppermute | solution.py:300
  140.1 3.5 %shard_map.76 = (f32[520,128]{1,0:T(8,128)S(1)}, f32[512,128]{1,0:T(8,128)S(1)}, f32[1536,128]{1,0:T(8,128)S(1)}) custom-call(bf16[2048,3072]{1,0:T(8,128)(2,1)S(1)} %get-tuple-element.54.refs_0_, f32[768,128]{1,0:T(8,128)S(1)} %collective-permute-done.31.refs_1_, f32[384,128]{1,0:T(8,128)S(1)} %collective-permute-done.30.refs_2_, ...), custom_call_target="tpu_custom_call" | custom-call | flops 3221225472 | bytes 12582912 | tf_op jit(solution)/shard_map/pallas_call | solution.py:180
  145.7 3.6 %collective-permute-start.33 = (f32[520,128]{1,0:T(8,128)S(1)}, f32[520,128]{1,0:T(8,128)S(1)}, u32[]{:S(2)}, u32[]{:S(2)}) collective-permute-start(f32[520,128]{1,0:T(8,128)S(1)} %pad_maximum_fusion.9), channel_id=1, source_target_pairs={{0,2},{1,3},{2,0},{3,1},{4,6},{5,7},{6,4},{7,5},{8,10},{9,11},{10,... | collective-permute-start | bytes 798728 | tf_op jit(solution)/shard_map/ppermute | solution.py:303
  149.3 2.5 %shard_map.72 = (f32[776,128]{1,0:T(8,128)S(1)}, f32[768,128]{1,0:T(8,128)S(1)}, f32[1024,128]{1,0:T(8,128)}) custom-call(bf16[2048,3072]{1,0:T(8,128)(2,1)S(1)} %get-tuple-element.54.refs_0_, f32[512,128]{1,0:T(8,128)S(1)} %collective-permute-done.15.refs_1_, f32[512,128]{1,0:T(8,128)S(1)} %slice_add_fusion.10.refs_2_, ...), custom_call_target="tpu_custom_call" | custom-call | flops 3221225472 | bytes 12582912 | tf_op jit(solution)/shard_map/pallas_call | solution.py:180
  152.2 3.9 %collective-permute-done.33 = f32[520,128]{1,0:T(8,128)S(1)} collective-permute-done((f32[520,128]{1,0:T(8,128)S(1)}, f32[520,128]{1,0:T(8,128)S(1)}, u32[]{:S(2)}, u32[]{:S(2)}) %collective-permute-start.33) | collective-permute-done | bytes 266272 | tf_op jit(solution)/shard_map/ppermute | solution.py:303
  156.1 3.6 %collective-permute-done.16 = f32[776,128]{1,0:T(8,128)S(1)} collective-permute-done((f32[776,128]{1,0:T(8,128)S(1)}, f32[776,128]{1,0:T(8,128)S(1)}, u32[]{:S(2)}, u32[]{:S(2)}) %collective-permute-start.16) | collective-permute-done | bytes 397344 | tf_op jit(solution)/shard_map/ppermute | solution.py:300
  161.4 2.7 %shard_map.77 = (f32[776,128]{1,0:T(8,128)S(1)}, f32[768,128]{1,0:T(8,128)S(1)}, f32[1024,128]{1,0:T(8,128)}) custom-call(bf16[2048,3072]{1,0:T(8,128)(2,1)S(1)} %get-tuple-element.54.refs_0_, f32[512,128]{1,0:T(8,128)S(1)} %collective-permute-done.34.refs_1_, f32[512,128]{1,0:T(8,128)S(1)} %slice_add_fusion.6.refs_2_, ...), custom_call_target="tpu_custom_call" | custom-call | flops 3221225472 | bytes 12582912 | tf_op jit(solution)/shard_map/pallas_call | solution.py:180
  166.1 7.4 %collective-permute-done.35 = f32[776,128]{1,0:T(8,128)S(1)} collective-permute-done((f32[776,128]{1,0:T(8,128)S(1)}, f32[776,128]{1,0:T(8,128)S(1)}, u32[]{:S(2)}, u32[]{:S(2)}) %collective-permute-start.35) | collective-permute-done | bytes 397344 | tf_op jit(solution)/shard_map/ppermute | solution.py:300
  173.6 4.0 %collective-permute-done.18 = f32[392,128]{1,0:T(8,128)S(1)} collective-permute-done((f32[392,128]{1,0:T(8,128)S(1)}, f32[392,128]{1,0:T(8,128)S(1)}, u32[]{:S(2)}, u32[]{:S(2)}) %collective-permute-start.18) | collective-permute-done | bytes 200736 | tf_op jit(solution)/shard_map/ppermute | solution.py:300
  177.6 2.1 collective-permute-start.37
  179.7 3.6 %collective-permute-done.36 = f32[392,128]{1,0:T(8,128)S(1)} collective-permute-done((f32[392,128]{1,0:T(8,128)S(1)}, f32[392,128]{1,0:T(8,128)S(1)}, u32[]{:S(2)}, u32[]{:S(2)}) %collective-permute-start.36) | collective-permute-done | bytes 200736 | tf_op jit(solution)/shard_map/ppermute | solution.py:300
  183.4 2.0 collective-permute-done.37.refs_1_
  185.4 1.7 collective-permute-start.39
  187.2 7.4 %collective-permute-done.38 = f32[392,128]{1,0:T(8,128)S(1)} collective-permute-done((f32[392,128]{1,0:T(8,128)S(1)}, f32[392,128]{1,0:T(8,128)S(1)}, u32[]{:S(2)}, u32[]{:S(2)}) %collective-permute-start.38) | collective-permute-done | bytes 200736 | tf_op jit(solution)/shard_map/ppermute | solution.py:300
  195.3 5.0 %collective-permute-done.40.refs_10_ = f32[384,128]{1,0:T(8,128)S(1)} collective-permute-done((f32[384,128]{1,0:T(8,128)S(1)}, f32[384,128]{1,0:T(8,128)S(1)}, u32[]{:S(2)}, u32[]{:S(2)}) %collective-permute-start.40) | collective-permute-done | bytes 196640 | tf_op jit(solution)/shard_map/ppermute | solution.py:300
  201.1 1.7 shard_map.78
  203.3 4.9 %collective-permute-done.41.refs_9_ = f32[768,128]{1,0:T(8,128)S(1)} collective-permute-done((f32[768,128]{1,0:T(8,128)S(1)}, f32[768,128]{1,0:T(8,128)S(1)}, u32[]{:S(2)}, u32[]{:S(2)}) %collective-permute-start.41) | collective-permute-done | bytes 393248 | tf_op jit(solution)/shard_map/ppermute | solution.py:300
  (139 shorter events, 33.1 us)
Async XLA Ops:
  0.7 3.4 %copy-start = (bf16[16,16,128,128]{3,2,1,0:T(8,128)(2,1)S(1)}, bf16[16,16,128,128]{3,2,1,0:T(8,128)(2,1)}, u32[]{:S(2)}) copy-start(bf16[16,16,128,128]{3,2,1,0:T(8,128)(2,1)} %tiles_ref.1) | copy-start | bytes 25165828
  4.1 1.2 copy-start.1
  5.3 0.7 copy-start.2
  6.0 0.7 copy-start.3
  12.9 7.9 %collective-permute-start = (f32[776,128]{1,0:T(8,128)S(1)}, f32[776,128]{1,0:T(8,128)S(1)}, u32[]{:S(2)}, u32[]{:S(2)}) collective-permute-start(f32[776,128]{1,0:T(8,128)S(1)} %get-tuple-element.57), channel_id=1, source_target_pairs={{0,4},{1,9},{2,6},{3,11},{4,0},{5,13},{6,2},{7,15},{8,12},{9,1},{1... | collective-permute-start | bytes 1191944 | tf_op jit(solution)/shard_map/ppermute | solution.py:300
  20.9 6.8 %collective-permute-start.1 = (f32[392,128]{1,0:T(8,128)S(1)}, f32[392,128]{1,0:T(8,128)S(1)}, u32[]{:S(2)}, u32[]{:S(2)}) collective-permute-start(f32[392,128]{1,0:T(8,128)S(1)} %pad_maximum_fusion.10), channel_id=1, source_target_pairs={{0,8},{1,5},{2,10},{3,7},{4,12},{5,1},{6,14},{7,3},{8,0},{9,13},{1... | collective-permute-start | bytes 602120 | tf_op jit(solution)/shard_map/ppermute | solution.py:300
  27.8 10.9 %collective-permute-start.2 = (f32[392,128]{1,0:T(8,128)S(1)}, f32[392,128]{1,0:T(8,128)S(1)}, u32[]{:S(2)}, u32[]{:S(2)}) collective-permute-start(f32[392,128]{1,0:T(8,128)S(1)} %pad_maximum_fusion.11), channel_id=1, source_target_pairs={{0,16},{1,17},{2,18},{3,19},{4,20},{5,21},{6,22},{7,23},{8,24},{9,... | collective-permute-start | bytes 602120 | tf_op jit(solution)/shard_map/ppermute | solution.py:300
  33.1 10.0 %collective-permute-start.19 = (f32[776,128]{1,0:T(8,128)S(1)}, f32[776,128]{1,0:T(8,128)S(1)}, u32[]{:S(2)}, u32[]{:S(2)}) collective-permute-start(f32[776,128]{1,0:T(8,128)S(1)} %get-tuple-element.72), channel_id=1, source_target_pairs={{0,4},{1,9},{2,6},{3,11},{4,0},{5,13},{6,2},{7,15},{8,12},{9,1},{1... | collective-permute-start | bytes 1191944 | tf_op jit(solution)/shard_map/ppermute | solution.py:300
  38.7 5.8 %collective-permute-start.3 = (f32[384,128]{1,0:T(8,128)S(1)}, f32[384,128]{1,0:T(8,128)S(1)}, u32[]{:S(2)}, u32[]{:S(2)}) collective-permute-start(f32[384,128]{1,0:T(8,128)S(1)} %slice_add_fusion.24.refs_3_), channel_id=1, source_target_pairs={{0,8},{1,5},{2,10},{3,7},{4,12},{5,1},{6,14},{7,3},{8,0},{9,13},{1... | collective-permute-start | bytes 589832 | tf_op jit(solution)/shard_map/ppermute | solution.py:300
  43.2 10.0 %collective-permute-start.20 = (f32[392,128]{1,0:T(8,128)S(1)}, f32[392,128]{1,0:T(8,128)S(1)}, u32[]{:S(2)}, u32[]{:S(2)}) collective-permute-start(f32[392,128]{1,0:T(8,128)S(1)} %pad_maximum_fusion.16), channel_id=1, source_target_pairs={{0,8},{1,5},{2,10},{3,7},{4,12},{5,1},{6,14},{7,3},{8,0},{9,13},{1... | collective-permute-start | bytes 602120 | tf_op jit(solution)/shard_map/ppermute | solution.py:300
  44.5 8.9 %collective-permute-start.4 = (f32[768,128]{1,0:T(8,128)S(1)}, f32[768,128]{1,0:T(8,128)S(1)}, u32[]{:S(2)}, u32[]{:S(2)}) collective-permute-start(f32[768,128]{1,0:T(8,128)S(1)} %pad_maximum_fusion), channel_id=1, source_target_pairs={{0,4},{1,9},{2,6},{3,11},{4,0},{5,13},{6,2},{7,15},{8,12},{9,1},{1... | collective-permute-start | bytes 1179656 | tf_op jit(solution)/shard_map/ppermute | solution.py:300
  53.3 7.8 %collective-permute-start.21 = (f32[392,128]{1,0:T(8,128)S(1)}, f32[392,128]{1,0:T(8,128)S(1)}, u32[]{:S(2)}, u32[]{:S(2)}) collective-permute-start(f32[392,128]{1,0:T(8,128)S(1)} %pad_maximum_fusion.17), channel_id=1, source_target_pairs={{0,16},{1,17},{2,18},{3,19},{4,20},{5,21},{6,22},{7,23},{8,24},{9,... | collective-permute-start | bytes 602120 | tf_op jit(solution)/shard_map/ppermute | solution.py:300
  56.9 4.3 %collective-permute-start.5 = (f32[520,128]{1,0:T(8,128)S(1)}, f32[520,128]{1,0:T(8,128)S(1)}, u32[]{:S(2)}, u32[]{:S(2)}) collective-permute-start(f32[520,128]{1,0:T(8,128)S(1)} %get-tuple-element.60), channel_id=1, source_target_pairs={{0,1},{1,0},{2,3},{3,2},{4,5},{5,4},{6,7},{7,6},{8,9},{9,8},{10,11... | collective-permute-start | bytes 798728 | tf_op jit(solution)/shard_map/ppermute | solution.py:303
  61.1 7.3 %collective-permute-start.22 = (f32[384,128]{1,0:T(8,128)S(1)}, f32[384,128]{1,0:T(8,128)S(1)}, u32[]{:S(2)}, u32[]{:S(2)}) collective-permute-start(f32[384,128]{1,0:T(8,128)S(1)} %slice_add_fusion.19.refs_3_), channel_id=1, source_target_pairs={{0,8},{1,5},{2,10},{3,7},{4,12},{5,1},{6,14},{7,3},{8,0},{9,13},{1... | collective-permute-start | bytes 589832 | tf_op jit(solution)/shard_map/ppermute | solution.py:300
  61.3 8.8 %collective-permute-start.6 = (f32[520,128]{1,0:T(8,128)S(1)}, f32[520,128]{1,0:T(8,128)S(1)}, u32[]{:S(2)}, u32[]{:S(2)}) collective-permute-start(f32[520,128]{1,0:T(8,128)S(1)} %pad_maximum_fusion.6), channel_id=1, source_target_pairs={{0,2},{1,3},{2,0},{3,1},{4,6},{5,7},{6,4},{7,5},{8,10},{9,11},{10,... | collective-permute-start | bytes 798728 | tf_op jit(solution)/shard_map/ppermute | solution.py:303
  68.5 7.8 %collective-permute-start.23 = (f32[768,128]{1,0:T(8,128)S(1)}, f32[768,128]{1,0:T(8,128)S(1)}, u32[]{:S(2)}, u32[]{:S(2)}) collective-permute-start(f32[768,128]{1,0:T(8,128)S(1)} %pad_maximum_fusion.2), channel_id=1, source_target_pairs={{0,4},{1,9},{2,6},{3,11},{4,0},{5,13},{6,2},{7,15},{8,12},{9,1},{1... | collective-permute-start | bytes 1179656 | tf_op jit(solution)/shard_map/ppermute | solution.py:300
  70.2 9.8 %collective-permute-start.7 = (f32[512,128]{1,0:T(8,128)S(1)}, f32[512,128]{1,0:T(8,128)S(1)}, u32[]{:S(2)}, u32[]{:S(2)}) collective-permute-start(f32[512,128]{1,0:T(8,128)S(1)} %slice_add_fusion.12.refs_2_), channel_id=1, source_target_pairs={{0,1},{1,0},{2,3},{3,2},{4,5},{5,4},{6,7},{7,6},{8,9},{9,8},{10,11... | collective-permute-start | bytes 786440 | tf_op jit(solution)/shard_map/ppermute | solution.py:303
  79.8 4.4 %collective-permute-start.24 = (f32[520,128]{1,0:T(8,128)S(1)}, f32[520,128]{1,0:T(8,128)S(1)}, u32[]{:S(2)}, u32[]{:S(2)}) collective-permute-start(f32[520,128]{1,0:T(8,128)S(1)} %get-tuple-element.80), channel_id=1, source_target_pairs={{0,1},{1,0},{2,3},{3,2},{4,5},{5,4},{6,7},{7,6},{8,9},{9,8},{10,11... | collective-permute-start | bytes 798728 | tf_op jit(solution)/shard_map/ppermute | solution.py:303
  82.6 7.9 %collective-permute-start.8 = (f32[776,128]{1,0:T(8,128)S(1)}, f32[776,128]{1,0:T(8,128)S(1)}, u32[]{:S(2)}, u32[]{:S(2)}) collective-permute-start(f32[776,128]{1,0:T(8,128)S(1)} %get-tuple-element.62), channel_id=1, source_target_pairs={{0,4},{1,9},{2,6},{3,11},{4,0},{5,13},{6,2},{7,15},{8,12},{9,1},{1... | collective-permute-start | bytes 1191944 | tf_op jit(solution)/shard_map/ppermute | solution.py:300
  84.3 9.2 %collective-permute-start.25 = (f32[520,128]{1,0:T(8,128)S(1)}, f32[520,128]{1,0:T(8,128)S(1)}, u32[]{:S(2)}, u32[]{:S(2)}) collective-permute-start(f32[520,128]{1,0:T(8,128)S(1)} %pad_maximum_fusion.8), channel_id=1, source_target_pairs={{0,2},{1,3},{2,0},{3,1},{4,6},{5,7},{6,4},{7,5},{8,10},{9,11},{10,... | collective-permute-start | bytes 798728 | tf_op jit(solution)/shard_map/ppermute | solution.py:303
  90.6 5.8 %collective-permute-start.9 = (f32[392,128]{1,0:T(8,128)S(1)}, f32[392,128]{1,0:T(8,128)S(1)}, u32[]{:S(2)}, u32[]{:S(2)}) collective-permute-start(f32[392,128]{1,0:T(8,128)S(1)} %pad_maximum_fusion.12), channel_id=1, source_target_pairs={{0,8},{1,5},{2,10},{3,7},{4,12},{5,1},{6,14},{7,3},{8,0},{9,13},{1... | collective-permute-start | bytes 602120 | tf_op jit(solution)/shard_map/ppermute | solution.py:300
  93.5 3.0 %collective-permute-start.26 = (f32[512,128]{1,0:T(8,128)S(1)}, f32[512,128]{1,0:T(8,128)S(1)}, u32[]{:S(2)}, u32[]{:S(2)}) collective-permute-start(f32[512,128]{1,0:T(8,128)S(1)} %slice_add_fusion.8.refs_2_), channel_id=1, source_target_pairs={{0,1},{1,0},{2,3},{3,2},{4,5},{5,4},{6,7},{7,6},{8,9},{9,8},{10,11... | collective-permute-start | bytes 786440 | tf_op jit(solution)/shard_map/ppermute | solution.py:303
  96.5 10.8 %collective-permute-start.10 = (f32[392,128]{1,0:T(8,128)S(1)}, f32[392,128]{1,0:T(8,128)S(1)}, u32[]{:S(2)}, u32[]{:S(2)}) collective-permute-start(f32[392,128]{1,0:T(8,128)S(1)} %pad_maximum_fusion.13), channel_id=1, source_target_pairs={{0,16},{1,17},{2,18},{3,19},{4,20},{5,21},{6,22},{7,23},{8,24},{9,... | collective-permute-start | bytes 602120 | tf_op jit(solution)/shard_map/ppermute | solution.py:300
  99.1 8.2 %collective-permute-start.27 = (f32[776,128]{1,0:T(8,128)S(1)}, f32[776,128]{1,0:T(8,128)S(1)}, u32[]{:S(2)}, u32[]{:S(2)}) collective-permute-start(f32[776,128]{1,0:T(8,128)S(1)} %get-tuple-element.85), channel_id=1, source_target_pairs={{0,4},{1,9},{2,6},{3,11},{4,0},{5,13},{6,2},{7,15},{8,12},{9,1},{1... | collective-permute-start | bytes 1191944 | tf_op jit(solution)/shard_map/ppermute | solution.py:300
  107.3 5.7 %collective-permute-start.11 = (f32[384,128]{1,0:T(8,128)S(1)}, f32[384,128]{1,0:T(8,128)S(1)}, u32[]{:S(2)}, u32[]{:S(2)}) collective-permute-start(f32[384,128]{1,0:T(8,128)S(1)} %slice_add_fusion.22.refs_3_), channel_id=1, source_target_pairs={{0,8},{1,5},{2,10},{3,7},{4,12},{5,1},{6,14},{7,3},{8,0},{9,13},{1... | collective-permute-start | bytes 589832 | tf_op jit(solution)/shard_map/ppermute | solution.py:300
  107.5 8.0 %collective-permute-start.28 = (f32[392,128]{1,0:T(8,128)S(1)}, f32[392,128]{1,0:T(8,128)S(1)}, u32[]{:S(2)}, u32[]{:S(2)}) collective-permute-start(f32[392,128]{1,0:T(8,128)S(1)} %pad_maximum_fusion.18), channel_id=1, source_target_pairs={{0,8},{1,5},{2,10},{3,7},{4,12},{5,1},{6,14},{7,3},{8,0},{9,13},{1... | collective-permute-start | bytes 602120 | tf_op jit(solution)/shard_map/ppermute | solution.py:300
  113.0 7.8 %collective-permute-start.12 = (f32[768,128]{1,0:T(8,128)S(1)}, f32[768,128]{1,0:T(8,128)S(1)}, u32[]{:S(2)}, u32[]{:S(2)}) collective-permute-start(f32[768,128]{1,0:T(8,128)S(1)} %pad_maximum_fusion.1), channel_id=1, source_target_pairs={{0,4},{1,9},{2,6},{3,11},{4,0},{5,13},{6,2},{7,15},{8,12},{9,1},{1... | collective-permute-start | bytes 1179656 | tf_op jit(solution)/shard_map/ppermute | solution.py:300
  115.5 11.0 %collective-permute-start.29 = (f32[392,128]{1,0:T(8,128)S(1)}, f32[392,128]{1,0:T(8,128)S(1)}, u32[]{:S(2)}, u32[]{:S(2)}) collective-permute-start(f32[392,128]{1,0:T(8,128)S(1)} %pad_maximum_fusion.19), channel_id=1, source_target_pairs={{0,16},{1,17},{2,18},{3,19},{4,20},{5,21},{6,22},{7,23},{8,24},{9,... | collective-permute-start | bytes 602120 | tf_op jit(solution)/shard_map/ppermute | solution.py:300
  124.4 7.9 %collective-permute-start.13 = (f32[520,128]{1,0:T(8,128)S(1)}, f32[520,128]{1,0:T(8,128)S(1)}, u32[]{:S(2)}, u32[]{:S(2)}) collective-permute-start(f32[520,128]{1,0:T(8,128)S(1)} %get-tuple-element.64), channel_id=1, source_target_pairs={{0,1},{1,0},{2,3},{3,2},{4,5},{5,4},{6,7},{7,6},{8,9},{9,8},{10,11... | collective-permute-start | bytes 798728 | tf_op jit(solution)/shard_map/ppermute | solution.py:303
  126.5 5.7 %collective-permute-start.30 = (f32[384,128]{1,0:T(8,128)S(1)}, f32[384,128]{1,0:T(8,128)S(1)}, u32[]{:S(2)}, u32[]{:S(2)}) collective-permute-start(f32[384,128]{1,0:T(8,128)S(1)} %slice_add_fusion.17.refs_3_), channel_id=1, source_target_pairs={{0,8},{1,5},{2,10},{3,7},{4,12},{5,1},{6,14},{7,3},{8,0},{9,13},{1... | collective-permute-start | bytes 589832 | tf_op jit(solution)/shard_map/ppermute | solution.py:300
  132.3 7.8 %collective-permute-start.31 = (f32[768,128]{1,0:T(8,128)S(1)}, f32[768,128]{1,0:T(8,128)S(1)}, u32[]{:S(2)}, u32[]{:S(2)}) collective-permute-start(f32[768,128]{1,0:T(8,128)S(1)} %pad_maximum_fusion.3), channel_id=1, source_target_pairs={{0,4},{1,9},{2,6},{3,11},{4,0},{5,13},{6,2},{7,15},{8,12},{9,1},{1... | collective-permute-start | bytes 1179656 | tf_op jit(solution)/shard_map/ppermute | solution.py:300
  134.0 9.7 %collective-permute-start.14 = (f32[520,128]{1,0:T(8,128)S(1)}, f32[520,128]{1,0:T(8,128)S(1)}, u32[]{:S(2)}, u32[]{:S(2)}) collective-permute-start(f32[520,128]{1,0:T(8,128)S(1)} %pad_maximum_fusion.7), channel_id=1, source_target_pairs={{0,2},{1,3},{2,0},{3,1},{4,6},{5,7},{6,4},{7,5},{8,10},{9,11},{10,... | collective-permute-start | bytes 798728 | tf_op jit(solution)/shard_map/ppermute | solution.py:303
  143.7 1.6 collective-permute-start.32
  143.8 1.9 collective-permute-start.15
  145.7 10.4 %collective-permute-start.33 = (f32[520,128]{1,0:T(8,128)S(1)}, f32[520,128]{1,0:T(8,128)S(1)}, u32[]{:S(2)}, u32[]{:S(2)}) collective-permute-start(f32[520,128]{1,0:T(8,128)S(1)} %pad_maximum_fusion.9), channel_id=1, source_target_pairs={{0,2},{1,3},{2,0},{3,1},{4,6},{5,7},{6,4},{7,5},{8,10},{9,11},{10,... | collective-permute-start | bytes 798728 | tf_op jit(solution)/shard_map/ppermute | solution.py:303
  151.8 7.9 %collective-permute-start.16 = (f32[776,128]{1,0:T(8,128)S(1)}, f32[776,128]{1,0:T(8,128)S(1)}, u32[]{:S(2)}, u32[]{:S(2)}) collective-permute-start(f32[776,128]{1,0:T(8,128)S(1)} %get-tuple-element.67), channel_id=1, source_target_pairs={{0,4},{1,9},{2,6},{3,11},{4,0},{5,13},{6,2},{7,15},{8,12},{9,1},{1... | collective-permute-start | bytes 1191944 | tf_op jit(solution)/shard_map/ppermute | solution.py:300
  159.8 1.6 collective-permute-start.34
  159.9 5.8 %collective-permute-start.17 = (f32[392,128]{1,0:T(8,128)S(1)}, f32[392,128]{1,0:T(8,128)S(1)}, u32[]{:S(2)}, u32[]{:S(2)}) collective-permute-start(f32[392,128]{1,0:T(8,128)S(1)} %pad_maximum_fusion.14), channel_id=1, source_target_pairs={{0,8},{1,5},{2,10},{3,7},{4,12},{5,1},{6,14},{7,3},{8,0},{9,13},{1... | collective-permute-start | bytes 602120 | tf_op jit(solution)/shard_map/ppermute | solution.py:300
  165.7 7.8 %collective-permute-start.35 = (f32[776,128]{1,0:T(8,128)S(1)}, f32[776,128]{1,0:T(8,128)S(1)}, u32[]{:S(2)}, u32[]{:S(2)}) collective-permute-start(f32[776,128]{1,0:T(8,128)S(1)} %get-tuple-element.98), channel_id=1, source_target_pairs={{0,4},{1,9},{2,6},{3,11},{4,0},{5,13},{6,2},{7,15},{8,12},{9,1},{1... | collective-permute-start | bytes 1191944 | tf_op jit(solution)/shard_map/ppermute | solution.py:300
  166.0 11.6 %collective-permute-start.18 = (f32[392,128]{1,0:T(8,128)S(1)}, f32[392,128]{1,0:T(8,128)S(1)}, u32[]{:S(2)}, u32[]{:S(2)}) collective-permute-start(f32[392,128]{1,0:T(8,128)S(1)} %pad_maximum_fusion.15), channel_id=1, source_target_pairs={{0,16},{1,17},{2,18},{3,19},{4,20},{5,21},{6,22},{7,23},{8,24},{9,... | collective-permute-start | bytes 602120 | tf_op jit(solution)/shard_map/ppermute | solution.py:300
  177.6 5.7 %collective-permute-start.36 = (f32[392,128]{1,0:T(8,128)S(1)}, f32[392,128]{1,0:T(8,128)S(1)}, u32[]{:S(2)}, u32[]{:S(2)}) collective-permute-start(f32[392,128]{1,0:T(8,128)S(1)} %pad_maximum_fusion.20), channel_id=1, source_target_pairs={{0,8},{1,5},{2,10},{3,7},{4,12},{5,1},{6,14},{7,3},{8,0},{9,13},{1... | collective-permute-start | bytes 602120 | tf_op jit(solution)/shard_map/ppermute | solution.py:300
  177.6 7.8 %collective-permute-start.37 = (f32[384,128]{1,0:T(8,128)S(1)}, f32[384,128]{1,0:T(8,128)S(1)}, u32[]{:S(2)}, u32[]{:S(2)}) collective-permute-start(f32[384,128]{1,0:T(8,128)S(1)} %slice_add_fusion.15.refs_2_), channel_id=1, source_target_pairs={{0,8},{1,5},{2,10},{3,7},{4,12},{5,1},{6,14},{7,3},{8,0},{9,13},{1... | collective-permute-start | bytes 589832 | tf_op jit(solution)/shard_map/ppermute | solution.py:300
  185.4 9.2 %collective-permute-start.38 = (f32[392,128]{1,0:T(8,128)S(1)}, f32[392,128]{1,0:T(8,128)S(1)}, u32[]{:S(2)}, u32[]{:S(2)}) collective-permute-start(f32[392,128]{1,0:T(8,128)S(1)} %pad_maximum_fusion.21), channel_id=1, source_target_pairs={{0,16},{1,17},{2,18},{3,19},{4,20},{5,21},{6,22},{7,23},{8,24},{9,... | collective-permute-start | bytes 602120 | tf_op jit(solution)/shard_map/ppermute | solution.py:300
  185.4 9.2 %collective-permute-start.39 = (f32[768,128]{1,0:T(8,128)S(1)}, f32[768,128]{1,0:T(8,128)S(1)}, u32[]{:S(2)}, u32[]{:S(2)}) collective-permute-start(f32[768,128]{1,0:T(8,128)S(1)} %pad_maximum_fusion.4), channel_id=1, source_target_pairs={{0,4},{1,9},{2,6},{3,11},{4,0},{5,13},{6,2},{7,15},{8,12},{9,1},{1... | collective-permute-start | bytes 1179656 | tf_op jit(solution)/shard_map/ppermute | solution.py:300
  194.6 5.7 %collective-permute-start.40 = (f32[384,128]{1,0:T(8,128)S(1)}, f32[384,128]{1,0:T(8,128)S(1)}, u32[]{:S(2)}, u32[]{:S(2)}) collective-permute-start(f32[384,128]{1,0:T(8,128)S(1)} %slice_add_fusion.14.refs_11_), channel_id=1, source_target_pairs={{0,8},{1,5},{2,10},{3,7},{4,12},{5,1},{6,14},{7,3},{8,0},{9,13},{1... | collective-permute-start | bytes 589832 | tf_op jit(solution)/shard_map/ppermute | solution.py:300
  200.4 7.8 %collective-permute-start.41 = (f32[768,128]{1,0:T(8,128)S(1)}, f32[768,128]{1,0:T(8,128)S(1)}, u32[]{:S(2)}, u32[]{:S(2)}) collective-permute-start(f32[768,128]{1,0:T(8,128)S(1)} %pad_maximum_fusion.5), channel_id=1, source_target_pairs={{0,4},{1,9},{2,6},{3,11},{4,0},{5,13},{6,2},{7,15},{8,12},{9,1},{1... | collective-permute-start | bytes 1179656 | tf_op jit(solution)/shard_map/ppermute | solution.py:300

commit v7 on v5

--- a/solution.py
+++ b/solution.py
@@ -13,7 +13,7 @@
 PAIR = 2 * TILE
 UNITS = 4
 NORM_ROWS = 8
-BUFFERS = 4
+BEHIND = 0
 
 tiny_eps = 1e-06
 
@@ -34,66 +34,77 @@
 
 
 def fill_kernel(
-    pattern_ref, count_ref, place_ref, flip_ref, delays_ref, tiles_ref,
-    dense_ref, *rest,
+    place_ref, flip_ref, pattern_in, counts_in, delays_in, tiles_in,
+    dense_ref, even_left_ref, odd_left_ref, pattern_ref, counts_ref, delays_ref, tiles_ref, arrived,
 ):
-    left_refs, (buffer_ref, arrived) = rest[:-2], rest[-2:]
-    row_blocks = tiles_ref.shape[0]
     flip = flip_ref[0]
-
-    def fetch(position, slot):
+    row_blocks = tiles_in.shape[0]
+    small = [
+        pltpu.make_async_copy(source, target, arrived.at[row_blocks + i])
+        for i, (source, target) in enumerate(
+            [(pattern_in, pattern_ref), (counts_in, counts_ref), (delays_in, delays_ref)]
+        )
+    ]
+    for copy in small:
+        copy.start()
+
+    def fetch(position):
         return pltpu.make_async_copy(
-            tiles_ref.at[position ^ flip], buffer_ref.at[slot], arrived.at[slot]
+            tiles_in.at[position ^ flip], tiles_ref.at[position], arrived.at[position]
         )
 
-    for position in range(BUFFERS):
-        fetch(position, position).start()
+    for position in range(row_blocks):
+        fetch(position).start()
+    for copy in small:
+        copy.wait()
 
     low = low_lanes((TILE, TILE))
     for pair in range(row_blocks // 2):
         source = (pair ^ (flip // 2)) * PAIR
         even = delays_ref[pl.ds(pl.multiple_of(source, TILE), TILE), :]
         odd = delays_ref[pl.ds(pl.multiple_of(source + TILE, TILE), TILE), :]
-        left_refs[0][rows_of(pair), :] = jnp.where(low, even, turned(odd))
-        left_refs[1][rows_of(pair), :] = jnp.where(low, turned(even), odd)
+        even_left_ref[rows_of(pair), :] = jnp.where(low, even, turned(odd))
+        odd_left_ref[rows_of(pair), :] = jnp.where(low, turned(even), odd)
 
     @pl.loop(0, row_blocks)
     def _(position):
-        slot = lax.rem(position, BUFFERS)
         rows = pl.ds(pl.multiple_of(position * TILE, TILE), TILE)
         dense_ref[rows, :] = jnp.zeros((TILE, dense_ref.shape[1]), dense_ref.dtype)
-        fetch(position, slot).wait()
+        fetch(position).wait()
         block = position ^ flip
 
-        @pl.loop(0, count_ref[block, 0])
+        @pl.loop(0, counts_ref[block])
         def _(tile):
             place = place_ref[pattern_ref[block, tile]]
             lanes = pl.ds(pl.multiple_of(place * TILE, TILE), TILE)
-            dense_ref[rows, lanes] = buffer_ref[slot, tile]
-
-        @pl.when(position + BUFFERS < row_blocks)
-        def _():
-            fetch(position + BUFFERS, slot).start()
+            dense_ref[rows, lanes] = tiles_ref[position, tile]
 
 
 def fill_dense(kernel, pattern, counts, places, flip, delays):
-    row_blocks, slot_count = kernel.shape[:2]
+    row_blocks = kernel.shape[0]
     rows = row_blocks * TILE
     left = jax.ShapeDtypeStruct((rows // 2, TILE), jnp.float32)
     return pl.pallas_call(
         fill_kernel,
-        in_specs=[SCALARS] * 4 + [WHOLE, pl.BlockSpec(memory_space=pl.ANY)],
+        in_specs=[SCALARS] * 2 + [pl.BlockSpec(memory_space=pltpu.HBM)] * 4,
         out_specs=[WHOLE] * 3,
         out_shape=[jax.ShapeDtypeStruct((rows, CB_DEV * TILE), kernel.dtype), left, left],
         scratch_shapes=[
-            pltpu.VMEM((BUFFERS, slot_count, TILE, TILE), kernel.dtype),
-            pltpu.SemaphoreType.DMA((BUFFERS,)),
+            pltpu.SMEM(pattern.shape, jnp.int32),
+            pltpu.SMEM((row_blocks,), jnp.int32),
+            pltpu.VMEM(delays.shape, delays.dtype),
+            pltpu.VMEM(kernel.shape, kernel.dtype),
+            pltpu.SemaphoreType.DMA((row_blocks + 3,)),
         ],
-        compiler_params=pltpu.CompilerParams(vmem_limit_bytes=46 * 1024 * 1024),
+        compiler_params=pltpu.CompilerParams(vmem_limit_bytes=16 * 1024 * 1024),
         cost_estimate=pl.CostEstimate(
             flops=0, bytes_accessed=2 * kernel.size, transcendentals=0
         ),
-    )(pattern, counts, places, flip, delays, kernel)
+    )(
+        places,
+        flip,
+        *(pltpu.with_memory_space_constraint(x, pltpu.HBM) for x in (pattern, counts.reshape(-1), delays, kernel)),
+    )
 
 
 def norm_of(ref):
@@ -337,53 +348,76 @@
 
     dense, *lefts = fill_dense(kernel, pattern, counts, places, flip, delays)
 
-    def swap_normed(value, norm, swap):
-        got = swap(jnp.concatenate([value, norm]))
-        return got[: value.shape[0]], norm + got[value.shape[0] :]
-
     def reduce_rows(send, keep):
         half = keep.shape[0]
-        got = swap_rows(send, 0)
+        got = yield swap_rows, send, 0
         keep = keep + got[:half]
         norm = send[half:] + got[half:]
         send, mine = keep[: half // 2], keep[half // 2 :]
         for level in range(1, len(row_bits)):
-            got, norm = swap_normed(send, norm, lambda value: swap_rows(value, level))
-            mine = mine + got
-            send = mine
-        inner = swap_rows(mine, 1)
-        outer = swap_rows(jnp.concatenate([inner, mine]), 0)
+            got = yield swap_rows, jnp.concatenate([send, norm]), level
+            norm = norm + got[half // 2 :]
+            send = mine = mine + got[: half // 2]
+        inner = yield swap_rows, mine, 1
+        outer = yield swap_rows, jnp.concatenate([inner, mine]), 0
         return [outer, inner, mine], norm
 
     def reduce_cols(send, keep):
         half = keep.shape[0]
-        got = swap_cols(send, 0)
+        got = yield swap_cols, send, 0
         own = keep + got[:half]
         norm = send[half:] + got[half:]
         for bit in col_bits[1:]:
-            got, norm = swap_normed(own, norm, lambda value: swap_cols(value, bit))
-            own = own + got
-        return [swap_cols(own, 0), own], norm
+            got = yield swap_cols, jnp.concatenate([own, norm]), bit
+            norm = norm + got[half:]
+            own = own + got[:half]
+        other = yield swap_cols, own, 0
+        return [other, own], norm
 
     def chain(left):
         send, keep = back_product(dense, [left], True)
-        totals, norm = reduce_rows(send, keep)
+        totals, norm = yield from reduce_rows(send, keep)
         norms = [norm]
         rights = []
         for iteration in range(ITERS):
             past = [rights[-1], norms[-2]] if rights else []
             send, keep, right = fore_product(dense, [*totals, norms[-1], *past], not rights)
             rights.append(right)
-            halves, norm = reduce_cols(send, keep)
+            halves, norm = yield from reduce_cols(send, keep)
             norms.append(norm)
             send, keep, left = back_product(
                 dense, [*halves, norms[-1], left, norms[-2]], False
             )
-            totals, norm = reduce_rows(send, keep)
+            totals, norm = yield from reduce_rows(send, keep)
             norms.append(norm)
         return rights, norms, totals
 
-    chains = [chain(left) for left in lefts]
+    def tied(value, other):
+        return lax.optimization_barrier((value, other))[0]
+
+    runs = [chain(left) for left in lefts]
+    wanted = [next(run) for run in runs]
+    chains = [None] * len(runs)
+    gots = [None] * len(runs)
+    swap, latest, level = wanted[0]
+    gots[0] = swap(latest, level)
+    turn = 0
+    while None in chains:
+        mine = 0 if turn < BEHIND else (turn - BEHIND) % 2
+        turn += 1
+        if chains[mine] is not None:
+            continue
+        if gots[mine] is None:
+            swap, value, level = wanted[mine]
+            latest = tied(value, latest)
+        else:
+            try:
+                swap, latest, level = runs[mine].send(tied(gots[mine], latest))
+            except StopIteration as stop:
+                chains[mine] = stop.value
+                continue
+        gots[mine] = swap(latest, level)
+
     cells = dense.shape[1]
     model, misfit = last_call(
         functools.partial(model_kernel, ITERS),

time: 220 us -> 195 us (0.89)
  waiting for transfers between devices: 121 us -> 98.7 us
  starting transfers between devices: 43.8 us -> 56.5 us
  local copies, waits for them, and re-layouts: 7.83 us -> 0.6 us
  Pallas kernels: 44.2 us -> 37.5 us
    ppermute x12, waiting for transfers between devices: 22.6 us -> 7.24 us  [swap_cols(): lax.ppermute(value, 'cols', [(i, i ^ 1 << level) for i in range(col_count)])]
    ppermute x30, starting transfers between devices: 37.1 us -> 50 us  [swap_rows(): return lax.ppermute(value, ('rows', 'cols'), pairs)]
    unnamed x13 -> x0, local copies, waits for them, and re-layouts: 7.23 us -> none
    ppermute x30, waiting for transfers between devices: 98.5 us -> 91.5 us  [swap_rows(): return lax.ppermute(value, ('rows', 'cols'), pairs)]
    pallas_call x1, Pallas kernels: 11.2 us -> 4.48 us  [fill_dense(): pl.pallas_call(fill_kernel, in_specs=[SCALARS] * 2 + [pl.BlockSpec(memory...]
  transfers between devices with their start and end apart: 42 -> 42, of which waited for: 30 -> 30; matrix products, arithmetic and copies ran while one was open for 1% -> 1% of each run, Pallas kernels for 13% -> 15%
where the time goes in v7:
time: 195 us; the launch traced here: 196 us
  waiting for transfers between devices  98.7 us (51%)
  starting transfers between devices  56.5 us (29%)
  Pallas kernels  37.5 us (19%)
    ppermute x30, waiting for transfers between devices, swap_rows(): return lax.ppermute(value, ('rows', 'cols'), pairs)  91.5 us
    ppermute x30, starting transfers between devices, swap_rows(): return lax.ppermute(value, ('rows', 'cols'), pairs)  50 us
    pallas_call x10, Pallas kernels, product_call(): pl.pallas_call(body, in_specs=[WHOLE] * (1 + len(operands)), out_specs=[W...  29.6 us
    ppermute x12, waiting for transfers between devices, swap_cols(): lax.ppermute(value, 'cols', [(i, i ^ 1 << level) for i in range(col_count)])  7.24 us
    ppermute x12, starting transfers between devices, swap_cols(): lax.ppermute(value, 'cols', [(i, i ^ 1 << level) for i in range(col_count)])  6.48 us
    pallas_call x1, Pallas kernels, fill_dense(): pl.pallas_call(fill_kernel, in_specs=[SCALARS] * 2 + [pl.BlockSpec(memory...  4.48 us
  transfers between devices with their start and end apart: 42, of which 30 were waited for; matrix products, arithmetic and copies ran while one was open for 1% of the time, Pallas kernels for 15%

profile of v7, /device:TPU:0, one launch (start us, length us, event | category | flops | bytes accessed | tf_op | source)
XLA Modules:
  0.0 196.1 jit_solution(5579640382260877340)
XLA Ops:
  0.7 4.5 %shard_map.67 = (bf16[2048,3072]{1,0:T(8,128)(2,1)S(1)}, f32[1024,128]{1,0:T(8,128)S(1)}, f32[1024,128]{1,0:T(8,128)S(1)}) custom-call(s32[24]{0:T(128)S(1)} %fusion.place_ref, s32[1]{0:T(128)} %bitcast.1.flip_ref, s32[16,16]{1,0:T(8,128)} %pattern_in.1, s32[16]{0:T(128)} %bitcast.5, f32[2048,128]{1,0:T(8,128)} %delays_in.1, bf16[16,16,128,128]{3,2,1,0:T(8,128)(2,1)} %tiles_in.1), custom_call_target="tpu_custom_call" | custom-call | bytes 8388608 | tf_op jit(solution)/shard_map/pallas_call | solution.py:87
  5.2 2.5 %shard_map.68 = (f32[776,128]{1,0:T(8,128)S(1)}, f32[768,128]{1,0:T(8,128)S(1)}) custom-call(bf16[2048,3072]{1,0:T(8,128)(2,1)S(1)} %get-tuple-element.77.refs_0_, f32[1024,128]{1,0:T(8,128)S(1)} %get-tuple-element.78.refs_1_.refs_4_), custom_call_target="tpu_custom_call" | custom-call | flops 3221225472 | bytes 12582912 | tf_op jit(solution)/shard_map/pallas_call | solution.py:214
  7.7 3.9 %collective-permute-start = (f32[776,128]{1,0:T(8,128)S(1)}, f32[776,128]{1,0:T(8,128)S(1)}, u32[]{:S(2)}, u32[]{:S(2)}) collective-permute-start(f32[776,128]{1,0:T(8,128)S(1)} %get-tuple-element.80), channel_id=1, source_target_pairs={{0,4},{1,9},{2,6},{3,11},{4,0},{5,13},{6,2},{7,15},{8,12},{9,1},{1... | collective-permute-start | bytes 1191944 | tf_op jit(solution)/shard_map/ppermute | solution.py:334
  11.5 5.8 %collective-permute-done = f32[776,128]{1,0:T(8,128)S(1)} collective-permute-done((f32[776,128]{1,0:T(8,128)S(1)}, f32[776,128]{1,0:T(8,128)S(1)}, u32[]{:S(2)}, u32[]{:S(2)}) %collective-permute-start) | collective-permute-done | bytes 397344 | tf_op jit(solution)/shard_map/ppermute | solution.py:334
  17.4 2.1 %collective-permute-start.1 = (f32[392,128]{1,0:T(8,128)S(1)}, f32[392,128]{1,0:T(8,128)S(1)}, u32[]{:S(2)}, u32[]{:S(2)}) collective-permute-start(f32[392,128]{1,0:T(8,128)S(1)} %pad_maximum_fusion.10), channel_id=1, source_target_pairs={{0,8},{1,5},{2,10},{3,7},{4,12},{5,1},{6,14},{7,3},{8,0},{9,13},{1... | collective-permute-start | bytes 602120 | tf_op jit(solution)/shard_map/ppermute | solution.py:334
  19.6 2.5 %shard_map.69 = (f32[776,128]{1,0:T(8,128)S(1)}, f32[768,128]{1,0:T(8,128)S(1)}) custom-call(bf16[2048,3072]{1,0:T(8,128)(2,1)S(1)} %get-tuple-element.77.refs_0_, f32[1024,128]{1,0:T(8,128)S(1)} %get-tuple-element.82.refs_1_.refs_4_), custom_call_target="tpu_custom_call" | custom-call | flops 3221225472 | bytes 12582912 | tf_op jit(solution)/shard_map/pallas_call | solution.py:214
  23.9 3.2 %collective-permute-start.2 = (f32[392,128]{1,0:T(8,128)S(1)}, f32[392,128]{1,0:T(8,128)S(1)}, u32[]{:S(2)}, u32[]{:S(2)}) collective-permute-start(f32[392,128]{1,0:T(8,128)S(1)} %pad_maximum_fusion.11), channel_id=1, source_target_pairs={{0,16},{1,17},{2,18},{3,19},{4,20},{5,21},{6,22},{7,23},{8,24},{9,... | collective-permute-start | bytes 602120 | tf_op jit(solution)/shard_map/ppermute | solution.py:334
  27.1 2.9 %collective-permute-done.3 = f32[776,128]{1,0:T(8,128)S(1)} collective-permute-done((f32[776,128]{1,0:T(8,128)S(1)}, f32[776,128]{1,0:T(8,128)S(1)}, u32[]{:S(2)}, u32[]{:S(2)}) %collective-permute-start.3) | collective-permute-done | bytes 397344 | tf_op jit(solution)/shard_map/ppermute | solution.py:334
  30.1 5.1 %collective-permute-done.2 = f32[392,128]{1,0:T(8,128)S(1)} collective-permute-done((f32[392,128]{1,0:T(8,128)S(1)}, f32[392,128]{1,0:T(8,128)S(1)}, u32[]{:S(2)}, u32[]{:S(2)}) %collective-permute-start.2) | collective-permute-done | bytes 200736 | tf_op jit(solution)/shard_map/ppermute | solution.py:334
  36.7 2.4 %collective-permute-start.7 = (f32[392,128]{1,0:T(8,128)S(1)}, f32[392,128]{1,0:T(8,128)S(1)}, u32[]{:S(2)}, u32[]{:S(2)}) collective-permute-start(f32[392,128]{1,0:T(8,128)S(1)} %pad_maximum_fusion.13), channel_id=1, source_target_pairs={{0,16},{1,17},{2,18},{3,19},{4,20},{5,21},{6,22},{7,23},{8,24},{9,... | collective-permute-start | bytes 602120 | tf_op jit(solution)/shard_map/ppermute | solution.py:334
  39.1 4.2 %collective-permute-done.4.refs_2_ = f32[384,128]{1,0:T(8,128)S(1)} collective-permute-done((f32[384,128]{1,0:T(8,128)S(1)}, f32[384,128]{1,0:T(8,128)S(1)}, u32[]{:S(2)}, u32[]{:S(2)}) %collective-permute-start.4) | collective-permute-done | bytes 196640 | tf_op jit(solution)/shard_map/ppermute | solution.py:334
  43.3 6.3 %collective-permute-start.6 = (f32[768,128]{1,0:T(8,128)S(1)}, f32[768,128]{1,0:T(8,128)S(1)}, u32[]{:S(2)}, u32[]{:S(2)}) collective-permute-start(f32[768,128]{1,0:T(8,128)S(1)} %pad_maximum_fusion), channel_id=1, source_target_pairs={{0,4},{1,9},{2,6},{3,11},{4,0},{5,13},{6,2},{7,15},{8,12},{9,1},{1... | collective-permute-start | bytes 1179656 | tf_op jit(solution)/shard_map/ppermute | solution.py:334
  49.8 5.7 %collective-permute-done.6.refs_1_ = f32[768,128]{1,0:T(8,128)S(1)} collective-permute-done((f32[768,128]{1,0:T(8,128)S(1)}, f32[768,128]{1,0:T(8,128)S(1)}, u32[]{:S(2)}, u32[]{:S(2)}) %collective-permute-start.6) | collective-permute-done | bytes 393248 | tf_op jit(solution)/shard_map/ppermute | solution.py:334
  55.4 3.5 %shard_map.70 = (f32[520,128]{1,0:T(8,128)S(1)}, f32[512,128]{1,0:T(8,128)S(1)}, f32[1536,128]{1,0:T(8,128)S(1)}) custom-call(bf16[2048,3072]{1,0:T(8,128)(2,1)S(1)} %get-tuple-element.77.refs_0_, f32[768,128]{1,0:T(8,128)S(1)} %collective-permute-done.6.refs_1_, f32[384,128]{1,0:T(8,128)S(1)} %collective-permute-done.4.refs_2_, ...), custom_call_target="tpu_custom_call" | custom-call | flops 3221225472 | bytes 12582912 | tf_op jit(solution)/shard_map/pallas_call | solution.py:214
  59.1 2.1 %collective-permute-start.11 = (f32[768,128]{1,0:T(8,128)S(1)}, f32[768,128]{1,0:T(8,128)S(1)}, u32[]{:S(2)}, u32[]{:S(2)}) collective-permute-start(f32[768,128]{1,0:T(8,128)S(1)} %pad_maximum_fusion.1), channel_id=1, source_target_pairs={{0,4},{1,9},{2,6},{3,11},{4,0},{5,13},{6,2},{7,15},{8,12},{9,1},{1... | collective-permute-start | bytes 1179656 | tf_op jit(solution)/shard_map/ppermute | solution.py:334
  61.6 5.3 %collective-permute-done.11.refs_1_ = f32[768,128]{1,0:T(8,128)S(1)} collective-permute-done((f32[768,128]{1,0:T(8,128)S(1)}, f32[768,128]{1,0:T(8,128)S(1)}, u32[]{:S(2)}, u32[]{:S(2)}) %collective-permute-start.11) | collective-permute-done | bytes 393248 | tf_op jit(solution)/shard_map/ppermute | solution.py:334
  66.9 3.5 %shard_map.71 = (f32[520,128]{1,0:T(8,128)S(1)}, f32[512,128]{1,0:T(8,128)S(1)}, f32[1536,128]{1,0:T(8,128)S(1)}) custom-call(bf16[2048,3072]{1,0:T(8,128)(2,1)S(1)} %get-tuple-element.77.refs_0_, f32[768,128]{1,0:T(8,128)S(1)} %collective-permute-done.11.refs_1_, f32[384,128]{1,0:T(8,128)S(1)} %collective-permute-done.9.refs_2_, ...), custom_call_target="tpu_custom_call" | custom-call | flops 3221225472 | bytes 12582912 | tf_op jit(solution)/shard_map/pallas_call | solution.py:214
  72.5 2.7 %shard_map.72 = (f32[776,128]{1,0:T(8,128)S(1)}, f32[768,128]{1,0:T(8,128)S(1)}, f32[1024,128]{1,0:T(8,128)S(1)}) custom-call(bf16[2048,3072]{1,0:T(8,128)(2,1)S(1)} %get-tuple-element.77.refs_0_, f32[512,128]{1,0:T(8,128)S(1)} %collective-permute-done.12.refs_1_, f32[512,128]{1,0:T(8,128)S(1)} %slice_add_fusion.12.refs_2_, ...), custom_call_target="tpu_custom_call" | custom-call | flops 3221225472 | bytes 12582912 | tf_op jit(solution)/shard_map/pallas_call | solution.py:214
  75.3 2.1 %collective-permute-start.14 = (f32[776,128]{1,0:T(8,128)S(1)}, f32[776,128]{1,0:T(8,128)S(1)}, u32[]{:S(2)}, u32[]{:S(2)}) collective-permute-start(f32[776,128]{1,0:T(8,128)S(1)} %get-tuple-element.105), channel_id=1, source_target_pairs={{0,4},{1,9},{2,6},{3,11},{4,0},{5,13},{6,2},{7,15},{8,12},{9,1},{1... | collective-permute-start | bytes 1191944 | tf_op jit(solution)/shard_map/ppermute | solution.py:334
  77.3 3.3 %collective-permute-done.15 = f32[520,128]{1,0:T(8,128)S(1)} collective-permute-done((f32[520,128]{1,0:T(8,128)S(1)}, f32[520,128]{1,0:T(8,128)S(1)}, u32[]{:S(2)}, u32[]{:S(2)}) %collective-permute-start.15) | collective-permute-done | bytes 266272 | tf_op jit(solution)/shard_map/ppermute | solution.py:337
  80.8 2.4 %collective-permute-done.14 = f32[776,128]{1,0:T(8,128)S(1)} collective-permute-done((f32[776,128]{1,0:T(8,128)S(1)}, f32[776,128]{1,0:T(8,128)S(1)}, u32[]{:S(2)}, u32[]{:S(2)}) %collective-permute-start.14) | collective-permute-done | bytes 397344 | tf_op jit(solution)/shard_map/ppermute | solution.py:334
  83.3 2.5 %shard_map.73 = (f32[776,128]{1,0:T(8,128)S(1)}, f32[768,128]{1,0:T(8,128)S(1)}, f32[1024,128]{1,0:T(8,128)S(1)}) custom-call(bf16[2048,3072]{1,0:T(8,128)(2,1)S(1)} %get-tuple-element.77.refs_0_, f32[512,128]{1,0:T(8,128)S(1)} %collective-permute-done.17.refs_1_, f32[512,128]{1,0:T(8,128)S(1)} %slice_add_fusion.10.refs_2_, ...), custom_call_target="tpu_custom_call" | custom-call | flops 3221225472 | bytes 12582912 | tf_op jit(solution)/shard_map/pallas_call | solution.py:214
  85.9 2.1 %collective-permute-start.19 = (f32[776,128]{1,0:T(8,128)S(1)}, f32[776,128]{1,0:T(8,128)S(1)}, u32[]{:S(2)}, u32[]{:S(2)}) collective-permute-start(f32[776,128]{1,0:T(8,128)S(1)} %get-tuple-element.109), channel_id=1, source_target_pairs={{0,4},{1,9},{2,6},{3,11},{4,0},{5,13},{6,2},{7,15},{8,12},{9,1},{1... | collective-permute-start | bytes 1191944 | tf_op jit(solution)/shard_map/ppermute | solution.py:334
  90.7 3.1 %collective-permute-done.19 = f32[776,128]{1,0:T(8,128)S(1)} collective-permute-done((f32[776,128]{1,0:T(8,128)S(1)}, f32[776,128]{1,0:T(8,128)S(1)}, u32[]{:S(2)}, u32[]{:S(2)}) %collective-permute-start.19) | collective-permute-done | bytes 397344 | tf_op jit(solution)/shard_map/ppermute | solution.py:334
  93.9 2.1 %collective-permute-start.21 = (f32[392,128]{1,0:T(8,128)S(1)}, f32[392,128]{1,0:T(8,128)S(1)}, u32[]{:S(2)}, u32[]{:S(2)}) collective-permute-start(f32[392,128]{1,0:T(8,128)S(1)} %pad_maximum_fusion.16), channel_id=1, source_target_pairs={{0,8},{1,5},{2,10},{3,7},{4,12},{5,1},{6,14},{7,3},{8,0},{9,13},{1... | collective-permute-start | bytes 602120 | tf_op jit(solution)/shard_map/ppermute | solution.py:334
  95.9 4.2 %collective-permute-done.18 = f32[392,128]{1,0:T(8,128)S(1)} collective-permute-done((f32[392,128]{1,0:T(8,128)S(1)}, f32[392,128]{1,0:T(8,128)S(1)}, u32[]{:S(2)}, u32[]{:S(2)}) %collective-permute-start.18) | collective-permute-done | bytes 200736 | tf_op jit(solution)/shard_map/ppermute | solution.py:334
  103.2 4.6 %collective-permute-done.20.refs_2_ = f32[384,128]{1,0:T(8,128)S(1)} collective-permute-done((f32[384,128]{1,0:T(8,128)S(1)}, f32[384,128]{1,0:T(8,128)S(1)}, u32[]{:S(2)}, u32[]{:S(2)}) %collective-permute-start.20) | collective-permute-done | bytes 196640 | tf_op jit(solution)/shard_map/ppermute | solution.py:334
  107.9 3.4 %collective-permute-start.22 = (f32[768,128]{1,0:T(8,128)S(1)}, f32[768,128]{1,0:T(8,128)S(1)}, u32[]{:S(2)}, u32[]{:S(2)}) collective-permute-start(f32[768,128]{1,0:T(8,128)S(1)} %pad_maximum_fusion.2), channel_id=1, source_target_pairs={{0,4},{1,9},{2,6},{3,11},{4,0},{5,13},{6,2},{7,15},{8,12},{9,1},{1... | collective-permute-start | bytes 1179656 | tf_op jit(solution)/shard_map/ppermute | solution.py:334
  113.3 5.4 %collective-permute-done.22.refs_1_ = f32[768,128]{1,0:T(8,128)S(1)} collective-permute-done((f32[768,128]{1,0:T(8,128)S(1)}, f32[768,128]{1,0:T(8,128)S(1)}, u32[]{:S(2)}, u32[]{:S(2)}) %collective-permute-start.22) | collective-permute-done | bytes 393248 | tf_op jit(solution)/shard_map/ppermute | solution.py:334
  118.7 3.5 %shard_map.74 = (f32[520,128]{1,0:T(8,128)S(1)}, f32[512,128]{1,0:T(8,128)S(1)}, f32[1536,128]{1,0:T(8,128)S(1)}) custom-call(bf16[2048,3072]{1,0:T(8,128)(2,1)S(1)} %get-tuple-element.77.refs_0_, f32[768,128]{1,0:T(8,128)S(1)} %collective-permute-done.22.refs_1_, f32[384,128]{1,0:T(8,128)S(1)} %collective-permute-done.20.refs_2_, ...), custom_call_target="tpu_custom_call" | custom-call | flops 3221225472 | bytes 12582912 | tf_op jit(solution)/shard_map/pallas_call | solution.py:214
  122.4 2.5 %collective-permute-start.27 = (f32[768,128]{1,0:T(8,128)S(1)}, f32[768,128]{1,0:T(8,128)S(1)}, u32[]{:S(2)}, u32[]{:S(2)}) collective-permute-start(f32[768,128]{1,0:T(8,128)S(1)} %pad_maximum_fusion.3), channel_id=1, source_target_pairs={{0,4},{1,9},{2,6},{3,11},{4,0},{5,13},{6,2},{7,15},{8,12},{9,1},{1... | collective-permute-start | bytes 1179656 | tf_op jit(solution)/shard_map/ppermute | solution.py:334
  125.0 2.1 %collective-permute-start.26 = (f32[520,128]{1,0:T(8,128)S(1)}, f32[520,128]{1,0:T(8,128)S(1)}, u32[]{:S(2)}, u32[]{:S(2)}) collective-permute-start(f32[520,128]{1,0:T(8,128)S(1)} %pad_maximum_fusion.8), channel_id=1, source_target_pairs={{0,2},{1,3},{2,0},{3,1},{4,6},{5,7},{6,4},{7,5},{8,10},{9,11},{10,... | collective-permute-start | bytes 798728 | tf_op jit(solution)/shard_map/ppermute | solution.py:337
  127.1 3.6 %collective-permute-done.27.refs_1_ = f32[768,128]{1,0:T(8,128)S(1)} collective-permute-done((f32[768,128]{1,0:T(8,128)S(1)}, f32[768,128]{1,0:T(8,128)S(1)}, u32[]{:S(2)}, u32[]{:S(2)}) %collective-permute-start.27) | collective-permute-done | bytes 393248 | tf_op jit(solution)/shard_map/ppermute | solution.py:334
  130.7 3.5 %shard_map.75 = (f32[520,128]{1,0:T(8,128)S(1)}, f32[512,128]{1,0:T(8,128)S(1)}, f32[1536,128]{1,0:T(8,128)S(1)}) custom-call(bf16[2048,3072]{1,0:T(8,128)(2,1)S(1)} %get-tuple-element.77.refs_0_, f32[768,128]{1,0:T(8,128)S(1)} %collective-permute-done.27.refs_1_, f32[384,128]{1,0:T(8,128)S(1)} %collective-permute-done.25.refs_2_, ...), custom_call_target="tpu_custom_call" | custom-call | flops 3221225472 | bytes 12582912 | tf_op jit(solution)/shard_map/pallas_call | solution.py:214
  135.9 2.1 %collective-permute-start.31 = (f32[520,128]{1,0:T(8,128)S(1)}, f32[520,128]{1,0:T(8,128)S(1)}, u32[]{:S(2)}, u32[]{:S(2)}) collective-permute-start(f32[520,128]{1,0:T(8,128)S(1)} %pad_maximum_fusion.9), channel_id=1, source_target_pairs={{0,2},{1,3},{2,0},{3,1},{4,6},{5,7},{6,4},{7,5},{8,10},{9,11},{10,... | collective-permute-start | bytes 798728 | tf_op jit(solution)/shard_map/ppermute | solution.py:337
  138.0 2.5 %shard_map.76 = (f32[776,128]{1,0:T(8,128)S(1)}, f32[768,128]{1,0:T(8,128)S(1)}, f32[1024,128]{1,0:T(8,128)}) custom-call(bf16[2048,3072]{1,0:T(8,128)(2,1)S(1)} %get-tuple-element.77.refs_0_, f32[512,128]{1,0:T(8,128)S(1)} %collective-permute-done.28.refs_1_, f32[512,128]{1,0:T(8,128)S(1)} %slice_add_fusion.8.refs_2_, ...), custom_call_target="tpu_custom_call" | custom-call | flops 3221225472 | bytes 12582912 | tf_op jit(solution)/shard_map/pallas_call | solution.py:214
  140.6 2.1 %collective-permute-start.30 = (f32[776,128]{1,0:T(8,128)S(1)}, f32[776,128]{1,0:T(8,128)S(1)}, u32[]{:S(2)}, u32[]{:S(2)}) collective-permute-start(f32[776,128]{1,0:T(8,128)S(1)} %get-tuple-element.131), channel_id=1, source_target_pairs={{0,4},{1,9},{2,6},{3,11},{4,0},{5,13},{6,2},{7,15},{8,12},{9,1},{1... | collective-permute-start | bytes 1191944 | tf_op jit(solution)/shard_map/ppermute | solution.py:334
  142.6 2.1 %collective-permute-done.31 = f32[520,128]{1,0:T(8,128)S(1)} collective-permute-done((f32[520,128]{1,0:T(8,128)S(1)}, f32[520,128]{1,0:T(8,128)S(1)}, u32[]{:S(2)}, u32[]{:S(2)}) %collective-permute-start.31) | collective-permute-done | bytes 266272 | tf_op jit(solution)/shard_map/ppermute | solution.py:337
  144.8 3.6 %collective-permute-done.30 = f32[776,128]{1,0:T(8,128)S(1)} collective-permute-done((f32[776,128]{1,0:T(8,128)S(1)}, f32[776,128]{1,0:T(8,128)S(1)}, u32[]{:S(2)}, u32[]{:S(2)}) %collective-permute-start.30) | collective-permute-done | bytes 397344 | tf_op jit(solution)/shard_map/ppermute | solution.py:334
  148.6 2.8 %shard_map.77 = (f32[776,128]{1,0:T(8,128)S(1)}, f32[768,128]{1,0:T(8,128)S(1)}, f32[1024,128]{1,0:T(8,128)}) custom-call(bf16[2048,3072]{1,0:T(8,128)(2,1)S(1)} %get-tuple-element.77.refs_0_, f32[512,128]{1,0:T(8,128)S(1)} %collective-permute-done.33.refs_1_, f32[512,128]{1,0:T(8,128)S(1)} %slice_add_fusion.6.refs_2_, ...), custom_call_target="tpu_custom_call" | custom-call | flops 3221225472 | bytes 12582912 | tf_op jit(solution)/shard_map/pallas_call | solution.py:214
  151.4 2.1 %collective-permute-start.35 = (f32[776,128]{1,0:T(8,128)S(1)}, f32[776,128]{1,0:T(8,128)S(1)}, u32[]{:S(2)}, u32[]{:S(2)}) collective-permute-start(f32[776,128]{1,0:T(8,128)S(1)} %get-tuple-element.137), channel_id=1, source_target_pairs={{0,4},{1,9},{2,6},{3,11},{4,0},{5,13},{6,2},{7,15},{8,12},{9,1},{1... | collective-permute-start | bytes 1191944 | tf_op jit(solution)/shard_map/ppermute | solution.py:334
  156.1 3.2 %collective-permute-done.35 = f32[776,128]{1,0:T(8,128)S(1)} collective-permute-done((f32[776,128]{1,0:T(8,128)S(1)}, f32[776,128]{1,0:T(8,128)S(1)}, u32[]{:S(2)}, u32[]{:S(2)}) %collective-permute-start.35) | collective-permute-done | bytes 397344 | tf_op jit(solution)/shard_map/ppermute | solution.py:334
  159.4 2.1 %collective-permute-start.36 = (f32[392,128]{1,0:T(8,128)S(1)}, f32[392,128]{1,0:T(8,128)S(1)}, u32[]{:S(2)}, u32[]{:S(2)}) collective-permute-start(f32[392,128]{1,0:T(8,128)S(1)} %pad_maximum_fusion.20), channel_id=1, source_target_pairs={{0,8},{1,5},{2,10},{3,7},{4,12},{5,1},{6,14},{7,3},{8,0},{9,13},{1... | collective-permute-start | bytes 602120 | tf_op jit(solution)/shard_map/ppermute | solution.py:334
  161.5 4.0 %collective-permute-done.34 = f32[392,128]{1,0:T(8,128)S(1)} collective-permute-done((f32[392,128]{1,0:T(8,128)S(1)}, f32[392,128]{1,0:T(8,128)S(1)}, u32[]{:S(2)}, u32[]{:S(2)}) %collective-permute-start.34) | collective-permute-done | bytes 200736 | tf_op jit(solution)/shard_map/ppermute | solution.py:334
  168.7 3.3 %collective-permute-done.38.refs_1_ = f32[384,128]{1,0:T(8,128)S(1)} collective-permute-done((f32[384,128]{1,0:T(8,128)S(1)}, f32[384,128]{1,0:T(8,128)S(1)}, u32[]{:S(2)}, u32[]{:S(2)}) %collective-permute-start.38) | collective-permute-done | bytes 196640 | tf_op jit(solution)/shard_map/ppermute | solution.py:334
  172.1 6.6 %collective-permute-done.37 = f32[392,128]{1,0:T(8,128)S(1)} collective-permute-done((f32[392,128]{1,0:T(8,128)S(1)}, f32[392,128]{1,0:T(8,128)S(1)}, u32[]{:S(2)}, u32[]{:S(2)}) %collective-permute-start.37) | collective-permute-done | bytes 200736 | tf_op jit(solution)/shard_map/ppermute | solution.py:334
  180.0 6.5 %collective-permute-done.40.refs_10_ = f32[384,128]{1,0:T(8,128)S(1)} collective-permute-done((f32[384,128]{1,0:T(8,128)S(1)}, f32[384,128]{1,0:T(8,128)S(1)}, u32[]{:S(2)}, u32[]{:S(2)}) %collective-permute-start.40) | collective-permute-done | bytes 196640 | tf_op jit(solution)/shard_map/ppermute | solution.py:334
  190.0 4.4 %collective-permute-done.41.refs_9_ = f32[768,128]{1,0:T(8,128)S(1)} collective-permute-done((f32[768,128]{1,0:T(8,128)S(1)}, f32[768,128]{1,0:T(8,128)S(1)}, u32[]{:S(2)}, u32[]{:S(2)}) %collective-permute-start.41) | collective-permute-done | bytes 393248 | tf_op jit(solution)/shard_map/ppermute | solution.py:334
  (131 shorter events, 28.9 us)
Async XLA Ops:
  7.7 9.7 %collective-permute-start = (f32[776,128]{1,0:T(8,128)S(1)}, f32[776,128]{1,0:T(8,128)S(1)}, u32[]{:S(2)}, u32[]{:S(2)}) collective-permute-start(f32[776,128]{1,0:T(8,128)S(1)} %get-tuple-element.80), channel_id=1, source_target_pairs={{0,4},{1,9},{2,6},{3,11},{4,0},{5,13},{6,2},{7,15},{8,12},{9,1},{1... | collective-permute-start | bytes 1191944 | tf_op jit(solution)/shard_map/ppermute | solution.py:334
  17.4 6.4 %collective-permute-start.1 = (f32[392,128]{1,0:T(8,128)S(1)}, f32[392,128]{1,0:T(8,128)S(1)}, u32[]{:S(2)}, u32[]{:S(2)}) collective-permute-start(f32[392,128]{1,0:T(8,128)S(1)} %pad_maximum_fusion.10), channel_id=1, source_target_pairs={{0,8},{1,5},{2,10},{3,7},{4,12},{5,1},{6,14},{7,3},{8,0},{9,13},{1... | collective-permute-start | bytes 602120 | tf_op jit(solution)/shard_map/ppermute | solution.py:334
  22.1 7.9 %collective-permute-start.3 = (f32[776,128]{1,0:T(8,128)S(1)}, f32[776,128]{1,0:T(8,128)S(1)}, u32[]{:S(2)}, u32[]{:S(2)}) collective-permute-start(f32[776,128]{1,0:T(8,128)S(1)} %get-tuple-element.84), channel_id=1, source_target_pairs={{0,4},{1,9},{2,6},{3,11},{4,0},{5,13},{6,2},{7,15},{8,12},{9,1},{1... | collective-permute-start | bytes 1191944 | tf_op jit(solution)/shard_map/ppermute | solution.py:334
  23.9 11.3 %collective-permute-start.2 = (f32[392,128]{1,0:T(8,128)S(1)}, f32[392,128]{1,0:T(8,128)S(1)}, u32[]{:S(2)}, u32[]{:S(2)}) collective-permute-start(f32[392,128]{1,0:T(8,128)S(1)} %pad_maximum_fusion.11), channel_id=1, source_target_pairs={{0,16},{1,17},{2,18},{3,19},{4,20},{5,21},{6,22},{7,23},{8,24},{9,... | collective-permute-start | bytes 602120 | tf_op jit(solution)/shard_map/ppermute | solution.py:334
  30.1 6.6 %collective-permute-start.5 = (f32[392,128]{1,0:T(8,128)S(1)}, f32[392,128]{1,0:T(8,128)S(1)}, u32[]{:S(2)}, u32[]{:S(2)}) collective-permute-start(f32[392,128]{1,0:T(8,128)S(1)} %pad_maximum_fusion.12), channel_id=1, source_target_pairs={{0,8},{1,5},{2,10},{3,7},{4,12},{5,1},{6,14},{7,3},{8,0},{9,13},{1... | collective-permute-start | bytes 602120 | tf_op jit(solution)/shard_map/ppermute | solution.py:334
  35.2 8.0 %collective-permute-start.4 = (f32[384,128]{1,0:T(8,128)S(1)}, f32[384,128]{1,0:T(8,128)S(1)}, u32[]{:S(2)}, u32[]{:S(2)}) collective-permute-start(f32[384,128]{1,0:T(8,128)S(1)} %slice_add_fusion.25.refs_3_), channel_id=1, source_target_pairs={{0,8},{1,5},{2,10},{3,7},{4,12},{5,1},{6,14},{7,3},{8,0},{9,13},{1... | collective-permute-start | bytes 589832 | tf_op jit(solution)/shard_map/ppermute | solution.py:334
  36.7 12.9 %collective-permute-start.7 = (f32[392,128]{1,0:T(8,128)S(1)}, f32[392,128]{1,0:T(8,128)S(1)}, u32[]{:S(2)}, u32[]{:S(2)}) collective-permute-start(f32[392,128]{1,0:T(8,128)S(1)} %pad_maximum_fusion.13), channel_id=1, source_target_pairs={{0,16},{1,17},{2,18},{3,19},{4,20},{5,21},{6,22},{7,23},{8,24},{9,... | collective-permute-start | bytes 602120 | tf_op jit(solution)/shard_map/ppermute | solution.py:334
  43.3 12.1 %collective-permute-start.6 = (f32[768,128]{1,0:T(8,128)S(1)}, f32[768,128]{1,0:T(8,128)S(1)}, u32[]{:S(2)}, u32[]{:S(2)}) collective-permute-start(f32[768,128]{1,0:T(8,128)S(1)} %pad_maximum_fusion), channel_id=1, source_target_pairs={{0,4},{1,9},{2,6},{3,11},{4,0},{5,13},{6,2},{7,15},{8,12},{9,1},{1... | collective-permute-start | bytes 1179656 | tf_op jit(solution)/shard_map/ppermute | solution.py:334
  49.7 9.4 %collective-permute-start.9 = (f32[384,128]{1,0:T(8,128)S(1)}, f32[384,128]{1,0:T(8,128)S(1)}, u32[]{:S(2)}, u32[]{:S(2)}) collective-permute-start(f32[384,128]{1,0:T(8,128)S(1)} %slice_add_fusion.24.refs_3_), channel_id=1, source_target_pairs={{0,8},{1,5},{2,10},{3,7},{4,12},{5,1},{6,14},{7,3},{8,0},{9,13},{1... | collective-permute-start | bytes 589832 | tf_op jit(solution)/shard_map/ppermute | solution.py:334
  59.0 2.2 %collective-permute-start.8 = (f32[520,128]{1,0:T(8,128)S(1)}, f32[520,128]{1,0:T(8,128)S(1)}, u32[]{:S(2)}, u32[]{:S(2)}) collective-permute-start(f32[520,128]{1,0:T(8,128)S(1)} %get-tuple-element.95), channel_id=1, source_target_pairs={{0,1},{1,0},{2,3},{3,2},{4,5},{5,4},{6,7},{7,6},{8,9},{9,8},{10,11... | collective-permute-start | bytes 798728 | tf_op jit(solution)/shard_map/ppermute | solution.py:337
  59.1 7.8 %collective-permute-start.11 = (f32[768,128]{1,0:T(8,128)S(1)}, f32[768,128]{1,0:T(8,128)S(1)}, u32[]{:S(2)}, u32[]{:S(2)}) collective-permute-start(f32[768,128]{1,0:T(8,128)S(1)} %pad_maximum_fusion.1), channel_id=1, source_target_pairs={{0,4},{1,9},{2,6},{3,11},{4,0},{5,13},{6,2},{7,15},{8,12},{9,1},{1... | collective-permute-start | bytes 1179656 | tf_op jit(solution)/shard_map/ppermute | solution.py:334
  61.2 9.3 %collective-permute-start.10 = (f32[520,128]{1,0:T(8,128)S(1)}, f32[520,128]{1,0:T(8,128)S(1)}, u32[]{:S(2)}, u32[]{:S(2)}) collective-permute-start(f32[520,128]{1,0:T(8,128)S(1)} %pad_maximum_fusion.6), channel_id=1, source_target_pairs={{0,2},{1,3},{2,0},{3,1},{4,6},{5,7},{6,4},{7,5},{8,10},{9,11},{10,... | collective-permute-start | bytes 798728 | tf_op jit(solution)/shard_map/ppermute | solution.py:337
  70.5 1.6 collective-permute-start.13
  70.6 1.9 collective-permute-start.12
  72.1 8.5 %collective-permute-start.15 = (f32[520,128]{1,0:T(8,128)S(1)}, f32[520,128]{1,0:T(8,128)S(1)}, u32[]{:S(2)}, u32[]{:S(2)}) collective-permute-start(f32[520,128]{1,0:T(8,128)S(1)} %pad_maximum_fusion.7), channel_id=1, source_target_pairs={{0,2},{1,3},{2,0},{3,1},{4,6},{5,7},{6,4},{7,5},{8,10},{9,11},{10,... | collective-permute-start | bytes 798728 | tf_op jit(solution)/shard_map/ppermute | solution.py:337
  75.3 7.9 %collective-permute-start.14 = (f32[776,128]{1,0:T(8,128)S(1)}, f32[776,128]{1,0:T(8,128)S(1)}, u32[]{:S(2)}, u32[]{:S(2)}) collective-permute-start(f32[776,128]{1,0:T(8,128)S(1)} %get-tuple-element.105), channel_id=1, source_target_pairs={{0,4},{1,9},{2,6},{3,11},{4,0},{5,13},{6,2},{7,15},{8,12},{9,1},{1... | collective-permute-start | bytes 1191944 | tf_op jit(solution)/shard_map/ppermute | solution.py:334
  80.7 2.6 %collective-permute-start.17 = (f32[512,128]{1,0:T(8,128)S(1)}, f32[512,128]{1,0:T(8,128)S(1)}, u32[]{:S(2)}, u32[]{:S(2)}) collective-permute-start(f32[512,128]{1,0:T(8,128)S(1)} %slice_add_fusion.10.refs_2_), channel_id=1, source_target_pairs={{0,1},{1,0},{2,3},{3,2},{4,5},{5,4},{6,7},{7,6},{8,9},{9,8},{10,11... | collective-permute-start | bytes 786440 | tf_op jit(solution)/shard_map/ppermute | solution.py:337
  83.3 5.8 %collective-permute-start.16 = (f32[392,128]{1,0:T(8,128)S(1)}, f32[392,128]{1,0:T(8,128)S(1)}, u32[]{:S(2)}, u32[]{:S(2)}) collective-permute-start(f32[392,128]{1,0:T(8,128)S(1)} %pad_maximum_fusion.14), channel_id=1, source_target_pairs={{0,8},{1,5},{2,10},{3,7},{4,12},{5,1},{6,14},{7,3},{8,0},{9,13},{1... | collective-permute-start | bytes 602120 | tf_op jit(solution)/shard_map/ppermute | solution.py:334
  85.9 7.9 %collective-permute-start.19 = (f32[776,128]{1,0:T(8,128)S(1)}, f32[776,128]{1,0:T(8,128)S(1)}, u32[]{:S(2)}, u32[]{:S(2)}) collective-permute-start(f32[776,128]{1,0:T(8,128)S(1)} %get-tuple-element.109), channel_id=1, source_target_pairs={{0,4},{1,9},{2,6},{3,11},{4,0},{5,13},{6,2},{7,15},{8,12},{9,1},{1... | collective-permute-start | bytes 1191944 | tf_op jit(solution)/shard_map/ppermute | solution.py:334
  89.1 11.1 %collective-permute-start.18 = (f32[392,128]{1,0:T(8,128)S(1)}, f32[392,128]{1,0:T(8,128)S(1)}, u32[]{:S(2)}, u32[]{:S(2)}) collective-permute-start(f32[392,128]{1,0:T(8,128)S(1)} %pad_maximum_fusion.15), channel_id=1, source_target_pairs={{0,16},{1,17},{2,18},{3,19},{4,20},{5,21},{6,22},{7,23},{8,24},{9,... | collective-permute-start | bytes 602120 | tf_op jit(solution)/shard_map/ppermute | solution.py:334
  93.9 7.7 %collective-permute-start.21 = (f32[392,128]{1,0:T(8,128)S(1)}, f32[392,128]{1,0:T(8,128)S(1)}, u32[]{:S(2)}, u32[]{:S(2)}) collective-permute-start(f32[392,128]{1,0:T(8,128)S(1)} %pad_maximum_fusion.16), channel_id=1, source_target_pairs={{0,8},{1,5},{2,10},{3,7},{4,12},{5,1},{6,14},{7,3},{8,0},{9,13},{1... | collective-permute-start | bytes 602120 | tf_op jit(solution)/shard_map/ppermute | solution.py:334
  100.2 7.7 %collective-permute-start.20 = (f32[384,128]{1,0:T(8,128)S(1)}, f32[384,128]{1,0:T(8,128)S(1)}, u32[]{:S(2)}, u32[]{:S(2)}) collective-permute-start(f32[384,128]{1,0:T(8,128)S(1)} %slice_add_fusion.23.refs_3_), channel_id=1, source_target_pairs={{0,8},{1,5},{2,10},{3,7},{4,12},{5,1},{6,14},{7,3},{8,0},{9,13},{1... | collective-permute-start | bytes 589832 | tf_op jit(solution)/shard_map/ppermute | solution.py:334
  101.6 11.6 %collective-permute-start.23 = (f32[392,128]{1,0:T(8,128)S(1)}, f32[392,128]{1,0:T(8,128)S(1)}, u32[]{:S(2)}, u32[]{:S(2)}) collective-permute-start(f32[392,128]{1,0:T(8,128)S(1)} %pad_maximum_fusion.17), channel_id=1, source_target_pairs={{0,16},{1,17},{2,18},{3,19},{4,20},{5,21},{6,22},{7,23},{8,24},{9,... | collective-permute-start | bytes 602120 | tf_op jit(solution)/shard_map/ppermute | solution.py:334
  107.9 10.8 %collective-permute-start.22 = (f32[768,128]{1,0:T(8,128)S(1)}, f32[768,128]{1,0:T(8,128)S(1)}, u32[]{:S(2)}, u32[]{:S(2)}) collective-permute-start(f32[768,128]{1,0:T(8,128)S(1)} %pad_maximum_fusion.2), channel_id=1, source_target_pairs={{0,4},{1,9},{2,6},{3,11},{4,0},{5,13},{6,2},{7,15},{8,12},{9,1},{1... | collective-permute-start | bytes 1179656 | tf_op jit(solution)/shard_map/ppermute | solution.py:334
  113.2 9.1 %collective-permute-start.25 = (f32[384,128]{1,0:T(8,128)S(1)}, f32[384,128]{1,0:T(8,128)S(1)}, u32[]{:S(2)}, u32[]{:S(2)}) collective-permute-start(f32[384,128]{1,0:T(8,128)S(1)} %slice_add_fusion.22.refs_3_), channel_id=1, source_target_pairs={{0,8},{1,5},{2,10},{3,7},{4,12},{5,1},{6,14},{7,3},{8,0},{9,13},{1... | collective-permute-start | bytes 589832 | tf_op jit(solution)/shard_map/ppermute | solution.py:334
  122.3 2.7 %collective-permute-start.24 = (f32[520,128]{1,0:T(8,128)S(1)}, f32[520,128]{1,0:T(8,128)S(1)}, u32[]{:S(2)}, u32[]{:S(2)}) collective-permute-start(f32[520,128]{1,0:T(8,128)S(1)} %get-tuple-element.119), channel_id=1, source_target_pairs={{0,1},{1,0},{2,3},{3,2},{4,5},{5,4},{6,7},{7,6},{8,9},{9,8},{10,11... | collective-permute-start | bytes 798728 | tf_op jit(solution)/shard_map/ppermute | solution.py:337
  122.4 8.3 %collective-permute-start.27 = (f32[768,128]{1,0:T(8,128)S(1)}, f32[768,128]{1,0:T(8,128)S(1)}, u32[]{:S(2)}, u32[]{:S(2)}) collective-permute-start(f32[768,128]{1,0:T(8,128)S(1)} %pad_maximum_fusion.3), channel_id=1, source_target_pairs={{0,4},{1,9},{2,6},{3,11},{4,0},{5,13},{6,2},{7,15},{8,12},{9,1},{1... | collective-permute-start | bytes 1179656 | tf_op jit(solution)/shard_map/ppermute | solution.py:334
  125.0 9.3 %collective-permute-start.26 = (f32[520,128]{1,0:T(8,128)S(1)}, f32[520,128]{1,0:T(8,128)S(1)}, u32[]{:S(2)}, u32[]{:S(2)}) collective-permute-start(f32[520,128]{1,0:T(8,128)S(1)} %pad_maximum_fusion.8), channel_id=1, source_target_pairs={{0,2},{1,3},{2,0},{3,1},{4,6},{5,7},{6,4},{7,5},{8,10},{9,11},{10,... | collective-permute-start | bytes 798728 | tf_op jit(solution)/shard_map/ppermute | solution.py:337
  134.2 1.6 collective-permute-start.29
  134.4 3.6 %collective-permute-start.28 = (f32[512,128]{1,0:T(8,128)S(1)}, f32[512,128]{1,0:T(8,128)S(1)}, u32[]{:S(2)}, u32[]{:S(2)}) collective-permute-start(f32[512,128]{1,0:T(8,128)S(1)} %slice_add_fusion.8.refs_2_), channel_id=1, source_target_pairs={{0,1},{1,0},{2,3},{3,2},{4,5},{5,4},{6,7},{7,6},{8,9},{9,8},{10,11... | collective-permute-start | bytes 786440 | tf_op jit(solution)/shard_map/ppermute | solution.py:337
  135.9 8.8 %collective-permute-start.31 = (f32[520,128]{1,0:T(8,128)S(1)}, f32[520,128]{1,0:T(8,128)S(1)}, u32[]{:S(2)}, u32[]{:S(2)}) collective-permute-start(f32[520,128]{1,0:T(8,128)S(1)} %pad_maximum_fusion.9), channel_id=1, source_target_pairs={{0,2},{1,3},{2,0},{3,1},{4,6},{5,7},{6,4},{7,5},{8,10},{9,11},{10,... | collective-permute-start | bytes 798728 | tf_op jit(solution)/shard_map/ppermute | solution.py:337
  140.6 7.9 %collective-permute-start.30 = (f32[776,128]{1,0:T(8,128)S(1)}, f32[776,128]{1,0:T(8,128)S(1)}, u32[]{:S(2)}, u32[]{:S(2)}) collective-permute-start(f32[776,128]{1,0:T(8,128)S(1)} %get-tuple-element.131), channel_id=1, source_target_pairs={{0,4},{1,9},{2,6},{3,11},{4,0},{5,13},{6,2},{7,15},{8,12},{9,1},{1... | collective-permute-start | bytes 1191944 | tf_op jit(solution)/shard_map/ppermute | solution.py:334
  144.7 3.9 %collective-permute-start.33 = (f32[512,128]{1,0:T(8,128)S(1)}, f32[512,128]{1,0:T(8,128)S(1)}, u32[]{:S(2)}, u32[]{:S(2)}) collective-permute-start(f32[512,128]{1,0:T(8,128)S(1)} %slice_add_fusion.6.refs_2_), channel_id=1, source_target_pairs={{0,1},{1,0},{2,3},{3,2},{4,5},{5,4},{6,7},{7,6},{8,9},{9,8},{10,11... | collective-permute-start | bytes 786440 | tf_op jit(solution)/shard_map/ppermute | solution.py:337
  148.5 5.8 %collective-permute-start.32 = (f32[392,128]{1,0:T(8,128)S(1)}, f32[392,128]{1,0:T(8,128)S(1)}, u32[]{:S(2)}, u32[]{:S(2)}) collective-permute-start(f32[392,128]{1,0:T(8,128)S(1)} %pad_maximum_fusion.18), channel_id=1, source_target_pairs={{0,8},{1,5},{2,10},{3,7},{4,12},{5,1},{6,14},{7,3},{8,0},{9,13},{1... | collective-permute-start | bytes 602120 | tf_op jit(solution)/shard_map/ppermute | solution.py:334
  151.4 7.9 %collective-permute-start.35 = (f32[776,128]{1,0:T(8,128)S(1)}, f32[776,128]{1,0:T(8,128)S(1)}, u32[]{:S(2)}, u32[]{:S(2)}) collective-permute-start(f32[776,128]{1,0:T(8,128)S(1)} %get-tuple-element.137), channel_id=1, source_target_pairs={{0,4},{1,9},{2,6},{3,11},{4,0},{5,13},{6,2},{7,15},{8,12},{9,1},{1... | collective-permute-start | bytes 1191944 | tf_op jit(solution)/shard_map/ppermute | solution.py:334
  154.4 11.1 %collective-permute-start.34 = (f32[392,128]{1,0:T(8,128)S(1)}, f32[392,128]{1,0:T(8,128)S(1)}, u32[]{:S(2)}, u32[]{:S(2)}) collective-permute-start(f32[392,128]{1,0:T(8,128)S(1)} %pad_maximum_fusion.19), channel_id=1, source_target_pairs={{0,16},{1,17},{2,18},{3,19},{4,20},{5,21},{6,22},{7,23},{8,24},{9,... | collective-permute-start | bytes 602120 | tf_op jit(solution)/shard_map/ppermute | solution.py:334
  159.4 7.3 %collective-permute-start.36 = (f32[392,128]{1,0:T(8,128)S(1)}, f32[392,128]{1,0:T(8,128)S(1)}, u32[]{:S(2)}, u32[]{:S(2)}) collective-permute-start(f32[392,128]{1,0:T(8,128)S(1)} %pad_maximum_fusion.20), channel_id=1, source_target_pairs={{0,8},{1,5},{2,10},{3,7},{4,12},{5,1},{6,14},{7,3},{8,0},{9,13},{1... | collective-permute-start | bytes 602120 | tf_op jit(solution)/shard_map/ppermute | solution.py:334
  165.5 6.6 %collective-permute-start.38 = (f32[384,128]{1,0:T(8,128)S(1)}, f32[384,128]{1,0:T(8,128)S(1)}, u32[]{:S(2)}, u32[]{:S(2)}) collective-permute-start(f32[384,128]{1,0:T(8,128)S(1)} %slice_add_fusion.21.refs_2_), channel_id=1, source_target_pairs={{0,8},{1,5},{2,10},{3,7},{4,12},{5,1},{6,14},{7,3},{8,0},{9,13},{1... | collective-permute-start | bytes 589832 | tf_op jit(solution)/shard_map/ppermute | solution.py:334
  166.7 11.9 %collective-permute-start.37 = (f32[392,128]{1,0:T(8,128)S(1)}, f32[392,128]{1,0:T(8,128)S(1)}, u32[]{:S(2)}, u32[]{:S(2)}) collective-permute-start(f32[392,128]{1,0:T(8,128)S(1)} %pad_maximum_fusion.21), channel_id=1, source_target_pairs={{0,16},{1,17},{2,18},{3,19},{4,20},{5,21},{6,22},{7,23},{8,24},{9,... | collective-permute-start | bytes 602120 | tf_op jit(solution)/shard_map/ppermute | solution.py:334
  178.7 7.9 %collective-permute-start.40 = (f32[384,128]{1,0:T(8,128)S(1)}, f32[384,128]{1,0:T(8,128)S(1)}, u32[]{:S(2)}, u32[]{:S(2)}) collective-permute-start(f32[384,128]{1,0:T(8,128)S(1)} %slice_add_fusion.20.refs_11_), channel_id=1, source_target_pairs={{0,8},{1,5},{2,10},{3,7},{4,12},{5,1},{6,14},{7,3},{8,0},{9,13},{1... | collective-permute-start | bytes 589832 | tf_op jit(solution)/shard_map/ppermute | solution.py:334
  178.8 11.2 %collective-permute-start.39 = (f32[768,128]{1,0:T(8,128)S(1)}, f32[768,128]{1,0:T(8,128)S(1)}, u32[]{:S(2)}, u32[]{:S(2)}) collective-permute-start(f32[768,128]{1,0:T(8,128)S(1)} %pad_maximum_fusion.4), channel_id=1, source_target_pairs={{0,4},{1,9},{2,6},{3,11},{4,0},{5,13},{6,2},{7,15},{8,12},{9,1},{1... | collective-permute-start | bytes 1179656 | tf_op jit(solution)/shard_map/ppermute | solution.py:334
  186.6 7.8 %collective-permute-start.41 = (f32[768,128]{1,0:T(8,128)S(1)}, f32[768,128]{1,0:T(8,128)S(1)}, u32[]{:S(2)}, u32[]{:S(2)}) collective-permute-start(f32[768,128]{1,0:T(8,128)S(1)} %pad_maximum_fusion.5), channel_id=1, source_target_pairs={{0,4},{1,9},{2,6},{3,11},{4,0},{5,13},{6,2},{7,15},{8,12},{9,1},{1... | collective-permute-start | bytes 1179656 | tf_op jit(solution)/shard_map/ppermute | solution.py:334

commit v8 on v7

--- a/solution.py
+++ b/solution.py
@@ -13,7 +13,8 @@
 PAIR = 2 * TILE
 UNITS = 4
 NORM_ROWS = 8
-BEHIND = 0
+ROW_TIMES = (8, 6, 11)
+COL_TIME = 22
 
 tiny_eps = 1e-06
 
@@ -34,10 +35,9 @@
 
 
 def fill_kernel(
-    place_ref, flip_ref, pattern_in, counts_in, delays_in, tiles_in,
+    place_ref, pattern_in, counts_in, delays_in, tiles_in,
     dense_ref, even_left_ref, odd_left_ref, pattern_ref, counts_ref, delays_ref, tiles_ref, arrived,
 ):
-    flip = flip_ref[0]
     row_blocks = tiles_in.shape[0]
     small = [
         pltpu.make_async_copy(source, target, arrived.at[row_blocks + i])
@@ -50,7 +50,7 @@
 
     def fetch(position):
         return pltpu.make_async_copy(
-            tiles_in.at[position ^ flip], tiles_ref.at[position], arrived.at[position]
+            tiles_in.at[position], tiles_ref.at[position], arrived.at[position]
         )
 
     for position in range(row_blocks):
@@ -60,9 +60,7 @@
 
     low = low_lanes((TILE, TILE))
     for pair in range(row_blocks // 2):
-        source = (pair ^ (flip // 2)) * PAIR
-        even = delays_ref[pl.ds(pl.multiple_of(source, TILE), TILE), :]
-        odd = delays_ref[pl.ds(pl.multiple_of(source + TILE, TILE), TILE), :]
+        even, odd = delays_ref[rows_of(2 * pair), :], delays_ref[rows_of(2 * pair + 1), :]
         even_left_ref[rows_of(pair), :] = jnp.where(low, even, turned(odd))
         odd_left_ref[rows_of(pair), :] = jnp.where(low, turned(even), odd)
 
@@ -71,22 +69,21 @@
         rows = pl.ds(pl.multiple_of(position * TILE, TILE), TILE)
         dense_ref[rows, :] = jnp.zeros((TILE, dense_ref.shape[1]), dense_ref.dtype)
         fetch(position).wait()
-        block = position ^ flip
-
-        @pl.loop(0, counts_ref[block])
+
+        @pl.loop(0, counts_ref[position])
         def _(tile):
-            place = place_ref[pattern_ref[block, tile]]
+            place = place_ref[pattern_ref[position, tile]]
             lanes = pl.ds(pl.multiple_of(place * TILE, TILE), TILE)
             dense_ref[rows, lanes] = tiles_ref[position, tile]
 
 
-def fill_dense(kernel, pattern, counts, places, flip, delays):
+def fill_dense(kernel, pattern, counts, places, delays):
     row_blocks = kernel.shape[0]
     rows = row_blocks * TILE
     left = jax.ShapeDtypeStruct((rows // 2, TILE), jnp.float32)
     return pl.pallas_call(
         fill_kernel,
-        in_specs=[SCALARS] * 2 + [pl.BlockSpec(memory_space=pltpu.HBM)] * 4,
+        in_specs=[SCALARS] + [pl.BlockSpec(memory_space=pltpu.HBM)] * 4,
         out_specs=[WHOLE] * 3,
         out_shape=[jax.ShapeDtypeStruct((rows, CB_DEV * TILE), kernel.dtype), left, left],
         scratch_shapes=[
@@ -102,7 +99,6 @@
         ),
     )(
         places,
-        flip,
         *(pltpu.with_memory_space_constraint(x, pltpu.HBM) for x in (pattern, counts.reshape(-1), delays, kernel)),
     )
 
@@ -151,12 +147,13 @@
 
 def back_kernel(first, *refs):
     if first:
-        dense_ref, own_ref, send_ref, keep_ref, turned_ref = refs
-        parts, raw_ref, scales = [(own_ref, 2)], None, (None, None, None)
+        dense_ref, total_ref, send_ref, keep_ref, turned_ref = refs
+        raw_ref, scales = None, (None, None, None)
     else:
-        (dense_ref, other_ref, own_ref, scale_ref, past_ref, past_scale_ref,
+        (dense_ref, total_ref, scale_ref, past_ref, past_scale_ref,
          send_ref, keep_ref, raw_ref, turned_ref) = refs
-        parts, scales = [(other_ref, 1), (own_ref, 1)], (scale_ref, past_ref, past_scale_ref)
+        scales = (scale_ref, past_ref, past_scale_ref)
+    parts = [(total_ref, 1)]
     sums = []
     half = turned_ref.shape[0]
     for pair, value, squares in next_vector(parts, raw_ref, *scales):
@@ -176,12 +173,11 @@
 
 def fore_kernel(first, *refs):
     if first:
-        (dense_ref, outer_ref, inner_ref, mine_ref, scale_ref,
-         send_ref, keep_ref, raw_ref, wide_ref) = refs
+        dense_ref, outer_ref, inner_ref, mine_ref, scale_ref, send_ref, raw_ref, wide_ref = refs
         scales = (scale_ref, None, None)
     else:
         (dense_ref, outer_ref, inner_ref, mine_ref, scale_ref, past_ref, past_scale_ref,
-         send_ref, keep_ref, raw_ref, wide_ref) = refs
+         send_ref, raw_ref, wide_ref) = refs
         scales = (scale_ref, past_ref, past_scale_ref)
     parts = [(outer_ref, 2), (inner_ref, 1), (mine_ref, 1)]
     low = low_lanes((TILE, TILE))
@@ -192,7 +188,7 @@
         wide_ref[rows_of(2 * pair + 1), :] = jnp.where(low, other, value).astype(wide_ref.dtype)
         if squares is not None:
             sums.append(squares)
-    send_ref[keep_ref.shape[0] :, :] = jnp.broadcast_to(squares_row(sums), (NORM_ROWS, TILE))
+    send_ref[dense_ref.shape[0] // 2 :, :] = jnp.broadcast_to(squares_row(sums), (NORM_ROWS, TILE))
     step = 4
     for start in range(0, dense_ref.shape[0] // TILE, step):
         product = jnp.dot(
@@ -202,20 +198,15 @@
         )
         for pair in range(step // 2):
             even, odd = product[rows_of(2 * pair), :], product[rows_of(2 * pair + 1), :]
-            store_message(start // 2 + pair, jnp.where(low, even, odd), send_ref, keep_ref)
-
-
-def product_call(body, dense, operands, half, raw_rows, scratch):
-    message = jax.ShapeDtypeStruct((half + NORM_ROWS, TILE), jnp.float32)
-    kept = jax.ShapeDtypeStruct((half, TILE), jnp.float32)
-    shapes = [message, kept]
-    if raw_rows:
-        shapes.append(jax.ShapeDtypeStruct((raw_rows, TILE), jnp.float32))
+            send_ref[rows_of(start // 2 + pair), :] = jnp.where(low, even, odd)
+
+
+def product_call(body, dense, operands, out_rows, scratch):
     return pl.pallas_call(
         body,
         in_specs=[WHOLE] * (1 + len(operands)),
-        out_specs=[WHOLE] * len(shapes),
-        out_shape=shapes,
+        out_specs=[WHOLE] * len(out_rows),
+        out_shape=[jax.ShapeDtypeStruct((rows, TILE), jnp.float32) for rows in out_rows],
         scratch_shapes=[scratch],
         compiler_params=pltpu.CompilerParams(vmem_limit_bytes=12 * 1024 * 1024),
         cost_estimate=pl.CostEstimate(
@@ -225,19 +216,17 @@
 
 
 def back_product(dense, operands, first):
-    scratch = pltpu.VMEM((TILE // 2, dense.shape[0]), dense.dtype)
-    raw_rows = 0 if first else dense.shape[0] // 2
-    return product_call(
-        functools.partial(back_kernel, first), dense, operands, dense.shape[1] // 4, raw_rows, scratch
-    )
+    rows, cells = dense.shape
+    scratch = pltpu.VMEM((TILE // 2, rows), dense.dtype)
+    out_rows = [cells // 4 + NORM_ROWS, cells // 4] + ([] if first else [rows // 2])
+    return product_call(functools.partial(back_kernel, first), dense, operands, out_rows, scratch)
 
 
 def fore_product(dense, operands, first):
-    scratch = pltpu.VMEM((dense.shape[1], TILE), dense.dtype)
-    return product_call(
-        functools.partial(fore_kernel, first),
-        dense, operands, dense.shape[0] // 4, dense.shape[1] // 2, scratch,
-    )
+    rows, cells = dense.shape
+    scratch = pltpu.VMEM((cells, TILE), dense.dtype)
+    out_rows = [rows // 2 + NORM_ROWS, cells // 2]
+    return product_call(functools.partial(fore_kernel, first), dense, operands, out_rows, scratch)
 
 
 def rotation(norms):
@@ -319,7 +308,6 @@
 
 def on_device(row_count, col_count, kernel, pattern, counts, delays):
     row_bits = list(range(row_count.bit_length() - 1))
-    col_bits = list(range(col_count.bit_length() - 1))
     row_index = lax.axis_index("rows")
     core = lax.axis_index("cols") & 1
 
@@ -333,9 +321,6 @@
                 pairs.append((row * col_count + col, partner * col_count + col))
         return lax.ppermute(value, ("rows", "cols"), pairs)
 
-    def swap_cols(value, level):
-        return lax.ppermute(value, "cols", [(i, i ^ (1 << level)) for i in range(col_count)])
-
     bits = [(row_index >> bit) & 1 for bit in row_bits[:2]]
     outer_side = jnp.where(core == 0, bits[0], bits[1])
     inner_side = jnp.where(core == 0, bits[1], bits[0])
@@ -343,51 +328,41 @@
     blocks = jnp.arange(CB_DEV, dtype=jnp.int32)
     unit = CB_DEV // UNITS
     places = ((blocks // unit) ^ mask) * unit + blocks % unit
-    flip = ((1 - core) * (kernel.shape[0] // 2)).astype(jnp.int32).reshape(1)
     mask = mask.reshape(1)
 
-    dense, *lefts = fill_dense(kernel, pattern, counts, places, flip, delays)
+    dense, *lefts = fill_dense(kernel, pattern, counts, places, delays)
 
     def reduce_rows(send, keep):
         half = keep.shape[0]
-        got = yield swap_rows, send, 0
+        got = yield ROW_TIMES[0], swap_rows, send, 0
         keep = keep + got[:half]
         norm = send[half:] + got[half:]
         send, mine = keep[: half // 2], keep[half // 2 :]
         for level in range(1, len(row_bits)):
-            got = yield swap_rows, jnp.concatenate([send, norm]), level
+            message = jnp.concatenate([send, norm])
+            got = yield ROW_TIMES[min(level, 2)], swap_rows, message, level
             norm = norm + got[half // 2 :]
             send = mine = mine + got[: half // 2]
-        inner = yield swap_rows, mine, 1
-        outer = yield swap_rows, jnp.concatenate([inner, mine]), 0
+        inner = yield ROW_TIMES[1], swap_rows, mine, 1
+        outer = yield ROW_TIMES[0], swap_rows, jnp.concatenate([inner, mine]), 0
         return [outer, inner, mine], norm
 
-    def reduce_cols(send, keep):
-        half = keep.shape[0]
-        got = yield swap_cols, send, 0
-        own = keep + got[:half]
-        norm = send[half:] + got[half:]
-        for bit in col_bits[1:]:
-            got = yield swap_cols, jnp.concatenate([own, norm]), bit
-            norm = norm + got[half:]
-            own = own + got[:half]
-        other = yield swap_cols, own, 0
-        return [other, own], norm
-
-    def chain(left):
+    def sum_cols(value, turned_group):
+        group = list(range(col_count))
+        return lax.psum(value, "cols", axis_index_groups=[group[::-1] if turned_group else group])
+
+    def chain(left, second):
         send, keep = back_product(dense, [left], True)
         totals, norm = yield from reduce_rows(send, keep)
         norms = [norm]
         rights = []
         for iteration in range(ITERS):
             past = [rights[-1], norms[-2]] if rights else []
-            send, keep, right = fore_product(dense, [*totals, norms[-1], *past], not rights)
+            message, right = fore_product(dense, [*totals, norms[-1], *past], not rights)
             rights.append(right)
-            halves, norm = yield from reduce_cols(send, keep)
-            norms.append(norm)
-            send, keep, left = back_product(
-                dense, [*halves, norms[-1], left, norms[-2]], False
-            )
+            total = yield COL_TIME, sum_cols, message, second
+            norms.append(total[-NORM_ROWS:])
+            send, keep, left = back_product(dense, [total, norms[-1], left, norms[-2]], False)
             totals, norm = yield from reduce_rows(send, keep)
             norms.append(norm)
         return rights, norms, totals
@@ -395,28 +370,27 @@
     def tied(value, other):
         return lax.optimization_barrier((value, other))[0]
 
-    runs = [chain(left) for left in lefts]
+    runs = [chain(left, second) for second, left in enumerate(lefts)]
     wanted = [next(run) for run in runs]
     chains = [None] * len(runs)
     gots = [None] * len(runs)
-    swap, latest, level = wanted[0]
-    gots[0] = swap(latest, level)
-    turn = 0
+    length, transfer, latest, level = wanted[0]
+    due = [length, length]
+    gots[0] = transfer(latest, level)
     while None in chains:
-        mine = 0 if turn < BEHIND else (turn - BEHIND) % 2
-        turn += 1
-        if chains[mine] is not None:
-            continue
+        mine = due.index(min(due))
         if gots[mine] is None:
-            swap, value, level = wanted[mine]
+            length, transfer, value, level = wanted[mine]
             latest = tied(value, latest)
         else:
             try:
-                swap, latest, level = runs[mine].send(tied(gots[mine], latest))
+                length, transfer, latest, level = runs[mine].send(tied(gots[mine], latest))
             except StopIteration as stop:
                 chains[mine] = stop.value
+                due[mine] = float("inf")
                 continue
-        gots[mine] = swap(latest, level)
+        gots[mine] = transfer(latest, level)
+        due[mine] += length
 
     cells = dense.shape[1]
     model, misfit = last_call(

time: 195 us -> 357 us (1.83)
  waiting for transfers between devices: 98.7 us -> 190 us
  local copies, waits for them, and re-layouts: 0.6 us -> 50.8 us
  between operations: 1.3 us -> 14.2 us
  other arithmetic: 1.4 us -> 7.99 us
    psum x0 -> x4, waiting for transfers between devices: none -> 85.2 us  [sum_cols(): lax.psum(value, 'cols', axis_index_groups=[group[::-1] if turned_group el...]
    unnamed x0 -> x68, local copies, waits for them, and re-layouts: none -> 47.5 us
    ppermute x30, waiting for transfers between devices: 91.5 us -> 104 us  [swap_rows(): return lax.ppermute(value, ('rows', 'cols'), pairs)]
    ppermute x12 -> x0, waiting for transfers between devices: 7.24 us -> none  [swap_cols(): lax.ppermute(value, 'cols', [(i, i ^ 1 << level) for i in range(col_count)])]
    ppermute x12 -> x0, starting transfers between devices: 6.48 us -> none  [swap_cols(): lax.ppermute(value, 'cols', [(i, i ^ 1 << level) for i in range(col_count)])]
    ppermute x30, starting transfers between devices: 50 us -> 54.3 us  [swap_rows(): return lax.ppermute(value, ('rows', 'cols'), pairs)]
  transfers between devices with their start and end apart: 42 -> 34, of which waited for: 30 -> 28; matrix products, arithmetic and copies ran while one was open for 1% -> 2% of each run, Pallas kernels for 15% -> 7%
where the time goes in v8:
time: 357 us; the launch traced here: 356 us
  waiting for transfers between devices  190 us (53%)
  starting transfers between devices  54.9 us (15%)
  local copies, waits for them, and re-layouts  50.8 us (14%)
  Pallas kernels  38.9 us (11%)
  between operations  14.2 us (4%)
  other arithmetic  7.99 us (2%)
    ppermute x30, waiting for transfers between devices, swap_rows(): return lax.ppermute(value, ('rows', 'cols'), pairs)  104 us
    psum x4, waiting for transfers between devices, sum_cols(): lax.psum(value, 'cols', axis_index_groups=[group[::-1] if turned_group el...  85.2 us
    ppermute x30, starting transfers between devices, swap_rows(): return lax.ppermute(value, ('rows', 'cols'), pairs)  54.3 us
    unnamed x68, local copies, waits for them, and re-layouts  47.5 us
    pallas_call x10, Pallas kernels, product_call(): pl.pallas_call(body, in_specs=[WHOLE] * (1 + len(operands)), out_specs=[W...  31.1 us
  transfers between devices with their start and end apart: 34, of which 28 were waited for; matrix products, arithmetic and copies ran while one was open for 2% of the time, Pallas kernels for 7%

profile of v8, /device:TPU:0, one launch (start us, length us, event | category | flops | bytes accessed | tf_op | source)
XLA Modules:
  0.0 356.3 jit_solution(18262137527031424556)
XLA Ops:
  7.2 4.4 %shard_map.67 = (bf16[2048,3072]{1,0:T(8,128)(2,1)S(1)}, f32[1024,128]{1,0:T(8,128)S(1)}, f32[1024,128]{1,0:T(8,128)S(1)}) custom-call(s32[24]{0:T(128)S(1)} %fusion.place_ref, s32[16,16]{1,0:T(8,128)} %pattern_in.1, s32[16]{0:T(128)} %bitcast.4, f32[2048,128]{1,0:T(8,128)} %delays_in.1, bf16[16,16,128,128]{3,2,1,0:T(8,128)(2,1)} %tiles_in.1), custom_call_target="tpu_custom_call" | custom-call | bytes 8388608 | tf_op jit(solution)/shard_map/pallas_call | solution.py:84
  14.1 3.1 collective-permute-start
  17.2 5.8 %collective-permute-done = f32[776,128]{1,0:T(8,128)S(1)} collective-permute-done((f32[776,128]{1,0:T(8,128)S(1)}, f32[776,128]{1,0:T(8,128)S(1)}, u32[]{:S(2)}, u32[]{:S(2)}) %collective-permute-start) | collective-permute-done | bytes 397344 | tf_op jit(solution)/shard_map/ppermute | solution.py:322
  29.3 6.5 %collective-permute-done.3 = f32[776,128]{1,0:T(8,128)S(1)} collective-permute-done((f32[776,128]{1,0:T(8,128)S(1)}, f32[776,128]{1,0:T(8,128)S(1)}, u32[]{:S(2)}, u32[]{:S(2)}) %collective-permute-start.3) | collective-permute-done | bytes 397344 | tf_op jit(solution)/shard_map/ppermute | solution.py:322
  36.0 4.4 %collective-permute-start.2 = (f32[392,128]{1,0:T(8,128)S(1)}, f32[392,128]{1,0:T(8,128)S(1)}, u32[]{:S(2)}, u32[]{:S(2)}) collective-permute-start(f32[392,128]{1,0:T(8,128)S(1)} %pad_maximum_fusion.7), channel_id=1, source_target_pairs={{0,16},{1,17},{2,18},{3,19},{4,20},{5,21},{6,22},{7,23},{8,24},{9,... | collective-permute-start | bytes 602120 | tf_op jit(solution)/shard_map/ppermute | solution.py:322
  42.9 5.2 %collective-permute-done.2 = f32[392,128]{1,0:T(8,128)S(1)} collective-permute-done((f32[392,128]{1,0:T(8,128)S(1)}, f32[392,128]{1,0:T(8,128)S(1)}, u32[]{:S(2)}, u32[]{:S(2)}) %collective-permute-start.2) | collective-permute-done | bytes 200736 | tf_op jit(solution)/shard_map/ppermute | solution.py:322
  48.5 3.4 collective-permute-start.7
  51.9 4.2 %collective-permute-done.5.refs_2_ = f32[384,128]{1,0:T(8,128)S(1)} collective-permute-done((f32[384,128]{1,0:T(8,128)S(1)}, f32[384,128]{1,0:T(8,128)S(1)}, u32[]{:S(2)}, u32[]{:S(2)}) %collective-permute-start.5) | collective-permute-done | bytes 196640 | tf_op jit(solution)/shard_map/ppermute | solution.py:322
  60.9 4.2 %collective-permute-done.6.refs_1_ = f32[768,128]{1,0:T(8,128)S(1)} collective-permute-done((f32[768,128]{1,0:T(8,128)S(1)}, f32[768,128]{1,0:T(8,128)S(1)}, u32[]{:S(2)}, u32[]{:S(2)}) %collective-permute-start.6) | collective-permute-done | bytes 393248 | tf_op jit(solution)/shard_map/ppermute | solution.py:322
  65.1 4.3 %shard_map.70 = (f32[1032,128]{1,0:T(8,128)}, f32[1536,128]{1,0:T(8,128)S(1)}) custom-call(bf16[2048,3072]{1,0:T(8,128)(2,1)S(1)} %get-tuple-element.65.refs_0_, f32[768,128]{1,0:T(8,128)S(1)} %collective-permute-done.6.refs_1_, f32[384,128]{1,0:T(8,128)S(1)} %collective-permute-done.5.refs_2_, f32[384,128]{1,0:T(8,128)S(1)} %slice_add_fusion.17.refs_3_, ...), custom_call_target="tpu_custom_call" | custom-call | flops 3221225472 | bytes 12582912 | tf_op jit(solution)/shard_map/pallas_call | solution.py:205
  69.5 2.5 collective-permute-start.9
  73.0 4.8 %collective-permute-done.9.refs_1_ = f32[768,128]{1,0:T(8,128)S(1)} collective-permute-done((f32[768,128]{1,0:T(8,128)S(1)}, f32[768,128]{1,0:T(8,128)S(1)}, u32[]{:S(2)}, u32[]{:S(2)}) %collective-permute-start.9) | collective-permute-done | bytes 393248 | tf_op jit(solution)/shard_map/ppermute | solution.py:322
  77.8 4.7 %copy-done.1 = bf16[2048,3072]{1,0:T(8,128)(2,1)S(1)} copy-done((bf16[2048,3072]{1,0:T(8,128)(2,1)S(1)}, bf16[2048,3072]{1,0:T(8,128)(2,1)}, u32[]{:S(2)}) %copy-start.1) | copy-done | bytes 12582936
  82.5 4.3 %shard_map.71 = (f32[1032,128]{1,0:T(8,128)}, f32[1536,128]{1,0:T(8,128)S(1)}) custom-call(bf16[2048,3072]{1,0:T(8,128)(2,1)S(1)} %copy-done.1, f32[768,128]{1,0:T(8,128)S(1)} %collective-permute-done.9.refs_1_, f32[384,128]{1,0:T(8,128)S(1)} %collective-permute-done.8.refs_2_, f32[384,128]{1,0:T(8,128)S(1)} %slice_add_fusion.16.refs_3_, ...), custom_call_target="tpu_custom_call" | custom-call | flops 3221225472 | bytes 12582912 | tf_op jit(solution)/shard_map/pallas_call | solution.py:205
  86.8 20.4 %all-reduce.5.cloned.1.call-done.refs_1_ = f32[1032,128]{1,0:T(8,128)} async-done(((f32[1032,128]{1,0:T(8,128)}), f32[1032,128]{1,0:T(8,128)}) %all-reduce.5.cloned.1.call-update) | async-done | bytes 528400 | tf_op jit(solution)/shard_map/psum | solution.py:352
  107.9 4.6 %copy-done.2 = bf16[2048,3072]{1,0:T(8,128)(2,1)S(1)} copy-done((bf16[2048,3072]{1,0:T(8,128)(2,1)S(1)}, bf16[2048,3072]{1,0:T(8,128)(2,1)}, u32[]{:S(2)}) %copy-start.2) | copy-done | bytes 12582936
  113.5 2.5 shard_map.72
  118.3 6.3 %collective-permute-done.10 = f32[776,128]{1,0:T(8,128)S(1)} collective-permute-done((f32[776,128]{1,0:T(8,128)S(1)}, f32[776,128]{1,0:T(8,128)S(1)}, u32[]{:S(2)}, u32[]{:S(2)}) %collective-permute-start.10) | collective-permute-done | bytes 397344 | tf_op jit(solution)/shard_map/ppermute | solution.py:322
  128.7 22.2 %all-reduce.7.cloned.1.call-done.refs_1_ = f32[1032,128]{1,0:T(8,128)} async-done(((f32[1032,128]{1,0:T(8,128)}), f32[1032,128]{1,0:T(8,128)}) %all-reduce.7.cloned.1.call-update) | async-done | bytes 528400 | tf_op jit(solution)/shard_map/psum | solution.py:352
  151.5 4.6 %copy-done.3 = bf16[2048,3072]{1,0:T(8,128)(2,1)S(1)} copy-done((bf16[2048,3072]{1,0:T(8,128)(2,1)S(1)}, bf16[2048,3072]{1,0:T(8,128)(2,1)}, u32[]{:S(2)}) %copy-start.3) | copy-done | bytes 12582936
  157.2 2.5 shard_map.73
  161.3 6.3 %collective-permute-done.13 = f32[776,128]{1,0:T(8,128)S(1)} collective-permute-done((f32[776,128]{1,0:T(8,128)S(1)}, f32[776,128]{1,0:T(8,128)S(1)}, u32[]{:S(2)}, u32[]{:S(2)}) %collective-permute-start.13) | collective-permute-done | bytes 397344 | tf_op jit(solution)/shard_map/ppermute | solution.py:322
  171.6 3.2 collective-permute-done.14
  174.9 4.6 %collective-permute-done.12 = f32[392,128]{1,0:T(8,128)S(1)} collective-permute-done((f32[392,128]{1,0:T(8,128)S(1)}, f32[392,128]{1,0:T(8,128)S(1)}, u32[]{:S(2)}, u32[]{:S(2)}) %collective-permute-start.12) | collective-permute-done | bytes 200736 | tf_op jit(solution)/shard_map/ppermute | solution.py:322
  179.5 2.7 collective-permute-start.15
  182.2 3.4 collective-permute-start.17
  187.3 3.7 %collective-permute-done.17 = f32[392,128]{1,0:T(8,128)S(1)} collective-permute-done((f32[392,128]{1,0:T(8,128)S(1)}, f32[392,128]{1,0:T(8,128)S(1)}, u32[]{:S(2)}, u32[]{:S(2)}) %collective-permute-start.17) | collective-permute-done | bytes 200736 | tf_op jit(solution)/shard_map/ppermute | solution.py:322
  191.1 2.7 collective-permute-start.18
  194.0 4.6 %copy-done.4 = bf16[2048,3072]{1,0:T(8,128)(2,1)S(1)} copy-done((bf16[2048,3072]{1,0:T(8,128)(2,1)S(1)}, bf16[2048,3072]{1,0:T(8,128)(2,1)}, u32[]{:S(2)}) %copy-start.4) | copy-done | bytes 12582936
  198.5 3.5 shard_map.74
  205.8 5.9 %collective-permute-done.19.refs_1_ = f32[768,128]{1,0:T(8,128)S(1)} collective-permute-done((f32[768,128]{1,0:T(8,128)}, f32[768,128]{1,0:T(8,128)S(1)}, u32[]{:S(2)}, u32[]{:S(2)}) %collective-permute-start.19) | collective-permute-done | bytes 393248 | tf_op jit(solution)/shard_map/ppermute | solution.py:322
  212.4 4.6 %copy-done.5 = bf16[2048,3072]{1,0:T(8,128)(2,1)S(1)} copy-done((bf16[2048,3072]{1,0:T(8,128)(2,1)S(1)}, bf16[2048,3072]{1,0:T(8,128)(2,1)}, u32[]{:S(2)}) %copy-start.5) | copy-done | bytes 12582936
  218.6 3.5 shard_map.75
  223.0 21.4 %all-reduce.9.cloned.1.call-done.refs_1_ = f32[1032,128]{1,0:T(8,128)} async-done(((f32[1032,128]{1,0:T(8,128)}), f32[1032,128]{1,0:T(8,128)}) %all-reduce.9.cloned.1.call-update) | async-done | bytes 528400 | tf_op jit(solution)/shard_map/psum | solution.py:352
  245.1 4.6 %copy-done.6 = bf16[2048,3072]{1,0:T(8,128)(2,1)S(1)} copy-done((bf16[2048,3072]{1,0:T(8,128)(2,1)S(1)}, bf16[2048,3072]{1,0:T(8,128)(2,1)}, u32[]{:S(2)}) %copy-start.6) | copy-done | bytes 12582936
  252.4 3.0 shard_map.76
  256.9 6.6 %collective-permute-done.20 = f32[776,128]{1,0:T(8,128)} collective-permute-done((f32[776,128]{1,0:T(8,128)}, f32[776,128]{1,0:T(8,128)}, u32[]{:S(2)}, u32[]{:S(2)}) %collective-permute-start.20) | collective-permute-done | bytes 397344 | tf_op jit(solution)/shard_map/ppermute | solution.py:322
  268.3 21.1 %all-reduce.11.cloned.1.call-done.refs_1_ = f32[1032,128]{1,0:T(8,128)} async-done(((f32[1032,128]{1,0:T(8,128)}), f32[1032,128]{1,0:T(8,128)}) %all-reduce.11.cloned.1.call-update) | async-done | bytes 528400 | tf_op jit(solution)/shard_map/psum | solution.py:352
  290.1 4.6 %copy-done.7 = bf16[2048,3072]{1,0:T(8,128)(2,1)S(1)} copy-done((bf16[2048,3072]{1,0:T(8,128)(2,1)S(1)}, bf16[2048,3072]{1,0:T(8,128)(2,1)}, u32[]{:S(2)}) %copy-start.7) | copy-done | bytes 12582936
  297.5 2.5 shard_map.77
  303.2 4.7 %collective-permute-done.23 = f32[776,128]{1,0:T(8,128)S(1)} collective-permute-done((f32[776,128]{1,0:T(8,128)S(1)}, f32[776,128]{1,0:T(8,128)S(1)}, u32[]{:S(2)}, u32[]{:S(2)}) %collective-permute-start.23) | collective-permute-done | bytes 397344 | tf_op jit(solution)/shard_map/ppermute | solution.py:322
  311.9 3.2 collective-permute-done.24
  315.2 4.6 %collective-permute-done.22 = f32[392,128]{1,0:T(8,128)S(1)} collective-permute-done((f32[392,128]{1,0:T(8,128)S(1)}, f32[392,128]{1,0:T(8,128)S(1)}, u32[]{:S(2)}, u32[]{:S(2)}) %collective-permute-start.22) | collective-permute-done | bytes 200736 | tf_op jit(solution)/shard_map/ppermute | solution.py:322
  319.8 2.7 collective-permute-start.26
  322.5 3.4 collective-permute-start.25
  326.2 6.0 %collective-permute-done.25 = f32[392,128]{1,0:T(8,128)S(1)} collective-permute-done((f32[392,128]{1,0:T(8,128)S(1)}, f32[392,128]{1,0:T(8,128)S(1)}, u32[]{:S(2)}, u32[]{:S(2)}) %collective-permute-start.25) | collective-permute-done | bytes 200736 | tf_op jit(solution)/shard_map/ppermute | solution.py:322
  332.7 7.5 %collective-permute-done.28.refs_10_ = f32[384,128]{1,0:T(8,128)S(1)} collective-permute-done((f32[384,128]{1,0:T(8,128)S(1)}, f32[384,128]{1,0:T(8,128)S(1)}, u32[]{:S(2)}, u32[]{:S(2)}) %collective-permute-start.28) | collective-permute-done | bytes 196640 | tf_op jit(solution)/shard_map/ppermute | solution.py:322
  342.7 5.4 %collective-permute-done.29.refs_9_ = f32[768,128]{1,0:T(8,128)S(1)} collective-permute-done((f32[768,128]{1,0:T(8,128)S(1)}, f32[768,128]{1,0:T(8,128)S(1)}, u32[]{:S(2)}, u32[]{:S(2)}) %collective-permute-start.29) | collective-permute-done | bytes 393248 | tf_op jit(solution)/shard_map/ppermute | solution.py:322
  (171 shorter events, 67.2 us)
Async XLA Ops:
  7.2 100.0 %all-reduce.5.cloned.1.call-start = ((), (), s32[]{:S(2)}) async-start(), calls=%async_computation | async-start | bytes 1056768 | tf_op jit(solution)/shard_map/psum | solution.py:352
  11.6 53.5 %copy-start = (bf16[2048,3072]{1,0:T(8,128)(2,1)}, bf16[2048,3072]{1,0:T(8,128)(2,1)S(1)}, u32[]{:S(2)}) copy-start(bf16[2048,3072]{1,0:T(8,128)(2,1)S(1)} %get-tuple-element.65.refs_0_) | copy-start | bytes 37748740
  14.1 8.9 %collective-permute-start = (f32[776,128]{1,0:T(8,128)S(1)}, f32[776,128]{1,0:T(8,128)S(1)}, u32[]{:S(2)}, u32[]{:S(2)}) collective-permute-start(f32[776,128]{1,0:T(8,128)S(1)} %get-tuple-element.68), channel_id=1, source_target_pairs={{0,4},{1,9},{2,6},{3,11},{4,0},{5,13},{6,2},{7,15},{8,12},{9,1},{1... | collective-permute-start | bytes 1191944 | tf_op jit(solution)/shard_map/ppermute | solution.py:322
  23.1 6.2 %collective-permute-start.1 = (f32[392,128]{1,0:T(8,128)S(1)}, f32[392,128]{1,0:T(8,128)S(1)}, u32[]{:S(2)}, u32[]{:S(2)}) collective-permute-start(f32[392,128]{1,0:T(8,128)S(1)} %pad_maximum_fusion.6), channel_id=1, source_target_pairs={{0,8},{1,5},{2,10},{3,7},{4,12},{5,1},{6,14},{7,3},{8,0},{9,13},{1... | collective-permute-start | bytes 602120 | tf_op jit(solution)/shard_map/ppermute | solution.py:322
  28.0 7.9 %collective-permute-start.3 = (f32[776,128]{1,0:T(8,128)S(1)}, f32[776,128]{1,0:T(8,128)S(1)}, u32[]{:S(2)}, u32[]{:S(2)}) collective-permute-start(f32[776,128]{1,0:T(8,128)S(1)} %get-tuple-element.72), channel_id=1, source_target_pairs={{0,4},{1,9},{2,6},{3,11},{4,0},{5,13},{6,2},{7,15},{8,12},{9,1},{1... | collective-permute-start | bytes 1191944 | tf_op jit(solution)/shard_map/ppermute | solution.py:322
  35.9 6.9 %collective-permute-start.4 = (f32[392,128]{1,0:T(8,128)S(1)}, f32[392,128]{1,0:T(8,128)S(1)}, u32[]{:S(2)}, u32[]{:S(2)}) collective-permute-start(f32[392,128]{1,0:T(8,128)S(1)} %pad_maximum_fusion.8), channel_id=1, source_target_pairs={{0,8},{1,5},{2,10},{3,7},{4,12},{5,1},{6,14},{7,3},{8,0},{9,13},{1... | collective-permute-start | bytes 602120 | tf_op jit(solution)/shard_map/ppermute | solution.py:322
  36.0 12.1 %collective-permute-start.2 = (f32[392,128]{1,0:T(8,128)S(1)}, f32[392,128]{1,0:T(8,128)S(1)}, u32[]{:S(2)}, u32[]{:S(2)}) collective-permute-start(f32[392,128]{1,0:T(8,128)S(1)} %pad_maximum_fusion.7), channel_id=1, source_target_pairs={{0,16},{1,17},{2,18},{3,19},{4,20},{5,21},{6,22},{7,23},{8,24},{9,... | collective-permute-start | bytes 602120 | tf_op jit(solution)/shard_map/ppermute | solution.py:322
  48.1 8.0 %collective-permute-start.5 = (f32[384,128]{1,0:T(8,128)S(1)}, f32[384,128]{1,0:T(8,128)S(1)}, u32[]{:S(2)}, u32[]{:S(2)}) collective-permute-start(f32[384,128]{1,0:T(8,128)S(1)} %slice_add_fusion.17.refs_3_), channel_id=1, source_target_pairs={{0,8},{1,5},{2,10},{3,7},{4,12},{5,1},{6,14},{7,3},{8,0},{9,13},{1... | collective-permute-start | bytes 589832 | tf_op jit(solution)/shard_map/ppermute | solution.py:322
  48.5 11.6 %collective-permute-start.7 = (f32[392,128]{1,0:T(8,128)S(1)}, f32[392,128]{1,0:T(8,128)S(1)}, u32[]{:S(2)}, u32[]{:S(2)}) collective-permute-start(f32[392,128]{1,0:T(8,128)S(1)} %pad_maximum_fusion.9), channel_id=1, source_target_pairs={{0,16},{1,17},{2,18},{3,19},{4,20},{5,21},{6,22},{7,23},{8,24},{9,... | collective-permute-start | bytes 602120 | tf_op jit(solution)/shard_map/ppermute | solution.py:322
  56.2 9.0 %collective-permute-start.6 = (f32[768,128]{1,0:T(8,128)S(1)}, f32[768,128]{1,0:T(8,128)S(1)}, u32[]{:S(2)}, u32[]{:S(2)}) collective-permute-start(f32[768,128]{1,0:T(8,128)S(1)} %pad_maximum_fusion), channel_id=1, source_target_pairs={{0,4},{1,9},{2,6},{3,11},{4,0},{5,13},{6,2},{7,15},{8,12},{9,1},{1... | collective-permute-start | bytes 1179656 | tf_op jit(solution)/shard_map/ppermute | solution.py:322
  60.8 8.6 %collective-permute-start.8 = (f32[384,128]{1,0:T(8,128)S(1)}, f32[384,128]{1,0:T(8,128)S(1)}, u32[]{:S(2)}, u32[]{:S(2)}) collective-permute-start(f32[384,128]{1,0:T(8,128)S(1)} %slice_add_fusion.16.refs_3_), channel_id=1, source_target_pairs={{0,8},{1,5},{2,10},{3,7},{4,12},{5,1},{6,14},{7,3},{8,0},{9,13},{1... | collective-permute-start | bytes 589832 | tf_op jit(solution)/shard_map/ppermute | solution.py:322
  69.5 8.3 %collective-permute-start.9 = (f32[768,128]{1,0:T(8,128)S(1)}, f32[768,128]{1,0:T(8,128)S(1)}, u32[]{:S(2)}, u32[]{:S(2)}) collective-permute-start(f32[768,128]{1,0:T(8,128)S(1)} %pad_maximum_fusion.1), channel_id=1, source_target_pairs={{0,4},{1,9},{2,6},{3,11},{4,0},{5,13},{6,2},{7,15},{8,12},{9,1},{1... | collective-permute-start | bytes 1179656 | tf_op jit(solution)/shard_map/ppermute | solution.py:322
  72.7 78.1 %all-reduce.7.cloned.1.call-start = ((), (), s32[]{:S(2)}) async-start(), calls=%async_computation.1 | async-start | bytes 1056768 | tf_op jit(solution)/shard_map/psum | solution.py:352
  77.8 4.7 %copy-start.1 = (bf16[2048,3072]{1,0:T(8,128)(2,1)S(1)}, bf16[2048,3072]{1,0:T(8,128)(2,1)}, u32[]{:S(2)}) copy-start(bf16[2048,3072]{1,0:T(8,128)(2,1)} %copy-done) | copy-start | bytes 37748740
  116.8 7.8 %collective-permute-start.10 = (f32[776,128]{1,0:T(8,128)S(1)}, f32[776,128]{1,0:T(8,128)S(1)}, u32[]{:S(2)}, u32[]{:S(2)}) collective-permute-start(f32[776,128]{1,0:T(8,128)S(1)} %get-tuple-element.88), channel_id=1, source_target_pairs={{0,4},{1,9},{2,6},{3,11},{4,0},{5,13},{6,2},{7,15},{8,12},{9,1},{1... | collective-permute-start | bytes 1191944 | tf_op jit(solution)/shard_map/ppermute | solution.py:322
  118.3 126.1 %all-reduce.9.cloned.1.call-start = ((), (), s32[]{:S(2)}) async-start(), calls=%async_computation.2 | async-start | bytes 1056768 | tf_op jit(solution)/shard_map/psum | solution.py:352
  127.1 34.1 %collective-permute-start.11 = (f32[392,128]{1,0:T(8,128)S(1)}, f32[392,128]{1,0:T(8,128)S(1)}, u32[]{:S(2)}, u32[]{:S(2)}) collective-permute-start(f32[392,128]{1,0:T(8,128)S(1)} %pad_maximum_fusion.10), channel_id=1, source_target_pairs={{0,8},{1,5},{2,10},{3,7},{4,12},{5,1},{6,14},{7,3},{8,0},{9,13},{1... | collective-permute-start | bytes 602120 | tf_op jit(solution)/shard_map/ppermute | solution.py:322
  159.7 34.3 %copy-start.14 = (f32[1024,128]{1,0:T(8,128)}, f32[1024,128]{1,0:T(8,128)S(1)}, u32[]{:S(2)}) copy-start(f32[1024,128]{1,0:T(8,128)S(1)} %get-tuple-element.112.refs_3_) | copy-start | bytes 1572868
  159.7 7.9 %collective-permute-start.13 = (f32[776,128]{1,0:T(8,128)S(1)}, f32[776,128]{1,0:T(8,128)S(1)}, u32[]{:S(2)}, u32[]{:S(2)}) collective-permute-start(f32[776,128]{1,0:T(8,128)S(1)} %get-tuple-element.91), channel_id=1, source_target_pairs={{0,4},{1,9},{2,6},{3,11},{4,0},{5,13},{6,2},{7,15},{8,12},{9,1},{1... | collective-permute-start | bytes 1191944 | tf_op jit(solution)/shard_map/ppermute | solution.py:322
  167.7 7.2 %collective-permute-start.14 = (f32[392,128]{1,0:T(8,128)S(1)}, f32[392,128]{1,0:T(8,128)S(1)}, u32[]{:S(2)}, u32[]{:S(2)}) collective-permute-start(f32[392,128]{1,0:T(8,128)S(1)} %pad_maximum_fusion.12), channel_id=1, source_target_pairs={{0,8},{1,5},{2,10},{3,7},{4,12},{5,1},{6,14},{7,3},{8,0},{9,13},{1... | collective-permute-start | bytes 602120 | tf_op jit(solution)/shard_map/ppermute | solution.py:322
  169.2 10.3 %collective-permute-start.12 = (f32[392,128]{1,0:T(8,128)S(1)}, f32[392,128]{1,0:T(8,128)S(1)}, u32[]{:S(2)}, u32[]{:S(2)}) collective-permute-start(f32[392,128]{1,0:T(8,128)S(1)} %pad_maximum_fusion.11), channel_id=1, source_target_pairs={{0,16},{1,17},{2,18},{3,19},{4,20},{5,21},{6,22},{7,23},{8,24},{9,... | collective-permute-start | bytes 602120 | tf_op jit(solution)/shard_map/ppermute | solution.py:322
  174.9 12.4 %copy-start.32 = (f32[8,128]{1,0:T(8,128)}, f32[8,128]{1,0:T(8,128)S(1)}, u32[]{:S(2)}) copy-start(f32[8,128]{1,0:T(8,128)S(1)} %slice_add_fusion.26) | copy-start | bytes 12292
  179.5 6.5 %collective-permute-start.15 = (f32[384,128]{1,0:T(8,128)S(1)}, f32[384,128]{1,0:T(8,128)S(1)}, u32[]{:S(2)}, u32[]{:S(2)}) collective-permute-start(f32[384,128]{1,0:T(8,128)S(1)} %slice_add_fusion.15.refs_3_), channel_id=1, source_target_pairs={{0,8},{1,5},{2,10},{3,7},{4,12},{5,1},{6,14},{7,3},{8,0},{9,13},{1... | collective-permute-start | bytes 589832 | tf_op jit(solution)/shard_map/ppermute | solution.py:322
  182.2 8.8 %collective-permute-start.17 = (f32[392,128]{1,0:T(8,128)S(1)}, f32[392,128]{1,0:T(8,128)S(1)}, u32[]{:S(2)}, u32[]{:S(2)}) collective-permute-start(f32[392,128]{1,0:T(8,128)S(1)} %pad_maximum_fusion.13), channel_id=1, source_target_pairs={{0,16},{1,17},{2,18},{3,19},{4,20},{5,21},{6,22},{7,23},{8,24},{9,... | collective-permute-start | bytes 602120 | tf_op jit(solution)/shard_map/ppermute | solution.py:322
  186.1 7.8 %collective-permute-start.16 = (f32[768,128]{1,0:T(8,128)S(1)}, f32[768,128]{1,0:T(8,128)S(1)}, u32[]{:S(2)}, u32[]{:S(2)}) collective-permute-start(f32[768,128]{1,0:T(8,128)S(1)} %pad_maximum_fusion.2), channel_id=1, source_target_pairs={{0,4},{1,9},{2,6},{3,11},{4,0},{5,13},{6,2},{7,15},{8,12},{9,1},{1... | collective-permute-start | bytes 1179656 | tf_op jit(solution)/shard_map/ppermute | solution.py:322
  187.3 24.3 %copy-start.20 = (f32[8,128]{1,0:T(8,128)}, f32[8,128]{1,0:T(8,128)S(1)}, u32[]{:S(2)}) copy-start(f32[8,128]{1,0:T(8,128)S(1)} %slice_add_fusion.25.refs_4_.refs_6_) | copy-start | bytes 12292
  191.1 13.8 %copy-start.33 = (f32[8,128]{1,0:T(8,128)S(1)}, f32[8,128]{1,0:T(8,128)}, u32[]{:S(2)}) copy-start(f32[8,128]{1,0:T(8,128)} %copy-done.32) | copy-start | bytes 12292
  191.1 11.8 %collective-permute-start.18 = (f32[384,128]{1,0:T(8,128)S(1)}, f32[384,128]{1,0:T(8,128)S(1)}, u32[]{:S(2)}, u32[]{:S(2)}) collective-permute-start(f32[384,128]{1,0:T(8,128)S(1)} %slice_add_fusion.14.refs_3_), channel_id=1, source_target_pairs={{0,8},{1,5},{2,10},{3,7},{4,12},{5,1},{6,14},{7,3},{8,0},{9,13},{1... | collective-permute-start | bytes 589832 | tf_op jit(solution)/shard_map/ppermute | solution.py:322
  193.9 4.6 %copy-start.4 = (bf16[2048,3072]{1,0:T(8,128)(2,1)S(1)}, bf16[2048,3072]{1,0:T(8,128)(2,1)}, u32[]{:S(2)}) copy-start(bf16[2048,3072]{1,0:T(8,128)(2,1)} %copy-done) | copy-start | bytes 37748740
  203.6 8.0 %collective-permute-start.19 = (f32[768,128]{1,0:T(8,128)}, f32[768,128]{1,0:T(8,128)S(1)}, u32[]{:S(2)}, u32[]{:S(2)}) collective-permute-start(f32[768,128]{1,0:T(8,128)} %pad_maximum_fusion.3), channel_id=1, source_target_pairs={{0,4},{1,9},{2,6},{3,11},{4,0},{5,13},{6,2},{7,15},{8,12},{9,1},{1... | collective-permute-start | bytes 1179656 | tf_op jit(solution)/shard_map/ppermute | solution.py:322
  205.5 83.9 %all-reduce.11.cloned.1.call-start = ((), (), s32[]{:S(2)}) async-start(), calls=%async_computation.3 | async-start | bytes 1056768 | tf_op jit(solution)/shard_map/psum | solution.py:352
  212.4 4.6 %copy-start.5 = (bf16[2048,3072]{1,0:T(8,128)(2,1)S(1)}, bf16[2048,3072]{1,0:T(8,128)(2,1)}, u32[]{:S(2)}) copy-start(bf16[2048,3072]{1,0:T(8,128)(2,1)} %copy-done) | copy-start | bytes 37748740
  245.1 10.4 %copy-start.25 = (f32[8,128]{1,0:T(8,128)}, f32[8,128]{1,0:T(8,128)S(1)}, u32[]{:S(2)}) copy-start(f32[8,128]{1,0:T(8,128)S(1)} %slice.215.refs_2_.refs_5_.refs_7_) | copy-start | bytes 12292
  245.1 4.6 %copy-start.6 = (bf16[2048,3072]{1,0:T(8,128)(2,1)S(1)}, bf16[2048,3072]{1,0:T(8,128)(2,1)}, u32[]{:S(2)}) copy-start(bf16[2048,3072]{1,0:T(8,128)(2,1)} %copy-done) | copy-start | bytes 37748740
  255.4 8.1 %collective-permute-start.20 = (f32[776,128]{1,0:T(8,128)}, f32[776,128]{1,0:T(8,128)}, u32[]{:S(2)}, u32[]{:S(2)}) collective-permute-start(f32[776,128]{1,0:T(8,128)} %get-tuple-element.108), channel_id=1, source_target_pairs={{0,4},{1,9},{2,6},{3,11},{4,0},{5,13},{6,2},{7,15},{8,12},{9,1},{1... | collective-permute-start | bytes 1191944 | tf_op jit(solution)/shard_map/ppermute | solution.py:322
  266.8 34.7 %collective-permute-start.21 = (f32[392,128]{1,0:T(8,128)}, f32[392,128]{1,0:T(8,128)S(1)}, u32[]{:S(2)}, u32[]{:S(2)}) collective-permute-start(f32[392,128]{1,0:T(8,128)} %pad_maximum_fusion.14), channel_id=1, source_target_pairs={{0,8},{1,5},{2,10},{3,7},{4,12},{5,1},{6,14},{7,3},{8,0},{9,13},{1... | collective-permute-start | bytes 602120 | tf_op jit(solution)/shard_map/ppermute | solution.py:322
  290.1 4.6 %copy-start.7 = (bf16[2048,3072]{1,0:T(8,128)(2,1)S(1)}, bf16[2048,3072]{1,0:T(8,128)(2,1)}, u32[]{:S(2)}) copy-start(bf16[2048,3072]{1,0:T(8,128)(2,1)} %copy-done) | copy-start | bytes 37748740
  297.4 4.8 %copy-start.28 = (f32[768,128]{1,0:T(8,128)S(1)}, f32[768,128]{1,0:T(8,128)}, u32[]{:S(2)}) copy-start(f32[768,128]{1,0:T(8,128)} %copy-done.27) | copy-start | bytes 1179652
  297.4 43.0 %copy-start.22 = (f32[8,128]{1,0:T(8,128)S(1)}, f32[8,128]{1,0:T(8,128)}, u32[]{:S(2)}) copy-start(f32[8,128]{1,0:T(8,128)} %copy-done.20) | copy-start | bytes 12292
  297.5 43.0 %copy-start.26 = (f32[8,128]{1,0:T(8,128)S(1)}, f32[8,128]{1,0:T(8,128)}, u32[]{:S(2)}) copy-start(f32[8,128]{1,0:T(8,128)} %copy-done.25) | copy-start | bytes 12292
  300.0 7.9 %collective-permute-start.23 = (f32[776,128]{1,0:T(8,128)S(1)}, f32[776,128]{1,0:T(8,128)S(1)}, u32[]{:S(2)}, u32[]{:S(2)}) collective-permute-start(f32[776,128]{1,0:T(8,128)S(1)} %get-tuple-element.113), channel_id=1, source_target_pairs={{0,4},{1,9},{2,6},{3,11},{4,0},{5,13},{6,2},{7,15},{8,12},{9,1},{1... | collective-permute-start | bytes 1191944 | tf_op jit(solution)/shard_map/ppermute | solution.py:322
  308.0 7.2 %collective-permute-start.24 = (f32[392,128]{1,0:T(8,128)S(1)}, f32[392,128]{1,0:T(8,128)S(1)}, u32[]{:S(2)}, u32[]{:S(2)}) collective-permute-start(f32[392,128]{1,0:T(8,128)S(1)} %pad_maximum_fusion.16), channel_id=1, source_target_pairs={{0,8},{1,5},{2,10},{3,7},{4,12},{5,1},{6,14},{7,3},{8,0},{9,13},{1... | collective-permute-start | bytes 602120 | tf_op jit(solution)/shard_map/ppermute | solution.py:322
  309.5 10.3 %collective-permute-start.22 = (f32[392,128]{1,0:T(8,128)S(1)}, f32[392,128]{1,0:T(8,128)S(1)}, u32[]{:S(2)}, u32[]{:S(2)}) collective-permute-start(f32[392,128]{1,0:T(8,128)S(1)} %pad_maximum_fusion.15), channel_id=1, source_target_pairs={{0,16},{1,17},{2,18},{3,19},{4,20},{5,21},{6,22},{7,23},{8,24},{9,... | collective-permute-start | bytes 602120 | tf_op jit(solution)/shard_map/ppermute | solution.py:322
  319.8 6.4 %collective-permute-start.26 = (f32[384,128]{1,0:T(8,128)S(1)}, f32[384,128]{1,0:T(8,128)S(1)}, u32[]{:S(2)}, u32[]{:S(2)}) collective-permute-start(f32[384,128]{1,0:T(8,128)S(1)} %slice_add_fusion.13.refs_2_), channel_id=1, source_target_pairs={{0,8},{1,5},{2,10},{3,7},{4,12},{5,1},{6,14},{7,3},{8,0},{9,13},{1... | collective-permute-start | bytes 589832 | tf_op jit(solution)/shard_map/ppermute | solution.py:322
  322.5 9.7 %collective-permute-start.25 = (f32[392,128]{1,0:T(8,128)S(1)}, f32[392,128]{1,0:T(8,128)S(1)}, u32[]{:S(2)}, u32[]{:S(2)}) collective-permute-start(f32[392,128]{1,0:T(8,128)S(1)} %pad_maximum_fusion.17), channel_id=1, source_target_pairs={{0,16},{1,17},{2,18},{3,19},{4,20},{5,21},{6,22},{7,23},{8,24},{9,... | collective-permute-start | bytes 602120 | tf_op jit(solution)/shard_map/ppermute | solution.py:322
  332.3 7.9 %collective-permute-start.28 = (f32[384,128]{1,0:T(8,128)S(1)}, f32[384,128]{1,0:T(8,128)S(1)}, u32[]{:S(2)}, u32[]{:S(2)}) collective-permute-start(f32[384,128]{1,0:T(8,128)S(1)} %slice_add_fusion.12.refs_11_), channel_id=1, source_target_pairs={{0,8},{1,5},{2,10},{3,7},{4,12},{5,1},{6,14},{7,3},{8,0},{9,13},{1... | collective-permute-start | bytes 589832 | tf_op jit(solution)/shard_map/ppermute | solution.py:322
  332.7 9.9 %collective-permute-start.27 = (f32[768,128]{1,0:T(8,128)S(1)}, f32[768,128]{1,0:T(8,128)S(1)}, u32[]{:S(2)}, u32[]{:S(2)}) collective-permute-start(f32[768,128]{1,0:T(8,128)S(1)} %pad_maximum_fusion.4), channel_id=1, source_target_pairs={{0,4},{1,9},{2,6},{3,11},{4,0},{5,13},{6,2},{7,15},{8,12},{9,1},{1... | collective-permute-start | bytes 1179656 | tf_op jit(solution)/shard_map/ppermute | solution.py:322
  340.2 7.8 %collective-permute-start.29 = (f32[768,128]{1,0:T(8,128)S(1)}, f32[768,128]{1,0:T(8,128)S(1)}, u32[]{:S(2)}, u32[]{:S(2)}) collective-permute-start(f32[768,128]{1,0:T(8,128)S(1)} %pad_maximum_fusion.5), channel_id=1, source_target_pairs={{0,4},{1,9},{2,6},{3,11},{4,0},{5,13},{6,2},{7,15},{8,12},{9,1},{1... | collective-permute-start | bytes 1179656 | tf_op jit(solution)/shard_map/ppermute | solution.py:322
  (20 other events, 24.5 us)
Sparse Core Ops, SparseCore 0:
  72.9 34.2 all-reduce.4
  118.4 32.4 all-reduce.6
  205.6 38.7 all-reduce.8
  257.1 32.3 all-reduce.10

commit v9 on v7

--- a/solution.py
+++ b/solution.py
@@ -13,7 +13,7 @@
 PAIR = 2 * TILE
 UNITS = 4
 NORM_ROWS = 8
-BEHIND = 0
+BEHIND = 1
 
 tiny_eps = 1e-06
 

time: 195 us -> 201 us (1.031)
  waiting for transfers between devices: 98.7 us -> 137 us
  starting transfers between devices: 56.5 us -> 23.6 us
    ppermute x30, waiting for transfers between devices: 91.5 us -> 133 us  [swap_rows(): return lax.ppermute(value, ('rows', 'cols'), pairs)]
    ppermute x30, starting transfers between devices: 50 us -> 22 us  [swap_rows(): return lax.ppermute(value, ('rows', 'cols'), pairs)]
    ppermute x12, starting transfers between devices: 6.48 us -> 1.56 us  [swap_cols(): lax.ppermute(value, 'cols', [(i, i ^ 1 << level) for i in range(col_count)])]
    ppermute x12, waiting for transfers between devices: 7.24 us -> 4.42 us  [swap_cols(): lax.ppermute(value, 'cols', [(i, i ^ 1 << level) for i in range(col_count)])]
  transfers between devices with their start and end apart: 42 -> 42, of which waited for: 30 -> 28; matrix products, arithmetic and copies ran while one was open for 1% -> 1% of each run, Pallas kernels for 15% -> 14%
where the time goes in v9:
time: 201 us; the launch traced here: 202 us
  waiting for transfers between devices  137 us (68%)
  Pallas kernels  38.4 us (19%)
  starting transfers between devices  23.6 us (12%)
    ppermute x30, waiting for transfers between devices, swap_rows(): return lax.ppermute(value, ('rows', 'cols'), pairs)  133 us
    pallas_call x10, Pallas kernels, product_call(): pl.pallas_call(body, in_specs=[WHOLE] * (1 + len(operands)), out_specs=[W...  29.6 us
    ppermute x30, starting transfers between devices, swap_rows(): return lax.ppermute(value, ('rows', 'cols'), pairs)  22 us
    pallas_call x1, Pallas kernels, fill_dense(): pl.pallas_call(fill_kernel, in_specs=[SCALARS] * 2 + [pl.BlockSpec(memory...  5.31 us
    ppermute x12, waiting for transfers between devices, swap_cols(): lax.ppermute(value, 'cols', [(i, i ^ 1 << level) for i in range(col_count)])  4.42 us
  transfers between devices with their start and end apart: 42, of which 28 were waited for; matrix products, arithmetic and copies ran while one was open for 1% of the time, Pallas kernels for 14%

profile of v9, /device:TPU:0, one launch (start us, length us, event | category | flops | bytes accessed | tf_op | source)
XLA Modules:
  0.0 202.3 jit_solution(2245114382300098435)
XLA Ops:
  0.7 5.3 %shard_map.67 = (bf16[2048,3072]{1,0:T(8,128)(2,1)S(1)}, f32[1024,128]{1,0:T(8,128)S(1)}, f32[1024,128]{1,0:T(8,128)S(1)}) custom-call(s32[24]{0:T(128)S(1)} %fusion.place_ref, s32[1]{0:T(128)} %bitcast.1.flip_ref, s32[16,16]{1,0:T(8,128)} %pattern_in.1, s32[16]{0:T(128)} %bitcast.5, f32[2048,128]{1,0:T(8,128)} %delays_in.1, bf16[16,16,128,128]{3,2,1,0:T(8,128)(2,1)} %tiles_in.1), custom_call_target="tpu_custom_call" | custom-call | bytes 8388608 | tf_op jit(solution)/shard_map/pallas_call | solution.py:87
  6.0 2.5 %shard_map.68 = (f32[776,128]{1,0:T(8,128)S(1)}, f32[768,128]{1,0:T(8,128)S(1)}) custom-call(bf16[2048,3072]{1,0:T(8,128)(2,1)S(1)} %get-tuple-element.77.refs_0_, f32[1024,128]{1,0:T(8,128)S(1)} %get-tuple-element.78.refs_1_.refs_4_), custom_call_target="tpu_custom_call" | custom-call | flops 3221225472 | bytes 12582912 | tf_op jit(solution)/shard_map/pallas_call | solution.py:214
  8.5 2.7 %collective-permute-start = (f32[776,128]{1,0:T(8,128)S(1)}, f32[776,128]{1,0:T(8,128)S(1)}, u32[]{:S(2)}, u32[]{:S(2)}) collective-permute-start(f32[776,128]{1,0:T(8,128)S(1)} %get-tuple-element.80), channel_id=1, source_target_pairs={{0,4},{1,9},{2,6},{3,11},{4,0},{5,13},{6,2},{7,15},{8,12},{9,1},{1... | collective-permute-start | bytes 1191944 | tf_op jit(solution)/shard_map/ppermute | solution.py:334
  11.2 5.8 %collective-permute-done = f32[776,128]{1,0:T(8,128)S(1)} collective-permute-done((f32[776,128]{1,0:T(8,128)S(1)}, f32[776,128]{1,0:T(8,128)S(1)}, u32[]{:S(2)}, u32[]{:S(2)}) %collective-permute-start) | collective-permute-done | bytes 397344 | tf_op jit(solution)/shard_map/ppermute | solution.py:334
  17.1 2.5 %collective-permute-start.1 = (f32[392,128]{1,0:T(8,128)S(1)}, f32[392,128]{1,0:T(8,128)S(1)}, u32[]{:S(2)}, u32[]{:S(2)}) collective-permute-start(f32[392,128]{1,0:T(8,128)S(1)} %pad_maximum_fusion.10), channel_id=1, source_target_pairs={{0,8},{1,5},{2,10},{3,7},{4,12},{5,1},{6,14},{7,3},{8,0},{9,13},{1... | collective-permute-start | bytes 602120 | tf_op jit(solution)/shard_map/ppermute | solution.py:334
  19.5 3.7 %collective-permute-done.1 = f32[392,128]{1,0:T(8,128)S(1)} collective-permute-done((f32[392,128]{1,0:T(8,128)S(1)}, f32[392,128]{1,0:T(8,128)S(1)}, u32[]{:S(2)}, u32[]{:S(2)}) %collective-permute-start.1) | collective-permute-done | bytes 200736 | tf_op jit(solution)/shard_map/ppermute | solution.py:334
  23.3 3.5 %collective-permute-start.2 = (f32[392,128]{1,0:T(8,128)S(1)}, f32[392,128]{1,0:T(8,128)S(1)}, u32[]{:S(2)}, u32[]{:S(2)}) collective-permute-start(f32[392,128]{1,0:T(8,128)S(1)} %pad_maximum_fusion.11), channel_id=1, source_target_pairs={{0,16},{1,17},{2,18},{3,19},{4,20},{5,21},{6,22},{7,23},{8,24},{9,... | collective-permute-start | bytes 602120 | tf_op jit(solution)/shard_map/ppermute | solution.py:334
  26.8 2.5 %shard_map.69 = (f32[776,128]{1,0:T(8,128)S(1)}, f32[768,128]{1,0:T(8,128)S(1)}) custom-call(bf16[2048,3072]{1,0:T(8,128)(2,1)S(1)} %get-tuple-element.77.refs_0_, f32[1024,128]{1,0:T(8,128)S(1)} %get-tuple-element.83.refs_1_.refs_4_), custom_call_target="tpu_custom_call" | custom-call | flops 3221225472 | bytes 12582912 | tf_op jit(solution)/shard_map/pallas_call | solution.py:214
  29.8 3.9 %collective-permute-done.2 = f32[392,128]{1,0:T(8,128)S(1)} collective-permute-done((f32[392,128]{1,0:T(8,128)S(1)}, f32[392,128]{1,0:T(8,128)S(1)}, u32[]{:S(2)}, u32[]{:S(2)}) %collective-permute-start.2) | collective-permute-done | bytes 200736 | tf_op jit(solution)/shard_map/ppermute | solution.py:334
  34.6 5.2 %collective-permute-done.4 = f32[776,128]{1,0:T(8,128)S(1)} collective-permute-done((f32[776,128]{1,0:T(8,128)S(1)}, f32[776,128]{1,0:T(8,128)S(1)}, u32[]{:S(2)}, u32[]{:S(2)}) %collective-permute-start.4) | collective-permute-done | bytes 397344 | tf_op jit(solution)/shard_map/ppermute | solution.py:334
  40.9 9.1 %collective-permute-done.6 = f32[392,128]{1,0:T(8,128)S(1)} collective-permute-done((f32[392,128]{1,0:T(8,128)S(1)}, f32[392,128]{1,0:T(8,128)S(1)}, u32[]{:S(2)}, u32[]{:S(2)}) %collective-permute-start.6) | collective-permute-done | bytes 200736 | tf_op jit(solution)/shard_map/ppermute | solution.py:334
  50.1 3.5 %shard_map.70 = (f32[520,128]{1,0:T(8,128)S(1)}, f32[512,128]{1,0:T(8,128)S(1)}, f32[1536,128]{1,0:T(8,128)S(1)}) custom-call(bf16[2048,3072]{1,0:T(8,128)(2,1)S(1)} %get-tuple-element.77.refs_0_, f32[768,128]{1,0:T(8,128)S(1)} %collective-permute-done.5.refs_1_, f32[384,128]{1,0:T(8,128)S(1)} %collective-permute-done.3.refs_2_, ...), custom_call_target="tpu_custom_call" | custom-call | flops 3221225472 | bytes 12582912 | tf_op jit(solution)/shard_map/pallas_call | solution.py:214
  53.7 4.1 %collective-permute-done.8 = f32[392,128]{1,0:T(8,128)S(1)} collective-permute-done((f32[392,128]{1,0:T(8,128)S(1)}, f32[392,128]{1,0:T(8,128)S(1)}, u32[]{:S(2)}, u32[]{:S(2)}) %collective-permute-start.8) | collective-permute-done | bytes 200736 | tf_op jit(solution)/shard_map/ppermute | solution.py:334
  58.2 7.5 %collective-permute-done.10.refs_2_ = f32[384,128]{1,0:T(8,128)S(1)} collective-permute-done((f32[384,128]{1,0:T(8,128)S(1)}, f32[384,128]{1,0:T(8,128)S(1)}, u32[]{:S(2)}, u32[]{:S(2)}) %collective-permute-start.10) | collective-permute-done | bytes 196640 | tf_op jit(solution)/shard_map/ppermute | solution.py:334
  66.0 7.6 %collective-permute-done.12.refs_1_ = f32[768,128]{1,0:T(8,128)S(1)} collective-permute-done((f32[768,128]{1,0:T(8,128)S(1)}, f32[768,128]{1,0:T(8,128)S(1)}, u32[]{:S(2)}, u32[]{:S(2)}) %collective-permute-start.12) | collective-permute-done | bytes 393248 | tf_op jit(solution)/shard_map/ppermute | solution.py:334
  73.6 3.5 %shard_map.71 = (f32[520,128]{1,0:T(8,128)S(1)}, f32[512,128]{1,0:T(8,128)S(1)}, f32[1536,128]{1,0:T(8,128)S(1)}) custom-call(bf16[2048,3072]{1,0:T(8,128)(2,1)S(1)} %get-tuple-element.77.refs_0_, f32[768,128]{1,0:T(8,128)S(1)} %collective-permute-done.12.refs_1_, f32[384,128]{1,0:T(8,128)S(1)} %collective-permute-done.10.refs_2_, ...), custom_call_target="tpu_custom_call" | custom-call | flops 3221225472 | bytes 12582912 | tf_op jit(solution)/shard_map/pallas_call | solution.py:214
  77.2 2.7 %shard_map.72 = (f32[776,128]{1,0:T(8,128)S(1)}, f32[768,128]{1,0:T(8,128)S(1)}, f32[1024,128]{1,0:T(8,128)S(1)}) custom-call(bf16[2048,3072]{1,0:T(8,128)(2,1)S(1)} %get-tuple-element.77.refs_0_, f32[512,128]{1,0:T(8,128)S(1)} %collective-permute-done.11.refs_1_, f32[512,128]{1,0:T(8,128)S(1)} %slice_add_fusion.12.refs_2_, ...), custom_call_target="tpu_custom_call" | custom-call | flops 3221225472 | bytes 12582912 | tf_op jit(solution)/shard_map/pallas_call | solution.py:214
  80.2 7.6 %collective-permute-done.13 = f32[776,128]{1,0:T(8,128)S(1)} collective-permute-done((f32[776,128]{1,0:T(8,128)S(1)}, f32[776,128]{1,0:T(8,128)S(1)}, u32[]{:S(2)}, u32[]{:S(2)}) %collective-permute-start.13) | collective-permute-done | bytes 397344 | tf_op jit(solution)/shard_map/ppermute | solution.py:334
  88.0 1.0 collective-permute-done.16
  89.1 4.6 %collective-permute-done.15 = f32[392,128]{1,0:T(8,128)S(1)} collective-permute-done((f32[392,128]{1,0:T(8,128)S(1)}, f32[392,128]{1,0:T(8,128)S(1)}, u32[]{:S(2)}, u32[]{:S(2)}) %collective-permute-start.15) | collective-permute-done | bytes 200736 | tf_op jit(solution)/shard_map/ppermute | solution.py:334
  93.8 2.5 %shard_map.73 = (f32[776,128]{1,0:T(8,128)S(1)}, f32[768,128]{1,0:T(8,128)S(1)}, f32[1024,128]{1,0:T(8,128)S(1)}) custom-call(bf16[2048,3072]{1,0:T(8,128)(2,1)S(1)} %get-tuple-element.77.refs_0_, f32[512,128]{1,0:T(8,128)S(1)} %collective-permute-done.18.refs_1_, f32[512,128]{1,0:T(8,128)S(1)} %slice_add_fusion.10.refs_2_, ...), custom_call_target="tpu_custom_call" | custom-call | flops 3221225472 | bytes 12582912 | tf_op jit(solution)/shard_map/pallas_call | solution.py:214
  96.5 8.0 %collective-permute-done.17 = f32[392,128]{1,0:T(8,128)S(1)} collective-permute-done((f32[392,128]{1,0:T(8,128)S(1)}, f32[392,128]{1,0:T(8,128)S(1)}, u32[]{:S(2)}, u32[]{:S(2)}) %collective-permute-start.17) | collective-permute-done | bytes 200736 | tf_op jit(solution)/shard_map/ppermute | solution.py:334
  104.7 2.1 %collective-permute-start.22 = (f32[392,128]{1,0:T(8,128)S(1)}, f32[392,128]{1,0:T(8,128)S(1)}, u32[]{:S(2)}, u32[]{:S(2)}) collective-permute-start(f32[392,128]{1,0:T(8,128)S(1)} %pad_maximum_fusion.16), channel_id=1, source_target_pairs={{0,8},{1,5},{2,10},{3,7},{4,12},{5,1},{6,14},{7,3},{8,0},{9,13},{1... | collective-permute-start | bytes 602120 | tf_op jit(solution)/shard_map/ppermute | solution.py:334
  106.8 3.5 %collective-permute-done.19.refs_2_ = f32[384,128]{1,0:T(8,128)S(1)} collective-permute-done((f32[384,128]{1,0:T(8,128)S(1)}, f32[384,128]{1,0:T(8,128)S(1)}, u32[]{:S(2)}, u32[]{:S(2)}) %collective-permute-start.19) | collective-permute-done | bytes 196640 | tf_op jit(solution)/shard_map/ppermute | solution.py:334
  110.6 2.1 %collective-permute-done.22 = f32[392,128]{1,0:T(8,128)S(1)} collective-permute-done((f32[392,128]{1,0:T(8,128)S(1)}, f32[392,128]{1,0:T(8,128)S(1)}, u32[]{:S(2)}, u32[]{:S(2)}) %collective-permute-start.22) | collective-permute-done | bytes 200736 | tf_op jit(solution)/shard_map/ppermute | solution.py:334
  112.7 2.3 %collective-permute-start.24 = (f32[392,128]{1,0:T(8,128)S(1)}, f32[392,128]{1,0:T(8,128)S(1)}, u32[]{:S(2)}, u32[]{:S(2)}) collective-permute-start(f32[392,128]{1,0:T(8,128)S(1)} %pad_maximum_fusion.17), channel_id=1, source_target_pairs={{0,16},{1,17},{2,18},{3,19},{4,20},{5,21},{6,22},{7,23},{8,24},{9,... | collective-permute-start | bytes 602120 | tf_op jit(solution)/shard_map/ppermute | solution.py:334
  115.0 3.1 %collective-permute-done.21.refs_1_ = f32[768,128]{1,0:T(8,128)S(1)} collective-permute-done((f32[768,128]{1,0:T(8,128)S(1)}, f32[768,128]{1,0:T(8,128)S(1)}, u32[]{:S(2)}, u32[]{:S(2)}) %collective-permute-start.21) | collective-permute-done | bytes 393248 | tf_op jit(solution)/shard_map/ppermute | solution.py:334
  118.1 3.5 %shard_map.74 = (f32[520,128]{1,0:T(8,128)S(1)}, f32[512,128]{1,0:T(8,128)S(1)}, f32[1536,128]{1,0:T(8,128)S(1)}) custom-call(bf16[2048,3072]{1,0:T(8,128)(2,1)S(1)} %get-tuple-element.77.refs_0_, f32[768,128]{1,0:T(8,128)S(1)} %collective-permute-done.21.refs_1_, f32[384,128]{1,0:T(8,128)S(1)} %collective-permute-done.19.refs_2_, ...), custom_call_target="tpu_custom_call" | custom-call | flops 3221225472 | bytes 12582912 | tf_op jit(solution)/shard_map/pallas_call | solution.py:214
  122.4 1.3 collective-permute-done.24
  124.0 5.5 %collective-permute-done.26.refs_2_ = f32[384,128]{1,0:T(8,128)S(1)} collective-permute-done((f32[384,128]{1,0:T(8,128)S(1)}, f32[384,128]{1,0:T(8,128)S(1)}, u32[]{:S(2)}, u32[]{:S(2)}) %collective-permute-start.26) | collective-permute-done | bytes 196640 | tf_op jit(solution)/shard_map/ppermute | solution.py:334
  129.9 2.5 %collective-permute-done.25 = f32[520,128]{1,0:T(8,128)S(1)} collective-permute-done((f32[520,128]{1,0:T(8,128)S(1)}, f32[520,128]{1,0:T(8,128)S(1)}, u32[]{:S(2)}, u32[]{:S(2)}) %collective-permute-start.25) | collective-permute-done | bytes 266272 | tf_op jit(solution)/shard_map/ppermute | solution.py:337
  132.5 4.9 %collective-permute-done.28.refs_1_ = f32[768,128]{1,0:T(8,128)S(1)} collective-permute-done((f32[768,128]{1,0:T(8,128)S(1)}, f32[768,128]{1,0:T(8,128)S(1)}, u32[]{:S(2)}, u32[]{:S(2)}) %collective-permute-start.28) | collective-permute-done | bytes 393248 | tf_op jit(solution)/shard_map/ppermute | solution.py:334
  137.4 3.5 %shard_map.75 = (f32[520,128]{1,0:T(8,128)S(1)}, f32[512,128]{1,0:T(8,128)S(1)}, f32[1536,128]{1,0:T(8,128)S(1)}) custom-call(bf16[2048,3072]{1,0:T(8,128)(2,1)S(1)} %get-tuple-element.77.refs_0_, f32[768,128]{1,0:T(8,128)S(1)} %collective-permute-done.28.refs_1_, f32[384,128]{1,0:T(8,128)S(1)} %collective-permute-done.26.refs_2_, ...), custom_call_target="tpu_custom_call" | custom-call | flops 3221225472 | bytes 12582912 | tf_op jit(solution)/shard_map/pallas_call | solution.py:214
  141.0 2.5 %shard_map.76 = (f32[776,128]{1,0:T(8,128)S(1)}, f32[768,128]{1,0:T(8,128)S(1)}, f32[1024,128]{1,0:T(8,128)}) custom-call(bf16[2048,3072]{1,0:T(8,128)(2,1)S(1)} %get-tuple-element.77.refs_0_, f32[512,128]{1,0:T(8,128)S(1)} %collective-permute-done.27.refs_1_, f32[512,128]{1,0:T(8,128)S(1)} %slice_add_fusion.8.refs_2_, ...), custom_call_target="tpu_custom_call" | custom-call | flops 3221225472 | bytes 12582912 | tf_op jit(solution)/shard_map/pallas_call | solution.py:214
  144.1 7.4 %collective-permute-done.29 = f32[776,128]{1,0:T(8,128)S(1)} collective-permute-done((f32[776,128]{1,0:T(8,128)S(1)}, f32[776,128]{1,0:T(8,128)S(1)}, u32[]{:S(2)}, u32[]{:S(2)}) %collective-permute-start.29) | collective-permute-done | bytes 397344 | tf_op jit(solution)/shard_map/ppermute | solution.py:334
  151.7 0.9 collective-permute-done.32
  152.7 4.6 %collective-permute-done.31 = f32[392,128]{1,0:T(8,128)S(1)} collective-permute-done((f32[392,128]{1,0:T(8,128)S(1)}, f32[392,128]{1,0:T(8,128)S(1)}, u32[]{:S(2)}, u32[]{:S(2)}) %collective-permute-start.31) | collective-permute-done | bytes 200736 | tf_op jit(solution)/shard_map/ppermute | solution.py:334
  157.5 2.7 %shard_map.77 = (f32[776,128]{1,0:T(8,128)S(1)}, f32[768,128]{1,0:T(8,128)S(1)}, f32[1024,128]{1,0:T(8,128)}) custom-call(bf16[2048,3072]{1,0:T(8,128)(2,1)S(1)} %get-tuple-element.77.refs_0_, f32[512,128]{1,0:T(8,128)S(1)} %collective-permute-done.34.refs_1_, f32[512,128]{1,0:T(8,128)S(1)} %slice_add_fusion.6.refs_2_, ...), custom_call_target="tpu_custom_call" | custom-call | flops 3221225472 | bytes 12582912 | tf_op jit(solution)/shard_map/pallas_call | solution.py:214
  160.6 7.6 %collective-permute-done.33 = f32[392,128]{1,0:T(8,128)S(1)} collective-permute-done((f32[392,128]{1,0:T(8,128)S(1)}, f32[392,128]{1,0:T(8,128)S(1)}, u32[]{:S(2)}, u32[]{:S(2)}) %collective-permute-start.33) | collective-permute-done | bytes 200736 | tf_op jit(solution)/shard_map/ppermute | solution.py:334
  168.4 2.2 %collective-permute-start.36 = (f32[392,128]{1,0:T(8,128)S(1)}, f32[392,128]{1,0:T(8,128)S(1)}, u32[]{:S(2)}, u32[]{:S(2)}) collective-permute-start(f32[392,128]{1,0:T(8,128)S(1)} %pad_maximum_fusion.20), channel_id=1, source_target_pairs={{0,8},{1,5},{2,10},{3,7},{4,12},{5,1},{6,14},{7,3},{8,0},{9,13},{1... | collective-permute-start | bytes 602120 | tf_op jit(solution)/shard_map/ppermute | solution.py:334
  170.6 3.3 %collective-permute-done.37.refs_1_ = f32[384,128]{1,0:T(8,128)S(1)} collective-permute-done((f32[384,128]{1,0:T(8,128)S(1)}, f32[384,128]{1,0:T(8,128)S(1)}, u32[]{:S(2)}, u32[]{:S(2)}) %collective-permute-start.37) | collective-permute-done | bytes 196640 | tf_op jit(solution)/shard_map/ppermute | solution.py:334
  174.0 2.1 %collective-permute-done.36 = f32[392,128]{1,0:T(8,128)S(1)} collective-permute-done((f32[392,128]{1,0:T(8,128)S(1)}, f32[392,128]{1,0:T(8,128)S(1)}, u32[]{:S(2)}, u32[]{:S(2)}) %collective-permute-start.36) | collective-permute-done | bytes 200736 | tf_op jit(solution)/shard_map/ppermute | solution.py:334
  176.2 1.5 collective-permute-start.38
  177.9 9.1 %collective-permute-done.38 = f32[392,128]{1,0:T(8,128)S(1)} collective-permute-done((f32[392,128]{1,0:T(8,128)S(1)}, f32[392,128]{1,0:T(8,128)S(1)}, u32[]{:S(2)}, u32[]{:S(2)}) %collective-permute-start.38) | collective-permute-done | bytes 200736 | tf_op jit(solution)/shard_map/ppermute | solution.py:334
  187.2 5.6 %collective-permute-done.40.refs_10_ = f32[384,128]{1,0:T(8,128)S(1)} collective-permute-done((f32[384,128]{1,0:T(8,128)S(1)}, f32[384,128]{1,0:T(8,128)S(1)}, u32[]{:S(2)}, u32[]{:S(2)}) %collective-permute-start.40) | collective-permute-done | bytes 196640 | tf_op jit(solution)/shard_map/ppermute | solution.py:334
  193.2 1.7 shard_map.78
  195.4 5.3 %collective-permute-done.41.refs_9_ = f32[768,128]{1,0:T(8,128)S(1)} collective-permute-done((f32[768,128]{1,0:T(8,128)S(1)}, f32[768,128]{1,0:T(8,128)S(1)}, u32[]{:S(2)}, u32[]{:S(2)}) %collective-permute-start.41) | collective-permute-done | bytes 393248 | tf_op jit(solution)/shard_map/ppermute | solution.py:334
  200.7 1.7 shard_map.79
  (131 shorter events, 8.9 us)
Async XLA Ops:
  8.5 8.5 %collective-permute-start = (f32[776,128]{1,0:T(8,128)S(1)}, f32[776,128]{1,0:T(8,128)S(1)}, u32[]{:S(2)}, u32[]{:S(2)}) collective-permute-start(f32[776,128]{1,0:T(8,128)S(1)} %get-tuple-element.80), channel_id=1, source_target_pairs={{0,4},{1,9},{2,6},{3,11},{4,0},{5,13},{6,2},{7,15},{8,12},{9,1},{1... | collective-permute-start | bytes 1191944 | tf_op jit(solution)/shard_map/ppermute | solution.py:334
  17.1 6.2 %collective-permute-start.1 = (f32[392,128]{1,0:T(8,128)S(1)}, f32[392,128]{1,0:T(8,128)S(1)}, u32[]{:S(2)}, u32[]{:S(2)}) collective-permute-start(f32[392,128]{1,0:T(8,128)S(1)} %pad_maximum_fusion.10), channel_id=1, source_target_pairs={{0,8},{1,5},{2,10},{3,7},{4,12},{5,1},{6,14},{7,3},{8,0},{9,13},{1... | collective-permute-start | bytes 602120 | tf_op jit(solution)/shard_map/ppermute | solution.py:334
  23.3 10.5 %collective-permute-start.2 = (f32[392,128]{1,0:T(8,128)S(1)}, f32[392,128]{1,0:T(8,128)S(1)}, u32[]{:S(2)}, u32[]{:S(2)}) collective-permute-start(f32[392,128]{1,0:T(8,128)S(1)} %pad_maximum_fusion.11), channel_id=1, source_target_pairs={{0,16},{1,17},{2,18},{3,19},{4,20},{5,21},{6,22},{7,23},{8,24},{9,... | collective-permute-start | bytes 602120 | tf_op jit(solution)/shard_map/ppermute | solution.py:334
  29.3 10.5 %collective-permute-start.4 = (f32[776,128]{1,0:T(8,128)S(1)}, f32[776,128]{1,0:T(8,128)S(1)}, u32[]{:S(2)}, u32[]{:S(2)}) collective-permute-start(f32[776,128]{1,0:T(8,128)S(1)} %get-tuple-element.85), channel_id=1, source_target_pairs={{0,4},{1,9},{2,6},{3,11},{4,0},{5,13},{6,2},{7,15},{8,12},{9,1},{1... | collective-permute-start | bytes 1191944 | tf_op jit(solution)/shard_map/ppermute | solution.py:334
  33.8 6.1 %collective-permute-start.3 = (f32[384,128]{1,0:T(8,128)S(1)}, f32[384,128]{1,0:T(8,128)S(1)}, u32[]{:S(2)}, u32[]{:S(2)}) collective-permute-start(f32[384,128]{1,0:T(8,128)S(1)} %slice_add_fusion.25.refs_3_), channel_id=1, source_target_pairs={{0,8},{1,5},{2,10},{3,7},{4,12},{5,1},{6,14},{7,3},{8,0},{9,13},{1... | collective-permute-start | bytes 589832 | tf_op jit(solution)/shard_map/ppermute | solution.py:334
  39.9 10.1 %collective-permute-start.6 = (f32[392,128]{1,0:T(8,128)S(1)}, f32[392,128]{1,0:T(8,128)S(1)}, u32[]{:S(2)}, u32[]{:S(2)}) collective-permute-start(f32[392,128]{1,0:T(8,128)S(1)} %pad_maximum_fusion.12), channel_id=1, source_target_pairs={{0,8},{1,5},{2,10},{3,7},{4,12},{5,1},{6,14},{7,3},{8,0},{9,13},{1... | collective-permute-start | bytes 602120 | tf_op jit(solution)/shard_map/ppermute | solution.py:334
  40.0 10.1 %collective-permute-start.5 = (f32[768,128]{1,0:T(8,128)S(1)}, f32[768,128]{1,0:T(8,128)S(1)}, u32[]{:S(2)}, u32[]{:S(2)}) collective-permute-start(f32[768,128]{1,0:T(8,128)S(1)} %pad_maximum_fusion), channel_id=1, source_target_pairs={{0,4},{1,9},{2,6},{3,11},{4,0},{5,13},{6,2},{7,15},{8,12},{9,1},{1... | collective-permute-start | bytes 1179656 | tf_op jit(solution)/shard_map/ppermute | solution.py:334
  50.1 7.8 %collective-permute-start.8 = (f32[392,128]{1,0:T(8,128)S(1)}, f32[392,128]{1,0:T(8,128)S(1)}, u32[]{:S(2)}, u32[]{:S(2)}) collective-permute-start(f32[392,128]{1,0:T(8,128)S(1)} %pad_maximum_fusion.13), channel_id=1, source_target_pairs={{0,16},{1,17},{2,18},{3,19},{4,20},{5,21},{6,22},{7,23},{8,24},{9,... | collective-permute-start | bytes 602120 | tf_op jit(solution)/shard_map/ppermute | solution.py:334
  53.7 4.3 %collective-permute-start.7 = (f32[520,128]{1,0:T(8,128)S(1)}, f32[520,128]{1,0:T(8,128)S(1)}, u32[]{:S(2)}, u32[]{:S(2)}) collective-permute-start(f32[520,128]{1,0:T(8,128)S(1)} %get-tuple-element.94), channel_id=1, source_target_pairs={{0,1},{1,0},{2,3},{3,2},{4,5},{5,4},{6,7},{7,6},{8,9},{9,8},{10,11... | collective-permute-start | bytes 798728 | tf_op jit(solution)/shard_map/ppermute | solution.py:337
  57.9 7.8 %collective-permute-start.10 = (f32[384,128]{1,0:T(8,128)S(1)}, f32[384,128]{1,0:T(8,128)S(1)}, u32[]{:S(2)}, u32[]{:S(2)}) collective-permute-start(f32[384,128]{1,0:T(8,128)S(1)} %slice_add_fusion.24.refs_3_), channel_id=1, source_target_pairs={{0,8},{1,5},{2,10},{3,7},{4,12},{5,1},{6,14},{7,3},{8,0},{9,13},{1... | collective-permute-start | bytes 589832 | tf_op jit(solution)/shard_map/ppermute | solution.py:334
  58.1 7.8 %collective-permute-start.9 = (f32[520,128]{1,0:T(8,128)S(1)}, f32[520,128]{1,0:T(8,128)S(1)}, u32[]{:S(2)}, u32[]{:S(2)}) collective-permute-start(f32[520,128]{1,0:T(8,128)S(1)} %pad_maximum_fusion.6), channel_id=1, source_target_pairs={{0,2},{1,3},{2,0},{3,1},{4,6},{5,7},{6,4},{7,5},{8,10},{9,11},{10,... | collective-permute-start | bytes 798728 | tf_op jit(solution)/shard_map/ppermute | solution.py:337
  65.7 7.8 %collective-permute-start.12 = (f32[768,128]{1,0:T(8,128)S(1)}, f32[768,128]{1,0:T(8,128)S(1)}, u32[]{:S(2)}, u32[]{:S(2)}) collective-permute-start(f32[768,128]{1,0:T(8,128)S(1)} %pad_maximum_fusion.1), channel_id=1, source_target_pairs={{0,4},{1,9},{2,6},{3,11},{4,0},{5,13},{6,2},{7,15},{8,12},{9,1},{1... | collective-permute-start | bytes 1179656 | tf_op jit(solution)/shard_map/ppermute | solution.py:334
  65.9 11.3 %collective-permute-start.11 = (f32[512,128]{1,0:T(8,128)S(1)}, f32[512,128]{1,0:T(8,128)S(1)}, u32[]{:S(2)}, u32[]{:S(2)}) collective-permute-start(f32[512,128]{1,0:T(8,128)S(1)} %slice_add_fusion.12.refs_2_), channel_id=1, source_target_pairs={{0,1},{1,0},{2,3},{3,2},{4,5},{5,4},{6,7},{7,6},{8,9},{9,8},{10,11... | collective-permute-start | bytes 786440 | tf_op jit(solution)/shard_map/ppermute | solution.py:337
  77.1 2.9 %collective-permute-start.14 = (f32[520,128]{1,0:T(8,128)S(1)}, f32[520,128]{1,0:T(8,128)S(1)}, u32[]{:S(2)}, u32[]{:S(2)}) collective-permute-start(f32[520,128]{1,0:T(8,128)S(1)} %get-tuple-element.100), channel_id=1, source_target_pairs={{0,1},{1,0},{2,3},{3,2},{4,5},{5,4},{6,7},{7,6},{8,9},{9,8},{10,11... | collective-permute-start | bytes 798728 | tf_op jit(solution)/shard_map/ppermute | solution.py:337
  79.9 7.9 %collective-permute-start.13 = (f32[776,128]{1,0:T(8,128)S(1)}, f32[776,128]{1,0:T(8,128)S(1)}, u32[]{:S(2)}, u32[]{:S(2)}) collective-permute-start(f32[776,128]{1,0:T(8,128)S(1)} %get-tuple-element.103), channel_id=1, source_target_pairs={{0,4},{1,9},{2,6},{3,11},{4,0},{5,13},{6,2},{7,15},{8,12},{9,1},{1... | collective-permute-start | bytes 1191944 | tf_op jit(solution)/shard_map/ppermute | solution.py:334
  80.1 8.8 %collective-permute-start.16 = (f32[520,128]{1,0:T(8,128)S(1)}, f32[520,128]{1,0:T(8,128)S(1)}, u32[]{:S(2)}, u32[]{:S(2)}) collective-permute-start(f32[520,128]{1,0:T(8,128)S(1)} %pad_maximum_fusion.7), channel_id=1, source_target_pairs={{0,2},{1,3},{2,0},{3,1},{4,6},{5,7},{6,4},{7,5},{8,10},{9,11},{10,... | collective-permute-start | bytes 798728 | tf_op jit(solution)/shard_map/ppermute | solution.py:337
  87.9 5.8 %collective-permute-start.15 = (f32[392,128]{1,0:T(8,128)S(1)}, f32[392,128]{1,0:T(8,128)S(1)}, u32[]{:S(2)}, u32[]{:S(2)}) collective-permute-start(f32[392,128]{1,0:T(8,128)S(1)} %pad_maximum_fusion.14), channel_id=1, source_target_pairs={{0,8},{1,5},{2,10},{3,7},{4,12},{5,1},{6,14},{7,3},{8,0},{9,13},{1... | collective-permute-start | bytes 602120 | tf_op jit(solution)/shard_map/ppermute | solution.py:334
  89.0 4.9 %collective-permute-start.18 = (f32[512,128]{1,0:T(8,128)S(1)}, f32[512,128]{1,0:T(8,128)S(1)}, u32[]{:S(2)}, u32[]{:S(2)}) collective-permute-start(f32[512,128]{1,0:T(8,128)S(1)} %slice_add_fusion.10.refs_2_), channel_id=1, source_target_pairs={{0,1},{1,0},{2,3},{3,2},{4,5},{5,4},{6,7},{7,6},{8,9},{9,8},{10,11... | collective-permute-start | bytes 786440 | tf_op jit(solution)/shard_map/ppermute | solution.py:337
  93.7 10.7 %collective-permute-start.17 = (f32[392,128]{1,0:T(8,128)S(1)}, f32[392,128]{1,0:T(8,128)S(1)}, u32[]{:S(2)}, u32[]{:S(2)}) collective-permute-start(f32[392,128]{1,0:T(8,128)S(1)} %pad_maximum_fusion.15), channel_id=1, source_target_pairs={{0,16},{1,17},{2,18},{3,19},{4,20},{5,21},{6,22},{7,23},{8,24},{9,... | collective-permute-start | bytes 602120 | tf_op jit(solution)/shard_map/ppermute | solution.py:334
  96.4 8.2 %collective-permute-start.20 = (f32[776,128]{1,0:T(8,128)S(1)}, f32[776,128]{1,0:T(8,128)S(1)}, u32[]{:S(2)}, u32[]{:S(2)}) collective-permute-start(f32[776,128]{1,0:T(8,128)S(1)} %get-tuple-element.110), channel_id=1, source_target_pairs={{0,4},{1,9},{2,6},{3,11},{4,0},{5,13},{6,2},{7,15},{8,12},{9,1},{1... | collective-permute-start | bytes 1191944 | tf_op jit(solution)/shard_map/ppermute | solution.py:334
  104.5 5.7 %collective-permute-start.19 = (f32[384,128]{1,0:T(8,128)S(1)}, f32[384,128]{1,0:T(8,128)S(1)}, u32[]{:S(2)}, u32[]{:S(2)}) collective-permute-start(f32[384,128]{1,0:T(8,128)S(1)} %slice_add_fusion.23.refs_3_), channel_id=1, source_target_pairs={{0,8},{1,5},{2,10},{3,7},{4,12},{5,1},{6,14},{7,3},{8,0},{9,13},{1... | collective-permute-start | bytes 589832 | tf_op jit(solution)/shard_map/ppermute | solution.py:334
  104.7 8.0 %collective-permute-start.22 = (f32[392,128]{1,0:T(8,128)S(1)}, f32[392,128]{1,0:T(8,128)S(1)}, u32[]{:S(2)}, u32[]{:S(2)}) collective-permute-start(f32[392,128]{1,0:T(8,128)S(1)} %pad_maximum_fusion.16), channel_id=1, source_target_pairs={{0,8},{1,5},{2,10},{3,7},{4,12},{5,1},{6,14},{7,3},{8,0},{9,13},{1... | collective-permute-start | bytes 602120 | tf_op jit(solution)/shard_map/ppermute | solution.py:334
  110.3 7.8 %collective-permute-start.21 = (f32[768,128]{1,0:T(8,128)S(1)}, f32[768,128]{1,0:T(8,128)S(1)}, u32[]{:S(2)}, u32[]{:S(2)}) collective-permute-start(f32[768,128]{1,0:T(8,128)S(1)} %pad_maximum_fusion.2), channel_id=1, source_target_pairs={{0,4},{1,9},{2,6},{3,11},{4,0},{5,13},{6,2},{7,15},{8,12},{9,1},{1... | collective-permute-start | bytes 1179656 | tf_op jit(solution)/shard_map/ppermute | solution.py:334
  112.7 11.0 %collective-permute-start.24 = (f32[392,128]{1,0:T(8,128)S(1)}, f32[392,128]{1,0:T(8,128)S(1)}, u32[]{:S(2)}, u32[]{:S(2)}) collective-permute-start(f32[392,128]{1,0:T(8,128)S(1)} %pad_maximum_fusion.17), channel_id=1, source_target_pairs={{0,16},{1,17},{2,18},{3,19},{4,20},{5,21},{6,22},{7,23},{8,24},{9,... | collective-permute-start | bytes 602120 | tf_op jit(solution)/shard_map/ppermute | solution.py:334
  121.7 2.2 %collective-permute-start.23 = (f32[520,128]{1,0:T(8,128)S(1)}, f32[520,128]{1,0:T(8,128)S(1)}, u32[]{:S(2)}, u32[]{:S(2)}) collective-permute-start(f32[520,128]{1,0:T(8,128)S(1)} %get-tuple-element.118), channel_id=1, source_target_pairs={{0,1},{1,0},{2,3},{3,2},{4,5},{5,4},{6,7},{7,6},{8,9},{9,8},{10,11... | collective-permute-start | bytes 798728 | tf_op jit(solution)/shard_map/ppermute | solution.py:337
  123.8 5.7 %collective-permute-start.26 = (f32[384,128]{1,0:T(8,128)S(1)}, f32[384,128]{1,0:T(8,128)S(1)}, u32[]{:S(2)}, u32[]{:S(2)}) collective-permute-start(f32[384,128]{1,0:T(8,128)S(1)} %slice_add_fusion.22.refs_3_), channel_id=1, source_target_pairs={{0,8},{1,5},{2,10},{3,7},{4,12},{5,1},{6,14},{7,3},{8,0},{9,13},{1... | collective-permute-start | bytes 589832 | tf_op jit(solution)/shard_map/ppermute | solution.py:334
  123.9 8.5 %collective-permute-start.25 = (f32[520,128]{1,0:T(8,128)S(1)}, f32[520,128]{1,0:T(8,128)S(1)}, u32[]{:S(2)}, u32[]{:S(2)}) collective-permute-start(f32[520,128]{1,0:T(8,128)S(1)} %pad_maximum_fusion.8), channel_id=1, source_target_pairs={{0,2},{1,3},{2,0},{3,1},{4,6},{5,7},{6,4},{7,5},{8,10},{9,11},{10,... | collective-permute-start | bytes 798728 | tf_op jit(solution)/shard_map/ppermute | solution.py:337
  129.5 7.8 %collective-permute-start.28 = (f32[768,128]{1,0:T(8,128)S(1)}, f32[768,128]{1,0:T(8,128)S(1)}, u32[]{:S(2)}, u32[]{:S(2)}) collective-permute-start(f32[768,128]{1,0:T(8,128)S(1)} %pad_maximum_fusion.3), channel_id=1, source_target_pairs={{0,4},{1,9},{2,6},{3,11},{4,0},{5,13},{6,2},{7,15},{8,12},{9,1},{1... | collective-permute-start | bytes 1179656 | tf_op jit(solution)/shard_map/ppermute | solution.py:334
  132.4 8.6 %collective-permute-start.27 = (f32[512,128]{1,0:T(8,128)S(1)}, f32[512,128]{1,0:T(8,128)S(1)}, u32[]{:S(2)}, u32[]{:S(2)}) collective-permute-start(f32[512,128]{1,0:T(8,128)S(1)} %slice_add_fusion.8.refs_2_), channel_id=1, source_target_pairs={{0,1},{1,0},{2,3},{3,2},{4,5},{5,4},{6,7},{7,6},{8,9},{9,8},{10,11... | collective-permute-start | bytes 786440 | tf_op jit(solution)/shard_map/ppermute | solution.py:337
  140.9 3.0 %collective-permute-start.30 = (f32[520,128]{1,0:T(8,128)S(1)}, f32[520,128]{1,0:T(8,128)S(1)}, u32[]{:S(2)}, u32[]{:S(2)}) collective-permute-start(f32[520,128]{1,0:T(8,128)S(1)} %get-tuple-element.126), channel_id=1, source_target_pairs={{0,1},{1,0},{2,3},{3,2},{4,5},{5,4},{6,7},{7,6},{8,9},{9,8},{10,11... | collective-permute-start | bytes 798728 | tf_op jit(solution)/shard_map/ppermute | solution.py:337
  143.6 7.9 %collective-permute-start.29 = (f32[776,128]{1,0:T(8,128)S(1)}, f32[776,128]{1,0:T(8,128)S(1)}, u32[]{:S(2)}, u32[]{:S(2)}) collective-permute-start(f32[776,128]{1,0:T(8,128)S(1)} %get-tuple-element.129), channel_id=1, source_target_pairs={{0,4},{1,9},{2,6},{3,11},{4,0},{5,13},{6,2},{7,15},{8,12},{9,1},{1... | collective-permute-start | bytes 1191944 | tf_op jit(solution)/shard_map/ppermute | solution.py:334
  144.0 8.6 %collective-permute-start.32 = (f32[520,128]{1,0:T(8,128)S(1)}, f32[520,128]{1,0:T(8,128)S(1)}, u32[]{:S(2)}, u32[]{:S(2)}) collective-permute-start(f32[520,128]{1,0:T(8,128)S(1)} %pad_maximum_fusion.9), channel_id=1, source_target_pairs={{0,2},{1,3},{2,0},{3,1},{4,6},{5,7},{6,4},{7,5},{8,10},{9,11},{10,... | collective-permute-start | bytes 798728 | tf_op jit(solution)/shard_map/ppermute | solution.py:337
  151.6 5.8 %collective-permute-start.31 = (f32[392,128]{1,0:T(8,128)S(1)}, f32[392,128]{1,0:T(8,128)S(1)}, u32[]{:S(2)}, u32[]{:S(2)}) collective-permute-start(f32[392,128]{1,0:T(8,128)S(1)} %pad_maximum_fusion.18), channel_id=1, source_target_pairs={{0,8},{1,5},{2,10},{3,7},{4,12},{5,1},{6,14},{7,3},{8,0},{9,13},{1... | collective-permute-start | bytes 602120 | tf_op jit(solution)/shard_map/ppermute | solution.py:334
  152.6 4.9 %collective-permute-start.34 = (f32[512,128]{1,0:T(8,128)S(1)}, f32[512,128]{1,0:T(8,128)S(1)}, u32[]{:S(2)}, u32[]{:S(2)}) collective-permute-start(f32[512,128]{1,0:T(8,128)S(1)} %slice_add_fusion.6.refs_2_), channel_id=1, source_target_pairs={{0,1},{1,0},{2,3},{3,2},{4,5},{5,4},{6,7},{7,6},{8,9},{9,8},{10,11... | collective-permute-start | bytes 786440 | tf_op jit(solution)/shard_map/ppermute | solution.py:337
  157.4 10.8 %collective-permute-start.33 = (f32[392,128]{1,0:T(8,128)S(1)}, f32[392,128]{1,0:T(8,128)S(1)}, u32[]{:S(2)}, u32[]{:S(2)}) collective-permute-start(f32[392,128]{1,0:T(8,128)S(1)} %pad_maximum_fusion.19), channel_id=1, source_target_pairs={{0,16},{1,17},{2,18},{3,19},{4,20},{5,21},{6,22},{7,23},{8,24},{9,... | collective-permute-start | bytes 602120 | tf_op jit(solution)/shard_map/ppermute | solution.py:334
  160.2 8.0 %collective-permute-start.35 = (f32[776,128]{1,0:T(8,128)S(1)}, f32[776,128]{1,0:T(8,128)S(1)}, u32[]{:S(2)}, u32[]{:S(2)}) collective-permute-start(f32[776,128]{1,0:T(8,128)S(1)} %get-tuple-element.138), channel_id=1, source_target_pairs={{0,4},{1,9},{2,6},{3,11},{4,0},{5,13},{6,2},{7,15},{8,12},{9,1},{1... | collective-permute-start | bytes 1191944 | tf_op jit(solution)/shard_map/ppermute | solution.py:334
  168.2 5.7 %collective-permute-start.37 = (f32[384,128]{1,0:T(8,128)S(1)}, f32[384,128]{1,0:T(8,128)S(1)}, u32[]{:S(2)}, u32[]{:S(2)}) collective-permute-start(f32[384,128]{1,0:T(8,128)S(1)} %slice_add_fusion.21.refs_2_), channel_id=1, source_target_pairs={{0,8},{1,5},{2,10},{3,7},{4,12},{5,1},{6,14},{7,3},{8,0},{9,13},{1... | collective-permute-start | bytes 589832 | tf_op jit(solution)/shard_map/ppermute | solution.py:334
  168.4 7.7 %collective-permute-start.36 = (f32[392,128]{1,0:T(8,128)S(1)}, f32[392,128]{1,0:T(8,128)S(1)}, u32[]{:S(2)}, u32[]{:S(2)}) collective-permute-start(f32[392,128]{1,0:T(8,128)S(1)} %pad_maximum_fusion.20), channel_id=1, source_target_pairs={{0,8},{1,5},{2,10},{3,7},{4,12},{5,1},{6,14},{7,3},{8,0},{9,13},{1... | collective-permute-start | bytes 602120 | tf_op jit(solution)/shard_map/ppermute | solution.py:334
  176.2 10.9 %collective-permute-start.38 = (f32[392,128]{1,0:T(8,128)S(1)}, f32[392,128]{1,0:T(8,128)S(1)}, u32[]{:S(2)}, u32[]{:S(2)}) collective-permute-start(f32[392,128]{1,0:T(8,128)S(1)} %pad_maximum_fusion.21), channel_id=1, source_target_pairs={{0,16},{1,17},{2,18},{3,19},{4,20},{5,21},{6,22},{7,23},{8,24},{9,... | collective-permute-start | bytes 602120 | tf_op jit(solution)/shard_map/ppermute | solution.py:334
  177.6 9.5 %collective-permute-start.39 = (f32[768,128]{1,0:T(8,128)S(1)}, f32[768,128]{1,0:T(8,128)S(1)}, u32[]{:S(2)}, u32[]{:S(2)}) collective-permute-start(f32[768,128]{1,0:T(8,128)S(1)} %pad_maximum_fusion.4), channel_id=1, source_target_pairs={{0,4},{1,9},{2,6},{3,11},{4,0},{5,13},{6,2},{7,15},{8,12},{9,1},{1... | collective-permute-start | bytes 1179656 | tf_op jit(solution)/shard_map/ppermute | solution.py:334
  187.1 5.7 %collective-permute-start.40 = (f32[384,128]{1,0:T(8,128)S(1)}, f32[384,128]{1,0:T(8,128)S(1)}, u32[]{:S(2)}, u32[]{:S(2)}) collective-permute-start(f32[384,128]{1,0:T(8,128)S(1)} %slice_add_fusion.20.refs_11_), channel_id=1, source_target_pairs={{0,8},{1,5},{2,10},{3,7},{4,12},{5,1},{6,14},{7,3},{8,0},{9,13},{1... | collective-permute-start | bytes 589832 | tf_op jit(solution)/shard_map/ppermute | solution.py:334
  192.8 7.8 %collective-permute-start.41 = (f32[768,128]{1,0:T(8,128)S(1)}, f32[768,128]{1,0:T(8,128)S(1)}, u32[]{:S(2)}, u32[]{:S(2)}) collective-permute-start(f32[768,128]{1,0:T(8,128)S(1)} %pad_maximum_fusion.5), channel_id=1, source_target_pairs={{0,4},{1,9},{2,6},{3,11},{4,0},{5,13},{6,2},{7,15},{8,12},{9,1},{1... | collective-permute-start | bytes 1179656 | tf_op jit(solution)/shard_map/ppermute | solution.py:334

commit v10 on v9

--- a/solution.py
+++ b/solution.py
@@ -13,7 +13,9 @@
 PAIR = 2 * TILE
 UNITS = 4
 NORM_ROWS = 8
-BEHIND = 1
+ROW_TIMES = (7.5, 5.5, 10.5)
+COL_TIMES = (3.0, 8.0)
+FORE_TIME, BACK_TIME = 3.5, 2.5
 
 tiny_eps = 1e-06
 
@@ -350,28 +352,29 @@
 
     def reduce_rows(send, keep):
         half = keep.shape[0]
-        got = yield swap_rows, send, 0
+        got = yield BACK_TIME + ROW_TIMES[0], swap_rows, send, 0
         keep = keep + got[:half]
         norm = send[half:] + got[half:]
         send, mine = keep[: half // 2], keep[half // 2 :]
         for level in range(1, len(row_bits)):
-            got = yield swap_rows, jnp.concatenate([send, norm]), level
+            message = jnp.concatenate([send, norm])
+            got = yield ROW_TIMES[min(level, 2)], swap_rows, message, level
             norm = norm + got[half // 2 :]
             send = mine = mine + got[: half // 2]
-        inner = yield swap_rows, mine, 1
-        outer = yield swap_rows, jnp.concatenate([inner, mine]), 0
+        inner = yield ROW_TIMES[1], swap_rows, mine, 1
+        outer = yield ROW_TIMES[0], swap_rows, jnp.concatenate([inner, mine]), 0
         return [outer, inner, mine], norm
 
     def reduce_cols(send, keep):
         half = keep.shape[0]
-        got = yield swap_cols, send, 0
+        got = yield FORE_TIME + COL_TIMES[0], swap_cols, send, 0
         own = keep + got[:half]
         norm = send[half:] + got[half:]
         for bit in col_bits[1:]:
-            got = yield swap_cols, jnp.concatenate([own, norm]), bit
+            got = yield COL_TIMES[1], swap_cols, jnp.concatenate([own, norm]), bit
             norm = norm + got[half:]
             own = own + got[:half]
-        other = yield swap_cols, own, 0
+        other = yield COL_TIMES[0], swap_cols, own, 0
         return [other, own], norm
 
     def chain(left):
@@ -399,24 +402,23 @@
     wanted = [next(run) for run in runs]
     chains = [None] * len(runs)
     gots = [None] * len(runs)
-    swap, latest, level = wanted[0]
+    length, swap, latest, level = wanted[0]
+    due = [length, length]
     gots[0] = swap(latest, level)
-    turn = 0
     while None in chains:
-        mine = 0 if turn < BEHIND else (turn - BEHIND) % 2
-        turn += 1
-        if chains[mine] is not None:
-            continue
+        mine = due.index(min(due))
         if gots[mine] is None:
-            swap, value, level = wanted[mine]
+            length, swap, value, level = wanted[mine]
             latest = tied(value, latest)
         else:
             try:
-                swap, latest, level = runs[mine].send(tied(gots[mine], latest))
+                length, swap, latest, level = runs[mine].send(tied(gots[mine], latest))
             except StopIteration as stop:
                 chains[mine] = stop.value
+                due[mine] = float("inf")
                 continue
         gots[mine] = swap(latest, level)
+        due[mine] += length
 
     cells = dense.shape[1]
     model, misfit = last_call(

time: 201 us -> 214 us (1.065)
  starting transfers between devices: 23.6 us -> 67.7 us
  waiting for transfers between devices: 137 us -> 107 us
    ppermute x30, starting transfers between devices: 22 us -> 64.2 us  [swap_rows(): return lax.ppermute(value, ('rows', 'cols'), pairs)]
    ppermute x30, waiting for transfers between devices: 133 us -> 95.1 us  [swap_rows(): return lax.ppermute(value, ('rows', 'cols'), pairs)]
    ppermute x12, waiting for transfers between devices: 4.42 us -> 11.8 us  [swap_cols(): lax.ppermute(value, 'cols', [(i, i ^ 1 << level) for i in range(col_count)])]
  transfers between devices with their start and end apart: 42 -> 42, of which waited for: 28 -> 30; matrix products, arithmetic and copies ran while one was open for 1% -> 1% of each run, Pallas kernels for 14% -> 13%
where the time goes in v10:
time: 214 us; the launch traced here: 215 us
  waiting for transfers between devices  107 us (50%)
  starting transfers between devices  67.7 us (32%)
  Pallas kernels  37.4 us (17%)
    ppermute x30, waiting for transfers between devices, swap_rows(): return lax.ppermute(value, ('rows', 'cols'), pairs)  95.1 us
    ppermute x30, starting transfers between devices, swap_rows(): return lax.ppermute(value, ('rows', 'cols'), pairs)  64.2 us
    pallas_call x10, Pallas kernels, product_call(): pl.pallas_call(body, in_specs=[WHOLE] * (1 + len(operands)), out_specs=[W...  29.6 us
    ppermute x12, waiting for transfers between devices, swap_cols(): lax.ppermute(value, 'cols', [(i, i ^ 1 << level) for i in range(col_count)])  11.8 us
    pallas_call x1, Pallas kernels, fill_dense(): pl.pallas_call(fill_kernel, in_specs=[SCALARS] * 2 + [pl.BlockSpec(memory...  4.4 us
  transfers between devices with their start and end apart: 42, of which 30 were waited for; matrix products, arithmetic and copies ran while one was open for 1% of the time, Pallas kernels for 13%

profile of v10, /device:TPU:0, one launch (start us, length us, event | category | flops | bytes accessed | tf_op | source)
XLA Modules:
  0.0 215.2 jit_solution(10186865973296142388)
XLA Ops:
  0.7 4.4 %shard_map.67 = (bf16[2048,3072]{1,0:T(8,128)(2,1)S(1)}, f32[1024,128]{1,0:T(8,128)S(1)}, f32[1024,128]{1,0:T(8,128)S(1)}) custom-call(s32[24]{0:T(128)S(1)} %fusion.place_ref, s32[1]{0:T(128)} %bitcast.1.flip_ref, s32[16,16]{1,0:T(8,128)} %pattern_in.1, s32[16]{0:T(128)} %bitcast.5, f32[2048,128]{1,0:T(8,128)} %delays_in.1, bf16[16,16,128,128]{3,2,1,0:T(8,128)(2,1)} %tiles_in.1), custom_call_target="tpu_custom_call" | custom-call | bytes 8388608 | tf_op jit(solution)/shard_map/pallas_call | solution.py:89
  5.1 2.5 %shard_map.68 = (f32[776,128]{1,0:T(8,128)S(1)}, f32[768,128]{1,0:T(8,128)S(1)}) custom-call(bf16[2048,3072]{1,0:T(8,128)(2,1)S(1)} %get-tuple-element.77.refs_0_, f32[1024,128]{1,0:T(8,128)S(1)} %get-tuple-element.78.refs_1_.refs_4_), custom_call_target="tpu_custom_call" | custom-call | flops 3221225472 | bytes 12582912 | tf_op jit(solution)/shard_map/pallas_call | solution.py:216
  7.6 3.0 %collective-permute-start = (f32[776,128]{1,0:T(8,128)S(1)}, f32[776,128]{1,0:T(8,128)S(1)}, u32[]{:S(2)}, u32[]{:S(2)}) collective-permute-start(f32[776,128]{1,0:T(8,128)S(1)} %get-tuple-element.80), channel_id=1, source_target_pairs={{0,4},{1,9},{2,6},{3,11},{4,0},{5,13},{6,2},{7,15},{8,12},{9,1},{1... | collective-permute-start | bytes 1191944 | tf_op jit(solution)/shard_map/ppermute | solution.py:336
  10.6 5.8 %collective-permute-done = f32[776,128]{1,0:T(8,128)S(1)} collective-permute-done((f32[776,128]{1,0:T(8,128)S(1)}, f32[776,128]{1,0:T(8,128)S(1)}, u32[]{:S(2)}, u32[]{:S(2)}) %collective-permute-start) | collective-permute-done | bytes 397344 | tf_op jit(solution)/shard_map/ppermute | solution.py:336
  16.5 2.2 %collective-permute-start.1 = (f32[392,128]{1,0:T(8,128)S(1)}, f32[392,128]{1,0:T(8,128)S(1)}, u32[]{:S(2)}, u32[]{:S(2)}) collective-permute-start(f32[392,128]{1,0:T(8,128)S(1)} %pad_maximum_fusion.10), channel_id=1, source_target_pairs={{0,8},{1,5},{2,10},{3,7},{4,12},{5,1},{6,14},{7,3},{8,0},{9,13},{1... | collective-permute-start | bytes 602120 | tf_op jit(solution)/shard_map/ppermute | solution.py:336
  18.7 2.5 %shard_map.69 = (f32[776,128]{1,0:T(8,128)S(1)}, f32[768,128]{1,0:T(8,128)S(1)}) custom-call(bf16[2048,3072]{1,0:T(8,128)(2,1)S(1)} %get-tuple-element.77.refs_0_, f32[1024,128]{1,0:T(8,128)S(1)} %get-tuple-element.82.refs_1_.refs_4_), custom_call_target="tpu_custom_call" | custom-call | flops 3221225472 | bytes 12582912 | tf_op jit(solution)/shard_map/pallas_call | solution.py:216
  21.2 2.1 collective-permute-start.3
  23.3 5.7 %collective-permute-done.3 = f32[776,128]{1,0:T(8,128)S(1)} collective-permute-done((f32[776,128]{1,0:T(8,128)S(1)}, f32[776,128]{1,0:T(8,128)S(1)}, u32[]{:S(2)}, u32[]{:S(2)}) %collective-permute-start.3) | collective-permute-done | bytes 397344 | tf_op jit(solution)/shard_map/ppermute | solution.py:336
  29.2 3.1 %collective-permute-start.2 = (f32[392,128]{1,0:T(8,128)S(1)}, f32[392,128]{1,0:T(8,128)S(1)}, u32[]{:S(2)}, u32[]{:S(2)}) collective-permute-start(f32[392,128]{1,0:T(8,128)S(1)} %pad_maximum_fusion.11), channel_id=1, source_target_pairs={{0,16},{1,17},{2,18},{3,19},{4,20},{5,21},{6,22},{7,23},{8,24},{9,... | collective-permute-start | bytes 602120 | tf_op jit(solution)/shard_map/ppermute | solution.py:336
  32.3 4.4 %collective-permute-done.4 = f32[392,128]{1,0:T(8,128)S(1)} collective-permute-done((f32[392,128]{1,0:T(8,128)S(1)}, f32[392,128]{1,0:T(8,128)S(1)}, u32[]{:S(2)}, u32[]{:S(2)}) %collective-permute-start.4) | collective-permute-done | bytes 200736 | tf_op jit(solution)/shard_map/ppermute | solution.py:336
  36.8 4.0 %collective-permute-done.2 = f32[392,128]{1,0:T(8,128)S(1)} collective-permute-done((f32[392,128]{1,0:T(8,128)S(1)}, f32[392,128]{1,0:T(8,128)S(1)}, u32[]{:S(2)}, u32[]{:S(2)}) %collective-permute-start.2) | collective-permute-done | bytes 200736 | tf_op jit(solution)/shard_map/ppermute | solution.py:336
  40.8 2.9 %collective-permute-start.5 = (f32[384,128]{1,0:T(8,128)S(1)}, f32[384,128]{1,0:T(8,128)S(1)}, u32[]{:S(2)}, u32[]{:S(2)}) collective-permute-start(f32[384,128]{1,0:T(8,128)S(1)} %slice_add_fusion.25.refs_3_), channel_id=1, source_target_pairs={{0,8},{1,5},{2,10},{3,7},{4,12},{5,1},{6,14},{7,3},{8,0},{9,13},{1... | collective-permute-start | bytes 589832 | tf_op jit(solution)/shard_map/ppermute | solution.py:336
  43.7 3.3 %collective-permute-start.7 = (f32[392,128]{1,0:T(8,128)S(1)}, f32[392,128]{1,0:T(8,128)S(1)}, u32[]{:S(2)}, u32[]{:S(2)}) collective-permute-start(f32[392,128]{1,0:T(8,128)S(1)} %pad_maximum_fusion.13), channel_id=1, source_target_pairs={{0,16},{1,17},{2,18},{3,19},{4,20},{5,21},{6,22},{7,23},{8,24},{9,... | collective-permute-start | bytes 602120 | tf_op jit(solution)/shard_map/ppermute | solution.py:336
  47.0 3.8 %collective-permute-done.5.refs_2_ = f32[384,128]{1,0:T(8,128)S(1)} collective-permute-done((f32[384,128]{1,0:T(8,128)S(1)}, f32[384,128]{1,0:T(8,128)S(1)}, u32[]{:S(2)}, u32[]{:S(2)}) %collective-permute-start.5) | collective-permute-done | bytes 196640 | tf_op jit(solution)/shard_map/ppermute | solution.py:336
  51.0 1.9 collective-permute-done.7
  52.9 3.5 %collective-permute-start.9 = (f32[384,128]{1,0:T(8,128)S(1)}, f32[384,128]{1,0:T(8,128)S(1)}, u32[]{:S(2)}, u32[]{:S(2)}) collective-permute-start(f32[384,128]{1,0:T(8,128)S(1)} %slice_add_fusion.24.refs_3_), channel_id=1, source_target_pairs={{0,8},{1,5},{2,10},{3,7},{4,12},{5,1},{6,14},{7,3},{8,0},{9,13},{1... | collective-permute-start | bytes 589832 | tf_op jit(solution)/shard_map/ppermute | solution.py:336
  56.4 2.3 %collective-permute-done.6.refs_1_ = f32[768,128]{1,0:T(8,128)S(1)} collective-permute-done((f32[768,128]{1,0:T(8,128)S(1)}, f32[768,128]{1,0:T(8,128)S(1)}, u32[]{:S(2)}, u32[]{:S(2)}) %collective-permute-start.6) | collective-permute-done | bytes 393248 | tf_op jit(solution)/shard_map/ppermute | solution.py:336
  58.7 3.5 %shard_map.70 = (f32[520,128]{1,0:T(8,128)S(1)}, f32[512,128]{1,0:T(8,128)S(1)}, f32[1536,128]{1,0:T(8,128)S(1)}) custom-call(bf16[2048,3072]{1,0:T(8,128)(2,1)S(1)} %get-tuple-element.77.refs_0_, f32[768,128]{1,0:T(8,128)S(1)} %collective-permute-done.6.refs_1_, f32[384,128]{1,0:T(8,128)S(1)} %collective-permute-done.5.refs_2_, ...), custom_call_target="tpu_custom_call" | custom-call | flops 3221225472 | bytes 12582912 | tf_op jit(solution)/shard_map/pallas_call | solution.py:216
  64.0 6.2 %collective-permute-done.11.refs_1_ = f32[768,128]{1,0:T(8,128)S(1)} collective-permute-done((f32[768,128]{1,0:T(8,128)S(1)}, f32[768,128]{1,0:T(8,128)S(1)}, u32[]{:S(2)}, u32[]{:S(2)}) %collective-permute-start.11) | collective-permute-done | bytes 393248 | tf_op jit(solution)/shard_map/ppermute | solution.py:336
  70.2 3.5 %shard_map.71 = (f32[520,128]{1,0:T(8,128)S(1)}, f32[512,128]{1,0:T(8,128)S(1)}, f32[1536,128]{1,0:T(8,128)S(1)}) custom-call(bf16[2048,3072]{1,0:T(8,128)(2,1)S(1)} %get-tuple-element.77.refs_0_, f32[768,128]{1,0:T(8,128)S(1)} %collective-permute-done.11.refs_1_, f32[384,128]{1,0:T(8,128)S(1)} %collective-permute-done.9.refs_2_, ...), custom_call_target="tpu_custom_call" | custom-call | flops 3221225472 | bytes 12582912 | tf_op jit(solution)/shard_map/pallas_call | solution.py:216
  75.7 2.7 %shard_map.72 = (f32[776,128]{1,0:T(8,128)S(1)}, f32[768,128]{1,0:T(8,128)S(1)}, f32[1024,128]{1,0:T(8,128)S(1)}) custom-call(bf16[2048,3072]{1,0:T(8,128)(2,1)S(1)} %get-tuple-element.77.refs_0_, f32[512,128]{1,0:T(8,128)S(1)} %collective-permute-done.12.refs_1_, f32[512,128]{1,0:T(8,128)S(1)} %slice_add_fusion.12.refs_2_, ...), custom_call_target="tpu_custom_call" | custom-call | flops 3221225472 | bytes 12582912 | tf_op jit(solution)/shard_map/pallas_call | solution.py:216
  79.5 4.4 %collective-permute-done.15 = f32[520,128]{1,0:T(8,128)S(1)} collective-permute-done((f32[520,128]{1,0:T(8,128)S(1)}, f32[520,128]{1,0:T(8,128)S(1)}, u32[]{:S(2)}, u32[]{:S(2)}) %collective-permute-start.15) | collective-permute-done | bytes 266272 | tf_op jit(solution)/shard_map/ppermute | solution.py:339
  84.1 2.3 %collective-permute-done.14 = f32[776,128]{1,0:T(8,128)S(1)} collective-permute-done((f32[776,128]{1,0:T(8,128)S(1)}, f32[776,128]{1,0:T(8,128)S(1)}, u32[]{:S(2)}, u32[]{:S(2)}) %collective-permute-start.14) | collective-permute-done | bytes 397344 | tf_op jit(solution)/shard_map/ppermute | solution.py:336
  88.2 2.5 %shard_map.73 = (f32[776,128]{1,0:T(8,128)S(1)}, f32[768,128]{1,0:T(8,128)S(1)}, f32[1024,128]{1,0:T(8,128)S(1)}) custom-call(bf16[2048,3072]{1,0:T(8,128)(2,1)S(1)} %get-tuple-element.77.refs_0_, f32[512,128]{1,0:T(8,128)S(1)} %collective-permute-done.17.refs_1_, f32[512,128]{1,0:T(8,128)S(1)} %slice_add_fusion.10.refs_2_, ...), custom_call_target="tpu_custom_call" | custom-call | flops 3221225472 | bytes 12582912 | tf_op jit(solution)/shard_map/pallas_call | solution.py:216
  92.6 6.0 %collective-permute-done.19 = f32[776,128]{1,0:T(8,128)S(1)} collective-permute-done((f32[776,128]{1,0:T(8,128)S(1)}, f32[776,128]{1,0:T(8,128)S(1)}, u32[]{:S(2)}, u32[]{:S(2)}) %collective-permute-start.19) | collective-permute-done | bytes 397344 | tf_op jit(solution)/shard_map/ppermute | solution.py:336
  99.1 4.9 %collective-permute-start.18 = (f32[392,128]{1,0:T(8,128)S(1)}, f32[392,128]{1,0:T(8,128)S(1)}, u32[]{:S(2)}, u32[]{:S(2)}) collective-permute-start(f32[392,128]{1,0:T(8,128)S(1)} %pad_maximum_fusion.15), channel_id=1, source_target_pairs={{0,16},{1,17},{2,18},{3,19},{4,20},{5,21},{6,22},{7,23},{8,24},{9,... | collective-permute-start | bytes 602120 | tf_op jit(solution)/shard_map/ppermute | solution.py:336
  104.0 1.9 collective-permute-done.20
  106.0 3.2 %collective-permute-done.18 = f32[392,128]{1,0:T(8,128)S(1)} collective-permute-done((f32[392,128]{1,0:T(8,128)S(1)}, f32[392,128]{1,0:T(8,128)S(1)}, u32[]{:S(2)}, u32[]{:S(2)}) %collective-permute-start.18) | collective-permute-done | bytes 200736 | tf_op jit(solution)/shard_map/ppermute | solution.py:336
  109.2 5.3 %collective-permute-start.21 = (f32[384,128]{1,0:T(8,128)S(1)}, f32[384,128]{1,0:T(8,128)S(1)}, u32[]{:S(2)}, u32[]{:S(2)}) collective-permute-start(f32[384,128]{1,0:T(8,128)S(1)} %slice_add_fusion.23.refs_3_), channel_id=1, source_target_pairs={{0,8},{1,5},{2,10},{3,7},{4,12},{5,1},{6,14},{7,3},{8,0},{9,13},{1... | collective-permute-start | bytes 589832 | tf_op jit(solution)/shard_map/ppermute | solution.py:336
  114.5 3.4 %collective-permute-start.23 = (f32[392,128]{1,0:T(8,128)S(1)}, f32[392,128]{1,0:T(8,128)S(1)}, u32[]{:S(2)}, u32[]{:S(2)}) collective-permute-start(f32[392,128]{1,0:T(8,128)S(1)} %pad_maximum_fusion.17), channel_id=1, source_target_pairs={{0,16},{1,17},{2,18},{3,19},{4,20},{5,21},{6,22},{7,23},{8,24},{9,... | collective-permute-start | bytes 602120 | tf_op jit(solution)/shard_map/ppermute | solution.py:336
  119.8 5.1 %collective-permute-done.23 = f32[392,128]{1,0:T(8,128)S(1)} collective-permute-done((f32[392,128]{1,0:T(8,128)S(1)}, f32[392,128]{1,0:T(8,128)S(1)}, u32[]{:S(2)}, u32[]{:S(2)}) %collective-permute-start.23) | collective-permute-done | bytes 200736 | tf_op jit(solution)/shard_map/ppermute | solution.py:336
  124.9 2.6 %collective-permute-start.25 = (f32[384,128]{1,0:T(8,128)S(1)}, f32[384,128]{1,0:T(8,128)S(1)}, u32[]{:S(2)}, u32[]{:S(2)}) collective-permute-start(f32[384,128]{1,0:T(8,128)S(1)} %slice_add_fusion.22.refs_3_), channel_id=1, source_target_pairs={{0,8},{1,5},{2,10},{3,7},{4,12},{5,1},{6,14},{7,3},{8,0},{9,13},{1... | collective-permute-start | bytes 589832 | tf_op jit(solution)/shard_map/ppermute | solution.py:336
  128.0 3.5 %shard_map.74 = (f32[520,128]{1,0:T(8,128)S(1)}, f32[512,128]{1,0:T(8,128)S(1)}, f32[1536,128]{1,0:T(8,128)S(1)}) custom-call(bf16[2048,3072]{1,0:T(8,128)(2,1)S(1)} %get-tuple-element.77.refs_0_, f32[768,128]{1,0:T(8,128)S(1)} %collective-permute-done.22.refs_1_, f32[384,128]{1,0:T(8,128)S(1)} %collective-permute-done.21.refs_2_, ...), custom_call_target="tpu_custom_call" | custom-call | flops 3221225472 | bytes 12582912 | tf_op jit(solution)/shard_map/pallas_call | solution.py:216
  134.3 5.2 %collective-permute-done.27.refs_1_ = f32[768,128]{1,0:T(8,128)S(1)} collective-permute-done((f32[768,128]{1,0:T(8,128)S(1)}, f32[768,128]{1,0:T(8,128)S(1)}, u32[]{:S(2)}, u32[]{:S(2)}) %collective-permute-start.27) | collective-permute-done | bytes 393248 | tf_op jit(solution)/shard_map/ppermute | solution.py:336
  139.5 3.5 %shard_map.75 = (f32[520,128]{1,0:T(8,128)S(1)}, f32[512,128]{1,0:T(8,128)S(1)}, f32[1536,128]{1,0:T(8,128)S(1)}) custom-call(bf16[2048,3072]{1,0:T(8,128)(2,1)S(1)} %get-tuple-element.77.refs_0_, f32[768,128]{1,0:T(8,128)S(1)} %collective-permute-done.27.refs_1_, f32[384,128]{1,0:T(8,128)S(1)} %collective-permute-done.25.refs_2_, ...), custom_call_target="tpu_custom_call" | custom-call | flops 3221225472 | bytes 12582912 | tf_op jit(solution)/shard_map/pallas_call | solution.py:216
  145.8 2.5 %shard_map.76 = (f32[776,128]{1,0:T(8,128)S(1)}, f32[768,128]{1,0:T(8,128)S(1)}, f32[1024,128]{1,0:T(8,128)}) custom-call(bf16[2048,3072]{1,0:T(8,128)(2,1)S(1)} %get-tuple-element.77.refs_0_, f32[512,128]{1,0:T(8,128)S(1)} %collective-permute-done.28.refs_1_, f32[512,128]{1,0:T(8,128)S(1)} %slice_add_fusion.8.refs_2_, ...), custom_call_target="tpu_custom_call" | custom-call | flops 3221225472 | bytes 12582912 | tf_op jit(solution)/shard_map/pallas_call | solution.py:216
  149.4 3.9 %collective-permute-done.31 = f32[520,128]{1,0:T(8,128)S(1)} collective-permute-done((f32[520,128]{1,0:T(8,128)S(1)}, f32[520,128]{1,0:T(8,128)S(1)}, u32[]{:S(2)}, u32[]{:S(2)}) %collective-permute-start.31) | collective-permute-done | bytes 266272 | tf_op jit(solution)/shard_map/ppermute | solution.py:339
  153.4 2.9 %collective-permute-done.30 = f32[776,128]{1,0:T(8,128)S(1)} collective-permute-done((f32[776,128]{1,0:T(8,128)S(1)}, f32[776,128]{1,0:T(8,128)S(1)}, u32[]{:S(2)}, u32[]{:S(2)}) %collective-permute-start.30) | collective-permute-done | bytes 397344 | tf_op jit(solution)/shard_map/ppermute | solution.py:336
  156.4 2.1 collective-permute-start.32
  158.4 2.8 %shard_map.77 = (f32[776,128]{1,0:T(8,128)S(1)}, f32[768,128]{1,0:T(8,128)S(1)}, f32[1024,128]{1,0:T(8,128)}) custom-call(bf16[2048,3072]{1,0:T(8,128)(2,1)S(1)} %get-tuple-element.77.refs_0_, f32[512,128]{1,0:T(8,128)S(1)} %collective-permute-done.33.refs_1_, f32[512,128]{1,0:T(8,128)S(1)} %slice_add_fusion.6.refs_2_, ...), custom_call_target="tpu_custom_call" | custom-call | flops 3221225472 | bytes 12582912 | tf_op jit(solution)/shard_map/pallas_call | solution.py:216
  162.5 6.6 %collective-permute-done.35 = f32[776,128]{1,0:T(8,128)S(1)} collective-permute-done((f32[776,128]{1,0:T(8,128)S(1)}, f32[776,128]{1,0:T(8,128)S(1)}, u32[]{:S(2)}, u32[]{:S(2)}) %collective-permute-start.35) | collective-permute-done | bytes 397344 | tf_op jit(solution)/shard_map/ppermute | solution.py:336
  169.3 7.2 %collective-permute-start.34 = (f32[392,128]{1,0:T(8,128)S(1)}, f32[392,128]{1,0:T(8,128)S(1)}, u32[]{:S(2)}, u32[]{:S(2)}) collective-permute-start(f32[392,128]{1,0:T(8,128)S(1)} %pad_maximum_fusion.19), channel_id=1, source_target_pairs={{0,16},{1,17},{2,18},{3,19},{4,20},{5,21},{6,22},{7,23},{8,24},{9,... | collective-permute-start | bytes 602120 | tf_op jit(solution)/shard_map/ppermute | solution.py:336
  176.5 7.5 %collective-permute-done.34 = f32[392,128]{1,0:T(8,128)S(1)} collective-permute-done((f32[392,128]{1,0:T(8,128)S(1)}, f32[392,128]{1,0:T(8,128)S(1)}, u32[]{:S(2)}, u32[]{:S(2)}) %collective-permute-start.34) | collective-permute-done | bytes 200736 | tf_op jit(solution)/shard_map/ppermute | solution.py:336
  184.0 2.9 %collective-permute-start.38 = (f32[384,128]{1,0:T(8,128)S(1)}, f32[384,128]{1,0:T(8,128)S(1)}, u32[]{:S(2)}, u32[]{:S(2)}) collective-permute-start(f32[384,128]{1,0:T(8,128)S(1)} %slice_add_fusion.21.refs_2_), channel_id=1, source_target_pairs={{0,8},{1,5},{2,10},{3,7},{4,12},{5,1},{6,14},{7,3},{8,0},{9,13},{1... | collective-permute-start | bytes 589832 | tf_op jit(solution)/shard_map/ppermute | solution.py:336
  187.0 3.4 %collective-permute-start.37 = (f32[392,128]{1,0:T(8,128)S(1)}, f32[392,128]{1,0:T(8,128)S(1)}, u32[]{:S(2)}, u32[]{:S(2)}) collective-permute-start(f32[392,128]{1,0:T(8,128)S(1)} %pad_maximum_fusion.21), channel_id=1, source_target_pairs={{0,16},{1,17},{2,18},{3,19},{4,20},{5,21},{6,22},{7,23},{8,24},{9,... | collective-permute-start | bytes 602120 | tf_op jit(solution)/shard_map/ppermute | solution.py:336
  190.7 7.1 %collective-permute-done.37 = f32[392,128]{1,0:T(8,128)S(1)} collective-permute-done((f32[392,128]{1,0:T(8,128)S(1)}, f32[392,128]{1,0:T(8,128)S(1)}, u32[]{:S(2)}, u32[]{:S(2)}) %collective-permute-start.37) | collective-permute-done | bytes 200736 | tf_op jit(solution)/shard_map/ppermute | solution.py:336
  198.8 6.9 %collective-permute-done.40.refs_10_ = f32[384,128]{1,0:T(8,128)S(1)} collective-permute-done((f32[384,128]{1,0:T(8,128)S(1)}, f32[384,128]{1,0:T(8,128)S(1)}, u32[]{:S(2)}, u32[]{:S(2)}) %collective-permute-start.40) | collective-permute-done | bytes 196640 | tf_op jit(solution)/shard_map/ppermute | solution.py:336
  208.6 4.9 %collective-permute-done.41.refs_9_ = f32[768,128]{1,0:T(8,128)S(1)} collective-permute-done((f32[768,128]{1,0:T(8,128)S(1)}, f32[768,128]{1,0:T(8,128)S(1)}, u32[]{:S(2)}, u32[]{:S(2)}) %collective-permute-start.41) | collective-permute-done | bytes 393248 | tf_op jit(solution)/shard_map/ppermute | solution.py:336
  (131 shorter events, 26.0 us)
Async XLA Ops:
  7.6 8.8 %collective-permute-start = (f32[776,128]{1,0:T(8,128)S(1)}, f32[776,128]{1,0:T(8,128)S(1)}, u32[]{:S(2)}, u32[]{:S(2)}) collective-permute-start(f32[776,128]{1,0:T(8,128)S(1)} %get-tuple-element.80), channel_id=1, source_target_pairs={{0,4},{1,9},{2,6},{3,11},{4,0},{5,13},{6,2},{7,15},{8,12},{9,1},{1... | collective-permute-start | bytes 1191944 | tf_op jit(solution)/shard_map/ppermute | solution.py:336
  16.5 6.7 %collective-permute-start.1 = (f32[392,128]{1,0:T(8,128)S(1)}, f32[392,128]{1,0:T(8,128)S(1)}, u32[]{:S(2)}, u32[]{:S(2)}) collective-permute-start(f32[392,128]{1,0:T(8,128)S(1)} %pad_maximum_fusion.10), channel_id=1, source_target_pairs={{0,8},{1,5},{2,10},{3,7},{4,12},{5,1},{6,14},{7,3},{8,0},{9,13},{1... | collective-permute-start | bytes 602120 | tf_op jit(solution)/shard_map/ppermute | solution.py:336
  21.2 7.9 %collective-permute-start.3 = (f32[776,128]{1,0:T(8,128)S(1)}, f32[776,128]{1,0:T(8,128)S(1)}, u32[]{:S(2)}, u32[]{:S(2)}) collective-permute-start(f32[776,128]{1,0:T(8,128)S(1)} %get-tuple-element.84), channel_id=1, source_target_pairs={{0,4},{1,9},{2,6},{3,11},{4,0},{5,13},{6,2},{7,15},{8,12},{9,1},{1... | collective-permute-start | bytes 1191944 | tf_op jit(solution)/shard_map/ppermute | solution.py:336
  29.1 7.6 %collective-permute-start.4 = (f32[392,128]{1,0:T(8,128)S(1)}, f32[392,128]{1,0:T(8,128)S(1)}, u32[]{:S(2)}, u32[]{:S(2)}) collective-permute-start(f32[392,128]{1,0:T(8,128)S(1)} %pad_maximum_fusion.12), channel_id=1, source_target_pairs={{0,8},{1,5},{2,10},{3,7},{4,12},{5,1},{6,14},{7,3},{8,0},{9,13},{1... | collective-permute-start | bytes 602120 | tf_op jit(solution)/shard_map/ppermute | solution.py:336
  29.2 11.5 %collective-permute-start.2 = (f32[392,128]{1,0:T(8,128)S(1)}, f32[392,128]{1,0:T(8,128)S(1)}, u32[]{:S(2)}, u32[]{:S(2)}) collective-permute-start(f32[392,128]{1,0:T(8,128)S(1)} %pad_maximum_fusion.11), channel_id=1, source_target_pairs={{0,16},{1,17},{2,18},{3,19},{4,20},{5,21},{6,22},{7,23},{8,24},{9,... | collective-permute-start | bytes 602120 | tf_op jit(solution)/shard_map/ppermute | solution.py:336
  40.8 10.1 %collective-permute-start.5 = (f32[384,128]{1,0:T(8,128)S(1)}, f32[384,128]{1,0:T(8,128)S(1)}, u32[]{:S(2)}, u32[]{:S(2)}) collective-permute-start(f32[384,128]{1,0:T(8,128)S(1)} %slice_add_fusion.25.refs_3_), channel_id=1, source_target_pairs={{0,8},{1,5},{2,10},{3,7},{4,12},{5,1},{6,14},{7,3},{8,0},{9,13},{1... | collective-permute-start | bytes 589832 | tf_op jit(solution)/shard_map/ppermute | solution.py:336
  43.7 9.2 %collective-permute-start.7 = (f32[392,128]{1,0:T(8,128)S(1)}, f32[392,128]{1,0:T(8,128)S(1)}, u32[]{:S(2)}, u32[]{:S(2)}) collective-permute-start(f32[392,128]{1,0:T(8,128)S(1)} %pad_maximum_fusion.13), channel_id=1, source_target_pairs={{0,16},{1,17},{2,18},{3,19},{4,20},{5,21},{6,22},{7,23},{8,24},{9,... | collective-permute-start | bytes 602120 | tf_op jit(solution)/shard_map/ppermute | solution.py:336
  50.9 7.8 %collective-permute-start.6 = (f32[768,128]{1,0:T(8,128)S(1)}, f32[768,128]{1,0:T(8,128)S(1)}, u32[]{:S(2)}, u32[]{:S(2)}) collective-permute-start(f32[768,128]{1,0:T(8,128)S(1)} %pad_maximum_fusion), channel_id=1, source_target_pairs={{0,4},{1,9},{2,6},{3,11},{4,0},{5,13},{6,2},{7,15},{8,12},{9,1},{1... | collective-permute-start | bytes 1179656 | tf_op jit(solution)/shard_map/ppermute | solution.py:336
  52.9 9.5 %collective-permute-start.9 = (f32[384,128]{1,0:T(8,128)S(1)}, f32[384,128]{1,0:T(8,128)S(1)}, u32[]{:S(2)}, u32[]{:S(2)}) collective-permute-start(f32[384,128]{1,0:T(8,128)S(1)} %slice_add_fusion.24.refs_3_), channel_id=1, source_target_pairs={{0,8},{1,5},{2,10},{3,7},{4,12},{5,1},{6,14},{7,3},{8,0},{9,13},{1... | collective-permute-start | bytes 589832 | tf_op jit(solution)/shard_map/ppermute | solution.py:336
  62.2 1.6 collective-permute-start.8
  62.4 7.8 %collective-permute-start.11 = (f32[768,128]{1,0:T(8,128)S(1)}, f32[768,128]{1,0:T(8,128)S(1)}, u32[]{:S(2)}, u32[]{:S(2)}) collective-permute-start(f32[768,128]{1,0:T(8,128)S(1)} %pad_maximum_fusion.1), channel_id=1, source_target_pairs={{0,4},{1,9},{2,6},{3,11},{4,0},{5,13},{6,2},{7,15},{8,12},{9,1},{1... | collective-permute-start | bytes 1179656 | tf_op jit(solution)/shard_map/ppermute | solution.py:336
  63.9 9.9 %collective-permute-start.10 = (f32[520,128]{1,0:T(8,128)S(1)}, f32[520,128]{1,0:T(8,128)S(1)}, u32[]{:S(2)}, u32[]{:S(2)}) collective-permute-start(f32[520,128]{1,0:T(8,128)S(1)} %pad_maximum_fusion.6), channel_id=1, source_target_pairs={{0,2},{1,3},{2,0},{3,1},{4,6},{5,7},{6,4},{7,5},{8,10},{9,11},{10,... | collective-permute-start | bytes 798728 | tf_op jit(solution)/shard_map/ppermute | solution.py:339
  73.7 1.6 collective-permute-start.13
  73.9 1.9 collective-permute-start.12
  75.4 8.5 %collective-permute-start.15 = (f32[520,128]{1,0:T(8,128)S(1)}, f32[520,128]{1,0:T(8,128)S(1)}, u32[]{:S(2)}, u32[]{:S(2)}) collective-permute-start(f32[520,128]{1,0:T(8,128)S(1)} %pad_maximum_fusion.7), channel_id=1, source_target_pairs={{0,2},{1,3},{2,0},{3,1},{4,6},{5,7},{6,4},{7,5},{8,10},{9,11},{10,... | collective-permute-start | bytes 798728 | tf_op jit(solution)/shard_map/ppermute | solution.py:339
  78.5 7.9 %collective-permute-start.14 = (f32[776,128]{1,0:T(8,128)S(1)}, f32[776,128]{1,0:T(8,128)S(1)}, u32[]{:S(2)}, u32[]{:S(2)}) collective-permute-start(f32[776,128]{1,0:T(8,128)S(1)} %get-tuple-element.105), channel_id=1, source_target_pairs={{0,4},{1,9},{2,6},{3,11},{4,0},{5,13},{6,2},{7,15},{8,12},{9,1},{1... | collective-permute-start | bytes 1191944 | tf_op jit(solution)/shard_map/ppermute | solution.py:336
  84.0 4.3 %collective-permute-start.17 = (f32[512,128]{1,0:T(8,128)S(1)}, f32[512,128]{1,0:T(8,128)S(1)}, u32[]{:S(2)}, u32[]{:S(2)}) collective-permute-start(f32[512,128]{1,0:T(8,128)S(1)} %slice_add_fusion.10.refs_2_), channel_id=1, source_target_pairs={{0,1},{1,0},{2,3},{3,2},{4,5},{5,4},{6,7},{7,6},{8,9},{9,8},{10,11... | collective-permute-start | bytes 786440 | tf_op jit(solution)/shard_map/ppermute | solution.py:339
  86.5 6.1 %collective-permute-start.16 = (f32[392,128]{1,0:T(8,128)S(1)}, f32[392,128]{1,0:T(8,128)S(1)}, u32[]{:S(2)}, u32[]{:S(2)}) collective-permute-start(f32[392,128]{1,0:T(8,128)S(1)} %pad_maximum_fusion.14), channel_id=1, source_target_pairs={{0,8},{1,5},{2,10},{3,7},{4,12},{5,1},{6,14},{7,3},{8,0},{9,13},{1... | collective-permute-start | bytes 602120 | tf_op jit(solution)/shard_map/ppermute | solution.py:336
  90.8 7.9 %collective-permute-start.19 = (f32[776,128]{1,0:T(8,128)S(1)}, f32[776,128]{1,0:T(8,128)S(1)}, u32[]{:S(2)}, u32[]{:S(2)}) collective-permute-start(f32[776,128]{1,0:T(8,128)S(1)} %get-tuple-element.109), channel_id=1, source_target_pairs={{0,4},{1,9},{2,6},{3,11},{4,0},{5,13},{6,2},{7,15},{8,12},{9,1},{1... | collective-permute-start | bytes 1191944 | tf_op jit(solution)/shard_map/ppermute | solution.py:336
  98.8 7.2 %collective-permute-start.20 = (f32[392,128]{1,0:T(8,128)S(1)}, f32[392,128]{1,0:T(8,128)S(1)}, u32[]{:S(2)}, u32[]{:S(2)}) collective-permute-start(f32[392,128]{1,0:T(8,128)S(1)} %pad_maximum_fusion.16), channel_id=1, source_target_pairs={{0,8},{1,5},{2,10},{3,7},{4,12},{5,1},{6,14},{7,3},{8,0},{9,13},{1... | collective-permute-start | bytes 602120 | tf_op jit(solution)/shard_map/ppermute | solution.py:336
  99.1 10.1 %collective-permute-start.18 = (f32[392,128]{1,0:T(8,128)S(1)}, f32[392,128]{1,0:T(8,128)S(1)}, u32[]{:S(2)}, u32[]{:S(2)}) collective-permute-start(f32[392,128]{1,0:T(8,128)S(1)} %pad_maximum_fusion.15), channel_id=1, source_target_pairs={{0,16},{1,17},{2,18},{3,19},{4,20},{5,21},{6,22},{7,23},{8,24},{9,... | collective-permute-start | bytes 602120 | tf_op jit(solution)/shard_map/ppermute | solution.py:336
  109.2 8.9 %collective-permute-start.21 = (f32[384,128]{1,0:T(8,128)S(1)}, f32[384,128]{1,0:T(8,128)S(1)}, u32[]{:S(2)}, u32[]{:S(2)}) collective-permute-start(f32[384,128]{1,0:T(8,128)S(1)} %slice_add_fusion.23.refs_3_), channel_id=1, source_target_pairs={{0,8},{1,5},{2,10},{3,7},{4,12},{5,1},{6,14},{7,3},{8,0},{9,13},{1... | collective-permute-start | bytes 589832 | tf_op jit(solution)/shard_map/ppermute | solution.py:336
  114.5 10.4 %collective-permute-start.23 = (f32[392,128]{1,0:T(8,128)S(1)}, f32[392,128]{1,0:T(8,128)S(1)}, u32[]{:S(2)}, u32[]{:S(2)}) collective-permute-start(f32[392,128]{1,0:T(8,128)S(1)} %pad_maximum_fusion.17), channel_id=1, source_target_pairs={{0,16},{1,17},{2,18},{3,19},{4,20},{5,21},{6,22},{7,23},{8,24},{9,... | collective-permute-start | bytes 602120 | tf_op jit(solution)/shard_map/ppermute | solution.py:336
  118.2 9.8 %collective-permute-start.22 = (f32[768,128]{1,0:T(8,128)S(1)}, f32[768,128]{1,0:T(8,128)S(1)}, u32[]{:S(2)}, u32[]{:S(2)}) collective-permute-start(f32[768,128]{1,0:T(8,128)S(1)} %pad_maximum_fusion.2), channel_id=1, source_target_pairs={{0,4},{1,9},{2,6},{3,11},{4,0},{5,13},{6,2},{7,15},{8,12},{9,1},{1... | collective-permute-start | bytes 1179656 | tf_op jit(solution)/shard_map/ppermute | solution.py:336
  124.9 6.7 %collective-permute-start.25 = (f32[384,128]{1,0:T(8,128)S(1)}, f32[384,128]{1,0:T(8,128)S(1)}, u32[]{:S(2)}, u32[]{:S(2)}) collective-permute-start(f32[384,128]{1,0:T(8,128)S(1)} %slice_add_fusion.22.refs_3_), channel_id=1, source_target_pairs={{0,8},{1,5},{2,10},{3,7},{4,12},{5,1},{6,14},{7,3},{8,0},{9,13},{1... | collective-permute-start | bytes 589832 | tf_op jit(solution)/shard_map/ppermute | solution.py:336
  131.5 1.9 collective-permute-start.24
  131.7 7.8 %collective-permute-start.27 = (f32[768,128]{1,0:T(8,128)S(1)}, f32[768,128]{1,0:T(8,128)S(1)}, u32[]{:S(2)}, u32[]{:S(2)}) collective-permute-start(f32[768,128]{1,0:T(8,128)S(1)} %pad_maximum_fusion.3), channel_id=1, source_target_pairs={{0,4},{1,9},{2,6},{3,11},{4,0},{5,13},{6,2},{7,15},{8,12},{9,1},{1... | collective-permute-start | bytes 1179656 | tf_op jit(solution)/shard_map/ppermute | solution.py:336
  133.5 9.6 %collective-permute-start.26 = (f32[520,128]{1,0:T(8,128)S(1)}, f32[520,128]{1,0:T(8,128)S(1)}, u32[]{:S(2)}, u32[]{:S(2)}) collective-permute-start(f32[520,128]{1,0:T(8,128)S(1)} %pad_maximum_fusion.8), channel_id=1, source_target_pairs={{0,2},{1,3},{2,0},{3,1},{4,6},{5,7},{6,4},{7,5},{8,10},{9,11},{10,... | collective-permute-start | bytes 798728 | tf_op jit(solution)/shard_map/ppermute | solution.py:339
  143.1 1.6 collective-permute-start.29
  143.2 2.6 %collective-permute-start.28 = (f32[512,128]{1,0:T(8,128)S(1)}, f32[512,128]{1,0:T(8,128)S(1)}, u32[]{:S(2)}, u32[]{:S(2)}) collective-permute-start(f32[512,128]{1,0:T(8,128)S(1)} %slice_add_fusion.8.refs_2_), channel_id=1, source_target_pairs={{0,1},{1,0},{2,3},{3,2},{4,5},{5,4},{6,7},{7,6},{8,9},{9,8},{10,11... | collective-permute-start | bytes 786440 | tf_op jit(solution)/shard_map/ppermute | solution.py:339
  144.7 8.5 %collective-permute-start.31 = (f32[520,128]{1,0:T(8,128)S(1)}, f32[520,128]{1,0:T(8,128)S(1)}, u32[]{:S(2)}, u32[]{:S(2)}) collective-permute-start(f32[520,128]{1,0:T(8,128)S(1)} %pad_maximum_fusion.9), channel_id=1, source_target_pairs={{0,2},{1,3},{2,0},{3,1},{4,6},{5,7},{6,4},{7,5},{8,10},{9,11},{10,... | collective-permute-start | bytes 798728 | tf_op jit(solution)/shard_map/ppermute | solution.py:339
  148.4 7.9 %collective-permute-start.30 = (f32[776,128]{1,0:T(8,128)S(1)}, f32[776,128]{1,0:T(8,128)S(1)}, u32[]{:S(2)}, u32[]{:S(2)}) collective-permute-start(f32[776,128]{1,0:T(8,128)S(1)} %get-tuple-element.131), channel_id=1, source_target_pairs={{0,4},{1,9},{2,6},{3,11},{4,0},{5,13},{6,2},{7,15},{8,12},{9,1},{1... | collective-permute-start | bytes 1191944 | tf_op jit(solution)/shard_map/ppermute | solution.py:336
  153.3 5.1 %collective-permute-start.33 = (f32[512,128]{1,0:T(8,128)S(1)}, f32[512,128]{1,0:T(8,128)S(1)}, u32[]{:S(2)}, u32[]{:S(2)}) collective-permute-start(f32[512,128]{1,0:T(8,128)S(1)} %slice_add_fusion.6.refs_2_), channel_id=1, source_target_pairs={{0,1},{1,0},{2,3},{3,2},{4,5},{5,4},{6,7},{7,6},{8,9},{9,8},{10,11... | collective-permute-start | bytes 786440 | tf_op jit(solution)/shard_map/ppermute | solution.py:339
  156.4 6.1 %collective-permute-start.32 = (f32[392,128]{1,0:T(8,128)S(1)}, f32[392,128]{1,0:T(8,128)S(1)}, u32[]{:S(2)}, u32[]{:S(2)}) collective-permute-start(f32[392,128]{1,0:T(8,128)S(1)} %pad_maximum_fusion.18), channel_id=1, source_target_pairs={{0,8},{1,5},{2,10},{3,7},{4,12},{5,1},{6,14},{7,3},{8,0},{9,13},{1... | collective-permute-start | bytes 602120 | tf_op jit(solution)/shard_map/ppermute | solution.py:336
  161.2 7.9 %collective-permute-start.35 = (f32[776,128]{1,0:T(8,128)S(1)}, f32[776,128]{1,0:T(8,128)S(1)}, u32[]{:S(2)}, u32[]{:S(2)}) collective-permute-start(f32[776,128]{1,0:T(8,128)S(1)} %get-tuple-element.137), channel_id=1, source_target_pairs={{0,4},{1,9},{2,6},{3,11},{4,0},{5,13},{6,2},{7,15},{8,12},{9,1},{1... | collective-permute-start | bytes 1191944 | tf_op jit(solution)/shard_map/ppermute | solution.py:336
  169.2 7.3 %collective-permute-start.36 = (f32[392,128]{1,0:T(8,128)S(1)}, f32[392,128]{1,0:T(8,128)S(1)}, u32[]{:S(2)}, u32[]{:S(2)}) collective-permute-start(f32[392,128]{1,0:T(8,128)S(1)} %pad_maximum_fusion.20), channel_id=1, source_target_pairs={{0,8},{1,5},{2,10},{3,7},{4,12},{5,1},{6,14},{7,3},{8,0},{9,13},{1... | collective-permute-start | bytes 602120 | tf_op jit(solution)/shard_map/ppermute | solution.py:336
  169.3 14.8 %collective-permute-start.34 = (f32[392,128]{1,0:T(8,128)S(1)}, f32[392,128]{1,0:T(8,128)S(1)}, u32[]{:S(2)}, u32[]{:S(2)}) collective-permute-start(f32[392,128]{1,0:T(8,128)S(1)} %pad_maximum_fusion.19), channel_id=1, source_target_pairs={{0,16},{1,17},{2,18},{3,19},{4,20},{5,21},{6,22},{7,23},{8,24},{9,... | collective-permute-start | bytes 602120 | tf_op jit(solution)/shard_map/ppermute | solution.py:336
  184.0 6.6 %collective-permute-start.38 = (f32[384,128]{1,0:T(8,128)S(1)}, f32[384,128]{1,0:T(8,128)S(1)}, u32[]{:S(2)}, u32[]{:S(2)}) collective-permute-start(f32[384,128]{1,0:T(8,128)S(1)} %slice_add_fusion.21.refs_2_), channel_id=1, source_target_pairs={{0,8},{1,5},{2,10},{3,7},{4,12},{5,1},{6,14},{7,3},{8,0},{9,13},{1... | collective-permute-start | bytes 589832 | tf_op jit(solution)/shard_map/ppermute | solution.py:336
  187.0 10.8 %collective-permute-start.37 = (f32[392,128]{1,0:T(8,128)S(1)}, f32[392,128]{1,0:T(8,128)S(1)}, u32[]{:S(2)}, u32[]{:S(2)}) collective-permute-start(f32[392,128]{1,0:T(8,128)S(1)} %pad_maximum_fusion.21), channel_id=1, source_target_pairs={{0,16},{1,17},{2,18},{3,19},{4,20},{5,21},{6,22},{7,23},{8,24},{9,... | collective-permute-start | bytes 602120 | tf_op jit(solution)/shard_map/ppermute | solution.py:336
  197.8 7.9 %collective-permute-start.40 = (f32[384,128]{1,0:T(8,128)S(1)}, f32[384,128]{1,0:T(8,128)S(1)}, u32[]{:S(2)}, u32[]{:S(2)}) collective-permute-start(f32[384,128]{1,0:T(8,128)S(1)} %slice_add_fusion.20.refs_11_), channel_id=1, source_target_pairs={{0,8},{1,5},{2,10},{3,7},{4,12},{5,1},{6,14},{7,3},{8,0},{9,13},{1... | collective-permute-start | bytes 589832 | tf_op jit(solution)/shard_map/ppermute | solution.py:336
  198.1 10.5 %collective-permute-start.39 = (f32[768,128]{1,0:T(8,128)S(1)}, f32[768,128]{1,0:T(8,128)S(1)}, u32[]{:S(2)}, u32[]{:S(2)}) collective-permute-start(f32[768,128]{1,0:T(8,128)S(1)} %pad_maximum_fusion.4), channel_id=1, source_target_pairs={{0,4},{1,9},{2,6},{3,11},{4,0},{5,13},{6,2},{7,15},{8,12},{9,1},{1... | collective-permute-start | bytes 1179656 | tf_op jit(solution)/shard_map/ppermute | solution.py:336
  205.7 7.8 %collective-permute-start.41 = (f32[768,128]{1,0:T(8,128)S(1)}, f32[768,128]{1,0:T(8,128)S(1)}, u32[]{:S(2)}, u32[]{:S(2)}) collective-permute-start(f32[768,128]{1,0:T(8,128)S(1)} %pad_maximum_fusion.5), channel_id=1, source_target_pairs={{0,4},{1,9},{2,6},{3,11},{4,0},{5,13},{6,2},{7,15},{8,12},{9,1},{1... | collective-permute-start | bytes 1179656 | tf_op jit(solution)/shard_map/ppermute | solution.py:336

commit v11 on v7

--- a/solution.py
+++ b/solution.py
@@ -141,21 +141,24 @@
                 position += 1
 
 
-def store_message(pair, value, send_ref, keep_ref):
-    half = keep_ref.shape[0] // TILE
-    if pair < half:
-        send_ref[rows_of(pair), :] = value
-    else:
-        keep_ref[rows_of(pair - half), :] = value
-
-
-def back_kernel(first, *refs):
+def back_pairs(dense_ref, turned_ref, out_ref, start):
+    for pair in range(out_ref.shape[0] // TILE):
+        product = jnp.dot(
+            turned_ref[...],
+            dense_ref[:, rows_of(start + pair, PAIR)],
+            preferred_element_type=jnp.float32,
+        )
+        stacked = jnp.concatenate([product[:, :TILE], product[:, TILE:]], axis=0)
+        out_ref[rows_of(pair), :] = stacked.T
+
+
+def back_send_kernel(first, *refs):
     if first:
-        dense_ref, own_ref, send_ref, keep_ref, turned_ref = refs
+        dense_ref, own_ref, send_ref, turned_ref = refs
         parts, raw_ref, scales = [(own_ref, 2)], None, (None, None, None)
     else:
         (dense_ref, other_ref, own_ref, scale_ref, past_ref, past_scale_ref,
-         send_ref, keep_ref, raw_ref, turned_ref) = refs
+         send_ref, turned_ref, raw_ref) = refs
         parts, scales = [(other_ref, 1), (own_ref, 1)], (scale_ref, past_ref, past_scale_ref)
     sums = []
     half = turned_ref.shape[0]
@@ -165,23 +168,35 @@
         turned_ref[:, rows_of(2 * pair + 1)] = flat[half:]
         if squares is not None:
             sums.append(squares)
-    send_ref[keep_ref.shape[0] :, :] = jnp.broadcast_to(squares_row(sums), (NORM_ROWS, TILE))
-    for pair in range(dense_ref.shape[1] // PAIR):
+    send_ref[-NORM_ROWS:, :] = jnp.broadcast_to(squares_row(sums), (NORM_ROWS, TILE))
+    back_pairs(dense_ref, turned_ref, send_ref, 0)
+
+
+def back_keep_kernel(dense_ref, turned_ref, keep_ref):
+    back_pairs(dense_ref, turned_ref, keep_ref, keep_ref.shape[0] // TILE)
+
+
+def fore_pairs(dense_ref, wide_ref, out_ref, start):
+    low = low_lanes((TILE, TILE))
+    step = 2
+    for pair in range(0, out_ref.shape[0] // TILE, step):
         product = jnp.dot(
-            turned_ref[...], dense_ref[:, rows_of(pair, PAIR)], preferred_element_type=jnp.float32
+            dense_ref[(start + pair) * PAIR : (start + pair + step) * PAIR, :],
+            wide_ref[...],
+            preferred_element_type=jnp.float32,
         )
-        stacked = jnp.concatenate([product[:, :TILE], product[:, TILE:]], axis=0)
-        store_message(pair, stacked.T, send_ref, keep_ref)
-
-
-def fore_kernel(first, *refs):
+        for i in range(step):
+            even, odd = product[rows_of(2 * i), :], product[rows_of(2 * i + 1), :]
+            out_ref[rows_of(pair + i), :] = jnp.where(low, even, odd)
+
+
+def fore_send_kernel(first, *refs):
     if first:
-        (dense_ref, outer_ref, inner_ref, mine_ref, scale_ref,
-         send_ref, keep_ref, raw_ref, wide_ref) = refs
+        (dense_ref, outer_ref, inner_ref, mine_ref, scale_ref, send_ref, wide_ref, raw_ref) = refs
         scales = (scale_ref, None, None)
     else:
         (dense_ref, outer_ref, inner_ref, mine_ref, scale_ref, past_ref, past_scale_ref,
-         send_ref, keep_ref, raw_ref, wide_ref) = refs
+         send_ref, wide_ref, raw_ref) = refs
         scales = (scale_ref, past_ref, past_scale_ref)
     parts = [(outer_ref, 2), (inner_ref, 1), (mine_ref, 1)]
     low = low_lanes((TILE, TILE))
@@ -192,52 +207,54 @@
         wide_ref[rows_of(2 * pair + 1), :] = jnp.where(low, other, value).astype(wide_ref.dtype)
         if squares is not None:
             sums.append(squares)
-    send_ref[keep_ref.shape[0] :, :] = jnp.broadcast_to(squares_row(sums), (NORM_ROWS, TILE))
-    step = 4
-    for start in range(0, dense_ref.shape[0] // TILE, step):
-        product = jnp.dot(
-            dense_ref[start * TILE : (start + step) * TILE, :],
-            wide_ref[...],
-            preferred_element_type=jnp.float32,
-        )
-        for pair in range(step // 2):
-            even, odd = product[rows_of(2 * pair), :], product[rows_of(2 * pair + 1), :]
-            store_message(start // 2 + pair, jnp.where(low, even, odd), send_ref, keep_ref)
-
-
-def product_call(body, dense, operands, half, raw_rows, scratch):
-    message = jax.ShapeDtypeStruct((half + NORM_ROWS, TILE), jnp.float32)
-    kept = jax.ShapeDtypeStruct((half, TILE), jnp.float32)
-    shapes = [message, kept]
-    if raw_rows:
-        shapes.append(jax.ShapeDtypeStruct((raw_rows, TILE), jnp.float32))
+    send_ref[-NORM_ROWS:, :] = jnp.broadcast_to(squares_row(sums), (NORM_ROWS, TILE))
+    fore_pairs(dense_ref, wide_ref, send_ref, 0)
+
+
+def fore_keep_kernel(dense_ref, wide_ref, keep_ref):
+    fore_pairs(dense_ref, wide_ref, keep_ref, keep_ref.shape[0] // TILE)
+
+
+def product_call(body, dense, operands, shapes):
     return pl.pallas_call(
         body,
         in_specs=[WHOLE] * (1 + len(operands)),
         out_specs=[WHOLE] * len(shapes),
         out_shape=shapes,
-        scratch_shapes=[scratch],
         compiler_params=pltpu.CompilerParams(vmem_limit_bytes=12 * 1024 * 1024),
         cost_estimate=pl.CostEstimate(
-            flops=4 * TILE * dense.size, bytes_accessed=2 * dense.size, transcendentals=0
+            flops=2 * TILE * dense.size, bytes_accessed=dense.size, transcendentals=0
         ),
     )(dense, *operands)
 
 
+def float_rows(rows):
+    return jax.ShapeDtypeStruct((rows, TILE), jnp.float32)
+
+
 def back_product(dense, operands, first):
-    scratch = pltpu.VMEM((TILE // 2, dense.shape[0]), dense.dtype)
-    raw_rows = 0 if first else dense.shape[0] // 2
-    return product_call(
-        functools.partial(back_kernel, first), dense, operands, dense.shape[1] // 4, raw_rows, scratch
-    )
+    rows, cells = dense.shape
+    shapes = [float_rows(cells // 4 + NORM_ROWS), jax.ShapeDtypeStruct((TILE // 2, rows), dense.dtype)]
+    shapes += [] if first else [float_rows(rows // 2)]
+    send, flat, *raw = product_call(
+        functools.partial(back_send_kernel, first), dense, operands, shapes
+    )
+    (keep,) = product_call(back_keep_kernel, dense, [flat], [float_rows(cells // 4)])
+    return send, keep, *raw
 
 
 def fore_product(dense, operands, first):
-    scratch = pltpu.VMEM((dense.shape[1], TILE), dense.dtype)
-    return product_call(
-        functools.partial(fore_kernel, first),
-        dense, operands, dense.shape[0] // 4, dense.shape[1] // 2, scratch,
-    )
+    rows, cells = dense.shape
+    shapes = [
+        float_rows(rows // 4 + NORM_ROWS),
+        jax.ShapeDtypeStruct((cells, TILE), dense.dtype),
+        float_rows(cells // 2),
+    ]
+    send, wide, raw = product_call(
+        functools.partial(fore_send_kernel, first), dense, operands, shapes
+    )
+    (keep,) = product_call(fore_keep_kernel, dense, [wide], [float_rows(rows // 4)])
+    return send, keep, raw
 
 
 def rotation(norms):

time: 195 us -> 191 us (0.979)
  starting transfers between devices: 56.5 us -> 35.6 us
  waiting for transfers between devices: 98.7 us -> 112 us
  Pallas kernels: 37.5 us -> 40 us
    ppermute x30, starting transfers between devices: 50 us -> 31.2 us  [swap_rows(): return lax.ppermute(value, ('rows', 'cols'), pairs)]
    ppermute x30, waiting for transfers between devices: 91.5 us -> 104 us  [swap_rows(): return lax.ppermute(value, ('rows', 'cols'), pairs)]
    ppermute x12, starting transfers between devices: 6.48 us -> 4.46 us  [swap_cols(): lax.ppermute(value, 'cols', [(i, i ^ 1 << level) for i in range(col_count)])]
    pallas_call x10 -> x20, Pallas kernels: 29.6 us -> 31.4 us  [product_call(): pl.pallas_call(body, in_specs=[WHOLE] * (1 + len(operands)), out_specs=[W...]
  transfers between devices with their start and end apart: 42 -> 42, of which waited for: 30 -> 27; matrix products, arithmetic and copies ran while one was open for 1% -> 1% of each run, Pallas kernels for 15% -> 17%
where the time goes in v11:
time: 191 us; the launch traced here: 192 us
  waiting for transfers between devices  112 us (59%)
  Pallas kernels  40 us (21%)
  starting transfers between devices  35.6 us (19%)
    ppermute x30, waiting for transfers between devices, swap_rows(): return lax.ppermute(value, ('rows', 'cols'), pairs)  104 us
    pallas_call x20, Pallas kernels, product_call(): pl.pallas_call(body, in_specs=[WHOLE] * (1 + len(operands)), out_specs=[W...  31.4 us
    ppermute x30, starting transfers between devices, swap_rows(): return lax.ppermute(value, ('rows', 'cols'), pairs)  31.2 us
    ppermute x12, waiting for transfers between devices, swap_cols(): lax.ppermute(value, 'cols', [(i, i ^ 1 << level) for i in range(col_count)])  8.45 us
    pallas_call x1, Pallas kernels, fill_dense(): pl.pallas_call(fill_kernel, in_specs=[SCALARS] * 2 + [pl.BlockSpec(memory...  5.2 us
    ppermute x12, starting transfers between devices, swap_cols(): lax.ppermute(value, 'cols', [(i, i ^ 1 << level) for i in range(col_count)])  4.46 us
  transfers between devices with their start and end apart: 42, of which 27 were waited for; matrix products, arithmetic and copies ran while one was open for 1% of the time, Pallas kernels for 17%

profile of v11, /device:TPU:0, one launch (start us, length us, event | category | flops | bytes accessed | tf_op | source)
XLA Modules:
  0.0 191.5 jit_solution(18180886273554490382)
XLA Ops:
  0.7 5.2 %shard_map.67 = (bf16[2048,3072]{1,0:T(8,128)(2,1)S(1)}, f32[1024,128]{1,0:T(8,128)S(1)}, f32[1024,128]{1,0:T(8,128)S(1)}) custom-call(s32[24]{0:T(128)S(1)} %fusion.place_ref, s32[1]{0:T(128)} %bitcast.1.flip_ref, s32[16,16]{1,0:T(8,128)} %pattern_in.1, s32[16]{0:T(128)} %bitcast.5, f32[2048,128]{1,0:T(8,128)} %delays_in.1, bf16[16,16,128,128]{3,2,1,0:T(8,128)(2,1)} %tiles_in.1), custom_call_target="tpu_custom_call" | custom-call | bytes 8388608 | tf_op jit(solution)/shard_map/pallas_call | solution.py:87
  5.9 1.4 shard_map.68
  7.3 3.5 %collective-permute-start = (f32[776,128]{1,0:T(8,128)S(1)}, f32[776,128]{1,0:T(8,128)S(1)}, u32[]{:S(2)}, u32[]{:S(2)}) collective-permute-start(f32[776,128]{1,0:T(8,128)S(1)} %get-tuple-element.80), channel_id=1, source_target_pairs={{0,4},{1,9},{2,6},{3,11},{4,0},{5,13},{6,2},{7,15},{8,12},{9,1},{1... | collective-permute-start | bytes 1191944 | tf_op jit(solution)/shard_map/ppermute | solution.py:351
  12.0 4.5 %collective-permute-done = f32[776,128]{1,0:T(8,128)S(1)} collective-permute-done((f32[776,128]{1,0:T(8,128)S(1)}, f32[776,128]{1,0:T(8,128)S(1)}, u32[]{:S(2)}, u32[]{:S(2)}) %collective-permute-start) | collective-permute-done | bytes 397344 | tf_op jit(solution)/shard_map/ppermute | solution.py:351
  20.2 1.6 collective-permute-start.3
  22.5 2.6 %collective-permute-start.2 = (f32[392,128]{1,0:T(8,128)S(1)}, f32[392,128]{1,0:T(8,128)S(1)}, u32[]{:S(2)}, u32[]{:S(2)}) collective-permute-start(f32[392,128]{1,0:T(8,128)S(1)} %pad_maximum_fusion.11), channel_id=1, source_target_pairs={{0,16},{1,17},{2,18},{3,19},{4,20},{5,21},{6,22},{7,23},{8,24},{9,... | collective-permute-start | bytes 602120 | tf_op jit(solution)/shard_map/ppermute | solution.py:351
  25.1 3.0 %collective-permute-done.3 = f32[776,128]{1,0:T(8,128)S(1)} collective-permute-done((f32[776,128]{1,0:T(8,128)S(1)}, f32[776,128]{1,0:T(8,128)S(1)}, u32[]{:S(2)}, u32[]{:S(2)}) %collective-permute-start.3) | collective-permute-done | bytes 397344 | tf_op jit(solution)/shard_map/ppermute | solution.py:351
  29.5 4.1 %collective-permute-done.2 = f32[392,128]{1,0:T(8,128)S(1)} collective-permute-done((f32[392,128]{1,0:T(8,128)S(1)}, f32[392,128]{1,0:T(8,128)S(1)}, u32[]{:S(2)}, u32[]{:S(2)}) %collective-permute-start.2) | collective-permute-done | bytes 200736 | tf_op jit(solution)/shard_map/ppermute | solution.py:351
  34.8 2.1 %collective-permute-start.7 = (f32[392,128]{1,0:T(8,128)S(1)}, f32[392,128]{1,0:T(8,128)S(1)}, u32[]{:S(2)}, u32[]{:S(2)}) collective-permute-start(f32[392,128]{1,0:T(8,128)S(1)} %pad_maximum_fusion.13), channel_id=1, source_target_pairs={{0,16},{1,17},{2,18},{3,19},{4,20},{5,21},{6,22},{7,23},{8,24},{9,... | collective-permute-start | bytes 602120 | tf_op jit(solution)/shard_map/ppermute | solution.py:351
  36.8 2.7 %collective-permute-done.4.refs_2_ = f32[384,128]{1,0:T(8,128)S(1)} collective-permute-done((f32[384,128]{1,0:T(8,128)S(1)}, f32[384,128]{1,0:T(8,128)S(1)}, u32[]{:S(2)}, u32[]{:S(2)}) %collective-permute-start.4) | collective-permute-done | bytes 196640 | tf_op jit(solution)/shard_map/ppermute | solution.py:351
  39.6 8.6 %collective-permute-start.6 = (f32[768,128]{1,0:T(8,128)S(1)}, f32[768,128]{1,0:T(8,128)S(1)}, u32[]{:S(2)}, u32[]{:S(2)}) collective-permute-start(f32[768,128]{1,0:T(8,128)S(1)} %pad_maximum_fusion), channel_id=1, source_target_pairs={{0,4},{1,9},{2,6},{3,11},{4,0},{5,13},{6,2},{7,15},{8,12},{9,1},{1... | collective-permute-start | bytes 1179656 | tf_op jit(solution)/shard_map/ppermute | solution.py:351
  48.3 7.7 %collective-permute-done.6.refs_1_ = f32[768,128]{1,0:T(8,128)S(1)} collective-permute-done((f32[768,128]{1,0:T(8,128)S(1)}, f32[768,128]{1,0:T(8,128)S(1)}, u32[]{:S(2)}, u32[]{:S(2)}) %collective-permute-start.6) | collective-permute-done | bytes 393248 | tf_op jit(solution)/shard_map/ppermute | solution.py:351
  56.1 1.9 shard_map.72
  58.0 1.8 shard_map.73
  60.6 7.1 %collective-permute-done.11.refs_1_ = f32[768,128]{1,0:T(8,128)S(1)} collective-permute-done((f32[768,128]{1,0:T(8,128)S(1)}, f32[768,128]{1,0:T(8,128)S(1)}, u32[]{:S(2)}, u32[]{:S(2)}) %collective-permute-start.11) | collective-permute-done | bytes 393248 | tf_op jit(solution)/shard_map/ppermute | solution.py:351
  67.7 1.9 shard_map.74
  69.7 1.8 shard_map.75
  73.2 1.4 shard_map.76
  75.3 1.5 shard_map.77
  76.8 3.8 %collective-permute-done.15 = f32[520,128]{1,0:T(8,128)S(1)} collective-permute-done((f32[520,128]{1,0:T(8,128)S(1)}, f32[520,128]{1,0:T(8,128)S(1)}, u32[]{:S(2)}, u32[]{:S(2)}) %collective-permute-start.15) | collective-permute-done | bytes 266272 | tf_op jit(solution)/shard_map/ppermute | solution.py:354
  80.7 1.9 collective-permute-done.14
  82.7 1.4 shard_map.78
  86.1 4.2 %collective-permute-done.16 = f32[392,128]{1,0:T(8,128)S(1)} collective-permute-done((f32[392,128]{1,0:T(8,128)S(1)}, f32[392,128]{1,0:T(8,128)S(1)}, u32[]{:S(2)}, u32[]{:S(2)}) %collective-permute-start.16) | collective-permute-done | bytes 200736 | tf_op jit(solution)/shard_map/ppermute | solution.py:351
  90.4 1.7 collective-permute-done.19
  92.2 2.1 %collective-permute-start.21 = (f32[392,128]{1,0:T(8,128)S(1)}, f32[392,128]{1,0:T(8,128)S(1)}, u32[]{:S(2)}, u32[]{:S(2)}) collective-permute-start(f32[392,128]{1,0:T(8,128)S(1)} %pad_maximum_fusion.16), channel_id=1, source_target_pairs={{0,8},{1,5},{2,10},{3,7},{4,12},{5,1},{6,14},{7,3},{8,0},{9,13},{1... | collective-permute-start | bytes 602120 | tf_op jit(solution)/shard_map/ppermute | solution.py:351
  94.2 5.2 %collective-permute-done.18 = f32[392,128]{1,0:T(8,128)S(1)} collective-permute-done((f32[392,128]{1,0:T(8,128)S(1)}, f32[392,128]{1,0:T(8,128)S(1)}, u32[]{:S(2)}, u32[]{:S(2)}) %collective-permute-start.18) | collective-permute-done | bytes 200736 | tf_op jit(solution)/shard_map/ppermute | solution.py:351
  99.5 1.4 collective-permute-done.21
  101.4 8.6 %collective-permute-done.20.refs_2_ = f32[384,128]{1,0:T(8,128)S(1)} collective-permute-done((f32[384,128]{1,0:T(8,128)S(1)}, f32[384,128]{1,0:T(8,128)S(1)}, u32[]{:S(2)}, u32[]{:S(2)}) %collective-permute-start.20) | collective-permute-done | bytes 196640 | tf_op jit(solution)/shard_map/ppermute | solution.py:351
  111.4 6.5 %collective-permute-done.22.refs_1_ = f32[768,128]{1,0:T(8,128)S(1)} collective-permute-done((f32[768,128]{1,0:T(8,128)S(1)}, f32[768,128]{1,0:T(8,128)S(1)}, u32[]{:S(2)}, u32[]{:S(2)}) %collective-permute-start.22) | collective-permute-done | bytes 393248 | tf_op jit(solution)/shard_map/ppermute | solution.py:351
  117.9 1.9 %shard_map.80 = (f32[520,128]{1,0:T(8,128)S(1)}, bf16[3072,128]{1,0:T(8,128)(2,1)S(1)}, f32[1536,128]{1,0:T(8,128)S(1)}) custom-call(bf16[2048,3072]{1,0:T(8,128)(2,1)S(1)} %get-tuple-element.77.refs_0_.dense_ref, f32[768,128]{1,0:T(8,128)S(1)} %collective-permute-done.22.refs_1_, f32[384,128]{1,0:T(8,128)S(1)} %collective-permute-done.20.refs_2_, ...), custom_call_target="tpu_custom_call" | custom-call | flops 1610612736 | bytes 6291456 | tf_op jit(solution)/shard_map/pallas_call | solution.py:219
  119.9 1.8 shard_map.81
  123.7 5.9 %collective-permute-done.27.refs_1_ = f32[768,128]{1,0:T(8,128)S(1)} collective-permute-done((f32[768,128]{1,0:T(8,128)S(1)}, f32[768,128]{1,0:T(8,128)S(1)}, u32[]{:S(2)}, u32[]{:S(2)}) %collective-permute-start.27) | collective-permute-done | bytes 393248 | tf_op jit(solution)/shard_map/ppermute | solution.py:351
  129.6 1.9 %shard_map.82 = (f32[520,128]{1,0:T(8,128)S(1)}, bf16[3072,128]{1,0:T(8,128)(2,1)S(1)}, f32[1536,128]{1,0:T(8,128)S(1)}) custom-call(bf16[2048,3072]{1,0:T(8,128)(2,1)S(1)} %get-tuple-element.77.refs_0_.dense_ref, f32[768,128]{1,0:T(8,128)S(1)} %collective-permute-done.27.refs_1_, f32[384,128]{1,0:T(8,128)S(1)} %collective-permute-done.25.refs_2_, ...), custom_call_target="tpu_custom_call" | custom-call | flops 1610612736 | bytes 6291456 | tf_op jit(solution)/shard_map/pallas_call | solution.py:219
  131.6 1.8 shard_map.83
  134.1 1.8 collective-permute-start.31
  135.9 1.4 shard_map.84
  138.8 3.6 %collective-permute-done.31 = f32[520,128]{1,0:T(8,128)S(1)} collective-permute-done((f32[520,128]{1,0:T(8,128)S(1)}, f32[520,128]{1,0:T(8,128)S(1)}, u32[]{:S(2)}, u32[]{:S(2)}) %collective-permute-start.31) | collective-permute-done | bytes 266272 | tf_op jit(solution)/shard_map/ppermute | solution.py:354
  142.6 2.6 %collective-permute-done.30 = f32[776,128]{1,0:T(8,128)S(1)} collective-permute-done((f32[776,128]{1,0:T(8,128)S(1)}, f32[776,128]{1,0:T(8,128)S(1)}, u32[]{:S(2)}, u32[]{:S(2)}) %collective-permute-start.30) | collective-permute-done | bytes 397344 | tf_op jit(solution)/shard_map/ppermute | solution.py:351
  145.4 1.6 shard_map.86
  148.5 6.7 %collective-permute-done.32 = f32[392,128]{1,0:T(8,128)S(1)} collective-permute-done((f32[392,128]{1,0:T(8,128)S(1)}, f32[392,128]{1,0:T(8,128)S(1)}, u32[]{:S(2)}, u32[]{:S(2)}) %collective-permute-start.32) | collective-permute-done | bytes 200736 | tf_op jit(solution)/shard_map/ppermute | solution.py:351
  155.5 1.6 collective-permute-start.36
  157.1 5.0 %collective-permute-done.34 = f32[392,128]{1,0:T(8,128)S(1)} collective-permute-done((f32[392,128]{1,0:T(8,128)S(1)}, f32[392,128]{1,0:T(8,128)S(1)}, u32[]{:S(2)}, u32[]{:S(2)}) %collective-permute-start.34) | collective-permute-done | bytes 200736 | tf_op jit(solution)/shard_map/ppermute | solution.py:351
  164.8 5.1 %collective-permute-done.38.refs_1_ = f32[384,128]{1,0:T(8,128)S(1)} collective-permute-done((f32[384,128]{1,0:T(8,128)S(1)}, f32[384,128]{1,0:T(8,128)S(1)}, u32[]{:S(2)}, u32[]{:S(2)}) %collective-permute-start.38) | collective-permute-done | bytes 196640 | tf_op jit(solution)/shard_map/ppermute | solution.py:351
  169.9 4.2 %collective-permute-done.37 = f32[392,128]{1,0:T(8,128)S(1)} collective-permute-done((f32[392,128]{1,0:T(8,128)S(1)}, f32[392,128]{1,0:T(8,128)S(1)}, u32[]{:S(2)}, u32[]{:S(2)}) %collective-permute-start.37) | collective-permute-done | bytes 200736 | tf_op jit(solution)/shard_map/ppermute | solution.py:351
  174.4 7.6 %collective-permute-done.40.refs_10_ = f32[384,128]{1,0:T(8,128)S(1)} collective-permute-done((f32[384,128]{1,0:T(8,128)S(1)}, f32[384,128]{1,0:T(8,128)S(1)}, u32[]{:S(2)}, u32[]{:S(2)}) %collective-permute-start.40) | collective-permute-done | bytes 196640 | tf_op jit(solution)/shard_map/ppermute | solution.py:351
  182.1 1.7 shard_map.88
  184.3 5.5 %collective-permute-done.41.refs_9_ = f32[768,128]{1,0:T(8,128)S(1)} collective-permute-done((f32[768,128]{1,0:T(8,128)S(1)}, f32[768,128]{1,0:T(8,128)S(1)}, u32[]{:S(2)}, u32[]{:S(2)}) %collective-permute-start.41) | collective-permute-done | bytes 393248 | tf_op jit(solution)/shard_map/ppermute | solution.py:351
  189.8 1.7 shard_map.89
  (141 shorter events, 25.6 us)
Async XLA Ops:
  7.3 9.3 %collective-permute-start = (f32[776,128]{1,0:T(8,128)S(1)}, f32[776,128]{1,0:T(8,128)S(1)}, u32[]{:S(2)}, u32[]{:S(2)}) collective-permute-start(f32[776,128]{1,0:T(8,128)S(1)} %get-tuple-element.80), channel_id=1, source_target_pairs={{0,4},{1,9},{2,6},{3,11},{4,0},{5,13},{6,2},{7,15},{8,12},{9,1},{1... | collective-permute-start | bytes 1191944 | tf_op jit(solution)/shard_map/ppermute | solution.py:351
  16.6 5.8 %collective-permute-start.1 = (f32[392,128]{1,0:T(8,128)S(1)}, f32[392,128]{1,0:T(8,128)S(1)}, u32[]{:S(2)}, u32[]{:S(2)}) collective-permute-start(f32[392,128]{1,0:T(8,128)S(1)} %pad_maximum_fusion.10), channel_id=1, source_target_pairs={{0,8},{1,5},{2,10},{3,7},{4,12},{5,1},{6,14},{7,3},{8,0},{9,13},{1... | collective-permute-start | bytes 602120 | tf_op jit(solution)/shard_map/ppermute | solution.py:351
  20.2 7.9 %collective-permute-start.3 = (f32[776,128]{1,0:T(8,128)S(1)}, f32[776,128]{1,0:T(8,128)S(1)}, u32[]{:S(2)}, u32[]{:S(2)}) collective-permute-start(f32[776,128]{1,0:T(8,128)S(1)} %get-tuple-element.84), channel_id=1, source_target_pairs={{0,4},{1,9},{2,6},{3,11},{4,0},{5,13},{6,2},{7,15},{8,12},{9,1},{1... | collective-permute-start | bytes 1191944 | tf_op jit(solution)/shard_map/ppermute | solution.py:351
  22.5 11.1 %collective-permute-start.2 = (f32[392,128]{1,0:T(8,128)S(1)}, f32[392,128]{1,0:T(8,128)S(1)}, u32[]{:S(2)}, u32[]{:S(2)}) collective-permute-start(f32[392,128]{1,0:T(8,128)S(1)} %pad_maximum_fusion.11), channel_id=1, source_target_pairs={{0,16},{1,17},{2,18},{3,19},{4,20},{5,21},{6,22},{7,23},{8,24},{9,... | collective-permute-start | bytes 602120 | tf_op jit(solution)/shard_map/ppermute | solution.py:351
  28.2 6.5 %collective-permute-start.5 = (f32[392,128]{1,0:T(8,128)S(1)}, f32[392,128]{1,0:T(8,128)S(1)}, u32[]{:S(2)}, u32[]{:S(2)}) collective-permute-start(f32[392,128]{1,0:T(8,128)S(1)} %pad_maximum_fusion.12), channel_id=1, source_target_pairs={{0,8},{1,5},{2,10},{3,7},{4,12},{5,1},{6,14},{7,3},{8,0},{9,13},{1... | collective-permute-start | bytes 602120 | tf_op jit(solution)/shard_map/ppermute | solution.py:351
  33.6 6.0 %collective-permute-start.4 = (f32[384,128]{1,0:T(8,128)S(1)}, f32[384,128]{1,0:T(8,128)S(1)}, u32[]{:S(2)}, u32[]{:S(2)}) collective-permute-start(f32[384,128]{1,0:T(8,128)S(1)} %slice_add_fusion.25.refs_3_), channel_id=1, source_target_pairs={{0,8},{1,5},{2,10},{3,7},{4,12},{5,1},{6,14},{7,3},{8,0},{9,13},{1... | collective-permute-start | bytes 589832 | tf_op jit(solution)/shard_map/ppermute | solution.py:351
  34.8 13.4 %collective-permute-start.7 = (f32[392,128]{1,0:T(8,128)S(1)}, f32[392,128]{1,0:T(8,128)S(1)}, u32[]{:S(2)}, u32[]{:S(2)}) collective-permute-start(f32[392,128]{1,0:T(8,128)S(1)} %pad_maximum_fusion.13), channel_id=1, source_target_pairs={{0,16},{1,17},{2,18},{3,19},{4,20},{5,21},{6,22},{7,23},{8,24},{9,... | collective-permute-start | bytes 602120 | tf_op jit(solution)/shard_map/ppermute | solution.py:351
  39.6 16.5 %collective-permute-start.6 = (f32[768,128]{1,0:T(8,128)S(1)}, f32[768,128]{1,0:T(8,128)S(1)}, u32[]{:S(2)}, u32[]{:S(2)}) collective-permute-start(f32[768,128]{1,0:T(8,128)S(1)} %pad_maximum_fusion), channel_id=1, source_target_pairs={{0,4},{1,9},{2,6},{3,11},{4,0},{5,13},{6,2},{7,15},{8,12},{9,1},{1... | collective-permute-start | bytes 1179656 | tf_op jit(solution)/shard_map/ppermute | solution.py:351
  48.2 11.6 %collective-permute-start.9 = (f32[384,128]{1,0:T(8,128)S(1)}, f32[384,128]{1,0:T(8,128)S(1)}, u32[]{:S(2)}, u32[]{:S(2)}) collective-permute-start(f32[384,128]{1,0:T(8,128)S(1)} %slice_add_fusion.24.refs_3_), channel_id=1, source_target_pairs={{0,8},{1,5},{2,10},{3,7},{4,12},{5,1},{6,14},{7,3},{8,0},{9,13},{1... | collective-permute-start | bytes 589832 | tf_op jit(solution)/shard_map/ppermute | solution.py:351
  57.9 2.5 %collective-permute-start.8 = (f32[520,128]{1,0:T(8,128)S(1)}, f32[520,128]{1,0:T(8,128)S(1)}, u32[]{:S(2)}, u32[]{:S(2)}) collective-permute-start(f32[520,128]{1,0:T(8,128)S(1)} %get-tuple-element.95), channel_id=1, source_target_pairs={{0,1},{1,0},{2,3},{3,2},{4,5},{5,4},{6,7},{7,6},{8,9},{9,8},{10,11... | collective-permute-start | bytes 798728 | tf_op jit(solution)/shard_map/ppermute | solution.py:354
  59.9 7.8 %collective-permute-start.11 = (f32[768,128]{1,0:T(8,128)S(1)}, f32[768,128]{1,0:T(8,128)S(1)}, u32[]{:S(2)}, u32[]{:S(2)}) collective-permute-start(f32[768,128]{1,0:T(8,128)S(1)} %pad_maximum_fusion.1), channel_id=1, source_target_pairs={{0,4},{1,9},{2,6},{3,11},{4,0},{5,13},{6,2},{7,15},{8,12},{9,1},{1... | collective-permute-start | bytes 1179656 | tf_op jit(solution)/shard_map/ppermute | solution.py:351
  60.5 10.9 %collective-permute-start.10 = (f32[520,128]{1,0:T(8,128)S(1)}, f32[520,128]{1,0:T(8,128)S(1)}, u32[]{:S(2)}, u32[]{:S(2)}) collective-permute-start(f32[520,128]{1,0:T(8,128)S(1)} %pad_maximum_fusion.6), channel_id=1, source_target_pairs={{0,2},{1,3},{2,0},{3,1},{4,6},{5,7},{6,4},{7,5},{8,10},{9,11},{10,... | collective-permute-start | bytes 798728 | tf_op jit(solution)/shard_map/ppermute | solution.py:354
  69.6 2.5 %collective-permute-start.13 = (f32[520,128]{1,0:T(8,128)S(1)}, f32[520,128]{1,0:T(8,128)S(1)}, u32[]{:S(2)}, u32[]{:S(2)}) collective-permute-start(f32[520,128]{1,0:T(8,128)S(1)} %get-tuple-element.99), channel_id=1, source_target_pairs={{0,1},{1,0},{2,3},{3,2},{4,5},{5,4},{6,7},{7,6},{8,9},{9,8},{10,11... | collective-permute-start | bytes 798728 | tf_op jit(solution)/shard_map/ppermute | solution.py:354
  71.5 1.7 collective-permute-start.12
  72.1 8.4 %collective-permute-start.15 = (f32[520,128]{1,0:T(8,128)S(1)}, f32[520,128]{1,0:T(8,128)S(1)}, u32[]{:S(2)}, u32[]{:S(2)}) collective-permute-start(f32[520,128]{1,0:T(8,128)S(1)} %pad_maximum_fusion.7), channel_id=1, source_target_pairs={{0,2},{1,3},{2,0},{3,1},{4,6},{5,7},{6,4},{7,5},{8,10},{9,11},{10,... | collective-permute-start | bytes 798728 | tf_op jit(solution)/shard_map/ppermute | solution.py:354
  74.7 7.9 %collective-permute-start.14 = (f32[776,128]{1,0:T(8,128)S(1)}, f32[776,128]{1,0:T(8,128)S(1)}, u32[]{:S(2)}, u32[]{:S(2)}) collective-permute-start(f32[776,128]{1,0:T(8,128)S(1)} %get-tuple-element.105), channel_id=1, source_target_pairs={{0,4},{1,9},{2,6},{3,11},{4,0},{5,13},{6,2},{7,15},{8,12},{9,1},{1... | collective-permute-start | bytes 1191944 | tf_op jit(solution)/shard_map/ppermute | solution.py:351
  80.6 2.2 %collective-permute-start.17 = (f32[512,128]{1,0:T(8,128)S(1)}, f32[512,128]{1,0:T(8,128)S(1)}, u32[]{:S(2)}, u32[]{:S(2)}) collective-permute-start(f32[512,128]{1,0:T(8,128)S(1)} %slice_add_fusion.10.refs_2_), channel_id=1, source_target_pairs={{0,1},{1,0},{2,3},{3,2},{4,5},{5,4},{6,7},{7,6},{8,9},{9,8},{10,11... | collective-permute-start | bytes 786440 | tf_op jit(solution)/shard_map/ppermute | solution.py:354
  82.7 7.6 %collective-permute-start.16 = (f32[392,128]{1,0:T(8,128)S(1)}, f32[392,128]{1,0:T(8,128)S(1)}, u32[]{:S(2)}, u32[]{:S(2)}) collective-permute-start(f32[392,128]{1,0:T(8,128)S(1)} %pad_maximum_fusion.14), channel_id=1, source_target_pairs={{0,8},{1,5},{2,10},{3,7},{4,12},{5,1},{6,14},{7,3},{8,0},{9,13},{1... | collective-permute-start | bytes 602120 | tf_op jit(solution)/shard_map/ppermute | solution.py:351
  84.2 7.9 %collective-permute-start.19 = (f32[776,128]{1,0:T(8,128)S(1)}, f32[776,128]{1,0:T(8,128)S(1)}, u32[]{:S(2)}, u32[]{:S(2)}) collective-permute-start(f32[776,128]{1,0:T(8,128)S(1)} %get-tuple-element.109), channel_id=1, source_target_pairs={{0,4},{1,9},{2,6},{3,11},{4,0},{5,13},{6,2},{7,15},{8,12},{9,1},{1... | collective-permute-start | bytes 1191944 | tf_op jit(solution)/shard_map/ppermute | solution.py:351
  90.3 9.1 %collective-permute-start.18 = (f32[392,128]{1,0:T(8,128)S(1)}, f32[392,128]{1,0:T(8,128)S(1)}, u32[]{:S(2)}, u32[]{:S(2)}) collective-permute-start(f32[392,128]{1,0:T(8,128)S(1)} %pad_maximum_fusion.15), channel_id=1, source_target_pairs={{0,16},{1,17},{2,18},{3,19},{4,20},{5,21},{6,22},{7,23},{8,24},{9,... | collective-permute-start | bytes 602120 | tf_op jit(solution)/shard_map/ppermute | solution.py:351
  92.2 8.8 %collective-permute-start.21 = (f32[392,128]{1,0:T(8,128)S(1)}, f32[392,128]{1,0:T(8,128)S(1)}, u32[]{:S(2)}, u32[]{:S(2)}) collective-permute-start(f32[392,128]{1,0:T(8,128)S(1)} %pad_maximum_fusion.16), channel_id=1, source_target_pairs={{0,8},{1,5},{2,10},{3,7},{4,12},{5,1},{6,14},{7,3},{8,0},{9,13},{1... | collective-permute-start | bytes 602120 | tf_op jit(solution)/shard_map/ppermute | solution.py:351
  99.5 10.6 %collective-permute-start.20 = (f32[384,128]{1,0:T(8,128)S(1)}, f32[384,128]{1,0:T(8,128)S(1)}, u32[]{:S(2)}, u32[]{:S(2)}) collective-permute-start(f32[384,128]{1,0:T(8,128)S(1)} %slice_add_fusion.23.refs_3_), channel_id=1, source_target_pairs={{0,8},{1,5},{2,10},{3,7},{4,12},{5,1},{6,14},{7,3},{8,0},{9,13},{1... | collective-permute-start | bytes 589832 | tf_op jit(solution)/shard_map/ppermute | solution.py:351
  101.0 10.0 %collective-permute-start.23 = (f32[392,128]{1,0:T(8,128)S(1)}, f32[392,128]{1,0:T(8,128)S(1)}, u32[]{:S(2)}, u32[]{:S(2)}) collective-permute-start(f32[392,128]{1,0:T(8,128)S(1)} %pad_maximum_fusion.17), channel_id=1, source_target_pairs={{0,16},{1,17},{2,18},{3,19},{4,20},{5,21},{6,22},{7,23},{8,24},{9,... | collective-permute-start | bytes 602120 | tf_op jit(solution)/shard_map/ppermute | solution.py:351
  110.1 7.8 %collective-permute-start.22 = (f32[768,128]{1,0:T(8,128)S(1)}, f32[768,128]{1,0:T(8,128)S(1)}, u32[]{:S(2)}, u32[]{:S(2)}) collective-permute-start(f32[768,128]{1,0:T(8,128)S(1)} %pad_maximum_fusion.2), channel_id=1, source_target_pairs={{0,4},{1,9},{2,6},{3,11},{4,0},{5,13},{6,2},{7,15},{8,12},{9,1},{1... | collective-permute-start | bytes 1179656 | tf_op jit(solution)/shard_map/ppermute | solution.py:351
  111.0 10.7 %collective-permute-start.25 = (f32[384,128]{1,0:T(8,128)S(1)}, f32[384,128]{1,0:T(8,128)S(1)}, u32[]{:S(2)}, u32[]{:S(2)}) collective-permute-start(f32[384,128]{1,0:T(8,128)S(1)} %slice_add_fusion.22.refs_3_), channel_id=1, source_target_pairs={{0,8},{1,5},{2,10},{3,7},{4,12},{5,1},{6,14},{7,3},{8,0},{9,13},{1... | collective-permute-start | bytes 589832 | tf_op jit(solution)/shard_map/ppermute | solution.py:351
  119.8 2.9 %collective-permute-start.24 = (f32[520,128]{1,0:T(8,128)S(1)}, f32[520,128]{1,0:T(8,128)S(1)}, u32[]{:S(2)}, u32[]{:S(2)}) collective-permute-start(f32[520,128]{1,0:T(8,128)S(1)} %get-tuple-element.119), channel_id=1, source_target_pairs={{0,1},{1,0},{2,3},{3,2},{4,5},{5,4},{6,7},{7,6},{8,9},{9,8},{10,11... | collective-permute-start | bytes 798728 | tf_op jit(solution)/shard_map/ppermute | solution.py:354
  121.7 7.8 %collective-permute-start.27 = (f32[768,128]{1,0:T(8,128)S(1)}, f32[768,128]{1,0:T(8,128)S(1)}, u32[]{:S(2)}, u32[]{:S(2)}) collective-permute-start(f32[768,128]{1,0:T(8,128)S(1)} %pad_maximum_fusion.3), channel_id=1, source_target_pairs={{0,4},{1,9},{2,6},{3,11},{4,0},{5,13},{6,2},{7,15},{8,12},{9,1},{1... | collective-permute-start | bytes 1179656 | tf_op jit(solution)/shard_map/ppermute | solution.py:351
  122.8 10.6 %collective-permute-start.26 = (f32[520,128]{1,0:T(8,128)S(1)}, f32[520,128]{1,0:T(8,128)S(1)}, u32[]{:S(2)}, u32[]{:S(2)}) collective-permute-start(f32[520,128]{1,0:T(8,128)S(1)} %pad_maximum_fusion.8), channel_id=1, source_target_pairs={{0,2},{1,3},{2,0},{3,1},{4,6},{5,7},{6,4},{7,5},{8,10},{9,11},{10,... | collective-permute-start | bytes 798728 | tf_op jit(solution)/shard_map/ppermute | solution.py:354
  131.5 2.5 %collective-permute-start.29 = (f32[520,128]{1,0:T(8,128)S(1)}, f32[520,128]{1,0:T(8,128)S(1)}, u32[]{:S(2)}, u32[]{:S(2)}) collective-permute-start(f32[520,128]{1,0:T(8,128)S(1)} %get-tuple-element.125), channel_id=1, source_target_pairs={{0,1},{1,0},{2,3},{3,2},{4,5},{5,4},{6,7},{7,6},{8,9},{9,8},{10,11... | collective-permute-start | bytes 798728 | tf_op jit(solution)/shard_map/ppermute | solution.py:354
  133.4 2.5 %collective-permute-start.28 = (f32[512,128]{1,0:T(8,128)S(1)}, f32[512,128]{1,0:T(8,128)S(1)}, u32[]{:S(2)}, u32[]{:S(2)}) collective-permute-start(f32[512,128]{1,0:T(8,128)S(1)} %slice_add_fusion.8.refs_2_), channel_id=1, source_target_pairs={{0,1},{1,0},{2,3},{3,2},{4,5},{5,4},{6,7},{7,6},{8,9},{9,8},{10,11... | collective-permute-start | bytes 786440 | tf_op jit(solution)/shard_map/ppermute | solution.py:354
  134.1 8.4 %collective-permute-start.31 = (f32[520,128]{1,0:T(8,128)S(1)}, f32[520,128]{1,0:T(8,128)S(1)}, u32[]{:S(2)}, u32[]{:S(2)}) collective-permute-start(f32[520,128]{1,0:T(8,128)S(1)} %pad_maximum_fusion.9), channel_id=1, source_target_pairs={{0,2},{1,3},{2,0},{3,1},{4,6},{5,7},{6,4},{7,5},{8,10},{9,11},{10,... | collective-permute-start | bytes 798728 | tf_op jit(solution)/shard_map/ppermute | solution.py:354
  137.3 7.9 %collective-permute-start.30 = (f32[776,128]{1,0:T(8,128)S(1)}, f32[776,128]{1,0:T(8,128)S(1)}, u32[]{:S(2)}, u32[]{:S(2)}) collective-permute-start(f32[776,128]{1,0:T(8,128)S(1)} %get-tuple-element.131), channel_id=1, source_target_pairs={{0,4},{1,9},{2,6},{3,11},{4,0},{5,13},{6,2},{7,15},{8,12},{9,1},{1... | collective-permute-start | bytes 1191944 | tf_op jit(solution)/shard_map/ppermute | solution.py:351
  142.5 2.9 %collective-permute-start.33 = (f32[512,128]{1,0:T(8,128)S(1)}, f32[512,128]{1,0:T(8,128)S(1)}, u32[]{:S(2)}, u32[]{:S(2)}) collective-permute-start(f32[512,128]{1,0:T(8,128)S(1)} %slice_add_fusion.6.refs_2_), channel_id=1, source_target_pairs={{0,1},{1,0},{2,3},{3,2},{4,5},{5,4},{6,7},{7,6},{8,9},{9,8},{10,11... | collective-permute-start | bytes 786440 | tf_op jit(solution)/shard_map/ppermute | solution.py:354
  145.3 10.0 %collective-permute-start.32 = (f32[392,128]{1,0:T(8,128)S(1)}, f32[392,128]{1,0:T(8,128)S(1)}, u32[]{:S(2)}, u32[]{:S(2)}) collective-permute-start(f32[392,128]{1,0:T(8,128)S(1)} %pad_maximum_fusion.18), channel_id=1, source_target_pairs={{0,8},{1,5},{2,10},{3,7},{4,12},{5,1},{6,14},{7,3},{8,0},{9,13},{1... | collective-permute-start | bytes 602120 | tf_op jit(solution)/shard_map/ppermute | solution.py:351
  147.0 8.4 %collective-permute-start.35 = (f32[776,128]{1,0:T(8,128)S(1)}, f32[776,128]{1,0:T(8,128)S(1)}, u32[]{:S(2)}, u32[]{:S(2)}) collective-permute-start(f32[776,128]{1,0:T(8,128)S(1)} %get-tuple-element.137), channel_id=1, source_target_pairs={{0,4},{1,9},{2,6},{3,11},{4,0},{5,13},{6,2},{7,15},{8,12},{9,1},{1... | collective-permute-start | bytes 1191944 | tf_op jit(solution)/shard_map/ppermute | solution.py:351
  155.3 6.8 %collective-permute-start.34 = (f32[392,128]{1,0:T(8,128)S(1)}, f32[392,128]{1,0:T(8,128)S(1)}, u32[]{:S(2)}, u32[]{:S(2)}) collective-permute-start(f32[392,128]{1,0:T(8,128)S(1)} %pad_maximum_fusion.19), channel_id=1, source_target_pairs={{0,16},{1,17},{2,18},{3,19},{4,20},{5,21},{6,22},{7,23},{8,24},{9,... | collective-permute-start | bytes 602120 | tf_op jit(solution)/shard_map/ppermute | solution.py:351
  155.5 7.9 %collective-permute-start.36 = (f32[392,128]{1,0:T(8,128)S(1)}, f32[392,128]{1,0:T(8,128)S(1)}, u32[]{:S(2)}, u32[]{:S(2)}) collective-permute-start(f32[392,128]{1,0:T(8,128)S(1)} %pad_maximum_fusion.20), channel_id=1, source_target_pairs={{0,8},{1,5},{2,10},{3,7},{4,12},{5,1},{6,14},{7,3},{8,0},{9,13},{1... | collective-permute-start | bytes 602120 | tf_op jit(solution)/shard_map/ppermute | solution.py:351
  162.1 7.7 %collective-permute-start.38 = (f32[384,128]{1,0:T(8,128)S(1)}, f32[384,128]{1,0:T(8,128)S(1)}, u32[]{:S(2)}, u32[]{:S(2)}) collective-permute-start(f32[384,128]{1,0:T(8,128)S(1)} %slice_add_fusion.21.refs_2_), channel_id=1, source_target_pairs={{0,8},{1,5},{2,10},{3,7},{4,12},{5,1},{6,14},{7,3},{8,0},{9,13},{1... | collective-permute-start | bytes 589832 | tf_op jit(solution)/shard_map/ppermute | solution.py:351
  163.5 10.5 %collective-permute-start.37 = (f32[392,128]{1,0:T(8,128)S(1)}, f32[392,128]{1,0:T(8,128)S(1)}, u32[]{:S(2)}, u32[]{:S(2)}) collective-permute-start(f32[392,128]{1,0:T(8,128)S(1)} %pad_maximum_fusion.21), channel_id=1, source_target_pairs={{0,16},{1,17},{2,18},{3,19},{4,20},{5,21},{6,22},{7,23},{8,24},{9,... | collective-permute-start | bytes 602120 | tf_op jit(solution)/shard_map/ppermute | solution.py:351
  174.1 7.9 %collective-permute-start.40 = (f32[384,128]{1,0:T(8,128)S(1)}, f32[384,128]{1,0:T(8,128)S(1)}, u32[]{:S(2)}, u32[]{:S(2)}) collective-permute-start(f32[384,128]{1,0:T(8,128)S(1)} %slice_add_fusion.20.refs_11_), channel_id=1, source_target_pairs={{0,8},{1,5},{2,10},{3,7},{4,12},{5,1},{6,14},{7,3},{8,0},{9,13},{1... | collective-permute-start | bytes 589832 | tf_op jit(solution)/shard_map/ppermute | solution.py:351
  174.2 10.2 %collective-permute-start.39 = (f32[768,128]{1,0:T(8,128)S(1)}, f32[768,128]{1,0:T(8,128)S(1)}, u32[]{:S(2)}, u32[]{:S(2)}) collective-permute-start(f32[768,128]{1,0:T(8,128)S(1)} %pad_maximum_fusion.4), channel_id=1, source_target_pairs={{0,4},{1,9},{2,6},{3,11},{4,0},{5,13},{6,2},{7,15},{8,12},{9,1},{1... | collective-permute-start | bytes 1179656 | tf_op jit(solution)/shard_map/ppermute | solution.py:351
  182.0 7.8 %collective-permute-start.41 = (f32[768,128]{1,0:T(8,128)S(1)}, f32[768,128]{1,0:T(8,128)S(1)}, u32[]{:S(2)}, u32[]{:S(2)}) collective-permute-start(f32[768,128]{1,0:T(8,128)S(1)} %pad_maximum_fusion.5), channel_id=1, source_target_pairs={{0,4},{1,9},{2,6},{3,11},{4,0},{5,13},{6,2},{7,15},{8,12},{9,1},{1... | collective-permute-start | bytes 1179656 | tf_op jit(solution)/shard_map/ppermute | solution.py:351

commit v12 on v11

--- a/solution.py
+++ b/solution.py
@@ -190,12 +190,19 @@
             out_ref[rows_of(pair + i), :] = jnp.where(low, even, odd)
 
 
+def pair_rows(unit_ref, pair, rows):
+    pairs = rows // PAIR // UNITS
+    start = (unit_ref[pair // pairs] * pairs + pair % pairs) * PAIR
+    return [pl.ds(pl.multiple_of(start + half * TILE, TILE), TILE) for half in range(2)]
+
+
 def fore_send_kernel(first, *refs):
     if first:
-        (dense_ref, outer_ref, inner_ref, mine_ref, scale_ref, send_ref, wide_ref, raw_ref) = refs
+        (dense_ref, unit_ref, outer_ref, inner_ref, mine_ref, scale_ref,
+         send_ref, wide_ref, raw_ref) = refs
         scales = (scale_ref, None, None)
     else:
-        (dense_ref, outer_ref, inner_ref, mine_ref, scale_ref, past_ref, past_scale_ref,
+        (dense_ref, unit_ref, outer_ref, inner_ref, mine_ref, scale_ref, past_ref, past_scale_ref,
          send_ref, wide_ref, raw_ref) = refs
         scales = (scale_ref, past_ref, past_scale_ref)
     parts = [(outer_ref, 2), (inner_ref, 1), (mine_ref, 1)]
@@ -203,8 +210,9 @@
     sums = []
     for pair, value, squares in next_vector(parts, raw_ref, *scales):
         other = turned(value)
-        wide_ref[rows_of(2 * pair), :] = jnp.where(low, value, other).astype(wide_ref.dtype)
-        wide_ref[rows_of(2 * pair + 1), :] = jnp.where(low, other, value).astype(wide_ref.dtype)
+        even, odd = pair_rows(unit_ref, pair, wide_ref.shape[0])
+        wide_ref[even, :] = jnp.where(low, value, other).astype(wide_ref.dtype)
+        wide_ref[odd, :] = jnp.where(low, other, value).astype(wide_ref.dtype)
         if squares is not None:
             sums.append(squares)
     send_ref[-NORM_ROWS:, :] = jnp.broadcast_to(squares_row(sums), (NORM_ROWS, TILE))
@@ -215,17 +223,18 @@
     fore_pairs(dense_ref, wide_ref, keep_ref, keep_ref.shape[0] // TILE)
 
 
-def product_call(body, dense, operands, shapes):
+def product_call(body, dense, operands, shapes, units=None):
+    scalars = [] if units is None else [units]
     return pl.pallas_call(
         body,
-        in_specs=[WHOLE] * (1 + len(operands)),
+        in_specs=[WHOLE] + [SCALARS] * len(scalars) + [WHOLE] * len(operands),
         out_specs=[WHOLE] * len(shapes),
         out_shape=shapes,
         compiler_params=pltpu.CompilerParams(vmem_limit_bytes=12 * 1024 * 1024),
         cost_estimate=pl.CostEstimate(
             flops=2 * TILE * dense.size, bytes_accessed=dense.size, transcendentals=0
         ),
-    )(dense, *operands)
+    )(dense, *scalars, *operands)
 
 
 def float_rows(rows):
@@ -243,7 +252,7 @@
     return send, keep, *raw
 
 
-def fore_product(dense, operands, first):
+def fore_product(dense, units, operands, first):
     rows, cells = dense.shape
     shapes = [
         float_rows(rows // 4 + NORM_ROWS),
@@ -251,7 +260,7 @@
         float_rows(cells // 2),
     ]
     send, wide, raw = product_call(
-        functools.partial(fore_send_kernel, first), dense, operands, shapes
+        functools.partial(fore_send_kernel, first), dense, operands, shapes, units
     )
     (keep,) = product_call(fore_keep_kernel, dense, [wide], [float_rows(rows // 4)])
     return send, keep, raw
@@ -276,17 +285,14 @@
     return alphas, betas, steps, misfit, misfit * rotate_cos
 
 
-def store_in_order(out_ref, mask, pair, low, values):
-    pairs = out_ref.shape[0] // PAIR // UNITS
-    start = (((pair // pairs) ^ mask) * pairs + pair % pairs) * PAIR
+def store_in_order(out_ref, unit_ref, pair, low, values):
     ours, theirs = values
-    even = pl.ds(pl.multiple_of(start, TILE), TILE)
-    odd = pl.ds(pl.multiple_of(start + TILE, TILE), TILE)
+    even, odd = pair_rows(unit_ref, pair, out_ref.shape[0])
     out_ref[even, :] = jnp.where(low, ours, turned(theirs))
     out_ref[odd, :] = jnp.where(low, turned(ours), theirs)
 
 
-def model_kernel(count, mask_ref, *refs):
+def model_kernel(count, unit_ref, *refs):
     ins, (model_ref, misfit_ref) = refs[:-2], refs[-2:]
     chains = [ins[: len(ins) // 2], ins[len(ins) // 2 :]]
     low = low_lanes((TILE, TILE))
@@ -302,10 +308,10 @@
                 search = right if j == 0 else right - steps[j - 1][1] * search
                 total = steps[j][0] * search if j == 0 else total + steps[j][0] * search
             values.append(total)
-        store_in_order(model_ref, mask_ref[0], pair, low, values)
-
-
-def gradient_kernel(mask_ref, *refs):
+        store_in_order(model_ref, unit_ref, pair, low, values)
+
+
+def gradient_kernel(unit_ref, *refs):
     ins, gradient_ref = refs[:-1], refs[-1]
     chains = [ins[: len(ins) // 2], ins[len(ins) // 2 :]]
     low = low_lanes((TILE, TILE))
@@ -318,10 +324,10 @@
         factors.append(factor)
     for ours, theirs in zip(*vectors):
         values = [factors[0] * ours[1], factors[1] * theirs[1]]
-        store_in_order(gradient_ref, mask_ref[0], ours[0], low, values)
-
-
-def last_call(body, mask, operands, shapes):
+        store_in_order(gradient_ref, unit_ref, ours[0], low, values)
+
+
+def last_call(body, units, operands, shapes):
     return pl.pallas_call(
         body,
         in_specs=[SCALARS] + [WHOLE] * len(operands),
@@ -331,7 +337,7 @@
         cost_estimate=pl.CostEstimate(
             flops=0, bytes_accessed=8 * shapes[0][0] * TILE, transcendentals=0
         ),
-    )(mask, *operands)
+    )(units, *operands)
 
 
 def on_device(row_count, col_count, kernel, pattern, counts, delays):
@@ -340,7 +346,9 @@
     row_index = lax.axis_index("rows")
     core = lax.axis_index("cols") & 1
 
-    orders = [row_bits, [row_bits[1], row_bits[0], *row_bits[2:]]]
+    near, far, *rest = row_bits
+    orders = [[near, far, *rest, far, near], [far, near, *rest, far, near]]
+    steps = len(orders[0])
 
     def swap_rows(value, level):
         pairs = []
@@ -361,7 +369,8 @@
     unit = CB_DEV // UNITS
     places = ((blocks // unit) ^ mask) * unit + blocks % unit
     flip = ((1 - core) * (kernel.shape[0] // 2)).astype(jnp.int32).reshape(1)
-    mask = mask.reshape(1)
+    units = jnp.where(core == 0, jnp.array([0, 1, 2, 3]), jnp.array([0, 2, 1, 3])).astype(jnp.int32)
+    own_units = units ^ mask
 
     dense, *lefts = fill_dense(kernel, pattern, counts, places, flip, delays)
 
@@ -375,8 +384,8 @@
             got = yield swap_rows, jnp.concatenate([send, norm]), level
             norm = norm + got[half // 2 :]
             send = mine = mine + got[: half // 2]
-        inner = yield swap_rows, mine, 1
-        outer = yield swap_rows, jnp.concatenate([inner, mine]), 0
+        inner = yield swap_rows, mine, steps - 2
+        outer = yield swap_rows, jnp.concatenate([inner, mine]), steps - 1
         return [outer, inner, mine], norm
 
     def reduce_cols(send, keep):
@@ -398,7 +407,7 @@
         rights = []
         for iteration in range(ITERS):
             past = [rights[-1], norms[-2]] if rights else []
-            send, keep, right = fore_product(dense, [*totals, norms[-1], *past], not rights)
+            send, keep, right = fore_product(dense, units, [*totals, norms[-1], *past], not rights)
             rights.append(right)
             halves, norm = yield from reduce_cols(send, keep)
             norms.append(norm)
@@ -438,13 +447,13 @@
     cells = dense.shape[1]
     model, misfit = last_call(
         functools.partial(model_kernel, ITERS),
-        mask,
+        own_units,
         [operand for rights, norms, _ in chains for operand in [*rights, *norms]],
         [(cells, TILE), (NORM_ROWS, TILE)],
     )
     (gradient,) = last_call(
         gradient_kernel,
-        mask,
+        own_units,
         [operand for rights, norms, totals in chains for operand in [*totals, rights[-1], *norms]],
         [(cells, TILE)],
     )

time: 191 us -> 198 us (1.037)
  starting transfers between devices: 35.6 us -> 40.9 us
  Pallas kernels: 40 us -> 42.9 us
  waiting for transfers between devices: 112 us -> 110 us
    ppermute x30, starting transfers between devices: 31.2 us -> 34.6 us  [swap_rows(): return lax.ppermute(value, ('rows', 'cols'), pairs)]
    pallas_call x20, Pallas kernels: 31.4 us -> 34.1 us  [product_call(): pl.pallas_call(body, in_specs=[WHOLE] + [SCALARS] * len(scalars) + [WHOLE...]
    ppermute x12, waiting for transfers between devices: 8.45 us -> 6.28 us  [swap_cols(): lax.ppermute(value, 'cols', [(i, i ^ 1 << level) for i in range(col_count)])]
  transfers between devices with their start and end apart: 42 -> 42, of which waited for: 27 -> 28; matrix products, arithmetic and copies ran while one was open for 1% -> 1% of each run, Pallas kernels for 17% -> 18%
where the time goes in v12:
time: 198 us; the launch traced here: 197 us
  waiting for transfers between devices  110 us (56%)
  Pallas kernels  42.9 us (22%)
  starting transfers between devices  40.9 us (21%)
    ppermute x30, waiting for transfers between devices, swap_rows(): return lax.ppermute(value, ('rows', 'cols'), pairs)  104 us
    ppermute x30, starting transfers between devices, swap_rows(): return lax.ppermute(value, ('rows', 'cols'), pairs)  34.6 us
    pallas_call x20, Pallas kernels, product_call(): pl.pallas_call(body, in_specs=[WHOLE] + [SCALARS] * len(scalars) + [WHOLE...  34.1 us
    ppermute x12, waiting for transfers between devices, swap_cols(): lax.ppermute(value, 'cols', [(i, i ^ 1 << level) for i in range(col_count)])  6.28 us
    ppermute x12, starting transfers between devices, swap_cols(): lax.ppermute(value, 'cols', [(i, i ^ 1 << level) for i in range(col_count)])  6.27 us
    pallas_call x2, Pallas kernels, last_call(): pl.pallas_call(body, in_specs=[SCALARS] + [WHOLE] * len(operands), out_sp...  4.47 us
    pallas_call x1, Pallas kernels, fill_dense(): pl.pallas_call(fill_kernel, in_specs=[SCALARS] * 2 + [pl.BlockSpec(memory...  4.4 us
  transfers between devices with their start and end apart: 42, of which 28 were waited for; matrix products, arithmetic and copies ran while one was open for 1% of the time, Pallas kernels for 18%

profile of v12, /device:TPU:0, one launch (start us, length us, event | category | flops | bytes accessed | tf_op | source)
XLA Modules:
  0.0 197.3 jit_solution(7072850088537535558)
XLA Ops:
  0.7 4.4 %shard_map.85 = (bf16[2048,3072]{1,0:T(8,128)(2,1)S(1)}, f32[1024,128]{1,0:T(8,128)S(1)}, f32[1024,128]{1,0:T(8,128)S(1)}) custom-call(s32[24]{0:T(128)S(1)} %fusion.place_ref, s32[1]{0:T(128)} %bitcast.flip_ref, s32[16,16]{1,0:T(8,128)} %pattern_in.1, s32[16]{0:T(128)} %bitcast.4, f32[2048,128]{1,0:T(8,128)} %delays_in.1, bf16[16,16,128,128]{3,2,1,0:T(8,128)(2,1)} %tiles_in.1), custom_call_target="tpu_custom_call" | custom-call | bytes 8388608 | tf_op jit(solution)/shard_map/pallas_call | solution.py:87
  6.5 4.3 %collective-permute-start = (f32[776,128]{1,0:T(8,128)S(1)}, f32[776,128]{1,0:T(8,128)S(1)}, u32[]{:S(2)}, u32[]{:S(2)}) collective-permute-start(f32[776,128]{1,0:T(8,128)S(1)} %get-tuple-element.80), channel_id=1, source_target_pairs={{0,4},{1,9},{2,6},{3,11},{4,0},{5,13},{6,2},{7,15},{8,12},{9,1},{1... | collective-permute-start | bytes 1191944 | tf_op jit(solution)/shard_map/ppermute | solution.py:359
  14.8 1.8 collective-permute-done
  18.3 2.0 %collective-permute-start.3 = (f32[776,128]{1,0:T(8,128)S(1)}, f32[776,128]{1,0:T(8,128)S(1)}, u32[]{:S(2)}, u32[]{:S(2)}) collective-permute-start(f32[776,128]{1,0:T(8,128)S(1)} %get-tuple-element.84), channel_id=1, source_target_pairs={{0,4},{1,9},{2,6},{3,11},{4,0},{5,13},{6,2},{7,15},{8,12},{9,1},{1... | collective-permute-start | bytes 1191944 | tf_op jit(solution)/shard_map/ppermute | solution.py:359
  20.3 6.4 %collective-permute-done.1 = f32[392,128]{1,0:T(8,128)S(1)} collective-permute-done((f32[392,128]{1,0:T(8,128)S(1)}, f32[392,128]{1,0:T(8,128)S(1)}, u32[]{:S(2)}, u32[]{:S(2)}) %collective-permute-start.1) | collective-permute-done | bytes 200736 | tf_op jit(solution)/shard_map/ppermute | solution.py:359
  27.0 3.4 %collective-permute-start.5 = (f32[392,128]{1,0:T(8,128)S(1)}, f32[392,128]{1,0:T(8,128)S(1)}, u32[]{:S(2)}, u32[]{:S(2)}) collective-permute-start(f32[392,128]{1,0:T(8,128)S(1)} %pad_maximum_fusion.12), channel_id=1, source_target_pairs={{0,8},{1,5},{2,10},{3,7},{4,12},{5,1},{6,14},{7,3},{8,0},{9,13},{1... | collective-permute-start | bytes 602120 | tf_op jit(solution)/shard_map/ppermute | solution.py:359
  30.4 5.2 %collective-permute-done.2 = f32[392,128]{1,0:T(8,128)S(1)} collective-permute-done((f32[392,128]{1,0:T(8,128)S(1)}, f32[392,128]{1,0:T(8,128)S(1)}, u32[]{:S(2)}, u32[]{:S(2)}) %collective-permute-start.2) | collective-permute-done | bytes 200736 | tf_op jit(solution)/shard_map/ppermute | solution.py:359
  35.8 2.5 %collective-permute-done.5 = f32[392,128]{1,0:T(8,128)S(1)} collective-permute-done((f32[392,128]{1,0:T(8,128)S(1)}, f32[392,128]{1,0:T(8,128)S(1)}, u32[]{:S(2)}, u32[]{:S(2)}) %collective-permute-start.5) | collective-permute-done | bytes 200736 | tf_op jit(solution)/shard_map/ppermute | solution.py:359
  39.0 3.0 %collective-permute-done.4.refs_3_ = f32[384,128]{1,0:T(8,128)S(1)} collective-permute-done((f32[384,128]{1,0:T(8,128)S(1)}, f32[384,128]{1,0:T(8,128)S(1)}, u32[]{:S(2)}, u32[]{:S(2)}) %collective-permute-start.4) | collective-permute-done | bytes 196640 | tf_op jit(solution)/shard_map/ppermute | solution.py:359
  43.4 3.0 %collective-permute-done.7 = f32[392,128]{1,0:T(8,128)S(1)} collective-permute-done((f32[392,128]{1,0:T(8,128)S(1)}, f32[392,128]{1,0:T(8,128)S(1)}, u32[]{:S(2)}, u32[]{:S(2)}) %collective-permute-start.7) | collective-permute-done | bytes 200736 | tf_op jit(solution)/shard_map/ppermute | solution.py:359
  46.4 3.9 %collective-permute-done.6.refs_2_ = f32[768,128]{1,0:T(8,128)S(1)} collective-permute-done((f32[768,128]{1,0:T(8,128)S(1)}, f32[768,128]{1,0:T(8,128)S(1)}, u32[]{:S(2)}, u32[]{:S(2)}) %collective-permute-start.6) | collective-permute-done | bytes 393248 | tf_op jit(solution)/shard_map/ppermute | solution.py:359
  50.3 2.5 %shard_map.90 = (f32[520,128]{1,0:T(8,128)S(1)}, bf16[3072,128]{1,0:T(8,128)(2,1)S(1)}, f32[1536,128]{1,0:T(8,128)S(1)}) custom-call(bf16[2048,3072]{1,0:T(8,128)(2,1)S(1)} %get-tuple-element.77.refs_0_.dense_ref, s32[4]{0:T(128)S(1)} %get-tuple-element.151.refs_1_, f32[768,128]{1,0:T(8,128)S(1)} %collective-permute-done.6.refs_2_, ...), custom_call_target="tpu_custom_call" | custom-call | flops 1610612736 | bytes 6291456 | tf_op jit(solution)/shard_map/pallas_call | solution.py:228
  52.9 1.8 shard_map.91
  54.8 1.8 collective-permute-start.11
  56.7 9.6 %collective-permute-done.11.refs_2_ = f32[768,128]{1,0:T(8,128)S(1)} collective-permute-done((f32[768,128]{1,0:T(8,128)S(1)}, f32[768,128]{1,0:T(8,128)S(1)}, u32[]{:S(2)}, u32[]{:S(2)}) %collective-permute-start.11) | collective-permute-done | bytes 393248 | tf_op jit(solution)/shard_map/ppermute | solution.py:359
  66.4 2.5 %shard_map.92 = (f32[520,128]{1,0:T(8,128)S(1)}, bf16[3072,128]{1,0:T(8,128)(2,1)S(1)}, f32[1536,128]{1,0:T(8,128)S(1)}) custom-call(bf16[2048,3072]{1,0:T(8,128)(2,1)S(1)} %get-tuple-element.77.refs_0_.dense_ref, s32[4]{0:T(128)S(1)} %get-tuple-element.151.refs_1_, f32[768,128]{1,0:T(8,128)S(1)} %collective-permute-done.11.refs_2_, ...), custom_call_target="tpu_custom_call" | custom-call | flops 1610612736 | bytes 6291456 | tf_op jit(solution)/shard_map/pallas_call | solution.py:228
  69.0 1.8 shard_map.93
  74.1 1.7 collective-permute-start.14
  77.3 2.6 %collective-permute-done.15 = f32[520,128]{1,0:T(8,128)S(1)} collective-permute-done((f32[520,128]{1,0:T(8,128)S(1)}, f32[520,128]{1,0:T(8,128)S(1)}, u32[]{:S(2)}, u32[]{:S(2)}) %collective-permute-start.15) | collective-permute-done | bytes 266272 | tf_op jit(solution)/shard_map/ppermute | solution.py:362
  80.0 2.0 %collective-permute-done.14 = f32[776,128]{1,0:T(8,128)S(1)} collective-permute-done((f32[776,128]{1,0:T(8,128)S(1)}, f32[776,128]{1,0:T(8,128)S(1)}, u32[]{:S(2)}, u32[]{:S(2)}) %collective-permute-start.14) | collective-permute-done | bytes 397344 | tf_op jit(solution)/shard_map/ppermute | solution.py:359
  83.6 1.7 collective-permute-start.19
  86.6 2.0 %collective-permute-done.16 = f32[392,128]{1,0:T(8,128)S(1)} collective-permute-done((f32[392,128]{1,0:T(8,128)S(1)}, f32[392,128]{1,0:T(8,128)S(1)}, u32[]{:S(2)}, u32[]{:S(2)}) %collective-permute-start.16) | collective-permute-done | bytes 200736 | tf_op jit(solution)/shard_map/ppermute | solution.py:359
  88.7 2.2 %collective-permute-start.18 = (f32[392,128]{1,0:T(8,128)S(1)}, f32[392,128]{1,0:T(8,128)S(1)}, u32[]{:S(2)}, u32[]{:S(2)}) collective-permute-start(f32[392,128]{1,0:T(8,128)S(1)} %pad_maximum_fusion.15), channel_id=1, source_target_pairs={{0,16},{1,17},{2,18},{3,19},{4,20},{5,21},{6,22},{7,23},{8,24},{9,... | collective-permute-start | bytes 602120 | tf_op jit(solution)/shard_map/ppermute | solution.py:359
  91.6 3.4 %collective-permute-start.21 = (f32[392,128]{1,0:T(8,128)S(1)}, f32[392,128]{1,0:T(8,128)S(1)}, u32[]{:S(2)}, u32[]{:S(2)}) collective-permute-start(f32[392,128]{1,0:T(8,128)S(1)} %pad_maximum_fusion.16), channel_id=1, source_target_pairs={{0,8},{1,5},{2,10},{3,7},{4,12},{5,1},{6,14},{7,3},{8,0},{9,13},{1... | collective-permute-start | bytes 602120 | tf_op jit(solution)/shard_map/ppermute | solution.py:359
  95.1 4.3 %collective-permute-done.18 = f32[392,128]{1,0:T(8,128)S(1)} collective-permute-done((f32[392,128]{1,0:T(8,128)S(1)}, f32[392,128]{1,0:T(8,128)S(1)}, u32[]{:S(2)}, u32[]{:S(2)}) %collective-permute-start.18) | collective-permute-done | bytes 200736 | tf_op jit(solution)/shard_map/ppermute | solution.py:359
  100.4 1.9 collective-permute-start.23
  102.3 4.9 %collective-permute-done.20.refs_3_ = f32[384,128]{1,0:T(8,128)S(1)} collective-permute-done((f32[384,128]{1,0:T(8,128)S(1)}, f32[384,128]{1,0:T(8,128)S(1)}, u32[]{:S(2)}, u32[]{:S(2)}) %collective-permute-start.20) | collective-permute-done | bytes 196640 | tf_op jit(solution)/shard_map/ppermute | solution.py:359
  107.3 4.0 %collective-permute-done.23 = f32[392,128]{1,0:T(8,128)S(1)} collective-permute-done((f32[392,128]{1,0:T(8,128)S(1)}, f32[392,128]{1,0:T(8,128)S(1)}, u32[]{:S(2)}, u32[]{:S(2)}) %collective-permute-start.23) | collective-permute-done | bytes 200736 | tf_op jit(solution)/shard_map/ppermute | solution.py:359
  111.4 3.7 %collective-permute-done.22.refs_2_ = f32[768,128]{1,0:T(8,128)S(1)} collective-permute-done((f32[768,128]{1,0:T(8,128)S(1)}, f32[768,128]{1,0:T(8,128)S(1)}, u32[]{:S(2)}, u32[]{:S(2)}) %collective-permute-start.22) | collective-permute-done | bytes 393248 | tf_op jit(solution)/shard_map/ppermute | solution.py:359
  115.1 2.6 %shard_map.98 = (f32[520,128]{1,0:T(8,128)S(1)}, bf16[3072,128]{1,0:T(8,128)(2,1)S(1)}, f32[1536,128]{1,0:T(8,128)S(1)}) custom-call(bf16[2048,3072]{1,0:T(8,128)(2,1)S(1)} %get-tuple-element.77.refs_0_.dense_ref, s32[4]{0:T(128)S(1)} %get-tuple-element.151.refs_1_, f32[768,128]{1,0:T(8,128)S(1)} %collective-permute-done.22.refs_2_, ...), custom_call_target="tpu_custom_call" | custom-call | flops 1610612736 | bytes 6291456 | tf_op jit(solution)/shard_map/pallas_call | solution.py:228
  117.8 1.8 shard_map.99
  119.8 1.9 collective-permute-start.26
  121.6 9.5 %collective-permute-done.27.refs_2_ = f32[768,128]{1,0:T(8,128)S(1)} collective-permute-done((f32[768,128]{1,0:T(8,128)S(1)}, f32[768,128]{1,0:T(8,128)S(1)}, u32[]{:S(2)}, u32[]{:S(2)}) %collective-permute-start.27) | collective-permute-done | bytes 393248 | tf_op jit(solution)/shard_map/ppermute | solution.py:359
  131.2 2.6 %shard_map.100 = (f32[520,128]{1,0:T(8,128)S(1)}, bf16[3072,128]{1,0:T(8,128)(2,1)S(1)}, f32[1536,128]{1,0:T(8,128)S(1)}) custom-call(bf16[2048,3072]{1,0:T(8,128)(2,1)S(1)} %get-tuple-element.77.refs_0_.dense_ref, s32[4]{0:T(128)S(1)} %get-tuple-element.151.refs_1_, f32[768,128]{1,0:T(8,128)S(1)} %collective-permute-done.27.refs_2_, ...), custom_call_target="tpu_custom_call" | custom-call | flops 1610612736 | bytes 6291456 | tf_op jit(solution)/shard_map/pallas_call | solution.py:228
  133.9 1.8 shard_map.101
  141.1 3.7 %collective-permute-done.31 = f32[520,128]{1,0:T(8,128)S(1)} collective-permute-done((f32[520,128]{1,0:T(8,128)S(1)}, f32[520,128]{1,0:T(8,128)S(1)}, u32[]{:S(2)}, u32[]{:S(2)}) %collective-permute-start.31) | collective-permute-done | bytes 266272 | tf_op jit(solution)/shard_map/ppermute | solution.py:362
  144.9 2.4 %collective-permute-done.30 = f32[776,128]{1,0:T(8,128)S(1)} collective-permute-done((f32[776,128]{1,0:T(8,128)S(1)}, f32[776,128]{1,0:T(8,128)S(1)}, u32[]{:S(2)}, u32[]{:S(2)}) %collective-permute-start.30) | collective-permute-done | bytes 397344 | tf_op jit(solution)/shard_map/ppermute | solution.py:359
  147.5 1.6 shard_map.104
  151.1 6.4 %collective-permute-done.32 = f32[392,128]{1,0:T(8,128)S(1)} collective-permute-done((f32[392,128]{1,0:T(8,128)S(1)}, f32[392,128]{1,0:T(8,128)S(1)}, u32[]{:S(2)}, u32[]{:S(2)}) %collective-permute-start.32) | collective-permute-done | bytes 200736 | tf_op jit(solution)/shard_map/ppermute | solution.py:359
  158.1 2.6 %collective-permute-start.36 = (f32[392,128]{1,0:T(8,128)S(1)}, f32[392,128]{1,0:T(8,128)S(1)}, u32[]{:S(2)}, u32[]{:S(2)}) collective-permute-start(f32[392,128]{1,0:T(8,128)S(1)} %pad_maximum_fusion.20), channel_id=1, source_target_pairs={{0,8},{1,5},{2,10},{3,7},{4,12},{5,1},{6,14},{7,3},{8,0},{9,13},{1... | collective-permute-start | bytes 602120 | tf_op jit(solution)/shard_map/ppermute | solution.py:359
  160.7 5.3 %collective-permute-done.34 = f32[392,128]{1,0:T(8,128)S(1)} collective-permute-done((f32[392,128]{1,0:T(8,128)S(1)}, f32[392,128]{1,0:T(8,128)S(1)}, u32[]{:S(2)}, u32[]{:S(2)}) %collective-permute-start.34) | collective-permute-done | bytes 200736 | tf_op jit(solution)/shard_map/ppermute | solution.py:359
  169.2 4.4 %collective-permute-done.38.refs_1_ = f32[384,128]{1,0:T(8,128)S(1)} collective-permute-done((f32[384,128]{1,0:T(8,128)S(1)}, f32[384,128]{1,0:T(8,128)S(1)}, u32[]{:S(2)}, u32[]{:S(2)}) %collective-permute-start.38) | collective-permute-done | bytes 196640 | tf_op jit(solution)/shard_map/ppermute | solution.py:359
  173.6 3.4 %collective-permute-done.37 = f32[392,128]{1,0:T(8,128)S(1)} collective-permute-done((f32[392,128]{1,0:T(8,128)S(1)}, f32[392,128]{1,0:T(8,128)S(1)}, u32[]{:S(2)}, u32[]{:S(2)}) %collective-permute-start.37) | collective-permute-done | bytes 200736 | tf_op jit(solution)/shard_map/ppermute | solution.py:359
  178.0 4.8 %collective-permute-done.40.refs_10_ = f32[384,128]{1,0:T(8,128)S(1)} collective-permute-done((f32[384,128]{1,0:T(8,128)S(1)}, f32[384,128]{1,0:T(8,128)S(1)}, u32[]{:S(2)}, u32[]{:S(2)}) %collective-permute-start.40) | collective-permute-done | bytes 196640 | tf_op jit(solution)/shard_map/ppermute | solution.py:359
  184.2 2.3 %shard_map.106 = (f32[3072,128]{1,0:T(8,128)}, f32[8,128]{1,0:T(8,128)S(1)}) custom-call(s32[4]{0:T(128)S(1)} %get-tuple-element.152.unit_ref, f32[1536,128]{1,0:T(8,128)S(1)} %get-tuple-element.93.refs_6_.refs_0_, f32[1536,128]{1,0:T(8,128)S(1)} %get-tuple-element.118.refs_1_.refs_3_, f32[8,128]{1,0:T(8,128)S(1)} %slice_add_fusion.47.refs_5_.refs_2_.refs_4_, ...), custom_call_target="tpu_custom_call" | custom-call | bytes 3145728 | tf_op jit(solution)/shard_map/pallas_call | solution.py:331
  186.9 2.3 %collective-permute-done.39.refs_0_ = f32[768,128]{1,0:T(8,128)S(1)} collective-permute-done((f32[768,128]{1,0:T(8,128)S(1)}, f32[768,128]{1,0:T(8,128)S(1)}, u32[]{:S(2)}, u32[]{:S(2)}) %collective-permute-start.39) | collective-permute-done | bytes 393248 | tf_op jit(solution)/shard_map/ppermute | solution.py:359
  189.3 5.8 %collective-permute-done.41.refs_9_ = f32[768,128]{1,0:T(8,128)S(1)} collective-permute-done((f32[768,128]{1,0:T(8,128)S(1)}, f32[768,128]{1,0:T(8,128)S(1)}, u32[]{:S(2)}, u32[]{:S(2)}) %collective-permute-start.41) | collective-permute-done | bytes 393248 | tf_op jit(solution)/shard_map/ppermute | solution.py:359
  195.1 2.2 %shard_map.107 = f32[3072,128]{1,0:T(8,128)} custom-call(s32[4]{0:T(128)S(1)} %get-tuple-element.152.unit_ref, f32[768,128]{1,0:T(8,128)S(1)} %collective-permute-done.39.refs_0_, f32[384,128]{1,0:T(8,128)S(1)} %collective-permute-done.38.refs_1_, f32[384,128]{1,0:T(8,128)S(1)} %slice_add_fusion.21.refs_2_, ...), custom_call_target="tpu_custom_call" | custom-call | bytes 3145728 | tf_op jit(solution)/shard_map/pallas_call | solution.py:331
  (144 shorter events, 34.2 us)
Async XLA Ops:
  6.5 10.1 %collective-permute-start = (f32[776,128]{1,0:T(8,128)S(1)}, f32[776,128]{1,0:T(8,128)S(1)}, u32[]{:S(2)}, u32[]{:S(2)}) collective-permute-start(f32[776,128]{1,0:T(8,128)S(1)} %get-tuple-element.80), channel_id=1, source_target_pairs={{0,4},{1,9},{2,6},{3,11},{4,0},{5,13},{6,2},{7,15},{8,12},{9,1},{1... | collective-permute-start | bytes 1191944 | tf_op jit(solution)/shard_map/ppermute | solution.py:359
  13.5 4.8 %copy-start = (s32[4]{0:T(128)S(1)}, s32[4]{0:T(128)}, u32[]{:S(2)}) copy-start(s32[4]{0:T(128)} %constant.40.clone) | copy-start | bytes 52
  16.7 10.0 %collective-permute-start.1 = (f32[392,128]{1,0:T(8,128)S(1)}, f32[392,128]{1,0:T(8,128)S(1)}, u32[]{:S(2)}, u32[]{:S(2)}) collective-permute-start(f32[392,128]{1,0:T(8,128)S(1)} %pad_maximum_fusion.10), channel_id=1, source_target_pairs={{0,8},{1,5},{2,10},{3,7},{4,12},{5,1},{6,14},{7,3},{8,0},{9,13},{1... | collective-permute-start | bytes 602120 | tf_op jit(solution)/shard_map/ppermute | solution.py:359
  18.3 8.5 %collective-permute-start.3 = (f32[776,128]{1,0:T(8,128)S(1)}, f32[776,128]{1,0:T(8,128)S(1)}, u32[]{:S(2)}, u32[]{:S(2)}) collective-permute-start(f32[776,128]{1,0:T(8,128)S(1)} %get-tuple-element.84), channel_id=1, source_target_pairs={{0,4},{1,9},{2,6},{3,11},{4,0},{5,13},{6,2},{7,15},{8,12},{9,1},{1... | collective-permute-start | bytes 1191944 | tf_op jit(solution)/shard_map/ppermute | solution.py:359
  26.8 8.8 %collective-permute-start.2 = (f32[392,128]{1,0:T(8,128)S(1)}, f32[392,128]{1,0:T(8,128)S(1)}, u32[]{:S(2)}, u32[]{:S(2)}) collective-permute-start(f32[392,128]{1,0:T(8,128)S(1)} %pad_maximum_fusion.11), channel_id=1, source_target_pairs={{0,16},{1,17},{2,18},{3,19},{4,20},{5,21},{6,22},{7,23},{8,24},{9,... | collective-permute-start | bytes 602120 | tf_op jit(solution)/shard_map/ppermute | solution.py:359
  27.0 11.3 %collective-permute-start.5 = (f32[392,128]{1,0:T(8,128)S(1)}, f32[392,128]{1,0:T(8,128)S(1)}, u32[]{:S(2)}, u32[]{:S(2)}) collective-permute-start(f32[392,128]{1,0:T(8,128)S(1)} %pad_maximum_fusion.12), channel_id=1, source_target_pairs={{0,8},{1,5},{2,10},{3,7},{4,12},{5,1},{6,14},{7,3},{8,0},{9,13},{1... | collective-permute-start | bytes 602120 | tf_op jit(solution)/shard_map/ppermute | solution.py:359
  35.7 6.4 %collective-permute-start.4 = (f32[384,128]{1,0:T(8,128)S(1)}, f32[384,128]{1,0:T(8,128)S(1)}, u32[]{:S(2)}, u32[]{:S(2)}) collective-permute-start(f32[384,128]{1,0:T(8,128)S(1)} %slice_add_fusion.25.refs_4_), channel_id=1, source_target_pairs={{0,8},{1,9},{2,10},{3,11},{4,12},{5,13},{6,14},{7,15},{8,0},{9,1},... | collective-permute-start | bytes 589832 | tf_op jit(solution)/shard_map/ppermute | solution.py:359
  38.4 7.9 %collective-permute-start.7 = (f32[392,128]{1,0:T(8,128)S(1)}, f32[392,128]{1,0:T(8,128)S(1)}, u32[]{:S(2)}, u32[]{:S(2)}) collective-permute-start(f32[392,128]{1,0:T(8,128)S(1)} %pad_maximum_fusion.13), channel_id=1, source_target_pairs={{0,16},{1,17},{2,18},{3,19},{4,20},{5,21},{6,22},{7,23},{8,24},{9,... | collective-permute-start | bytes 602120 | tf_op jit(solution)/shard_map/ppermute | solution.py:359
  42.1 8.2 %collective-permute-start.6 = (f32[768,128]{1,0:T(8,128)S(1)}, f32[768,128]{1,0:T(8,128)S(1)}, u32[]{:S(2)}, u32[]{:S(2)}) collective-permute-start(f32[768,128]{1,0:T(8,128)S(1)} %pad_maximum_fusion), channel_id=1, source_target_pairs={{0,4},{1,5},{2,6},{3,7},{4,0},{5,1},{6,2},{7,3},{8,12},{9,13},{10,... | collective-permute-start | bytes 1179656 | tf_op jit(solution)/shard_map/ppermute | solution.py:359
  46.3 8.4 %collective-permute-start.9 = (f32[384,128]{1,0:T(8,128)S(1)}, f32[384,128]{1,0:T(8,128)S(1)}, u32[]{:S(2)}, u32[]{:S(2)}) collective-permute-start(f32[384,128]{1,0:T(8,128)S(1)} %slice_add_fusion.24.refs_4_), channel_id=1, source_target_pairs={{0,8},{1,9},{2,10},{3,11},{4,12},{5,13},{6,14},{7,15},{8,0},{9,1},... | collective-permute-start | bytes 589832 | tf_op jit(solution)/shard_map/ppermute | solution.py:359
  52.9 3.7 %collective-permute-start.8 = (f32[520,128]{1,0:T(8,128)S(1)}, f32[520,128]{1,0:T(8,128)S(1)}, u32[]{:S(2)}, u32[]{:S(2)}) collective-permute-start(f32[520,128]{1,0:T(8,128)S(1)} %get-tuple-element.95), channel_id=1, source_target_pairs={{0,1},{1,0},{2,3},{3,2},{4,5},{5,4},{6,7},{7,6},{8,9},{9,8},{10,11... | collective-permute-start | bytes 798728 | tf_op jit(solution)/shard_map/ppermute | solution.py:362
  54.8 11.6 %collective-permute-start.11 = (f32[768,128]{1,0:T(8,128)S(1)}, f32[768,128]{1,0:T(8,128)S(1)}, u32[]{:S(2)}, u32[]{:S(2)}) collective-permute-start(f32[768,128]{1,0:T(8,128)S(1)} %pad_maximum_fusion.1), channel_id=1, source_target_pairs={{0,4},{1,5},{2,6},{3,7},{4,0},{5,1},{6,2},{7,3},{8,12},{9,13},{10,... | collective-permute-start | bytes 1179656 | tf_op jit(solution)/shard_map/ppermute | solution.py:359
  56.7 14.1 %collective-permute-start.10 = (f32[520,128]{1,0:T(8,128)S(1)}, f32[520,128]{1,0:T(8,128)S(1)}, u32[]{:S(2)}, u32[]{:S(2)}) collective-permute-start(f32[520,128]{1,0:T(8,128)S(1)} %pad_maximum_fusion.6), channel_id=1, source_target_pairs={{0,2},{1,3},{2,0},{3,1},{4,6},{5,7},{6,4},{7,5},{8,10},{9,11},{10,... | collective-permute-start | bytes 798728 | tf_op jit(solution)/shard_map/ppermute | solution.py:362
  68.9 2.5 %collective-permute-start.13 = (f32[520,128]{1,0:T(8,128)S(1)}, f32[520,128]{1,0:T(8,128)S(1)}, u32[]{:S(2)}, u32[]{:S(2)}) collective-permute-start(f32[520,128]{1,0:T(8,128)S(1)} %get-tuple-element.99), channel_id=1, source_target_pairs={{0,1},{1,0},{2,3},{3,2},{4,5},{5,4},{6,7},{7,6},{8,9},{9,8},{10,11... | collective-permute-start | bytes 798728 | tf_op jit(solution)/shard_map/ppermute | solution.py:362
  70.8 1.9 collective-permute-start.12
  71.5 8.4 %collective-permute-start.15 = (f32[520,128]{1,0:T(8,128)S(1)}, f32[520,128]{1,0:T(8,128)S(1)}, u32[]{:S(2)}, u32[]{:S(2)}) collective-permute-start(f32[520,128]{1,0:T(8,128)S(1)} %pad_maximum_fusion.7), channel_id=1, source_target_pairs={{0,2},{1,3},{2,0},{3,1},{4,6},{5,7},{6,4},{7,5},{8,10},{9,11},{10,... | collective-permute-start | bytes 798728 | tf_op jit(solution)/shard_map/ppermute | solution.py:362
  74.1 7.9 %collective-permute-start.14 = (f32[776,128]{1,0:T(8,128)S(1)}, f32[776,128]{1,0:T(8,128)S(1)}, u32[]{:S(2)}, u32[]{:S(2)}) collective-permute-start(f32[776,128]{1,0:T(8,128)S(1)} %get-tuple-element.105), channel_id=1, source_target_pairs={{0,4},{1,9},{2,6},{3,11},{4,0},{5,13},{6,2},{7,15},{8,12},{9,1},{1... | collective-permute-start | bytes 1191944 | tf_op jit(solution)/shard_map/ppermute | solution.py:359
  79.9 2.3 %collective-permute-start.17 = (f32[512,128]{1,0:T(8,128)S(1)}, f32[512,128]{1,0:T(8,128)S(1)}, u32[]{:S(2)}, u32[]{:S(2)}) collective-permute-start(f32[512,128]{1,0:T(8,128)S(1)} %slice_add_fusion.10.refs_2_), channel_id=1, source_target_pairs={{0,1},{1,0},{2,3},{3,2},{4,5},{5,4},{6,7},{7,6},{8,9},{9,8},{10,11... | collective-permute-start | bytes 786440 | tf_op jit(solution)/shard_map/ppermute | solution.py:362
  82.1 6.5 %collective-permute-start.16 = (f32[392,128]{1,0:T(8,128)S(1)}, f32[392,128]{1,0:T(8,128)S(1)}, u32[]{:S(2)}, u32[]{:S(2)}) collective-permute-start(f32[392,128]{1,0:T(8,128)S(1)} %pad_maximum_fusion.14), channel_id=1, source_target_pairs={{0,8},{1,5},{2,10},{3,7},{4,12},{5,1},{6,14},{7,3},{8,0},{9,13},{1... | collective-permute-start | bytes 602120 | tf_op jit(solution)/shard_map/ppermute | solution.py:359
  83.6 7.9 %collective-permute-start.19 = (f32[776,128]{1,0:T(8,128)S(1)}, f32[776,128]{1,0:T(8,128)S(1)}, u32[]{:S(2)}, u32[]{:S(2)}) collective-permute-start(f32[776,128]{1,0:T(8,128)S(1)} %get-tuple-element.109), channel_id=1, source_target_pairs={{0,4},{1,9},{2,6},{3,11},{4,0},{5,13},{6,2},{7,15},{8,12},{9,1},{1... | collective-permute-start | bytes 1191944 | tf_op jit(solution)/shard_map/ppermute | solution.py:359
  88.7 10.7 %collective-permute-start.18 = (f32[392,128]{1,0:T(8,128)S(1)}, f32[392,128]{1,0:T(8,128)S(1)}, u32[]{:S(2)}, u32[]{:S(2)}) collective-permute-start(f32[392,128]{1,0:T(8,128)S(1)} %pad_maximum_fusion.15), channel_id=1, source_target_pairs={{0,16},{1,17},{2,18},{3,19},{4,20},{5,21},{6,22},{7,23},{8,24},{9,... | collective-permute-start | bytes 602120 | tf_op jit(solution)/shard_map/ppermute | solution.py:359
  91.6 8.7 %collective-permute-start.21 = (f32[392,128]{1,0:T(8,128)S(1)}, f32[392,128]{1,0:T(8,128)S(1)}, u32[]{:S(2)}, u32[]{:S(2)}) collective-permute-start(f32[392,128]{1,0:T(8,128)S(1)} %pad_maximum_fusion.16), channel_id=1, source_target_pairs={{0,8},{1,5},{2,10},{3,7},{4,12},{5,1},{6,14},{7,3},{8,0},{9,13},{1... | collective-permute-start | bytes 602120 | tf_op jit(solution)/shard_map/ppermute | solution.py:359
  99.4 7.8 %collective-permute-start.20 = (f32[384,128]{1,0:T(8,128)S(1)}, f32[384,128]{1,0:T(8,128)S(1)}, u32[]{:S(2)}, u32[]{:S(2)}) collective-permute-start(f32[384,128]{1,0:T(8,128)S(1)} %slice_add_fusion.23.refs_4_), channel_id=1, source_target_pairs={{0,8},{1,9},{2,10},{3,11},{4,12},{5,13},{6,14},{7,15},{8,0},{9,1},... | collective-permute-start | bytes 589832 | tf_op jit(solution)/shard_map/ppermute | solution.py:359
  100.4 10.9 %collective-permute-start.23 = (f32[392,128]{1,0:T(8,128)S(1)}, f32[392,128]{1,0:T(8,128)S(1)}, u32[]{:S(2)}, u32[]{:S(2)}) collective-permute-start(f32[392,128]{1,0:T(8,128)S(1)} %pad_maximum_fusion.17), channel_id=1, source_target_pairs={{0,16},{1,17},{2,18},{3,19},{4,20},{5,21},{6,22},{7,23},{8,24},{9,... | collective-permute-start | bytes 602120 | tf_op jit(solution)/shard_map/ppermute | solution.py:359
  107.2 7.8 %collective-permute-start.22 = (f32[768,128]{1,0:T(8,128)S(1)}, f32[768,128]{1,0:T(8,128)S(1)}, u32[]{:S(2)}, u32[]{:S(2)}) collective-permute-start(f32[768,128]{1,0:T(8,128)S(1)} %pad_maximum_fusion.2), channel_id=1, source_target_pairs={{0,4},{1,5},{2,6},{3,7},{4,0},{5,1},{6,2},{7,3},{8,12},{9,13},{10,... | collective-permute-start | bytes 1179656 | tf_op jit(solution)/shard_map/ppermute | solution.py:359
  111.3 8.2 %collective-permute-start.25 = (f32[384,128]{1,0:T(8,128)S(1)}, f32[384,128]{1,0:T(8,128)S(1)}, u32[]{:S(2)}, u32[]{:S(2)}) collective-permute-start(f32[384,128]{1,0:T(8,128)S(1)} %slice_add_fusion.22.refs_4_), channel_id=1, source_target_pairs={{0,8},{1,9},{2,10},{3,11},{4,12},{5,13},{6,14},{7,15},{8,0},{9,1},... | collective-permute-start | bytes 589832 | tf_op jit(solution)/shard_map/ppermute | solution.py:359
  117.7 2.0 %collective-permute-start.24 = (f32[520,128]{1,0:T(8,128)S(1)}, f32[520,128]{1,0:T(8,128)S(1)}, u32[]{:S(2)}, u32[]{:S(2)}) collective-permute-start(f32[520,128]{1,0:T(8,128)S(1)} %get-tuple-element.119), channel_id=1, source_target_pairs={{0,1},{1,0},{2,3},{3,2},{4,5},{5,4},{6,7},{7,6},{8,9},{9,8},{10,11... | collective-permute-start | bytes 798728 | tf_op jit(solution)/shard_map/ppermute | solution.py:362
  119.6 11.6 %collective-permute-start.27 = (f32[768,128]{1,0:T(8,128)S(1)}, f32[768,128]{1,0:T(8,128)S(1)}, u32[]{:S(2)}, u32[]{:S(2)}) collective-permute-start(f32[768,128]{1,0:T(8,128)S(1)} %pad_maximum_fusion.3), channel_id=1, source_target_pairs={{0,4},{1,5},{2,6},{3,7},{4,0},{5,1},{6,2},{7,3},{8,12},{9,13},{10,... | collective-permute-start | bytes 1179656 | tf_op jit(solution)/shard_map/ppermute | solution.py:359
  119.8 15.9 %collective-permute-start.26 = (f32[520,128]{1,0:T(8,128)S(1)}, f32[520,128]{1,0:T(8,128)S(1)}, u32[]{:S(2)}, u32[]{:S(2)}) collective-permute-start(f32[520,128]{1,0:T(8,128)S(1)} %pad_maximum_fusion.8), channel_id=1, source_target_pairs={{0,2},{1,3},{2,0},{3,1},{4,6},{5,7},{6,4},{7,5},{8,10},{9,11},{10,... | collective-permute-start | bytes 798728 | tf_op jit(solution)/shard_map/ppermute | solution.py:362
  133.8 2.5 %collective-permute-start.29 = (f32[520,128]{1,0:T(8,128)S(1)}, f32[520,128]{1,0:T(8,128)S(1)}, u32[]{:S(2)}, u32[]{:S(2)}) collective-permute-start(f32[520,128]{1,0:T(8,128)S(1)} %get-tuple-element.125), channel_id=1, source_target_pairs={{0,1},{1,0},{2,3},{3,2},{4,5},{5,4},{6,7},{7,6},{8,9},{9,8},{10,11... | collective-permute-start | bytes 798728 | tf_op jit(solution)/shard_map/ppermute | solution.py:362
  135.7 2.2 %collective-permute-start.28 = (f32[512,128]{1,0:T(8,128)S(1)}, f32[512,128]{1,0:T(8,128)S(1)}, u32[]{:S(2)}, u32[]{:S(2)}) collective-permute-start(f32[512,128]{1,0:T(8,128)S(1)} %slice_add_fusion.8.refs_2_), channel_id=1, source_target_pairs={{0,1},{1,0},{2,3},{3,2},{4,5},{5,4},{6,7},{7,6},{8,9},{9,8},{10,11... | collective-permute-start | bytes 786440 | tf_op jit(solution)/shard_map/ppermute | solution.py:362
  136.4 8.4 %collective-permute-start.31 = (f32[520,128]{1,0:T(8,128)S(1)}, f32[520,128]{1,0:T(8,128)S(1)}, u32[]{:S(2)}, u32[]{:S(2)}) collective-permute-start(f32[520,128]{1,0:T(8,128)S(1)} %pad_maximum_fusion.9), channel_id=1, source_target_pairs={{0,2},{1,3},{2,0},{3,1},{4,6},{5,7},{6,4},{7,5},{8,10},{9,11},{10,... | collective-permute-start | bytes 798728 | tf_op jit(solution)/shard_map/ppermute | solution.py:362
  139.4 7.9 %collective-permute-start.30 = (f32[776,128]{1,0:T(8,128)S(1)}, f32[776,128]{1,0:T(8,128)S(1)}, u32[]{:S(2)}, u32[]{:S(2)}) collective-permute-start(f32[776,128]{1,0:T(8,128)S(1)} %get-tuple-element.131), channel_id=1, source_target_pairs={{0,4},{1,9},{2,6},{3,11},{4,0},{5,13},{6,2},{7,15},{8,12},{9,1},{1... | collective-permute-start | bytes 1191944 | tf_op jit(solution)/shard_map/ppermute | solution.py:359
  144.8 2.6 %collective-permute-start.33 = (f32[512,128]{1,0:T(8,128)S(1)}, f32[512,128]{1,0:T(8,128)S(1)}, u32[]{:S(2)}, u32[]{:S(2)}) collective-permute-start(f32[512,128]{1,0:T(8,128)S(1)} %slice_add_fusion.6.refs_2_), channel_id=1, source_target_pairs={{0,1},{1,0},{2,3},{3,2},{4,5},{5,4},{6,7},{7,6},{8,9},{9,8},{10,11... | collective-permute-start | bytes 786440 | tf_op jit(solution)/shard_map/ppermute | solution.py:362
  147.4 10.1 %collective-permute-start.32 = (f32[392,128]{1,0:T(8,128)S(1)}, f32[392,128]{1,0:T(8,128)S(1)}, u32[]{:S(2)}, u32[]{:S(2)}) collective-permute-start(f32[392,128]{1,0:T(8,128)S(1)} %pad_maximum_fusion.18), channel_id=1, source_target_pairs={{0,8},{1,5},{2,10},{3,7},{4,12},{5,1},{6,14},{7,3},{8,0},{9,13},{1... | collective-permute-start | bytes 602120 | tf_op jit(solution)/shard_map/ppermute | solution.py:359
  149.1 8.9 %collective-permute-start.35 = (f32[776,128]{1,0:T(8,128)S(1)}, f32[776,128]{1,0:T(8,128)S(1)}, u32[]{:S(2)}, u32[]{:S(2)}) collective-permute-start(f32[776,128]{1,0:T(8,128)S(1)} %get-tuple-element.137), channel_id=1, source_target_pairs={{0,4},{1,9},{2,6},{3,11},{4,0},{5,13},{6,2},{7,15},{8,12},{9,1},{1... | collective-permute-start | bytes 1191944 | tf_op jit(solution)/shard_map/ppermute | solution.py:359
  157.5 8.4 %collective-permute-start.34 = (f32[392,128]{1,0:T(8,128)S(1)}, f32[392,128]{1,0:T(8,128)S(1)}, u32[]{:S(2)}, u32[]{:S(2)}) collective-permute-start(f32[392,128]{1,0:T(8,128)S(1)} %pad_maximum_fusion.19), channel_id=1, source_target_pairs={{0,16},{1,17},{2,18},{3,19},{4,20},{5,21},{6,22},{7,23},{8,24},{9,... | collective-permute-start | bytes 602120 | tf_op jit(solution)/shard_map/ppermute | solution.py:359
  158.1 9.4 %collective-permute-start.36 = (f32[392,128]{1,0:T(8,128)S(1)}, f32[392,128]{1,0:T(8,128)S(1)}, u32[]{:S(2)}, u32[]{:S(2)}) collective-permute-start(f32[392,128]{1,0:T(8,128)S(1)} %pad_maximum_fusion.20), channel_id=1, source_target_pairs={{0,8},{1,5},{2,10},{3,7},{4,12},{5,1},{6,14},{7,3},{8,0},{9,13},{1... | collective-permute-start | bytes 602120 | tf_op jit(solution)/shard_map/ppermute | solution.py:359
  166.0 7.7 %collective-permute-start.38 = (f32[384,128]{1,0:T(8,128)S(1)}, f32[384,128]{1,0:T(8,128)S(1)}, u32[]{:S(2)}, u32[]{:S(2)}) collective-permute-start(f32[384,128]{1,0:T(8,128)S(1)} %slice_add_fusion.21.refs_2_), channel_id=1, source_target_pairs={{0,8},{1,9},{2,10},{3,11},{4,12},{5,13},{6,14},{7,15},{8,0},{9,1},... | collective-permute-start | bytes 589832 | tf_op jit(solution)/shard_map/ppermute | solution.py:359
  167.6 9.4 %collective-permute-start.37 = (f32[392,128]{1,0:T(8,128)S(1)}, f32[392,128]{1,0:T(8,128)S(1)}, u32[]{:S(2)}, u32[]{:S(2)}) collective-permute-start(f32[392,128]{1,0:T(8,128)S(1)} %pad_maximum_fusion.21), channel_id=1, source_target_pairs={{0,16},{1,17},{2,18},{3,19},{4,20},{5,21},{6,22},{7,23},{8,24},{9,... | collective-permute-start | bytes 602120 | tf_op jit(solution)/shard_map/ppermute | solution.py:359
  177.0 5.7 %collective-permute-start.40 = (f32[384,128]{1,0:T(8,128)S(1)}, f32[384,128]{1,0:T(8,128)S(1)}, u32[]{:S(2)}, u32[]{:S(2)}) collective-permute-start(f32[384,128]{1,0:T(8,128)S(1)} %slice_add_fusion.20.refs_11_), channel_id=1, source_target_pairs={{0,8},{1,9},{2,10},{3,11},{4,12},{5,13},{6,14},{7,15},{8,0},{9,1},... | collective-permute-start | bytes 589832 | tf_op jit(solution)/shard_map/ppermute | solution.py:359
  177.1 12.1 %collective-permute-start.39 = (f32[768,128]{1,0:T(8,128)S(1)}, f32[768,128]{1,0:T(8,128)S(1)}, u32[]{:S(2)}, u32[]{:S(2)}) collective-permute-start(f32[768,128]{1,0:T(8,128)S(1)} %pad_maximum_fusion.4), channel_id=1, source_target_pairs={{0,4},{1,5},{2,6},{3,7},{4,0},{5,1},{6,2},{7,3},{8,12},{9,13},{10,... | collective-permute-start | bytes 1179656 | tf_op jit(solution)/shard_map/ppermute | solution.py:359
  182.8 12.2 %collective-permute-start.41 = (f32[768,128]{1,0:T(8,128)S(1)}, f32[768,128]{1,0:T(8,128)S(1)}, u32[]{:S(2)}, u32[]{:S(2)}) collective-permute-start(f32[768,128]{1,0:T(8,128)S(1)} %pad_maximum_fusion.5), channel_id=1, source_target_pairs={{0,4},{1,5},{2,6},{3,7},{4,0},{5,1},{6,2},{7,3},{8,12},{9,13},{10,... | collective-permute-start | bytes 1179656 | tf_op jit(solution)/shard_map/ppermute | solution.py:359

commit v13 on v11

--- a/solution.py
+++ b/solution.py
@@ -239,8 +239,12 @@
     send, flat, *raw = product_call(
         functools.partial(back_send_kernel, first), dense, operands, shapes
     )
-    (keep,) = product_call(back_keep_kernel, dense, [flat], [float_rows(cells // 4)])
-    return send, keep, *raw
+
+
+    def keep(flat):
+        return product_call(back_keep_kernel, dense, [flat], [float_rows(cells // 4)])[0]
+
+    return send, (keep, flat), *raw
 
 
 def fore_product(dense, operands, first):
@@ -253,8 +257,12 @@
     send, wide, raw = product_call(
         functools.partial(fore_send_kernel, first), dense, operands, shapes
     )
-    (keep,) = product_call(fore_keep_kernel, dense, [wide], [float_rows(rows // 4)])
-    return send, keep, raw
+
+
+    def keep(wide):
+        return product_call(fore_keep_kernel, dense, [wide], [float_rows(rows // 4)])[0]
+
+    return send, (keep, wide), raw
 
 
 def rotation(norms):
@@ -365,30 +373,37 @@
 
     dense, *lefts = fill_dense(kernel, pattern, counts, places, flip, delays)
 
-    def reduce_rows(send, keep):
-        half = keep.shape[0]
-        got = yield swap_rows, send, 0
-        keep = keep + got[:half]
+    def tied(value, other):
+        return lax.optimization_barrier((value, other))[0]
+
+    def kept_half(kept, ahead):
+        half, operand = kept
+        return half(tied(operand, ahead))
+
+    def reduce_rows(send, kept):
+        half = send.shape[0] - NORM_ROWS
+        got, ahead = yield swap_rows, send, 0
+        keep = kept_half(kept, ahead) + got[:half]
         norm = send[half:] + got[half:]
         send, mine = keep[: half // 2], keep[half // 2 :]
         for level in range(1, len(row_bits)):
-            got = yield swap_rows, jnp.concatenate([send, norm]), level
+            got, _ = yield swap_rows, jnp.concatenate([send, norm]), level
             norm = norm + got[half // 2 :]
             send = mine = mine + got[: half // 2]
-        inner = yield swap_rows, mine, 1
-        outer = yield swap_rows, jnp.concatenate([inner, mine]), 0
+        inner, _ = yield swap_rows, mine, 1
+        outer, _ = yield swap_rows, jnp.concatenate([inner, mine]), 0
         return [outer, inner, mine], norm
 
-    def reduce_cols(send, keep):
-        half = keep.shape[0]
-        got = yield swap_cols, send, 0
-        own = keep + got[:half]
+    def reduce_cols(send, kept):
+        half = send.shape[0] - NORM_ROWS
+        got, ahead = yield swap_cols, send, 0
+        own = kept_half(kept, ahead) + got[:half]
         norm = send[half:] + got[half:]
         for bit in col_bits[1:]:
-            got = yield swap_cols, jnp.concatenate([own, norm]), bit
+            got, _ = yield swap_cols, jnp.concatenate([own, norm]), bit
             norm = norm + got[half:]
             own = own + got[:half]
-        other = yield swap_cols, own, 0
+        other, _ = yield swap_cols, own, 0
         return [other, own], norm
 
     def chain(left):
@@ -409,15 +424,13 @@
             norms.append(norm)
         return rights, norms, totals
 
-    def tied(value, other):
-        return lax.optimization_barrier((value, other))[0]
-
     runs = [chain(left) for left in lefts]
     wanted = [next(run) for run in runs]
     chains = [None] * len(runs)
     gots = [None] * len(runs)
-    swap, latest, level = wanted[0]
-    gots[0] = swap(latest, level)
+    swap, value, level = wanted[0]
+    gots[0] = swap(value, level)
+    latest = wanted[1][1]
     turn = 0
     while None in chains:
         mine = 0 if turn < BEHIND else (turn - BEHIND) % 2
@@ -429,7 +442,7 @@
             latest = tied(value, latest)
         else:
             try:
-                swap, latest, level = runs[mine].send(tied(gots[mine], latest))
+                swap, latest, level = runs[mine].send((tied(gots[mine], latest), latest))
             except StopIteration as stop:
                 chains[mine] = stop.value
                 continue

time: 191 us -> 190 us (level)
    ppermute x30, waiting for transfers between devices: 104 us -> 98.8 us  [swap_rows(): return lax.ppermute(value, ('rows', 'cols'), pairs)]
    ppermute x12, waiting for transfers between devices: 8.45 us -> 13.1 us  [swap_cols(): lax.ppermute(value, 'cols', [(i, i ^ 1 << level) for i in range(col_count)])]
  transfers between devices with their start and end apart: 42 -> 42, of which waited for: 27 -> 26; matrix products, arithmetic and copies ran while one was open for 1% -> 1% of each run, Pallas kernels for 17% -> 17%
where the time goes in v13:
time: 190 us
  waiting for transfers between devices  112 us (59%)
  Pallas kernels  39.4 us (21%)
  starting transfers between devices  34.7 us (18%)
    ppermute x30, waiting for transfers between devices, swap_rows(): return lax.ppermute(value, ('rows', 'cols'), pairs)  98.8 us
    pallas_call x20, Pallas kernels, product_call(): pl.pallas_call(body, in_specs=[WHOLE] * (1 + len(operands)), out_specs=[W...  31.4 us
    ppermute x30, starting transfers between devices, swap_rows(): return lax.ppermute(value, ('rows', 'cols'), pairs)  29.9 us
    ppermute x12, waiting for transfers between devices, swap_cols(): lax.ppermute(value, 'cols', [(i, i ^ 1 << level) for i in range(col_count)])  13.1 us
    ppermute x12, starting transfers between devices, swap_cols(): lax.ppermute(value, 'cols', [(i, i ^ 1 << level) for i in range(col_count)])  4.82 us
    pallas_call x1, Pallas kernels, fill_dense(): pl.pallas_call(fill_kernel, in_specs=[SCALARS] * 2 + [pl.BlockSpec(memory...  4.64 us
  transfers between devices with their start and end apart: 42, of which 26 were waited for; matrix products, arithmetic and copies ran while one was open for 1% of the time, Pallas kernels for 17%

profile of v13, /device:TPU:0, one launch (start us, length us, event | category | flops | bytes accessed | tf_op | source)
XLA Modules:
  0.0 189.5 jit_solution(17045717044025076598)
XLA Ops:
  0.7 4.6 %shard_map.67 = (bf16[2048,3072]{1,0:T(8,128)(2,1)S(1)}, f32[1024,128]{1,0:T(8,128)S(1)}, f32[1024,128]{1,0:T(8,128)S(1)}) custom-call(s32[24]{0:T(128)S(1)} %fusion.place_ref, s32[1]{0:T(128)} %bitcast.1.flip_ref, s32[16,16]{1,0:T(8,128)} %pattern_in.1, s32[16]{0:T(128)} %bitcast.5, f32[2048,128]{1,0:T(8,128)} %delays_in.1, bf16[16,16,128,128]{3,2,1,0:T(8,128)(2,1)} %tiles_in.1), custom_call_target="tpu_custom_call" | custom-call | bytes 8388608 | tf_op jit(solution)/shard_map/pallas_call | solution.py:87
  5.3 1.4 shard_map.68
  6.7 4.3 %collective-permute-start = (f32[776,128]{1,0:T(8,128)S(1)}, f32[776,128]{1,0:T(8,128)S(1)}, u32[]{:S(2)}, u32[]{:S(2)}) collective-permute-start(f32[776,128]{1,0:T(8,128)S(1)} %get-tuple-element.93), channel_id=1, source_target_pairs={{0,4},{1,9},{2,6},{3,11},{4,0},{5,13},{6,2},{7,15},{8,12},{9,1},{1... | collective-permute-start | bytes 1191944 | tf_op jit(solution)/shard_map/ppermute | solution.py:359
  11.0 1.4 shard_map.69
  13.7 3.1 %collective-permute-done = f32[776,128]{1,0:T(8,128)S(1)} collective-permute-done((f32[776,128]{1,0:T(8,128)S(1)}, f32[776,128]{1,0:T(8,128)S(1)}, u32[]{:S(2)}, u32[]{:S(2)}) %collective-permute-start) | collective-permute-done | bytes 397344 | tf_op jit(solution)/shard_map/ppermute | solution.py:359
  17.8 2.0 %collective-permute-start.3 = (f32[776,128]{1,0:T(8,128)S(1)}, f32[776,128]{1,0:T(8,128)S(1)}, u32[]{:S(2)}, u32[]{:S(2)}) collective-permute-start(f32[776,128]{1,0:T(8,128)S(1)} %get-tuple-element.95), channel_id=1, source_target_pairs={{0,4},{1,9},{2,6},{3,11},{4,0},{5,13},{6,2},{7,15},{8,12},{9,1},{1... | collective-permute-start | bytes 1191944 | tf_op jit(solution)/shard_map/ppermute | solution.py:359
  19.8 7.1 %collective-permute-done.1 = f32[392,128]{1,0:T(8,128)S(1)} collective-permute-done((f32[392,128]{1,0:T(8,128)S(1)}, f32[392,128]{1,0:T(8,128)S(1)}, u32[]{:S(2)}, u32[]{:S(2)}) %collective-permute-start.1) | collective-permute-done | bytes 200736 | tf_op jit(solution)/shard_map/ppermute | solution.py:359
  29.4 2.4 %collective-permute-start.5 = (f32[392,128]{1,0:T(8,128)S(1)}, f32[392,128]{1,0:T(8,128)S(1)}, u32[]{:S(2)}, u32[]{:S(2)}) collective-permute-start(f32[392,128]{1,0:T(8,128)S(1)} %pad_maximum_fusion.12), channel_id=1, source_target_pairs={{0,8},{1,5},{2,10},{3,7},{4,12},{5,1},{6,14},{7,3},{8,0},{9,13},{1... | collective-permute-start | bytes 602120 | tf_op jit(solution)/shard_map/ppermute | solution.py:359
  31.8 3.9 %collective-permute-done.2 = f32[392,128]{1,0:T(8,128)S(1)} collective-permute-done((f32[392,128]{1,0:T(8,128)S(1)}, f32[392,128]{1,0:T(8,128)S(1)}, u32[]{:S(2)}, u32[]{:S(2)}) %collective-permute-start.2) | collective-permute-done | bytes 200736 | tf_op jit(solution)/shard_map/ppermute | solution.py:359
  35.8 2.3 %collective-permute-done.5 = f32[392,128]{1,0:T(8,128)S(1)} collective-permute-done((f32[392,128]{1,0:T(8,128)S(1)}, f32[392,128]{1,0:T(8,128)S(1)}, u32[]{:S(2)}, u32[]{:S(2)}) %collective-permute-start.5) | collective-permute-done | bytes 200736 | tf_op jit(solution)/shard_map/ppermute | solution.py:359
  38.6 8.8 %collective-permute-done.4.refs_2_ = f32[384,128]{1,0:T(8,128)S(1)} collective-permute-done((f32[384,128]{1,0:T(8,128)S(1)}, f32[384,128]{1,0:T(8,128)S(1)}, u32[]{:S(2)}, u32[]{:S(2)}) %collective-permute-start.4) | collective-permute-done | bytes 196640 | tf_op jit(solution)/shard_map/ppermute | solution.py:359
  48.7 6.6 %collective-permute-done.6.refs_1_ = f32[768,128]{1,0:T(8,128)S(1)} collective-permute-done((f32[768,128]{1,0:T(8,128)S(1)}, f32[768,128]{1,0:T(8,128)S(1)}, u32[]{:S(2)}, u32[]{:S(2)}) %collective-permute-start.6) | collective-permute-done | bytes 393248 | tf_op jit(solution)/shard_map/ppermute | solution.py:359
  55.3 1.9 shard_map.72
  57.4 1.8 shard_map.73
  59.2 1.8 collective-permute-start.10
  61.1 4.0 %collective-permute-done.11.refs_1_ = f32[768,128]{1,0:T(8,128)S(1)} collective-permute-done((f32[768,128]{1,0:T(8,128)S(1)}, f32[768,128]{1,0:T(8,128)S(1)}, u32[]{:S(2)}, u32[]{:S(2)}) %collective-permute-start.11) | collective-permute-done | bytes 393248 | tf_op jit(solution)/shard_map/ppermute | solution.py:359
  65.1 1.9 shard_map.74
  68.2 1.8 shard_map.75
  70.4 1.4 shard_map.76
  71.9 1.6 collective-permute-start.15
  73.4 5.5 %collective-permute-done.14 = f32[520,128]{1,0:T(8,128)S(1)} collective-permute-done((f32[520,128]{1,0:T(8,128)S(1)}, f32[520,128]{1,0:T(8,128)S(1)}, u32[]{:S(2)}, u32[]{:S(2)}) %collective-permute-start.14) | collective-permute-done | bytes 266272 | tf_op jit(solution)/shard_map/ppermute | solution.py:362
  79.1 1.5 shard_map.77
  81.0 1.4 shard_map.78
  82.4 1.6 collective-permute-start.19
  84.0 3.5 %collective-permute-done.16 = f32[392,128]{1,0:T(8,128)S(1)} collective-permute-done((f32[392,128]{1,0:T(8,128)S(1)}, f32[392,128]{1,0:T(8,128)S(1)}, u32[]{:S(2)}, u32[]{:S(2)}) %collective-permute-start.16) | collective-permute-done | bytes 200736 | tf_op jit(solution)/shard_map/ppermute | solution.py:359
  90.4 1.8 collective-permute-start.21
  92.3 6.1 %collective-permute-done.18 = f32[392,128]{1,0:T(8,128)S(1)} collective-permute-done((f32[392,128]{1,0:T(8,128)S(1)}, f32[392,128]{1,0:T(8,128)S(1)}, u32[]{:S(2)}, u32[]{:S(2)}) %collective-permute-start.18) | collective-permute-done | bytes 200736 | tf_op jit(solution)/shard_map/ppermute | solution.py:359
  98.5 3.1 %collective-permute-start.23 = (f32[392,128]{1,0:T(8,128)S(1)}, f32[392,128]{1,0:T(8,128)S(1)}, u32[]{:S(2)}, u32[]{:S(2)}) collective-permute-start(f32[392,128]{1,0:T(8,128)S(1)} %pad_maximum_fusion.17), channel_id=1, source_target_pairs={{0,16},{1,17},{2,18},{3,19},{4,20},{5,21},{6,22},{7,23},{8,24},{9,... | collective-permute-start | bytes 602120 | tf_op jit(solution)/shard_map/ppermute | solution.py:359
  101.7 7.3 %collective-permute-done.20.refs_2_ = f32[384,128]{1,0:T(8,128)S(1)} collective-permute-done((f32[384,128]{1,0:T(8,128)S(1)}, f32[384,128]{1,0:T(8,128)S(1)}, u32[]{:S(2)}, u32[]{:S(2)}) %collective-permute-start.20) | collective-permute-done | bytes 196640 | tf_op jit(solution)/shard_map/ppermute | solution.py:359
  110.0 8.6 %collective-permute-done.22.refs_1_ = f32[768,128]{1,0:T(8,128)S(1)} collective-permute-done((f32[768,128]{1,0:T(8,128)S(1)}, f32[768,128]{1,0:T(8,128)S(1)}, u32[]{:S(2)}, u32[]{:S(2)}) %collective-permute-start.22) | collective-permute-done | bytes 393248 | tf_op jit(solution)/shard_map/ppermute | solution.py:359
  118.6 1.9 %shard_map.80 = (f32[520,128]{1,0:T(8,128)S(1)}, bf16[3072,128]{1,0:T(8,128)(2,1)S(1)}, f32[1536,128]{1,0:T(8,128)S(1)}) custom-call(bf16[2048,3072]{1,0:T(8,128)(2,1)S(1)} %get-tuple-element.87.refs_0_.dense_ref, f32[768,128]{1,0:T(8,128)S(1)} %collective-permute-done.22.refs_1_, f32[384,128]{1,0:T(8,128)S(1)} %collective-permute-done.20.refs_2_, ...), custom_call_target="tpu_custom_call" | custom-call | flops 1610612736 | bytes 6291456 | tf_op jit(solution)/shard_map/pallas_call | solution.py:219
  121.0 1.8 shard_map.81
  122.9 1.4 collective-permute-start.26
  124.3 4.2 %collective-permute-done.27.refs_1_ = f32[768,128]{1,0:T(8,128)S(1)} collective-permute-done((f32[768,128]{1,0:T(8,128)S(1)}, f32[768,128]{1,0:T(8,128)S(1)}, u32[]{:S(2)}, u32[]{:S(2)}) %collective-permute-start.27) | collective-permute-done | bytes 393248 | tf_op jit(solution)/shard_map/ppermute | solution.py:359
  128.5 1.9 %shard_map.82 = (f32[520,128]{1,0:T(8,128)S(1)}, bf16[3072,128]{1,0:T(8,128)(2,1)S(1)}, f32[1536,128]{1,0:T(8,128)S(1)}) custom-call(bf16[2048,3072]{1,0:T(8,128)(2,1)S(1)} %get-tuple-element.87.refs_0_.dense_ref, f32[768,128]{1,0:T(8,128)S(1)} %collective-permute-done.27.refs_1_, f32[384,128]{1,0:T(8,128)S(1)} %collective-permute-done.25.refs_2_, ...), custom_call_target="tpu_custom_call" | custom-call | flops 1610612736 | bytes 6291456 | tf_op jit(solution)/shard_map/pallas_call | solution.py:219
  131.6 1.8 shard_map.83
  134.1 1.4 shard_map.84
  136.7 5.6 %collective-permute-done.31 = f32[520,128]{1,0:T(8,128)S(1)} collective-permute-done((f32[520,128]{1,0:T(8,128)S(1)}, f32[520,128]{1,0:T(8,128)S(1)}, u32[]{:S(2)}, u32[]{:S(2)}) %collective-permute-start.31) | collective-permute-done | bytes 266272 | tf_op jit(solution)/shard_map/ppermute | solution.py:362
  144.0 1.6 shard_map.86
  146.4 4.1 %collective-permute-done.32 = f32[392,128]{1,0:T(8,128)S(1)} collective-permute-done((f32[392,128]{1,0:T(8,128)S(1)}, f32[392,128]{1,0:T(8,128)S(1)}, u32[]{:S(2)}, u32[]{:S(2)}) %collective-permute-start.32) | collective-permute-done | bytes 200736 | tf_op jit(solution)/shard_map/ppermute | solution.py:359
  153.6 2.1 %collective-permute-start.36 = (f32[392,128]{1,0:T(8,128)S(1)}, f32[392,128]{1,0:T(8,128)S(1)}, u32[]{:S(2)}, u32[]{:S(2)}) collective-permute-start(f32[392,128]{1,0:T(8,128)S(1)} %pad_maximum_fusion.20), channel_id=1, source_target_pairs={{0,8},{1,5},{2,10},{3,7},{4,12},{5,1},{6,14},{7,3},{8,0},{9,13},{1... | collective-permute-start | bytes 602120 | tf_op jit(solution)/shard_map/ppermute | solution.py:359
  155.7 6.0 %collective-permute-done.34 = f32[392,128]{1,0:T(8,128)S(1)} collective-permute-done((f32[392,128]{1,0:T(8,128)S(1)}, f32[392,128]{1,0:T(8,128)S(1)}, u32[]{:S(2)}, u32[]{:S(2)}) %collective-permute-start.34) | collective-permute-done | bytes 200736 | tf_op jit(solution)/shard_map/ppermute | solution.py:359
  163.2 5.9 %collective-permute-done.38.refs_1_ = f32[384,128]{1,0:T(8,128)S(1)} collective-permute-done((f32[384,128]{1,0:T(8,128)S(1)}, f32[384,128]{1,0:T(8,128)S(1)}, u32[]{:S(2)}, u32[]{:S(2)}) %collective-permute-start.38) | collective-permute-done | bytes 196640 | tf_op jit(solution)/shard_map/ppermute | solution.py:359
  169.2 2.9 %collective-permute-done.37 = f32[392,128]{1,0:T(8,128)S(1)} collective-permute-done((f32[392,128]{1,0:T(8,128)S(1)}, f32[392,128]{1,0:T(8,128)S(1)}, u32[]{:S(2)}, u32[]{:S(2)}) %collective-permute-start.37) | collective-permute-done | bytes 200736 | tf_op jit(solution)/shard_map/ppermute | solution.py:359
  173.1 6.9 %collective-permute-done.40.refs_10_ = f32[384,128]{1,0:T(8,128)S(1)} collective-permute-done((f32[384,128]{1,0:T(8,128)S(1)}, f32[384,128]{1,0:T(8,128)S(1)}, u32[]{:S(2)}, u32[]{:S(2)}) %collective-permute-start.40) | collective-permute-done | bytes 196640 | tf_op jit(solution)/shard_map/ppermute | solution.py:359
  180.9 1.7 shard_map.88
  183.2 4.7 %collective-permute-done.41.refs_9_ = f32[768,128]{1,0:T(8,128)S(1)} collective-permute-done((f32[768,128]{1,0:T(8,128)S(1)}, f32[768,128]{1,0:T(8,128)S(1)}, u32[]{:S(2)}, u32[]{:S(2)}) %collective-permute-start.41) | collective-permute-done | bytes 393248 | tf_op jit(solution)/shard_map/ppermute | solution.py:359
  187.9 1.7 shard_map.89
  (141 shorter events, 26.0 us)
Async XLA Ops:
  6.7 10.1 %collective-permute-start = (f32[776,128]{1,0:T(8,128)S(1)}, f32[776,128]{1,0:T(8,128)S(1)}, u32[]{:S(2)}, u32[]{:S(2)}) collective-permute-start(f32[776,128]{1,0:T(8,128)S(1)} %get-tuple-element.93), channel_id=1, source_target_pairs={{0,4},{1,9},{2,6},{3,11},{4,0},{5,13},{6,2},{7,15},{8,12},{9,1},{1... | collective-permute-start | bytes 1191944 | tf_op jit(solution)/shard_map/ppermute | solution.py:359
  16.9 10.0 %collective-permute-start.1 = (f32[392,128]{1,0:T(8,128)S(1)}, f32[392,128]{1,0:T(8,128)S(1)}, u32[]{:S(2)}, u32[]{:S(2)}) collective-permute-start(f32[392,128]{1,0:T(8,128)S(1)} %pad_maximum_fusion.10), channel_id=1, source_target_pairs={{0,8},{1,5},{2,10},{3,7},{4,12},{5,1},{6,14},{7,3},{8,0},{9,13},{1... | collective-permute-start | bytes 602120 | tf_op jit(solution)/shard_map/ppermute | solution.py:359
  17.8 11.6 %collective-permute-start.3 = (f32[776,128]{1,0:T(8,128)S(1)}, f32[776,128]{1,0:T(8,128)S(1)}, u32[]{:S(2)}, u32[]{:S(2)}) collective-permute-start(f32[776,128]{1,0:T(8,128)S(1)} %get-tuple-element.95), channel_id=1, source_target_pairs={{0,4},{1,9},{2,6},{3,11},{4,0},{5,13},{6,2},{7,15},{8,12},{9,1},{1... | collective-permute-start | bytes 1191944 | tf_op jit(solution)/shard_map/ppermute | solution.py:359
  27.0 8.7 %collective-permute-start.2 = (f32[392,128]{1,0:T(8,128)S(1)}, f32[392,128]{1,0:T(8,128)S(1)}, u32[]{:S(2)}, u32[]{:S(2)}) collective-permute-start(f32[392,128]{1,0:T(8,128)S(1)} %pad_maximum_fusion.11), channel_id=1, source_target_pairs={{0,16},{1,17},{2,18},{3,19},{4,20},{5,21},{6,22},{7,23},{8,24},{9,... | collective-permute-start | bytes 602120 | tf_op jit(solution)/shard_map/ppermute | solution.py:359
  29.4 8.7 %collective-permute-start.5 = (f32[392,128]{1,0:T(8,128)S(1)}, f32[392,128]{1,0:T(8,128)S(1)}, u32[]{:S(2)}, u32[]{:S(2)}) collective-permute-start(f32[392,128]{1,0:T(8,128)S(1)} %pad_maximum_fusion.12), channel_id=1, source_target_pairs={{0,8},{1,5},{2,10},{3,7},{4,12},{5,1},{6,14},{7,3},{8,0},{9,13},{1... | collective-permute-start | bytes 602120 | tf_op jit(solution)/shard_map/ppermute | solution.py:359
  35.7 11.6 %collective-permute-start.4 = (f32[384,128]{1,0:T(8,128)S(1)}, f32[384,128]{1,0:T(8,128)S(1)}, u32[]{:S(2)}, u32[]{:S(2)}) collective-permute-start(f32[384,128]{1,0:T(8,128)S(1)} %slice_add_fusion.25.refs_3_), channel_id=1, source_target_pairs={{0,8},{1,5},{2,10},{3,7},{4,12},{5,1},{6,14},{7,3},{8,0},{9,13},{1... | collective-permute-start | bytes 589832 | tf_op jit(solution)/shard_map/ppermute | solution.py:359
  38.2 9.3 %collective-permute-start.7 = (f32[392,128]{1,0:T(8,128)S(1)}, f32[392,128]{1,0:T(8,128)S(1)}, u32[]{:S(2)}, u32[]{:S(2)}) collective-permute-start(f32[392,128]{1,0:T(8,128)S(1)} %pad_maximum_fusion.13), channel_id=1, source_target_pairs={{0,16},{1,17},{2,18},{3,19},{4,20},{5,21},{6,22},{7,23},{8,24},{9,... | collective-permute-start | bytes 602120 | tf_op jit(solution)/shard_map/ppermute | solution.py:359
  47.4 7.8 %collective-permute-start.6 = (f32[768,128]{1,0:T(8,128)S(1)}, f32[768,128]{1,0:T(8,128)S(1)}, u32[]{:S(2)}, u32[]{:S(2)}) collective-permute-start(f32[768,128]{1,0:T(8,128)S(1)} %pad_maximum_fusion), channel_id=1, source_target_pairs={{0,4},{1,9},{2,6},{3,11},{4,0},{5,13},{6,2},{7,15},{8,12},{9,1},{1... | collective-permute-start | bytes 1179656 | tf_op jit(solution)/shard_map/ppermute | solution.py:359
  47.5 9.7 %collective-permute-start.8 = (f32[384,128]{1,0:T(8,128)S(1)}, f32[384,128]{1,0:T(8,128)S(1)}, u32[]{:S(2)}, u32[]{:S(2)}) collective-permute-start(f32[384,128]{1,0:T(8,128)S(1)} %slice_add_fusion.24.refs_3_), channel_id=1, source_target_pairs={{0,8},{1,5},{2,10},{3,7},{4,12},{5,1},{6,14},{7,3},{8,0},{9,13},{1... | collective-permute-start | bytes 589832 | tf_op jit(solution)/shard_map/ppermute | solution.py:359
  57.2 2.0 %collective-permute-start.9 = (f32[520,128]{1,0:T(8,128)S(1)}, f32[520,128]{1,0:T(8,128)S(1)}, u32[]{:S(2)}, u32[]{:S(2)}) collective-permute-start(f32[520,128]{1,0:T(8,128)S(1)} %get-tuple-element.107), channel_id=1, source_target_pairs={{0,1},{1,0},{2,3},{3,2},{4,5},{5,4},{6,7},{7,6},{8,9},{9,8},{10,11... | collective-permute-start | bytes 798728 | tf_op jit(solution)/shard_map/ppermute | solution.py:362
  57.3 7.8 %collective-permute-start.11 = (f32[768,128]{1,0:T(8,128)S(1)}, f32[768,128]{1,0:T(8,128)S(1)}, u32[]{:S(2)}, u32[]{:S(2)}) collective-permute-start(f32[768,128]{1,0:T(8,128)S(1)} %pad_maximum_fusion.1), channel_id=1, source_target_pairs={{0,4},{1,9},{2,6},{3,11},{4,0},{5,13},{6,2},{7,15},{8,12},{9,1},{1... | collective-permute-start | bytes 1179656 | tf_op jit(solution)/shard_map/ppermute | solution.py:359
  59.2 8.8 %collective-permute-start.10 = (f32[520,128]{1,0:T(8,128)S(1)}, f32[520,128]{1,0:T(8,128)S(1)}, u32[]{:S(2)}, u32[]{:S(2)}) collective-permute-start(f32[520,128]{1,0:T(8,128)S(1)} %pad_maximum_fusion.6), channel_id=1, source_target_pairs={{0,2},{1,3},{2,0},{3,1},{4,6},{5,7},{6,4},{7,5},{8,10},{9,11},{10,... | collective-permute-start | bytes 798728 | tf_op jit(solution)/shard_map/ppermute | solution.py:362
  67.0 3.0 %collective-permute-start.13 = (f32[520,128]{1,0:T(8,128)S(1)}, f32[520,128]{1,0:T(8,128)S(1)}, u32[]{:S(2)}, u32[]{:S(2)}) collective-permute-start(f32[520,128]{1,0:T(8,128)S(1)} %get-tuple-element.112), channel_id=1, source_target_pairs={{0,1},{1,0},{2,3},{3,2},{4,5},{5,4},{6,7},{7,6},{8,9},{9,8},{10,11... | collective-permute-start | bytes 798728 | tf_op jit(solution)/shard_map/ppermute | solution.py:362
  68.1 2.3 %collective-permute-start.12 = (f32[512,128]{1,0:T(8,128)S(1)}, f32[512,128]{1,0:T(8,128)S(1)}, u32[]{:S(2)}, u32[]{:S(2)}) collective-permute-start(f32[512,128]{1,0:T(8,128)S(1)} %slice_add_fusion.12.refs_2_), channel_id=1, source_target_pairs={{0,1},{1,0},{2,3},{3,2},{4,5},{5,4},{6,7},{7,6},{8,9},{9,8},{10,11... | collective-permute-start | bytes 786440 | tf_op jit(solution)/shard_map/ppermute | solution.py:362
  70.1 8.9 %collective-permute-start.14 = (f32[520,128]{1,0:T(8,128)S(1)}, f32[520,128]{1,0:T(8,128)S(1)}, u32[]{:S(2)}, u32[]{:S(2)}) collective-permute-start(f32[520,128]{1,0:T(8,128)S(1)} %pad_maximum_fusion.7), channel_id=1, source_target_pairs={{0,2},{1,3},{2,0},{3,1},{4,6},{5,7},{6,4},{7,5},{8,10},{9,11},{10,... | collective-permute-start | bytes 798728 | tf_op jit(solution)/shard_map/ppermute | solution.py:362
  71.9 8.7 %collective-permute-start.15 = (f32[776,128]{1,0:T(8,128)S(1)}, f32[776,128]{1,0:T(8,128)S(1)}, u32[]{:S(2)}, u32[]{:S(2)}) collective-permute-start(f32[776,128]{1,0:T(8,128)S(1)} %get-tuple-element.119), channel_id=1, source_target_pairs={{0,4},{1,9},{2,6},{3,11},{4,0},{5,13},{6,2},{7,15},{8,12},{9,1},{1... | collective-permute-start | bytes 1191944 | tf_op jit(solution)/shard_map/ppermute | solution.py:359
  79.0 2.0 %collective-permute-start.17 = (f32[512,128]{1,0:T(8,128)S(1)}, f32[512,128]{1,0:T(8,128)S(1)}, u32[]{:S(2)}, u32[]{:S(2)}) collective-permute-start(f32[512,128]{1,0:T(8,128)S(1)} %slice_add_fusion.10.refs_2_), channel_id=1, source_target_pairs={{0,1},{1,0},{2,3},{3,2},{4,5},{5,4},{6,7},{7,6},{8,9},{9,8},{10,11... | collective-permute-start | bytes 786440 | tf_op jit(solution)/shard_map/ppermute | solution.py:362
  80.7 6.9 %collective-permute-start.16 = (f32[392,128]{1,0:T(8,128)S(1)}, f32[392,128]{1,0:T(8,128)S(1)}, u32[]{:S(2)}, u32[]{:S(2)}) collective-permute-start(f32[392,128]{1,0:T(8,128)S(1)} %pad_maximum_fusion.14), channel_id=1, source_target_pairs={{0,8},{1,5},{2,10},{3,7},{4,12},{5,1},{6,14},{7,3},{8,0},{9,13},{1... | collective-permute-start | bytes 602120 | tf_op jit(solution)/shard_map/ppermute | solution.py:359
  82.4 7.9 %collective-permute-start.19 = (f32[776,128]{1,0:T(8,128)S(1)}, f32[776,128]{1,0:T(8,128)S(1)}, u32[]{:S(2)}, u32[]{:S(2)}) collective-permute-start(f32[776,128]{1,0:T(8,128)S(1)} %get-tuple-element.124), channel_id=1, source_target_pairs={{0,4},{1,9},{2,6},{3,11},{4,0},{5,13},{6,2},{7,15},{8,12},{9,1},{1... | collective-permute-start | bytes 1191944 | tf_op jit(solution)/shard_map/ppermute | solution.py:359
  87.6 10.8 %collective-permute-start.18 = (f32[392,128]{1,0:T(8,128)S(1)}, f32[392,128]{1,0:T(8,128)S(1)}, u32[]{:S(2)}, u32[]{:S(2)}) collective-permute-start(f32[392,128]{1,0:T(8,128)S(1)} %pad_maximum_fusion.15), channel_id=1, source_target_pairs={{0,16},{1,17},{2,18},{3,19},{4,20},{5,21},{6,22},{7,23},{8,24},{9,... | collective-permute-start | bytes 602120 | tf_op jit(solution)/shard_map/ppermute | solution.py:359
  90.4 8.0 %collective-permute-start.21 = (f32[392,128]{1,0:T(8,128)S(1)}, f32[392,128]{1,0:T(8,128)S(1)}, u32[]{:S(2)}, u32[]{:S(2)}) collective-permute-start(f32[392,128]{1,0:T(8,128)S(1)} %pad_maximum_fusion.16), channel_id=1, source_target_pairs={{0,8},{1,5},{2,10},{3,7},{4,12},{5,1},{6,14},{7,3},{8,0},{9,13},{1... | collective-permute-start | bytes 602120 | tf_op jit(solution)/shard_map/ppermute | solution.py:359
  98.4 10.5 %collective-permute-start.20 = (f32[384,128]{1,0:T(8,128)S(1)}, f32[384,128]{1,0:T(8,128)S(1)}, u32[]{:S(2)}, u32[]{:S(2)}) collective-permute-start(f32[384,128]{1,0:T(8,128)S(1)} %slice_add_fusion.23.refs_3_), channel_id=1, source_target_pairs={{0,8},{1,5},{2,10},{3,7},{4,12},{5,1},{6,14},{7,3},{8,0},{9,13},{1... | collective-permute-start | bytes 589832 | tf_op jit(solution)/shard_map/ppermute | solution.py:359
  98.5 11.4 %collective-permute-start.23 = (f32[392,128]{1,0:T(8,128)S(1)}, f32[392,128]{1,0:T(8,128)S(1)}, u32[]{:S(2)}, u32[]{:S(2)}) collective-permute-start(f32[392,128]{1,0:T(8,128)S(1)} %pad_maximum_fusion.17), channel_id=1, source_target_pairs={{0,16},{1,17},{2,18},{3,19},{4,20},{5,21},{6,22},{7,23},{8,24},{9,... | collective-permute-start | bytes 602120 | tf_op jit(solution)/shard_map/ppermute | solution.py:359
  109.0 9.6 %collective-permute-start.22 = (f32[768,128]{1,0:T(8,128)S(1)}, f32[768,128]{1,0:T(8,128)S(1)}, u32[]{:S(2)}, u32[]{:S(2)}) collective-permute-start(f32[768,128]{1,0:T(8,128)S(1)} %pad_maximum_fusion.2), channel_id=1, source_target_pairs={{0,4},{1,9},{2,6},{3,11},{4,0},{5,13},{6,2},{7,15},{8,12},{9,1},{1... | collective-permute-start | bytes 1179656 | tf_op jit(solution)/shard_map/ppermute | solution.py:359
  109.9 10.7 %collective-permute-start.25 = (f32[384,128]{1,0:T(8,128)S(1)}, f32[384,128]{1,0:T(8,128)S(1)}, u32[]{:S(2)}, u32[]{:S(2)}) collective-permute-start(f32[384,128]{1,0:T(8,128)S(1)} %slice_add_fusion.22.refs_3_), channel_id=1, source_target_pairs={{0,8},{1,5},{2,10},{3,7},{4,12},{5,1},{6,14},{7,3},{8,0},{9,13},{1... | collective-permute-start | bytes 589832 | tf_op jit(solution)/shard_map/ppermute | solution.py:359
  120.5 2.3 %collective-permute-start.24 = (f32[520,128]{1,0:T(8,128)S(1)}, f32[520,128]{1,0:T(8,128)S(1)}, u32[]{:S(2)}, u32[]{:S(2)}) collective-permute-start(f32[520,128]{1,0:T(8,128)S(1)} %get-tuple-element.135), channel_id=1, source_target_pairs={{0,1},{1,0},{2,3},{3,2},{4,5},{5,4},{6,7},{7,6},{8,9},{9,8},{10,11... | collective-permute-start | bytes 798728 | tf_op jit(solution)/shard_map/ppermute | solution.py:362
  120.6 7.8 %collective-permute-start.27 = (f32[768,128]{1,0:T(8,128)S(1)}, f32[768,128]{1,0:T(8,128)S(1)}, u32[]{:S(2)}, u32[]{:S(2)}) collective-permute-start(f32[768,128]{1,0:T(8,128)S(1)} %pad_maximum_fusion.3), channel_id=1, source_target_pairs={{0,4},{1,9},{2,6},{3,11},{4,0},{5,13},{6,2},{7,15},{8,12},{9,1},{1... | collective-permute-start | bytes 1179656 | tf_op jit(solution)/shard_map/ppermute | solution.py:359
  122.9 8.6 %collective-permute-start.26 = (f32[520,128]{1,0:T(8,128)S(1)}, f32[520,128]{1,0:T(8,128)S(1)}, u32[]{:S(2)}, u32[]{:S(2)}) collective-permute-start(f32[520,128]{1,0:T(8,128)S(1)} %pad_maximum_fusion.8), channel_id=1, source_target_pairs={{0,2},{1,3},{2,0},{3,1},{4,6},{5,7},{6,4},{7,5},{8,10},{9,11},{10,... | collective-permute-start | bytes 798728 | tf_op jit(solution)/shard_map/ppermute | solution.py:362
  130.4 2.9 %collective-permute-start.29 = (f32[520,128]{1,0:T(8,128)S(1)}, f32[520,128]{1,0:T(8,128)S(1)}, u32[]{:S(2)}, u32[]{:S(2)}) collective-permute-start(f32[520,128]{1,0:T(8,128)S(1)} %get-tuple-element.142), channel_id=1, source_target_pairs={{0,1},{1,0},{2,3},{3,2},{4,5},{5,4},{6,7},{7,6},{8,9},{9,8},{10,11... | collective-permute-start | bytes 798728 | tf_op jit(solution)/shard_map/ppermute | solution.py:362
  131.5 2.6 %collective-permute-start.28 = (f32[512,128]{1,0:T(8,128)S(1)}, f32[512,128]{1,0:T(8,128)S(1)}, u32[]{:S(2)}, u32[]{:S(2)}) collective-permute-start(f32[512,128]{1,0:T(8,128)S(1)} %slice_add_fusion.8.refs_2_), channel_id=1, source_target_pairs={{0,1},{1,0},{2,3},{3,2},{4,5},{5,4},{6,7},{7,6},{8,9},{9,8},{10,11... | collective-permute-start | bytes 786440 | tf_op jit(solution)/shard_map/ppermute | solution.py:362
  133.5 8.9 %collective-permute-start.31 = (f32[520,128]{1,0:T(8,128)S(1)}, f32[520,128]{1,0:T(8,128)S(1)}, u32[]{:S(2)}, u32[]{:S(2)}) collective-permute-start(f32[520,128]{1,0:T(8,128)S(1)} %pad_maximum_fusion.9), channel_id=1, source_target_pairs={{0,2},{1,3},{2,0},{3,1},{4,6},{5,7},{6,4},{7,5},{8,10},{9,11},{10,... | collective-permute-start | bytes 798728 | tf_op jit(solution)/shard_map/ppermute | solution.py:362
  135.5 8.2 %collective-permute-start.30 = (f32[776,128]{1,0:T(8,128)S(1)}, f32[776,128]{1,0:T(8,128)S(1)}, u32[]{:S(2)}, u32[]{:S(2)}) collective-permute-start(f32[776,128]{1,0:T(8,128)S(1)} %get-tuple-element.149), channel_id=1, source_target_pairs={{0,4},{1,9},{2,6},{3,11},{4,0},{5,13},{6,2},{7,15},{8,12},{9,1},{1... | collective-permute-start | bytes 1191944 | tf_op jit(solution)/shard_map/ppermute | solution.py:359
  142.3 1.6 collective-permute-start.33
  143.9 6.6 %collective-permute-start.32 = (f32[392,128]{1,0:T(8,128)S(1)}, f32[392,128]{1,0:T(8,128)S(1)}, u32[]{:S(2)}, u32[]{:S(2)}) collective-permute-start(f32[392,128]{1,0:T(8,128)S(1)} %pad_maximum_fusion.18), channel_id=1, source_target_pairs={{0,8},{1,5},{2,10},{3,7},{4,12},{5,1},{6,14},{7,3},{8,0},{9,13},{1... | collective-permute-start | bytes 602120 | tf_op jit(solution)/shard_map/ppermute | solution.py:359
  145.6 7.9 %collective-permute-start.35 = (f32[776,128]{1,0:T(8,128)S(1)}, f32[776,128]{1,0:T(8,128)S(1)}, u32[]{:S(2)}, u32[]{:S(2)}) collective-permute-start(f32[776,128]{1,0:T(8,128)S(1)} %get-tuple-element.156), channel_id=1, source_target_pairs={{0,4},{1,9},{2,6},{3,11},{4,0},{5,13},{6,2},{7,15},{8,12},{9,1},{1... | collective-permute-start | bytes 1191944 | tf_op jit(solution)/shard_map/ppermute | solution.py:359
  150.5 11.1 %collective-permute-start.34 = (f32[392,128]{1,0:T(8,128)S(1)}, f32[392,128]{1,0:T(8,128)S(1)}, u32[]{:S(2)}, u32[]{:S(2)}) collective-permute-start(f32[392,128]{1,0:T(8,128)S(1)} %pad_maximum_fusion.19), channel_id=1, source_target_pairs={{0,16},{1,17},{2,18},{3,19},{4,20},{5,21},{6,22},{7,23},{8,24},{9,... | collective-permute-start | bytes 602120 | tf_op jit(solution)/shard_map/ppermute | solution.py:359
  153.6 8.8 %collective-permute-start.36 = (f32[392,128]{1,0:T(8,128)S(1)}, f32[392,128]{1,0:T(8,128)S(1)}, u32[]{:S(2)}, u32[]{:S(2)}) collective-permute-start(f32[392,128]{1,0:T(8,128)S(1)} %pad_maximum_fusion.20), channel_id=1, source_target_pairs={{0,8},{1,5},{2,10},{3,7},{4,12},{5,1},{6,14},{7,3},{8,0},{9,13},{1... | collective-permute-start | bytes 602120 | tf_op jit(solution)/shard_map/ppermute | solution.py:359
  161.7 7.5 %collective-permute-start.38 = (f32[384,128]{1,0:T(8,128)S(1)}, f32[384,128]{1,0:T(8,128)S(1)}, u32[]{:S(2)}, u32[]{:S(2)}) collective-permute-start(f32[384,128]{1,0:T(8,128)S(1)} %slice_add_fusion.21.refs_2_), channel_id=1, source_target_pairs={{0,8},{1,5},{2,10},{3,7},{4,12},{5,1},{6,14},{7,3},{8,0},{9,13},{1... | collective-permute-start | bytes 589832 | tf_op jit(solution)/shard_map/ppermute | solution.py:359
  162.5 9.6 %collective-permute-start.37 = (f32[392,128]{1,0:T(8,128)S(1)}, f32[392,128]{1,0:T(8,128)S(1)}, u32[]{:S(2)}, u32[]{:S(2)}) collective-permute-start(f32[392,128]{1,0:T(8,128)S(1)} %pad_maximum_fusion.21), channel_id=1, source_target_pairs={{0,16},{1,17},{2,18},{3,19},{4,20},{5,21},{6,22},{7,23},{8,24},{9,... | collective-permute-start | bytes 602120 | tf_op jit(solution)/shard_map/ppermute | solution.py:359
  172.1 7.9 %collective-permute-start.40 = (f32[384,128]{1,0:T(8,128)S(1)}, f32[384,128]{1,0:T(8,128)S(1)}, u32[]{:S(2)}, u32[]{:S(2)}) collective-permute-start(f32[384,128]{1,0:T(8,128)S(1)} %slice_add_fusion.20.refs_11_), channel_id=1, source_target_pairs={{0,8},{1,5},{2,10},{3,7},{4,12},{5,1},{6,14},{7,3},{8,0},{9,13},{1... | collective-permute-start | bytes 589832 | tf_op jit(solution)/shard_map/ppermute | solution.py:359
  172.2 11.0 %collective-permute-start.39 = (f32[768,128]{1,0:T(8,128)S(1)}, f32[768,128]{1,0:T(8,128)S(1)}, u32[]{:S(2)}, u32[]{:S(2)}) collective-permute-start(f32[768,128]{1,0:T(8,128)S(1)} %pad_maximum_fusion.4), channel_id=1, source_target_pairs={{0,4},{1,9},{2,6},{3,11},{4,0},{5,13},{6,2},{7,15},{8,12},{9,1},{1... | collective-permute-start | bytes 1179656 | tf_op jit(solution)/shard_map/ppermute | solution.py:359
  180.0 7.8 %collective-permute-start.41 = (f32[768,128]{1,0:T(8,128)S(1)}, f32[768,128]{1,0:T(8,128)S(1)}, u32[]{:S(2)}, u32[]{:S(2)}) collective-permute-start(f32[768,128]{1,0:T(8,128)S(1)} %pad_maximum_fusion.5), channel_id=1, source_target_pairs={{0,4},{1,9},{2,6},{3,11},{4,0},{5,13},{6,2},{7,15},{8,12},{9,1},{1... | collective-permute-start | bytes 1179656 | tf_op jit(solution)/shard_map/ppermute | solution.py:359

commit v14 on v13

--- a/solution.py
+++ b/solution.py
@@ -118,27 +118,37 @@
     return row + turned(row)
 
 
-def next_vector(parts, raw_ref, scale_ref, past_ref, past_scale_ref):
+def next_vector(units, pairs, raw_ref, scale_ref, past_ref, past_scale_ref, other=False):
     if scale_ref is not None:
         scale = norm_of(scale_ref)
     if past_ref is not None:
         past_scale = norm_of(past_scale_ref)
     position = 0
-    for part, units in parts:
-        pairs = part.shape[0] // TILE // units
-        for unit in range(units):
-            squares = jnp.zeros((NORM_ROWS, TILE), jnp.float32)
-            for pair in range(pairs):
-                value = part[rows_of(unit * pairs + pair), :]
-                if scale_ref is not None:
-                    value = value / scale
-                if past_ref is not None:
-                    value = value - scale * (past_ref[rows_of(position), :] / past_scale)
-                if raw_ref is not None:
-                    raw_ref[rows_of(position), :] = value
-                squares += jnp.sum((value * value).reshape(-1, NORM_ROWS, TILE), axis=0)
-                yield position, value, squares if pair == pairs - 1 else None
-                position += 1
+    for places in units:
+        squares = jnp.zeros((NORM_ROWS, TILE), jnp.float32)
+        for pair in range(pairs):
+            value, *others = [ref[rows_of(start + pair), :] for ref, start in places]
+            if others:
+                value = jnp.where(other, others[0], value)
+            if scale_ref is not None:
+                value = value / scale
+            if past_ref is not None:
+                value = value - scale * (past_ref[rows_of(position), :] / past_scale)
+            if raw_ref is not None:
+                raw_ref[rows_of(position), :] = value
+            squares += jnp.sum((value * value).reshape(-1, NORM_ROWS, TILE), axis=0)
+            yield position, value, squares if pair == pairs - 1 else None
+            position += 1
+
+
+def gathered_units(outer_ref, inner_ref, mine_ref, crossed):
+    pairs = mine_ref.shape[0] // TILE
+    second, third = (outer_ref, pairs), (inner_ref, 0)
+    if crossed:
+        middle = [(second, third), (third, second)]
+    else:
+        middle = [(second,), (third,)]
+    return [((outer_ref, 0),), *middle, ((mine_ref, 0),)], pairs
 
 
 def back_pairs(dense_ref, turned_ref, out_ref, start):
@@ -155,14 +165,16 @@
 def back_send_kernel(first, *refs):
     if first:
         dense_ref, own_ref, send_ref, turned_ref = refs
-        parts, raw_ref, scales = [(own_ref, 2)], None, (None, None, None)
+        pairs = own_ref.shape[0] // PAIR
+        units, raw_ref, scales = [((own_ref, 0),), ((own_ref, pairs),)], None, (None, None, None)
     else:
         (dense_ref, other_ref, own_ref, scale_ref, past_ref, past_scale_ref,
          send_ref, turned_ref, raw_ref) = refs
-        parts, scales = [(other_ref, 1), (own_ref, 1)], (scale_ref, past_ref, past_scale_ref)
+        pairs = own_ref.shape[0] // TILE
+        units, scales = [((other_ref, 0),), ((own_ref, 0),)], (scale_ref, past_ref, past_scale_ref)
     sums = []
     half = turned_ref.shape[0]
-    for pair, value, squares in next_vector(parts, raw_ref, *scales):
+    for pair, value, squares in next_vector(units, pairs, raw_ref, *scales):
         flat = value.T.astype(turned_ref.dtype)
         turned_ref[:, rows_of(2 * pair)] = flat[:half]
         turned_ref[:, rows_of(2 * pair + 1)] = flat[half:]
@@ -190,18 +202,16 @@
             out_ref[rows_of(pair + i), :] = jnp.where(low, even, odd)
 
 
-def fore_send_kernel(first, *refs):
-    if first:
-        (dense_ref, outer_ref, inner_ref, mine_ref, scale_ref, send_ref, wide_ref, raw_ref) = refs
-        scales = (scale_ref, None, None)
-    else:
-        (dense_ref, outer_ref, inner_ref, mine_ref, scale_ref, past_ref, past_scale_ref,
-         send_ref, wide_ref, raw_ref) = refs
-        scales = (scale_ref, past_ref, past_scale_ref)
-    parts = [(outer_ref, 2), (inner_ref, 1), (mine_ref, 1)]
+def fore_send_kernel(first, crossed, *refs):
+    core_ref, dense_ref, outer_ref, inner_ref, mine_ref, scale_ref, *refs = refs
+    past_ref, past_scale_ref = (None, None) if first else refs[:2]
+    send_ref, wide_ref, raw_ref = refs[-3:]
+    scales = (scale_ref, past_ref, past_scale_ref)
+    units, pairs = gathered_units(outer_ref, inner_ref, mine_ref, crossed)
     low = low_lanes((TILE, TILE))
     sums = []
-    for pair, value, squares in next_vector(parts, raw_ref, *scales):
+    vector = next_vector(units, pairs, raw_ref, *scales, other=core_ref[0] != 0)
+    for pair, value, squares in vector:
         other = turned(value)
         wide_ref[rows_of(2 * pair), :] = jnp.where(low, value, other).astype(wide_ref.dtype)
         wide_ref[rows_of(2 * pair + 1), :] = jnp.where(low, other, value).astype(wide_ref.dtype)
@@ -215,17 +225,17 @@
     fore_pairs(dense_ref, wide_ref, keep_ref, keep_ref.shape[0] // TILE)
 
 
-def product_call(body, dense, operands, shapes):
+def product_call(body, dense, operands, shapes, scalars=()):
     return pl.pallas_call(
         body,
-        in_specs=[WHOLE] * (1 + len(operands)),
+        in_specs=[SCALARS] * len(scalars) + [WHOLE] * (1 + len(operands)),
         out_specs=[WHOLE] * len(shapes),
         out_shape=shapes,
         compiler_params=pltpu.CompilerParams(vmem_limit_bytes=12 * 1024 * 1024),
         cost_estimate=pl.CostEstimate(
             flops=2 * TILE * dense.size, bytes_accessed=dense.size, transcendentals=0
         ),
-    )(dense, *operands)
+    )(*scalars, dense, *operands)
 
 
 def float_rows(rows):
@@ -247,7 +257,7 @@
     return send, (keep, flat), *raw
 
 
-def fore_product(dense, operands, first):
+def fore_product(core, dense, operands, first, crossed):
     rows, cells = dense.shape
     shapes = [
         float_rows(rows // 4 + NORM_ROWS),
@@ -255,7 +265,7 @@
         float_rows(cells // 2),
     ]
     send, wide, raw = product_call(
-        functools.partial(fore_send_kernel, first), dense, operands, shapes
+        functools.partial(fore_send_kernel, first, crossed), dense, operands, shapes, [core]
     )
 
 
@@ -294,7 +304,7 @@
     out_ref[odd, :] = jnp.where(low, turned(ours), theirs)
 
 
-def model_kernel(count, mask_ref, *refs):
+def model_kernel(count, mask_ref, core_ref, *refs):
     ins, (model_ref, misfit_ref) = refs[:-2], refs[-2:]
     chains = [ins[: len(ins) // 2], ins[len(ins) // 2 :]]
     low = low_lanes((TILE, TILE))
@@ -313,33 +323,33 @@
         store_in_order(model_ref, mask_ref[0], pair, low, values)
 
 
-def gradient_kernel(mask_ref, *refs):
+def gradient_kernel(mask_ref, core_ref, *refs):
     ins, gradient_ref = refs[:-1], refs[-1]
     chains = [ins[: len(ins) // 2], ins[len(ins) // 2 :]]
     low = low_lanes((TILE, TILE))
     vectors = []
     factors = []
-    for outer_ref, inner_ref, mine_ref, past_ref, *norms in chains:
-        alphas, betas, _, _, factor = rotation(norms)
-        parts = [(outer_ref, 2), (inner_ref, 1), (mine_ref, 1)]
-        vectors.append(next_vector(parts, None, norms[-1], past_ref, norms[-2]))
-        factors.append(factor)
+    for second, (outer_ref, inner_ref, mine_ref, past_ref, *norms) in enumerate(chains):
+        units, pairs = gathered_units(outer_ref, inner_ref, mine_ref, not second)
+        scales = (norms[-1], past_ref, norms[-2])
+        vectors.append(next_vector(units, pairs, None, *scales, other=core_ref[0] != 0))
+        factors.append(rotation(norms)[-1])
     for ours, theirs in zip(*vectors):
         values = [factors[0] * ours[1], factors[1] * theirs[1]]
         store_in_order(gradient_ref, mask_ref[0], ours[0], low, values)
 
 
-def last_call(body, mask, operands, shapes):
+def last_call(body, scalars, operands, shapes):
     return pl.pallas_call(
         body,
-        in_specs=[SCALARS] + [WHOLE] * len(operands),
+        in_specs=[SCALARS] * len(scalars) + [WHOLE] * len(operands),
         out_specs=[WHOLE] * len(shapes),
         out_shape=[jax.ShapeDtypeStruct(shape, jnp.float32) for shape in shapes],
         compiler_params=pltpu.CompilerParams(vmem_limit_bytes=12 * 1024 * 1024),
         cost_estimate=pl.CostEstimate(
             flops=0, bytes_accessed=8 * shapes[0][0] * TILE, transcendentals=0
         ),
-    )(mask, *operands)
+    )(*scalars, *operands)
 
 
 def on_device(row_count, col_count, kernel, pattern, counts, delays):
@@ -348,13 +358,17 @@
     row_index = lax.axis_index("rows")
     core = lax.axis_index("cols") & 1
 
-    orders = [row_bits, [row_bits[1], row_bits[0], *row_bits[2:]]]
-
-    def swap_rows(value, level):
+    near, far, *rest = row_bits
+    add_up = [[near, far, *rest], [far, near, *rest]]
+    gather = [[[far, near], [far, near]], [[far, near], [near, far]]]
+    steps = len(row_bits) + 2
+
+    def swap_rows(second, value, level):
         pairs = []
         for row in range(row_count):
             for col in range(col_count):
-                partner = row ^ (1 << orders[col & 1][level])
+                order = add_up[col & 1] + gather[second][col & 1]
+                partner = row ^ (1 << order[level])
                 pairs.append((row * col_count + col, partner * col_count + col))
         return lax.ppermute(value, ("rows", "cols"), pairs)
 
@@ -370,6 +384,7 @@
     places = ((blocks // unit) ^ mask) * unit + blocks % unit
     flip = ((1 - core) * (kernel.shape[0] // 2)).astype(jnp.int32).reshape(1)
     mask = mask.reshape(1)
+    core_index = core.astype(jnp.int32).reshape(1)
 
     dense, *lefts = fill_dense(kernel, pattern, counts, places, flip, delays)
 
@@ -380,7 +395,7 @@
         half, operand = kept
         return half(tied(operand, ahead))
 
-    def reduce_rows(send, kept):
+    def reduce_rows(swap_rows, send, kept):
         half = send.shape[0] - NORM_ROWS
         got, ahead = yield swap_rows, send, 0
         keep = kept_half(kept, ahead) + got[:half]
@@ -390,8 +405,8 @@
             got, _ = yield swap_rows, jnp.concatenate([send, norm]), level
             norm = norm + got[half // 2 :]
             send = mine = mine + got[: half // 2]
-        inner, _ = yield swap_rows, mine, 1
-        outer, _ = yield swap_rows, jnp.concatenate([inner, mine]), 0
+        inner, _ = yield swap_rows, mine, steps - 2
+        outer, _ = yield swap_rows, jnp.concatenate([inner, mine]), steps - 1
         return [outer, inner, mine], norm
 
     def reduce_cols(send, kept):
@@ -406,25 +421,28 @@
         other, _ = yield swap_cols, own, 0
         return [other, own], norm
 
-    def chain(left):
+    def chain(second, left):
+        swap = functools.partial(swap_rows, second)
         send, keep = back_product(dense, [left], True)
-        totals, norm = yield from reduce_rows(send, keep)
+        totals, norm = yield from reduce_rows(swap, send, keep)
         norms = [norm]
         rights = []
         for iteration in range(ITERS):
             past = [rights[-1], norms[-2]] if rights else []
-            send, keep, right = fore_product(dense, [*totals, norms[-1], *past], not rights)
+            send, keep, right = fore_product(
+                core_index, dense, [*totals, norms[-1], *past], not rights, not second
+            )
             rights.append(right)
             halves, norm = yield from reduce_cols(send, keep)
             norms.append(norm)
             send, keep, left = back_product(
                 dense, [*halves, norms[-1], left, norms[-2]], False
             )
-            totals, norm = yield from reduce_rows(send, keep)
+            totals, norm = yield from reduce_rows(swap, send, keep)
             norms.append(norm)
         return rights, norms, totals
 
-    runs = [chain(left) for left in lefts]
+    runs = [chain(second, left) for second, left in enumerate(lefts)]
     wanted = [next(run) for run in runs]
     chains = [None] * len(runs)
     gots = [None] * len(runs)
@@ -451,13 +469,13 @@
     cells = dense.shape[1]
     model, misfit = last_call(
         functools.partial(model_kernel, ITERS),
-        mask,
+        [mask, core_index],
         [operand for rights, norms, _ in chains for operand in [*rights, *norms]],
         [(cells, TILE), (NORM_ROWS, TILE)],
     )
     (gradient,) = last_call(
         gradient_kernel,
-        mask,
+        [mask, core_index],
         [operand for rights, norms, totals in chains for operand in [*totals, rights[-1], *norms]],
         [(cells, TILE)],
     )

time: 190 us -> 189 us (level)
  starting transfers between devices: 34.7 us -> 50 us
  waiting for transfers between devices: 112 us -> 97 us
    ppermute x30, starting transfers between devices: 29.9 us -> 46.5 us  [swap_rows(): return lax.ppermute(value, ('rows', 'cols'), pairs)]
    ppermute x30, waiting for transfers between devices: 98.8 us -> 85 us  [swap_rows(): return lax.ppermute(value, ('rows', 'cols'), pairs)]
  transfers between devices with their start and end apart: 42 -> 42, of which waited for: 26 -> 28; matrix products, arithmetic and copies ran while one was open for 1% -> 1% of each run, Pallas kernels for 17% -> 17%
where the time goes in v14:
time: 189 us; the launch traced here: 190 us
  waiting for transfers between devices  97 us (51%)
  starting transfers between devices  50 us (26%)
  Pallas kernels  39.6 us (21%)
    ppermute x30, waiting for transfers between devices, swap_rows(): return lax.ppermute(value, ('rows', 'cols'), pairs)  85 us
    ppermute x30, starting transfers between devices, swap_rows(): return lax.ppermute(value, ('rows', 'cols'), pairs)  46.5 us
    pallas_call x20, Pallas kernels, product_call(): pl.pallas_call(body, in_specs=[SCALARS] * len(scalars) + [WHOLE] * (1 + l...  31.4 us
    ppermute x12, waiting for transfers between devices, swap_cols(): lax.ppermute(value, 'cols', [(i, i ^ 1 << level) for i in range(col_count)])  12.1 us
    pallas_call x1, Pallas kernels, fill_dense(): pl.pallas_call(fill_kernel, in_specs=[SCALARS] * 2 + [pl.BlockSpec(memory...  4.78 us
  transfers between devices with their start and end apart: 42, of which 28 were waited for; matrix products, arithmetic and copies ran while one was open for 1% of the time, Pallas kernels for 17%

profile of v14, /device:TPU:0, one launch (start us, length us, event | category | flops | bytes accessed | tf_op | source)
XLA Modules:
  0.0 190.1 jit_solution(1631616640012510219)
XLA Ops:
  0.7 4.8 %shard_map.67 = (bf16[2048,3072]{1,0:T(8,128)(2,1)S(1)}, f32[1024,128]{1,0:T(8,128)S(1)}, f32[1024,128]{1,0:T(8,128)S(1)}) custom-call(s32[24]{0:T(128)S(1)} %fusion.place_ref, s32[1]{0:T(128)} %bitcast.2.flip_ref, s32[16,16]{1,0:T(8,128)} %pattern_in.1, s32[16]{0:T(128)} %bitcast.6, f32[2048,128]{1,0:T(8,128)} %delays_in.1, bf16[16,16,128,128]{3,2,1,0:T(8,128)(2,1)} %tiles_in.1), custom_call_target="tpu_custom_call" | custom-call | bytes 8388608 | tf_op jit(solution)/shard_map/pallas_call | solution.py:87
  6.8 2.7 %collective-permute-start = (f32[776,128]{1,0:T(8,128)S(1)}, f32[776,128]{1,0:T(8,128)S(1)}, u32[]{:S(2)}, u32[]{:S(2)}) collective-permute-start(f32[776,128]{1,0:T(8,128)S(1)} %get-tuple-element.93), channel_id=1, source_target_pairs={{0,4},{1,9},{2,6},{3,11},{4,0},{5,13},{6,2},{7,15},{8,12},{9,1},{1... | collective-permute-start | bytes 1191944 | tf_op jit(solution)/shard_map/ppermute | solution.py:373
  12.2 3.1 %collective-permute-done = f32[776,128]{1,0:T(8,128)S(1)} collective-permute-done((f32[776,128]{1,0:T(8,128)S(1)}, f32[776,128]{1,0:T(8,128)S(1)}, u32[]{:S(2)}, u32[]{:S(2)}) %collective-permute-start) | collective-permute-done | bytes 397344 | tf_op jit(solution)/shard_map/ppermute | solution.py:373
  15.4 2.1 %collective-permute-start.1 = (f32[392,128]{1,0:T(8,128)S(1)}, f32[392,128]{1,0:T(8,128)S(1)}, u32[]{:S(2)}, u32[]{:S(2)}) collective-permute-start(f32[392,128]{1,0:T(8,128)S(1)} %pad_maximum_fusion.10), channel_id=1, source_target_pairs={{0,8},{1,5},{2,10},{3,7},{4,12},{5,1},{6,14},{7,3},{8,0},{9,13},{1... | collective-permute-start | bytes 602120 | tf_op jit(solution)/shard_map/ppermute | solution.py:373
  17.6 1.5 collective-permute-start.3
  19.1 4.3 %collective-permute-done.1 = f32[392,128]{1,0:T(8,128)S(1)} collective-permute-done((f32[392,128]{1,0:T(8,128)S(1)}, f32[392,128]{1,0:T(8,128)S(1)}, u32[]{:S(2)}, u32[]{:S(2)}) %collective-permute-start.1) | collective-permute-done | bytes 200736 | tf_op jit(solution)/shard_map/ppermute | solution.py:373
  23.5 3.1 %collective-permute-start.2 = (f32[392,128]{1,0:T(8,128)S(1)}, f32[392,128]{1,0:T(8,128)S(1)}, u32[]{:S(2)}, u32[]{:S(2)}) collective-permute-start(f32[392,128]{1,0:T(8,128)S(1)} %pad_maximum_fusion.11), channel_id=1, source_target_pairs={{0,16},{1,17},{2,18},{3,19},{4,20},{5,21},{6,22},{7,23},{8,24},{9,... | collective-permute-start | bytes 602120 | tf_op jit(solution)/shard_map/ppermute | solution.py:373
  28.0 3.2 %collective-permute-start.5 = (f32[392,128]{1,0:T(8,128)S(1)}, f32[392,128]{1,0:T(8,128)S(1)}, u32[]{:S(2)}, u32[]{:S(2)}) collective-permute-start(f32[392,128]{1,0:T(8,128)S(1)} %pad_maximum_fusion.12), channel_id=1, source_target_pairs={{0,8},{1,5},{2,10},{3,7},{4,12},{5,1},{6,14},{7,3},{8,0},{9,13},{1... | collective-permute-start | bytes 602120 | tf_op jit(solution)/shard_map/ppermute | solution.py:373
  31.1 2.8 %collective-permute-done.2 = f32[392,128]{1,0:T(8,128)S(1)} collective-permute-done((f32[392,128]{1,0:T(8,128)S(1)}, f32[392,128]{1,0:T(8,128)S(1)}, u32[]{:S(2)}, u32[]{:S(2)}) %collective-permute-start.2) | collective-permute-done | bytes 200736 | tf_op jit(solution)/shard_map/ppermute | solution.py:373
  34.0 3.0 %collective-permute-done.5 = f32[392,128]{1,0:T(8,128)S(1)} collective-permute-done((f32[392,128]{1,0:T(8,128)S(1)}, f32[392,128]{1,0:T(8,128)S(1)}, u32[]{:S(2)}, u32[]{:S(2)}) %collective-permute-start.5) | collective-permute-done | bytes 200736 | tf_op jit(solution)/shard_map/ppermute | solution.py:373
  37.1 2.4 %collective-permute-start.7 = (f32[392,128]{1,0:T(8,128)S(1)}, f32[392,128]{1,0:T(8,128)S(1)}, u32[]{:S(2)}, u32[]{:S(2)}) collective-permute-start(f32[392,128]{1,0:T(8,128)S(1)} %pad_maximum_fusion.13), channel_id=1, source_target_pairs={{0,16},{1,17},{2,18},{3,19},{4,20},{5,21},{6,22},{7,23},{8,24},{9,... | collective-permute-start | bytes 602120 | tf_op jit(solution)/shard_map/ppermute | solution.py:373
  40.6 1.9 %collective-permute-start.6 = (f32[768,128]{1,0:T(8,128)S(1)}, f32[768,128]{1,0:T(8,128)S(1)}, u32[]{:S(2)}, u32[]{:S(2)}) collective-permute-start(f32[768,128]{1,0:T(8,128)S(1)} %pad_maximum_fusion), channel_id=1, source_target_pairs={{0,4},{1,5},{2,6},{3,7},{4,0},{5,1},{6,2},{7,3},{8,12},{9,13},{10,... | collective-permute-start | bytes 1179656 | tf_op jit(solution)/shard_map/ppermute | solution.py:373
  42.5 3.4 %collective-permute-done.7 = f32[392,128]{1,0:T(8,128)S(1)} collective-permute-done((f32[392,128]{1,0:T(8,128)S(1)}, f32[392,128]{1,0:T(8,128)S(1)}, u32[]{:S(2)}, u32[]{:S(2)}) %collective-permute-start.7) | collective-permute-done | bytes 200736 | tf_op jit(solution)/shard_map/ppermute | solution.py:373
  46.5 2.2 %collective-permute-done.6.refs_2_ = f32[768,128]{1,0:T(8,128)S(1)} collective-permute-done((f32[768,128]{1,0:T(8,128)S(1)}, f32[768,128]{1,0:T(8,128)S(1)}, u32[]{:S(2)}, u32[]{:S(2)}) %collective-permute-start.6) | collective-permute-done | bytes 393248 | tf_op jit(solution)/shard_map/ppermute | solution.py:373
  48.6 1.9 %shard_map.72 = (f32[520,128]{1,0:T(8,128)S(1)}, bf16[3072,128]{1,0:T(8,128)(2,1)S(1)}, f32[1536,128]{1,0:T(8,128)S(1)}) custom-call(s32[1]{0:T(128)} %bitcast.1.refs_0_.core_ref, bf16[2048,3072]{1,0:T(8,128)(2,1)S(1)} %get-tuple-element.87.refs_0_.dense_ref.refs_1_, f32[768,128]{1,0:T(8,128)S(1)} %collective-permute-done.6.refs_2_, ...), custom_call_target="tpu_custom_call" | custom-call | flops 1610612736 | bytes 6291456 | tf_op jit(solution)/shard_map/pallas_call | solution.py:229
  51.7 3.4 %collective-permute-start.11 = (f32[768,128]{1,0:T(8,128)S(1)}, f32[768,128]{1,0:T(8,128)S(1)}, u32[]{:S(2)}, u32[]{:S(2)}) collective-permute-start(f32[768,128]{1,0:T(8,128)S(1)} %pad_maximum_fusion.1), channel_id=1, source_target_pairs={{0,4},{1,9},{2,6},{3,11},{4,0},{5,13},{6,2},{7,15},{8,12},{9,1},{1... | collective-permute-start | bytes 1179656 | tf_op jit(solution)/shard_map/ppermute | solution.py:373
  55.1 1.8 shard_map.73
  57.9 2.9 %collective-permute-done.11.refs_2_ = f32[768,128]{1,0:T(8,128)S(1)} collective-permute-done((f32[768,128]{1,0:T(8,128)S(1)}, f32[768,128]{1,0:T(8,128)S(1)}, u32[]{:S(2)}, u32[]{:S(2)}) %collective-permute-start.11) | collective-permute-done | bytes 393248 | tf_op jit(solution)/shard_map/ppermute | solution.py:373
  60.8 1.9 shard_map.74
  63.6 1.8 shard_map.75
  67.9 1.9 %collective-permute-start.15 = (f32[776,128]{1,0:T(8,128)S(1)}, f32[776,128]{1,0:T(8,128)S(1)}, u32[]{:S(2)}, u32[]{:S(2)}) collective-permute-start(f32[776,128]{1,0:T(8,128)S(1)} %get-tuple-element.119), channel_id=1, source_target_pairs={{0,4},{1,9},{2,6},{3,11},{4,0},{5,13},{6,2},{7,15},{8,12},{9,1},{1... | collective-permute-start | bytes 1191944 | tf_op jit(solution)/shard_map/ppermute | solution.py:373
  69.8 4.5 %collective-permute-done.14 = f32[520,128]{1,0:T(8,128)S(1)} collective-permute-done((f32[520,128]{1,0:T(8,128)S(1)}, f32[520,128]{1,0:T(8,128)S(1)}, u32[]{:S(2)}, u32[]{:S(2)}) %collective-permute-start.14) | collective-permute-done | bytes 266272 | tf_op jit(solution)/shard_map/ppermute | solution.py:376
  74.4 1.5 shard_map.77
  79.4 2.4 %collective-permute-done.16 = f32[392,128]{1,0:T(8,128)S(1)} collective-permute-done((f32[392,128]{1,0:T(8,128)S(1)}, f32[392,128]{1,0:T(8,128)S(1)}, u32[]{:S(2)}, u32[]{:S(2)}) %collective-permute-start.16) | collective-permute-done | bytes 200736 | tf_op jit(solution)/shard_map/ppermute | solution.py:373
  81.9 7.4 %collective-permute-start.18 = (f32[392,128]{1,0:T(8,128)S(1)}, f32[392,128]{1,0:T(8,128)S(1)}, u32[]{:S(2)}, u32[]{:S(2)}) collective-permute-start(f32[392,128]{1,0:T(8,128)S(1)} %pad_maximum_fusion.15), channel_id=1, source_target_pairs={{0,16},{1,17},{2,18},{3,19},{4,20},{5,21},{6,22},{7,23},{8,24},{9,... | collective-permute-start | bytes 602120 | tf_op jit(solution)/shard_map/ppermute | solution.py:373
  90.8 6.1 %collective-permute-done.18 = f32[392,128]{1,0:T(8,128)S(1)} collective-permute-done((f32[392,128]{1,0:T(8,128)S(1)}, f32[392,128]{1,0:T(8,128)S(1)}, u32[]{:S(2)}, u32[]{:S(2)}) %collective-permute-start.18) | collective-permute-done | bytes 200736 | tf_op jit(solution)/shard_map/ppermute | solution.py:373
  97.9 1.5 collective-permute-start.23
  99.4 5.5 %collective-permute-done.20.refs_3_ = f32[384,128]{1,0:T(8,128)S(1)} collective-permute-done((f32[384,128]{1,0:T(8,128)S(1)}, f32[384,128]{1,0:T(8,128)S(1)}, u32[]{:S(2)}, u32[]{:S(2)}) %collective-permute-start.20) | collective-permute-done | bytes 196640 | tf_op jit(solution)/shard_map/ppermute | solution.py:373
  105.4 3.3 %collective-permute-done.23 = f32[392,128]{1,0:T(8,128)S(1)} collective-permute-done((f32[392,128]{1,0:T(8,128)S(1)}, f32[392,128]{1,0:T(8,128)S(1)}, u32[]{:S(2)}, u32[]{:S(2)}) %collective-permute-start.23) | collective-permute-done | bytes 200736 | tf_op jit(solution)/shard_map/ppermute | solution.py:373
  108.8 6.0 %collective-permute-done.22.refs_2_ = f32[768,128]{1,0:T(8,128)S(1)} collective-permute-done((f32[768,128]{1,0:T(8,128)S(1)}, f32[768,128]{1,0:T(8,128)S(1)}, u32[]{:S(2)}, u32[]{:S(2)}) %collective-permute-start.22) | collective-permute-done | bytes 393248 | tf_op jit(solution)/shard_map/ppermute | solution.py:373
  114.8 1.9 %shard_map.80 = (f32[520,128]{1,0:T(8,128)S(1)}, bf16[3072,128]{1,0:T(8,128)(2,1)S(1)}, f32[1536,128]{1,0:T(8,128)S(1)}) custom-call(s32[1]{0:T(128)} %bitcast.1.refs_0_.core_ref, bf16[2048,3072]{1,0:T(8,128)(2,1)S(1)} %get-tuple-element.87.refs_0_.dense_ref.refs_1_, f32[768,128]{1,0:T(8,128)S(1)} %collective-permute-done.22.refs_2_, ...), custom_call_target="tpu_custom_call" | custom-call | flops 1610612736 | bytes 6291456 | tf_op jit(solution)/shard_map/pallas_call | solution.py:229
  118.0 1.8 shard_map.81
  119.9 4.8 %collective-permute-done.27.refs_2_ = f32[768,128]{1,0:T(8,128)S(1)} collective-permute-done((f32[768,128]{1,0:T(8,128)S(1)}, f32[768,128]{1,0:T(8,128)S(1)}, u32[]{:S(2)}, u32[]{:S(2)}) %collective-permute-start.27) | collective-permute-done | bytes 393248 | tf_op jit(solution)/shard_map/ppermute | solution.py:373
  124.7 1.9 %shard_map.82 = (f32[520,128]{1,0:T(8,128)S(1)}, bf16[3072,128]{1,0:T(8,128)(2,1)S(1)}, f32[1536,128]{1,0:T(8,128)S(1)}) custom-call(s32[1]{0:T(128)} %bitcast.1.refs_0_.core_ref, bf16[2048,3072]{1,0:T(8,128)(2,1)S(1)} %get-tuple-element.87.refs_0_.dense_ref.refs_1_, f32[768,128]{1,0:T(8,128)S(1)} %collective-permute-done.27.refs_2_, ...), custom_call_target="tpu_custom_call" | custom-call | flops 1610612736 | bytes 6291456 | tf_op jit(solution)/shard_map/pallas_call | solution.py:229
  126.7 1.5 collective-permute-done.26
  128.3 1.8 shard_map.83
  133.6 5.5 %collective-permute-done.31 = f32[520,128]{1,0:T(8,128)S(1)} collective-permute-done((f32[520,128]{1,0:T(8,128)S(1)}, f32[520,128]{1,0:T(8,128)S(1)}, u32[]{:S(2)}, u32[]{:S(2)}) %collective-permute-start.31) | collective-permute-done | bytes 266272 | tf_op jit(solution)/shard_map/ppermute | solution.py:376
  141.6 1.6 shard_map.86
  144.6 2.3 %collective-permute-done.32 = f32[392,128]{1,0:T(8,128)S(1)} collective-permute-done((f32[392,128]{1,0:T(8,128)S(1)}, f32[392,128]{1,0:T(8,128)S(1)}, u32[]{:S(2)}, u32[]{:S(2)}) %collective-permute-start.32) | collective-permute-done | bytes 200736 | tf_op jit(solution)/shard_map/ppermute | solution.py:373
  147.0 6.5 %collective-permute-start.34 = (f32[392,128]{1,0:T(8,128)S(1)}, f32[392,128]{1,0:T(8,128)S(1)}, u32[]{:S(2)}, u32[]{:S(2)}) collective-permute-start(f32[392,128]{1,0:T(8,128)S(1)} %pad_maximum_fusion.19), channel_id=1, source_target_pairs={{0,16},{1,17},{2,18},{3,19},{4,20},{5,21},{6,22},{7,23},{8,24},{9,... | collective-permute-start | bytes 602120 | tf_op jit(solution)/shard_map/ppermute | solution.py:373
  155.0 6.1 %collective-permute-done.34 = f32[392,128]{1,0:T(8,128)S(1)} collective-permute-done((f32[392,128]{1,0:T(8,128)S(1)}, f32[392,128]{1,0:T(8,128)S(1)}, u32[]{:S(2)}, u32[]{:S(2)}) %collective-permute-start.34) | collective-permute-done | bytes 200736 | tf_op jit(solution)/shard_map/ppermute | solution.py:373
  163.2 5.5 %collective-permute-done.38.refs_1_ = f32[384,128]{1,0:T(8,128)S(1)} collective-permute-done((f32[384,128]{1,0:T(8,128)S(1)}, f32[384,128]{1,0:T(8,128)S(1)}, u32[]{:S(2)}, u32[]{:S(2)}) %collective-permute-start.38) | collective-permute-done | bytes 196640 | tf_op jit(solution)/shard_map/ppermute | solution.py:373
  168.8 3.9 %collective-permute-done.37 = f32[392,128]{1,0:T(8,128)S(1)} collective-permute-done((f32[392,128]{1,0:T(8,128)S(1)}, f32[392,128]{1,0:T(8,128)S(1)}, u32[]{:S(2)}, u32[]{:S(2)}) %collective-permute-start.37) | collective-permute-done | bytes 200736 | tf_op jit(solution)/shard_map/ppermute | solution.py:373
  172.9 5.6 %collective-permute-done.40.refs_10_ = f32[384,128]{1,0:T(8,128)S(1)} collective-permute-done((f32[384,128]{1,0:T(8,128)S(1)}, f32[384,128]{1,0:T(8,128)S(1)}, u32[]{:S(2)}, u32[]{:S(2)}) %collective-permute-start.40) | collective-permute-done | bytes 196640 | tf_op jit(solution)/shard_map/ppermute | solution.py:373
  178.6 1.7 shard_map.88
  180.9 3.4 %collective-permute-done.39.refs_0_ = f32[768,128]{1,0:T(8,128)S(1)} collective-permute-done((f32[768,128]{1,0:T(8,128)S(1)}, f32[768,128]{1,0:T(8,128)S(1)}, u32[]{:S(2)}, u32[]{:S(2)}) %collective-permute-start.39) | collective-permute-done | bytes 393248 | tf_op jit(solution)/shard_map/ppermute | solution.py:373
  184.2 4.2 %collective-permute-done.41.refs_9_ = f32[768,128]{1,0:T(8,128)S(1)} collective-permute-done((f32[768,128]{1,0:T(8,128)S(1)}, f32[768,128]{1,0:T(8,128)S(1)}, u32[]{:S(2)}, u32[]{:S(2)}) %collective-permute-start.41) | collective-permute-done | bytes 393248 | tf_op jit(solution)/shard_map/ppermute | solution.py:373
  188.4 1.7 shard_map.89
  (141 shorter events, 32.9 us)
Async XLA Ops:
  6.8 8.5 %collective-permute-start = (f32[776,128]{1,0:T(8,128)S(1)}, f32[776,128]{1,0:T(8,128)S(1)}, u32[]{:S(2)}, u32[]{:S(2)}) collective-permute-start(f32[776,128]{1,0:T(8,128)S(1)} %get-tuple-element.93), channel_id=1, source_target_pairs={{0,4},{1,9},{2,6},{3,11},{4,0},{5,13},{6,2},{7,15},{8,12},{9,1},{1... | collective-permute-start | bytes 1191944 | tf_op jit(solution)/shard_map/ppermute | solution.py:373
  15.4 8.0 %collective-permute-start.1 = (f32[392,128]{1,0:T(8,128)S(1)}, f32[392,128]{1,0:T(8,128)S(1)}, u32[]{:S(2)}, u32[]{:S(2)}) collective-permute-start(f32[392,128]{1,0:T(8,128)S(1)} %pad_maximum_fusion.10), channel_id=1, source_target_pairs={{0,8},{1,5},{2,10},{3,7},{4,12},{5,1},{6,14},{7,3},{8,0},{9,13},{1... | collective-permute-start | bytes 602120 | tf_op jit(solution)/shard_map/ppermute | solution.py:373
  17.6 10.3 %collective-permute-start.3 = (f32[776,128]{1,0:T(8,128)S(1)}, f32[776,128]{1,0:T(8,128)S(1)}, u32[]{:S(2)}, u32[]{:S(2)}) collective-permute-start(f32[776,128]{1,0:T(8,128)S(1)} %get-tuple-element.95), channel_id=1, source_target_pairs={{0,4},{1,9},{2,6},{3,11},{4,0},{5,13},{6,2},{7,15},{8,12},{9,1},{1... | collective-permute-start | bytes 1191944 | tf_op jit(solution)/shard_map/ppermute | solution.py:373
  23.5 10.4 %collective-permute-start.2 = (f32[392,128]{1,0:T(8,128)S(1)}, f32[392,128]{1,0:T(8,128)S(1)}, u32[]{:S(2)}, u32[]{:S(2)}) collective-permute-start(f32[392,128]{1,0:T(8,128)S(1)} %pad_maximum_fusion.11), channel_id=1, source_target_pairs={{0,16},{1,17},{2,18},{3,19},{4,20},{5,21},{6,22},{7,23},{8,24},{9,... | collective-permute-start | bytes 602120 | tf_op jit(solution)/shard_map/ppermute | solution.py:373
  28.0 9.0 %collective-permute-start.5 = (f32[392,128]{1,0:T(8,128)S(1)}, f32[392,128]{1,0:T(8,128)S(1)}, u32[]{:S(2)}, u32[]{:S(2)}) collective-permute-start(f32[392,128]{1,0:T(8,128)S(1)} %pad_maximum_fusion.12), channel_id=1, source_target_pairs={{0,8},{1,5},{2,10},{3,7},{4,12},{5,1},{6,14},{7,3},{8,0},{9,13},{1... | collective-permute-start | bytes 602120 | tf_op jit(solution)/shard_map/ppermute | solution.py:373
  33.9 6.7 %collective-permute-start.4 = (f32[384,128]{1,0:T(8,128)S(1)}, f32[384,128]{1,0:T(8,128)S(1)}, u32[]{:S(2)}, u32[]{:S(2)}) collective-permute-start(f32[384,128]{1,0:T(8,128)S(1)} %slice_add_fusion.25.refs_4_), channel_id=1, source_target_pairs={{0,8},{1,9},{2,10},{3,11},{4,12},{5,13},{6,14},{7,15},{8,0},{9,1},... | collective-permute-start | bytes 589832 | tf_op jit(solution)/shard_map/ppermute | solution.py:373
  37.1 8.8 %collective-permute-start.7 = (f32[392,128]{1,0:T(8,128)S(1)}, f32[392,128]{1,0:T(8,128)S(1)}, u32[]{:S(2)}, u32[]{:S(2)}) collective-permute-start(f32[392,128]{1,0:T(8,128)S(1)} %pad_maximum_fusion.13), channel_id=1, source_target_pairs={{0,16},{1,17},{2,18},{3,19},{4,20},{5,21},{6,22},{7,23},{8,24},{9,... | collective-permute-start | bytes 602120 | tf_op jit(solution)/shard_map/ppermute | solution.py:373
  40.6 8.0 %collective-permute-start.6 = (f32[768,128]{1,0:T(8,128)S(1)}, f32[768,128]{1,0:T(8,128)S(1)}, u32[]{:S(2)}, u32[]{:S(2)}) collective-permute-start(f32[768,128]{1,0:T(8,128)S(1)} %pad_maximum_fusion), channel_id=1, source_target_pairs={{0,4},{1,5},{2,6},{3,7},{4,0},{5,1},{6,2},{7,3},{8,12},{9,13},{10,... | collective-permute-start | bytes 1179656 | tf_op jit(solution)/shard_map/ppermute | solution.py:373
  45.9 5.7 %collective-permute-start.8 = (f32[384,128]{1,0:T(8,128)S(1)}, f32[384,128]{1,0:T(8,128)S(1)}, u32[]{:S(2)}, u32[]{:S(2)}) collective-permute-start(f32[384,128]{1,0:T(8,128)S(1)} %slice_add_fusion.24.refs_4_), channel_id=1, source_target_pairs={{0,8},{1,5},{2,10},{3,7},{4,12},{5,1},{6,14},{7,3},{8,0},{9,13},{1... | collective-permute-start | bytes 589832 | tf_op jit(solution)/shard_map/ppermute | solution.py:373
  50.5 6.3 %collective-permute-start.9 = (f32[520,128]{1,0:T(8,128)S(1)}, f32[520,128]{1,0:T(8,128)S(1)}, u32[]{:S(2)}, u32[]{:S(2)}) collective-permute-start(f32[520,128]{1,0:T(8,128)S(1)} %get-tuple-element.107), channel_id=1, source_target_pairs={{0,1},{1,0},{2,3},{3,2},{4,5},{5,4},{6,7},{7,6},{8,9},{9,8},{10,11... | collective-permute-start | bytes 798728 | tf_op jit(solution)/shard_map/ppermute | solution.py:376
  51.7 9.2 %collective-permute-start.11 = (f32[768,128]{1,0:T(8,128)S(1)}, f32[768,128]{1,0:T(8,128)S(1)}, u32[]{:S(2)}, u32[]{:S(2)}) collective-permute-start(f32[768,128]{1,0:T(8,128)S(1)} %pad_maximum_fusion.1), channel_id=1, source_target_pairs={{0,4},{1,9},{2,6},{3,11},{4,0},{5,13},{6,2},{7,15},{8,12},{9,1},{1... | collective-permute-start | bytes 1179656 | tf_op jit(solution)/shard_map/ppermute | solution.py:373
  57.0 6.5 %collective-permute-start.10 = (f32[520,128]{1,0:T(8,128)S(1)}, f32[520,128]{1,0:T(8,128)S(1)}, u32[]{:S(2)}, u32[]{:S(2)}) collective-permute-start(f32[520,128]{1,0:T(8,128)S(1)} %pad_maximum_fusion.6), channel_id=1, source_target_pairs={{0,2},{1,3},{2,0},{3,1},{4,6},{5,7},{6,4},{7,5},{8,10},{9,11},{10,... | collective-permute-start | bytes 798728 | tf_op jit(solution)/shard_map/ppermute | solution.py:376
  62.8 2.6 %collective-permute-start.13 = (f32[520,128]{1,0:T(8,128)S(1)}, f32[520,128]{1,0:T(8,128)S(1)}, u32[]{:S(2)}, u32[]{:S(2)}) collective-permute-start(f32[520,128]{1,0:T(8,128)S(1)} %get-tuple-element.112), channel_id=1, source_target_pairs={{0,1},{1,0},{2,3},{3,2},{4,5},{5,4},{6,7},{7,6},{8,9},{9,8},{10,11... | collective-permute-start | bytes 798728 | tf_op jit(solution)/shard_map/ppermute | solution.py:376
  63.5 3.0 %collective-permute-start.12 = (f32[512,128]{1,0:T(8,128)S(1)}, f32[512,128]{1,0:T(8,128)S(1)}, u32[]{:S(2)}, u32[]{:S(2)}) collective-permute-start(f32[512,128]{1,0:T(8,128)S(1)} %slice_add_fusion.12.refs_2_), channel_id=1, source_target_pairs={{0,1},{1,0},{2,3},{3,2},{4,5},{5,4},{6,7},{7,6},{8,9},{9,8},{10,11... | collective-permute-start | bytes 786440 | tf_op jit(solution)/shard_map/ppermute | solution.py:376
  65.4 8.9 %collective-permute-start.14 = (f32[520,128]{1,0:T(8,128)S(1)}, f32[520,128]{1,0:T(8,128)S(1)}, u32[]{:S(2)}, u32[]{:S(2)}) collective-permute-start(f32[520,128]{1,0:T(8,128)S(1)} %pad_maximum_fusion.7), channel_id=1, source_target_pairs={{0,2},{1,3},{2,0},{3,1},{4,6},{5,7},{6,4},{7,5},{8,10},{9,11},{10,... | collective-permute-start | bytes 798728 | tf_op jit(solution)/shard_map/ppermute | solution.py:376
  67.9 8.0 %collective-permute-start.15 = (f32[776,128]{1,0:T(8,128)S(1)}, f32[776,128]{1,0:T(8,128)S(1)}, u32[]{:S(2)}, u32[]{:S(2)}) collective-permute-start(f32[776,128]{1,0:T(8,128)S(1)} %get-tuple-element.119), channel_id=1, source_target_pairs={{0,4},{1,9},{2,6},{3,11},{4,0},{5,13},{6,2},{7,15},{8,12},{9,1},{1... | collective-permute-start | bytes 1191944 | tf_op jit(solution)/shard_map/ppermute | solution.py:373
  74.3 2.8 %collective-permute-start.17 = (f32[512,128]{1,0:T(8,128)S(1)}, f32[512,128]{1,0:T(8,128)S(1)}, u32[]{:S(2)}, u32[]{:S(2)}) collective-permute-start(f32[512,128]{1,0:T(8,128)S(1)} %slice_add_fusion.10.refs_2_), channel_id=1, source_target_pairs={{0,1},{1,0},{2,3},{3,2},{4,5},{5,4},{6,7},{7,6},{8,9},{9,8},{10,11... | collective-permute-start | bytes 786440 | tf_op jit(solution)/shard_map/ppermute | solution.py:376
  76.0 5.8 %collective-permute-start.16 = (f32[392,128]{1,0:T(8,128)S(1)}, f32[392,128]{1,0:T(8,128)S(1)}, u32[]{:S(2)}, u32[]{:S(2)}) collective-permute-start(f32[392,128]{1,0:T(8,128)S(1)} %pad_maximum_fusion.14), channel_id=1, source_target_pairs={{0,8},{1,5},{2,10},{3,7},{4,12},{5,1},{6,14},{7,3},{8,0},{9,13},{1... | collective-permute-start | bytes 602120 | tf_op jit(solution)/shard_map/ppermute | solution.py:373
  78.6 12.0 %collective-permute-start.19 = (f32[776,128]{1,0:T(8,128)S(1)}, f32[776,128]{1,0:T(8,128)S(1)}, u32[]{:S(2)}, u32[]{:S(2)}) collective-permute-start(f32[776,128]{1,0:T(8,128)S(1)} %get-tuple-element.124), channel_id=1, source_target_pairs={{0,4},{1,9},{2,6},{3,11},{4,0},{5,13},{6,2},{7,15},{8,12},{9,1},{1... | collective-permute-start | bytes 1191944 | tf_op jit(solution)/shard_map/ppermute | solution.py:373
  81.9 15.0 %collective-permute-start.18 = (f32[392,128]{1,0:T(8,128)S(1)}, f32[392,128]{1,0:T(8,128)S(1)}, u32[]{:S(2)}, u32[]{:S(2)}) collective-permute-start(f32[392,128]{1,0:T(8,128)S(1)} %pad_maximum_fusion.15), channel_id=1, source_target_pairs={{0,16},{1,17},{2,18},{3,19},{4,20},{5,21},{6,22},{7,23},{8,24},{9,... | collective-permute-start | bytes 602120 | tf_op jit(solution)/shard_map/ppermute | solution.py:373
  90.7 7.1 %collective-permute-start.21 = (f32[392,128]{1,0:T(8,128)S(1)}, f32[392,128]{1,0:T(8,128)S(1)}, u32[]{:S(2)}, u32[]{:S(2)}) collective-permute-start(f32[392,128]{1,0:T(8,128)S(1)} %pad_maximum_fusion.16), channel_id=1, source_target_pairs={{0,8},{1,5},{2,10},{3,7},{4,12},{5,1},{6,14},{7,3},{8,0},{9,13},{1... | collective-permute-start | bytes 602120 | tf_op jit(solution)/shard_map/ppermute | solution.py:373
  96.9 8.0 %collective-permute-start.20 = (f32[384,128]{1,0:T(8,128)S(1)}, f32[384,128]{1,0:T(8,128)S(1)}, u32[]{:S(2)}, u32[]{:S(2)}) collective-permute-start(f32[384,128]{1,0:T(8,128)S(1)} %slice_add_fusion.23.refs_4_), channel_id=1, source_target_pairs={{0,8},{1,9},{2,10},{3,11},{4,12},{5,13},{6,14},{7,15},{8,0},{9,1},... | collective-permute-start | bytes 589832 | tf_op jit(solution)/shard_map/ppermute | solution.py:373
  97.9 10.8 %collective-permute-start.23 = (f32[392,128]{1,0:T(8,128)S(1)}, f32[392,128]{1,0:T(8,128)S(1)}, u32[]{:S(2)}, u32[]{:S(2)}) collective-permute-start(f32[392,128]{1,0:T(8,128)S(1)} %pad_maximum_fusion.17), channel_id=1, source_target_pairs={{0,16},{1,17},{2,18},{3,19},{4,20},{5,21},{6,22},{7,23},{8,24},{9,... | collective-permute-start | bytes 602120 | tf_op jit(solution)/shard_map/ppermute | solution.py:373
  104.9 9.9 %collective-permute-start.22 = (f32[768,128]{1,0:T(8,128)S(1)}, f32[768,128]{1,0:T(8,128)S(1)}, u32[]{:S(2)}, u32[]{:S(2)}) collective-permute-start(f32[768,128]{1,0:T(8,128)S(1)} %pad_maximum_fusion.2), channel_id=1, source_target_pairs={{0,4},{1,5},{2,6},{3,7},{4,0},{5,1},{6,2},{7,3},{8,12},{9,13},{10,... | collective-permute-start | bytes 1179656 | tf_op jit(solution)/shard_map/ppermute | solution.py:373
  108.7 8.1 %collective-permute-start.25 = (f32[384,128]{1,0:T(8,128)S(1)}, f32[384,128]{1,0:T(8,128)S(1)}, u32[]{:S(2)}, u32[]{:S(2)}) collective-permute-start(f32[384,128]{1,0:T(8,128)S(1)} %slice_add_fusion.22.refs_4_), channel_id=1, source_target_pairs={{0,8},{1,5},{2,10},{3,7},{4,12},{5,1},{6,14},{7,3},{8,0},{9,13},{1... | collective-permute-start | bytes 589832 | tf_op jit(solution)/shard_map/ppermute | solution.py:373
  116.8 3.0 %collective-permute-start.24 = (f32[520,128]{1,0:T(8,128)S(1)}, f32[520,128]{1,0:T(8,128)S(1)}, u32[]{:S(2)}, u32[]{:S(2)}) collective-permute-start(f32[520,128]{1,0:T(8,128)S(1)} %get-tuple-element.135), channel_id=1, source_target_pairs={{0,1},{1,0},{2,3},{3,2},{4,5},{5,4},{6,7},{7,6},{8,9},{9,8},{10,11... | collective-permute-start | bytes 798728 | tf_op jit(solution)/shard_map/ppermute | solution.py:376
  116.9 7.8 %collective-permute-start.27 = (f32[768,128]{1,0:T(8,128)S(1)}, f32[768,128]{1,0:T(8,128)S(1)}, u32[]{:S(2)}, u32[]{:S(2)}) collective-permute-start(f32[768,128]{1,0:T(8,128)S(1)} %pad_maximum_fusion.3), channel_id=1, source_target_pairs={{0,4},{1,9},{2,6},{3,11},{4,0},{5,13},{6,2},{7,15},{8,12},{9,1},{1... | collective-permute-start | bytes 1179656 | tf_op jit(solution)/shard_map/ppermute | solution.py:373
  119.9 8.3 %collective-permute-start.26 = (f32[520,128]{1,0:T(8,128)S(1)}, f32[520,128]{1,0:T(8,128)S(1)}, u32[]{:S(2)}, u32[]{:S(2)}) collective-permute-start(f32[520,128]{1,0:T(8,128)S(1)} %pad_maximum_fusion.8), channel_id=1, source_target_pairs={{0,2},{1,3},{2,0},{3,1},{4,6},{5,7},{6,4},{7,5},{8,10},{9,11},{10,... | collective-permute-start | bytes 798728 | tf_op jit(solution)/shard_map/ppermute | solution.py:376
  126.7 3.4 %collective-permute-start.29 = (f32[520,128]{1,0:T(8,128)S(1)}, f32[520,128]{1,0:T(8,128)S(1)}, u32[]{:S(2)}, u32[]{:S(2)}) collective-permute-start(f32[520,128]{1,0:T(8,128)S(1)} %get-tuple-element.142), channel_id=1, source_target_pairs={{0,1},{1,0},{2,3},{3,2},{4,5},{5,4},{6,7},{7,6},{8,9},{9,8},{10,11... | collective-permute-start | bytes 798728 | tf_op jit(solution)/shard_map/ppermute | solution.py:376
  128.2 2.9 %collective-permute-start.28 = (f32[512,128]{1,0:T(8,128)S(1)}, f32[512,128]{1,0:T(8,128)S(1)}, u32[]{:S(2)}, u32[]{:S(2)}) collective-permute-start(f32[512,128]{1,0:T(8,128)S(1)} %slice_add_fusion.8.refs_2_), channel_id=1, source_target_pairs={{0,1},{1,0},{2,3},{3,2},{4,5},{5,4},{6,7},{7,6},{8,9},{9,8},{10,11... | collective-permute-start | bytes 786440 | tf_op jit(solution)/shard_map/ppermute | solution.py:376
  130.2 8.9 %collective-permute-start.31 = (f32[520,128]{1,0:T(8,128)S(1)}, f32[520,128]{1,0:T(8,128)S(1)}, u32[]{:S(2)}, u32[]{:S(2)}) collective-permute-start(f32[520,128]{1,0:T(8,128)S(1)} %pad_maximum_fusion.9), channel_id=1, source_target_pairs={{0,2},{1,3},{2,0},{3,1},{4,6},{5,7},{6,4},{7,5},{8,10},{9,11},{10,... | collective-permute-start | bytes 798728 | tf_op jit(solution)/shard_map/ppermute | solution.py:376
  132.5 7.9 %collective-permute-start.30 = (f32[776,128]{1,0:T(8,128)S(1)}, f32[776,128]{1,0:T(8,128)S(1)}, u32[]{:S(2)}, u32[]{:S(2)}) collective-permute-start(f32[776,128]{1,0:T(8,128)S(1)} %get-tuple-element.149), channel_id=1, source_target_pairs={{0,4},{1,9},{2,6},{3,11},{4,0},{5,13},{6,2},{7,15},{8,12},{9,1},{1... | collective-permute-start | bytes 1191944 | tf_op jit(solution)/shard_map/ppermute | solution.py:373
  139.1 2.5 %collective-permute-start.33 = (f32[512,128]{1,0:T(8,128)S(1)}, f32[512,128]{1,0:T(8,128)S(1)}, u32[]{:S(2)}, u32[]{:S(2)}) collective-permute-start(f32[512,128]{1,0:T(8,128)S(1)} %slice_add_fusion.6.refs_2_), channel_id=1, source_target_pairs={{0,1},{1,0},{2,3},{3,2},{4,5},{5,4},{6,7},{7,6},{8,9},{9,8},{10,11... | collective-permute-start | bytes 786440 | tf_op jit(solution)/shard_map/ppermute | solution.py:376
  140.6 6.3 %collective-permute-start.32 = (f32[392,128]{1,0:T(8,128)S(1)}, f32[392,128]{1,0:T(8,128)S(1)}, u32[]{:S(2)}, u32[]{:S(2)}) collective-permute-start(f32[392,128]{1,0:T(8,128)S(1)} %pad_maximum_fusion.18), channel_id=1, source_target_pairs={{0,8},{1,5},{2,10},{3,7},{4,12},{5,1},{6,14},{7,3},{8,0},{9,13},{1... | collective-permute-start | bytes 602120 | tf_op jit(solution)/shard_map/ppermute | solution.py:373
  143.2 11.5 %collective-permute-start.35 = (f32[776,128]{1,0:T(8,128)S(1)}, f32[776,128]{1,0:T(8,128)S(1)}, u32[]{:S(2)}, u32[]{:S(2)}) collective-permute-start(f32[776,128]{1,0:T(8,128)S(1)} %get-tuple-element.156), channel_id=1, source_target_pairs={{0,4},{1,9},{2,6},{3,11},{4,0},{5,13},{6,2},{7,15},{8,12},{9,1},{1... | collective-permute-start | bytes 1191944 | tf_op jit(solution)/shard_map/ppermute | solution.py:373
  147.0 14.1 %collective-permute-start.34 = (f32[392,128]{1,0:T(8,128)S(1)}, f32[392,128]{1,0:T(8,128)S(1)}, u32[]{:S(2)}, u32[]{:S(2)}) collective-permute-start(f32[392,128]{1,0:T(8,128)S(1)} %pad_maximum_fusion.19), channel_id=1, source_target_pairs={{0,16},{1,17},{2,18},{3,19},{4,20},{5,21},{6,22},{7,23},{8,24},{9,... | collective-permute-start | bytes 602120 | tf_op jit(solution)/shard_map/ppermute | solution.py:373
  154.9 7.6 %collective-permute-start.36 = (f32[392,128]{1,0:T(8,128)S(1)}, f32[392,128]{1,0:T(8,128)S(1)}, u32[]{:S(2)}, u32[]{:S(2)}) collective-permute-start(f32[392,128]{1,0:T(8,128)S(1)} %pad_maximum_fusion.20), channel_id=1, source_target_pairs={{0,8},{1,5},{2,10},{3,7},{4,12},{5,1},{6,14},{7,3},{8,0},{9,13},{1... | collective-permute-start | bytes 602120 | tf_op jit(solution)/shard_map/ppermute | solution.py:373
  161.1 7.7 %collective-permute-start.38 = (f32[384,128]{1,0:T(8,128)S(1)}, f32[384,128]{1,0:T(8,128)S(1)}, u32[]{:S(2)}, u32[]{:S(2)}) collective-permute-start(f32[384,128]{1,0:T(8,128)S(1)} %slice_add_fusion.21.refs_2_), channel_id=1, source_target_pairs={{0,8},{1,9},{2,10},{3,11},{4,12},{5,13},{6,14},{7,15},{8,0},{9,1},... | collective-permute-start | bytes 589832 | tf_op jit(solution)/shard_map/ppermute | solution.py:373
  162.5 10.2 %collective-permute-start.37 = (f32[392,128]{1,0:T(8,128)S(1)}, f32[392,128]{1,0:T(8,128)S(1)}, u32[]{:S(2)}, u32[]{:S(2)}) collective-permute-start(f32[392,128]{1,0:T(8,128)S(1)} %pad_maximum_fusion.21), channel_id=1, source_target_pairs={{0,16},{1,17},{2,18},{3,19},{4,20},{5,21},{6,22},{7,23},{8,24},{9,... | collective-permute-start | bytes 602120 | tf_op jit(solution)/shard_map/ppermute | solution.py:373
  172.7 5.8 %collective-permute-start.40 = (f32[384,128]{1,0:T(8,128)S(1)}, f32[384,128]{1,0:T(8,128)S(1)}, u32[]{:S(2)}, u32[]{:S(2)}) collective-permute-start(f32[384,128]{1,0:T(8,128)S(1)} %slice_add_fusion.20.refs_11_), channel_id=1, source_target_pairs={{0,8},{1,5},{2,10},{3,7},{4,12},{5,1},{6,14},{7,3},{8,0},{9,13},{1... | collective-permute-start | bytes 589832 | tf_op jit(solution)/shard_map/ppermute | solution.py:373
  172.8 11.4 %collective-permute-start.39 = (f32[768,128]{1,0:T(8,128)S(1)}, f32[768,128]{1,0:T(8,128)S(1)}, u32[]{:S(2)}, u32[]{:S(2)}) collective-permute-start(f32[768,128]{1,0:T(8,128)S(1)} %pad_maximum_fusion.4), channel_id=1, source_target_pairs={{0,4},{1,5},{2,6},{3,7},{4,0},{5,1},{6,2},{7,3},{8,12},{9,13},{10,... | collective-permute-start | bytes 1179656 | tf_op jit(solution)/shard_map/ppermute | solution.py:373
  178.6 9.9 %collective-permute-start.41 = (f32[768,128]{1,0:T(8,128)S(1)}, f32[768,128]{1,0:T(8,128)S(1)}, u32[]{:S(2)}, u32[]{:S(2)}) collective-permute-start(f32[768,128]{1,0:T(8,128)S(1)} %pad_maximum_fusion.5), channel_id=1, source_target_pairs={{0,4},{1,9},{2,6},{3,11},{4,0},{5,13},{6,2},{7,15},{8,12},{9,1},{1... | collective-permute-start | bytes 1179656 | tf_op jit(solution)/shard_map/ppermute | solution.py:373

commit v15 on v13

--- a/solution.py
+++ b/solution.py
@@ -40,7 +40,7 @@
     flip = flip_ref[0]
     row_blocks = tiles_in.shape[0]
     small = [
-        pltpu.make_async_copy(source, target, arrived.at[row_blocks + i])
+        pltpu.make_async_copy(source, target, arrived.at[2 * row_blocks + i])
         for i, (source, target) in enumerate(
             [(pattern_in, pattern_ref), (counts_in, counts_ref), (delays_in, delays_ref)]
         )
@@ -48,15 +48,25 @@
     for copy in small:
         copy.start()
 
-    def fetch(position):
+    half = tiles_in.shape[1] // 2
+
+    def fetch(position, upper):
+        slots = pl.ds(upper * half, half)
         return pltpu.make_async_copy(
-            tiles_in.at[position ^ flip], tiles_ref.at[position], arrived.at[position]
+            tiles_in.at[position ^ flip, slots],
+            tiles_ref.at[position, slots],
+            arrived.at[upper * row_blocks + position],
         )
 
     for position in range(row_blocks):
-        fetch(position).start()
+        fetch(position, 0).start()
     for copy in small:
         copy.wait()
+    for position in range(row_blocks):
+
+        @pl.when(counts_ref[position ^ flip] > half)
+        def _():
+            fetch(position, 1).start()
 
     low = low_lanes((TILE, TILE))
     for pair in range(row_blocks // 2):
@@ -69,15 +79,24 @@
     @pl.loop(0, row_blocks)
     def _(position):
         rows = pl.ds(pl.multiple_of(position * TILE, TILE), TILE)
+        block = position ^ flip
+        count = counts_ref[block]
+
+        def place(tile):
+            column = jnp.where(tile < count, place_ref[pattern_ref[block, tile]], CB_DEV)
+            lanes = pl.ds(pl.multiple_of(column * TILE, TILE), TILE)
+            dense_ref[rows, lanes] = tiles_ref[position, tile]
+
         dense_ref[rows, :] = jnp.zeros((TILE, dense_ref.shape[1]), dense_ref.dtype)
-        fetch(position).wait()
-        block = position ^ flip
-
-        @pl.loop(0, counts_ref[block])
-        def _(tile):
-            place = place_ref[pattern_ref[block, tile]]
-            lanes = pl.ds(pl.multiple_of(place * TILE, TILE), TILE)
-            dense_ref[rows, lanes] = tiles_ref[position, tile]
+        fetch(position, 0).wait()
+        for tile in range(half):
+            place(tile)
+
+        @pl.when(count > half)
+        def _():
+            fetch(position, 1).wait()
+            for tile in range(half, 2 * half):
+                place(tile)
 
 
 def fill_dense(kernel, pattern, counts, places, flip, delays):
@@ -88,13 +107,13 @@
         fill_kernel,
         in_specs=[SCALARS] * 2 + [pl.BlockSpec(memory_space=pltpu.HBM)] * 4,
         out_specs=[WHOLE] * 3,
-        out_shape=[jax.ShapeDtypeStruct((rows, CB_DEV * TILE), kernel.dtype), left, left],
+        out_shape=[jax.ShapeDtypeStruct((rows, (CB_DEV + 1) * TILE), kernel.dtype), left, left],
         scratch_shapes=[
             pltpu.SMEM(pattern.shape, jnp.int32),
             pltpu.SMEM((row_blocks,), jnp.int32),
             pltpu.VMEM(delays.shape, delays.dtype),
             pltpu.VMEM(kernel.shape, kernel.dtype),
-            pltpu.SemaphoreType.DMA((row_blocks + 3,)),
+            pltpu.SemaphoreType.DMA((2 * row_blocks + 3,)),
         ],
         compiler_params=pltpu.CompilerParams(vmem_limit_bytes=16 * 1024 * 1024),
         cost_estimate=pl.CostEstimate(
@@ -176,29 +195,25 @@
     back_pairs(dense_ref, turned_ref, keep_ref, keep_ref.shape[0] // TILE)
 
 
-def fore_pairs(dense_ref, wide_ref, out_ref, start):
+def fore_pairs(dense_ref, cells, wide_ref, add_ref, out_ref, start):
     low = low_lanes((TILE, TILE))
     step = 2
-    for pair in range(0, out_ref.shape[0] // TILE, step):
+    pairs = out_ref.shape[0] // TILE
+    for pair in range(0, pairs, step):
         product = jnp.dot(
-            dense_ref[(start + pair) * PAIR : (start + pair + step) * PAIR, :],
+            dense_ref[(start + pair) * PAIR : (start + pair + step) * PAIR, cells],
             wide_ref[...],
             preferred_element_type=jnp.float32,
         )
         for i in range(step):
             even, odd = product[rows_of(2 * i), :], product[rows_of(2 * i + 1), :]
-            out_ref[rows_of(pair + i), :] = jnp.where(low, even, odd)
-
-
-def fore_send_kernel(first, *refs):
-    if first:
-        (dense_ref, outer_ref, inner_ref, mine_ref, scale_ref, send_ref, wide_ref, raw_ref) = refs
-        scales = (scale_ref, None, None)
-    else:
-        (dense_ref, outer_ref, inner_ref, mine_ref, scale_ref, past_ref, past_scale_ref,
-         send_ref, wide_ref, raw_ref) = refs
-        scales = (scale_ref, past_ref, past_scale_ref)
-    parts = [(outer_ref, 2), (inner_ref, 1), (mine_ref, 1)]
+            value = jnp.where(low, even, odd)
+            if add_ref is not None:
+                value = value + add_ref[rows_of(start + pair + i), :]
+            out_ref[rows_of(pair + i), :] = value
+
+
+def fore_vector(parts, wide_ref, raw_ref, scales):
     low = low_lanes((TILE, TILE))
     sums = []
     for pair, value, squares in next_vector(parts, raw_ref, *scales):
@@ -207,20 +222,39 @@
         wide_ref[rows_of(2 * pair + 1), :] = jnp.where(low, other, value).astype(wide_ref.dtype)
         if squares is not None:
             sums.append(squares)
-    send_ref[-NORM_ROWS:, :] = jnp.broadcast_to(squares_row(sums), (NORM_ROWS, TILE))
-    fore_pairs(dense_ref, wide_ref, send_ref, 0)
-
-
-def fore_keep_kernel(dense_ref, wide_ref, keep_ref):
-    fore_pairs(dense_ref, wide_ref, keep_ref, keep_ref.shape[0] // TILE)
-
-
-def product_call(body, dense, operands, shapes):
+    return sums[0] + sums[1]
+
+
+def fore_own_kernel(first, dense_ref, inner_ref, mine_ref, scale_ref, *refs):
+    past_ref, past_scale_ref = (None, None) if first else refs[:2]
+    part_ref, sum_ref, raw_ref, wide_ref = refs[-4:]
+    parts = [(inner_ref, 1), (mine_ref, 1)]
+    sum_ref[...] = fore_vector(parts, wide_ref, raw_ref, (scale_ref, past_ref, past_scale_ref))
+    depth = wide_ref.shape[0]
+    fore_pairs(dense_ref, slice(depth, 2 * depth), wide_ref, None, part_ref, 0)
+
+
+def fore_send_kernel(first, dense_ref, outer_ref, part_ref, sum_ref, scale_ref, *refs):
+    past_ref, past_scale_ref = (None, None) if first else refs[:2]
+    send_ref, wide_ref, raw_ref = refs[-3:]
+    squares = fore_vector([(outer_ref, 2)], wide_ref, raw_ref, (scale_ref, past_ref, past_scale_ref))
+    row = squares_row([squares, sum_ref[...]])
+    send_ref[-NORM_ROWS:, :] = jnp.broadcast_to(row, (NORM_ROWS, TILE))
+    fore_pairs(dense_ref, slice(0, wide_ref.shape[0]), wide_ref, part_ref, send_ref, 0)
+
+
+def fore_keep_kernel(dense_ref, wide_ref, part_ref, keep_ref):
+    start = keep_ref.shape[0] // TILE
+    fore_pairs(dense_ref, slice(0, wide_ref.shape[0]), wide_ref, part_ref, keep_ref, start)
+
+
+def product_call(body, dense, operands, shapes, scratch=()):
     return pl.pallas_call(
         body,
         in_specs=[WHOLE] * (1 + len(operands)),
         out_specs=[WHOLE] * len(shapes),
         out_shape=shapes,
+        scratch_shapes=scratch,
         compiler_params=pltpu.CompilerParams(vmem_limit_bytes=12 * 1024 * 1024),
         cost_estimate=pl.CostEstimate(
             flops=2 * TILE * dense.size, bytes_accessed=dense.size, transcendentals=0
@@ -233,7 +267,7 @@
 
 
 def back_product(dense, operands, first):
-    rows, cells = dense.shape
+    rows, cells = dense.shape[0], CB_DEV * TILE
     shapes = [float_rows(cells // 4 + NORM_ROWS), jax.ShapeDtypeStruct((TILE // 2, rows), dense.dtype)]
     shapes += [] if first else [float_rows(rows // 2)]
     send, flat, *raw = product_call(
@@ -247,20 +281,30 @@
     return send, (keep, flat), *raw
 
 
+def fore_own_product(dense, operands, first):
+    rows, cells = dense.shape[0], CB_DEV * TILE
+    return product_call(
+        functools.partial(fore_own_kernel, first),
+        dense,
+        operands,
+        [float_rows(rows // 2), float_rows(NORM_ROWS), float_rows(cells // 4)],
+        [pltpu.VMEM((cells // 2, TILE), dense.dtype)],
+    )
+
+
 def fore_product(dense, operands, first):
-    rows, cells = dense.shape
+    rows, cells = dense.shape[0], CB_DEV * TILE
     shapes = [
         float_rows(rows // 4 + NORM_ROWS),
-        jax.ShapeDtypeStruct((cells, TILE), dense.dtype),
-        float_rows(cells // 2),
+        jax.ShapeDtypeStruct((cells // 2, TILE), dense.dtype),
+        float_rows(cells // 4),
     ]
     send, wide, raw = product_call(
         functools.partial(fore_send_kernel, first), dense, operands, shapes
     )
 
-
     def keep(wide):
-        return product_call(fore_keep_kernel, dense, [wide], [float_rows(rows // 4)])[0]
+        return product_call(fore_keep_kernel, dense, [wide, operands[1]], [float_rows(rows // 4)])[0]
 
     return send, (keep, wide), raw
 
@@ -298,7 +342,8 @@
     ins, (model_ref, misfit_ref) = refs[:-2], refs[-2:]
     chains = [ins[: len(ins) // 2], ins[len(ins) // 2 :]]
     low = low_lanes((TILE, TILE))
-    rotations = [rotation(refs_[count:]) for refs_ in chains]
+    rotations = [rotation(refs_[2 * count :]) for refs_ in chains]
+    half = model_ref.shape[0] // PAIR // 2
     misfits = [jnp.broadcast_to(r[3], misfit_ref.shape) for r in rotations]
     misfit_ref[...] = jnp.where(low_lanes(misfit_ref.shape), misfits[0], misfits[1])
     for pair in range(model_ref.shape[0] // PAIR):
@@ -306,7 +351,8 @@
         for refs_, (alphas, _, steps, _, _) in zip(chains, rotations):
             search = total = None
             for j in range(count):
-                right = refs_[j][rows_of(pair), :] / alphas[j]
+                right_ref = refs_[2 * j + pair // half]
+                right = right_ref[rows_of(pair % half), :] / alphas[j]
                 search = right if j == 0 else right - steps[j - 1][1] * search
                 total = steps[j][0] * search if j == 0 else total + steps[j][0] * search
             values.append(total)
@@ -319,14 +365,19 @@
     low = low_lanes((TILE, TILE))
     vectors = []
     factors = []
-    for outer_ref, inner_ref, mine_ref, past_ref, *norms in chains:
-        alphas, betas, _, _, factor = rotation(norms)
-        parts = [(outer_ref, 2), (inner_ref, 1), (mine_ref, 1)]
-        vectors.append(next_vector(parts, None, norms[-1], past_ref, norms[-2]))
-        factors.append(factor)
-    for ours, theirs in zip(*vectors):
-        values = [factors[0] * ours[1], factors[1] * theirs[1]]
-        store_in_order(gradient_ref, mask_ref[0], ours[0], low, values)
+    for outer_ref, inner_ref, mine_ref, past_ref, own_past_ref, *norms in chains:
+        halves = [
+            next_vector(parts, None, norms[-1], past, norms[-2])
+            for parts, past in [
+                ([(outer_ref, 2)], past_ref),
+                ([(inner_ref, 1), (mine_ref, 1)], own_past_ref),
+            ]
+        ]
+        vectors.append([value for half in halves for _, value, _ in half])
+        factors.append(rotation(norms)[-1])
+    for pair, (ours, theirs) in enumerate(zip(*vectors)):
+        values = [factors[0] * ours, factors[1] * theirs]
+        store_in_order(gradient_ref, mask_ref[0], pair, low, values)
 
 
 def last_call(body, mask, operands, shapes):
@@ -391,8 +442,8 @@
             norm = norm + got[half // 2 :]
             send = mine = mine + got[: half // 2]
         inner, _ = yield swap_rows, mine, 1
-        outer, _ = yield swap_rows, jnp.concatenate([inner, mine]), 0
-        return [outer, inner, mine], norm
+        outer, ahead = yield swap_rows, jnp.concatenate([inner, mine]), 0
+        return [outer, inner, mine], norm, ahead
 
     def reduce_cols(send, kept):
         half = send.shape[0] - NORM_ROWS
@@ -408,19 +459,26 @@
 
     def chain(left):
         send, keep = back_product(dense, [left], True)
-        totals, norm = yield from reduce_rows(send, keep)
+        totals, norm, ahead = yield from reduce_rows(send, keep)
         norms = [norm]
         rights = []
         for iteration in range(ITERS):
-            past = [rights[-1], norms[-2]] if rights else []
-            send, keep, right = fore_product(dense, [*totals, norms[-1], *past], not rights)
-            rights.append(right)
+            outer, *own = totals
+            pasts = [[right, norms[-2]] for right in rights[-1]] if rights else [[], []]
+            own = [tied(own[0], ahead), own[1]]
+            part, squares, own_right = fore_own_product(
+                dense, [*own, norms[-1], *pasts[1]], not rights
+            )
+            send, keep, right = fore_product(
+                dense, [outer, part, squares, norms[-1], *pasts[0]], not rights
+            )
+            rights.append([right, own_right])
             halves, norm = yield from reduce_cols(send, keep)
             norms.append(norm)
             send, keep, left = back_product(
                 dense, [*halves, norms[-1], left, norms[-2]], False
             )
-            totals, norm = yield from reduce_rows(send, keep)
+            totals, norm, ahead = yield from reduce_rows(send, keep)
             norms.append(norm)
         return rights, norms, totals
 
@@ -448,17 +506,17 @@
                 continue
         gots[mine] = swap(latest, level)
 
-    cells = dense.shape[1]
+    cells = CB_DEV * TILE
     model, misfit = last_call(
         functools.partial(model_kernel, ITERS),
         mask,
-        [operand for rights, norms, _ in chains for operand in [*rights, *norms]],
+        [operand for rights, norms, _ in chains for operand in [*sum(rights, []), *norms]],
         [(cells, TILE), (NORM_ROWS, TILE)],
     )
     (gradient,) = last_call(
         gradient_kernel,
         mask,
-        [operand for rights, norms, totals in chains for operand in [*totals, rights[-1], *norms]],
+        [operand for rights, norms, totals in chains for operand in [*totals, *rights[-1], *norms]],
         [(cells, TILE)],
     )
     return (model, gradient, misfit[0])

time: 190 us -> 185 us (0.974)
  waiting for transfers between devices: 112 us -> 104 us
  starting transfers between devices: 34.7 us -> 36.9 us
    ppermute x30, waiting for transfers between devices: 98.8 us -> 90.9 us  [swap_rows(): return lax.ppermute(value, ('rows', 'cols'), pairs)]
    ppermute x12, starting transfers between devices: 4.82 us -> 6.73 us  [swap_cols(): lax.ppermute(value, 'cols', [(i, i ^ 1 << level) for i in range(col_count)])]
    pallas_call x20 -> x24, Pallas kernels: 31.4 us -> 32.4 us  [product_call(): pl.pallas_call(body, in_specs=[WHOLE] * (1 + len(operands)), out_specs=[W...]
  transfers between devices with their start and end apart: 42 -> 42, of which waited for: 26 -> 27; matrix products, arithmetic and copies ran while one was open for 1% -> 1% of each run, Pallas kernels for 17% -> 18%
where the time goes in v15:
time: 185 us
  waiting for transfers between devices  104 us (56%)
  Pallas kernels  40.2 us (22%)
  starting transfers between devices  36.9 us (20%)
    ppermute x30, waiting for transfers between devices, swap_rows(): return lax.ppermute(value, ('rows', 'cols'), pairs)  90.9 us
    pallas_call x24, Pallas kernels, product_call(): pl.pallas_call(body, in_specs=[WHOLE] * (1 + len(operands)), out_specs=[W...  32.4 us
    ppermute x30, starting transfers between devices, swap_rows(): return lax.ppermute(value, ('rows', 'cols'), pairs)  30.2 us
    ppermute x12, waiting for transfers between devices, swap_cols(): lax.ppermute(value, 'cols', [(i, i ^ 1 << level) for i in range(col_count)])  13.6 us
    ppermute x12, starting transfers between devices, swap_cols(): lax.ppermute(value, 'cols', [(i, i ^ 1 << level) for i in range(col_count)])  6.73 us
    pallas_call x1, Pallas kernels, fill_dense(): pl.pallas_call(fill_kernel, in_specs=[SCALARS] * 2 + [pl.BlockSpec(memory...  4.4 us
  transfers between devices with their start and end apart: 42, of which 27 were waited for; matrix products, arithmetic and copies ran while one was open for 1% of the time, Pallas kernels for 18%

profile of v15, /device:TPU:0, one launch (start us, length us, event | category | flops | bytes accessed | tf_op | source)
XLA Modules:
  0.0 185.1 jit_solution(14870722837235913400)
XLA Ops:
  0.7 4.4 %shard_map.67 = (bf16[2048,3200]{1,0:T(8,128)(2,1)S(1)}, f32[1024,128]{1,0:T(8,128)S(1)}, f32[1024,128]{1,0:T(8,128)S(1)}) custom-call(s32[24]{0:T(128)S(1)} %fusion.place_ref, s32[1]{0:T(128)} %bitcast.1.flip_ref, s32[16,16]{1,0:T(8,128)} %pattern_in.1, s32[16]{0:T(128)} %bitcast.5, f32[2048,128]{1,0:T(8,128)} %delays_in.1, bf16[16,16,128,128]{3,2,1,0:T(8,128)(2,1)} %tiles_in.1), custom_call_target="tpu_custom_call" | custom-call | bytes 8388608 | tf_op jit(solution)/shard_map/pallas_call | solution.py:106
  5.1 1.4 shard_map.68
  6.5 3.0 %collective-permute-start = (f32[776,128]{1,0:T(8,128)S(1)}, f32[776,128]{1,0:T(8,128)S(1)}, u32[]{:S(2)}, u32[]{:S(2)}) collective-permute-start(f32[776,128]{1,0:T(8,128)S(1)} %get-tuple-element.109), channel_id=1, source_target_pairs={{0,4},{1,9},{2,6},{3,11},{4,0},{5,13},{6,2},{7,15},{8,12},{9,1},{1... | collective-permute-start | bytes 1191944 | tf_op jit(solution)/shard_map/ppermute | solution.py:410
  9.5 1.4 shard_map.69
  12.2 3.1 %collective-permute-done = f32[776,128]{1,0:T(8,128)S(1)} collective-permute-done((f32[776,128]{1,0:T(8,128)S(1)}, f32[776,128]{1,0:T(8,128)S(1)}, u32[]{:S(2)}, u32[]{:S(2)}) %collective-permute-start) | collective-permute-done | bytes 397344 | tf_op jit(solution)/shard_map/ppermute | solution.py:410
  15.4 3.3 %collective-permute-start.1 = (f32[392,128]{1,0:T(8,128)S(1)}, f32[392,128]{1,0:T(8,128)S(1)}, u32[]{:S(2)}, u32[]{:S(2)}) collective-permute-start(f32[392,128]{1,0:T(8,128)S(1)} %pad_maximum_fusion.10), channel_id=1, source_target_pairs={{0,8},{1,5},{2,10},{3,7},{4,12},{5,1},{6,14},{7,3},{8,0},{9,13},{1... | collective-permute-start | bytes 602120 | tf_op jit(solution)/shard_map/ppermute | solution.py:410
  18.7 2.0 %collective-permute-start.3 = (f32[776,128]{1,0:T(8,128)S(1)}, f32[776,128]{1,0:T(8,128)S(1)}, u32[]{:S(2)}, u32[]{:S(2)}) collective-permute-start(f32[776,128]{1,0:T(8,128)S(1)} %get-tuple-element.111), channel_id=1, source_target_pairs={{0,4},{1,9},{2,6},{3,11},{4,0},{5,13},{6,2},{7,15},{8,12},{9,1},{1... | collective-permute-start | bytes 1191944 | tf_op jit(solution)/shard_map/ppermute | solution.py:410
  20.8 5.9 %collective-permute-done.1 = f32[392,128]{1,0:T(8,128)S(1)} collective-permute-done((f32[392,128]{1,0:T(8,128)S(1)}, f32[392,128]{1,0:T(8,128)S(1)}, u32[]{:S(2)}, u32[]{:S(2)}) %collective-permute-start.1) | collective-permute-done | bytes 200736 | tf_op jit(solution)/shard_map/ppermute | solution.py:410
  28.3 2.2 %collective-permute-start.5 = (f32[392,128]{1,0:T(8,128)S(1)}, f32[392,128]{1,0:T(8,128)S(1)}, u32[]{:S(2)}, u32[]{:S(2)}) collective-permute-start(f32[392,128]{1,0:T(8,128)S(1)} %pad_maximum_fusion.12), channel_id=1, source_target_pairs={{0,8},{1,5},{2,10},{3,7},{4,12},{5,1},{6,14},{7,3},{8,0},{9,13},{1... | collective-permute-start | bytes 602120 | tf_op jit(solution)/shard_map/ppermute | solution.py:410
  30.5 4.5 %collective-permute-done.2 = f32[392,128]{1,0:T(8,128)S(1)} collective-permute-done((f32[392,128]{1,0:T(8,128)S(1)}, f32[392,128]{1,0:T(8,128)S(1)}, u32[]{:S(2)}, u32[]{:S(2)}) %collective-permute-start.2) | collective-permute-done | bytes 200736 | tf_op jit(solution)/shard_map/ppermute | solution.py:410
  36.3 1.9 %collective-permute-start.7 = (f32[392,128]{1,0:T(8,128)S(1)}, f32[392,128]{1,0:T(8,128)S(1)}, u32[]{:S(2)}, u32[]{:S(2)}) collective-permute-start(f32[392,128]{1,0:T(8,128)S(1)} %pad_maximum_fusion.13), channel_id=1, source_target_pairs={{0,16},{1,17},{2,18},{3,19},{4,20},{5,21},{6,22},{7,23},{8,24},{9,... | collective-permute-start | bytes 602120 | tf_op jit(solution)/shard_map/ppermute | solution.py:410
  38.2 8.3 %collective-permute-done.4.inner_ref = f32[384,128]{1,0:T(8,128)S(1)} collective-permute-done((f32[384,128]{1,0:T(8,128)S(1)}, f32[384,128]{1,0:T(8,128)S(1)}, u32[]{:S(2)}, u32[]{:S(2)}) %collective-permute-start.4) | collective-permute-done | bytes 196640 | tf_op jit(solution)/shard_map/ppermute | solution.py:410
  46.7 1.9 %shard_map.72 = (f32[1024,128]{1,0:T(8,128)S(1)}, f32[8,128]{1,0:T(8,128)S(1)}, f32[768,128]{1,0:T(8,128)S(1)}) custom-call(bf16[2048,3200]{1,0:T(8,128)(2,1)S(1)} %get-tuple-element.103.refs_0_.dense_ref, f32[384,128]{1,0:T(8,128)S(1)} %collective-permute-done.4.inner_ref, f32[384,128]{1,0:T(8,128)S(1)} %slice_add_fusion.25.mine_ref, ...), custom_call_target="tpu_custom_call" | custom-call | flops 1677721600 | bytes 6553600 | tf_op jit(solution)/shard_map/pallas_call | solution.py:252
  48.6 5.7 %collective-permute-done.6.outer_ref = f32[768,128]{1,0:T(8,128)S(1)} collective-permute-done((f32[768,128]{1,0:T(8,128)S(1)}, f32[768,128]{1,0:T(8,128)S(1)}, u32[]{:S(2)}, u32[]{:S(2)}) %collective-permute-start.6) | collective-permute-done | bytes 393248 | tf_op jit(solution)/shard_map/ppermute | solution.py:410
  57.1 1.5 collective-permute-start.10
  58.6 1.9 %shard_map.75 = (f32[1024,128]{1,0:T(8,128)S(1)}, f32[8,128]{1,0:T(8,128)S(1)}, f32[768,128]{1,0:T(8,128)S(1)}) custom-call(bf16[2048,3200]{1,0:T(8,128)(2,1)S(1)} %get-tuple-element.103.refs_0_.dense_ref, f32[384,128]{1,0:T(8,128)S(1)} %collective-permute-done.8.inner_ref, f32[384,128]{1,0:T(8,128)S(1)} %slice_add_fusion.24.mine_ref, ...), custom_call_target="tpu_custom_call" | custom-call | flops 1677721600 | bytes 6553600 | tf_op jit(solution)/shard_map/pallas_call | solution.py:252
  60.5 2.9 %collective-permute-done.11.outer_ref = f32[768,128]{1,0:T(8,128)S(1)} collective-permute-done((f32[768,128]{1,0:T(8,128)S(1)}, f32[768,128]{1,0:T(8,128)S(1)}, u32[]{:S(2)}, u32[]{:S(2)}) %collective-permute-start.11) | collective-permute-done | bytes 393248 | tf_op jit(solution)/shard_map/ppermute | solution.py:410
  66.8 1.5 collective-permute-start.14
  68.3 1.4 shard_map.78
  69.8 5.9 %collective-permute-done.14 = f32[520,128]{1,0:T(8,128)S(1)} collective-permute-done((f32[520,128]{1,0:T(8,128)S(1)}, f32[520,128]{1,0:T(8,128)S(1)}, u32[]{:S(2)}, u32[]{:S(2)}) %collective-permute-start.14) | collective-permute-done | bytes 266272 | tf_op jit(solution)/shard_map/ppermute | solution.py:413
  78.0 1.6 shard_map.80
  79.6 1.6 collective-permute-start.19
  81.1 3.9 %collective-permute-done.16 = f32[392,128]{1,0:T(8,128)S(1)} collective-permute-done((f32[392,128]{1,0:T(8,128)S(1)}, f32[392,128]{1,0:T(8,128)S(1)}, u32[]{:S(2)}, u32[]{:S(2)}) %collective-permute-start.16) | collective-permute-done | bytes 200736 | tf_op jit(solution)/shard_map/ppermute | solution.py:410
  85.1 1.9 %collective-permute-start.18 = (f32[392,128]{1,0:T(8,128)S(1)}, f32[392,128]{1,0:T(8,128)S(1)}, u32[]{:S(2)}, u32[]{:S(2)}) collective-permute-start(f32[392,128]{1,0:T(8,128)S(1)} %pad_maximum_fusion.15), channel_id=1, source_target_pairs={{0,16},{1,17},{2,18},{3,19},{4,20},{5,21},{6,22},{7,23},{8,24},{9,... | collective-permute-start | bytes 602120 | tf_op jit(solution)/shard_map/ppermute | solution.py:410
  89.5 6.2 %collective-permute-done.18 = f32[392,128]{1,0:T(8,128)S(1)} collective-permute-done((f32[392,128]{1,0:T(8,128)S(1)}, f32[392,128]{1,0:T(8,128)S(1)}, u32[]{:S(2)}, u32[]{:S(2)}) %collective-permute-start.18) | collective-permute-done | bytes 200736 | tf_op jit(solution)/shard_map/ppermute | solution.py:410
  95.8 2.5 %collective-permute-start.23 = (f32[392,128]{1,0:T(8,128)S(1)}, f32[392,128]{1,0:T(8,128)S(1)}, u32[]{:S(2)}, u32[]{:S(2)}) collective-permute-start(f32[392,128]{1,0:T(8,128)S(1)} %pad_maximum_fusion.17), channel_id=1, source_target_pairs={{0,16},{1,17},{2,18},{3,19},{4,20},{5,21},{6,22},{7,23},{8,24},{9,... | collective-permute-start | bytes 602120 | tf_op jit(solution)/shard_map/ppermute | solution.py:410
  98.3 7.5 %collective-permute-done.20.inner_ref = f32[384,128]{1,0:T(8,128)S(1)} collective-permute-done((f32[384,128]{1,0:T(8,128)S(1)}, f32[384,128]{1,0:T(8,128)S(1)}, u32[]{:S(2)}, u32[]{:S(2)}) %collective-permute-start.20) | collective-permute-done | bytes 196640 | tf_op jit(solution)/shard_map/ppermute | solution.py:410
  105.9 1.7 collective-permute-done.23
  108.2 1.9 %shard_map.82 = (f32[1024,128]{1,0:T(8,128)S(1)}, f32[8,128]{1,0:T(8,128)S(1)}, f32[768,128]{1,0:T(8,128)S(1)}) custom-call(bf16[2048,3200]{1,0:T(8,128)(2,1)S(1)} %get-tuple-element.103.refs_0_.dense_ref, f32[384,128]{1,0:T(8,128)S(1)} %collective-permute-done.20.inner_ref, f32[384,128]{1,0:T(8,128)S(1)} %slice_add_fusion.23.mine_ref, ...), custom_call_target="tpu_custom_call" | custom-call | flops 1677721600 | bytes 6553600 | tf_op jit(solution)/shard_map/pallas_call | solution.py:252
  110.1 5.2 %collective-permute-done.22.outer_ref = f32[768,128]{1,0:T(8,128)S(1)} collective-permute-done((f32[768,128]{1,0:T(8,128)S(1)}, f32[768,128]{1,0:T(8,128)S(1)}, u32[]{:S(2)}, u32[]{:S(2)}) %collective-permute-start.22) | collective-permute-done | bytes 393248 | tf_op jit(solution)/shard_map/ppermute | solution.py:410
  118.2 1.6 collective-permute-start.26
  119.8 1.9 %shard_map.85 = (f32[1024,128]{1,0:T(8,128)S(1)}, f32[8,128]{1,0:T(8,128)S(1)}, f32[768,128]{1,0:T(8,128)S(1)}) custom-call(bf16[2048,3200]{1,0:T(8,128)(2,1)S(1)} %get-tuple-element.103.refs_0_.dense_ref, f32[384,128]{1,0:T(8,128)S(1)} %collective-permute-done.25.inner_ref, f32[384,128]{1,0:T(8,128)S(1)} %slice_add_fusion.22.mine_ref, ...), custom_call_target="tpu_custom_call" | custom-call | flops 1677721600 | bytes 6553600 | tf_op jit(solution)/shard_map/pallas_call | solution.py:252
  121.7 2.7 %collective-permute-done.27.outer_ref = f32[768,128]{1,0:T(8,128)S(1)} collective-permute-done((f32[768,128]{1,0:T(8,128)S(1)}, f32[768,128]{1,0:T(8,128)S(1)}, u32[]{:S(2)}, u32[]{:S(2)}) %collective-permute-start.27) | collective-permute-done | bytes 393248 | tf_op jit(solution)/shard_map/ppermute | solution.py:410
  127.8 1.5 collective-permute-start.31
  129.4 1.5 shard_map.88
  131.4 5.3 %collective-permute-done.31 = f32[520,128]{1,0:T(8,128)S(1)} collective-permute-done((f32[520,128]{1,0:T(8,128)S(1)}, f32[520,128]{1,0:T(8,128)S(1)}, u32[]{:S(2)}, u32[]{:S(2)}) %collective-permute-start.31) | collective-permute-done | bytes 266272 | tf_op jit(solution)/shard_map/ppermute | solution.py:413
  139.1 1.5 shard_map.90
  140.6 1.7 collective-permute-start.35
  142.3 3.8 %collective-permute-done.32 = f32[392,128]{1,0:T(8,128)S(1)} collective-permute-done((f32[392,128]{1,0:T(8,128)S(1)}, f32[392,128]{1,0:T(8,128)S(1)}, u32[]{:S(2)}, u32[]{:S(2)}) %collective-permute-start.32) | collective-permute-done | bytes 200736 | tf_op jit(solution)/shard_map/ppermute | solution.py:410
  148.6 1.8 collective-permute-start.36
  150.4 5.6 %collective-permute-done.34 = f32[392,128]{1,0:T(8,128)S(1)} collective-permute-done((f32[392,128]{1,0:T(8,128)S(1)}, f32[392,128]{1,0:T(8,128)S(1)}, u32[]{:S(2)}, u32[]{:S(2)}) %collective-permute-start.34) | collective-permute-done | bytes 200736 | tf_op jit(solution)/shard_map/ppermute | solution.py:410
  156.7 1.4 collective-permute-start.37
  158.0 5.6 %collective-permute-done.38.refs_1_ = f32[384,128]{1,0:T(8,128)S(1)} collective-permute-done((f32[384,128]{1,0:T(8,128)S(1)}, f32[384,128]{1,0:T(8,128)S(1)}, u32[]{:S(2)}, u32[]{:S(2)}) %collective-permute-start.38) | collective-permute-done | bytes 196640 | tf_op jit(solution)/shard_map/ppermute | solution.py:410
  163.6 4.0 %collective-permute-done.37 = f32[392,128]{1,0:T(8,128)S(1)} collective-permute-done((f32[392,128]{1,0:T(8,128)S(1)}, f32[392,128]{1,0:T(8,128)S(1)}, u32[]{:S(2)}, u32[]{:S(2)}) %collective-permute-start.37) | collective-permute-done | bytes 200736 | tf_op jit(solution)/shard_map/ppermute | solution.py:410
  168.6 6.9 %collective-permute-done.40.refs_11_ = f32[384,128]{1,0:T(8,128)S(1)} collective-permute-done((f32[384,128]{1,0:T(8,128)S(1)}, f32[384,128]{1,0:T(8,128)S(1)}, u32[]{:S(2)}, u32[]{:S(2)}) %collective-permute-start.40) | collective-permute-done | bytes 196640 | tf_op jit(solution)/shard_map/ppermute | solution.py:410
  176.4 1.7 shard_map.92
  178.6 4.7 %collective-permute-done.41.refs_10_ = f32[768,128]{1,0:T(8,128)S(1)} collective-permute-done((f32[768,128]{1,0:T(8,128)S(1)}, f32[768,128]{1,0:T(8,128)S(1)}, u32[]{:S(2)}, u32[]{:S(2)}) %collective-permute-start.41) | collective-permute-done | bytes 393248 | tf_op jit(solution)/shard_map/ppermute | solution.py:410
  183.4 1.7 shard_map.93
  (145 shorter events, 30.7 us)
Async XLA Ops:
  6.5 8.8 %collective-permute-start = (f32[776,128]{1,0:T(8,128)S(1)}, f32[776,128]{1,0:T(8,128)S(1)}, u32[]{:S(2)}, u32[]{:S(2)}) collective-permute-start(f32[776,128]{1,0:T(8,128)S(1)} %get-tuple-element.109), channel_id=1, source_target_pairs={{0,4},{1,9},{2,6},{3,11},{4,0},{5,13},{6,2},{7,15},{8,12},{9,1},{1... | collective-permute-start | bytes 1191944 | tf_op jit(solution)/shard_map/ppermute | solution.py:410
  15.4 11.3 %collective-permute-start.1 = (f32[392,128]{1,0:T(8,128)S(1)}, f32[392,128]{1,0:T(8,128)S(1)}, u32[]{:S(2)}, u32[]{:S(2)}) collective-permute-start(f32[392,128]{1,0:T(8,128)S(1)} %pad_maximum_fusion.10), channel_id=1, source_target_pairs={{0,8},{1,5},{2,10},{3,7},{4,12},{5,1},{6,14},{7,3},{8,0},{9,13},{1... | collective-permute-start | bytes 602120 | tf_op jit(solution)/shard_map/ppermute | solution.py:410
  18.7 9.4 %collective-permute-start.3 = (f32[776,128]{1,0:T(8,128)S(1)}, f32[776,128]{1,0:T(8,128)S(1)}, u32[]{:S(2)}, u32[]{:S(2)}) collective-permute-start(f32[776,128]{1,0:T(8,128)S(1)} %get-tuple-element.111), channel_id=1, source_target_pairs={{0,4},{1,9},{2,6},{3,11},{4,0},{5,13},{6,2},{7,15},{8,12},{9,1},{1... | collective-permute-start | bytes 1191944 | tf_op jit(solution)/shard_map/ppermute | solution.py:410
  26.7 8.3 %collective-permute-start.2 = (f32[392,128]{1,0:T(8,128)S(1)}, f32[392,128]{1,0:T(8,128)S(1)}, u32[]{:S(2)}, u32[]{:S(2)}) collective-permute-start(f32[392,128]{1,0:T(8,128)S(1)} %pad_maximum_fusion.11), channel_id=1, source_target_pairs={{0,16},{1,17},{2,18},{3,19},{4,20},{5,21},{6,22},{7,23},{8,24},{9,... | collective-permute-start | bytes 602120 | tf_op jit(solution)/shard_map/ppermute | solution.py:410
  28.3 8.0 %collective-permute-start.5 = (f32[392,128]{1,0:T(8,128)S(1)}, f32[392,128]{1,0:T(8,128)S(1)}, u32[]{:S(2)}, u32[]{:S(2)}) collective-permute-start(f32[392,128]{1,0:T(8,128)S(1)} %pad_maximum_fusion.12), channel_id=1, source_target_pairs={{0,8},{1,5},{2,10},{3,7},{4,12},{5,1},{6,14},{7,3},{8,0},{9,13},{1... | collective-permute-start | bytes 602120 | tf_op jit(solution)/shard_map/ppermute | solution.py:410
  35.0 11.5 %collective-permute-start.4 = (f32[384,128]{1,0:T(8,128)S(1)}, f32[384,128]{1,0:T(8,128)S(1)}, u32[]{:S(2)}, u32[]{:S(2)}) collective-permute-start(f32[384,128]{1,0:T(8,128)S(1)} %slice_add_fusion.25.mine_ref), channel_id=1, source_target_pairs={{0,8},{1,5},{2,10},{3,7},{4,12},{5,1},{6,14},{7,3},{8,0},{9,13},{1... | collective-permute-start | bytes 589832 | tf_op jit(solution)/shard_map/ppermute | solution.py:410
  36.3 10.3 %collective-permute-start.7 = (f32[392,128]{1,0:T(8,128)S(1)}, f32[392,128]{1,0:T(8,128)S(1)}, u32[]{:S(2)}, u32[]{:S(2)}) collective-permute-start(f32[392,128]{1,0:T(8,128)S(1)} %pad_maximum_fusion.13), channel_id=1, source_target_pairs={{0,16},{1,17},{2,18},{3,19},{4,20},{5,21},{6,22},{7,23},{8,24},{9,... | collective-permute-start | bytes 602120 | tf_op jit(solution)/shard_map/ppermute | solution.py:410
  46.5 7.8 %collective-permute-start.6 = (f32[768,128]{1,0:T(8,128)S(1)}, f32[768,128]{1,0:T(8,128)S(1)}, u32[]{:S(2)}, u32[]{:S(2)}) collective-permute-start(f32[768,128]{1,0:T(8,128)S(1)} %pad_maximum_fusion), channel_id=1, source_target_pairs={{0,4},{1,9},{2,6},{3,11},{4,0},{5,13},{6,2},{7,15},{8,12},{9,1},{1... | collective-permute-start | bytes 1179656 | tf_op jit(solution)/shard_map/ppermute | solution.py:410
  46.6 8.9 %collective-permute-start.8 = (f32[384,128]{1,0:T(8,128)S(1)}, f32[384,128]{1,0:T(8,128)S(1)}, u32[]{:S(2)}, u32[]{:S(2)}) collective-permute-start(f32[384,128]{1,0:T(8,128)S(1)} %slice_add_fusion.24.mine_ref), channel_id=1, source_target_pairs={{0,8},{1,5},{2,10},{3,7},{4,12},{5,1},{6,14},{7,3},{8,0},{9,13},{1... | collective-permute-start | bytes 589832 | tf_op jit(solution)/shard_map/ppermute | solution.py:410
  55.4 1.6 collective-permute-start.9
  55.6 7.8 %collective-permute-start.11 = (f32[768,128]{1,0:T(8,128)S(1)}, f32[768,128]{1,0:T(8,128)S(1)}, u32[]{:S(2)}, u32[]{:S(2)}) collective-permute-start(f32[768,128]{1,0:T(8,128)S(1)} %pad_maximum_fusion.1), channel_id=1, source_target_pairs={{0,4},{1,9},{2,6},{3,11},{4,0},{5,13},{6,2},{7,15},{8,12},{9,1},{1... | collective-permute-start | bytes 1179656 | tf_op jit(solution)/shard_map/ppermute | solution.py:410
  57.1 8.5 %collective-permute-start.10 = (f32[520,128]{1,0:T(8,128)S(1)}, f32[520,128]{1,0:T(8,128)S(1)}, u32[]{:S(2)}, u32[]{:S(2)}) collective-permute-start(f32[520,128]{1,0:T(8,128)S(1)} %pad_maximum_fusion.6), channel_id=1, source_target_pairs={{0,2},{1,3},{2,0},{3,1},{4,6},{5,7},{6,4},{7,5},{8,10},{9,11},{10,... | collective-permute-start | bytes 798728 | tf_op jit(solution)/shard_map/ppermute | solution.py:413
  64.5 2.2 %collective-permute-start.13 = (f32[520,128]{1,0:T(8,128)S(1)}, f32[520,128]{1,0:T(8,128)S(1)}, u32[]{:S(2)}, u32[]{:S(2)}) collective-permute-start(f32[520,128]{1,0:T(8,128)S(1)} %get-tuple-element.135), channel_id=1, source_target_pairs={{0,1},{1,0},{2,3},{3,2},{4,5},{5,4},{6,7},{7,6},{8,9},{9,8},{10,11... | collective-permute-start | bytes 798728 | tf_op jit(solution)/shard_map/ppermute | solution.py:413
  65.7 2.6 %collective-permute-start.12 = (f32[512,128]{1,0:T(8,128)S(1)}, f32[512,128]{1,0:T(8,128)S(1)}, u32[]{:S(2)}, u32[]{:S(2)}) collective-permute-start(f32[512,128]{1,0:T(8,128)S(1)} %slice_add_fusion.12.refs_2_), channel_id=1, source_target_pairs={{0,1},{1,0},{2,3},{3,2},{4,5},{5,4},{6,7},{7,6},{8,9},{9,8},{10,11... | collective-permute-start | bytes 786440 | tf_op jit(solution)/shard_map/ppermute | solution.py:413
  66.8 8.9 %collective-permute-start.14 = (f32[520,128]{1,0:T(8,128)S(1)}, f32[520,128]{1,0:T(8,128)S(1)}, u32[]{:S(2)}, u32[]{:S(2)}) collective-permute-start(f32[520,128]{1,0:T(8,128)S(1)} %pad_maximum_fusion.7), channel_id=1, source_target_pairs={{0,2},{1,3},{2,0},{3,1},{4,6},{5,7},{6,4},{7,5},{8,10},{9,11},{10,... | collective-permute-start | bytes 798728 | tf_op jit(solution)/shard_map/ppermute | solution.py:413
  69.7 7.9 %collective-permute-start.15 = (f32[776,128]{1,0:T(8,128)S(1)}, f32[776,128]{1,0:T(8,128)S(1)}, u32[]{:S(2)}, u32[]{:S(2)}) collective-permute-start(f32[776,128]{1,0:T(8,128)S(1)} %get-tuple-element.142), channel_id=1, source_target_pairs={{0,4},{1,9},{2,6},{3,11},{4,0},{5,13},{6,2},{7,15},{8,12},{9,1},{1... | collective-permute-start | bytes 1191944 | tf_op jit(solution)/shard_map/ppermute | solution.py:410
  75.7 2.3 %collective-permute-start.17 = (f32[512,128]{1,0:T(8,128)S(1)}, f32[512,128]{1,0:T(8,128)S(1)}, u32[]{:S(2)}, u32[]{:S(2)}) collective-permute-start(f32[512,128]{1,0:T(8,128)S(1)} %slice_add_fusion.10.refs_2_), channel_id=1, source_target_pairs={{0,1},{1,0},{2,3},{3,2},{4,5},{5,4},{6,7},{7,6},{8,9},{9,8},{10,11... | collective-permute-start | bytes 786440 | tf_op jit(solution)/shard_map/ppermute | solution.py:413
  77.7 7.3 %collective-permute-start.16 = (f32[392,128]{1,0:T(8,128)S(1)}, f32[392,128]{1,0:T(8,128)S(1)}, u32[]{:S(2)}, u32[]{:S(2)}) collective-permute-start(f32[392,128]{1,0:T(8,128)S(1)} %pad_maximum_fusion.14), channel_id=1, source_target_pairs={{0,8},{1,5},{2,10},{3,7},{4,12},{5,1},{6,14},{7,3},{8,0},{9,13},{1... | collective-permute-start | bytes 602120 | tf_op jit(solution)/shard_map/ppermute | solution.py:410
  79.6 8.7 %collective-permute-start.19 = (f32[776,128]{1,0:T(8,128)S(1)}, f32[776,128]{1,0:T(8,128)S(1)}, u32[]{:S(2)}, u32[]{:S(2)}) collective-permute-start(f32[776,128]{1,0:T(8,128)S(1)} %get-tuple-element.147), channel_id=1, source_target_pairs={{0,4},{1,9},{2,6},{3,11},{4,0},{5,13},{6,2},{7,15},{8,12},{9,1},{1... | collective-permute-start | bytes 1191944 | tf_op jit(solution)/shard_map/ppermute | solution.py:410
  85.1 10.6 %collective-permute-start.18 = (f32[392,128]{1,0:T(8,128)S(1)}, f32[392,128]{1,0:T(8,128)S(1)}, u32[]{:S(2)}, u32[]{:S(2)}) collective-permute-start(f32[392,128]{1,0:T(8,128)S(1)} %pad_maximum_fusion.15), channel_id=1, source_target_pairs={{0,16},{1,17},{2,18},{3,19},{4,20},{5,21},{6,22},{7,23},{8,24},{9,... | collective-permute-start | bytes 602120 | tf_op jit(solution)/shard_map/ppermute | solution.py:410
  88.4 7.4 %collective-permute-start.21 = (f32[392,128]{1,0:T(8,128)S(1)}, f32[392,128]{1,0:T(8,128)S(1)}, u32[]{:S(2)}, u32[]{:S(2)}) collective-permute-start(f32[392,128]{1,0:T(8,128)S(1)} %pad_maximum_fusion.16), channel_id=1, source_target_pairs={{0,8},{1,5},{2,10},{3,7},{4,12},{5,1},{6,14},{7,3},{8,0},{9,13},{1... | collective-permute-start | bytes 602120 | tf_op jit(solution)/shard_map/ppermute | solution.py:410
  95.7 10.1 %collective-permute-start.20 = (f32[384,128]{1,0:T(8,128)S(1)}, f32[384,128]{1,0:T(8,128)S(1)}, u32[]{:S(2)}, u32[]{:S(2)}) collective-permute-start(f32[384,128]{1,0:T(8,128)S(1)} %slice_add_fusion.23.mine_ref), channel_id=1, source_target_pairs={{0,8},{1,5},{2,10},{3,7},{4,12},{5,1},{6,14},{7,3},{8,0},{9,13},{1... | collective-permute-start | bytes 589832 | tf_op jit(solution)/shard_map/ppermute | solution.py:410
  95.8 11.8 %collective-permute-start.23 = (f32[392,128]{1,0:T(8,128)S(1)}, f32[392,128]{1,0:T(8,128)S(1)}, u32[]{:S(2)}, u32[]{:S(2)}) collective-permute-start(f32[392,128]{1,0:T(8,128)S(1)} %pad_maximum_fusion.17), channel_id=1, source_target_pairs={{0,16},{1,17},{2,18},{3,19},{4,20},{5,21},{6,22},{7,23},{8,24},{9,... | collective-permute-start | bytes 602120 | tf_op jit(solution)/shard_map/ppermute | solution.py:410
  105.8 9.5 %collective-permute-start.22 = (f32[768,128]{1,0:T(8,128)S(1)}, f32[768,128]{1,0:T(8,128)S(1)}, u32[]{:S(2)}, u32[]{:S(2)}) collective-permute-start(f32[768,128]{1,0:T(8,128)S(1)} %pad_maximum_fusion.2), channel_id=1, source_target_pairs={{0,4},{1,9},{2,6},{3,11},{4,0},{5,13},{6,2},{7,15},{8,12},{9,1},{1... | collective-permute-start | bytes 1179656 | tf_op jit(solution)/shard_map/ppermute | solution.py:410
  107.6 8.9 %collective-permute-start.25 = (f32[384,128]{1,0:T(8,128)S(1)}, f32[384,128]{1,0:T(8,128)S(1)}, u32[]{:S(2)}, u32[]{:S(2)}) collective-permute-start(f32[384,128]{1,0:T(8,128)S(1)} %slice_add_fusion.22.mine_ref), channel_id=1, source_target_pairs={{0,8},{1,5},{2,10},{3,7},{4,12},{5,1},{6,14},{7,3},{8,0},{9,13},{1... | collective-permute-start | bytes 589832 | tf_op jit(solution)/shard_map/ppermute | solution.py:410
  116.4 1.6 collective-permute-start.24
  116.6 7.8 %collective-permute-start.27 = (f32[768,128]{1,0:T(8,128)S(1)}, f32[768,128]{1,0:T(8,128)S(1)}, u32[]{:S(2)}, u32[]{:S(2)}) collective-permute-start(f32[768,128]{1,0:T(8,128)S(1)} %pad_maximum_fusion.3), channel_id=1, source_target_pairs={{0,4},{1,9},{2,6},{3,11},{4,0},{5,13},{6,2},{7,15},{8,12},{9,1},{1... | collective-permute-start | bytes 1179656 | tf_op jit(solution)/shard_map/ppermute | solution.py:410
  118.2 8.5 %collective-permute-start.26 = (f32[520,128]{1,0:T(8,128)S(1)}, f32[520,128]{1,0:T(8,128)S(1)}, u32[]{:S(2)}, u32[]{:S(2)}) collective-permute-start(f32[520,128]{1,0:T(8,128)S(1)} %pad_maximum_fusion.8), channel_id=1, source_target_pairs={{0,2},{1,3},{2,0},{3,1},{4,6},{5,7},{6,4},{7,5},{8,10},{9,11},{10,... | collective-permute-start | bytes 798728 | tf_op jit(solution)/shard_map/ppermute | solution.py:413
  125.5 2.2 %collective-permute-start.29 = (f32[520,128]{1,0:T(8,128)S(1)}, f32[520,128]{1,0:T(8,128)S(1)}, u32[]{:S(2)}, u32[]{:S(2)}) collective-permute-start(f32[520,128]{1,0:T(8,128)S(1)} %get-tuple-element.173), channel_id=1, source_target_pairs={{0,1},{1,0},{2,3},{3,2},{4,5},{5,4},{6,7},{7,6},{8,9},{9,8},{10,11... | collective-permute-start | bytes 798728 | tf_op jit(solution)/shard_map/ppermute | solution.py:413
  126.7 2.7 %collective-permute-start.28 = (f32[512,128]{1,0:T(8,128)S(1)}, f32[512,128]{1,0:T(8,128)S(1)}, u32[]{:S(2)}, u32[]{:S(2)}) collective-permute-start(f32[512,128]{1,0:T(8,128)S(1)} %slice_add_fusion.8.refs_2_), channel_id=1, source_target_pairs={{0,1},{1,0},{2,3},{3,2},{4,5},{5,4},{6,7},{7,6},{8,9},{9,8},{10,11... | collective-permute-start | bytes 786440 | tf_op jit(solution)/shard_map/ppermute | solution.py:413
  127.8 8.9 %collective-permute-start.31 = (f32[520,128]{1,0:T(8,128)S(1)}, f32[520,128]{1,0:T(8,128)S(1)}, u32[]{:S(2)}, u32[]{:S(2)}) collective-permute-start(f32[520,128]{1,0:T(8,128)S(1)} %pad_maximum_fusion.9), channel_id=1, source_target_pairs={{0,2},{1,3},{2,0},{3,1},{4,6},{5,7},{6,4},{7,5},{8,10},{9,11},{10,... | collective-permute-start | bytes 798728 | tf_op jit(solution)/shard_map/ppermute | solution.py:413
  130.9 7.8 %collective-permute-start.30 = (f32[776,128]{1,0:T(8,128)S(1)}, f32[776,128]{1,0:T(8,128)S(1)}, u32[]{:S(2)}, u32[]{:S(2)}) collective-permute-start(f32[776,128]{1,0:T(8,128)S(1)} %get-tuple-element.180), channel_id=1, source_target_pairs={{0,4},{1,9},{2,6},{3,11},{4,0},{5,13},{6,2},{7,15},{8,12},{9,1},{1... | collective-permute-start | bytes 1191944 | tf_op jit(solution)/shard_map/ppermute | solution.py:410
  136.7 2.4 %collective-permute-start.33 = (f32[512,128]{1,0:T(8,128)S(1)}, f32[512,128]{1,0:T(8,128)S(1)}, u32[]{:S(2)}, u32[]{:S(2)}) collective-permute-start(f32[512,128]{1,0:T(8,128)S(1)} %slice_add_fusion.6.refs_2_), channel_id=1, source_target_pairs={{0,1},{1,0},{2,3},{3,2},{4,5},{5,4},{6,7},{7,6},{8,9},{9,8},{10,11... | collective-permute-start | bytes 786440 | tf_op jit(solution)/shard_map/ppermute | solution.py:413
  138.8 7.4 %collective-permute-start.32 = (f32[392,128]{1,0:T(8,128)S(1)}, f32[392,128]{1,0:T(8,128)S(1)}, u32[]{:S(2)}, u32[]{:S(2)}) collective-permute-start(f32[392,128]{1,0:T(8,128)S(1)} %pad_maximum_fusion.18), channel_id=1, source_target_pairs={{0,8},{1,5},{2,10},{3,7},{4,12},{5,1},{6,14},{7,3},{8,0},{9,13},{1... | collective-permute-start | bytes 602120 | tf_op jit(solution)/shard_map/ppermute | solution.py:410
  140.6 7.9 %collective-permute-start.35 = (f32[776,128]{1,0:T(8,128)S(1)}, f32[776,128]{1,0:T(8,128)S(1)}, u32[]{:S(2)}, u32[]{:S(2)}) collective-permute-start(f32[776,128]{1,0:T(8,128)S(1)} %get-tuple-element.187), channel_id=1, source_target_pairs={{0,4},{1,9},{2,6},{3,11},{4,0},{5,13},{6,2},{7,15},{8,12},{9,1},{1... | collective-permute-start | bytes 1191944 | tf_op jit(solution)/shard_map/ppermute | solution.py:410
  146.2 9.8 %collective-permute-start.34 = (f32[392,128]{1,0:T(8,128)S(1)}, f32[392,128]{1,0:T(8,128)S(1)}, u32[]{:S(2)}, u32[]{:S(2)}) collective-permute-start(f32[392,128]{1,0:T(8,128)S(1)} %pad_maximum_fusion.19), channel_id=1, source_target_pairs={{0,16},{1,17},{2,18},{3,19},{4,20},{5,21},{6,22},{7,23},{8,24},{9,... | collective-permute-start | bytes 602120 | tf_op jit(solution)/shard_map/ppermute | solution.py:410
  148.6 8.0 %collective-permute-start.36 = (f32[392,128]{1,0:T(8,128)S(1)}, f32[392,128]{1,0:T(8,128)S(1)}, u32[]{:S(2)}, u32[]{:S(2)}) collective-permute-start(f32[392,128]{1,0:T(8,128)S(1)} %pad_maximum_fusion.20), channel_id=1, source_target_pairs={{0,8},{1,5},{2,10},{3,7},{4,12},{5,1},{6,14},{7,3},{8,0},{9,13},{1... | collective-permute-start | bytes 602120 | tf_op jit(solution)/shard_map/ppermute | solution.py:410
  156.0 7.5 %collective-permute-start.38 = (f32[384,128]{1,0:T(8,128)S(1)}, f32[384,128]{1,0:T(8,128)S(1)}, u32[]{:S(2)}, u32[]{:S(2)}) collective-permute-start(f32[384,128]{1,0:T(8,128)S(1)} %slice_add_fusion.21.refs_2_), channel_id=1, source_target_pairs={{0,8},{1,5},{2,10},{3,7},{4,12},{5,1},{6,14},{7,3},{8,0},{9,13},{1... | collective-permute-start | bytes 589832 | tf_op jit(solution)/shard_map/ppermute | solution.py:410
  156.7 10.9 %collective-permute-start.37 = (f32[392,128]{1,0:T(8,128)S(1)}, f32[392,128]{1,0:T(8,128)S(1)}, u32[]{:S(2)}, u32[]{:S(2)}) collective-permute-start(f32[392,128]{1,0:T(8,128)S(1)} %pad_maximum_fusion.21), channel_id=1, source_target_pairs={{0,16},{1,17},{2,18},{3,19},{4,20},{5,21},{6,22},{7,23},{8,24},{9,... | collective-permute-start | bytes 602120 | tf_op jit(solution)/shard_map/ppermute | solution.py:410
  167.6 7.9 %collective-permute-start.40 = (f32[384,128]{1,0:T(8,128)S(1)}, f32[384,128]{1,0:T(8,128)S(1)}, u32[]{:S(2)}, u32[]{:S(2)}) collective-permute-start(f32[384,128]{1,0:T(8,128)S(1)} %slice_add_fusion.20.refs_12_), channel_id=1, source_target_pairs={{0,8},{1,5},{2,10},{3,7},{4,12},{5,1},{6,14},{7,3},{8,0},{9,13},{1... | collective-permute-start | bytes 589832 | tf_op jit(solution)/shard_map/ppermute | solution.py:410
  167.7 10.9 %collective-permute-start.39 = (f32[768,128]{1,0:T(8,128)S(1)}, f32[768,128]{1,0:T(8,128)S(1)}, u32[]{:S(2)}, u32[]{:S(2)}) collective-permute-start(f32[768,128]{1,0:T(8,128)S(1)} %pad_maximum_fusion.4), channel_id=1, source_target_pairs={{0,4},{1,9},{2,6},{3,11},{4,0},{5,13},{6,2},{7,15},{8,12},{9,1},{1... | collective-permute-start | bytes 1179656 | tf_op jit(solution)/shard_map/ppermute | solution.py:410
  175.5 7.8 %collective-permute-start.41 = (f32[768,128]{1,0:T(8,128)S(1)}, f32[768,128]{1,0:T(8,128)S(1)}, u32[]{:S(2)}, u32[]{:S(2)}) collective-permute-start(f32[768,128]{1,0:T(8,128)S(1)} %pad_maximum_fusion.5), channel_id=1, source_target_pairs={{0,4},{1,9},{2,6},{3,11},{4,0},{5,13},{6,2},{7,15},{8,12},{9,1},{1... | collective-permute-start | bytes 1179656 | tf_op jit(solution)/shard_map/ppermute | solution.py:410

commit v16 on v15

--- a/solution.py
+++ b/solution.py
@@ -275,10 +275,8 @@
     )
 
 
-    def keep(flat):
-        return product_call(back_keep_kernel, dense, [flat], [float_rows(cells // 4)])[0]
-
-    return send, (keep, flat), *raw
+    (keep,) = product_call(back_keep_kernel, dense, [flat], [float_rows(cells // 4)])
+    return send, keep, *raw
 
 
 def fore_own_product(dense, operands, first):
@@ -431,10 +429,10 @@
         half, operand = kept
         return half(tied(operand, ahead))
 
-    def reduce_rows(send, kept):
-        half = send.shape[0] - NORM_ROWS
-        got, ahead = yield swap_rows, send, 0
-        keep = kept_half(kept, ahead) + got[:half]
+    def reduce_rows(send, keep):
+        half = keep.shape[0]
+        got, _ = yield swap_rows, send, 0
+        keep = keep + got[:half]
         norm = send[half:] + got[half:]
         send, mine = keep[: half // 2], keep[half // 2 :]
         for level in range(1, len(row_bits)):

time: 185 us -> 184 us (level)
  waiting for transfers between devices: 104 us -> 100 us
    ppermute x30, starting transfers between devices: 30.2 us -> 32.7 us  [swap_rows(): return lax.ppermute(value, ('rows', 'cols'), pairs)]
    ppermute x12, waiting for transfers between devices: 13.6 us -> 11.5 us  [swap_cols(): lax.ppermute(value, 'cols', [(i, i ^ 1 << level) for i in range(col_count)])]
    ppermute x30, waiting for transfers between devices: 90.9 us -> 89 us  [swap_rows(): return lax.ppermute(value, ('rows', 'cols'), pairs)]
  transfers between devices with their start and end apart: 42 -> 42, of which waited for: 27 -> 32; matrix products, arithmetic and copies ran while one was open for 1% -> 1% of each run, Pallas kernels for 18% -> 18%
where the time goes in v16:
time: 184 us
  waiting for transfers between devices  100 us (54%)
  Pallas kernels  41.7 us (23%)
  starting transfers between devices  38.4 us (21%)
    ppermute x30, waiting for transfers between devices, swap_rows(): return lax.ppermute(value, ('rows', 'cols'), pairs)  89 us
    ppermute x30, starting transfers between devices, swap_rows(): return lax.ppermute(value, ('rows', 'cols'), pairs)  32.7 us
    pallas_call x24, Pallas kernels, product_call(): pl.pallas_call(body, in_specs=[WHOLE] * (1 + len(operands)), out_specs=[W...  32.4 us
    ppermute x12, waiting for transfers between devices, swap_cols(): lax.ppermute(value, 'cols', [(i, i ^ 1 << level) for i in range(col_count)])  11.5 us
    pallas_call x1, Pallas kernels, fill_dense(): pl.pallas_call(fill_kernel, in_specs=[SCALARS] * 2 + [pl.BlockSpec(memory...  5.92 us
    ppermute x12, starting transfers between devices, swap_cols(): lax.ppermute(value, 'cols', [(i, i ^ 1 << level) for i in range(col_count)])  5.75 us
  transfers between devices with their start and end apart: 42, of which 32 were waited for; matrix products, arithmetic and copies ran while one was open for 1% of the time, Pallas kernels for 18%

profile of v16, /device:TPU:0, one launch (start us, length us, event | category | flops | bytes accessed | tf_op | source)
XLA Modules:
  0.0 184.1 jit_solution(5147726928764001051)
XLA Ops:
  0.7 5.9 %shard_map.67 = (bf16[2048,3200]{1,0:T(8,128)(2,1)S(1)}, f32[1024,128]{1,0:T(8,128)S(1)}, f32[1024,128]{1,0:T(8,128)S(1)}) custom-call(s32[24]{0:T(128)S(1)} %fusion.place_ref, s32[1]{0:T(128)} %bitcast.1.flip_ref, s32[16,16]{1,0:T(8,128)} %pattern_in.1, s32[16]{0:T(128)} %bitcast.5, f32[2048,128]{1,0:T(8,128)} %delays_in.1, bf16[16,16,128,128]{3,2,1,0:T(8,128)(2,1)} %tiles_in.1), custom_call_target="tpu_custom_call" | custom-call | bytes 8388608 | tf_op jit(solution)/shard_map/pallas_call | solution.py:106
  8.0 1.5 collective-permute-start
  12.2 3.7 %collective-permute-done = f32[776,128]{1,0:T(8,128)S(1)} collective-permute-done((f32[776,128]{1,0:T(8,128)S(1)}, f32[776,128]{1,0:T(8,128)S(1)}, u32[]{:S(2)}, u32[]{:S(2)}) %collective-permute-start) | collective-permute-done | bytes 397344 | tf_op jit(solution)/shard_map/ppermute | solution.py:408
  16.0 3.0 %collective-permute-start.1 = (f32[392,128]{1,0:T(8,128)S(1)}, f32[392,128]{1,0:T(8,128)S(1)}, u32[]{:S(2)}, u32[]{:S(2)}) collective-permute-start(f32[392,128]{1,0:T(8,128)S(1)} %pad_maximum_fusion.10), channel_id=1, source_target_pairs={{0,8},{1,5},{2,10},{3,7},{4,12},{5,1},{6,14},{7,3},{8,0},{9,13},{1... | collective-permute-start | bytes 602120 | tf_op jit(solution)/shard_map/ppermute | solution.py:408
  21.5 2.7 %collective-permute-done.1 = f32[392,128]{1,0:T(8,128)S(1)} collective-permute-done((f32[392,128]{1,0:T(8,128)S(1)}, f32[392,128]{1,0:T(8,128)S(1)}, u32[]{:S(2)}, u32[]{:S(2)}) %collective-permute-start.1) | collective-permute-done | bytes 200736 | tf_op jit(solution)/shard_map/ppermute | solution.py:408
  24.2 1.8 collective-permute-start.2
  26.0 2.2 %collective-permute-done.3 = f32[776,128]{1,0:T(8,128)S(1)} collective-permute-done((f32[776,128]{1,0:T(8,128)S(1)}, f32[776,128]{1,0:T(8,128)S(1)}, u32[]{:S(2)}, u32[]{:S(2)}) %collective-permute-start.3) | collective-permute-done | bytes 397344 | tf_op jit(solution)/shard_map/ppermute | solution.py:408
  28.4 6.1 %collective-permute-done.2 = f32[392,128]{1,0:T(8,128)S(1)} collective-permute-done((f32[392,128]{1,0:T(8,128)S(1)}, f32[392,128]{1,0:T(8,128)S(1)}, u32[]{:S(2)}, u32[]{:S(2)}) %collective-permute-start.2) | collective-permute-done | bytes 200736 | tf_op jit(solution)/shard_map/ppermute | solution.py:408
  35.9 2.2 %collective-permute-start.7 = (f32[392,128]{1,0:T(8,128)S(1)}, f32[392,128]{1,0:T(8,128)S(1)}, u32[]{:S(2)}, u32[]{:S(2)}) collective-permute-start(f32[392,128]{1,0:T(8,128)S(1)} %pad_maximum_fusion.13), channel_id=1, source_target_pairs={{0,16},{1,17},{2,18},{3,19},{4,20},{5,21},{6,22},{7,23},{8,24},{9,... | collective-permute-start | bytes 602120 | tf_op jit(solution)/shard_map/ppermute | solution.py:408
  38.0 8.1 %collective-permute-done.4.inner_ref = f32[384,128]{1,0:T(8,128)S(1)} collective-permute-done((f32[384,128]{1,0:T(8,128)S(1)}, f32[384,128]{1,0:T(8,128)S(1)}, u32[]{:S(2)}, u32[]{:S(2)}) %collective-permute-start.4) | collective-permute-done | bytes 196640 | tf_op jit(solution)/shard_map/ppermute | solution.py:408
  46.2 1.6 collective-permute-start.6
  48.1 1.9 %shard_map.72 = (f32[1024,128]{1,0:T(8,128)S(1)}, f32[8,128]{1,0:T(8,128)S(1)}, f32[768,128]{1,0:T(8,128)S(1)}) custom-call(bf16[2048,3200]{1,0:T(8,128)(2,1)S(1)} %get-tuple-element.97.refs_0_.dense_ref, f32[384,128]{1,0:T(8,128)S(1)} %collective-permute-done.4.inner_ref, f32[384,128]{1,0:T(8,128)S(1)} %slice_add_fusion.25.mine_ref, ...), custom_call_target="tpu_custom_call" | custom-call | flops 1677721600 | bytes 6553600 | tf_op jit(solution)/shard_map/pallas_call | solution.py:252
  50.0 4.1 %collective-permute-done.6.outer_ref = f32[768,128]{1,0:T(8,128)S(1)} collective-permute-done((f32[768,128]{1,0:T(8,128)S(1)}, f32[768,128]{1,0:T(8,128)S(1)}, u32[]{:S(2)}, u32[]{:S(2)}) %collective-permute-start.6) | collective-permute-done | bytes 393248 | tf_op jit(solution)/shard_map/ppermute | solution.py:408
  55.3 1.6 collective-permute-start.11
  57.9 2.8 %collective-permute-start.10 = (f32[520,128]{1,0:T(8,128)S(1)}, f32[520,128]{1,0:T(8,128)S(1)}, u32[]{:S(2)}, u32[]{:S(2)}) collective-permute-start(f32[520,128]{1,0:T(8,128)S(1)} %pad_maximum_fusion.6), channel_id=1, source_target_pairs={{0,2},{1,3},{2,0},{3,1},{4,6},{5,7},{6,4},{7,5},{8,10},{9,11},{10,... | collective-permute-start | bytes 798728 | tf_op jit(solution)/shard_map/ppermute | solution.py:411
  60.7 1.9 %shard_map.75 = (f32[1024,128]{1,0:T(8,128)S(1)}, f32[8,128]{1,0:T(8,128)S(1)}, f32[768,128]{1,0:T(8,128)S(1)}) custom-call(bf16[2048,3200]{1,0:T(8,128)(2,1)S(1)} %get-tuple-element.97.refs_0_.dense_ref, f32[384,128]{1,0:T(8,128)S(1)} %collective-permute-done.8.inner_ref, f32[384,128]{1,0:T(8,128)S(1)} %slice_add_fusion.24.mine_ref, ...), custom_call_target="tpu_custom_call" | custom-call | flops 1677721600 | bytes 6553600 | tf_op jit(solution)/shard_map/pallas_call | solution.py:252
  64.3 1.6 collective-permute-done.10
  67.1 1.8 collective-permute-start.15
  70.4 2.0 %collective-permute-start.14 = (f32[776,128]{1,0:T(8,128)S(1)}, f32[776,128]{1,0:T(8,128)S(1)}, u32[]{:S(2)}, u32[]{:S(2)}) collective-permute-start(f32[776,128]{1,0:T(8,128)S(1)} %get-tuple-element.134), channel_id=1, source_target_pairs={{0,4},{1,9},{2,6},{3,11},{4,0},{5,13},{6,2},{7,15},{8,12},{9,1},{1... | collective-permute-start | bytes 1191944 | tf_op jit(solution)/shard_map/ppermute | solution.py:408
  73.6 2.3 %collective-permute-done.15 = f32[520,128]{1,0:T(8,128)S(1)} collective-permute-done((f32[520,128]{1,0:T(8,128)S(1)}, f32[520,128]{1,0:T(8,128)S(1)}, u32[]{:S(2)}, u32[]{:S(2)}) %collective-permute-start.15) | collective-permute-done | bytes 266272 | tf_op jit(solution)/shard_map/ppermute | solution.py:411
  76.1 2.2 %collective-permute-done.14 = f32[776,128]{1,0:T(8,128)S(1)} collective-permute-done((f32[776,128]{1,0:T(8,128)S(1)}, f32[776,128]{1,0:T(8,128)S(1)}, u32[]{:S(2)}, u32[]{:S(2)}) %collective-permute-start.14) | collective-permute-done | bytes 397344 | tf_op jit(solution)/shard_map/ppermute | solution.py:408
  78.4 1.7 collective-permute-start.16
  80.1 1.6 shard_map.80
  83.5 1.6 collective-permute-done.16
  85.2 2.8 %collective-permute-start.18 = (f32[392,128]{1,0:T(8,128)S(1)}, f32[392,128]{1,0:T(8,128)S(1)}, u32[]{:S(2)}, u32[]{:S(2)}) collective-permute-start(f32[392,128]{1,0:T(8,128)S(1)} %pad_maximum_fusion.15), channel_id=1, source_target_pairs={{0,16},{1,17},{2,18},{3,19},{4,20},{5,21},{6,22},{7,23},{8,24},{9,... | collective-permute-start | bytes 602120 | tf_op jit(solution)/shard_map/ppermute | solution.py:408
  88.0 1.6 collective-permute-done.19
  90.1 6.2 %collective-permute-done.18 = f32[392,128]{1,0:T(8,128)S(1)} collective-permute-done((f32[392,128]{1,0:T(8,128)S(1)}, f32[392,128]{1,0:T(8,128)S(1)}, u32[]{:S(2)}, u32[]{:S(2)}) %collective-permute-start.18) | collective-permute-done | bytes 200736 | tf_op jit(solution)/shard_map/ppermute | solution.py:408
  99.0 9.1 %collective-permute-done.20.inner_ref = f32[384,128]{1,0:T(8,128)S(1)} collective-permute-done((f32[384,128]{1,0:T(8,128)S(1)}, f32[384,128]{1,0:T(8,128)S(1)}, u32[]{:S(2)}, u32[]{:S(2)}) %collective-permute-start.20) | collective-permute-done | bytes 196640 | tf_op jit(solution)/shard_map/ppermute | solution.py:408
  109.0 1.9 %shard_map.82 = (f32[1024,128]{1,0:T(8,128)S(1)}, f32[8,128]{1,0:T(8,128)S(1)}, f32[768,128]{1,0:T(8,128)S(1)}) custom-call(bf16[2048,3200]{1,0:T(8,128)(2,1)S(1)} %get-tuple-element.97.refs_0_.dense_ref, f32[384,128]{1,0:T(8,128)S(1)} %collective-permute-done.20.inner_ref, f32[384,128]{1,0:T(8,128)S(1)} %slice_add_fusion.23.mine_ref, ...), custom_call_target="tpu_custom_call" | custom-call | flops 1677721600 | bytes 6553600 | tf_op jit(solution)/shard_map/pallas_call | solution.py:252
  110.9 5.0 %collective-permute-done.22.outer_ref = f32[768,128]{1,0:T(8,128)S(1)} collective-permute-done((f32[768,128]{1,0:T(8,128)S(1)}, f32[768,128]{1,0:T(8,128)S(1)}, u32[]{:S(2)}, u32[]{:S(2)}) %collective-permute-start.22) | collective-permute-done | bytes 393248 | tf_op jit(solution)/shard_map/ppermute | solution.py:408
  119.0 1.9 %shard_map.85 = (f32[1024,128]{1,0:T(8,128)S(1)}, f32[8,128]{1,0:T(8,128)S(1)}, f32[768,128]{1,0:T(8,128)S(1)}) custom-call(bf16[2048,3200]{1,0:T(8,128)(2,1)S(1)} %get-tuple-element.97.refs_0_.dense_ref, f32[384,128]{1,0:T(8,128)S(1)} %collective-permute-done.25.inner_ref, f32[384,128]{1,0:T(8,128)S(1)} %slice_add_fusion.22.mine_ref, ...), custom_call_target="tpu_custom_call" | custom-call | flops 1677721600 | bytes 6553600 | tf_op jit(solution)/shard_map/pallas_call | solution.py:252
  120.9 4.1 %collective-permute-done.27.outer_ref = f32[768,128]{1,0:T(8,128)S(1)} collective-permute-done((f32[768,128]{1,0:T(8,128)S(1)}, f32[768,128]{1,0:T(8,128)S(1)}, u32[]{:S(2)}, u32[]{:S(2)}) %collective-permute-start.27) | collective-permute-done | bytes 393248 | tf_op jit(solution)/shard_map/ppermute | solution.py:408
  128.9 1.5 shard_map.88
  131.9 5.4 %collective-permute-done.31 = f32[520,128]{1,0:T(8,128)S(1)} collective-permute-done((f32[520,128]{1,0:T(8,128)S(1)}, f32[520,128]{1,0:T(8,128)S(1)}, u32[]{:S(2)}, u32[]{:S(2)}) %collective-permute-start.31) | collective-permute-done | bytes 266272 | tf_op jit(solution)/shard_map/ppermute | solution.py:411
  139.0 1.5 shard_map.90
  142.9 2.1 %collective-permute-done.32 = f32[392,128]{1,0:T(8,128)S(1)} collective-permute-done((f32[392,128]{1,0:T(8,128)S(1)}, f32[392,128]{1,0:T(8,128)S(1)}, u32[]{:S(2)}, u32[]{:S(2)}) %collective-permute-start.32) | collective-permute-done | bytes 200736 | tf_op jit(solution)/shard_map/ppermute | solution.py:408
  145.2 3.1 %collective-permute-done.35 = f32[776,128]{1,0:T(8,128)S(1)} collective-permute-done((f32[776,128]{1,0:T(8,128)S(1)}, f32[776,128]{1,0:T(8,128)S(1)}, u32[]{:S(2)}, u32[]{:S(2)}) %collective-permute-start.35) | collective-permute-done | bytes 397344 | tf_op jit(solution)/shard_map/ppermute | solution.py:408
  148.4 1.5 collective-permute-start.36
  149.9 5.4 %collective-permute-done.34 = f32[392,128]{1,0:T(8,128)S(1)} collective-permute-done((f32[392,128]{1,0:T(8,128)S(1)}, f32[392,128]{1,0:T(8,128)S(1)}, u32[]{:S(2)}, u32[]{:S(2)}) %collective-permute-start.34) | collective-permute-done | bytes 200736 | tf_op jit(solution)/shard_map/ppermute | solution.py:408
  156.7 1.5 collective-permute-start.37
  158.2 5.1 %collective-permute-done.38.refs_1_ = f32[384,128]{1,0:T(8,128)S(1)} collective-permute-done((f32[384,128]{1,0:T(8,128)S(1)}, f32[384,128]{1,0:T(8,128)S(1)}, u32[]{:S(2)}, u32[]{:S(2)}) %collective-permute-start.38) | collective-permute-done | bytes 196640 | tf_op jit(solution)/shard_map/ppermute | solution.py:408
  163.3 3.3 %collective-permute-done.37 = f32[392,128]{1,0:T(8,128)S(1)} collective-permute-done((f32[392,128]{1,0:T(8,128)S(1)}, f32[392,128]{1,0:T(8,128)S(1)}, u32[]{:S(2)}, u32[]{:S(2)}) %collective-permute-start.37) | collective-permute-done | bytes 200736 | tf_op jit(solution)/shard_map/ppermute | solution.py:408
  166.7 2.1 %collective-permute-start.39 = (f32[768,128]{1,0:T(8,128)S(1)}, f32[768,128]{1,0:T(8,128)S(1)}, u32[]{:S(2)}, u32[]{:S(2)}) collective-permute-start(f32[768,128]{1,0:T(8,128)S(1)} %pad_maximum_fusion.4), channel_id=1, source_target_pairs={{0,4},{1,9},{2,6},{3,11},{4,0},{5,13},{6,2},{7,15},{8,12},{9,1},{1... | collective-permute-start | bytes 1179656 | tf_op jit(solution)/shard_map/ppermute | solution.py:408
  168.8 5.0 %collective-permute-done.40.refs_11_ = f32[384,128]{1,0:T(8,128)S(1)} collective-permute-done((f32[384,128]{1,0:T(8,128)S(1)}, f32[384,128]{1,0:T(8,128)S(1)}, u32[]{:S(2)}, u32[]{:S(2)}) %collective-permute-start.40) | collective-permute-done | bytes 196640 | tf_op jit(solution)/shard_map/ppermute | solution.py:408
  173.9 2.7 %collective-permute-start.41 = (f32[768,128]{1,0:T(8,128)S(1)}, f32[768,128]{1,0:T(8,128)S(1)}, u32[]{:S(2)}, u32[]{:S(2)}) collective-permute-start(f32[768,128]{1,0:T(8,128)S(1)} %pad_maximum_fusion.5), channel_id=1, source_target_pairs={{0,4},{1,9},{2,6},{3,11},{4,0},{5,13},{6,2},{7,15},{8,12},{9,1},{1... | collective-permute-start | bytes 1179656 | tf_op jit(solution)/shard_map/ppermute | solution.py:408
  176.6 1.7 shard_map.92
  178.9 3.5 %collective-permute-done.41.refs_10_ = f32[768,128]{1,0:T(8,128)S(1)} collective-permute-done((f32[768,128]{1,0:T(8,128)S(1)}, f32[768,128]{1,0:T(8,128)S(1)}, u32[]{:S(2)}, u32[]{:S(2)}) %collective-permute-start.41) | collective-permute-done | bytes 393248 | tf_op jit(solution)/shard_map/ppermute | solution.py:408
  182.4 1.7 shard_map.93
  (145 shorter events, 36.8 us)
Async XLA Ops:
  8.0 7.9 %collective-permute-start = (f32[776,128]{1,0:T(8,128)S(1)}, f32[776,128]{1,0:T(8,128)S(1)}, u32[]{:S(2)}, u32[]{:S(2)}) collective-permute-start(f32[776,128]{1,0:T(8,128)S(1)} %get-tuple-element.100), channel_id=1, source_target_pairs={{0,4},{1,9},{2,6},{3,11},{4,0},{5,13},{6,2},{7,15},{8,12},{9,1},{1... | collective-permute-start | bytes 1191944 | tf_op jit(solution)/shard_map/ppermute | solution.py:408
  16.0 8.2 %collective-permute-start.1 = (f32[392,128]{1,0:T(8,128)S(1)}, f32[392,128]{1,0:T(8,128)S(1)}, u32[]{:S(2)}, u32[]{:S(2)}) collective-permute-start(f32[392,128]{1,0:T(8,128)S(1)} %pad_maximum_fusion.10), channel_id=1, source_target_pairs={{0,8},{1,5},{2,10},{3,7},{4,12},{5,1},{6,14},{7,3},{8,0},{9,13},{1... | collective-permute-start | bytes 602120 | tf_op jit(solution)/shard_map/ppermute | solution.py:408
  20.3 7.9 %collective-permute-start.3 = (f32[776,128]{1,0:T(8,128)S(1)}, f32[776,128]{1,0:T(8,128)S(1)}, u32[]{:S(2)}, u32[]{:S(2)}) collective-permute-start(f32[776,128]{1,0:T(8,128)S(1)} %get-tuple-element.104), channel_id=1, source_target_pairs={{0,4},{1,9},{2,6},{3,11},{4,0},{5,13},{6,2},{7,15},{8,12},{9,1},{1... | collective-permute-start | bytes 1191944 | tf_op jit(solution)/shard_map/ppermute | solution.py:408
  24.2 10.3 %collective-permute-start.2 = (f32[392,128]{1,0:T(8,128)S(1)}, f32[392,128]{1,0:T(8,128)S(1)}, u32[]{:S(2)}, u32[]{:S(2)}) collective-permute-start(f32[392,128]{1,0:T(8,128)S(1)} %pad_maximum_fusion.11), channel_id=1, source_target_pairs={{0,16},{1,17},{2,18},{3,19},{4,20},{5,21},{6,22},{7,23},{8,24},{9,... | collective-permute-start | bytes 602120 | tf_op jit(solution)/shard_map/ppermute | solution.py:408
  28.3 7.5 %collective-permute-start.5 = (f32[392,128]{1,0:T(8,128)S(1)}, f32[392,128]{1,0:T(8,128)S(1)}, u32[]{:S(2)}, u32[]{:S(2)}) collective-permute-start(f32[392,128]{1,0:T(8,128)S(1)} %pad_maximum_fusion.12), channel_id=1, source_target_pairs={{0,8},{1,5},{2,10},{3,7},{4,12},{5,1},{6,14},{7,3},{8,0},{9,13},{1... | collective-permute-start | bytes 602120 | tf_op jit(solution)/shard_map/ppermute | solution.py:408
  34.6 11.6 %collective-permute-start.4 = (f32[384,128]{1,0:T(8,128)S(1)}, f32[384,128]{1,0:T(8,128)S(1)}, u32[]{:S(2)}, u32[]{:S(2)}) collective-permute-start(f32[384,128]{1,0:T(8,128)S(1)} %slice_add_fusion.25.mine_ref), channel_id=1, source_target_pairs={{0,8},{1,5},{2,10},{3,7},{4,12},{5,1},{6,14},{7,3},{8,0},{9,13},{1... | collective-permute-start | bytes 589832 | tf_op jit(solution)/shard_map/ppermute | solution.py:408
  35.9 11.9 %collective-permute-start.7 = (f32[392,128]{1,0:T(8,128)S(1)}, f32[392,128]{1,0:T(8,128)S(1)}, u32[]{:S(2)}, u32[]{:S(2)}) collective-permute-start(f32[392,128]{1,0:T(8,128)S(1)} %pad_maximum_fusion.13), channel_id=1, source_target_pairs={{0,16},{1,17},{2,18},{3,19},{4,20},{5,21},{6,22},{7,23},{8,24},{9,... | collective-permute-start | bytes 602120 | tf_op jit(solution)/shard_map/ppermute | solution.py:408
  46.2 7.8 %collective-permute-start.6 = (f32[768,128]{1,0:T(8,128)S(1)}, f32[768,128]{1,0:T(8,128)S(1)}, u32[]{:S(2)}, u32[]{:S(2)}) collective-permute-start(f32[768,128]{1,0:T(8,128)S(1)} %pad_maximum_fusion), channel_id=1, source_target_pairs={{0,4},{1,9},{2,6},{3,11},{4,0},{5,13},{6,2},{7,15},{8,12},{9,1},{1... | collective-permute-start | bytes 1179656 | tf_op jit(solution)/shard_map/ppermute | solution.py:408
  47.8 7.4 %collective-permute-start.8 = (f32[384,128]{1,0:T(8,128)S(1)}, f32[384,128]{1,0:T(8,128)S(1)}, u32[]{:S(2)}, u32[]{:S(2)}) collective-permute-start(f32[384,128]{1,0:T(8,128)S(1)} %slice_add_fusion.24.mine_ref), channel_id=1, source_target_pairs={{0,8},{1,5},{2,10},{3,7},{4,12},{5,1},{6,14},{7,3},{8,0},{9,13},{1... | collective-permute-start | bytes 589832 | tf_op jit(solution)/shard_map/ppermute | solution.py:408
  55.1 2.7 %collective-permute-start.9 = (f32[520,128]{1,0:T(8,128)S(1)}, f32[520,128]{1,0:T(8,128)S(1)}, u32[]{:S(2)}, u32[]{:S(2)}) collective-permute-start(f32[520,128]{1,0:T(8,128)S(1)} %get-tuple-element.119), channel_id=1, source_target_pairs={{0,1},{1,0},{2,3},{3,2},{4,5},{5,4},{6,7},{7,6},{8,9},{9,8},{10,11... | collective-permute-start | bytes 798728 | tf_op jit(solution)/shard_map/ppermute | solution.py:411
  55.3 7.8 %collective-permute-start.11 = (f32[768,128]{1,0:T(8,128)S(1)}, f32[768,128]{1,0:T(8,128)S(1)}, u32[]{:S(2)}, u32[]{:S(2)}) collective-permute-start(f32[768,128]{1,0:T(8,128)S(1)} %pad_maximum_fusion.1), channel_id=1, source_target_pairs={{0,4},{1,9},{2,6},{3,11},{4,0},{5,13},{6,2},{7,15},{8,12},{9,1},{1... | collective-permute-start | bytes 1179656 | tf_op jit(solution)/shard_map/ppermute | solution.py:408
  57.9 8.0 %collective-permute-start.10 = (f32[520,128]{1,0:T(8,128)S(1)}, f32[520,128]{1,0:T(8,128)S(1)}, u32[]{:S(2)}, u32[]{:S(2)}) collective-permute-start(f32[520,128]{1,0:T(8,128)S(1)} %pad_maximum_fusion.6), channel_id=1, source_target_pairs={{0,2},{1,3},{2,0},{3,1},{4,6},{5,7},{6,4},{7,5},{8,10},{9,11},{10,... | collective-permute-start | bytes 798728 | tf_op jit(solution)/shard_map/ppermute | solution.py:411
  64.2 2.8 %collective-permute-start.13 = (f32[520,128]{1,0:T(8,128)S(1)}, f32[520,128]{1,0:T(8,128)S(1)}, u32[]{:S(2)}, u32[]{:S(2)}) collective-permute-start(f32[520,128]{1,0:T(8,128)S(1)} %get-tuple-element.127), channel_id=1, source_target_pairs={{0,1},{1,0},{2,3},{3,2},{4,5},{5,4},{6,7},{7,6},{8,9},{9,8},{10,11... | collective-permute-start | bytes 798728 | tf_op jit(solution)/shard_map/ppermute | solution.py:411
  65.9 3.0 %collective-permute-start.12 = (f32[512,128]{1,0:T(8,128)S(1)}, f32[512,128]{1,0:T(8,128)S(1)}, u32[]{:S(2)}, u32[]{:S(2)}) collective-permute-start(f32[512,128]{1,0:T(8,128)S(1)} %slice_add_fusion.12.refs_2_), channel_id=1, source_target_pairs={{0,1},{1,0},{2,3},{3,2},{4,5},{5,4},{6,7},{7,6},{8,9},{9,8},{10,11... | collective-permute-start | bytes 786440 | tf_op jit(solution)/shard_map/ppermute | solution.py:411
  67.1 8.9 %collective-permute-start.15 = (f32[520,128]{1,0:T(8,128)S(1)}, f32[520,128]{1,0:T(8,128)S(1)}, u32[]{:S(2)}, u32[]{:S(2)}) collective-permute-start(f32[520,128]{1,0:T(8,128)S(1)} %pad_maximum_fusion.7), channel_id=1, source_target_pairs={{0,2},{1,3},{2,0},{3,1},{4,6},{5,7},{6,4},{7,5},{8,10},{9,11},{10,... | collective-permute-start | bytes 798728 | tf_op jit(solution)/shard_map/ppermute | solution.py:411
  70.4 7.9 %collective-permute-start.14 = (f32[776,128]{1,0:T(8,128)S(1)}, f32[776,128]{1,0:T(8,128)S(1)}, u32[]{:S(2)}, u32[]{:S(2)}) collective-permute-start(f32[776,128]{1,0:T(8,128)S(1)} %get-tuple-element.134), channel_id=1, source_target_pairs={{0,4},{1,9},{2,6},{3,11},{4,0},{5,13},{6,2},{7,15},{8,12},{9,1},{1... | collective-permute-start | bytes 1191944 | tf_op jit(solution)/shard_map/ppermute | solution.py:408
  76.0 4.1 %collective-permute-start.17 = (f32[512,128]{1,0:T(8,128)S(1)}, f32[512,128]{1,0:T(8,128)S(1)}, u32[]{:S(2)}, u32[]{:S(2)}) collective-permute-start(f32[512,128]{1,0:T(8,128)S(1)} %slice_add_fusion.10.refs_2_), channel_id=1, source_target_pairs={{0,1},{1,0},{2,3},{3,2},{4,5},{5,4},{6,7},{7,6},{8,9},{9,8},{10,11... | collective-permute-start | bytes 786440 | tf_op jit(solution)/shard_map/ppermute | solution.py:411
  78.4 6.8 %collective-permute-start.16 = (f32[392,128]{1,0:T(8,128)S(1)}, f32[392,128]{1,0:T(8,128)S(1)}, u32[]{:S(2)}, u32[]{:S(2)}) collective-permute-start(f32[392,128]{1,0:T(8,128)S(1)} %pad_maximum_fusion.14), channel_id=1, source_target_pairs={{0,8},{1,5},{2,10},{3,7},{4,12},{5,1},{6,14},{7,3},{8,0},{9,13},{1... | collective-permute-start | bytes 602120 | tf_op jit(solution)/shard_map/ppermute | solution.py:408
  81.7 7.9 %collective-permute-start.19 = (f32[776,128]{1,0:T(8,128)S(1)}, f32[776,128]{1,0:T(8,128)S(1)}, u32[]{:S(2)}, u32[]{:S(2)}) collective-permute-start(f32[776,128]{1,0:T(8,128)S(1)} %get-tuple-element.138), channel_id=1, source_target_pairs={{0,4},{1,9},{2,6},{3,11},{4,0},{5,13},{6,2},{7,15},{8,12},{9,1},{1... | collective-permute-start | bytes 1191944 | tf_op jit(solution)/shard_map/ppermute | solution.py:408
  85.2 11.1 %collective-permute-start.18 = (f32[392,128]{1,0:T(8,128)S(1)}, f32[392,128]{1,0:T(8,128)S(1)}, u32[]{:S(2)}, u32[]{:S(2)}) collective-permute-start(f32[392,128]{1,0:T(8,128)S(1)} %pad_maximum_fusion.15), channel_id=1, source_target_pairs={{0,16},{1,17},{2,18},{3,19},{4,20},{5,21},{6,22},{7,23},{8,24},{9,... | collective-permute-start | bytes 602120 | tf_op jit(solution)/shard_map/ppermute | solution.py:408
  89.7 7.8 %collective-permute-start.21 = (f32[392,128]{1,0:T(8,128)S(1)}, f32[392,128]{1,0:T(8,128)S(1)}, u32[]{:S(2)}, u32[]{:S(2)}) collective-permute-start(f32[392,128]{1,0:T(8,128)S(1)} %pad_maximum_fusion.16), channel_id=1, source_target_pairs={{0,8},{1,5},{2,10},{3,7},{4,12},{5,1},{6,14},{7,3},{8,0},{9,13},{1... | collective-permute-start | bytes 602120 | tf_op jit(solution)/shard_map/ppermute | solution.py:408
  96.3 11.8 %collective-permute-start.20 = (f32[384,128]{1,0:T(8,128)S(1)}, f32[384,128]{1,0:T(8,128)S(1)}, u32[]{:S(2)}, u32[]{:S(2)}) collective-permute-start(f32[384,128]{1,0:T(8,128)S(1)} %slice_add_fusion.23.mine_ref), channel_id=1, source_target_pairs={{0,8},{1,5},{2,10},{3,7},{4,12},{5,1},{6,14},{7,3},{8,0},{9,13},{1... | collective-permute-start | bytes 589832 | tf_op jit(solution)/shard_map/ppermute | solution.py:408
  97.6 10.6 %collective-permute-start.23 = (f32[392,128]{1,0:T(8,128)S(1)}, f32[392,128]{1,0:T(8,128)S(1)}, u32[]{:S(2)}, u32[]{:S(2)}) collective-permute-start(f32[392,128]{1,0:T(8,128)S(1)} %pad_maximum_fusion.17), channel_id=1, source_target_pairs={{0,16},{1,17},{2,18},{3,19},{4,20},{5,21},{6,22},{7,23},{8,24},{9,... | collective-permute-start | bytes 602120 | tf_op jit(solution)/shard_map/ppermute | solution.py:408
  108.1 7.8 %collective-permute-start.22 = (f32[768,128]{1,0:T(8,128)S(1)}, f32[768,128]{1,0:T(8,128)S(1)}, u32[]{:S(2)}, u32[]{:S(2)}) collective-permute-start(f32[768,128]{1,0:T(8,128)S(1)} %pad_maximum_fusion.2), channel_id=1, source_target_pairs={{0,4},{1,9},{2,6},{3,11},{4,0},{5,13},{6,2},{7,15},{8,12},{9,1},{1... | collective-permute-start | bytes 1179656 | tf_op jit(solution)/shard_map/ppermute | solution.py:408
  108.3 8.9 %collective-permute-start.25 = (f32[384,128]{1,0:T(8,128)S(1)}, f32[384,128]{1,0:T(8,128)S(1)}, u32[]{:S(2)}, u32[]{:S(2)}) collective-permute-start(f32[384,128]{1,0:T(8,128)S(1)} %slice_add_fusion.22.mine_ref), channel_id=1, source_target_pairs={{0,8},{1,5},{2,10},{3,7},{4,12},{5,1},{6,14},{7,3},{8,0},{9,13},{1... | collective-permute-start | bytes 589832 | tf_op jit(solution)/shard_map/ppermute | solution.py:408
  117.1 1.6 collective-permute-start.24
  117.2 7.8 %collective-permute-start.27 = (f32[768,128]{1,0:T(8,128)S(1)}, f32[768,128]{1,0:T(8,128)S(1)}, u32[]{:S(2)}, u32[]{:S(2)}) collective-permute-start(f32[768,128]{1,0:T(8,128)S(1)} %pad_maximum_fusion.3), channel_id=1, source_target_pairs={{0,4},{1,9},{2,6},{3,11},{4,0},{5,13},{6,2},{7,15},{8,12},{9,1},{1... | collective-permute-start | bytes 1179656 | tf_op jit(solution)/shard_map/ppermute | solution.py:408
  118.8 8.5 %collective-permute-start.26 = (f32[520,128]{1,0:T(8,128)S(1)}, f32[520,128]{1,0:T(8,128)S(1)}, u32[]{:S(2)}, u32[]{:S(2)}) collective-permute-start(f32[520,128]{1,0:T(8,128)S(1)} %pad_maximum_fusion.8), channel_id=1, source_target_pairs={{0,2},{1,3},{2,0},{3,1},{4,6},{5,7},{6,4},{7,5},{8,10},{9,11},{10,... | collective-permute-start | bytes 798728 | tf_op jit(solution)/shard_map/ppermute | solution.py:411
  126.1 2.2 %collective-permute-start.29 = (f32[520,128]{1,0:T(8,128)S(1)}, f32[520,128]{1,0:T(8,128)S(1)}, u32[]{:S(2)}, u32[]{:S(2)}) collective-permute-start(f32[520,128]{1,0:T(8,128)S(1)} %get-tuple-element.163), channel_id=1, source_target_pairs={{0,1},{1,0},{2,3},{3,2},{4,5},{5,4},{6,7},{7,6},{8,9},{9,8},{10,11... | collective-permute-start | bytes 798728 | tf_op jit(solution)/shard_map/ppermute | solution.py:411
  127.3 1.6 collective-permute-start.28
  128.5 8.9 %collective-permute-start.31 = (f32[520,128]{1,0:T(8,128)S(1)}, f32[520,128]{1,0:T(8,128)S(1)}, u32[]{:S(2)}, u32[]{:S(2)}) collective-permute-start(f32[520,128]{1,0:T(8,128)S(1)} %pad_maximum_fusion.9), channel_id=1, source_target_pairs={{0,2},{1,3},{2,0},{3,1},{4,6},{5,7},{6,4},{7,5},{8,10},{9,11},{10,... | collective-permute-start | bytes 798728 | tf_op jit(solution)/shard_map/ppermute | solution.py:411
  130.4 7.8 %collective-permute-start.30 = (f32[776,128]{1,0:T(8,128)S(1)}, f32[776,128]{1,0:T(8,128)S(1)}, u32[]{:S(2)}, u32[]{:S(2)}) collective-permute-start(f32[776,128]{1,0:T(8,128)S(1)} %get-tuple-element.170), channel_id=1, source_target_pairs={{0,4},{1,9},{2,6},{3,11},{4,0},{5,13},{6,2},{7,15},{8,12},{9,1},{1... | collective-permute-start | bytes 1191944 | tf_op jit(solution)/shard_map/ppermute | solution.py:408
  137.4 1.6 collective-permute-start.33
  138.3 6.7 %collective-permute-start.32 = (f32[392,128]{1,0:T(8,128)S(1)}, f32[392,128]{1,0:T(8,128)S(1)}, u32[]{:S(2)}, u32[]{:S(2)}) collective-permute-start(f32[392,128]{1,0:T(8,128)S(1)} %pad_maximum_fusion.18), channel_id=1, source_target_pairs={{0,8},{1,5},{2,10},{3,7},{4,12},{5,1},{6,14},{7,3},{8,0},{9,13},{1... | collective-permute-start | bytes 602120 | tf_op jit(solution)/shard_map/ppermute | solution.py:408
  140.5 7.8 %collective-permute-start.35 = (f32[776,128]{1,0:T(8,128)S(1)}, f32[776,128]{1,0:T(8,128)S(1)}, u32[]{:S(2)}, u32[]{:S(2)}) collective-permute-start(f32[776,128]{1,0:T(8,128)S(1)} %get-tuple-element.176), channel_id=1, source_target_pairs={{0,4},{1,9},{2,6},{3,11},{4,0},{5,13},{6,2},{7,15},{8,12},{9,1},{1... | collective-permute-start | bytes 1191944 | tf_op jit(solution)/shard_map/ppermute | solution.py:408
  145.0 10.3 %collective-permute-start.34 = (f32[392,128]{1,0:T(8,128)S(1)}, f32[392,128]{1,0:T(8,128)S(1)}, u32[]{:S(2)}, u32[]{:S(2)}) collective-permute-start(f32[392,128]{1,0:T(8,128)S(1)} %pad_maximum_fusion.19), channel_id=1, source_target_pairs={{0,16},{1,17},{2,18},{3,19},{4,20},{5,21},{6,22},{7,23},{8,24},{9,... | collective-permute-start | bytes 602120 | tf_op jit(solution)/shard_map/ppermute | solution.py:408
  148.4 8.2 %collective-permute-start.36 = (f32[392,128]{1,0:T(8,128)S(1)}, f32[392,128]{1,0:T(8,128)S(1)}, u32[]{:S(2)}, u32[]{:S(2)}) collective-permute-start(f32[392,128]{1,0:T(8,128)S(1)} %pad_maximum_fusion.20), channel_id=1, source_target_pairs={{0,8},{1,5},{2,10},{3,7},{4,12},{5,1},{6,14},{7,3},{8,0},{9,13},{1... | collective-permute-start | bytes 602120 | tf_op jit(solution)/shard_map/ppermute | solution.py:408
  155.4 7.9 %collective-permute-start.38 = (f32[384,128]{1,0:T(8,128)S(1)}, f32[384,128]{1,0:T(8,128)S(1)}, u32[]{:S(2)}, u32[]{:S(2)}) collective-permute-start(f32[384,128]{1,0:T(8,128)S(1)} %slice_add_fusion.21.refs_2_), channel_id=1, source_target_pairs={{0,8},{1,5},{2,10},{3,7},{4,12},{5,1},{6,14},{7,3},{8,0},{9,13},{1... | collective-permute-start | bytes 589832 | tf_op jit(solution)/shard_map/ppermute | solution.py:408
  156.7 9.9 %collective-permute-start.37 = (f32[392,128]{1,0:T(8,128)S(1)}, f32[392,128]{1,0:T(8,128)S(1)}, u32[]{:S(2)}, u32[]{:S(2)}) collective-permute-start(f32[392,128]{1,0:T(8,128)S(1)} %pad_maximum_fusion.21), channel_id=1, source_target_pairs={{0,16},{1,17},{2,18},{3,19},{4,20},{5,21},{6,22},{7,23},{8,24},{9,... | collective-permute-start | bytes 602120 | tf_op jit(solution)/shard_map/ppermute | solution.py:408
  166.6 7.2 %collective-permute-start.40 = (f32[384,128]{1,0:T(8,128)S(1)}, f32[384,128]{1,0:T(8,128)S(1)}, u32[]{:S(2)}, u32[]{:S(2)}) collective-permute-start(f32[384,128]{1,0:T(8,128)S(1)} %slice_add_fusion.20.refs_12_), channel_id=1, source_target_pairs={{0,8},{1,5},{2,10},{3,7},{4,12},{5,1},{6,14},{7,3},{8,0},{9,13},{1... | collective-permute-start | bytes 589832 | tf_op jit(solution)/shard_map/ppermute | solution.py:408
  166.7 12.1 %collective-permute-start.39 = (f32[768,128]{1,0:T(8,128)S(1)}, f32[768,128]{1,0:T(8,128)S(1)}, u32[]{:S(2)}, u32[]{:S(2)}) collective-permute-start(f32[768,128]{1,0:T(8,128)S(1)} %pad_maximum_fusion.4), channel_id=1, source_target_pairs={{0,4},{1,9},{2,6},{3,11},{4,0},{5,13},{6,2},{7,15},{8,12},{9,1},{1... | collective-permute-start | bytes 1179656 | tf_op jit(solution)/shard_map/ppermute | solution.py:408
  173.9 8.5 %collective-permute-start.41 = (f32[768,128]{1,0:T(8,128)S(1)}, f32[768,128]{1,0:T(8,128)S(1)}, u32[]{:S(2)}, u32[]{:S(2)}) collective-permute-start(f32[768,128]{1,0:T(8,128)S(1)} %pad_maximum_fusion.5), channel_id=1, source_target_pairs={{0,4},{1,9},{2,6},{3,11},{4,0},{5,13},{6,2},{7,15},{8,12},{9,1},{1... | collective-permute-start | bytes 1179656 | tf_op jit(solution)/shard_map/ppermute | solution.py:408

commit v17 on v16

--- a/solution.py
+++ b/solution.py
@@ -13,6 +13,7 @@
 PAIR = 2 * TILE
 UNITS = 4
 NORM_ROWS = 8
+UNIT_ORDERS = ((0, 1, 2, 3), (0, 2, 1, 3))
 BEHIND = 0
 
 tiny_eps = 1e-06
@@ -160,18 +161,20 @@
                 position += 1
 
 
-def back_pairs(dense_ref, turned_ref, out_ref, start):
-    for pair in range(out_ref.shape[0] // TILE):
+def back_pairs(dense_ref, turned_ref, out_ref, units):
+    pairs = CB_DEV // 2 // UNITS
+    for pair in range(pairs * len(units)):
+        column = units[pair // pairs] * pairs + pair % pairs
         product = jnp.dot(
             turned_ref[...],
-            dense_ref[:, rows_of(start + pair, PAIR)],
+            dense_ref[:, rows_of(column, PAIR)],
             preferred_element_type=jnp.float32,
         )
         stacked = jnp.concatenate([product[:, :TILE], product[:, TILE:]], axis=0)
         out_ref[rows_of(pair), :] = stacked.T
 
 
-def back_send_kernel(first, *refs):
+def back_send_kernel(first, units, *refs):
     if first:
         dense_ref, own_ref, send_ref, turned_ref = refs
         parts, raw_ref, scales = [(own_ref, 2)], None, (None, None, None)
@@ -188,22 +191,30 @@
         if squares is not None:
             sums.append(squares)
     send_ref[-NORM_ROWS:, :] = jnp.broadcast_to(squares_row(sums), (NORM_ROWS, TILE))
-    back_pairs(dense_ref, turned_ref, send_ref, 0)
-
-
-def back_keep_kernel(dense_ref, turned_ref, keep_ref):
-    back_pairs(dense_ref, turned_ref, keep_ref, keep_ref.shape[0] // TILE)
-
-
-def fore_pairs(dense_ref, cells, wide_ref, add_ref, out_ref, start):
+    back_pairs(dense_ref, turned_ref, send_ref, units)
+
+
+def back_keep_kernel(units, dense_ref, turned_ref, keep_ref):
+    back_pairs(dense_ref, turned_ref, keep_ref, units)
+
+
+def fore_pairs(dense_ref, units, wide_ref, add_ref, out_ref, start):
+    depth = wide_ref.shape[0] // len(units)
+    runs = [(unit * depth, i * depth, depth) for i, unit in enumerate(units)]
+    if units[1] == units[0] + 1:
+        runs = [(units[0] * depth, 0, 2 * depth)]
     low = low_lanes((TILE, TILE))
     step = 2
     pairs = out_ref.shape[0] // TILE
     for pair in range(0, pairs, step):
-        product = jnp.dot(
-            dense_ref[(start + pair) * PAIR : (start + pair + step) * PAIR, cells],
-            wide_ref[...],
-            preferred_element_type=jnp.float32,
+        rows = slice((start + pair) * PAIR, (start + pair + step) * PAIR)
+        product = sum(
+            jnp.dot(
+                dense_ref[rows, cell : cell + size],
+                wide_ref[row : row + size, :],
+                preferred_element_type=jnp.float32,
+            )
+            for cell, row, size in runs
         )
         for i in range(step):
             even, odd = product[rows_of(2 * i), :], product[rows_of(2 * i + 1), :]
@@ -225,27 +236,26 @@
     return sums[0] + sums[1]
 
 
-def fore_own_kernel(first, dense_ref, inner_ref, mine_ref, scale_ref, *refs):
+def fore_own_kernel(first, units, dense_ref, inner_ref, mine_ref, scale_ref, *refs):
     past_ref, past_scale_ref = (None, None) if first else refs[:2]
     part_ref, sum_ref, raw_ref, wide_ref = refs[-4:]
     parts = [(inner_ref, 1), (mine_ref, 1)]
     sum_ref[...] = fore_vector(parts, wide_ref, raw_ref, (scale_ref, past_ref, past_scale_ref))
-    depth = wide_ref.shape[0]
-    fore_pairs(dense_ref, slice(depth, 2 * depth), wide_ref, None, part_ref, 0)
-
-
-def fore_send_kernel(first, dense_ref, outer_ref, part_ref, sum_ref, scale_ref, *refs):
+    fore_pairs(dense_ref, units, wide_ref, None, part_ref, 0)
+
+
+def fore_send_kernel(first, units, dense_ref, outer_ref, part_ref, sum_ref, scale_ref, *refs):
     past_ref, past_scale_ref = (None, None) if first else refs[:2]
     send_ref, wide_ref, raw_ref = refs[-3:]
     squares = fore_vector([(outer_ref, 2)], wide_ref, raw_ref, (scale_ref, past_ref, past_scale_ref))
     row = squares_row([squares, sum_ref[...]])
     send_ref[-NORM_ROWS:, :] = jnp.broadcast_to(row, (NORM_ROWS, TILE))
-    fore_pairs(dense_ref, slice(0, wide_ref.shape[0]), wide_ref, part_ref, send_ref, 0)
-
-
-def fore_keep_kernel(dense_ref, wide_ref, part_ref, keep_ref):
+    fore_pairs(dense_ref, units, wide_ref, part_ref, send_ref, 0)
+
+
+def fore_keep_kernel(units, dense_ref, wide_ref, part_ref, keep_ref):
     start = keep_ref.shape[0] // TILE
-    fore_pairs(dense_ref, slice(0, wide_ref.shape[0]), wide_ref, part_ref, keep_ref, start)
+    fore_pairs(dense_ref, units, wide_ref, part_ref, keep_ref, start)
 
 
 def product_call(body, dense, operands, shapes, scratch=()):
@@ -266,23 +276,24 @@
     return jax.ShapeDtypeStruct((rows, TILE), jnp.float32)
 
 
-def back_product(dense, operands, first):
+def back_product(order, dense, operands, first):
     rows, cells = dense.shape[0], CB_DEV * TILE
     shapes = [float_rows(cells // 4 + NORM_ROWS), jax.ShapeDtypeStruct((TILE // 2, rows), dense.dtype)]
     shapes += [] if first else [float_rows(rows // 2)]
     send, flat, *raw = product_call(
-        functools.partial(back_send_kernel, first), dense, operands, shapes
-    )
-
-
-    (keep,) = product_call(back_keep_kernel, dense, [flat], [float_rows(cells // 4)])
+        functools.partial(back_send_kernel, first, order[:2]), dense, operands, shapes
+    )
+
+
+    body = functools.partial(back_keep_kernel, order[2:])
+    (keep,) = product_call(body, dense, [flat], [float_rows(cells // 4)])
     return send, keep, *raw
 
 
-def fore_own_product(dense, operands, first):
+def fore_own_product(order, dense, operands, first):
     rows, cells = dense.shape[0], CB_DEV * TILE
     return product_call(
-        functools.partial(fore_own_kernel, first),
+        functools.partial(fore_own_kernel, first, order[2:]),
         dense,
         operands,
         [float_rows(rows // 2), float_rows(NORM_ROWS), float_rows(cells // 4)],
@@ -290,7 +301,7 @@
     )
 
 
-def fore_product(dense, operands, first):
+def fore_product(order, dense, operands, first):
     rows, cells = dense.shape[0], CB_DEV * TILE
     shapes = [
         float_rows(rows // 4 + NORM_ROWS),
@@ -298,11 +309,12 @@
         float_rows(cells // 4),
     ]
     send, wide, raw = product_call(
-        functools.partial(fore_send_kernel, first), dense, operands, shapes
+        functools.partial(fore_send_kernel, first, order[:2]), dense, operands, shapes
     )
 
     def keep(wide):
-        return product_call(fore_keep_kernel, dense, [wide, operands[1]], [float_rows(rows // 4)])[0]
+        body = functools.partial(fore_keep_kernel, order[:2])
+        return product_call(body, dense, [wide, operands[1]], [float_rows(rows // 4)])[0]
 
     return send, (keep, wide), raw
 
@@ -341,16 +353,17 @@
     chains = [ins[: len(ins) // 2], ins[len(ins) // 2 :]]
     low = low_lanes((TILE, TILE))
     rotations = [rotation(refs_[2 * count :]) for refs_ in chains]
-    half = model_ref.shape[0] // PAIR // 2
     misfits = [jnp.broadcast_to(r[3], misfit_ref.shape) for r in rotations]
     misfit_ref[...] = jnp.where(low_lanes(misfit_ref.shape), misfits[0], misfits[1])
+    pairs = model_ref.shape[0] // PAIR // UNITS
     for pair in range(model_ref.shape[0] // PAIR):
         values = []
-        for refs_, (alphas, _, steps, _, _) in zip(chains, rotations):
+        for order, refs_, (alphas, _, steps, _, _) in zip(UNIT_ORDERS, chains, rotations):
+            slot = order.index(pair // pairs)
+            rows = rows_of(slot % 2 * pairs + pair % pairs)
             search = total = None
             for j in range(count):
-                right_ref = refs_[2 * j + pair // half]
-                right = right_ref[rows_of(pair % half), :] / alphas[j]
+                right = refs_[2 * j + slot // 2][rows, :] / alphas[j]
                 search = right if j == 0 else right - steps[j - 1][1] * search
                 total = steps[j][0] * search if j == 0 else total + steps[j][0] * search
             values.append(total)
@@ -373,8 +386,12 @@
         ]
         vectors.append([value for half in halves for _, value, _ in half])
         factors.append(rotation(norms)[-1])
-    for pair, (ours, theirs) in enumerate(zip(*vectors)):
-        values = [factors[0] * ours, factors[1] * theirs]
+    pairs = gradient_ref.shape[0] // PAIR // UNITS
+    for pair in range(gradient_ref.shape[0] // PAIR):
+        values = []
+        for order, vector, factor in zip(UNIT_ORDERS, vectors, factors):
+            slot = order.index(pair // pairs)
+            values.append(factor * vector[slot * pairs + pair % pairs])
         store_in_order(gradient_ref, mask_ref[0], pair, low, values)
 
 
@@ -397,13 +414,15 @@
     row_index = lax.axis_index("rows")
     core = lax.axis_index("cols") & 1
 
-    orders = [row_bits, [row_bits[1], row_bits[0], *row_bits[2:]]]
-
-    def swap_rows(value, level):
+    near, far, *rest = row_bits
+    orders = [[near, far, *rest, far, near], [far, near, *rest, near, far]]
+    steps = len(orders[0])
+
+    def swap_rows(second, value, level):
         pairs = []
         for row in range(row_count):
             for col in range(col_count):
-                partner = row ^ (1 << orders[col & 1][level])
+                partner = row ^ (1 << orders[col & 1 ^ second][level])
                 pairs.append((row * col_count + col, partner * col_count + col))
         return lax.ppermute(value, ("rows", "cols"), pairs)
 
@@ -429,7 +448,7 @@
         half, operand = kept
         return half(tied(operand, ahead))
 
-    def reduce_rows(send, keep):
+    def reduce_rows(swap_rows, send, keep):
         half = keep.shape[0]
         got, _ = yield swap_rows, send, 0
         keep = keep + got[:half]
@@ -439,8 +458,8 @@
             got, _ = yield swap_rows, jnp.concatenate([send, norm]), level
             norm = norm + got[half // 2 :]
             send = mine = mine + got[: half // 2]
-        inner, _ = yield swap_rows, mine, 1
-        outer, ahead = yield swap_rows, jnp.concatenate([inner, mine]), 0
+        inner, _ = yield swap_rows, mine, steps - 2
+        outer, ahead = yield swap_rows, jnp.concatenate([inner, mine]), steps - 1
         return [outer, inner, mine], norm, ahead
 
     def reduce_cols(send, kept):
@@ -455,9 +474,11 @@
         other, _ = yield swap_cols, own, 0
         return [other, own], norm
 
-    def chain(left):
-        send, keep = back_product(dense, [left], True)
-        totals, norm, ahead = yield from reduce_rows(send, keep)
+    def chain(second, left):
+        order = UNIT_ORDERS[second]
+        swap = functools.partial(swap_rows, second)
+        send, keep = back_product(order, dense, [left], True)
+        totals, norm, ahead = yield from reduce_rows(swap, send, keep)
         norms = [norm]
         rights = []
         for iteration in range(ITERS):
@@ -465,22 +486,22 @@
             pasts = [[right, norms[-2]] for right in rights[-1]] if rights else [[], []]
             own = [tied(own[0], ahead), own[1]]
             part, squares, own_right = fore_own_product(
-                dense, [*own, norms[-1], *pasts[1]], not rights
+                order, dense, [*own, norms[-1], *pasts[1]], not rights
             )
             send, keep, right = fore_product(
-                dense, [outer, part, squares, norms[-1], *pasts[0]], not rights
+                order, dense, [outer, part, squares, norms[-1], *pasts[0]], not rights
             )
             rights.append([right, own_right])
             halves, norm = yield from reduce_cols(send, keep)
             norms.append(norm)
             send, keep, left = back_product(
-                dense, [*halves, norms[-1], left, norms[-2]], False
+                order, dense, [*halves, norms[-1], left, norms[-2]], False
             )
-            totals, norm, ahead = yield from reduce_rows(send, keep)
+            totals, norm, ahead = yield from reduce_rows(swap, send, keep)
             norms.append(norm)
         return rights, norms, totals
 
-    runs = [chain(left) for left in lefts]
+    runs = [chain(second, left) for second, left in enumerate(lefts)]
     wanted = [next(run) for run in runs]
     chains = [None] * len(runs)
     gots = [None] * len(runs)

time: 184 us -> 184 us (level)
  starting transfers between devices: 38.4 us -> 44.3 us
  waiting for transfers between devices: 100 us -> 95.9 us
    ppermute x30, starting transfers between devices: 32.7 us -> 39.4 us  [swap_rows(): return lax.ppermute(value, ('rows', 'cols'), pairs)]
    ppermute x12, waiting for transfers between devices: 11.5 us -> 9.11 us  [swap_cols(): lax.ppermute(value, 'cols', [(i, i ^ 1 << level) for i in range(col_count)])]
    ppermute x30, waiting for transfers between devices: 89 us -> 86.8 us  [swap_rows(): return lax.ppermute(value, ('rows', 'cols'), pairs)]
  transfers between devices with their start and end apart: 42 -> 42, of which waited for: 32 -> 31; matrix products, arithmetic and copies ran while one was open for 1% -> 1% of each run, Pallas kernels for 18% -> 18%
where the time goes in v17:
time: 184 us; the launch traced here: 185 us
  waiting for transfers between devices  95.9 us (52%)
  starting transfers between devices  44.3 us (24%)
  Pallas kernels  41.5 us (23%)
    ppermute x30, waiting for transfers between devices, swap_rows(): return lax.ppermute(value, ('rows', 'cols'), pairs)  86.8 us
    ppermute x30, starting transfers between devices, swap_rows(): return lax.ppermute(value, ('rows', 'cols'), pairs)  39.4 us
    pallas_call x24, Pallas kernels, product_call(): pl.pallas_call(body, in_specs=[WHOLE] * (1 + len(operands)), out_specs=[W...  32.4 us
    ppermute x12, waiting for transfers between devices, swap_cols(): lax.ppermute(value, 'cols', [(i, i ^ 1 << level) for i in range(col_count)])  9.11 us
    pallas_call x1, Pallas kernels, fill_dense(): pl.pallas_call(fill_kernel, in_specs=[SCALARS] * 2 + [pl.BlockSpec(memory...  5.72 us
    ppermute x12, starting transfers between devices, swap_cols(): lax.ppermute(value, 'cols', [(i, i ^ 1 << level) for i in range(col_count)])  4.86 us
  transfers between devices with their start and end apart: 42, of which 31 were waited for; matrix products, arithmetic and copies ran while one was open for 1% of the time, Pallas kernels for 18%

profile of v17, /device:TPU:0, one launch (start us, length us, event | category | flops | bytes accessed | tf_op | source)
XLA Modules:
  0.0 185.2 jit_solution(13114997149146289331)
XLA Ops:
  0.7 5.7 %shard_map.67 = (bf16[2048,3200]{1,0:T(8,128)(2,1)S(1)}, f32[1024,128]{1,0:T(8,128)S(1)}, f32[1024,128]{1,0:T(8,128)S(1)}) custom-call(s32[24]{0:T(128)S(1)} %fusion.place_ref, s32[1]{0:T(128)} %bitcast.1.flip_ref, s32[16,16]{1,0:T(8,128)} %pattern_in.1, s32[16]{0:T(128)} %bitcast.5, f32[2048,128]{1,0:T(8,128)} %delays_in.1, bf16[16,16,128,128]{3,2,1,0:T(8,128)(2,1)} %tiles_in.1), custom_call_target="tpu_custom_call" | custom-call | bytes 8388608 | tf_op jit(solution)/shard_map/pallas_call | solution.py:107
  7.8 1.7 collective-permute-start
  12.2 3.5 %collective-permute-done = f32[776,128]{1,0:T(8,128)S(1)} collective-permute-done((f32[776,128]{1,0:T(8,128)S(1)}, f32[776,128]{1,0:T(8,128)S(1)}, u32[]{:S(2)}, u32[]{:S(2)}) %collective-permute-start) | collective-permute-done | bytes 397344 | tf_op jit(solution)/shard_map/ppermute | solution.py:427
  15.8 2.8 %collective-permute-start.1 = (f32[392,128]{1,0:T(8,128)S(1)}, f32[392,128]{1,0:T(8,128)S(1)}, u32[]{:S(2)}, u32[]{:S(2)}) collective-permute-start(f32[392,128]{1,0:T(8,128)S(1)} %pad_maximum_fusion.10), channel_id=1, source_target_pairs={{0,8},{1,5},{2,10},{3,7},{4,12},{5,1},{6,14},{7,3},{8,0},{9,13},{1... | collective-permute-start | bytes 602120 | tf_op jit(solution)/shard_map/ppermute | solution.py:427
  19.9 2.3 %collective-permute-done.1 = f32[392,128]{1,0:T(8,128)S(1)} collective-permute-done((f32[392,128]{1,0:T(8,128)S(1)}, f32[392,128]{1,0:T(8,128)S(1)}, u32[]{:S(2)}, u32[]{:S(2)}) %collective-permute-start.1) | collective-permute-done | bytes 200736 | tf_op jit(solution)/shard_map/ppermute | solution.py:427
  22.3 3.6 %collective-permute-start.2 = (f32[392,128]{1,0:T(8,128)S(1)}, f32[392,128]{1,0:T(8,128)S(1)}, u32[]{:S(2)}, u32[]{:S(2)}) collective-permute-start(f32[392,128]{1,0:T(8,128)S(1)} %pad_maximum_fusion.11), channel_id=1, source_target_pairs={{0,16},{1,17},{2,18},{3,19},{4,20},{5,21},{6,22},{7,23},{8,24},{9,... | collective-permute-start | bytes 602120 | tf_op jit(solution)/shard_map/ppermute | solution.py:427
  25.9 8.0 %collective-permute-done.3 = f32[776,128]{1,0:T(8,128)S(1)} collective-permute-done((f32[776,128]{1,0:T(8,128)S(1)}, f32[776,128]{1,0:T(8,128)S(1)}, u32[]{:S(2)}, u32[]{:S(2)}) %collective-permute-start.3) | collective-permute-done | bytes 397344 | tf_op jit(solution)/shard_map/ppermute | solution.py:427
  34.0 2.3 %collective-permute-start.5 = (f32[392,128]{1,0:T(8,128)S(1)}, f32[392,128]{1,0:T(8,128)S(1)}, u32[]{:S(2)}, u32[]{:S(2)}) collective-permute-start(f32[392,128]{1,0:T(8,128)S(1)} %pad_maximum_fusion.12), channel_id=1, source_target_pairs={{0,4},{1,9},{2,6},{3,11},{4,0},{5,13},{6,2},{7,15},{8,12},{9,1},{1... | collective-permute-start | bytes 602120 | tf_op jit(solution)/shard_map/ppermute | solution.py:427
  36.8 3.2 %collective-permute-done.5 = f32[392,128]{1,0:T(8,128)S(1)} collective-permute-done((f32[392,128]{1,0:T(8,128)S(1)}, f32[392,128]{1,0:T(8,128)S(1)}, u32[]{:S(2)}, u32[]{:S(2)}) %collective-permute-start.5) | collective-permute-done | bytes 200736 | tf_op jit(solution)/shard_map/ppermute | solution.py:427
  40.3 6.9 %collective-permute-done.4.inner_ref = f32[384,128]{1,0:T(8,128)S(1)} collective-permute-done((f32[384,128]{1,0:T(8,128)S(1)}, f32[384,128]{1,0:T(8,128)S(1)}, u32[]{:S(2)}, u32[]{:S(2)}) %collective-permute-start.4) | collective-permute-done | bytes 196640 | tf_op jit(solution)/shard_map/ppermute | solution.py:427
  48.7 2.0 %collective-permute-start.8 = (f32[384,128]{1,0:T(8,128)S(1)}, f32[384,128]{1,0:T(8,128)S(1)}, u32[]{:S(2)}, u32[]{:S(2)}) collective-permute-start(f32[384,128]{1,0:T(8,128)S(1)} %slice_add_fusion.24.mine_ref), channel_id=1, source_target_pairs={{0,4},{1,9},{2,6},{3,11},{4,0},{5,13},{6,2},{7,15},{8,12},{9,1},{1... | collective-permute-start | bytes 589832 | tf_op jit(solution)/shard_map/ppermute | solution.py:427
  50.7 1.9 %shard_map.72 = (f32[1024,128]{1,0:T(8,128)S(1)}, f32[8,128]{1,0:T(8,128)S(1)}, f32[768,128]{1,0:T(8,128)S(1)}) custom-call(bf16[2048,3200]{1,0:T(8,128)(2,1)S(1)} %get-tuple-element.97.refs_0_.dense_ref, f32[384,128]{1,0:T(8,128)S(1)} %collective-permute-done.4.inner_ref, f32[384,128]{1,0:T(8,128)S(1)} %slice_add_fusion.25.mine_ref, ...), custom_call_target="tpu_custom_call" | custom-call | flops 1677721600 | bytes 6553600 | tf_op jit(solution)/shard_map/pallas_call | solution.py:262
  52.6 2.4 %collective-permute-done.6.outer_ref = f32[768,128]{1,0:T(8,128)S(1)} collective-permute-done((f32[768,128]{1,0:T(8,128)S(1)}, f32[768,128]{1,0:T(8,128)S(1)}, u32[]{:S(2)}, u32[]{:S(2)}) %collective-permute-start.6) | collective-permute-done | bytes 393248 | tf_op jit(solution)/shard_map/ppermute | solution.py:427
  58.4 1.9 %shard_map.75 = (f32[1024,128]{1,0:T(8,128)S(1)}, f32[8,128]{1,0:T(8,128)S(1)}, f32[768,128]{1,0:T(8,128)S(1)}) custom-call(bf16[2048,3200]{1,0:T(8,128)(2,1)S(1)} %get-tuple-element.97.refs_0_.dense_ref, f32[384,128]{1,0:T(8,128)S(1)} %collective-permute-done.8.inner_ref, f32[384,128]{1,0:T(8,128)S(1)} %slice_add_fusion.24.mine_ref, ...), custom_call_target="tpu_custom_call" | custom-call | flops 1677721600 | bytes 6553600 | tf_op jit(solution)/shard_map/pallas_call | solution.py:262
  60.3 4.7 %collective-permute-done.11.outer_ref = f32[768,128]{1,0:T(8,128)S(1)} collective-permute-done((f32[768,128]{1,0:T(8,128)S(1)}, f32[768,128]{1,0:T(8,128)S(1)}, u32[]{:S(2)}, u32[]{:S(2)}) %collective-permute-start.11) | collective-permute-done | bytes 393248 | tf_op jit(solution)/shard_map/ppermute | solution.py:427
  69.5 1.5 collective-permute-start.14
  72.3 4.0 %collective-permute-done.15 = f32[520,128]{1,0:T(8,128)S(1)} collective-permute-done((f32[520,128]{1,0:T(8,128)S(1)}, f32[520,128]{1,0:T(8,128)S(1)}, u32[]{:S(2)}, u32[]{:S(2)}) %collective-permute-start.15) | collective-permute-done | bytes 266272 | tf_op jit(solution)/shard_map/ppermute | solution.py:430
  78.0 1.6 shard_map.80
  79.6 1.7 collective-permute-start.19
  83.4 1.5 collective-permute-start.18
  84.8 4.6 %collective-permute-done.19 = f32[776,128]{1,0:T(8,128)S(1)} collective-permute-done((f32[776,128]{1,0:T(8,128)S(1)}, f32[776,128]{1,0:T(8,128)S(1)}, u32[]{:S(2)}, u32[]{:S(2)}) %collective-permute-start.19) | collective-permute-done | bytes 397344 | tf_op jit(solution)/shard_map/ppermute | solution.py:427
  89.6 4.1 %collective-permute-start.21 = (f32[392,128]{1,0:T(8,128)S(1)}, f32[392,128]{1,0:T(8,128)S(1)}, u32[]{:S(2)}, u32[]{:S(2)}) collective-permute-start(f32[392,128]{1,0:T(8,128)S(1)} %pad_maximum_fusion.16), channel_id=1, source_target_pairs={{0,4},{1,9},{2,6},{3,11},{4,0},{5,13},{6,2},{7,15},{8,12},{9,1},{1... | collective-permute-start | bytes 602120 | tf_op jit(solution)/shard_map/ppermute | solution.py:427
  93.8 2.9 %collective-permute-start.20 = (f32[384,128]{1,0:T(8,128)S(1)}, f32[384,128]{1,0:T(8,128)S(1)}, u32[]{:S(2)}, u32[]{:S(2)}) collective-permute-start(f32[384,128]{1,0:T(8,128)S(1)} %slice_add_fusion.23.mine_ref), channel_id=1, source_target_pairs={{0,8},{1,5},{2,10},{3,7},{4,12},{5,1},{6,14},{7,3},{8,0},{9,13},{1... | collective-permute-start | bytes 589832 | tf_op jit(solution)/shard_map/ppermute | solution.py:427
  99.5 5.1 %collective-permute-done.20.inner_ref = f32[384,128]{1,0:T(8,128)S(1)} collective-permute-done((f32[384,128]{1,0:T(8,128)S(1)}, f32[384,128]{1,0:T(8,128)S(1)}, u32[]{:S(2)}, u32[]{:S(2)}) %collective-permute-start.20) | collective-permute-done | bytes 196640 | tf_op jit(solution)/shard_map/ppermute | solution.py:427
  104.6 3.6 %collective-permute-start.22 = (f32[768,128]{1,0:T(8,128)S(1)}, f32[768,128]{1,0:T(8,128)S(1)}, u32[]{:S(2)}, u32[]{:S(2)}) collective-permute-start(f32[768,128]{1,0:T(8,128)S(1)} %pad_maximum_fusion.2), channel_id=1, source_target_pairs={{0,4},{1,9},{2,6},{3,11},{4,0},{5,13},{6,2},{7,15},{8,12},{9,1},{1... | collective-permute-start | bytes 1179656 | tf_op jit(solution)/shard_map/ppermute | solution.py:427
  108.3 1.9 %shard_map.82 = (f32[1024,128]{1,0:T(8,128)S(1)}, f32[8,128]{1,0:T(8,128)S(1)}, f32[768,128]{1,0:T(8,128)S(1)}) custom-call(bf16[2048,3200]{1,0:T(8,128)(2,1)S(1)} %get-tuple-element.97.refs_0_.dense_ref, f32[384,128]{1,0:T(8,128)S(1)} %collective-permute-done.20.inner_ref, f32[384,128]{1,0:T(8,128)S(1)} %slice_add_fusion.23.mine_ref, ...), custom_call_target="tpu_custom_call" | custom-call | flops 1677721600 | bytes 6553600 | tf_op jit(solution)/shard_map/pallas_call | solution.py:262
  110.2 3.7 %collective-permute-done.22.outer_ref = f32[768,128]{1,0:T(8,128)S(1)} collective-permute-done((f32[768,128]{1,0:T(8,128)S(1)}, f32[768,128]{1,0:T(8,128)S(1)}, u32[]{:S(2)}, u32[]{:S(2)}) %collective-permute-start.22) | collective-permute-done | bytes 393248 | tf_op jit(solution)/shard_map/ppermute | solution.py:427
  117.2 2.2 %collective-permute-start.26 = (f32[520,128]{1,0:T(8,128)S(1)}, f32[520,128]{1,0:T(8,128)S(1)}, u32[]{:S(2)}, u32[]{:S(2)}) collective-permute-start(f32[520,128]{1,0:T(8,128)S(1)} %pad_maximum_fusion.8), channel_id=1, source_target_pairs={{0,2},{1,3},{2,0},{3,1},{4,6},{5,7},{6,4},{7,5},{8,10},{9,11},{10,... | collective-permute-start | bytes 798728 | tf_op jit(solution)/shard_map/ppermute | solution.py:430
  119.4 1.9 %shard_map.85 = (f32[1024,128]{1,0:T(8,128)S(1)}, f32[8,128]{1,0:T(8,128)S(1)}, f32[768,128]{1,0:T(8,128)S(1)}) custom-call(bf16[2048,3200]{1,0:T(8,128)(2,1)S(1)} %get-tuple-element.97.refs_0_.dense_ref, f32[384,128]{1,0:T(8,128)S(1)} %collective-permute-done.25.inner_ref, f32[384,128]{1,0:T(8,128)S(1)} %slice_add_fusion.22.mine_ref, ...), custom_call_target="tpu_custom_call" | custom-call | flops 1677721600 | bytes 6553600 | tf_op jit(solution)/shard_map/pallas_call | solution.py:262
  121.3 2.6 %collective-permute-done.27.outer_ref = f32[768,128]{1,0:T(8,128)S(1)} collective-permute-done((f32[768,128]{1,0:T(8,128)S(1)}, f32[768,128]{1,0:T(8,128)S(1)}, u32[]{:S(2)}, u32[]{:S(2)}) %collective-permute-start.27) | collective-permute-done | bytes 393248 | tf_op jit(solution)/shard_map/ppermute | solution.py:427
  127.7 1.5 collective-permute-start.31
  129.2 1.5 shard_map.88
  133.1 3.4 %collective-permute-done.31 = f32[520,128]{1,0:T(8,128)S(1)} collective-permute-done((f32[520,128]{1,0:T(8,128)S(1)}, f32[520,128]{1,0:T(8,128)S(1)}, u32[]{:S(2)}, u32[]{:S(2)}) %collective-permute-start.31) | collective-permute-done | bytes 266272 | tf_op jit(solution)/shard_map/ppermute | solution.py:430
  136.6 1.9 %collective-permute-done.30 = f32[776,128]{1,0:T(8,128)S(1)} collective-permute-done((f32[776,128]{1,0:T(8,128)S(1)}, f32[776,128]{1,0:T(8,128)S(1)}, u32[]{:S(2)}, u32[]{:S(2)}) %collective-permute-start.30) | collective-permute-done | bytes 397344 | tf_op jit(solution)/shard_map/ppermute | solution.py:427
  138.8 1.5 shard_map.90
  140.3 2.0 %collective-permute-start.35 = (f32[776,128]{1,0:T(8,128)S(1)}, f32[776,128]{1,0:T(8,128)S(1)}, u32[]{:S(2)}, u32[]{:S(2)}) collective-permute-start(f32[776,128]{1,0:T(8,128)S(1)} %get-tuple-element.176), channel_id=1, source_target_pairs={{0,8},{1,5},{2,10},{3,7},{4,12},{5,1},{6,14},{7,3},{8,0},{9,13},{1... | collective-permute-start | bytes 1191944 | tf_op jit(solution)/shard_map/ppermute | solution.py:427
  144.6 8.3 %collective-permute-done.35 = f32[776,128]{1,0:T(8,128)S(1)} collective-permute-done((f32[776,128]{1,0:T(8,128)S(1)}, f32[776,128]{1,0:T(8,128)S(1)}, u32[]{:S(2)}, u32[]{:S(2)}) %collective-permute-start.35) | collective-permute-done | bytes 397344 | tf_op jit(solution)/shard_map/ppermute | solution.py:427
  153.0 1.6 collective-permute-start.36
  154.6 1.8 collective-permute-start.38
  156.4 2.4 %collective-permute-done.36 = f32[392,128]{1,0:T(8,128)S(1)} collective-permute-done((f32[392,128]{1,0:T(8,128)S(1)}, f32[392,128]{1,0:T(8,128)S(1)}, u32[]{:S(2)}, u32[]{:S(2)}) %collective-permute-start.36) | collective-permute-done | bytes 200736 | tf_op jit(solution)/shard_map/ppermute | solution.py:427
  159.0 3.5 %collective-permute-done.38.refs_1_ = f32[384,128]{1,0:T(8,128)S(1)} collective-permute-done((f32[384,128]{1,0:T(8,128)S(1)}, f32[384,128]{1,0:T(8,128)S(1)}, u32[]{:S(2)}, u32[]{:S(2)}) %collective-permute-start.38) | collective-permute-done | bytes 196640 | tf_op jit(solution)/shard_map/ppermute | solution.py:427
  162.5 5.3 %collective-permute-done.37 = f32[392,128]{1,0:T(8,128)S(1)} collective-permute-done((f32[392,128]{1,0:T(8,128)S(1)}, f32[392,128]{1,0:T(8,128)S(1)}, u32[]{:S(2)}, u32[]{:S(2)}) %collective-permute-start.37) | collective-permute-done | bytes 200736 | tf_op jit(solution)/shard_map/ppermute | solution.py:427
  167.8 1.6 collective-permute-start.40
  169.9 5.7 %collective-permute-done.40.refs_11_ = f32[384,128]{1,0:T(8,128)S(1)} collective-permute-done((f32[384,128]{1,0:T(8,128)S(1)}, f32[384,128]{1,0:T(8,128)S(1)}, u32[]{:S(2)}, u32[]{:S(2)}) %collective-permute-start.40) | collective-permute-done | bytes 196640 | tf_op jit(solution)/shard_map/ppermute | solution.py:427
  175.7 1.7 shard_map.92
  178.0 3.6 %collective-permute-done.39.refs_0_ = f32[768,128]{1,0:T(8,128)S(1)} collective-permute-done((f32[768,128]{1,0:T(8,128)S(1)}, f32[768,128]{1,0:T(8,128)S(1)}, u32[]{:S(2)}, u32[]{:S(2)}) %collective-permute-start.39) | collective-permute-done | bytes 393248 | tf_op jit(solution)/shard_map/ppermute | solution.py:427
  181.6 1.9 %collective-permute-done.41.refs_10_ = f32[768,128]{1,0:T(8,128)S(1)} collective-permute-done((f32[768,128]{1,0:T(8,128)S(1)}, f32[768,128]{1,0:T(8,128)S(1)}, u32[]{:S(2)}, u32[]{:S(2)}) %collective-permute-start.41) | collective-permute-done | bytes 393248 | tf_op jit(solution)/shard_map/ppermute | solution.py:427
  183.5 1.7 shard_map.93
  (145 shorter events, 36.8 us)
Async XLA Ops:
  7.8 7.9 %collective-permute-start = (f32[776,128]{1,0:T(8,128)S(1)}, f32[776,128]{1,0:T(8,128)S(1)}, u32[]{:S(2)}, u32[]{:S(2)}) collective-permute-start(f32[776,128]{1,0:T(8,128)S(1)} %get-tuple-element.100), channel_id=1, source_target_pairs={{0,4},{1,9},{2,6},{3,11},{4,0},{5,13},{6,2},{7,15},{8,12},{9,1},{1... | collective-permute-start | bytes 1191944 | tf_op jit(solution)/shard_map/ppermute | solution.py:427
  15.8 6.5 %collective-permute-start.1 = (f32[392,128]{1,0:T(8,128)S(1)}, f32[392,128]{1,0:T(8,128)S(1)}, u32[]{:S(2)}, u32[]{:S(2)}) collective-permute-start(f32[392,128]{1,0:T(8,128)S(1)} %pad_maximum_fusion.10), channel_id=1, source_target_pairs={{0,8},{1,5},{2,10},{3,7},{4,12},{5,1},{6,14},{7,3},{8,0},{9,13},{1... | collective-permute-start | bytes 602120 | tf_op jit(solution)/shard_map/ppermute | solution.py:427
  19.9 14.1 %collective-permute-start.3 = (f32[776,128]{1,0:T(8,128)S(1)}, f32[776,128]{1,0:T(8,128)S(1)}, u32[]{:S(2)}, u32[]{:S(2)}) collective-permute-start(f32[776,128]{1,0:T(8,128)S(1)} %get-tuple-element.104), channel_id=1, source_target_pairs={{0,8},{1,5},{2,10},{3,7},{4,12},{5,1},{6,14},{7,3},{8,0},{9,13},{1... | collective-permute-start | bytes 1191944 | tf_op jit(solution)/shard_map/ppermute | solution.py:427
  22.3 14.1 %collective-permute-start.2 = (f32[392,128]{1,0:T(8,128)S(1)}, f32[392,128]{1,0:T(8,128)S(1)}, u32[]{:S(2)}, u32[]{:S(2)}) collective-permute-start(f32[392,128]{1,0:T(8,128)S(1)} %pad_maximum_fusion.11), channel_id=1, source_target_pairs={{0,16},{1,17},{2,18},{3,19},{4,20},{5,21},{6,22},{7,23},{8,24},{9,... | collective-permute-start | bytes 602120 | tf_op jit(solution)/shard_map/ppermute | solution.py:427
  34.0 6.0 %collective-permute-start.5 = (f32[392,128]{1,0:T(8,128)S(1)}, f32[392,128]{1,0:T(8,128)S(1)}, u32[]{:S(2)}, u32[]{:S(2)}) collective-permute-start(f32[392,128]{1,0:T(8,128)S(1)} %pad_maximum_fusion.12), channel_id=1, source_target_pairs={{0,4},{1,9},{2,6},{3,11},{4,0},{5,13},{6,2},{7,15},{8,12},{9,1},{1... | collective-permute-start | bytes 602120 | tf_op jit(solution)/shard_map/ppermute | solution.py:427
  36.4 10.7 %collective-permute-start.4 = (f32[384,128]{1,0:T(8,128)S(1)}, f32[384,128]{1,0:T(8,128)S(1)}, u32[]{:S(2)}, u32[]{:S(2)}) collective-permute-start(f32[384,128]{1,0:T(8,128)S(1)} %slice_add_fusion.25.mine_ref), channel_id=1, source_target_pairs={{0,8},{1,5},{2,10},{3,7},{4,12},{5,1},{6,14},{7,3},{8,0},{9,13},{1... | collective-permute-start | bytes 589832 | tf_op jit(solution)/shard_map/ppermute | solution.py:427
  40.1 8.5 %collective-permute-start.7 = (f32[392,128]{1,0:T(8,128)S(1)}, f32[392,128]{1,0:T(8,128)S(1)}, u32[]{:S(2)}, u32[]{:S(2)}) collective-permute-start(f32[392,128]{1,0:T(8,128)S(1)} %pad_maximum_fusion.13), channel_id=1, source_target_pairs={{0,16},{1,17},{2,18},{3,19},{4,20},{5,21},{6,22},{7,23},{8,24},{9,... | collective-permute-start | bytes 602120 | tf_op jit(solution)/shard_map/ppermute | solution.py:427
  47.2 7.8 %collective-permute-start.6 = (f32[768,128]{1,0:T(8,128)S(1)}, f32[768,128]{1,0:T(8,128)S(1)}, u32[]{:S(2)}, u32[]{:S(2)}) collective-permute-start(f32[768,128]{1,0:T(8,128)S(1)} %pad_maximum_fusion), channel_id=1, source_target_pairs={{0,4},{1,9},{2,6},{3,11},{4,0},{5,13},{6,2},{7,15},{8,12},{9,1},{1... | collective-permute-start | bytes 1179656 | tf_op jit(solution)/shard_map/ppermute | solution.py:427
  48.7 8.4 %collective-permute-start.8 = (f32[384,128]{1,0:T(8,128)S(1)}, f32[384,128]{1,0:T(8,128)S(1)}, u32[]{:S(2)}, u32[]{:S(2)}) collective-permute-start(f32[384,128]{1,0:T(8,128)S(1)} %slice_add_fusion.24.mine_ref), channel_id=1, source_target_pairs={{0,4},{1,9},{2,6},{3,11},{4,0},{5,13},{6,2},{7,15},{8,12},{9,1},{1... | collective-permute-start | bytes 589832 | tf_op jit(solution)/shard_map/ppermute | solution.py:427
  56.1 2.1 %collective-permute-start.9 = (f32[520,128]{1,0:T(8,128)S(1)}, f32[520,128]{1,0:T(8,128)S(1)}, u32[]{:S(2)}, u32[]{:S(2)}) collective-permute-start(f32[520,128]{1,0:T(8,128)S(1)} %get-tuple-element.119), channel_id=1, source_target_pairs={{0,1},{1,0},{2,3},{3,2},{4,5},{5,4},{6,7},{7,6},{8,9},{9,8},{10,11... | collective-permute-start | bytes 798728 | tf_op jit(solution)/shard_map/ppermute | solution.py:430
  57.2 7.8 %collective-permute-start.11 = (f32[768,128]{1,0:T(8,128)S(1)}, f32[768,128]{1,0:T(8,128)S(1)}, u32[]{:S(2)}, u32[]{:S(2)}) collective-permute-start(f32[768,128]{1,0:T(8,128)S(1)} %pad_maximum_fusion.1), channel_id=1, source_target_pairs={{0,8},{1,5},{2,10},{3,7},{4,12},{5,1},{6,14},{7,3},{8,0},{9,13},{1... | collective-permute-start | bytes 1179656 | tf_op jit(solution)/shard_map/ppermute | solution.py:427
  58.3 8.0 %collective-permute-start.10 = (f32[520,128]{1,0:T(8,128)S(1)}, f32[520,128]{1,0:T(8,128)S(1)}, u32[]{:S(2)}, u32[]{:S(2)}) collective-permute-start(f32[520,128]{1,0:T(8,128)S(1)} %pad_maximum_fusion.6), channel_id=1, source_target_pairs={{0,2},{1,3},{2,0},{3,1},{4,6},{5,7},{6,4},{7,5},{8,10},{9,11},{10,... | collective-permute-start | bytes 798728 | tf_op jit(solution)/shard_map/ppermute | solution.py:430
  66.1 1.7 collective-permute-start.13
  66.4 1.7 collective-permute-start.12
  67.9 8.5 %collective-permute-start.15 = (f32[520,128]{1,0:T(8,128)S(1)}, f32[520,128]{1,0:T(8,128)S(1)}, u32[]{:S(2)}, u32[]{:S(2)}) collective-permute-start(f32[520,128]{1,0:T(8,128)S(1)} %pad_maximum_fusion.7), channel_id=1, source_target_pairs={{0,2},{1,3},{2,0},{3,1},{4,6},{5,7},{6,4},{7,5},{8,10},{9,11},{10,... | collective-permute-start | bytes 798728 | tf_op jit(solution)/shard_map/ppermute | solution.py:430
  69.5 7.9 %collective-permute-start.14 = (f32[776,128]{1,0:T(8,128)S(1)}, f32[776,128]{1,0:T(8,128)S(1)}, u32[]{:S(2)}, u32[]{:S(2)}) collective-permute-start(f32[776,128]{1,0:T(8,128)S(1)} %get-tuple-element.134), channel_id=1, source_target_pairs={{0,4},{1,9},{2,6},{3,11},{4,0},{5,13},{6,2},{7,15},{8,12},{9,1},{1... | collective-permute-start | bytes 1191944 | tf_op jit(solution)/shard_map/ppermute | solution.py:427
  76.4 1.6 collective-permute-start.17
  77.5 5.8 %collective-permute-start.16 = (f32[392,128]{1,0:T(8,128)S(1)}, f32[392,128]{1,0:T(8,128)S(1)}, u32[]{:S(2)}, u32[]{:S(2)}) collective-permute-start(f32[392,128]{1,0:T(8,128)S(1)} %pad_maximum_fusion.14), channel_id=1, source_target_pairs={{0,8},{1,5},{2,10},{3,7},{4,12},{5,1},{6,14},{7,3},{8,0},{9,13},{1... | collective-permute-start | bytes 602120 | tf_op jit(solution)/shard_map/ppermute | solution.py:427
  79.6 9.9 %collective-permute-start.19 = (f32[776,128]{1,0:T(8,128)S(1)}, f32[776,128]{1,0:T(8,128)S(1)}, u32[]{:S(2)}, u32[]{:S(2)}) collective-permute-start(f32[776,128]{1,0:T(8,128)S(1)} %get-tuple-element.138), channel_id=1, source_target_pairs={{0,8},{1,5},{2,10},{3,7},{4,12},{5,1},{6,14},{7,3},{8,0},{9,13},{1... | collective-permute-start | bytes 1191944 | tf_op jit(solution)/shard_map/ppermute | solution.py:427
  83.4 10.4 %collective-permute-start.18 = (f32[392,128]{1,0:T(8,128)S(1)}, f32[392,128]{1,0:T(8,128)S(1)}, u32[]{:S(2)}, u32[]{:S(2)}) collective-permute-start(f32[392,128]{1,0:T(8,128)S(1)} %pad_maximum_fusion.15), channel_id=1, source_target_pairs={{0,16},{1,17},{2,18},{3,19},{4,20},{5,21},{6,22},{7,23},{8,24},{9,... | collective-permute-start | bytes 602120 | tf_op jit(solution)/shard_map/ppermute | solution.py:427
  89.6 8.4 %collective-permute-start.21 = (f32[392,128]{1,0:T(8,128)S(1)}, f32[392,128]{1,0:T(8,128)S(1)}, u32[]{:S(2)}, u32[]{:S(2)}) collective-permute-start(f32[392,128]{1,0:T(8,128)S(1)} %pad_maximum_fusion.16), channel_id=1, source_target_pairs={{0,4},{1,9},{2,6},{3,11},{4,0},{5,13},{6,2},{7,15},{8,12},{9,1},{1... | collective-permute-start | bytes 602120 | tf_op jit(solution)/shard_map/ppermute | solution.py:427
  93.8 10.8 %collective-permute-start.20 = (f32[384,128]{1,0:T(8,128)S(1)}, f32[384,128]{1,0:T(8,128)S(1)}, u32[]{:S(2)}, u32[]{:S(2)}) collective-permute-start(f32[384,128]{1,0:T(8,128)S(1)} %slice_add_fusion.23.mine_ref), channel_id=1, source_target_pairs={{0,8},{1,5},{2,10},{3,7},{4,12},{5,1},{6,14},{7,3},{8,0},{9,13},{1... | collective-permute-start | bytes 589832 | tf_op jit(solution)/shard_map/ppermute | solution.py:427
  98.1 10.1 %collective-permute-start.23 = (f32[392,128]{1,0:T(8,128)S(1)}, f32[392,128]{1,0:T(8,128)S(1)}, u32[]{:S(2)}, u32[]{:S(2)}) collective-permute-start(f32[392,128]{1,0:T(8,128)S(1)} %pad_maximum_fusion.17), channel_id=1, source_target_pairs={{0,16},{1,17},{2,18},{3,19},{4,20},{5,21},{6,22},{7,23},{8,24},{9,... | collective-permute-start | bytes 602120 | tf_op jit(solution)/shard_map/ppermute | solution.py:427
  104.6 9.4 %collective-permute-start.22 = (f32[768,128]{1,0:T(8,128)S(1)}, f32[768,128]{1,0:T(8,128)S(1)}, u32[]{:S(2)}, u32[]{:S(2)}) collective-permute-start(f32[768,128]{1,0:T(8,128)S(1)} %pad_maximum_fusion.2), channel_id=1, source_target_pairs={{0,4},{1,9},{2,6},{3,11},{4,0},{5,13},{6,2},{7,15},{8,12},{9,1},{1... | collective-permute-start | bytes 1179656 | tf_op jit(solution)/shard_map/ppermute | solution.py:427
  108.2 7.8 %collective-permute-start.25 = (f32[384,128]{1,0:T(8,128)S(1)}, f32[384,128]{1,0:T(8,128)S(1)}, u32[]{:S(2)}, u32[]{:S(2)}) collective-permute-start(f32[384,128]{1,0:T(8,128)S(1)} %slice_add_fusion.22.mine_ref), channel_id=1, source_target_pairs={{0,4},{1,9},{2,6},{3,11},{4,0},{5,13},{6,2},{7,15},{8,12},{9,1},{1... | collective-permute-start | bytes 589832 | tf_op jit(solution)/shard_map/ppermute | solution.py:427
  115.1 2.1 %collective-permute-start.24 = (f32[520,128]{1,0:T(8,128)S(1)}, f32[520,128]{1,0:T(8,128)S(1)}, u32[]{:S(2)}, u32[]{:S(2)}) collective-permute-start(f32[520,128]{1,0:T(8,128)S(1)} %get-tuple-element.152), channel_id=1, source_target_pairs={{0,1},{1,0},{2,3},{3,2},{4,5},{5,4},{6,7},{7,6},{8,9},{9,8},{10,11... | collective-permute-start | bytes 798728 | tf_op jit(solution)/shard_map/ppermute | solution.py:430
  116.1 7.8 %collective-permute-start.27 = (f32[768,128]{1,0:T(8,128)S(1)}, f32[768,128]{1,0:T(8,128)S(1)}, u32[]{:S(2)}, u32[]{:S(2)}) collective-permute-start(f32[768,128]{1,0:T(8,128)S(1)} %pad_maximum_fusion.3), channel_id=1, source_target_pairs={{0,8},{1,5},{2,10},{3,7},{4,12},{5,1},{6,14},{7,3},{8,0},{9,13},{1... | collective-permute-start | bytes 1179656 | tf_op jit(solution)/shard_map/ppermute | solution.py:427
  117.2 9.2 %collective-permute-start.26 = (f32[520,128]{1,0:T(8,128)S(1)}, f32[520,128]{1,0:T(8,128)S(1)}, u32[]{:S(2)}, u32[]{:S(2)}) collective-permute-start(f32[520,128]{1,0:T(8,128)S(1)} %pad_maximum_fusion.8), channel_id=1, source_target_pairs={{0,2},{1,3},{2,0},{3,1},{4,6},{5,7},{6,4},{7,5},{8,10},{9,11},{10,... | collective-permute-start | bytes 798728 | tf_op jit(solution)/shard_map/ppermute | solution.py:430
  125.0 2.6 %collective-permute-start.29 = (f32[520,128]{1,0:T(8,128)S(1)}, f32[520,128]{1,0:T(8,128)S(1)}, u32[]{:S(2)}, u32[]{:S(2)}) collective-permute-start(f32[520,128]{1,0:T(8,128)S(1)} %get-tuple-element.163), channel_id=1, source_target_pairs={{0,1},{1,0},{2,3},{3,2},{4,5},{5,4},{6,7},{7,6},{8,9},{9,8},{10,11... | collective-permute-start | bytes 798728 | tf_op jit(solution)/shard_map/ppermute | solution.py:430
  126.5 2.8 %collective-permute-start.28 = (f32[512,128]{1,0:T(8,128)S(1)}, f32[512,128]{1,0:T(8,128)S(1)}, u32[]{:S(2)}, u32[]{:S(2)}) collective-permute-start(f32[512,128]{1,0:T(8,128)S(1)} %slice_add_fusion.8.refs_2_), channel_id=1, source_target_pairs={{0,1},{1,0},{2,3},{3,2},{4,5},{5,4},{6,7},{7,6},{8,9},{9,8},{10,11... | collective-permute-start | bytes 786440 | tf_op jit(solution)/shard_map/ppermute | solution.py:430
  127.7 8.8 %collective-permute-start.31 = (f32[520,128]{1,0:T(8,128)S(1)}, f32[520,128]{1,0:T(8,128)S(1)}, u32[]{:S(2)}, u32[]{:S(2)}) collective-permute-start(f32[520,128]{1,0:T(8,128)S(1)} %pad_maximum_fusion.9), channel_id=1, source_target_pairs={{0,2},{1,3},{2,0},{3,1},{4,6},{5,7},{6,4},{7,5},{8,10},{9,11},{10,... | collective-permute-start | bytes 798728 | tf_op jit(solution)/shard_map/ppermute | solution.py:430
  130.7 7.8 %collective-permute-start.30 = (f32[776,128]{1,0:T(8,128)S(1)}, f32[776,128]{1,0:T(8,128)S(1)}, u32[]{:S(2)}, u32[]{:S(2)}) collective-permute-start(f32[776,128]{1,0:T(8,128)S(1)} %get-tuple-element.170), channel_id=1, source_target_pairs={{0,4},{1,9},{2,6},{3,11},{4,0},{5,13},{6,2},{7,15},{8,12},{9,1},{1... | collective-permute-start | bytes 1191944 | tf_op jit(solution)/shard_map/ppermute | solution.py:427
  136.5 2.2 %collective-permute-start.33 = (f32[512,128]{1,0:T(8,128)S(1)}, f32[512,128]{1,0:T(8,128)S(1)}, u32[]{:S(2)}, u32[]{:S(2)}) collective-permute-start(f32[512,128]{1,0:T(8,128)S(1)} %slice_add_fusion.6.refs_2_), channel_id=1, source_target_pairs={{0,1},{1,0},{2,3},{3,2},{4,5},{5,4},{6,7},{7,6},{8,9},{9,8},{10,11... | collective-permute-start | bytes 786440 | tf_op jit(solution)/shard_map/ppermute | solution.py:430
  138.7 5.8 %collective-permute-start.32 = (f32[392,128]{1,0:T(8,128)S(1)}, f32[392,128]{1,0:T(8,128)S(1)}, u32[]{:S(2)}, u32[]{:S(2)}) collective-permute-start(f32[392,128]{1,0:T(8,128)S(1)} %pad_maximum_fusion.18), channel_id=1, source_target_pairs={{0,8},{1,5},{2,10},{3,7},{4,12},{5,1},{6,14},{7,3},{8,0},{9,13},{1... | collective-permute-start | bytes 602120 | tf_op jit(solution)/shard_map/ppermute | solution.py:427
  140.3 12.6 %collective-permute-start.35 = (f32[776,128]{1,0:T(8,128)S(1)}, f32[776,128]{1,0:T(8,128)S(1)}, u32[]{:S(2)}, u32[]{:S(2)}) collective-permute-start(f32[776,128]{1,0:T(8,128)S(1)} %get-tuple-element.176), channel_id=1, source_target_pairs={{0,8},{1,5},{2,10},{3,7},{4,12},{5,1},{6,14},{7,3},{8,0},{9,13},{1... | collective-permute-start | bytes 1191944 | tf_op jit(solution)/shard_map/ppermute | solution.py:427
  144.5 10.1 %collective-permute-start.34 = (f32[392,128]{1,0:T(8,128)S(1)}, f32[392,128]{1,0:T(8,128)S(1)}, u32[]{:S(2)}, u32[]{:S(2)}) collective-permute-start(f32[392,128]{1,0:T(8,128)S(1)} %pad_maximum_fusion.19), channel_id=1, source_target_pairs={{0,16},{1,17},{2,18},{3,19},{4,20},{5,21},{6,22},{7,23},{8,24},{9,... | collective-permute-start | bytes 602120 | tf_op jit(solution)/shard_map/ppermute | solution.py:427
  153.0 5.8 %collective-permute-start.36 = (f32[392,128]{1,0:T(8,128)S(1)}, f32[392,128]{1,0:T(8,128)S(1)}, u32[]{:S(2)}, u32[]{:S(2)}) collective-permute-start(f32[392,128]{1,0:T(8,128)S(1)} %pad_maximum_fusion.20), channel_id=1, source_target_pairs={{0,4},{1,9},{2,6},{3,11},{4,0},{5,13},{6,2},{7,15},{8,12},{9,1},{1... | collective-permute-start | bytes 602120 | tf_op jit(solution)/shard_map/ppermute | solution.py:427
  154.6 7.9 %collective-permute-start.38 = (f32[384,128]{1,0:T(8,128)S(1)}, f32[384,128]{1,0:T(8,128)S(1)}, u32[]{:S(2)}, u32[]{:S(2)}) collective-permute-start(f32[384,128]{1,0:T(8,128)S(1)} %slice_add_fusion.21.refs_2_), channel_id=1, source_target_pairs={{0,8},{1,5},{2,10},{3,7},{4,12},{5,1},{6,14},{7,3},{8,0},{9,13},{1... | collective-permute-start | bytes 589832 | tf_op jit(solution)/shard_map/ppermute | solution.py:427
  158.9 8.9 %collective-permute-start.37 = (f32[392,128]{1,0:T(8,128)S(1)}, f32[392,128]{1,0:T(8,128)S(1)}, u32[]{:S(2)}, u32[]{:S(2)}) collective-permute-start(f32[392,128]{1,0:T(8,128)S(1)} %pad_maximum_fusion.21), channel_id=1, source_target_pairs={{0,16},{1,17},{2,18},{3,19},{4,20},{5,21},{6,22},{7,23},{8,24},{9,... | collective-permute-start | bytes 602120 | tf_op jit(solution)/shard_map/ppermute | solution.py:427
  167.8 7.8 %collective-permute-start.40 = (f32[384,128]{1,0:T(8,128)S(1)}, f32[384,128]{1,0:T(8,128)S(1)}, u32[]{:S(2)}, u32[]{:S(2)}) collective-permute-start(f32[384,128]{1,0:T(8,128)S(1)} %slice_add_fusion.20.refs_12_), channel_id=1, source_target_pairs={{0,4},{1,9},{2,6},{3,11},{4,0},{5,13},{6,2},{7,15},{8,12},{9,1},{1... | collective-permute-start | bytes 589832 | tf_op jit(solution)/shard_map/ppermute | solution.py:427
  169.4 12.2 %collective-permute-start.39 = (f32[768,128]{1,0:T(8,128)S(1)}, f32[768,128]{1,0:T(8,128)S(1)}, u32[]{:S(2)}, u32[]{:S(2)}) collective-permute-start(f32[768,128]{1,0:T(8,128)S(1)} %pad_maximum_fusion.4), channel_id=1, source_target_pairs={{0,4},{1,9},{2,6},{3,11},{4,0},{5,13},{6,2},{7,15},{8,12},{9,1},{1... | collective-permute-start | bytes 1179656 | tf_op jit(solution)/shard_map/ppermute | solution.py:427
  175.6 7.8 %collective-permute-start.41 = (f32[768,128]{1,0:T(8,128)S(1)}, f32[768,128]{1,0:T(8,128)S(1)}, u32[]{:S(2)}, u32[]{:S(2)}) collective-permute-start(f32[768,128]{1,0:T(8,128)S(1)} %pad_maximum_fusion.5), channel_id=1, source_target_pairs={{0,8},{1,5},{2,10},{3,7},{4,12},{5,1},{6,14},{7,3},{8,0},{9,13},{1... | collective-permute-start | bytes 1179656 | tf_op jit(solution)/shard_map/ppermute | solution.py:427

commit v18 on v17

--- a/solution.py
+++ b/solution.py
@@ -14,7 +14,6 @@
 UNITS = 4
 NORM_ROWS = 8
 UNIT_ORDERS = ((0, 1, 2, 3), (0, 2, 1, 3))
-BEHIND = 0
 
 tiny_eps = 1e-06
 
@@ -505,24 +504,21 @@
     wanted = [next(run) for run in runs]
     chains = [None] * len(runs)
     gots = [None] * len(runs)
-    swap, value, level = wanted[0]
-    gots[0] = swap(value, level)
-    latest = wanted[1][1]
+    latest = None
+    for mine, (swap, value, level) in enumerate(wanted):
+        latest = value if latest is None else tied(value, latest)
+        gots[mine] = swap(latest, level)
     turn = 0
     while None in chains:
-        mine = 0 if turn < BEHIND else (turn - BEHIND) % 2
+        mine = turn % 2
         turn += 1
         if chains[mine] is not None:
             continue
-        if gots[mine] is None:
-            swap, value, level = wanted[mine]
-            latest = tied(value, latest)
-        else:
-            try:
-                swap, latest, level = runs[mine].send((tied(gots[mine], latest), latest))
-            except StopIteration as stop:
-                chains[mine] = stop.value
-                continue
+        try:
+            swap, latest, level = runs[mine].send((tied(gots[mine], latest), latest))
+        except StopIteration as stop:
+            chains[mine] = stop.value
+            continue
         gots[mine] = swap(latest, level)
 
     cells = CB_DEV * TILE

time: 184 us -> 207 us (1.12)
  waiting for transfers between devices: 95.9 us -> 114 us
  starting transfers between devices: 44.3 us -> 48.7 us
    ppermute x12, waiting for transfers between devices: 9.11 us -> 21.8 us  [swap_cols(): lax.ppermute(value, 'cols', [(i, i ^ 1 << level) for i in range(col_count)])]
    ppermute x30, waiting for transfers between devices: 86.8 us -> 92.3 us  [swap_rows(): return lax.ppermute(value, ('rows', 'cols'), pairs)]
    ppermute x30, starting transfers between devices: 39.4 us -> 42.3 us  [swap_rows(): return lax.ppermute(value, ('rows', 'cols'), pairs)]
  transfers between devices with their start and end apart: 42 -> 42, of which waited for: 31 -> 24; matrix products, arithmetic and copies ran while one was open for 1% -> 1% of each run, Pallas kernels for 18% -> 16%
where the time goes in v18:
time: 207 us
  waiting for transfers between devices  114 us (55%)
  starting transfers between devices  48.7 us (24%)
  Pallas kernels  40.2 us (19%)
    ppermute x30, waiting for transfers between devices, swap_rows(): return lax.ppermute(value, ('rows', 'cols'), pairs)  92.3 us
    ppermute x30, starting transfers between devices, swap_rows(): return lax.ppermute(value, ('rows', 'cols'), pairs)  42.3 us
    pallas_call x24, Pallas kernels, product_call(): pl.pallas_call(body, in_specs=[WHOLE] * (1 + len(operands)), out_specs=[W...  32.4 us
    ppermute x12, waiting for transfers between devices, swap_cols(): lax.ppermute(value, 'cols', [(i, i ^ 1 << level) for i in range(col_count)])  21.8 us
    ppermute x12, starting transfers between devices, swap_cols(): lax.ppermute(value, 'cols', [(i, i ^ 1 << level) for i in range(col_count)])  6.47 us
    pallas_call x1, Pallas kernels, fill_dense(): pl.pallas_call(fill_kernel, in_specs=[SCALARS] * 2 + [pl.BlockSpec(memory...  4.4 us
  transfers between devices with their start and end apart: 42, of which 24 were waited for; matrix products, arithmetic and copies ran while one was open for 1% of the time, Pallas kernels for 16%

profile of v18, /device:TPU:0, one launch (start us, length us, event | category | flops | bytes accessed | tf_op | source)
XLA Modules:
  0.0 206.6 jit_solution(10652137431000397940)
XLA Ops:
  0.7 4.4 %shard_map.67 = (bf16[2048,3200]{1,0:T(8,128)(2,1)S(1)}, f32[1024,128]{1,0:T(8,128)S(1)}, f32[1024,128]{1,0:T(8,128)S(1)}) custom-call(s32[24]{0:T(128)S(1)} %fusion.place_ref, s32[1]{0:T(128)} %bitcast.1.flip_ref, s32[16,16]{1,0:T(8,128)} %pattern_in.1, s32[16]{0:T(128)} %bitcast.5, f32[2048,128]{1,0:T(8,128)} %delays_in.1, bf16[16,16,128,128]{3,2,1,0:T(8,128)(2,1)} %tiles_in.1), custom_call_target="tpu_custom_call" | custom-call | bytes 8388608 | tf_op jit(solution)/shard_map/pallas_call | solution.py:106
  6.5 3.0 %collective-permute-start = (f32[776,128]{1,0:T(8,128)S(1)}, f32[776,128]{1,0:T(8,128)S(1)}, u32[]{:S(2)}, u32[]{:S(2)}) collective-permute-start(f32[776,128]{1,0:T(8,128)S(1)} %get-tuple-element.100), channel_id=1, source_target_pairs={{0,4},{1,9},{2,6},{3,11},{4,0},{5,13},{6,2},{7,15},{8,12},{9,1},{1... | collective-permute-start | bytes 1191944 | tf_op jit(solution)/shard_map/ppermute | solution.py:426
  10.9 2.4 %collective-permute-start.2 = (f32[776,128]{1,0:T(8,128)S(1)}, f32[776,128]{1,0:T(8,128)S(1)}, u32[]{:S(2)}, u32[]{:S(2)}) collective-permute-start(f32[776,128]{1,0:T(8,128)S(1)} %get-tuple-element.103), channel_id=1, source_target_pairs={{0,8},{1,5},{2,10},{3,7},{4,12},{5,1},{6,14},{7,3},{8,0},{9,13},{1... | collective-permute-start | bytes 1191944 | tf_op jit(solution)/shard_map/ppermute | solution.py:426
  16.1 4.5 %collective-permute-start.1 = (f32[392,128]{1,0:T(8,128)S(1)}, f32[392,128]{1,0:T(8,128)S(1)}, u32[]{:S(2)}, u32[]{:S(2)}) collective-permute-start(f32[392,128]{1,0:T(8,128)S(1)} %pad_maximum_fusion.10), channel_id=1, source_target_pairs={{0,8},{1,5},{2,10},{3,7},{4,12},{5,1},{6,14},{7,3},{8,0},{9,13},{1... | collective-permute-start | bytes 602120 | tf_op jit(solution)/shard_map/ppermute | solution.py:426
  20.7 2.4 %collective-permute-start.4 = (f32[392,128]{1,0:T(8,128)S(1)}, f32[392,128]{1,0:T(8,128)S(1)}, u32[]{:S(2)}, u32[]{:S(2)}) collective-permute-start(f32[392,128]{1,0:T(8,128)S(1)} %pad_maximum_fusion.11), channel_id=1, source_target_pairs={{0,4},{1,9},{2,6},{3,11},{4,0},{5,13},{6,2},{7,15},{8,12},{9,1},{1... | collective-permute-start | bytes 602120 | tf_op jit(solution)/shard_map/ppermute | solution.py:426
  23.1 2.4 %collective-permute-done.1 = f32[392,128]{1,0:T(8,128)S(1)} collective-permute-done((f32[392,128]{1,0:T(8,128)S(1)}, f32[392,128]{1,0:T(8,128)S(1)}, u32[]{:S(2)}, u32[]{:S(2)}) %collective-permute-start.1) | collective-permute-done | bytes 200736 | tf_op jit(solution)/shard_map/ppermute | solution.py:426
  25.5 6.1 %collective-permute-start.3 = (f32[392,128]{1,0:T(8,128)S(1)}, f32[392,128]{1,0:T(8,128)S(1)}, u32[]{:S(2)}, u32[]{:S(2)}) collective-permute-start(f32[392,128]{1,0:T(8,128)S(1)} %pad_maximum_fusion.12), channel_id=1, source_target_pairs={{0,16},{1,17},{2,18},{3,19},{4,20},{5,21},{6,22},{7,23},{8,24},{9,... | collective-permute-start | bytes 602120 | tf_op jit(solution)/shard_map/ppermute | solution.py:426
  31.8 11.0 %collective-permute-done.3 = f32[392,128]{1,0:T(8,128)S(1)} collective-permute-done((f32[392,128]{1,0:T(8,128)S(1)}, f32[392,128]{1,0:T(8,128)S(1)}, u32[]{:S(2)}, u32[]{:S(2)}) %collective-permute-start.3) | collective-permute-done | bytes 200736 | tf_op jit(solution)/shard_map/ppermute | solution.py:426
  42.9 2.0 collective-permute-done.6
  45.0 1.5 collective-permute-start.8
  46.5 4.2 %collective-permute-done.5.inner_ref = f32[384,128]{1,0:T(8,128)S(1)} collective-permute-done((f32[384,128]{1,0:T(8,128)S(1)}, f32[384,128]{1,0:T(8,128)S(1)}, u32[]{:S(2)}, u32[]{:S(2)}) %collective-permute-start.5) | collective-permute-done | bytes 196640 | tf_op jit(solution)/shard_map/ppermute | solution.py:426
  50.7 1.5 collective-permute-start.7
  52.3 1.9 shard_map.72
  54.3 5.6 %collective-permute-done.7.outer_ref = f32[768,128]{1,0:T(8,128)S(1)} collective-permute-done((f32[768,128]{1,0:T(8,128)S(1)}, f32[768,128]{1,0:T(8,128)S(1)}, u32[]{:S(2)}, u32[]{:S(2)}) %collective-permute-start.7) | collective-permute-done | bytes 393248 | tf_op jit(solution)/shard_map/ppermute | solution.py:426
  61.0 1.9 shard_map.74
  65.7 2.7 %collective-permute-start.11 = (f32[520,128]{1,0:T(8,128)S(1)}, f32[520,128]{1,0:T(8,128)S(1)}, u32[]{:S(2)}, u32[]{:S(2)}) collective-permute-start(f32[520,128]{1,0:T(8,128)S(1)} %pad_maximum_fusion.6), channel_id=1, source_target_pairs={{0,2},{1,3},{2,0},{3,1},{4,6},{5,7},{6,4},{7,5},{8,10},{9,11},{10,... | collective-permute-start | bytes 798728 | tf_op jit(solution)/shard_map/ppermute | solution.py:429
  69.5 6.0 %collective-permute-done.11 = f32[520,128]{1,0:T(8,128)S(1)} collective-permute-done((f32[520,128]{1,0:T(8,128)S(1)}, f32[520,128]{1,0:T(8,128)S(1)}, u32[]{:S(2)}, u32[]{:S(2)}) %collective-permute-start.11) | collective-permute-done | bytes 266272 | tf_op jit(solution)/shard_map/ppermute | solution.py:429
  75.7 5.0 %collective-permute-done.14 = f32[520,128]{1,0:T(8,128)S(1)} collective-permute-done((f32[520,128]{1,0:T(8,128)S(1)}, f32[520,128]{1,0:T(8,128)S(1)}, u32[]{:S(2)}, u32[]{:S(2)}) %collective-permute-start.14) | collective-permute-done | bytes 266272 | tf_op jit(solution)/shard_map/ppermute | solution.py:429
  82.2 1.6 collective-permute-start.15
  83.9 1.6 shard_map.80
  88.7 4.1 %collective-permute-done.15 = f32[776,128]{1,0:T(8,128)S(1)} collective-permute-done((f32[776,128]{1,0:T(8,128)S(1)}, f32[776,128]{1,0:T(8,128)S(1)}, u32[]{:S(2)}, u32[]{:S(2)}) %collective-permute-start.15) | collective-permute-done | bytes 397344 | tf_op jit(solution)/shard_map/ppermute | solution.py:426
  94.0 1.6 collective-permute-start.20
  95.6 5.9 %collective-permute-done.17 = f32[392,128]{1,0:T(8,128)S(1)} collective-permute-done((f32[392,128]{1,0:T(8,128)S(1)}, f32[392,128]{1,0:T(8,128)S(1)}, u32[]{:S(2)}, u32[]{:S(2)}) %collective-permute-start.17) | collective-permute-done | bytes 200736 | tf_op jit(solution)/shard_map/ppermute | solution.py:426
  101.7 3.0 %collective-permute-start.22 = (f32[392,128]{1,0:T(8,128)S(1)}, f32[392,128]{1,0:T(8,128)S(1)}, u32[]{:S(2)}, u32[]{:S(2)}) collective-permute-start(f32[392,128]{1,0:T(8,128)S(1)} %pad_maximum_fusion.17), channel_id=1, source_target_pairs={{0,16},{1,17},{2,18},{3,19},{4,20},{5,21},{6,22},{7,23},{8,24},{9,... | collective-permute-start | bytes 602120 | tf_op jit(solution)/shard_map/ppermute | solution.py:426
  104.7 10.6 %collective-permute-done.19 = f32[392,128]{1,0:T(8,128)S(1)} collective-permute-done((f32[392,128]{1,0:T(8,128)S(1)}, f32[392,128]{1,0:T(8,128)S(1)}, u32[]{:S(2)}, u32[]{:S(2)}) %collective-permute-start.19) | collective-permute-done | bytes 200736 | tf_op jit(solution)/shard_map/ppermute | solution.py:426
  115.4 2.0 collective-permute-done.22
  117.5 1.7 collective-permute-start.24
  119.2 4.0 %collective-permute-done.21.inner_ref = f32[384,128]{1,0:T(8,128)S(1)} collective-permute-done((f32[384,128]{1,0:T(8,128)S(1)}, f32[384,128]{1,0:T(8,128)S(1)}, u32[]{:S(2)}, u32[]{:S(2)}) %collective-permute-start.21) | collective-permute-done | bytes 196640 | tf_op jit(solution)/shard_map/ppermute | solution.py:426
  123.2 1.7 collective-permute-start.23
  125.0 1.9 shard_map.82
  126.9 5.6 %collective-permute-done.23.outer_ref = f32[768,128]{1,0:T(8,128)S(1)} collective-permute-done((f32[768,128]{1,0:T(8,128)S(1)}, f32[768,128]{1,0:T(8,128)S(1)}, u32[]{:S(2)}, u32[]{:S(2)}) %collective-permute-start.23) | collective-permute-done | bytes 393248 | tf_op jit(solution)/shard_map/ppermute | solution.py:426
  133.7 1.9 shard_map.84
  138.4 1.8 collective-permute-start.27
  141.6 6.1 %collective-permute-done.27 = f32[520,128]{1,0:T(8,128)S(1)} collective-permute-done((f32[520,128]{1,0:T(8,128)S(1)}, f32[520,128]{1,0:T(8,128)S(1)}, u32[]{:S(2)}, u32[]{:S(2)}) %collective-permute-start.27) | collective-permute-done | bytes 266272 | tf_op jit(solution)/shard_map/ppermute | solution.py:429
  147.8 4.7 %collective-permute-done.30 = f32[520,128]{1,0:T(8,128)S(1)} collective-permute-done((f32[520,128]{1,0:T(8,128)S(1)}, f32[520,128]{1,0:T(8,128)S(1)}, u32[]{:S(2)}, u32[]{:S(2)}) %collective-permute-start.30) | collective-permute-done | bytes 266272 | tf_op jit(solution)/shard_map/ppermute | solution.py:429
  152.6 1.5 shard_map.88
  154.2 1.6 collective-permute-start.31
  155.8 1.5 shard_map.89
  160.5 4.3 %collective-permute-done.31 = f32[776,128]{1,0:T(8,128)S(1)} collective-permute-done((f32[776,128]{1,0:T(8,128)S(1)}, f32[776,128]{1,0:T(8,128)S(1)}, u32[]{:S(2)}, u32[]{:S(2)}) %collective-permute-start.31) | collective-permute-done | bytes 397344 | tf_op jit(solution)/shard_map/ppermute | solution.py:426
  165.9 1.7 collective-permute-start.36
  167.6 6.4 %collective-permute-done.33 = f32[392,128]{1,0:T(8,128)S(1)} collective-permute-done((f32[392,128]{1,0:T(8,128)S(1)}, f32[392,128]{1,0:T(8,128)S(1)}, u32[]{:S(2)}, u32[]{:S(2)}) %collective-permute-start.33) | collective-permute-done | bytes 200736 | tf_op jit(solution)/shard_map/ppermute | solution.py:426
  174.2 3.0 %collective-permute-start.37 = (f32[392,128]{1,0:T(8,128)S(1)}, f32[392,128]{1,0:T(8,128)S(1)}, u32[]{:S(2)}, u32[]{:S(2)}) collective-permute-start(f32[392,128]{1,0:T(8,128)S(1)} %pad_maximum_fusion.21), channel_id=1, source_target_pairs={{0,16},{1,17},{2,18},{3,19},{4,20},{5,21},{6,22},{7,23},{8,24},{9,... | collective-permute-start | bytes 602120 | tf_op jit(solution)/shard_map/ppermute | solution.py:426
  177.1 10.5 %collective-permute-done.35 = f32[392,128]{1,0:T(8,128)S(1)} collective-permute-done((f32[392,128]{1,0:T(8,128)S(1)}, f32[392,128]{1,0:T(8,128)S(1)}, u32[]{:S(2)}, u32[]{:S(2)}) %collective-permute-start.35) | collective-permute-done | bytes 200736 | tf_op jit(solution)/shard_map/ppermute | solution.py:426
  187.8 2.0 collective-permute-done.37
  191.3 4.2 %collective-permute-done.38.refs_1_ = f32[384,128]{1,0:T(8,128)S(1)} collective-permute-done((f32[384,128]{1,0:T(8,128)S(1)}, f32[384,128]{1,0:T(8,128)S(1)}, u32[]{:S(2)}, u32[]{:S(2)}) %collective-permute-start.38) | collective-permute-done | bytes 196640 | tf_op jit(solution)/shard_map/ppermute | solution.py:426
  197.1 1.7 shard_map.92
  199.3 5.5 %collective-permute-done.41.refs_10_ = f32[768,128]{1,0:T(8,128)S(1)} collective-permute-done((f32[768,128]{1,0:T(8,128)S(1)}, f32[768,128]{1,0:T(8,128)S(1)}, u32[]{:S(2)}, u32[]{:S(2)}) %collective-permute-start.41) | collective-permute-done | bytes 393248 | tf_op jit(solution)/shard_map/ppermute | solution.py:426
  204.9 1.7 shard_map.93
  (145 shorter events, 30.8 us)
Async XLA Ops:
  6.5 9.5 %collective-permute-start = (f32[776,128]{1,0:T(8,128)S(1)}, f32[776,128]{1,0:T(8,128)S(1)}, u32[]{:S(2)}, u32[]{:S(2)}) collective-permute-start(f32[776,128]{1,0:T(8,128)S(1)} %get-tuple-element.100), channel_id=1, source_target_pairs={{0,4},{1,9},{2,6},{3,11},{4,0},{5,13},{6,2},{7,15},{8,12},{9,1},{1... | collective-permute-start | bytes 1191944 | tf_op jit(solution)/shard_map/ppermute | solution.py:426
  10.9 9.7 %collective-permute-start.2 = (f32[776,128]{1,0:T(8,128)S(1)}, f32[776,128]{1,0:T(8,128)S(1)}, u32[]{:S(2)}, u32[]{:S(2)}) collective-permute-start(f32[776,128]{1,0:T(8,128)S(1)} %get-tuple-element.103), channel_id=1, source_target_pairs={{0,8},{1,5},{2,10},{3,7},{4,12},{5,1},{6,14},{7,3},{8,0},{9,13},{1... | collective-permute-start | bytes 1191944 | tf_op jit(solution)/shard_map/ppermute | solution.py:426
  16.1 9.4 %collective-permute-start.1 = (f32[392,128]{1,0:T(8,128)S(1)}, f32[392,128]{1,0:T(8,128)S(1)}, u32[]{:S(2)}, u32[]{:S(2)}) collective-permute-start(f32[392,128]{1,0:T(8,128)S(1)} %pad_maximum_fusion.10), channel_id=1, source_target_pairs={{0,8},{1,5},{2,10},{3,7},{4,12},{5,1},{6,14},{7,3},{8,0},{9,13},{1... | collective-permute-start | bytes 602120 | tf_op jit(solution)/shard_map/ppermute | solution.py:426
  20.7 11.0 %collective-permute-start.4 = (f32[392,128]{1,0:T(8,128)S(1)}, f32[392,128]{1,0:T(8,128)S(1)}, u32[]{:S(2)}, u32[]{:S(2)}) collective-permute-start(f32[392,128]{1,0:T(8,128)S(1)} %pad_maximum_fusion.11), channel_id=1, source_target_pairs={{0,4},{1,9},{2,6},{3,11},{4,0},{5,13},{6,2},{7,15},{8,12},{9,1},{1... | collective-permute-start | bytes 602120 | tf_op jit(solution)/shard_map/ppermute | solution.py:426
  25.5 17.3 %collective-permute-start.3 = (f32[392,128]{1,0:T(8,128)S(1)}, f32[392,128]{1,0:T(8,128)S(1)}, u32[]{:S(2)}, u32[]{:S(2)}) collective-permute-start(f32[392,128]{1,0:T(8,128)S(1)} %pad_maximum_fusion.12), channel_id=1, source_target_pairs={{0,16},{1,17},{2,18},{3,19},{4,20},{5,21},{6,22},{7,23},{8,24},{9,... | collective-permute-start | bytes 602120 | tf_op jit(solution)/shard_map/ppermute | solution.py:426
  31.7 13.3 %collective-permute-start.6 = (f32[392,128]{1,0:T(8,128)S(1)}, f32[392,128]{1,0:T(8,128)S(1)}, u32[]{:S(2)}, u32[]{:S(2)}) collective-permute-start(f32[392,128]{1,0:T(8,128)S(1)} %pad_maximum_fusion.13), channel_id=1, source_target_pairs={{0,16},{1,17},{2,18},{3,19},{4,20},{5,21},{6,22},{7,23},{8,24},{9,... | collective-permute-start | bytes 602120 | tf_op jit(solution)/shard_map/ppermute | solution.py:426
  42.9 7.8 %collective-permute-start.5 = (f32[384,128]{1,0:T(8,128)S(1)}, f32[384,128]{1,0:T(8,128)S(1)}, u32[]{:S(2)}, u32[]{:S(2)}) collective-permute-start(f32[384,128]{1,0:T(8,128)S(1)} %slice_add_fusion.25.mine_ref), channel_id=1, source_target_pairs={{0,8},{1,5},{2,10},{3,7},{4,12},{5,1},{6,14},{7,3},{8,0},{9,13},{1... | collective-permute-start | bytes 589832 | tf_op jit(solution)/shard_map/ppermute | solution.py:426
  45.0 7.2 %collective-permute-start.8 = (f32[384,128]{1,0:T(8,128)S(1)}, f32[384,128]{1,0:T(8,128)S(1)}, u32[]{:S(2)}, u32[]{:S(2)}) collective-permute-start(f32[384,128]{1,0:T(8,128)S(1)} %slice_add_fusion.24.mine_ref), channel_id=1, source_target_pairs={{0,4},{1,9},{2,6},{3,11},{4,0},{5,13},{6,2},{7,15},{8,12},{9,1},{1... | collective-permute-start | bytes 589832 | tf_op jit(solution)/shard_map/ppermute | solution.py:426
  50.7 9.1 %collective-permute-start.7 = (f32[768,128]{1,0:T(8,128)S(1)}, f32[768,128]{1,0:T(8,128)S(1)}, u32[]{:S(2)}, u32[]{:S(2)}) collective-permute-start(f32[768,128]{1,0:T(8,128)S(1)} %pad_maximum_fusion), channel_id=1, source_target_pairs={{0,4},{1,9},{2,6},{3,11},{4,0},{5,13},{6,2},{7,15},{8,12},{9,1},{1... | collective-permute-start | bytes 1179656 | tf_op jit(solution)/shard_map/ppermute | solution.py:426
  52.2 8.8 %collective-permute-start.9 = (f32[768,128]{1,0:T(8,128)S(1)}, f32[768,128]{1,0:T(8,128)S(1)}, u32[]{:S(2)}, u32[]{:S(2)}) collective-permute-start(f32[768,128]{1,0:T(8,128)S(1)} %pad_maximum_fusion.1), channel_id=1, source_target_pairs={{0,8},{1,5},{2,10},{3,7},{4,12},{5,1},{6,14},{7,3},{8,0},{9,13},{1... | collective-permute-start | bytes 1179656 | tf_op jit(solution)/shard_map/ppermute | solution.py:426
  60.9 4.6 %collective-permute-start.10 = (f32[520,128]{1,0:T(8,128)S(1)}, f32[520,128]{1,0:T(8,128)S(1)}, u32[]{:S(2)}, u32[]{:S(2)}) collective-permute-start(f32[520,128]{1,0:T(8,128)S(1)} %get-tuple-element.120), channel_id=1, source_target_pairs={{0,1},{1,0},{2,3},{3,2},{4,5},{5,4},{6,7},{7,6},{8,9},{9,8},{10,11... | collective-permute-start | bytes 798728 | tf_op jit(solution)/shard_map/ppermute | solution.py:429
  64.0 5.3 %collective-permute-start.12 = (f32[520,128]{1,0:T(8,128)S(1)}, f32[520,128]{1,0:T(8,128)S(1)}, u32[]{:S(2)}, u32[]{:S(2)}) collective-permute-start(f32[520,128]{1,0:T(8,128)S(1)} %get-tuple-element.125), channel_id=1, source_target_pairs={{0,1},{1,0},{2,3},{3,2},{4,5},{5,4},{6,7},{7,6},{8,9},{9,8},{10,11... | collective-permute-start | bytes 798728 | tf_op jit(solution)/shard_map/ppermute | solution.py:429
  65.7 9.9 %collective-permute-start.11 = (f32[520,128]{1,0:T(8,128)S(1)}, f32[520,128]{1,0:T(8,128)S(1)}, u32[]{:S(2)}, u32[]{:S(2)}) collective-permute-start(f32[520,128]{1,0:T(8,128)S(1)} %pad_maximum_fusion.6), channel_id=1, source_target_pairs={{0,2},{1,3},{2,0},{3,1},{4,6},{5,7},{6,4},{7,5},{8,10},{9,11},{10,... | collective-permute-start | bytes 798728 | tf_op jit(solution)/shard_map/ppermute | solution.py:429
  69.4 11.2 %collective-permute-start.14 = (f32[520,128]{1,0:T(8,128)S(1)}, f32[520,128]{1,0:T(8,128)S(1)}, u32[]{:S(2)}, u32[]{:S(2)}) collective-permute-start(f32[520,128]{1,0:T(8,128)S(1)} %pad_maximum_fusion.7), channel_id=1, source_target_pairs={{0,2},{1,3},{2,0},{3,1},{4,6},{5,7},{6,4},{7,5},{8,10},{9,11},{10,... | collective-permute-start | bytes 798728 | tf_op jit(solution)/shard_map/ppermute | solution.py:429
  75.6 5.2 %collective-permute-start.13 = (f32[512,128]{1,0:T(8,128)S(1)}, f32[512,128]{1,0:T(8,128)S(1)}, u32[]{:S(2)}, u32[]{:S(2)}) collective-permute-start(f32[512,128]{1,0:T(8,128)S(1)} %slice_add_fusion.11.refs_2_), channel_id=1, source_target_pairs={{0,1},{1,0},{2,3},{3,2},{4,5},{5,4},{6,7},{7,6},{8,9},{9,8},{10,11... | collective-permute-start | bytes 786440 | tf_op jit(solution)/shard_map/ppermute | solution.py:429
  80.7 3.2 %collective-permute-start.16 = (f32[512,128]{1,0:T(8,128)S(1)}, f32[512,128]{1,0:T(8,128)S(1)}, u32[]{:S(2)}, u32[]{:S(2)}) collective-permute-start(f32[512,128]{1,0:T(8,128)S(1)} %slice_add_fusion.10.refs_2_), channel_id=1, source_target_pairs={{0,1},{1,0},{2,3},{3,2},{4,5},{5,4},{6,7},{7,6},{8,9},{9,8},{10,11... | collective-permute-start | bytes 786440 | tf_op jit(solution)/shard_map/ppermute | solution.py:429
  82.2 10.6 %collective-permute-start.15 = (f32[776,128]{1,0:T(8,128)S(1)}, f32[776,128]{1,0:T(8,128)S(1)}, u32[]{:S(2)}, u32[]{:S(2)}) collective-permute-start(f32[776,128]{1,0:T(8,128)S(1)} %get-tuple-element.135), channel_id=1, source_target_pairs={{0,4},{1,9},{2,6},{3,11},{4,0},{5,13},{6,2},{7,15},{8,12},{9,1},{1... | collective-permute-start | bytes 1191944 | tf_op jit(solution)/shard_map/ppermute | solution.py:426
  85.5 8.4 %collective-permute-start.18 = (f32[776,128]{1,0:T(8,128)S(1)}, f32[776,128]{1,0:T(8,128)S(1)}, u32[]{:S(2)}, u32[]{:S(2)}) collective-permute-start(f32[776,128]{1,0:T(8,128)S(1)} %get-tuple-element.137), channel_id=1, source_target_pairs={{0,8},{1,5},{2,10},{3,7},{4,12},{5,1},{6,14},{7,3},{8,0},{9,13},{1... | collective-permute-start | bytes 1191944 | tf_op jit(solution)/shard_map/ppermute | solution.py:426
  92.9 8.6 %collective-permute-start.17 = (f32[392,128]{1,0:T(8,128)S(1)}, f32[392,128]{1,0:T(8,128)S(1)}, u32[]{:S(2)}, u32[]{:S(2)}) collective-permute-start(f32[392,128]{1,0:T(8,128)S(1)} %pad_maximum_fusion.14), channel_id=1, source_target_pairs={{0,8},{1,5},{2,10},{3,7},{4,12},{5,1},{6,14},{7,3},{8,0},{9,13},{1... | collective-permute-start | bytes 602120 | tf_op jit(solution)/shard_map/ppermute | solution.py:426
  94.0 7.7 %collective-permute-start.20 = (f32[392,128]{1,0:T(8,128)S(1)}, f32[392,128]{1,0:T(8,128)S(1)}, u32[]{:S(2)}, u32[]{:S(2)}) collective-permute-start(f32[392,128]{1,0:T(8,128)S(1)} %pad_maximum_fusion.15), channel_id=1, source_target_pairs={{0,4},{1,9},{2,6},{3,11},{4,0},{5,13},{6,2},{7,15},{8,12},{9,1},{1... | collective-permute-start | bytes 602120 | tf_op jit(solution)/shard_map/ppermute | solution.py:426
  101.6 13.7 %collective-permute-start.19 = (f32[392,128]{1,0:T(8,128)S(1)}, f32[392,128]{1,0:T(8,128)S(1)}, u32[]{:S(2)}, u32[]{:S(2)}) collective-permute-start(f32[392,128]{1,0:T(8,128)S(1)} %pad_maximum_fusion.16), channel_id=1, source_target_pairs={{0,16},{1,17},{2,18},{3,19},{4,20},{5,21},{6,22},{7,23},{8,24},{9,... | collective-permute-start | bytes 602120 | tf_op jit(solution)/shard_map/ppermute | solution.py:426
  101.7 15.7 %collective-permute-start.22 = (f32[392,128]{1,0:T(8,128)S(1)}, f32[392,128]{1,0:T(8,128)S(1)}, u32[]{:S(2)}, u32[]{:S(2)}) collective-permute-start(f32[392,128]{1,0:T(8,128)S(1)} %pad_maximum_fusion.17), channel_id=1, source_target_pairs={{0,16},{1,17},{2,18},{3,19},{4,20},{5,21},{6,22},{7,23},{8,24},{9,... | collective-permute-start | bytes 602120 | tf_op jit(solution)/shard_map/ppermute | solution.py:426
  115.3 7.8 %collective-permute-start.21 = (f32[384,128]{1,0:T(8,128)S(1)}, f32[384,128]{1,0:T(8,128)S(1)}, u32[]{:S(2)}, u32[]{:S(2)}) collective-permute-start(f32[384,128]{1,0:T(8,128)S(1)} %slice_add_fusion.23.mine_ref), channel_id=1, source_target_pairs={{0,8},{1,5},{2,10},{3,7},{4,12},{5,1},{6,14},{7,3},{8,0},{9,13},{1... | collective-permute-start | bytes 589832 | tf_op jit(solution)/shard_map/ppermute | solution.py:426
  117.5 7.4 %collective-permute-start.24 = (f32[384,128]{1,0:T(8,128)S(1)}, f32[384,128]{1,0:T(8,128)S(1)}, u32[]{:S(2)}, u32[]{:S(2)}) collective-permute-start(f32[384,128]{1,0:T(8,128)S(1)} %slice_add_fusion.22.mine_ref), channel_id=1, source_target_pairs={{0,4},{1,9},{2,6},{3,11},{4,0},{5,13},{6,2},{7,15},{8,12},{9,1},{1... | collective-permute-start | bytes 589832 | tf_op jit(solution)/shard_map/ppermute | solution.py:426
  123.2 9.4 %collective-permute-start.23 = (f32[768,128]{1,0:T(8,128)S(1)}, f32[768,128]{1,0:T(8,128)S(1)}, u32[]{:S(2)}, u32[]{:S(2)}) collective-permute-start(f32[768,128]{1,0:T(8,128)S(1)} %pad_maximum_fusion.2), channel_id=1, source_target_pairs={{0,4},{1,9},{2,6},{3,11},{4,0},{5,13},{6,2},{7,15},{8,12},{9,1},{1... | collective-permute-start | bytes 1179656 | tf_op jit(solution)/shard_map/ppermute | solution.py:426
  124.9 8.8 %collective-permute-start.26 = (f32[768,128]{1,0:T(8,128)S(1)}, f32[768,128]{1,0:T(8,128)S(1)}, u32[]{:S(2)}, u32[]{:S(2)}) collective-permute-start(f32[768,128]{1,0:T(8,128)S(1)} %pad_maximum_fusion.3), channel_id=1, source_target_pairs={{0,8},{1,5},{2,10},{3,7},{4,12},{5,1},{6,14},{7,3},{8,0},{9,13},{1... | collective-permute-start | bytes 1179656 | tf_op jit(solution)/shard_map/ppermute | solution.py:426
  133.7 4.7 %collective-permute-start.25 = (f32[520,128]{1,0:T(8,128)S(1)}, f32[520,128]{1,0:T(8,128)S(1)}, u32[]{:S(2)}, u32[]{:S(2)}) collective-permute-start(f32[520,128]{1,0:T(8,128)S(1)} %get-tuple-element.153), channel_id=1, source_target_pairs={{0,1},{1,0},{2,3},{3,2},{4,5},{5,4},{6,7},{7,6},{8,9},{9,8},{10,11... | collective-permute-start | bytes 798728 | tf_op jit(solution)/shard_map/ppermute | solution.py:429
  136.8 4.4 %collective-permute-start.28 = (f32[520,128]{1,0:T(8,128)S(1)}, f32[520,128]{1,0:T(8,128)S(1)}, u32[]{:S(2)}, u32[]{:S(2)}) collective-permute-start(f32[520,128]{1,0:T(8,128)S(1)} %get-tuple-element.160), channel_id=1, source_target_pairs={{0,1},{1,0},{2,3},{3,2},{4,5},{5,4},{6,7},{7,6},{8,9},{9,8},{10,11... | collective-permute-start | bytes 798728 | tf_op jit(solution)/shard_map/ppermute | solution.py:429
  138.4 9.3 %collective-permute-start.27 = (f32[520,128]{1,0:T(8,128)S(1)}, f32[520,128]{1,0:T(8,128)S(1)}, u32[]{:S(2)}, u32[]{:S(2)}) collective-permute-start(f32[520,128]{1,0:T(8,128)S(1)} %pad_maximum_fusion.8), channel_id=1, source_target_pairs={{0,2},{1,3},{2,0},{3,1},{4,6},{5,7},{6,4},{7,5},{8,10},{9,11},{10,... | collective-permute-start | bytes 798728 | tf_op jit(solution)/shard_map/ppermute | solution.py:429
  141.3 11.2 %collective-permute-start.30 = (f32[520,128]{1,0:T(8,128)S(1)}, f32[520,128]{1,0:T(8,128)S(1)}, u32[]{:S(2)}, u32[]{:S(2)}) collective-permute-start(f32[520,128]{1,0:T(8,128)S(1)} %pad_maximum_fusion.9), channel_id=1, source_target_pairs={{0,2},{1,3},{2,0},{3,1},{4,6},{5,7},{6,4},{7,5},{8,10},{9,11},{10,... | collective-permute-start | bytes 798728 | tf_op jit(solution)/shard_map/ppermute | solution.py:429
  147.8 4.9 %collective-permute-start.29 = (f32[512,128]{1,0:T(8,128)S(1)}, f32[512,128]{1,0:T(8,128)S(1)}, u32[]{:S(2)}, u32[]{:S(2)}) collective-permute-start(f32[512,128]{1,0:T(8,128)S(1)} %slice_add_fusion.7.refs_2_), channel_id=1, source_target_pairs={{0,1},{1,0},{2,3},{3,2},{4,5},{5,4},{6,7},{7,6},{8,9},{9,8},{10,11... | collective-permute-start | bytes 786440 | tf_op jit(solution)/shard_map/ppermute | solution.py:429
  152.5 3.2 %collective-permute-start.32 = (f32[512,128]{1,0:T(8,128)S(1)}, f32[512,128]{1,0:T(8,128)S(1)}, u32[]{:S(2)}, u32[]{:S(2)}) collective-permute-start(f32[512,128]{1,0:T(8,128)S(1)} %slice_add_fusion.6.refs_2_), channel_id=1, source_target_pairs={{0,1},{1,0},{2,3},{3,2},{4,5},{5,4},{6,7},{7,6},{8,9},{9,8},{10,11... | collective-permute-start | bytes 786440 | tf_op jit(solution)/shard_map/ppermute | solution.py:429
  154.2 10.7 %collective-permute-start.31 = (f32[776,128]{1,0:T(8,128)S(1)}, f32[776,128]{1,0:T(8,128)S(1)}, u32[]{:S(2)}, u32[]{:S(2)}) collective-permute-start(f32[776,128]{1,0:T(8,128)S(1)} %get-tuple-element.171), channel_id=1, source_target_pairs={{0,4},{1,9},{2,6},{3,11},{4,0},{5,13},{6,2},{7,15},{8,12},{9,1},{1... | collective-permute-start | bytes 1191944 | tf_op jit(solution)/shard_map/ppermute | solution.py:426
  157.3 8.4 %collective-permute-start.34 = (f32[776,128]{1,0:T(8,128)S(1)}, f32[776,128]{1,0:T(8,128)S(1)}, u32[]{:S(2)}, u32[]{:S(2)}) collective-permute-start(f32[776,128]{1,0:T(8,128)S(1)} %get-tuple-element.174), channel_id=1, source_target_pairs={{0,8},{1,5},{2,10},{3,7},{4,12},{5,1},{6,14},{7,3},{8,0},{9,13},{1... | collective-permute-start | bytes 1191944 | tf_op jit(solution)/shard_map/ppermute | solution.py:426
  164.9 9.0 %collective-permute-start.33 = (f32[392,128]{1,0:T(8,128)S(1)}, f32[392,128]{1,0:T(8,128)S(1)}, u32[]{:S(2)}, u32[]{:S(2)}) collective-permute-start(f32[392,128]{1,0:T(8,128)S(1)} %pad_maximum_fusion.18), channel_id=1, source_target_pairs={{0,8},{1,5},{2,10},{3,7},{4,12},{5,1},{6,14},{7,3},{8,0},{9,13},{1... | collective-permute-start | bytes 602120 | tf_op jit(solution)/shard_map/ppermute | solution.py:426
  165.9 8.2 %collective-permute-start.36 = (f32[392,128]{1,0:T(8,128)S(1)}, f32[392,128]{1,0:T(8,128)S(1)}, u32[]{:S(2)}, u32[]{:S(2)}) collective-permute-start(f32[392,128]{1,0:T(8,128)S(1)} %pad_maximum_fusion.19), channel_id=1, source_target_pairs={{0,4},{1,9},{2,6},{3,11},{4,0},{5,13},{6,2},{7,15},{8,12},{9,1},{1... | collective-permute-start | bytes 602120 | tf_op jit(solution)/shard_map/ppermute | solution.py:426
  174.0 13.7 %collective-permute-start.35 = (f32[392,128]{1,0:T(8,128)S(1)}, f32[392,128]{1,0:T(8,128)S(1)}, u32[]{:S(2)}, u32[]{:S(2)}) collective-permute-start(f32[392,128]{1,0:T(8,128)S(1)} %pad_maximum_fusion.20), channel_id=1, source_target_pairs={{0,16},{1,17},{2,18},{3,19},{4,20},{5,21},{6,22},{7,23},{8,24},{9,... | collective-permute-start | bytes 602120 | tf_op jit(solution)/shard_map/ppermute | solution.py:426
  174.2 15.7 %collective-permute-start.37 = (f32[392,128]{1,0:T(8,128)S(1)}, f32[392,128]{1,0:T(8,128)S(1)}, u32[]{:S(2)}, u32[]{:S(2)}) collective-permute-start(f32[392,128]{1,0:T(8,128)S(1)} %pad_maximum_fusion.21), channel_id=1, source_target_pairs={{0,16},{1,17},{2,18},{3,19},{4,20},{5,21},{6,22},{7,23},{8,24},{9,... | collective-permute-start | bytes 602120 | tf_op jit(solution)/shard_map/ppermute | solution.py:426
  187.7 7.8 %collective-permute-start.38 = (f32[384,128]{1,0:T(8,128)S(1)}, f32[384,128]{1,0:T(8,128)S(1)}, u32[]{:S(2)}, u32[]{:S(2)}) collective-permute-start(f32[384,128]{1,0:T(8,128)S(1)} %slice_add_fusion.21.refs_2_), channel_id=1, source_target_pairs={{0,8},{1,5},{2,10},{3,7},{4,12},{5,1},{6,14},{7,3},{8,0},{9,13},{1... | collective-permute-start | bytes 589832 | tf_op jit(solution)/shard_map/ppermute | solution.py:426
  189.8 7.1 %collective-permute-start.40 = (f32[384,128]{1,0:T(8,128)S(1)}, f32[384,128]{1,0:T(8,128)S(1)}, u32[]{:S(2)}, u32[]{:S(2)}) collective-permute-start(f32[384,128]{1,0:T(8,128)S(1)} %slice_add_fusion.20.refs_12_), channel_id=1, source_target_pairs={{0,4},{1,9},{2,6},{3,11},{4,0},{5,13},{6,2},{7,15},{8,12},{9,1},{1... | collective-permute-start | bytes 589832 | tf_op jit(solution)/shard_map/ppermute | solution.py:426
  195.5 9.3 %collective-permute-start.39 = (f32[768,128]{1,0:T(8,128)S(1)}, f32[768,128]{1,0:T(8,128)S(1)}, u32[]{:S(2)}, u32[]{:S(2)}) collective-permute-start(f32[768,128]{1,0:T(8,128)S(1)} %pad_maximum_fusion.4), channel_id=1, source_target_pairs={{0,4},{1,9},{2,6},{3,11},{4,0},{5,13},{6,2},{7,15},{8,12},{9,1},{1... | collective-permute-start | bytes 1179656 | tf_op jit(solution)/shard_map/ppermute | solution.py:426
  197.0 7.8 %collective-permute-start.41 = (f32[768,128]{1,0:T(8,128)S(1)}, f32[768,128]{1,0:T(8,128)S(1)}, u32[]{:S(2)}, u32[]{:S(2)}) collective-permute-start(f32[768,128]{1,0:T(8,128)S(1)} %pad_maximum_fusion.5), channel_id=1, source_target_pairs={{0,8},{1,5},{2,10},{3,7},{4,12},{5,1},{6,14},{7,3},{8,0},{9,13},{1... | collective-permute-start | bytes 1179656 | tf_op jit(solution)/shard_map/ppermute | solution.py:426

commit v19 on v17

--- a/solution.py
+++ b/solution.py
@@ -14,7 +14,7 @@
 UNITS = 4
 NORM_ROWS = 8
 UNIT_ORDERS = ((0, 1, 2, 3), (0, 2, 1, 3))
-BEHIND = 0
+BEHIND = 1
 
 tiny_eps = 1e-06
 

time: 184 us -> 190 us (1.033)
  waiting for transfers between devices: 95.9 us -> 106 us
  starting transfers between devices: 44.3 us -> 40.7 us
    ppermute x30, waiting for transfers between devices: 86.8 us -> 93.3 us  [swap_rows(): return lax.ppermute(value, ('rows', 'cols'), pairs)]
    ppermute x30, starting transfers between devices: 39.4 us -> 33.1 us  [swap_rows(): return lax.ppermute(value, ('rows', 'cols'), pairs)]
    ppermute x12, waiting for transfers between devices: 9.11 us -> 12.3 us  [swap_cols(): lax.ppermute(value, 'cols', [(i, i ^ 1 << level) for i in range(col_count)])]
    ppermute x12, starting transfers between devices: 4.86 us -> 7.55 us  [swap_cols(): lax.ppermute(value, 'cols', [(i, i ^ 1 << level) for i in range(col_count)])]
  transfers between devices with their start and end apart: 42 -> 42, of which waited for: 31 -> 32; matrix products, arithmetic and copies ran while one was open for 1% -> 1% of each run, Pallas kernels for 18% -> 17%
where the time goes in v19:
time: 190 us
  waiting for transfers between devices  106 us (56%)
  starting transfers between devices  40.7 us (21%)
  Pallas kernels  40.1 us (21%)
    ppermute x30, waiting for transfers between devices, swap_rows(): return lax.ppermute(value, ('rows', 'cols'), pairs)  93.3 us
    ppermute x30, starting transfers between devices, swap_rows(): return lax.ppermute(value, ('rows', 'cols'), pairs)  33.1 us
    pallas_call x24, Pallas kernels, product_call(): pl.pallas_call(body, in_specs=[WHOLE] * (1 + len(operands)), out_specs=[W...  32.2 us
    ppermute x12, waiting for transfers between devices, swap_cols(): lax.ppermute(value, 'cols', [(i, i ^ 1 << level) for i in range(col_count)])  12.3 us
    ppermute x12, starting transfers between devices, swap_cols(): lax.ppermute(value, 'cols', [(i, i ^ 1 << level) for i in range(col_count)])  7.55 us
    pallas_call x1, Pallas kernels, fill_dense(): pl.pallas_call(fill_kernel, in_specs=[SCALARS] * 2 + [pl.BlockSpec(memory...  4.4 us
  transfers between devices with their start and end apart: 42, of which 32 were waited for; matrix products, arithmetic and copies ran while one was open for 1% of the time, Pallas kernels for 17%

profile of v19, /device:TPU:0, one launch (start us, length us, event | category | flops | bytes accessed | tf_op | source)
XLA Modules:
  0.0 190.0 jit_solution(2432751909350479347)
XLA Ops:
  0.7 4.4 %shard_map.67 = (bf16[2048,3200]{1,0:T(8,128)(2,1)S(1)}, f32[1024,128]{1,0:T(8,128)S(1)}, f32[1024,128]{1,0:T(8,128)S(1)}) custom-call(s32[24]{0:T(128)S(1)} %fusion.place_ref, s32[1]{0:T(128)} %bitcast.1.flip_ref, s32[16,16]{1,0:T(8,128)} %pattern_in.1, s32[16]{0:T(128)} %bitcast.5, f32[2048,128]{1,0:T(8,128)} %delays_in.1, bf16[16,16,128,128]{3,2,1,0:T(8,128)(2,1)} %tiles_in.1), custom_call_target="tpu_custom_call" | custom-call | bytes 8388608 | tf_op jit(solution)/shard_map/pallas_call | solution.py:107
  6.5 3.0 %collective-permute-start = (f32[776,128]{1,0:T(8,128)S(1)}, f32[776,128]{1,0:T(8,128)S(1)}, u32[]{:S(2)}, u32[]{:S(2)}) collective-permute-start(f32[776,128]{1,0:T(8,128)S(1)} %get-tuple-element.100), channel_id=1, source_target_pairs={{0,4},{1,9},{2,6},{3,11},{4,0},{5,13},{6,2},{7,15},{8,12},{9,1},{1... | collective-permute-start | bytes 1191944 | tf_op jit(solution)/shard_map/ppermute | solution.py:427
  12.2 3.1 %collective-permute-done = f32[776,128]{1,0:T(8,128)S(1)} collective-permute-done((f32[776,128]{1,0:T(8,128)S(1)}, f32[776,128]{1,0:T(8,128)S(1)}, u32[]{:S(2)}, u32[]{:S(2)}) %collective-permute-start) | collective-permute-done | bytes 397344 | tf_op jit(solution)/shard_map/ppermute | solution.py:427
  15.4 2.7 %collective-permute-start.1 = (f32[392,128]{1,0:T(8,128)S(1)}, f32[392,128]{1,0:T(8,128)S(1)}, u32[]{:S(2)}, u32[]{:S(2)}) collective-permute-start(f32[392,128]{1,0:T(8,128)S(1)} %pad_maximum_fusion.10), channel_id=1, source_target_pairs={{0,8},{1,5},{2,10},{3,7},{4,12},{5,1},{6,14},{7,3},{8,0},{9,13},{1... | collective-permute-start | bytes 602120 | tf_op jit(solution)/shard_map/ppermute | solution.py:427
  18.1 3.7 %collective-permute-done.1 = f32[392,128]{1,0:T(8,128)S(1)} collective-permute-done((f32[392,128]{1,0:T(8,128)S(1)}, f32[392,128]{1,0:T(8,128)S(1)}, u32[]{:S(2)}, u32[]{:S(2)}) %collective-permute-start.1) | collective-permute-done | bytes 200736 | tf_op jit(solution)/shard_map/ppermute | solution.py:427
  21.9 3.8 %collective-permute-start.2 = (f32[392,128]{1,0:T(8,128)S(1)}, f32[392,128]{1,0:T(8,128)S(1)}, u32[]{:S(2)}, u32[]{:S(2)}) collective-permute-start(f32[392,128]{1,0:T(8,128)S(1)} %pad_maximum_fusion.11), channel_id=1, source_target_pairs={{0,16},{1,17},{2,18},{3,19},{4,20},{5,21},{6,22},{7,23},{8,24},{9,... | collective-permute-start | bytes 602120 | tf_op jit(solution)/shard_map/ppermute | solution.py:427
  27.3 6.1 %collective-permute-done.2 = f32[392,128]{1,0:T(8,128)S(1)} collective-permute-done((f32[392,128]{1,0:T(8,128)S(1)}, f32[392,128]{1,0:T(8,128)S(1)}, u32[]{:S(2)}, u32[]{:S(2)}) %collective-permute-start.2) | collective-permute-done | bytes 200736 | tf_op jit(solution)/shard_map/ppermute | solution.py:427
  33.9 2.7 %collective-permute-done.4 = f32[776,128]{1,0:T(8,128)S(1)} collective-permute-done((f32[776,128]{1,0:T(8,128)S(1)}, f32[776,128]{1,0:T(8,128)S(1)}, u32[]{:S(2)}, u32[]{:S(2)}) %collective-permute-start.4) | collective-permute-done | bytes 397344 | tf_op jit(solution)/shard_map/ppermute | solution.py:427
  36.7 2.8 %collective-permute-start.6 = (f32[392,128]{1,0:T(8,128)S(1)}, f32[392,128]{1,0:T(8,128)S(1)}, u32[]{:S(2)}, u32[]{:S(2)}) collective-permute-start(f32[392,128]{1,0:T(8,128)S(1)} %pad_maximum_fusion.12), channel_id=1, source_target_pairs={{0,4},{1,9},{2,6},{3,11},{4,0},{5,13},{6,2},{7,15},{8,12},{9,1},{1... | collective-permute-start | bytes 602120 | tf_op jit(solution)/shard_map/ppermute | solution.py:427
  39.5 1.7 collective-permute-done.3.inner_ref
  41.2 2.0 %collective-permute-start.5 = (f32[768,128]{1,0:T(8,128)S(1)}, f32[768,128]{1,0:T(8,128)S(1)}, u32[]{:S(2)}, u32[]{:S(2)}) collective-permute-start(f32[768,128]{1,0:T(8,128)S(1)} %pad_maximum_fusion), channel_id=1, source_target_pairs={{0,4},{1,9},{2,6},{3,11},{4,0},{5,13},{6,2},{7,15},{8,12},{9,1},{1... | collective-permute-start | bytes 1179656 | tf_op jit(solution)/shard_map/ppermute | solution.py:427
  44.4 1.9 %shard_map.72 = (f32[1024,128]{1,0:T(8,128)S(1)}, f32[8,128]{1,0:T(8,128)S(1)}, f32[768,128]{1,0:T(8,128)S(1)}) custom-call(bf16[2048,3200]{1,0:T(8,128)(2,1)S(1)} %get-tuple-element.97.refs_0_.dense_ref, f32[384,128]{1,0:T(8,128)S(1)} %collective-permute-done.3.inner_ref, f32[384,128]{1,0:T(8,128)S(1)} %slice_add_fusion.25.mine_ref, ...), custom_call_target="tpu_custom_call" | custom-call | flops 1677721600 | bytes 6553600 | tf_op jit(solution)/shard_map/pallas_call | solution.py:262
  46.3 2.8 %collective-permute-done.5.outer_ref = f32[768,128]{1,0:T(8,128)S(1)} collective-permute-done((f32[768,128]{1,0:T(8,128)S(1)}, f32[768,128]{1,0:T(8,128)S(1)}, u32[]{:S(2)}, u32[]{:S(2)}) %collective-permute-start.5) | collective-permute-done | bytes 393248 | tf_op jit(solution)/shard_map/ppermute | solution.py:427
  50.2 3.0 %collective-permute-done.7 = f32[392,128]{1,0:T(8,128)S(1)} collective-permute-done((f32[392,128]{1,0:T(8,128)S(1)}, f32[392,128]{1,0:T(8,128)S(1)}, u32[]{:S(2)}, u32[]{:S(2)}) %collective-permute-start.7) | collective-permute-done | bytes 200736 | tf_op jit(solution)/shard_map/ppermute | solution.py:427
  56.9 2.1 %collective-permute-done.10.inner_ref = f32[384,128]{1,0:T(8,128)S(1)} collective-permute-done((f32[384,128]{1,0:T(8,128)S(1)}, f32[384,128]{1,0:T(8,128)S(1)}, u32[]{:S(2)}, u32[]{:S(2)}) %collective-permute-start.10) | collective-permute-done | bytes 196640 | tf_op jit(solution)/shard_map/ppermute | solution.py:427
  59.4 3.4 %collective-permute-done.9 = f32[520,128]{1,0:T(8,128)S(1)} collective-permute-done((f32[520,128]{1,0:T(8,128)S(1)}, f32[520,128]{1,0:T(8,128)S(1)}, u32[]{:S(2)}, u32[]{:S(2)}) %collective-permute-start.9) | collective-permute-done | bytes 266272 | tf_op jit(solution)/shard_map/ppermute | solution.py:430
  63.0 1.9 %shard_map.75 = (f32[1024,128]{1,0:T(8,128)S(1)}, f32[8,128]{1,0:T(8,128)S(1)}, f32[768,128]{1,0:T(8,128)S(1)}) custom-call(bf16[2048,3200]{1,0:T(8,128)(2,1)S(1)} %get-tuple-element.97.refs_0_.dense_ref, f32[384,128]{1,0:T(8,128)S(1)} %collective-permute-done.10.inner_ref, f32[384,128]{1,0:T(8,128)S(1)} %slice_add_fusion.24.mine_ref, ...), custom_call_target="tpu_custom_call" | custom-call | flops 1677721600 | bytes 6553600 | tf_op jit(solution)/shard_map/pallas_call | solution.py:262
  64.9 2.0 %collective-permute-done.12.outer_ref = f32[768,128]{1,0:T(8,128)S(1)} collective-permute-done((f32[768,128]{1,0:T(8,128)S(1)}, f32[768,128]{1,0:T(8,128)S(1)}, u32[]{:S(2)}, u32[]{:S(2)}) %collective-permute-start.12) | collective-permute-done | bytes 393248 | tf_op jit(solution)/shard_map/ppermute | solution.py:427
  69.5 1.9 collective-permute-start.13
  74.8 2.7 %collective-permute-done.13 = f32[776,128]{1,0:T(8,128)S(1)} collective-permute-done((f32[776,128]{1,0:T(8,128)S(1)}, f32[776,128]{1,0:T(8,128)S(1)}, u32[]{:S(2)}, u32[]{:S(2)}) %collective-permute-start.13) | collective-permute-done | bytes 397344 | tf_op jit(solution)/shard_map/ppermute | solution.py:427
  77.9 3.2 %collective-permute-done.16 = f32[520,128]{1,0:T(8,128)S(1)} collective-permute-done((f32[520,128]{1,0:T(8,128)S(1)}, f32[520,128]{1,0:T(8,128)S(1)}, u32[]{:S(2)}, u32[]{:S(2)}) %collective-permute-start.16) | collective-permute-done | bytes 266272 | tf_op jit(solution)/shard_map/ppermute | solution.py:430
  81.2 2.1 %collective-permute-done.15 = f32[392,128]{1,0:T(8,128)S(1)} collective-permute-done((f32[392,128]{1,0:T(8,128)S(1)}, f32[392,128]{1,0:T(8,128)S(1)}, u32[]{:S(2)}, u32[]{:S(2)}) %collective-permute-start.15) | collective-permute-done | bytes 200736 | tf_op jit(solution)/shard_map/ppermute | solution.py:427
  83.5 1.8 collective-permute-start.17
  86.7 2.1 %collective-permute-start.20 = (f32[776,128]{1,0:T(8,128)S(1)}, f32[776,128]{1,0:T(8,128)S(1)}, u32[]{:S(2)}, u32[]{:S(2)}) collective-permute-start(f32[776,128]{1,0:T(8,128)S(1)} %get-tuple-element.139), channel_id=1, source_target_pairs={{0,8},{1,5},{2,10},{3,7},{4,12},{5,1},{6,14},{7,3},{8,0},{9,13},{1... | collective-permute-start | bytes 1191944 | tf_op jit(solution)/shard_map/ppermute | solution.py:427
  90.1 4.5 %collective-permute-done.17 = f32[392,128]{1,0:T(8,128)S(1)} collective-permute-done((f32[392,128]{1,0:T(8,128)S(1)}, f32[392,128]{1,0:T(8,128)S(1)}, u32[]{:S(2)}, u32[]{:S(2)}) %collective-permute-start.17) | collective-permute-done | bytes 200736 | tf_op jit(solution)/shard_map/ppermute | solution.py:427
  94.7 3.3 %collective-permute-done.20 = f32[776,128]{1,0:T(8,128)S(1)} collective-permute-done((f32[776,128]{1,0:T(8,128)S(1)}, f32[776,128]{1,0:T(8,128)S(1)}, u32[]{:S(2)}, u32[]{:S(2)}) %collective-permute-start.20) | collective-permute-done | bytes 397344 | tf_op jit(solution)/shard_map/ppermute | solution.py:427
  99.2 3.0 %collective-permute-done.19.inner_ref = f32[384,128]{1,0:T(8,128)S(1)} collective-permute-done((f32[384,128]{1,0:T(8,128)S(1)}, f32[384,128]{1,0:T(8,128)S(1)}, u32[]{:S(2)}, u32[]{:S(2)}) %collective-permute-start.19) | collective-permute-done | bytes 196640 | tf_op jit(solution)/shard_map/ppermute | solution.py:427
  104.4 1.9 %shard_map.82 = (f32[1024,128]{1,0:T(8,128)S(1)}, f32[8,128]{1,0:T(8,128)S(1)}, f32[768,128]{1,0:T(8,128)S(1)}) custom-call(bf16[2048,3200]{1,0:T(8,128)(2,1)S(1)} %get-tuple-element.97.refs_0_.dense_ref, f32[384,128]{1,0:T(8,128)S(1)} %collective-permute-done.19.inner_ref, f32[384,128]{1,0:T(8,128)S(1)} %slice_add_fusion.23.mine_ref, ...), custom_call_target="tpu_custom_call" | custom-call | flops 1677721600 | bytes 6553600 | tf_op jit(solution)/shard_map/pallas_call | solution.py:262
  106.3 3.8 %collective-permute-done.21.outer_ref = f32[768,128]{1,0:T(8,128)S(1)} collective-permute-done((f32[768,128]{1,0:T(8,128)S(1)}, f32[768,128]{1,0:T(8,128)S(1)}, u32[]{:S(2)}, u32[]{:S(2)}) %collective-permute-start.21) | collective-permute-done | bytes 393248 | tf_op jit(solution)/shard_map/ppermute | solution.py:427
  111.3 3.6 %collective-permute-done.24 = f32[392,128]{1,0:T(8,128)S(1)} collective-permute-done((f32[392,128]{1,0:T(8,128)S(1)}, f32[392,128]{1,0:T(8,128)S(1)}, u32[]{:S(2)}, u32[]{:S(2)}) %collective-permute-start.24) | collective-permute-done | bytes 200736 | tf_op jit(solution)/shard_map/ppermute | solution.py:427
  116.2 2.5 %collective-permute-start.25 = (f32[520,128]{1,0:T(8,128)S(1)}, f32[520,128]{1,0:T(8,128)S(1)}, u32[]{:S(2)}, u32[]{:S(2)}) collective-permute-start(f32[520,128]{1,0:T(8,128)S(1)} %pad_maximum_fusion.8), channel_id=1, source_target_pairs={{0,2},{1,3},{2,0},{3,1},{4,6},{5,7},{6,4},{7,5},{8,10},{9,11},{10,... | collective-permute-start | bytes 798728 | tf_op jit(solution)/shard_map/ppermute | solution.py:430
  118.7 2.0 %collective-permute-done.26.inner_ref = f32[384,128]{1,0:T(8,128)S(1)} collective-permute-done((f32[384,128]{1,0:T(8,128)S(1)}, f32[384,128]{1,0:T(8,128)S(1)}, u32[]{:S(2)}, u32[]{:S(2)}) %collective-permute-start.26) | collective-permute-done | bytes 196640 | tf_op jit(solution)/shard_map/ppermute | solution.py:427
  120.8 2.5 %collective-permute-done.25 = f32[520,128]{1,0:T(8,128)S(1)} collective-permute-done((f32[520,128]{1,0:T(8,128)S(1)}, f32[520,128]{1,0:T(8,128)S(1)}, u32[]{:S(2)}, u32[]{:S(2)}) %collective-permute-start.25) | collective-permute-done | bytes 266272 | tf_op jit(solution)/shard_map/ppermute | solution.py:430
  123.4 1.9 %shard_map.85 = (f32[1024,128]{1,0:T(8,128)S(1)}, f32[8,128]{1,0:T(8,128)S(1)}, f32[768,128]{1,0:T(8,128)S(1)}) custom-call(bf16[2048,3200]{1,0:T(8,128)(2,1)S(1)} %get-tuple-element.97.refs_0_.dense_ref, f32[384,128]{1,0:T(8,128)S(1)} %collective-permute-done.26.inner_ref, f32[384,128]{1,0:T(8,128)S(1)} %slice_add_fusion.22.mine_ref, ...), custom_call_target="tpu_custom_call" | custom-call | flops 1677721600 | bytes 6553600 | tf_op jit(solution)/shard_map/pallas_call | solution.py:262
  125.3 3.2 %collective-permute-done.28.outer_ref = f32[768,128]{1,0:T(8,128)S(1)} collective-permute-done((f32[768,128]{1,0:T(8,128)S(1)}, f32[768,128]{1,0:T(8,128)S(1)}, u32[]{:S(2)}, u32[]{:S(2)}) %collective-permute-start.28) | collective-permute-done | bytes 393248 | tf_op jit(solution)/shard_map/ppermute | solution.py:427
  133.7 2.5 %collective-permute-start.32 = (f32[520,128]{1,0:T(8,128)S(1)}, f32[520,128]{1,0:T(8,128)S(1)}, u32[]{:S(2)}, u32[]{:S(2)}) collective-permute-start(f32[520,128]{1,0:T(8,128)S(1)} %pad_maximum_fusion.9), channel_id=1, source_target_pairs={{0,2},{1,3},{2,0},{3,1},{4,6},{5,7},{6,4},{7,5},{8,10},{9,11},{10,... | collective-permute-start | bytes 798728 | tf_op jit(solution)/shard_map/ppermute | solution.py:430
  136.2 2.9 %collective-permute-done.29 = f32[776,128]{1,0:T(8,128)S(1)} collective-permute-done((f32[776,128]{1,0:T(8,128)S(1)}, f32[776,128]{1,0:T(8,128)S(1)}, u32[]{:S(2)}, u32[]{:S(2)}) %collective-permute-start.29) | collective-permute-done | bytes 397344 | tf_op jit(solution)/shard_map/ppermute | solution.py:427
  139.3 3.2 %collective-permute-done.32 = f32[520,128]{1,0:T(8,128)S(1)} collective-permute-done((f32[520,128]{1,0:T(8,128)S(1)}, f32[520,128]{1,0:T(8,128)S(1)}, u32[]{:S(2)}, u32[]{:S(2)}) %collective-permute-start.32) | collective-permute-done | bytes 266272 | tf_op jit(solution)/shard_map/ppermute | solution.py:430
  142.6 2.4 %collective-permute-done.31 = f32[392,128]{1,0:T(8,128)S(1)} collective-permute-done((f32[392,128]{1,0:T(8,128)S(1)}, f32[392,128]{1,0:T(8,128)S(1)}, u32[]{:S(2)}, u32[]{:S(2)}) %collective-permute-start.31) | collective-permute-done | bytes 200736 | tf_op jit(solution)/shard_map/ppermute | solution.py:427
  146.7 1.8 collective-permute-start.35
  149.8 6.0 %collective-permute-done.33 = f32[392,128]{1,0:T(8,128)S(1)} collective-permute-done((f32[392,128]{1,0:T(8,128)S(1)}, f32[392,128]{1,0:T(8,128)S(1)}, u32[]{:S(2)}, u32[]{:S(2)}) %collective-permute-start.33) | collective-permute-done | bytes 200736 | tf_op jit(solution)/shard_map/ppermute | solution.py:427
  155.9 2.8 %collective-permute-done.35 = f32[776,128]{1,0:T(8,128)S(1)} collective-permute-done((f32[776,128]{1,0:T(8,128)S(1)}, f32[776,128]{1,0:T(8,128)S(1)}, u32[]{:S(2)}, u32[]{:S(2)}) %collective-permute-start.35) | collective-permute-done | bytes 397344 | tf_op jit(solution)/shard_map/ppermute | solution.py:427
  159.7 3.2 %collective-permute-done.37.refs_1_ = f32[384,128]{1,0:T(8,128)S(1)} collective-permute-done((f32[384,128]{1,0:T(8,128)S(1)}, f32[384,128]{1,0:T(8,128)S(1)}, u32[]{:S(2)}, u32[]{:S(2)}) %collective-permute-start.37) | collective-permute-done | bytes 196640 | tf_op jit(solution)/shard_map/ppermute | solution.py:427
  166.1 8.5 %collective-permute-done.38 = f32[392,128]{1,0:T(8,128)S(1)} collective-permute-done((f32[392,128]{1,0:T(8,128)S(1)}, f32[392,128]{1,0:T(8,128)S(1)}, u32[]{:S(2)}, u32[]{:S(2)}) %collective-permute-start.38) | collective-permute-done | bytes 200736 | tf_op jit(solution)/shard_map/ppermute | solution.py:427
  176.2 4.3 %collective-permute-done.40.refs_11_ = f32[384,128]{1,0:T(8,128)S(1)} collective-permute-done((f32[384,128]{1,0:T(8,128)S(1)}, f32[384,128]{1,0:T(8,128)S(1)}, u32[]{:S(2)}, u32[]{:S(2)}) %collective-permute-start.40) | collective-permute-done | bytes 196640 | tf_op jit(solution)/shard_map/ppermute | solution.py:427
  180.5 1.7 shard_map.92
  182.8 5.5 %collective-permute-done.41.refs_10_ = f32[768,128]{1,0:T(8,128)S(1)} collective-permute-done((f32[768,128]{1,0:T(8,128)S(1)}, f32[768,128]{1,0:T(8,128)S(1)}, u32[]{:S(2)}, u32[]{:S(2)}) %collective-permute-start.41) | collective-permute-done | bytes 393248 | tf_op jit(solution)/shard_map/ppermute | solution.py:427
  188.3 1.7 shard_map.93
  (145 shorter events, 42.8 us)
Async XLA Ops:
  6.5 8.8 %collective-permute-start = (f32[776,128]{1,0:T(8,128)S(1)}, f32[776,128]{1,0:T(8,128)S(1)}, u32[]{:S(2)}, u32[]{:S(2)}) collective-permute-start(f32[776,128]{1,0:T(8,128)S(1)} %get-tuple-element.100), channel_id=1, source_target_pairs={{0,4},{1,9},{2,6},{3,11},{4,0},{5,13},{6,2},{7,15},{8,12},{9,1},{1... | collective-permute-start | bytes 1191944 | tf_op jit(solution)/shard_map/ppermute | solution.py:427
  15.4 6.4 %collective-permute-start.1 = (f32[392,128]{1,0:T(8,128)S(1)}, f32[392,128]{1,0:T(8,128)S(1)}, u32[]{:S(2)}, u32[]{:S(2)}) collective-permute-start(f32[392,128]{1,0:T(8,128)S(1)} %pad_maximum_fusion.10), channel_id=1, source_target_pairs={{0,8},{1,5},{2,10},{3,7},{4,12},{5,1},{6,14},{7,3},{8,0},{9,13},{1... | collective-permute-start | bytes 602120 | tf_op jit(solution)/shard_map/ppermute | solution.py:427
  21.9 11.6 %collective-permute-start.2 = (f32[392,128]{1,0:T(8,128)S(1)}, f32[392,128]{1,0:T(8,128)S(1)}, u32[]{:S(2)}, u32[]{:S(2)}) collective-permute-start(f32[392,128]{1,0:T(8,128)S(1)} %pad_maximum_fusion.11), channel_id=1, source_target_pairs={{0,16},{1,17},{2,18},{3,19},{4,20},{5,21},{6,22},{7,23},{8,24},{9,... | collective-permute-start | bytes 602120 | tf_op jit(solution)/shard_map/ppermute | solution.py:427
  25.6 11.0 %collective-permute-start.4 = (f32[776,128]{1,0:T(8,128)S(1)}, f32[776,128]{1,0:T(8,128)S(1)}, u32[]{:S(2)}, u32[]{:S(2)}) collective-permute-start(f32[776,128]{1,0:T(8,128)S(1)} %get-tuple-element.105), channel_id=1, source_target_pairs={{0,8},{1,5},{2,10},{3,7},{4,12},{5,1},{6,14},{7,3},{8,0},{9,13},{1... | collective-permute-start | bytes 1191944 | tf_op jit(solution)/shard_map/ppermute | solution.py:427
  33.4 7.8 %collective-permute-start.3 = (f32[384,128]{1,0:T(8,128)S(1)}, f32[384,128]{1,0:T(8,128)S(1)}, u32[]{:S(2)}, u32[]{:S(2)}) collective-permute-start(f32[384,128]{1,0:T(8,128)S(1)} %slice_add_fusion.25.mine_ref), channel_id=1, source_target_pairs={{0,8},{1,5},{2,10},{3,7},{4,12},{5,1},{6,14},{7,3},{8,0},{9,13},{1... | collective-permute-start | bytes 589832 | tf_op jit(solution)/shard_map/ppermute | solution.py:427
  36.7 6.5 %collective-permute-start.6 = (f32[392,128]{1,0:T(8,128)S(1)}, f32[392,128]{1,0:T(8,128)S(1)}, u32[]{:S(2)}, u32[]{:S(2)}) collective-permute-start(f32[392,128]{1,0:T(8,128)S(1)} %pad_maximum_fusion.12), channel_id=1, source_target_pairs={{0,4},{1,9},{2,6},{3,11},{4,0},{5,13},{6,2},{7,15},{8,12},{9,1},{1... | collective-permute-start | bytes 602120 | tf_op jit(solution)/shard_map/ppermute | solution.py:427
  41.2 7.8 %collective-permute-start.5 = (f32[768,128]{1,0:T(8,128)S(1)}, f32[768,128]{1,0:T(8,128)S(1)}, u32[]{:S(2)}, u32[]{:S(2)}) collective-permute-start(f32[768,128]{1,0:T(8,128)S(1)} %pad_maximum_fusion), channel_id=1, source_target_pairs={{0,4},{1,9},{2,6},{3,11},{4,0},{5,13},{6,2},{7,15},{8,12},{9,1},{1... | collective-permute-start | bytes 1179656 | tf_op jit(solution)/shard_map/ppermute | solution.py:427
  43.3 9.9 %collective-permute-start.7 = (f32[392,128]{1,0:T(8,128)S(1)}, f32[392,128]{1,0:T(8,128)S(1)}, u32[]{:S(2)}, u32[]{:S(2)}) collective-permute-start(f32[392,128]{1,0:T(8,128)S(1)} %pad_maximum_fusion.13), channel_id=1, source_target_pairs={{0,16},{1,17},{2,18},{3,19},{4,20},{5,21},{6,22},{7,23},{8,24},{9,... | collective-permute-start | bytes 602120 | tf_op jit(solution)/shard_map/ppermute | solution.py:427
  50.2 5.6 %collective-permute-start.8 = (f32[520,128]{1,0:T(8,128)S(1)}, f32[520,128]{1,0:T(8,128)S(1)}, u32[]{:S(2)}, u32[]{:S(2)}) collective-permute-start(f32[520,128]{1,0:T(8,128)S(1)} %get-tuple-element.118), channel_id=1, source_target_pairs={{0,1},{1,0},{2,3},{3,2},{4,5},{5,4},{6,7},{7,6},{8,9},{9,8},{10,11... | collective-permute-start | bytes 798728 | tf_op jit(solution)/shard_map/ppermute | solution.py:430
  53.3 5.7 %collective-permute-start.10 = (f32[384,128]{1,0:T(8,128)S(1)}, f32[384,128]{1,0:T(8,128)S(1)}, u32[]{:S(2)}, u32[]{:S(2)}) collective-permute-start(f32[384,128]{1,0:T(8,128)S(1)} %slice_add_fusion.24.mine_ref), channel_id=1, source_target_pairs={{0,4},{1,9},{2,6},{3,11},{4,0},{5,13},{6,2},{7,15},{8,12},{9,1},{1... | collective-permute-start | bytes 589832 | tf_op jit(solution)/shard_map/ppermute | solution.py:427
  55.9 7.0 %collective-permute-start.9 = (f32[520,128]{1,0:T(8,128)S(1)}, f32[520,128]{1,0:T(8,128)S(1)}, u32[]{:S(2)}, u32[]{:S(2)}) collective-permute-start(f32[520,128]{1,0:T(8,128)S(1)} %pad_maximum_fusion.6), channel_id=1, source_target_pairs={{0,2},{1,3},{2,0},{3,1},{4,6},{5,7},{6,4},{7,5},{8,10},{9,11},{10,... | collective-permute-start | bytes 798728 | tf_op jit(solution)/shard_map/ppermute | solution.py:430
  59.1 7.8 %collective-permute-start.12 = (f32[768,128]{1,0:T(8,128)S(1)}, f32[768,128]{1,0:T(8,128)S(1)}, u32[]{:S(2)}, u32[]{:S(2)}) collective-permute-start(f32[768,128]{1,0:T(8,128)S(1)} %pad_maximum_fusion.1), channel_id=1, source_target_pairs={{0,8},{1,5},{2,10},{3,7},{4,12},{5,1},{6,14},{7,3},{8,0},{9,13},{1... | collective-permute-start | bytes 1179656 | tf_op jit(solution)/shard_map/ppermute | solution.py:427
  62.9 5.2 %collective-permute-start.11 = (f32[512,128]{1,0:T(8,128)S(1)}, f32[512,128]{1,0:T(8,128)S(1)}, u32[]{:S(2)}, u32[]{:S(2)}) collective-permute-start(f32[512,128]{1,0:T(8,128)S(1)} %slice_add_fusion.12.refs_2_), channel_id=1, source_target_pairs={{0,1},{1,0},{2,3},{3,2},{4,5},{5,4},{6,7},{7,6},{8,9},{9,8},{10,11... | collective-permute-start | bytes 786440 | tf_op jit(solution)/shard_map/ppermute | solution.py:430
  68.0 5.7 %collective-permute-start.14 = (f32[520,128]{1,0:T(8,128)S(1)}, f32[520,128]{1,0:T(8,128)S(1)}, u32[]{:S(2)}, u32[]{:S(2)}) collective-permute-start(f32[520,128]{1,0:T(8,128)S(1)} %get-tuple-element.128), channel_id=1, source_target_pairs={{0,1},{1,0},{2,3},{3,2},{4,5},{5,4},{6,7},{7,6},{8,9},{9,8},{10,11... | collective-permute-start | bytes 798728 | tf_op jit(solution)/shard_map/ppermute | solution.py:430
  69.5 7.9 %collective-permute-start.13 = (f32[776,128]{1,0:T(8,128)S(1)}, f32[776,128]{1,0:T(8,128)S(1)}, u32[]{:S(2)}, u32[]{:S(2)}) collective-permute-start(f32[776,128]{1,0:T(8,128)S(1)} %get-tuple-element.131), channel_id=1, source_target_pairs={{0,4},{1,9},{2,6},{3,11},{4,0},{5,13},{6,2},{7,15},{8,12},{9,1},{1... | collective-permute-start | bytes 1191944 | tf_op jit(solution)/shard_map/ppermute | solution.py:427
  73.7 7.4 %collective-permute-start.16 = (f32[520,128]{1,0:T(8,128)S(1)}, f32[520,128]{1,0:T(8,128)S(1)}, u32[]{:S(2)}, u32[]{:S(2)}) collective-permute-start(f32[520,128]{1,0:T(8,128)S(1)} %pad_maximum_fusion.7), channel_id=1, source_target_pairs={{0,2},{1,3},{2,0},{3,1},{4,6},{5,7},{6,4},{7,5},{8,10},{9,11},{10,... | collective-permute-start | bytes 798728 | tf_op jit(solution)/shard_map/ppermute | solution.py:430
  77.5 5.8 %collective-permute-start.15 = (f32[392,128]{1,0:T(8,128)S(1)}, f32[392,128]{1,0:T(8,128)S(1)}, u32[]{:S(2)}, u32[]{:S(2)}) collective-permute-start(f32[392,128]{1,0:T(8,128)S(1)} %pad_maximum_fusion.14), channel_id=1, source_target_pairs={{0,8},{1,5},{2,10},{3,7},{4,12},{5,1},{6,14},{7,3},{8,0},{9,13},{1... | collective-permute-start | bytes 602120 | tf_op jit(solution)/shard_map/ppermute | solution.py:427
  81.1 4.2 %collective-permute-start.18 = (f32[512,128]{1,0:T(8,128)S(1)}, f32[512,128]{1,0:T(8,128)S(1)}, u32[]{:S(2)}, u32[]{:S(2)}) collective-permute-start(f32[512,128]{1,0:T(8,128)S(1)} %slice_add_fusion.10.refs_2_), channel_id=1, source_target_pairs={{0,1},{1,0},{2,3},{3,2},{4,5},{5,4},{6,7},{7,6},{8,9},{9,8},{10,11... | collective-permute-start | bytes 786440 | tf_op jit(solution)/shard_map/ppermute | solution.py:430
  83.5 11.1 %collective-permute-start.17 = (f32[392,128]{1,0:T(8,128)S(1)}, f32[392,128]{1,0:T(8,128)S(1)}, u32[]{:S(2)}, u32[]{:S(2)}) collective-permute-start(f32[392,128]{1,0:T(8,128)S(1)} %pad_maximum_fusion.15), channel_id=1, source_target_pairs={{0,16},{1,17},{2,18},{3,19},{4,20},{5,21},{6,22},{7,23},{8,24},{9,... | collective-permute-start | bytes 602120 | tf_op jit(solution)/shard_map/ppermute | solution.py:427
  86.7 11.3 %collective-permute-start.20 = (f32[776,128]{1,0:T(8,128)S(1)}, f32[776,128]{1,0:T(8,128)S(1)}, u32[]{:S(2)}, u32[]{:S(2)}) collective-permute-start(f32[776,128]{1,0:T(8,128)S(1)} %get-tuple-element.139), channel_id=1, source_target_pairs={{0,8},{1,5},{2,10},{3,7},{4,12},{5,1},{6,14},{7,3},{8,0},{9,13},{1... | collective-permute-start | bytes 1191944 | tf_op jit(solution)/shard_map/ppermute | solution.py:427
  94.7 7.6 %collective-permute-start.19 = (f32[384,128]{1,0:T(8,128)S(1)}, f32[384,128]{1,0:T(8,128)S(1)}, u32[]{:S(2)}, u32[]{:S(2)}) collective-permute-start(f32[384,128]{1,0:T(8,128)S(1)} %slice_add_fusion.23.mine_ref), channel_id=1, source_target_pairs={{0,8},{1,5},{2,10},{3,7},{4,12},{5,1},{6,14},{7,3},{8,0},{9,13},{1... | collective-permute-start | bytes 589832 | tf_op jit(solution)/shard_map/ppermute | solution.py:427
  98.1 5.8 %collective-permute-start.22 = (f32[392,128]{1,0:T(8,128)S(1)}, f32[392,128]{1,0:T(8,128)S(1)}, u32[]{:S(2)}, u32[]{:S(2)}) collective-permute-start(f32[392,128]{1,0:T(8,128)S(1)} %pad_maximum_fusion.16), channel_id=1, source_target_pairs={{0,4},{1,9},{2,6},{3,11},{4,0},{5,13},{6,2},{7,15},{8,12},{9,1},{1... | collective-permute-start | bytes 602120 | tf_op jit(solution)/shard_map/ppermute | solution.py:427
  102.3 7.8 %collective-permute-start.21 = (f32[768,128]{1,0:T(8,128)S(1)}, f32[768,128]{1,0:T(8,128)S(1)}, u32[]{:S(2)}, u32[]{:S(2)}) collective-permute-start(f32[768,128]{1,0:T(8,128)S(1)} %pad_maximum_fusion.2), channel_id=1, source_target_pairs={{0,4},{1,9},{2,6},{3,11},{4,0},{5,13},{6,2},{7,15},{8,12},{9,1},{1... | collective-permute-start | bytes 1179656 | tf_op jit(solution)/shard_map/ppermute | solution.py:427
  104.0 10.9 %collective-permute-start.24 = (f32[392,128]{1,0:T(8,128)S(1)}, f32[392,128]{1,0:T(8,128)S(1)}, u32[]{:S(2)}, u32[]{:S(2)}) collective-permute-start(f32[392,128]{1,0:T(8,128)S(1)} %pad_maximum_fusion.17), channel_id=1, source_target_pairs={{0,16},{1,17},{2,18},{3,19},{4,20},{5,21},{6,22},{7,23},{8,24},{9,... | collective-permute-start | bytes 602120 | tf_op jit(solution)/shard_map/ppermute | solution.py:427
  111.2 4.9 %collective-permute-start.23 = (f32[520,128]{1,0:T(8,128)S(1)}, f32[520,128]{1,0:T(8,128)S(1)}, u32[]{:S(2)}, u32[]{:S(2)}) collective-permute-start(f32[520,128]{1,0:T(8,128)S(1)} %get-tuple-element.151), channel_id=1, source_target_pairs={{0,1},{1,0},{2,3},{3,2},{4,5},{5,4},{6,7},{7,6},{8,9},{9,8},{10,11... | collective-permute-start | bytes 798728 | tf_op jit(solution)/shard_map/ppermute | solution.py:430
  115.0 5.7 %collective-permute-start.26 = (f32[384,128]{1,0:T(8,128)S(1)}, f32[384,128]{1,0:T(8,128)S(1)}, u32[]{:S(2)}, u32[]{:S(2)}) collective-permute-start(f32[384,128]{1,0:T(8,128)S(1)} %slice_add_fusion.22.mine_ref), channel_id=1, source_target_pairs={{0,4},{1,9},{2,6},{3,11},{4,0},{5,13},{6,2},{7,15},{8,12},{9,1},{1... | collective-permute-start | bytes 589832 | tf_op jit(solution)/shard_map/ppermute | solution.py:427
  116.2 7.1 %collective-permute-start.25 = (f32[520,128]{1,0:T(8,128)S(1)}, f32[520,128]{1,0:T(8,128)S(1)}, u32[]{:S(2)}, u32[]{:S(2)}) collective-permute-start(f32[520,128]{1,0:T(8,128)S(1)} %pad_maximum_fusion.8), channel_id=1, source_target_pairs={{0,2},{1,3},{2,0},{3,1},{4,6},{5,7},{6,4},{7,5},{8,10},{9,11},{10,... | collective-permute-start | bytes 798728 | tf_op jit(solution)/shard_map/ppermute | solution.py:430
  120.7 7.8 %collective-permute-start.28 = (f32[768,128]{1,0:T(8,128)S(1)}, f32[768,128]{1,0:T(8,128)S(1)}, u32[]{:S(2)}, u32[]{:S(2)}) collective-permute-start(f32[768,128]{1,0:T(8,128)S(1)} %pad_maximum_fusion.3), channel_id=1, source_target_pairs={{0,8},{1,5},{2,10},{3,7},{4,12},{5,1},{6,14},{7,3},{8,0},{9,13},{1... | collective-permute-start | bytes 1179656 | tf_op jit(solution)/shard_map/ppermute | solution.py:427
  123.3 6.4 %collective-permute-start.27 = (f32[512,128]{1,0:T(8,128)S(1)}, f32[512,128]{1,0:T(8,128)S(1)}, u32[]{:S(2)}, u32[]{:S(2)}) collective-permute-start(f32[512,128]{1,0:T(8,128)S(1)} %slice_add_fusion.8.refs_2_), channel_id=1, source_target_pairs={{0,1},{1,0},{2,3},{3,2},{4,5},{5,4},{6,7},{7,6},{8,9},{9,8},{10,11... | collective-permute-start | bytes 786440 | tf_op jit(solution)/shard_map/ppermute | solution.py:430
  129.7 4.0 %collective-permute-start.30 = (f32[520,128]{1,0:T(8,128)S(1)}, f32[520,128]{1,0:T(8,128)S(1)}, u32[]{:S(2)}, u32[]{:S(2)}) collective-permute-start(f32[520,128]{1,0:T(8,128)S(1)} %get-tuple-element.164), channel_id=1, source_target_pairs={{0,1},{1,0},{2,3},{3,2},{4,5},{5,4},{6,7},{7,6},{8,9},{9,8},{10,11... | collective-permute-start | bytes 798728 | tf_op jit(solution)/shard_map/ppermute | solution.py:430
  131.3 7.8 %collective-permute-start.29 = (f32[776,128]{1,0:T(8,128)S(1)}, f32[776,128]{1,0:T(8,128)S(1)}, u32[]{:S(2)}, u32[]{:S(2)}) collective-permute-start(f32[776,128]{1,0:T(8,128)S(1)} %get-tuple-element.167), channel_id=1, source_target_pairs={{0,4},{1,9},{2,6},{3,11},{4,0},{5,13},{6,2},{7,15},{8,12},{9,1},{1... | collective-permute-start | bytes 1191944 | tf_op jit(solution)/shard_map/ppermute | solution.py:427
  133.7 8.7 %collective-permute-start.32 = (f32[520,128]{1,0:T(8,128)S(1)}, f32[520,128]{1,0:T(8,128)S(1)}, u32[]{:S(2)}, u32[]{:S(2)}) collective-permute-start(f32[520,128]{1,0:T(8,128)S(1)} %pad_maximum_fusion.9), channel_id=1, source_target_pairs={{0,2},{1,3},{2,0},{3,1},{4,6},{5,7},{6,4},{7,5},{8,10},{9,11},{10,... | collective-permute-start | bytes 798728 | tf_op jit(solution)/shard_map/ppermute | solution.py:430
  139.2 5.8 %collective-permute-start.31 = (f32[392,128]{1,0:T(8,128)S(1)}, f32[392,128]{1,0:T(8,128)S(1)}, u32[]{:S(2)}, u32[]{:S(2)}) collective-permute-start(f32[392,128]{1,0:T(8,128)S(1)} %pad_maximum_fusion.18), channel_id=1, source_target_pairs={{0,8},{1,5},{2,10},{3,7},{4,12},{5,1},{6,14},{7,3},{8,0},{9,13},{1... | collective-permute-start | bytes 602120 | tf_op jit(solution)/shard_map/ppermute | solution.py:427
  142.5 2.6 %collective-permute-start.34 = (f32[512,128]{1,0:T(8,128)S(1)}, f32[512,128]{1,0:T(8,128)S(1)}, u32[]{:S(2)}, u32[]{:S(2)}) collective-permute-start(f32[512,128]{1,0:T(8,128)S(1)} %slice_add_fusion.6.refs_2_), channel_id=1, source_target_pairs={{0,1},{1,0},{2,3},{3,2},{4,5},{5,4},{6,7},{7,6},{8,9},{9,8},{10,11... | collective-permute-start | bytes 786440 | tf_op jit(solution)/shard_map/ppermute | solution.py:430
  145.0 10.8 %collective-permute-start.33 = (f32[392,128]{1,0:T(8,128)S(1)}, f32[392,128]{1,0:T(8,128)S(1)}, u32[]{:S(2)}, u32[]{:S(2)}) collective-permute-start(f32[392,128]{1,0:T(8,128)S(1)} %pad_maximum_fusion.19), channel_id=1, source_target_pairs={{0,16},{1,17},{2,18},{3,19},{4,20},{5,21},{6,22},{7,23},{8,24},{9,... | collective-permute-start | bytes 602120 | tf_op jit(solution)/shard_map/ppermute | solution.py:427
  146.7 12.0 %collective-permute-start.35 = (f32[776,128]{1,0:T(8,128)S(1)}, f32[776,128]{1,0:T(8,128)S(1)}, u32[]{:S(2)}, u32[]{:S(2)}) collective-permute-start(f32[776,128]{1,0:T(8,128)S(1)} %get-tuple-element.177), channel_id=1, source_target_pairs={{0,8},{1,5},{2,10},{3,7},{4,12},{5,1},{6,14},{7,3},{8,0},{9,13},{1... | collective-permute-start | bytes 1191944 | tf_op jit(solution)/shard_map/ppermute | solution.py:427
  155.8 7.1 %collective-permute-start.37 = (f32[384,128]{1,0:T(8,128)S(1)}, f32[384,128]{1,0:T(8,128)S(1)}, u32[]{:S(2)}, u32[]{:S(2)}) collective-permute-start(f32[384,128]{1,0:T(8,128)S(1)} %slice_add_fusion.21.refs_2_), channel_id=1, source_target_pairs={{0,8},{1,5},{2,10},{3,7},{4,12},{5,1},{6,14},{7,3},{8,0},{9,13},{1... | collective-permute-start | bytes 589832 | tf_op jit(solution)/shard_map/ppermute | solution.py:427
  158.8 5.8 %collective-permute-start.36 = (f32[392,128]{1,0:T(8,128)S(1)}, f32[392,128]{1,0:T(8,128)S(1)}, u32[]{:S(2)}, u32[]{:S(2)}) collective-permute-start(f32[392,128]{1,0:T(8,128)S(1)} %pad_maximum_fusion.20), channel_id=1, source_target_pairs={{0,4},{1,9},{2,6},{3,11},{4,0},{5,13},{6,2},{7,15},{8,12},{9,1},{1... | collective-permute-start | bytes 602120 | tf_op jit(solution)/shard_map/ppermute | solution.py:427
  164.6 10.0 %collective-permute-start.38 = (f32[392,128]{1,0:T(8,128)S(1)}, f32[392,128]{1,0:T(8,128)S(1)}, u32[]{:S(2)}, u32[]{:S(2)}) collective-permute-start(f32[392,128]{1,0:T(8,128)S(1)} %pad_maximum_fusion.21), channel_id=1, source_target_pairs={{0,16},{1,17},{2,18},{3,19},{4,20},{5,21},{6,22},{7,23},{8,24},{9,... | collective-permute-start | bytes 602120 | tf_op jit(solution)/shard_map/ppermute | solution.py:427
  164.7 11.4 %collective-permute-start.39 = (f32[768,128]{1,0:T(8,128)S(1)}, f32[768,128]{1,0:T(8,128)S(1)}, u32[]{:S(2)}, u32[]{:S(2)}) collective-permute-start(f32[768,128]{1,0:T(8,128)S(1)} %pad_maximum_fusion.4), channel_id=1, source_target_pairs={{0,4},{1,9},{2,6},{3,11},{4,0},{5,13},{6,2},{7,15},{8,12},{9,1},{1... | collective-permute-start | bytes 1179656 | tf_op jit(solution)/shard_map/ppermute | solution.py:427
  174.7 5.7 %collective-permute-start.40 = (f32[384,128]{1,0:T(8,128)S(1)}, f32[384,128]{1,0:T(8,128)S(1)}, u32[]{:S(2)}, u32[]{:S(2)}) collective-permute-start(f32[384,128]{1,0:T(8,128)S(1)} %slice_add_fusion.20.refs_12_), channel_id=1, source_target_pairs={{0,4},{1,9},{2,6},{3,11},{4,0},{5,13},{6,2},{7,15},{8,12},{9,1},{1... | collective-permute-start | bytes 589832 | tf_op jit(solution)/shard_map/ppermute | solution.py:427
  180.4 7.8 %collective-permute-start.41 = (f32[768,128]{1,0:T(8,128)S(1)}, f32[768,128]{1,0:T(8,128)S(1)}, u32[]{:S(2)}, u32[]{:S(2)}) collective-permute-start(f32[768,128]{1,0:T(8,128)S(1)} %pad_maximum_fusion.5), channel_id=1, source_target_pairs={{0,8},{1,5},{2,10},{3,7},{4,12},{5,1},{6,14},{7,3},{8,0},{9,13},{1... | collective-permute-start | bytes 1179656 | tf_op jit(solution)/shard_map/ppermute | solution.py:427

commit v20 on v17

--- a/solution.py
+++ b/solution.py
@@ -61,7 +61,7 @@
 
     for position in range(row_blocks):
         fetch(position, 0).start()
-    for copy in small:
+    for copy in small[:2]:
         copy.wait()
     for position in range(row_blocks):
 
@@ -69,6 +69,33 @@
         def _():
             fetch(position, 1).start()
 
+    @pl.loop(0, row_blocks)
+    def _(position):
+        rows = pl.ds(pl.multiple_of(position * TILE, TILE), TILE)
+        dense_ref[rows, :] = jnp.zeros((TILE, dense_ref.shape[1]), dense_ref.dtype)
+
+    @pl.loop(0, row_blocks)
+    def _(position):
+        rows = pl.ds(pl.multiple_of(position * TILE, TILE), TILE)
+        block = position ^ flip
+        count = counts_ref[block]
+
+        def place(tile):
+            column = jnp.where(tile < count, place_ref[pattern_ref[block, tile]], CB_DEV)
+            lanes = pl.ds(pl.multiple_of(column * TILE, TILE), TILE)
+            dense_ref[rows, lanes] = tiles_ref[position, tile]
+
+        fetch(position, 0).wait()
+        for tile in range(half):
+            place(tile)
+
+        @pl.when(count > half)
+        def _():
+            fetch(position, 1).wait()
+            for tile in range(half, 2 * half):
+                place(tile)
+
+    small[2].wait()
     low = low_lanes((TILE, TILE))
     for pair in range(row_blocks // 2):
         source = (pair ^ (flip // 2)) * PAIR
@@ -76,28 +103,6 @@
         odd = delays_ref[pl.ds(pl.multiple_of(source + TILE, TILE), TILE), :]
         even_left_ref[rows_of(pair), :] = jnp.where(low, even, turned(odd))
         odd_left_ref[rows_of(pair), :] = jnp.where(low, turned(even), odd)
-
-    @pl.loop(0, row_blocks)
-    def _(position):
-        rows = pl.ds(pl.multiple_of(position * TILE, TILE), TILE)
-        block = position ^ flip
-        count = counts_ref[block]
-
-        def place(tile):
-            column = jnp.where(tile < count, place_ref[pattern_ref[block, tile]], CB_DEV)
-            lanes = pl.ds(pl.multiple_of(column * TILE, TILE), TILE)
-            dense_ref[rows, lanes] = tiles_ref[position, tile]
-
-        dense_ref[rows, :] = jnp.zeros((TILE, dense_ref.shape[1]), dense_ref.dtype)
-        fetch(position, 0).wait()
-        for tile in range(half):
-            place(tile)
-
-        @pl.when(count > half)
-        def _():
-            fetch(position, 1).wait()
-            for tile in range(half, 2 * half):
-                place(tile)
 
 
 def fill_dense(kernel, pattern, counts, places, flip, delays):
@@ -370,29 +375,94 @@
         store_in_order(model_ref, mask_ref[0], pair, low, values)
 
 
-def gradient_kernel(mask_ref, *refs):
-    ins, gradient_ref = refs[:-1], refs[-1]
-    chains = [ins[: len(ins) // 2], ins[len(ins) // 2 :]]
+def gathered_values(outer, own, norms):
+    factor = rotation(norms)[-1]
+    values = []
+    for half in (outer, own):
+        if half is not None:
+            parts, past_ref = half
+            vector = next_vector(parts, None, norms[-1], past_ref, norms[-2])
+            values += [factor * value for _, value, _ in vector]
+    return values
+
+
+def store_pair(ref, pair, low, ours, theirs):
+    ref[rows_of(2 * pair), :] = jnp.where(low, ours, turned(theirs))
+    ref[rows_of(2 * pair + 1), :] = jnp.where(low, turned(ours), theirs)
+
+
+def ready_kernel(outer_ref, inner_ref, mine_ref, past_ref, own_past_ref, *refs):
+    norms, refs = refs[: 2 * ITERS + 1], refs[2 * ITERS + 1 :]
+    second_inner_ref, second_mine_ref, second_past_ref, *second_norms, ready_ref, ours_ref = refs
     low = low_lanes((TILE, TILE))
-    vectors = []
-    factors = []
-    for outer_ref, inner_ref, mine_ref, past_ref, own_past_ref, *norms in chains:
-        halves = [
-            next_vector(parts, None, norms[-1], past, norms[-2])
-            for parts, past in [
-                ([(outer_ref, 2)], past_ref),
-                ([(inner_ref, 1), (mine_ref, 1)], own_past_ref),
-            ]
-        ]
-        vectors.append([value for half in halves for _, value, _ in half])
-        factors.append(rotation(norms)[-1])
-    pairs = gradient_ref.shape[0] // PAIR // UNITS
-    for pair in range(gradient_ref.shape[0] // PAIR):
-        values = []
-        for order, vector, factor in zip(UNIT_ORDERS, vectors, factors):
-            slot = order.index(pair // pairs)
-            values.append(factor * vector[slot * pairs + pair % pairs])
-        store_in_order(gradient_ref, mask_ref[0], pair, low, values)
+    ours = gathered_values(
+        ([(outer_ref, 2)], past_ref), ([(inner_ref, 1), (mine_ref, 1)], own_past_ref), norms
+    )
+    theirs = gathered_values(
+        None, ([(second_inner_ref, 1), (second_mine_ref, 1)], second_past_ref), second_norms
+    )
+    pairs = mine_ref.shape[0] // TILE
+    for slot, unit in enumerate(UNIT_ORDERS[1]):
+        start = UNIT_ORDERS[0].index(unit) * pairs
+        for pair in range(pairs):
+            if slot < 2:
+                ours_ref[rows_of(slot * pairs + pair), :] = ours[start + pair]
+            else:
+                done = (slot - 2) * pairs + pair
+                store_pair(ready_ref, done, low, ours[start + pair], theirs[done])
+
+
+def gradient_kernel(mask_ref, ready_ref, ours_ref, outer_ref, past_ref, *refs):
+    *norms, gradient_ref, last_ref, sent = refs
+    low = low_lanes((TILE, TILE))
+    size = gradient_ref.shape[0] // UNITS
+
+    def send(slot, source_ref):
+        rows = pl.ds(pl.multiple_of((UNIT_ORDERS[1][slot] ^ mask_ref[0]) * size, TILE), size)
+        source = source_ref.at[pl.ds(slot % 2 * size, size)]
+        return pltpu.make_async_copy(source, gradient_ref.at[rows], sent.at[slot])
+
+    copies = [send(slot, last_ref if slot < 2 else ready_ref) for slot in range(UNITS)]
+    for copy in copies[2:]:
+        copy.start()
+    theirs = gathered_values(([(outer_ref, 2)], past_ref), None, norms)
+    for slot, copy in enumerate(copies[:2]):
+        pairs = size // PAIR
+        for pair in range(slot * pairs, (slot + 1) * pairs):
+            store_pair(last_ref, pair, low, ours_ref[rows_of(pair), :], theirs[pair])
+        copy.start()
+    for copy in copies:
+        copy.wait()
+
+
+def gradient_of(mask, first, second):
+    (rights, norms, totals), (second_rights, second_norms, second_totals) = first, second
+    half = totals[0].shape[0]
+    cost = pl.CostEstimate(flops=0, bytes_accessed=16 * half * TILE, transcendentals=0)
+    params = pltpu.CompilerParams(vmem_limit_bytes=12 * 1024 * 1024)
+    operands = [*totals, *rights[-1], *norms]
+    operands += [*second_totals[1:], second_rights[-1][1], *second_norms]
+    ready, ours = pl.pallas_call(
+        ready_kernel,
+        in_specs=[WHOLE] * len(operands),
+        out_specs=[WHOLE] * 2,
+        out_shape=[float_rows(2 * half), float_rows(half)],
+        compiler_params=params,
+        cost_estimate=cost,
+    )(*operands)
+    operands = [ready, ours, second_totals[0], second_rights[-1][0], *second_norms]
+    return pl.pallas_call(
+        gradient_kernel,
+        in_specs=[SCALARS] + [WHOLE] * len(operands),
+        out_specs=pl.BlockSpec(memory_space=pl.ANY),
+        out_shape=float_rows(4 * half),
+        scratch_shapes=[
+            pltpu.VMEM((2 * half, TILE), jnp.float32),
+            pltpu.SemaphoreType.DMA((UNITS,)),
+        ],
+        compiler_params=params,
+        cost_estimate=cost,
+    )(mask, *operands)
 
 
 def last_call(body, mask, operands, shapes):
@@ -532,12 +602,7 @@
         [operand for rights, norms, _ in chains for operand in [*sum(rights, []), *norms]],
         [(cells, TILE), (NORM_ROWS, TILE)],
     )
-    (gradient,) = last_call(
-        gradient_kernel,
-        mask,
-        [operand for rights, norms, totals in chains for operand in [*totals, *rights[-1], *norms]],
-        [(cells, TILE)],
-    )
+    gradient = gradient_of(mask, *chains)
     return (model, gradient, misfit[0])
 
 

time: 184 us -> 184 us (level); the launches traced: 185 us -> 183 us
  no operation moved by 1% of the time
where the time goes in v20:
time: 184 us; the launch traced here: 183 us
  waiting for transfers between devices  95 us (52%)
  starting transfers between devices  43.6 us (24%)
  Pallas kernels  40.8 us (22%)
    ppermute x30, waiting for transfers between devices, swap_rows(): return lax.ppermute(value, ('rows', 'cols'), pairs)  85.5 us
    ppermute x30, starting transfers between devices, swap_rows(): return lax.ppermute(value, ('rows', 'cols'), pairs)  38 us
    pallas_call x24, Pallas kernels, product_call(): pl.pallas_call(body, in_specs=[WHOLE] * (1 + len(operands)), out_specs=[W...  32.2 us
    ppermute x12, waiting for transfers between devices, swap_cols(): lax.ppermute(value, 'cols', [(i, i ^ 1 << level) for i in range(col_count)])  9.5 us
    ppermute x12, starting transfers between devices, swap_cols(): lax.ppermute(value, 'cols', [(i, i ^ 1 << level) for i in range(col_count)])  5.64 us
    pallas_call x1, Pallas kernels, fill_dense(): pl.pallas_call(fill_kernel, in_specs=[SCALARS] * 2 + [pl.BlockSpec(memory...  5.27 us
  transfers between devices with their start and end apart: 42, of which 31 were waited for; matrix products, arithmetic and copies ran while one was open for 1% of the time, Pallas kernels for 18%

profile of v20, /device:TPU:0, one launch (start us, length us, event | category | flops | bytes accessed | tf_op | source)
XLA Modules:
  0.0 182.9 jit_solution(15924500166010046885)
XLA Ops:
  0.7 5.3 %shard_map.67 = (bf16[2048,3200]{1,0:T(8,128)(2,1)S(1)}, f32[1024,128]{1,0:T(8,128)S(1)}, f32[1024,128]{1,0:T(8,128)S(1)}) custom-call(s32[24]{0:T(128)S(1)} %fusion.place_ref, s32[1]{0:T(128)} %bitcast.1.flip_ref, s32[16,16]{1,0:T(8,128)} %pattern_in.1, s32[16]{0:T(128)} %bitcast.5, f32[2048,128]{1,0:T(8,128)} %delays_in.1, bf16[16,16,128,128]{3,2,1,0:T(8,128)(2,1)} %tiles_in.1), custom_call_target="tpu_custom_call" | custom-call | bytes 8388608 | tf_op jit(solution)/shard_map/pallas_call | solution.py:112
  5.9 1.4 shard_map.68
  7.3 1.8 collective-permute-start
  10.4 1.4 shard_map.70
  11.8 3.4 %collective-permute-done = f32[776,128]{1,0:T(8,128)S(1)} collective-permute-done((f32[776,128]{1,0:T(8,128)S(1)}, f32[776,128]{1,0:T(8,128)S(1)}, u32[]{:S(2)}, u32[]{:S(2)}) %collective-permute-start) | collective-permute-done | bytes 397344 | tf_op jit(solution)/shard_map/ppermute | solution.py:497
  15.3 3.0 %collective-permute-start.1 = (f32[392,128]{1,0:T(8,128)S(1)}, f32[392,128]{1,0:T(8,128)S(1)}, u32[]{:S(2)}, u32[]{:S(2)}) collective-permute-start(f32[392,128]{1,0:T(8,128)S(1)} %pad_maximum_fusion.10), channel_id=1, source_target_pairs={{0,8},{1,5},{2,10},{3,7},{4,12},{5,1},{6,14},{7,3},{8,0},{9,13},{1... | collective-permute-start | bytes 602120 | tf_op jit(solution)/shard_map/ppermute | solution.py:497
  19.7 2.3 %collective-permute-done.1 = f32[392,128]{1,0:T(8,128)S(1)} collective-permute-done((f32[392,128]{1,0:T(8,128)S(1)}, f32[392,128]{1,0:T(8,128)S(1)}, u32[]{:S(2)}, u32[]{:S(2)}) %collective-permute-start.1) | collective-permute-done | bytes 200736 | tf_op jit(solution)/shard_map/ppermute | solution.py:497
  22.1 2.9 %collective-permute-start.2 = (f32[392,128]{1,0:T(8,128)S(1)}, f32[392,128]{1,0:T(8,128)S(1)}, u32[]{:S(2)}, u32[]{:S(2)}) collective-permute-start(f32[392,128]{1,0:T(8,128)S(1)} %pad_maximum_fusion.11), channel_id=1, source_target_pairs={{0,16},{1,17},{2,18},{3,19},{4,20},{5,21},{6,22},{7,23},{8,24},{9,... | collective-permute-start | bytes 602120 | tf_op jit(solution)/shard_map/ppermute | solution.py:497
  25.1 8.8 %collective-permute-done.3 = f32[776,128]{1,0:T(8,128)S(1)} collective-permute-done((f32[776,128]{1,0:T(8,128)S(1)}, f32[776,128]{1,0:T(8,128)S(1)}, u32[]{:S(2)}, u32[]{:S(2)}) %collective-permute-start.3) | collective-permute-done | bytes 397344 | tf_op jit(solution)/shard_map/ppermute | solution.py:497
  34.1 1.7 collective-permute-start.4
  35.7 4.0 %collective-permute-done.5 = f32[392,128]{1,0:T(8,128)S(1)} collective-permute-done((f32[392,128]{1,0:T(8,128)S(1)}, f32[392,128]{1,0:T(8,128)S(1)}, u32[]{:S(2)}, u32[]{:S(2)}) %collective-permute-start.5) | collective-permute-done | bytes 200736 | tf_op jit(solution)/shard_map/ppermute | solution.py:497
  40.3 3.6 %collective-permute-done.4.inner_ref = f32[384,128]{1,0:T(8,128)S(1)} collective-permute-done((f32[384,128]{1,0:T(8,128)S(1)}, f32[384,128]{1,0:T(8,128)S(1)}, u32[]{:S(2)}, u32[]{:S(2)}) %collective-permute-start.4) | collective-permute-done | bytes 196640 | tf_op jit(solution)/shard_map/ppermute | solution.py:497
  44.0 2.2 %collective-permute-start.6 = (f32[768,128]{1,0:T(8,128)S(1)}, f32[768,128]{1,0:T(8,128)S(1)}, u32[]{:S(2)}, u32[]{:S(2)}) collective-permute-start(f32[768,128]{1,0:T(8,128)S(1)} %pad_maximum_fusion), channel_id=1, source_target_pairs={{0,4},{1,9},{2,6},{3,11},{4,0},{5,13},{6,2},{7,15},{8,12},{9,1},{1... | collective-permute-start | bytes 1179656 | tf_op jit(solution)/shard_map/ppermute | solution.py:497
  46.2 2.4 %collective-permute-done.7 = f32[392,128]{1,0:T(8,128)S(1)} collective-permute-done((f32[392,128]{1,0:T(8,128)S(1)}, f32[392,128]{1,0:T(8,128)S(1)}, u32[]{:S(2)}, u32[]{:S(2)}) %collective-permute-start.7) | collective-permute-done | bytes 200736 | tf_op jit(solution)/shard_map/ppermute | solution.py:497
  48.7 1.9 %shard_map.72 = (f32[1024,128]{1,0:T(8,128)S(1)}, f32[8,128]{1,0:T(8,128)S(1)}, f32[768,128]{1,0:T(8,128)S(1)}) custom-call(bf16[2048,3200]{1,0:T(8,128)(2,1)S(1)} %get-tuple-element.99.refs_0_.dense_ref, f32[384,128]{1,0:T(8,128)S(1)} %collective-permute-done.4.inner_ref, f32[384,128]{1,0:T(8,128)S(1)} %slice_add_fusion.25.mine_ref, ...), custom_call_target="tpu_custom_call" | custom-call | flops 1677721600 | bytes 6553600 | tf_op jit(solution)/shard_map/pallas_call | solution.py:267
  56.1 1.3 collective-permute-start.10
  57.5 1.9 %shard_map.75 = (f32[1024,128]{1,0:T(8,128)S(1)}, f32[8,128]{1,0:T(8,128)S(1)}, f32[768,128]{1,0:T(8,128)S(1)}) custom-call(bf16[2048,3200]{1,0:T(8,128)(2,1)S(1)} %get-tuple-element.99.refs_0_.dense_ref, f32[384,128]{1,0:T(8,128)S(1)} %collective-permute-done.8.inner_ref, f32[384,128]{1,0:T(8,128)S(1)} %slice_add_fusion.24.mine_ref, ...), custom_call_target="tpu_custom_call" | custom-call | flops 1677721600 | bytes 6553600 | tf_op jit(solution)/shard_map/pallas_call | solution.py:267
  59.4 2.8 %collective-permute-done.11.outer_ref = f32[768,128]{1,0:T(8,128)S(1)} collective-permute-done((f32[768,128]{1,0:T(8,128)S(1)}, f32[768,128]{1,0:T(8,128)S(1)}, u32[]{:S(2)}, u32[]{:S(2)}) %collective-permute-start.11) | collective-permute-done | bytes 393248 | tf_op jit(solution)/shard_map/ppermute | solution.py:497
  63.4 1.5 collective-permute-done.10
  66.1 1.6 collective-permute-start.15
  67.7 1.4 shard_map.78
  71.2 3.7 %collective-permute-done.15 = f32[520,128]{1,0:T(8,128)S(1)} collective-permute-done((f32[520,128]{1,0:T(8,128)S(1)}, f32[520,128]{1,0:T(8,128)S(1)}, u32[]{:S(2)}, u32[]{:S(2)}) %collective-permute-start.15) | collective-permute-done | bytes 266272 | tf_op jit(solution)/shard_map/ppermute | solution.py:500
  75.2 1.8 collective-permute-done.14
  77.2 1.4 shard_map.80
  78.6 2.1 %collective-permute-start.19 = (f32[776,128]{1,0:T(8,128)S(1)}, f32[776,128]{1,0:T(8,128)S(1)}, u32[]{:S(2)}, u32[]{:S(2)}) collective-permute-start(f32[776,128]{1,0:T(8,128)S(1)} %get-tuple-element.140), channel_id=1, source_target_pairs={{0,8},{1,5},{2,10},{3,7},{4,12},{5,1},{6,14},{7,3},{8,0},{9,13},{1... | collective-permute-start | bytes 1191944 | tf_op jit(solution)/shard_map/ppermute | solution.py:497
  83.0 2.6 %collective-permute-start.18 = (f32[392,128]{1,0:T(8,128)S(1)}, f32[392,128]{1,0:T(8,128)S(1)}, u32[]{:S(2)}, u32[]{:S(2)}) collective-permute-start(f32[392,128]{1,0:T(8,128)S(1)} %pad_maximum_fusion.15), channel_id=1, source_target_pairs={{0,16},{1,17},{2,18},{3,19},{4,20},{5,21},{6,22},{7,23},{8,24},{9,... | collective-permute-start | bytes 602120 | tf_op jit(solution)/shard_map/ppermute | solution.py:497
  85.6 6.6 %collective-permute-done.19 = f32[776,128]{1,0:T(8,128)S(1)} collective-permute-done((f32[776,128]{1,0:T(8,128)S(1)}, f32[776,128]{1,0:T(8,128)S(1)}, u32[]{:S(2)}, u32[]{:S(2)}) %collective-permute-start.19) | collective-permute-done | bytes 397344 | tf_op jit(solution)/shard_map/ppermute | solution.py:497
  93.1 4.2 %collective-permute-start.20 = (f32[384,128]{1,0:T(8,128)S(1)}, f32[384,128]{1,0:T(8,128)S(1)}, u32[]{:S(2)}, u32[]{:S(2)}) collective-permute-start(f32[384,128]{1,0:T(8,128)S(1)} %slice_add_fusion.23.mine_ref), channel_id=1, source_target_pairs={{0,8},{1,5},{2,10},{3,7},{4,12},{5,1},{6,14},{7,3},{8,0},{9,13},{1... | collective-permute-start | bytes 589832 | tf_op jit(solution)/shard_map/ppermute | solution.py:497
  98.1 2.6 %collective-permute-start.23 = (f32[392,128]{1,0:T(8,128)S(1)}, f32[392,128]{1,0:T(8,128)S(1)}, u32[]{:S(2)}, u32[]{:S(2)}) collective-permute-start(f32[392,128]{1,0:T(8,128)S(1)} %pad_maximum_fusion.17), channel_id=1, source_target_pairs={{0,16},{1,17},{2,18},{3,19},{4,20},{5,21},{6,22},{7,23},{8,24},{9,... | collective-permute-start | bytes 602120 | tf_op jit(solution)/shard_map/ppermute | solution.py:497
  100.7 5.2 %collective-permute-done.20.inner_ref = f32[384,128]{1,0:T(8,128)S(1)} collective-permute-done((f32[384,128]{1,0:T(8,128)S(1)}, f32[384,128]{1,0:T(8,128)S(1)}, u32[]{:S(2)}, u32[]{:S(2)}) %collective-permute-start.20) | collective-permute-done | bytes 196640 | tf_op jit(solution)/shard_map/ppermute | solution.py:497
  108.1 1.9 %shard_map.82 = (f32[1024,128]{1,0:T(8,128)S(1)}, f32[8,128]{1,0:T(8,128)S(1)}, f32[768,128]{1,0:T(8,128)S(1)}) custom-call(bf16[2048,3200]{1,0:T(8,128)(2,1)S(1)} %get-tuple-element.99.refs_0_.dense_ref, f32[384,128]{1,0:T(8,128)S(1)} %collective-permute-done.20.inner_ref, f32[384,128]{1,0:T(8,128)S(1)} %slice_add_fusion.23.mine_ref, ...), custom_call_target="tpu_custom_call" | custom-call | flops 1677721600 | bytes 6553600 | tf_op jit(solution)/shard_map/pallas_call | solution.py:267
  110.1 3.7 %collective-permute-done.22.outer_ref = f32[768,128]{1,0:T(8,128)S(1)} collective-permute-done((f32[768,128]{1,0:T(8,128)S(1)}, f32[768,128]{1,0:T(8,128)S(1)}, u32[]{:S(2)}, u32[]{:S(2)}) %collective-permute-start.22) | collective-permute-done | bytes 393248 | tf_op jit(solution)/shard_map/ppermute | solution.py:497
  117.9 1.9 %shard_map.85 = (f32[1024,128]{1,0:T(8,128)S(1)}, f32[8,128]{1,0:T(8,128)S(1)}, f32[768,128]{1,0:T(8,128)S(1)}) custom-call(bf16[2048,3200]{1,0:T(8,128)(2,1)S(1)} %get-tuple-element.99.refs_0_.dense_ref, f32[384,128]{1,0:T(8,128)S(1)} %collective-permute-done.25.inner_ref, f32[384,128]{1,0:T(8,128)S(1)} %slice_add_fusion.22.mine_ref, ...), custom_call_target="tpu_custom_call" | custom-call | flops 1677721600 | bytes 6553600 | tf_op jit(solution)/shard_map/pallas_call | solution.py:267
  119.8 4.0 %collective-permute-done.27.outer_ref = f32[768,128]{1,0:T(8,128)S(1)} collective-permute-done((f32[768,128]{1,0:T(8,128)S(1)}, f32[768,128]{1,0:T(8,128)S(1)}, u32[]{:S(2)}, u32[]{:S(2)}) %collective-permute-start.27) | collective-permute-done | bytes 393248 | tf_op jit(solution)/shard_map/ppermute | solution.py:497
  127.4 1.5 shard_map.88
  131.0 4.1 %collective-permute-done.31 = f32[520,128]{1,0:T(8,128)S(1)} collective-permute-done((f32[520,128]{1,0:T(8,128)S(1)}, f32[520,128]{1,0:T(8,128)S(1)}, u32[]{:S(2)}, u32[]{:S(2)}) %collective-permute-start.31) | collective-permute-done | bytes 266272 | tf_op jit(solution)/shard_map/ppermute | solution.py:500
  135.3 1.5 collective-permute-done.30
  137.1 1.5 shard_map.90
  138.6 1.9 %collective-permute-start.35 = (f32[776,128]{1,0:T(8,128)S(1)}, f32[776,128]{1,0:T(8,128)S(1)}, u32[]{:S(2)}, u32[]{:S(2)}) collective-permute-start(f32[776,128]{1,0:T(8,128)S(1)} %get-tuple-element.178), channel_id=1, source_target_pairs={{0,8},{1,5},{2,10},{3,7},{4,12},{5,1},{6,14},{7,3},{8,0},{9,13},{1... | collective-permute-start | bytes 1191944 | tf_op jit(solution)/shard_map/ppermute | solution.py:497
  143.6 8.2 %collective-permute-done.35 = f32[776,128]{1,0:T(8,128)S(1)} collective-permute-done((f32[776,128]{1,0:T(8,128)S(1)}, f32[776,128]{1,0:T(8,128)S(1)}, u32[]{:S(2)}, u32[]{:S(2)}) %collective-permute-start.35) | collective-permute-done | bytes 397344 | tf_op jit(solution)/shard_map/ppermute | solution.py:497
  152.6 2.9 %collective-permute-start.38 = (f32[384,128]{1,0:T(8,128)S(1)}, f32[384,128]{1,0:T(8,128)S(1)}, u32[]{:S(2)}, u32[]{:S(2)}) collective-permute-start(f32[384,128]{1,0:T(8,128)S(1)} %slice_add_fusion.21.mine_ref), channel_id=1, source_target_pairs={{0,8},{1,5},{2,10},{3,7},{4,12},{5,1},{6,14},{7,3},{8,0},{9,13},{1... | collective-permute-start | bytes 589832 | tf_op jit(solution)/shard_map/ppermute | solution.py:497
  155.5 2.1 %collective-permute-done.36 = f32[392,128]{1,0:T(8,128)S(1)} collective-permute-done((f32[392,128]{1,0:T(8,128)S(1)}, f32[392,128]{1,0:T(8,128)S(1)}, u32[]{:S(2)}, u32[]{:S(2)}) %collective-permute-start.36) | collective-permute-done | bytes 200736 | tf_op jit(solution)/shard_map/ppermute | solution.py:497
  158.7 2.6 %collective-permute-done.38.inner_ref = f32[384,128]{1,0:T(8,128)S(1)} collective-permute-done((f32[384,128]{1,0:T(8,128)S(1)}, f32[384,128]{1,0:T(8,128)S(1)}, u32[]{:S(2)}, u32[]{:S(2)}) %collective-permute-start.38) | collective-permute-done | bytes 196640 | tf_op jit(solution)/shard_map/ppermute | solution.py:497
  161.3 4.8 %collective-permute-done.37 = f32[392,128]{1,0:T(8,128)S(1)} collective-permute-done((f32[392,128]{1,0:T(8,128)S(1)}, f32[392,128]{1,0:T(8,128)S(1)}, u32[]{:S(2)}, u32[]{:S(2)}) %collective-permute-start.37) | collective-permute-done | bytes 200736 | tf_op jit(solution)/shard_map/ppermute | solution.py:497
  166.8 1.5 collective-permute-start.39
  168.3 5.4 %collective-permute-done.40.refs_5_ = f32[384,128]{1,0:T(8,128)S(1)} collective-permute-done((f32[384,128]{1,0:T(8,128)S(1)}, f32[384,128]{1,0:T(8,128)S(1)}, u32[]{:S(2)}, u32[]{:S(2)}) %collective-permute-start.40) | collective-permute-done | bytes 196640 | tf_op jit(solution)/shard_map/ppermute | solution.py:497
  173.8 1.8 shard_map.92
  176.1 4.2 %collective-permute-done.39.outer_ref = f32[768,128]{1,0:T(8,128)S(1)} collective-permute-done((f32[768,128]{1,0:T(8,128)S(1)}, f32[768,128]{1,0:T(8,128)S(1)}, u32[]{:S(2)}, u32[]{:S(2)}) %collective-permute-start.39) | collective-permute-done | bytes 393248 | tf_op jit(solution)/shard_map/ppermute | solution.py:497
  (146 shorter events, 38.7 us)
Async XLA Ops:
  7.3 7.9 %collective-permute-start = (f32[776,128]{1,0:T(8,128)S(1)}, f32[776,128]{1,0:T(8,128)S(1)}, u32[]{:S(2)}, u32[]{:S(2)}) collective-permute-start(f32[776,128]{1,0:T(8,128)S(1)} %get-tuple-element.102), channel_id=1, source_target_pairs={{0,4},{1,9},{2,6},{3,11},{4,0},{5,13},{6,2},{7,15},{8,12},{9,1},{1... | collective-permute-start | bytes 1191944 | tf_op jit(solution)/shard_map/ppermute | solution.py:497
  15.3 6.7 %collective-permute-start.1 = (f32[392,128]{1,0:T(8,128)S(1)}, f32[392,128]{1,0:T(8,128)S(1)}, u32[]{:S(2)}, u32[]{:S(2)}) collective-permute-start(f32[392,128]{1,0:T(8,128)S(1)} %pad_maximum_fusion.10), channel_id=1, source_target_pairs={{0,8},{1,5},{2,10},{3,7},{4,12},{5,1},{6,14},{7,3},{8,0},{9,13},{1... | collective-permute-start | bytes 602120 | tf_op jit(solution)/shard_map/ppermute | solution.py:497
  19.6 14.2 %collective-permute-start.3 = (f32[776,128]{1,0:T(8,128)S(1)}, f32[776,128]{1,0:T(8,128)S(1)}, u32[]{:S(2)}, u32[]{:S(2)}) collective-permute-start(f32[776,128]{1,0:T(8,128)S(1)} %get-tuple-element.106), channel_id=1, source_target_pairs={{0,8},{1,5},{2,10},{3,7},{4,12},{5,1},{6,14},{7,3},{8,0},{9,13},{1... | collective-permute-start | bytes 1191944 | tf_op jit(solution)/shard_map/ppermute | solution.py:497
  22.1 11.9 %collective-permute-start.2 = (f32[392,128]{1,0:T(8,128)S(1)}, f32[392,128]{1,0:T(8,128)S(1)}, u32[]{:S(2)}, u32[]{:S(2)}) collective-permute-start(f32[392,128]{1,0:T(8,128)S(1)} %pad_maximum_fusion.11), channel_id=1, source_target_pairs={{0,16},{1,17},{2,18},{3,19},{4,20},{5,21},{6,22},{7,23},{8,24},{9,... | collective-permute-start | bytes 602120 | tf_op jit(solution)/shard_map/ppermute | solution.py:497
  33.9 5.8 %collective-permute-start.5 = (f32[392,128]{1,0:T(8,128)S(1)}, f32[392,128]{1,0:T(8,128)S(1)}, u32[]{:S(2)}, u32[]{:S(2)}) collective-permute-start(f32[392,128]{1,0:T(8,128)S(1)} %pad_maximum_fusion.12), channel_id=1, source_target_pairs={{0,4},{1,9},{2,6},{3,11},{4,0},{5,13},{6,2},{7,15},{8,12},{9,1},{1... | collective-permute-start | bytes 602120 | tf_op jit(solution)/shard_map/ppermute | solution.py:497
  34.1 9.9 %collective-permute-start.4 = (f32[384,128]{1,0:T(8,128)S(1)}, f32[384,128]{1,0:T(8,128)S(1)}, u32[]{:S(2)}, u32[]{:S(2)}) collective-permute-start(f32[384,128]{1,0:T(8,128)S(1)} %slice_add_fusion.25.mine_ref), channel_id=1, source_target_pairs={{0,8},{1,5},{2,10},{3,7},{4,12},{5,1},{6,14},{7,3},{8,0},{9,13},{1... | collective-permute-start | bytes 589832 | tf_op jit(solution)/shard_map/ppermute | solution.py:497
  39.8 8.8 %collective-permute-start.7 = (f32[392,128]{1,0:T(8,128)S(1)}, f32[392,128]{1,0:T(8,128)S(1)}, u32[]{:S(2)}, u32[]{:S(2)}) collective-permute-start(f32[392,128]{1,0:T(8,128)S(1)} %pad_maximum_fusion.13), channel_id=1, source_target_pairs={{0,16},{1,17},{2,18},{3,19},{4,20},{5,21},{6,22},{7,23},{8,24},{9,... | collective-permute-start | bytes 602120 | tf_op jit(solution)/shard_map/ppermute | solution.py:497
  44.0 7.9 %collective-permute-start.6 = (f32[768,128]{1,0:T(8,128)S(1)}, f32[768,128]{1,0:T(8,128)S(1)}, u32[]{:S(2)}, u32[]{:S(2)}) collective-permute-start(f32[768,128]{1,0:T(8,128)S(1)} %pad_maximum_fusion), channel_id=1, source_target_pairs={{0,4},{1,9},{2,6},{3,11},{4,0},{5,13},{6,2},{7,15},{8,12},{9,1},{1... | collective-permute-start | bytes 1179656 | tf_op jit(solution)/shard_map/ppermute | solution.py:497
  48.6 5.7 %collective-permute-start.8 = (f32[384,128]{1,0:T(8,128)S(1)}, f32[384,128]{1,0:T(8,128)S(1)}, u32[]{:S(2)}, u32[]{:S(2)}) collective-permute-start(f32[384,128]{1,0:T(8,128)S(1)} %slice_add_fusion.24.mine_ref), channel_id=1, source_target_pairs={{0,4},{1,9},{2,6},{3,11},{4,0},{5,13},{6,2},{7,15},{8,12},{9,1},{1... | collective-permute-start | bytes 589832 | tf_op jit(solution)/shard_map/ppermute | solution.py:497
  53.0 3.0 %collective-permute-start.9 = (f32[520,128]{1,0:T(8,128)S(1)}, f32[520,128]{1,0:T(8,128)S(1)}, u32[]{:S(2)}, u32[]{:S(2)}) collective-permute-start(f32[520,128]{1,0:T(8,128)S(1)} %get-tuple-element.121), channel_id=1, source_target_pairs={{0,1},{1,0},{2,3},{3,2},{4,5},{5,4},{6,7},{7,6},{8,9},{9,8},{10,11... | collective-permute-start | bytes 798728 | tf_op jit(solution)/shard_map/ppermute | solution.py:500
  54.4 7.8 %collective-permute-start.11 = (f32[768,128]{1,0:T(8,128)S(1)}, f32[768,128]{1,0:T(8,128)S(1)}, u32[]{:S(2)}, u32[]{:S(2)}) collective-permute-start(f32[768,128]{1,0:T(8,128)S(1)} %pad_maximum_fusion.1), channel_id=1, source_target_pairs={{0,8},{1,5},{2,10},{3,7},{4,12},{5,1},{6,14},{7,3},{8,0},{9,13},{1... | collective-permute-start | bytes 1179656 | tf_op jit(solution)/shard_map/ppermute | solution.py:497
  56.1 8.7 %collective-permute-start.10 = (f32[520,128]{1,0:T(8,128)S(1)}, f32[520,128]{1,0:T(8,128)S(1)}, u32[]{:S(2)}, u32[]{:S(2)}) collective-permute-start(f32[520,128]{1,0:T(8,128)S(1)} %pad_maximum_fusion.6), channel_id=1, source_target_pairs={{0,2},{1,3},{2,0},{3,1},{4,6},{5,7},{6,4},{7,5},{8,10},{9,11},{10,... | collective-permute-start | bytes 798728 | tf_op jit(solution)/shard_map/ppermute | solution.py:500
  63.3 2.7 %collective-permute-start.13 = (f32[520,128]{1,0:T(8,128)S(1)}, f32[520,128]{1,0:T(8,128)S(1)}, u32[]{:S(2)}, u32[]{:S(2)}) collective-permute-start(f32[520,128]{1,0:T(8,128)S(1)} %get-tuple-element.129), channel_id=1, source_target_pairs={{0,1},{1,0},{2,3},{3,2},{4,5},{5,4},{6,7},{7,6},{8,9},{9,8},{10,11... | collective-permute-start | bytes 798728 | tf_op jit(solution)/shard_map/ppermute | solution.py:500
  64.9 2.8 %collective-permute-start.12 = (f32[512,128]{1,0:T(8,128)S(1)}, f32[512,128]{1,0:T(8,128)S(1)}, u32[]{:S(2)}, u32[]{:S(2)}) collective-permute-start(f32[512,128]{1,0:T(8,128)S(1)} %slice_add_fusion.12.refs_2_), channel_id=1, source_target_pairs={{0,1},{1,0},{2,3},{3,2},{4,5},{5,4},{6,7},{7,6},{8,9},{9,8},{10,11... | collective-permute-start | bytes 786440 | tf_op jit(solution)/shard_map/ppermute | solution.py:500
  66.1 8.9 %collective-permute-start.15 = (f32[520,128]{1,0:T(8,128)S(1)}, f32[520,128]{1,0:T(8,128)S(1)}, u32[]{:S(2)}, u32[]{:S(2)}) collective-permute-start(f32[520,128]{1,0:T(8,128)S(1)} %pad_maximum_fusion.7), channel_id=1, source_target_pairs={{0,2},{1,3},{2,0},{3,1},{4,6},{5,7},{6,4},{7,5},{8,10},{9,11},{10,... | collective-permute-start | bytes 798728 | tf_op jit(solution)/shard_map/ppermute | solution.py:500
  69.1 7.9 %collective-permute-start.14 = (f32[776,128]{1,0:T(8,128)S(1)}, f32[776,128]{1,0:T(8,128)S(1)}, u32[]{:S(2)}, u32[]{:S(2)}) collective-permute-start(f32[776,128]{1,0:T(8,128)S(1)} %get-tuple-element.136), channel_id=1, source_target_pairs={{0,4},{1,9},{2,6},{3,11},{4,0},{5,13},{6,2},{7,15},{8,12},{9,1},{1... | collective-permute-start | bytes 1191944 | tf_op jit(solution)/shard_map/ppermute | solution.py:497
  75.0 2.2 %collective-permute-start.17 = (f32[512,128]{1,0:T(8,128)S(1)}, f32[512,128]{1,0:T(8,128)S(1)}, u32[]{:S(2)}, u32[]{:S(2)}) collective-permute-start(f32[512,128]{1,0:T(8,128)S(1)} %slice_add_fusion.10.refs_2_), channel_id=1, source_target_pairs={{0,1},{1,0},{2,3},{3,2},{4,5},{5,4},{6,7},{7,6},{8,9},{9,8},{10,11... | collective-permute-start | bytes 786440 | tf_op jit(solution)/shard_map/ppermute | solution.py:500
  77.1 5.8 %collective-permute-start.16 = (f32[392,128]{1,0:T(8,128)S(1)}, f32[392,128]{1,0:T(8,128)S(1)}, u32[]{:S(2)}, u32[]{:S(2)}) collective-permute-start(f32[392,128]{1,0:T(8,128)S(1)} %pad_maximum_fusion.14), channel_id=1, source_target_pairs={{0,8},{1,5},{2,10},{3,7},{4,12},{5,1},{6,14},{7,3},{8,0},{9,13},{1... | collective-permute-start | bytes 602120 | tf_op jit(solution)/shard_map/ppermute | solution.py:497
  78.6 13.5 %collective-permute-start.19 = (f32[776,128]{1,0:T(8,128)S(1)}, f32[776,128]{1,0:T(8,128)S(1)}, u32[]{:S(2)}, u32[]{:S(2)}) collective-permute-start(f32[776,128]{1,0:T(8,128)S(1)} %get-tuple-element.140), channel_id=1, source_target_pairs={{0,8},{1,5},{2,10},{3,7},{4,12},{5,1},{6,14},{7,3},{8,0},{9,13},{1... | collective-permute-start | bytes 1191944 | tf_op jit(solution)/shard_map/ppermute | solution.py:497
  83.0 10.1 %collective-permute-start.18 = (f32[392,128]{1,0:T(8,128)S(1)}, f32[392,128]{1,0:T(8,128)S(1)}, u32[]{:S(2)}, u32[]{:S(2)}) collective-permute-start(f32[392,128]{1,0:T(8,128)S(1)} %pad_maximum_fusion.15), channel_id=1, source_target_pairs={{0,16},{1,17},{2,18},{3,19},{4,20},{5,21},{6,22},{7,23},{8,24},{9,... | collective-permute-start | bytes 602120 | tf_op jit(solution)/shard_map/ppermute | solution.py:497
  92.3 5.8 %collective-permute-start.21 = (f32[392,128]{1,0:T(8,128)S(1)}, f32[392,128]{1,0:T(8,128)S(1)}, u32[]{:S(2)}, u32[]{:S(2)}) collective-permute-start(f32[392,128]{1,0:T(8,128)S(1)} %pad_maximum_fusion.16), channel_id=1, source_target_pairs={{0,4},{1,9},{2,6},{3,11},{4,0},{5,13},{6,2},{7,15},{8,12},{9,1},{1... | collective-permute-start | bytes 602120 | tf_op jit(solution)/shard_map/ppermute | solution.py:497
  93.1 12.8 %collective-permute-start.20 = (f32[384,128]{1,0:T(8,128)S(1)}, f32[384,128]{1,0:T(8,128)S(1)}, u32[]{:S(2)}, u32[]{:S(2)}) collective-permute-start(f32[384,128]{1,0:T(8,128)S(1)} %slice_add_fusion.23.mine_ref), channel_id=1, source_target_pairs={{0,8},{1,5},{2,10},{3,7},{4,12},{5,1},{6,14},{7,3},{8,0},{9,13},{1... | collective-permute-start | bytes 589832 | tf_op jit(solution)/shard_map/ppermute | solution.py:497
  98.1 8.8 %collective-permute-start.23 = (f32[392,128]{1,0:T(8,128)S(1)}, f32[392,128]{1,0:T(8,128)S(1)}, u32[]{:S(2)}, u32[]{:S(2)}) collective-permute-start(f32[392,128]{1,0:T(8,128)S(1)} %pad_maximum_fusion.17), channel_id=1, source_target_pairs={{0,16},{1,17},{2,18},{3,19},{4,20},{5,21},{6,22},{7,23},{8,24},{9,... | collective-permute-start | bytes 602120 | tf_op jit(solution)/shard_map/ppermute | solution.py:497
  105.9 7.8 %collective-permute-start.22 = (f32[768,128]{1,0:T(8,128)S(1)}, f32[768,128]{1,0:T(8,128)S(1)}, u32[]{:S(2)}, u32[]{:S(2)}) collective-permute-start(f32[768,128]{1,0:T(8,128)S(1)} %pad_maximum_fusion.2), channel_id=1, source_target_pairs={{0,4},{1,9},{2,6},{3,11},{4,0},{5,13},{6,2},{7,15},{8,12},{9,1},{1... | collective-permute-start | bytes 1179656 | tf_op jit(solution)/shard_map/ppermute | solution.py:497
  107.0 8.9 %collective-permute-start.25 = (f32[384,128]{1,0:T(8,128)S(1)}, f32[384,128]{1,0:T(8,128)S(1)}, u32[]{:S(2)}, u32[]{:S(2)}) collective-permute-start(f32[384,128]{1,0:T(8,128)S(1)} %slice_add_fusion.22.mine_ref), channel_id=1, source_target_pairs={{0,4},{1,9},{2,6},{3,11},{4,0},{5,13},{6,2},{7,15},{8,12},{9,1},{1... | collective-permute-start | bytes 589832 | tf_op jit(solution)/shard_map/ppermute | solution.py:497
  114.9 2.1 %collective-permute-start.24 = (f32[520,128]{1,0:T(8,128)S(1)}, f32[520,128]{1,0:T(8,128)S(1)}, u32[]{:S(2)}, u32[]{:S(2)}) collective-permute-start(f32[520,128]{1,0:T(8,128)S(1)} %get-tuple-element.154), channel_id=1, source_target_pairs={{0,1},{1,0},{2,3},{3,2},{4,5},{5,4},{6,7},{7,6},{8,9},{9,8},{10,11... | collective-permute-start | bytes 798728 | tf_op jit(solution)/shard_map/ppermute | solution.py:500
  115.9 7.8 %collective-permute-start.27 = (f32[768,128]{1,0:T(8,128)S(1)}, f32[768,128]{1,0:T(8,128)S(1)}, u32[]{:S(2)}, u32[]{:S(2)}) collective-permute-start(f32[768,128]{1,0:T(8,128)S(1)} %pad_maximum_fusion.3), channel_id=1, source_target_pairs={{0,8},{1,5},{2,10},{3,7},{4,12},{5,1},{6,14},{7,3},{8,0},{9,13},{1... | collective-permute-start | bytes 1179656 | tf_op jit(solution)/shard_map/ppermute | solution.py:497
  117.1 8.0 %collective-permute-start.26 = (f32[520,128]{1,0:T(8,128)S(1)}, f32[520,128]{1,0:T(8,128)S(1)}, u32[]{:S(2)}, u32[]{:S(2)}) collective-permute-start(f32[520,128]{1,0:T(8,128)S(1)} %pad_maximum_fusion.8), channel_id=1, source_target_pairs={{0,2},{1,3},{2,0},{3,1},{4,6},{5,7},{6,4},{7,5},{8,10},{9,11},{10,... | collective-permute-start | bytes 798728 | tf_op jit(solution)/shard_map/ppermute | solution.py:500
  124.9 1.7 collective-permute-start.29
  125.1 2.3 %collective-permute-start.28 = (f32[512,128]{1,0:T(8,128)S(1)}, f32[512,128]{1,0:T(8,128)S(1)}, u32[]{:S(2)}, u32[]{:S(2)}) collective-permute-start(f32[512,128]{1,0:T(8,128)S(1)} %slice_add_fusion.8.refs_2_), channel_id=1, source_target_pairs={{0,1},{1,0},{2,3},{3,2},{4,5},{5,4},{6,7},{7,6},{8,9},{9,8},{10,11... | collective-permute-start | bytes 786440 | tf_op jit(solution)/shard_map/ppermute | solution.py:500
  126.6 8.5 %collective-permute-start.31 = (f32[520,128]{1,0:T(8,128)S(1)}, f32[520,128]{1,0:T(8,128)S(1)}, u32[]{:S(2)}, u32[]{:S(2)}) collective-permute-start(f32[520,128]{1,0:T(8,128)S(1)} %pad_maximum_fusion.9), channel_id=1, source_target_pairs={{0,2},{1,3},{2,0},{3,1},{4,6},{5,7},{6,4},{7,5},{8,10},{9,11},{10,... | collective-permute-start | bytes 798728 | tf_op jit(solution)/shard_map/ppermute | solution.py:500
  128.9 7.8 %collective-permute-start.30 = (f32[776,128]{1,0:T(8,128)S(1)}, f32[776,128]{1,0:T(8,128)S(1)}, u32[]{:S(2)}, u32[]{:S(2)}) collective-permute-start(f32[776,128]{1,0:T(8,128)S(1)} %get-tuple-element.172), channel_id=1, source_target_pairs={{0,4},{1,9},{2,6},{3,11},{4,0},{5,13},{6,2},{7,15},{8,12},{9,1},{1... | collective-permute-start | bytes 1191944 | tf_op jit(solution)/shard_map/ppermute | solution.py:497
  135.2 1.9 %collective-permute-start.33 = (f32[512,128]{1,0:T(8,128)S(1)}, f32[512,128]{1,0:T(8,128)S(1)}, u32[]{:S(2)}, u32[]{:S(2)}) collective-permute-start(f32[512,128]{1,0:T(8,128)S(1)} %slice_add_fusion.6.refs_2_), channel_id=1, source_target_pairs={{0,1},{1,0},{2,3},{3,2},{4,5},{5,4},{6,7},{7,6},{8,9},{9,8},{10,11... | collective-permute-start | bytes 786440 | tf_op jit(solution)/shard_map/ppermute | solution.py:500
  136.9 5.8 %collective-permute-start.32 = (f32[392,128]{1,0:T(8,128)S(1)}, f32[392,128]{1,0:T(8,128)S(1)}, u32[]{:S(2)}, u32[]{:S(2)}) collective-permute-start(f32[392,128]{1,0:T(8,128)S(1)} %pad_maximum_fusion.18), channel_id=1, source_target_pairs={{0,8},{1,5},{2,10},{3,7},{4,12},{5,1},{6,14},{7,3},{8,0},{9,13},{1... | collective-permute-start | bytes 602120 | tf_op jit(solution)/shard_map/ppermute | solution.py:497
  138.6 13.2 %collective-permute-start.35 = (f32[776,128]{1,0:T(8,128)S(1)}, f32[776,128]{1,0:T(8,128)S(1)}, u32[]{:S(2)}, u32[]{:S(2)}) collective-permute-start(f32[776,128]{1,0:T(8,128)S(1)} %get-tuple-element.178), channel_id=1, source_target_pairs={{0,8},{1,5},{2,10},{3,7},{4,12},{5,1},{6,14},{7,3},{8,0},{9,13},{1... | collective-permute-start | bytes 1191944 | tf_op jit(solution)/shard_map/ppermute | solution.py:497
  142.7 9.9 %collective-permute-start.34 = (f32[392,128]{1,0:T(8,128)S(1)}, f32[392,128]{1,0:T(8,128)S(1)}, u32[]{:S(2)}, u32[]{:S(2)}) collective-permute-start(f32[392,128]{1,0:T(8,128)S(1)} %pad_maximum_fusion.19), channel_id=1, source_target_pairs={{0,16},{1,17},{2,18},{3,19},{4,20},{5,21},{6,22},{7,23},{8,24},{9,... | collective-permute-start | bytes 602120 | tf_op jit(solution)/shard_map/ppermute | solution.py:497
  151.8 5.8 %collective-permute-start.36 = (f32[392,128]{1,0:T(8,128)S(1)}, f32[392,128]{1,0:T(8,128)S(1)}, u32[]{:S(2)}, u32[]{:S(2)}) collective-permute-start(f32[392,128]{1,0:T(8,128)S(1)} %pad_maximum_fusion.20), channel_id=1, source_target_pairs={{0,4},{1,9},{2,6},{3,11},{4,0},{5,13},{6,2},{7,15},{8,12},{9,1},{1... | collective-permute-start | bytes 602120 | tf_op jit(solution)/shard_map/ppermute | solution.py:497
  152.6 8.7 %collective-permute-start.38 = (f32[384,128]{1,0:T(8,128)S(1)}, f32[384,128]{1,0:T(8,128)S(1)}, u32[]{:S(2)}, u32[]{:S(2)}) collective-permute-start(f32[384,128]{1,0:T(8,128)S(1)} %slice_add_fusion.21.mine_ref), channel_id=1, source_target_pairs={{0,8},{1,5},{2,10},{3,7},{4,12},{5,1},{6,14},{7,3},{8,0},{9,13},{1... | collective-permute-start | bytes 589832 | tf_op jit(solution)/shard_map/ppermute | solution.py:497
  157.7 8.5 %collective-permute-start.37 = (f32[392,128]{1,0:T(8,128)S(1)}, f32[392,128]{1,0:T(8,128)S(1)}, u32[]{:S(2)}, u32[]{:S(2)}) collective-permute-start(f32[392,128]{1,0:T(8,128)S(1)} %pad_maximum_fusion.21), channel_id=1, source_target_pairs={{0,16},{1,17},{2,18},{3,19},{4,20},{5,21},{6,22},{7,23},{8,24},{9,... | collective-permute-start | bytes 602120 | tf_op jit(solution)/shard_map/ppermute | solution.py:497
  166.2 7.5 %collective-permute-start.40 = (f32[384,128]{1,0:T(8,128)S(1)}, f32[384,128]{1,0:T(8,128)S(1)}, u32[]{:S(2)}, u32[]{:S(2)}) collective-permute-start(f32[384,128]{1,0:T(8,128)S(1)} %slice_add_fusion.20.refs_6_), channel_id=1, source_target_pairs={{0,4},{1,9},{2,6},{3,11},{4,0},{5,13},{6,2},{7,15},{8,12},{9,1},{1... | collective-permute-start | bytes 589832 | tf_op jit(solution)/shard_map/ppermute | solution.py:497
  166.8 13.6 %collective-permute-start.39 = (f32[768,128]{1,0:T(8,128)S(1)}, f32[768,128]{1,0:T(8,128)S(1)}, u32[]{:S(2)}, u32[]{:S(2)}) collective-permute-start(f32[768,128]{1,0:T(8,128)S(1)} %pad_maximum_fusion.4), channel_id=1, source_target_pairs={{0,4},{1,9},{2,6},{3,11},{4,0},{5,13},{6,2},{7,15},{8,12},{9,1},{1... | collective-permute-start | bytes 1179656 | tf_op jit(solution)/shard_map/ppermute | solution.py:497
  173.8 7.8 %collective-permute-start.41 = (f32[768,128]{1,0:T(8,128)S(1)}, f32[768,128]{1,0:T(8,128)S(1)}, u32[]{:S(2)}, u32[]{:S(2)}) collective-permute-start(f32[768,128]{1,0:T(8,128)S(1)} %pad_maximum_fusion.5), channel_id=1, source_target_pairs={{0,8},{1,5},{2,10},{3,7},{4,12},{5,1},{6,14},{7,3},{8,0},{9,13},{1... | collective-permute-start | bytes 1179656 | tf_op jit(solution)/shard_map/ppermute | solution.py:497

commit v21 on v20

--- a/solution.py
+++ b/solution.py
@@ -146,8 +146,9 @@
 def next_vector(parts, raw_ref, scale_ref, past_ref, past_scale_ref):
     if scale_ref is not None:
         scale = norm_of(scale_ref)
+        shrink = 1.0 / scale
     if past_ref is not None:
-        past_scale = norm_of(past_scale_ref)
+        past_share = scale / norm_of(past_scale_ref)
     position = 0
     for part, units in parts:
         pairs = part.shape[0] // TILE // units
@@ -156,9 +157,9 @@
             for pair in range(pairs):
                 value = part[rows_of(unit * pairs + pair), :]
                 if scale_ref is not None:
-                    value = value / scale
+                    value = value * shrink
                 if past_ref is not None:
-                    value = value - scale * (past_ref[rows_of(position), :] / past_scale)
+                    value = value - past_share * past_ref[rows_of(position), :]
                 if raw_ref is not None:
                     raw_ref[rows_of(position), :] = value
                 squares += jnp.sum((value * value).reshape(-1, NORM_ROWS, TILE), axis=0)
@@ -209,7 +210,7 @@
     if units[1] == units[0] + 1:
         runs = [(units[0] * depth, 0, 2 * depth)]
     low = low_lanes((TILE, TILE))
-    step = 2
+    step = 4
     pairs = out_ref.shape[0] // TILE
     for pair in range(0, pairs, step):
         rows = slice((start + pair) * PAIR, (start + pair + step) * PAIR)

time: 184 us -> 184 us (level)
  waiting for transfers between devices: 95 us -> 100 us
  starting transfers between devices: 43.6 us -> 40.2 us
    ppermute x30, waiting for transfers between devices: 85.5 us -> 90.6 us  [swap_rows(): return lax.ppermute(value, ('rows', 'cols'), pairs)]
    ppermute x30, starting transfers between devices: 38 us -> 33.8 us  [swap_rows(): return lax.ppermute(value, ('rows', 'cols'), pairs)]
  transfers between devices with their start and end apart: 42 -> 42, of which waited for: 31 -> 32; matrix products, arithmetic and copies ran while one was open for 1% -> 1% of each run, Pallas kernels for 18% -> 18%
where the time goes in v21:
time: 184 us
  waiting for transfers between devices  100 us (54%)
  starting transfers between devices  40.2 us (22%)
  Pallas kernels  39.5 us (21%)
    ppermute x30, waiting for transfers between devices, swap_rows(): return lax.ppermute(value, ('rows', 'cols'), pairs)  90.6 us
    ppermute x30, starting transfers between devices, swap_rows(): return lax.ppermute(value, ('rows', 'cols'), pairs)  33.8 us
    pallas_call x24, Pallas kernels, product_call(): pl.pallas_call(body, in_specs=[WHOLE] * (1 + len(operands)), out_specs=[W...  32.2 us
    ppermute x12, waiting for transfers between devices, swap_cols(): lax.ppermute(value, 'cols', [(i, i ^ 1 << level) for i in range(col_count)])  9.63 us
    ppermute x12, starting transfers between devices, swap_cols(): lax.ppermute(value, 'cols', [(i, i ^ 1 << level) for i in range(col_count)])  6.36 us
    pallas_call x1, Pallas kernels, fill_dense(): pl.pallas_call(fill_kernel, in_specs=[SCALARS] * 2 + [pl.BlockSpec(memory...  4.01 us
  transfers between devices with their start and end apart: 42, of which 32 were waited for; matrix products, arithmetic and copies ran while one was open for 1% of the time, Pallas kernels for 18%

profile of v21, /device:TPU:0, one launch (start us, length us, event | category | flops | bytes accessed | tf_op | source)
XLA Modules:
  0.0 183.6 jit_solution(7822306493613852585)
XLA Ops:
  0.7 4.0 %shard_map.67 = (bf16[2048,3200]{1,0:T(8,128)(2,1)S(1)}, f32[1024,128]{1,0:T(8,128)S(1)}, f32[1024,128]{1,0:T(8,128)S(1)}) custom-call(s32[24]{0:T(128)S(1)} %fusion.place_ref, s32[1]{0:T(128)} %bitcast.1.flip_ref, s32[16,16]{1,0:T(8,128)} %pattern_in.1, s32[16]{0:T(128)} %bitcast.5, f32[2048,128]{1,0:T(8,128)} %delays_in.1, bf16[16,16,128,128]{3,2,1,0:T(8,128)(2,1)} %tiles_in.1), custom_call_target="tpu_custom_call" | custom-call | bytes 8388608 | tf_op jit(solution)/shard_map/pallas_call | solution.py:112
  6.1 3.0 %collective-permute-start = (f32[776,128]{1,0:T(8,128)S(1)}, f32[776,128]{1,0:T(8,128)S(1)}, u32[]{:S(2)}, u32[]{:S(2)}) collective-permute-start(f32[776,128]{1,0:T(8,128)S(1)} %get-tuple-element.102), channel_id=1, source_target_pairs={{0,4},{1,9},{2,6},{3,11},{4,0},{5,13},{6,2},{7,15},{8,12},{9,1},{1... | collective-permute-start | bytes 1191944 | tf_op jit(solution)/shard_map/ppermute | solution.py:498
  11.8 3.1 %collective-permute-done = f32[776,128]{1,0:T(8,128)S(1)} collective-permute-done((f32[776,128]{1,0:T(8,128)S(1)}, f32[776,128]{1,0:T(8,128)S(1)}, u32[]{:S(2)}, u32[]{:S(2)}) %collective-permute-start) | collective-permute-done | bytes 397344 | tf_op jit(solution)/shard_map/ppermute | solution.py:498
  15.0 3.3 %collective-permute-start.1 = (f32[392,128]{1,0:T(8,128)S(1)}, f32[392,128]{1,0:T(8,128)S(1)}, u32[]{:S(2)}, u32[]{:S(2)}) collective-permute-start(f32[392,128]{1,0:T(8,128)S(1)} %pad_maximum_fusion.10), channel_id=1, source_target_pairs={{0,8},{1,5},{2,10},{3,7},{4,12},{5,1},{6,14},{7,3},{8,0},{9,13},{1... | collective-permute-start | bytes 602120 | tf_op jit(solution)/shard_map/ppermute | solution.py:498
  19.7 2.3 %collective-permute-done.1 = f32[392,128]{1,0:T(8,128)S(1)} collective-permute-done((f32[392,128]{1,0:T(8,128)S(1)}, f32[392,128]{1,0:T(8,128)S(1)}, u32[]{:S(2)}, u32[]{:S(2)}) %collective-permute-start.1) | collective-permute-done | bytes 200736 | tf_op jit(solution)/shard_map/ppermute | solution.py:498
  22.1 3.1 %collective-permute-start.2 = (f32[392,128]{1,0:T(8,128)S(1)}, f32[392,128]{1,0:T(8,128)S(1)}, u32[]{:S(2)}, u32[]{:S(2)}) collective-permute-start(f32[392,128]{1,0:T(8,128)S(1)} %pad_maximum_fusion.11), channel_id=1, source_target_pairs={{0,16},{1,17},{2,18},{3,19},{4,20},{5,21},{6,22},{7,23},{8,24},{9,... | collective-permute-start | bytes 602120 | tf_op jit(solution)/shard_map/ppermute | solution.py:498
  25.2 8.6 %collective-permute-done.3 = f32[776,128]{1,0:T(8,128)S(1)} collective-permute-done((f32[776,128]{1,0:T(8,128)S(1)}, f32[776,128]{1,0:T(8,128)S(1)}, u32[]{:S(2)}, u32[]{:S(2)}) %collective-permute-start.3) | collective-permute-done | bytes 397344 | tf_op jit(solution)/shard_map/ppermute | solution.py:498
  35.2 1.5 collective-permute-start.4
  36.7 3.0 %collective-permute-done.5 = f32[392,128]{1,0:T(8,128)S(1)} collective-permute-done((f32[392,128]{1,0:T(8,128)S(1)}, f32[392,128]{1,0:T(8,128)S(1)}, u32[]{:S(2)}, u32[]{:S(2)}) %collective-permute-start.5) | collective-permute-done | bytes 200736 | tf_op jit(solution)/shard_map/ppermute | solution.py:498
  40.4 4.8 %collective-permute-done.4.inner_ref = f32[384,128]{1,0:T(8,128)S(1)} collective-permute-done((f32[384,128]{1,0:T(8,128)S(1)}, f32[384,128]{1,0:T(8,128)S(1)}, u32[]{:S(2)}, u32[]{:S(2)}) %collective-permute-start.4) | collective-permute-done | bytes 196640 | tf_op jit(solution)/shard_map/ppermute | solution.py:498
  46.1 2.2 %collective-permute-done.7 = f32[392,128]{1,0:T(8,128)S(1)} collective-permute-done((f32[392,128]{1,0:T(8,128)S(1)}, f32[392,128]{1,0:T(8,128)S(1)}, u32[]{:S(2)}, u32[]{:S(2)}) %collective-permute-start.7) | collective-permute-done | bytes 200736 | tf_op jit(solution)/shard_map/ppermute | solution.py:498
  49.5 1.9 %shard_map.72 = (f32[1024,128]{1,0:T(8,128)S(1)}, f32[8,128]{1,0:T(8,128)S(1)}, f32[768,128]{1,0:T(8,128)S(1)}) custom-call(bf16[2048,3200]{1,0:T(8,128)(2,1)S(1)} %get-tuple-element.99.refs_0_.dense_ref, f32[384,128]{1,0:T(8,128)S(1)} %collective-permute-done.4.inner_ref, f32[384,128]{1,0:T(8,128)S(1)} %slice_add_fusion.25.mine_ref, ...), custom_call_target="tpu_custom_call" | custom-call | flops 1677721600 | bytes 6553600 | tf_op jit(solution)/shard_map/pallas_call | solution.py:268
  51.4 1.6 collective-permute-done.6.outer_ref
  57.1 1.9 %shard_map.75 = (f32[1024,128]{1,0:T(8,128)S(1)}, f32[8,128]{1,0:T(8,128)S(1)}, f32[768,128]{1,0:T(8,128)S(1)}) custom-call(bf16[2048,3200]{1,0:T(8,128)(2,1)S(1)} %get-tuple-element.99.refs_0_.dense_ref, f32[384,128]{1,0:T(8,128)S(1)} %collective-permute-done.8.inner_ref, f32[384,128]{1,0:T(8,128)S(1)} %slice_add_fusion.24.mine_ref, ...), custom_call_target="tpu_custom_call" | custom-call | flops 1677721600 | bytes 6553600 | tf_op jit(solution)/shard_map/pallas_call | solution.py:268
  59.0 4.0 %collective-permute-done.11.outer_ref = f32[768,128]{1,0:T(8,128)S(1)} collective-permute-done((f32[768,128]{1,0:T(8,128)S(1)}, f32[768,128]{1,0:T(8,128)S(1)}, u32[]{:S(2)}, u32[]{:S(2)}) %collective-permute-start.11) | collective-permute-done | bytes 393248 | tf_op jit(solution)/shard_map/ppermute | solution.py:498
  67.4 1.4 shard_map.78
  70.9 4.0 %collective-permute-done.15 = f32[520,128]{1,0:T(8,128)S(1)} collective-permute-done((f32[520,128]{1,0:T(8,128)S(1)}, f32[520,128]{1,0:T(8,128)S(1)}, u32[]{:S(2)}, u32[]{:S(2)}) %collective-permute-start.15) | collective-permute-done | bytes 266272 | tf_op jit(solution)/shard_map/ppermute | solution.py:501
  75.2 1.6 collective-permute-done.14
  76.9 1.4 shard_map.80
  78.4 2.1 %collective-permute-start.19 = (f32[776,128]{1,0:T(8,128)S(1)}, f32[776,128]{1,0:T(8,128)S(1)}, u32[]{:S(2)}, u32[]{:S(2)}) collective-permute-start(f32[776,128]{1,0:T(8,128)S(1)} %get-tuple-element.140), channel_id=1, source_target_pairs={{0,8},{1,5},{2,10},{3,7},{4,12},{5,1},{6,14},{7,3},{8,0},{9,13},{1... | collective-permute-start | bytes 1191944 | tf_op jit(solution)/shard_map/ppermute | solution.py:498
  82.7 1.8 collective-permute-start.18
  84.5 7.4 %collective-permute-done.19 = f32[776,128]{1,0:T(8,128)S(1)} collective-permute-done((f32[776,128]{1,0:T(8,128)S(1)}, f32[776,128]{1,0:T(8,128)S(1)}, u32[]{:S(2)}, u32[]{:S(2)}) %collective-permute-start.19) | collective-permute-done | bytes 397344 | tf_op jit(solution)/shard_map/ppermute | solution.py:498
  92.6 3.6 %collective-permute-start.20 = (f32[384,128]{1,0:T(8,128)S(1)}, f32[384,128]{1,0:T(8,128)S(1)}, u32[]{:S(2)}, u32[]{:S(2)}) collective-permute-start(f32[384,128]{1,0:T(8,128)S(1)} %slice_add_fusion.23.mine_ref), channel_id=1, source_target_pairs={{0,8},{1,5},{2,10},{3,7},{4,12},{5,1},{6,14},{7,3},{8,0},{9,13},{1... | collective-permute-start | bytes 589832 | tf_op jit(solution)/shard_map/ppermute | solution.py:498
  96.2 1.5 collective-permute-done.21
  98.8 5.0 %collective-permute-done.20.inner_ref = f32[384,128]{1,0:T(8,128)S(1)} collective-permute-done((f32[384,128]{1,0:T(8,128)S(1)}, f32[384,128]{1,0:T(8,128)S(1)}, u32[]{:S(2)}, u32[]{:S(2)}) %collective-permute-start.20) | collective-permute-done | bytes 196640 | tf_op jit(solution)/shard_map/ppermute | solution.py:498
  103.8 2.3 %collective-permute-done.23 = f32[392,128]{1,0:T(8,128)S(1)} collective-permute-done((f32[392,128]{1,0:T(8,128)S(1)}, f32[392,128]{1,0:T(8,128)S(1)}, u32[]{:S(2)}, u32[]{:S(2)}) %collective-permute-start.23) | collective-permute-done | bytes 200736 | tf_op jit(solution)/shard_map/ppermute | solution.py:498
  106.6 1.9 %shard_map.82 = (f32[1024,128]{1,0:T(8,128)S(1)}, f32[8,128]{1,0:T(8,128)S(1)}, f32[768,128]{1,0:T(8,128)S(1)}) custom-call(bf16[2048,3200]{1,0:T(8,128)(2,1)S(1)} %get-tuple-element.99.refs_0_.dense_ref, f32[384,128]{1,0:T(8,128)S(1)} %collective-permute-done.20.inner_ref, f32[384,128]{1,0:T(8,128)S(1)} %slice_add_fusion.23.mine_ref, ...), custom_call_target="tpu_custom_call" | custom-call | flops 1677721600 | bytes 6553600 | tf_op jit(solution)/shard_map/pallas_call | solution.py:268
  108.5 3.1 %collective-permute-done.22.outer_ref = f32[768,128]{1,0:T(8,128)S(1)} collective-permute-done((f32[768,128]{1,0:T(8,128)S(1)}, f32[768,128]{1,0:T(8,128)S(1)}, u32[]{:S(2)}, u32[]{:S(2)}) %collective-permute-start.22) | collective-permute-done | bytes 393248 | tf_op jit(solution)/shard_map/ppermute | solution.py:498
  115.2 1.8 %collective-permute-start.26 = (f32[520,128]{1,0:T(8,128)S(1)}, f32[520,128]{1,0:T(8,128)S(1)}, u32[]{:S(2)}, u32[]{:S(2)}) collective-permute-start(f32[520,128]{1,0:T(8,128)S(1)} %pad_maximum_fusion.8), channel_id=1, source_target_pairs={{0,2},{1,3},{2,0},{3,1},{4,6},{5,7},{6,4},{7,5},{8,10},{9,11},{10,... | collective-permute-start | bytes 798728 | tf_op jit(solution)/shard_map/ppermute | solution.py:501
  117.0 1.9 %shard_map.85 = (f32[1024,128]{1,0:T(8,128)S(1)}, f32[8,128]{1,0:T(8,128)S(1)}, f32[768,128]{1,0:T(8,128)S(1)}) custom-call(bf16[2048,3200]{1,0:T(8,128)(2,1)S(1)} %get-tuple-element.99.refs_0_.dense_ref, f32[384,128]{1,0:T(8,128)S(1)} %collective-permute-done.25.inner_ref, f32[384,128]{1,0:T(8,128)S(1)} %slice_add_fusion.22.mine_ref, ...), custom_call_target="tpu_custom_call" | custom-call | flops 1677721600 | bytes 6553600 | tf_op jit(solution)/shard_map/pallas_call | solution.py:268
  118.9 2.7 %collective-permute-done.27.outer_ref = f32[768,128]{1,0:T(8,128)S(1)} collective-permute-done((f32[768,128]{1,0:T(8,128)S(1)}, f32[768,128]{1,0:T(8,128)S(1)}, u32[]{:S(2)}, u32[]{:S(2)}) %collective-permute-start.27) | collective-permute-done | bytes 393248 | tf_op jit(solution)/shard_map/ppermute | solution.py:498
  122.8 1.5 collective-permute-done.26
  125.5 1.8 collective-permute-start.31
  127.3 1.5 shard_map.88
  130.8 3.5 %collective-permute-done.31 = f32[520,128]{1,0:T(8,128)S(1)} collective-permute-done((f32[520,128]{1,0:T(8,128)S(1)}, f32[520,128]{1,0:T(8,128)S(1)}, u32[]{:S(2)}, u32[]{:S(2)}) %collective-permute-start.31) | collective-permute-done | bytes 266272 | tf_op jit(solution)/shard_map/ppermute | solution.py:501
  134.5 2.2 %collective-permute-done.30 = f32[776,128]{1,0:T(8,128)S(1)} collective-permute-done((f32[776,128]{1,0:T(8,128)S(1)}, f32[776,128]{1,0:T(8,128)S(1)}, u32[]{:S(2)}, u32[]{:S(2)}) %collective-permute-start.30) | collective-permute-done | bytes 397344 | tf_op jit(solution)/shard_map/ppermute | solution.py:498
  136.8 1.5 shard_map.90
  138.4 2.0 %collective-permute-start.35 = (f32[776,128]{1,0:T(8,128)S(1)}, f32[776,128]{1,0:T(8,128)S(1)}, u32[]{:S(2)}, u32[]{:S(2)}) collective-permute-start(f32[776,128]{1,0:T(8,128)S(1)} %get-tuple-element.178), channel_id=1, source_target_pairs={{0,8},{1,5},{2,10},{3,7},{4,12},{5,1},{6,14},{7,3},{8,0},{9,13},{1... | collective-permute-start | bytes 1191944 | tf_op jit(solution)/shard_map/ppermute | solution.py:498
  142.7 7.1 %collective-permute-done.35 = f32[776,128]{1,0:T(8,128)S(1)} collective-permute-done((f32[776,128]{1,0:T(8,128)S(1)}, f32[776,128]{1,0:T(8,128)S(1)}, u32[]{:S(2)}, u32[]{:S(2)}) %collective-permute-start.35) | collective-permute-done | bytes 397344 | tf_op jit(solution)/shard_map/ppermute | solution.py:498
  149.9 2.3 %collective-permute-start.36 = (f32[392,128]{1,0:T(8,128)S(1)}, f32[392,128]{1,0:T(8,128)S(1)}, u32[]{:S(2)}, u32[]{:S(2)}) collective-permute-start(f32[392,128]{1,0:T(8,128)S(1)} %pad_maximum_fusion.20), channel_id=1, source_target_pairs={{0,4},{1,9},{2,6},{3,11},{4,0},{5,13},{6,2},{7,15},{8,12},{9,1},{1... | collective-permute-start | bytes 602120 | tf_op jit(solution)/shard_map/ppermute | solution.py:498
  153.8 3.9 %collective-permute-done.36 = f32[392,128]{1,0:T(8,128)S(1)} collective-permute-done((f32[392,128]{1,0:T(8,128)S(1)}, f32[392,128]{1,0:T(8,128)S(1)}, u32[]{:S(2)}, u32[]{:S(2)}) %collective-permute-start.36) | collective-permute-done | bytes 200736 | tf_op jit(solution)/shard_map/ppermute | solution.py:498
  157.8 3.3 %collective-permute-done.38.inner_ref = f32[384,128]{1,0:T(8,128)S(1)} collective-permute-done((f32[384,128]{1,0:T(8,128)S(1)}, f32[384,128]{1,0:T(8,128)S(1)}, u32[]{:S(2)}, u32[]{:S(2)}) %collective-permute-start.38) | collective-permute-done | bytes 196640 | tf_op jit(solution)/shard_map/ppermute | solution.py:498
  161.1 5.5 %collective-permute-done.37 = f32[392,128]{1,0:T(8,128)S(1)} collective-permute-done((f32[392,128]{1,0:T(8,128)S(1)}, f32[392,128]{1,0:T(8,128)S(1)}, u32[]{:S(2)}, u32[]{:S(2)}) %collective-permute-start.37) | collective-permute-done | bytes 200736 | tf_op jit(solution)/shard_map/ppermute | solution.py:498
  166.9 1.8 collective-permute-start.39
  168.7 5.7 %collective-permute-done.40.refs_5_ = f32[384,128]{1,0:T(8,128)S(1)} collective-permute-done((f32[384,128]{1,0:T(8,128)S(1)}, f32[384,128]{1,0:T(8,128)S(1)}, u32[]{:S(2)}, u32[]{:S(2)}) %collective-permute-start.40) | collective-permute-done | bytes 196640 | tf_op jit(solution)/shard_map/ppermute | solution.py:498
  174.6 1.8 shard_map.92
  176.8 3.2 %collective-permute-done.39.outer_ref = f32[768,128]{1,0:T(8,128)S(1)} collective-permute-done((f32[768,128]{1,0:T(8,128)S(1)}, f32[768,128]{1,0:T(8,128)S(1)}, u32[]{:S(2)}, u32[]{:S(2)}) %collective-permute-start.39) | collective-permute-done | bytes 393248 | tf_op jit(solution)/shard_map/ppermute | solution.py:498
  180.4 1.9 %collective-permute-done.41.outer_ref = f32[768,128]{1,0:T(8,128)S(1)} collective-permute-done((f32[768,128]{1,0:T(8,128)S(1)}, f32[768,128]{1,0:T(8,128)S(1)}, u32[]{:S(2)}, u32[]{:S(2)}) %collective-permute-start.41) | collective-permute-done | bytes 393248 | tf_op jit(solution)/shard_map/ppermute | solution.py:498
  (146 shorter events, 39.3 us)
Async XLA Ops:
  6.1 8.8 %collective-permute-start = (f32[776,128]{1,0:T(8,128)S(1)}, f32[776,128]{1,0:T(8,128)S(1)}, u32[]{:S(2)}, u32[]{:S(2)}) collective-permute-start(f32[776,128]{1,0:T(8,128)S(1)} %get-tuple-element.102), channel_id=1, source_target_pairs={{0,4},{1,9},{2,6},{3,11},{4,0},{5,13},{6,2},{7,15},{8,12},{9,1},{1... | collective-permute-start | bytes 1191944 | tf_op jit(solution)/shard_map/ppermute | solution.py:498
  15.0 7.0 %collective-permute-start.1 = (f32[392,128]{1,0:T(8,128)S(1)}, f32[392,128]{1,0:T(8,128)S(1)}, u32[]{:S(2)}, u32[]{:S(2)}) collective-permute-start(f32[392,128]{1,0:T(8,128)S(1)} %pad_maximum_fusion.10), channel_id=1, source_target_pairs={{0,8},{1,5},{2,10},{3,7},{4,12},{5,1},{6,14},{7,3},{8,0},{9,13},{1... | collective-permute-start | bytes 602120 | tf_op jit(solution)/shard_map/ppermute | solution.py:498
  19.6 14.2 %collective-permute-start.3 = (f32[776,128]{1,0:T(8,128)S(1)}, f32[776,128]{1,0:T(8,128)S(1)}, u32[]{:S(2)}, u32[]{:S(2)}) collective-permute-start(f32[776,128]{1,0:T(8,128)S(1)} %get-tuple-element.106), channel_id=1, source_target_pairs={{0,8},{1,5},{2,10},{3,7},{4,12},{5,1},{6,14},{7,3},{8,0},{9,13},{1... | collective-permute-start | bytes 1191944 | tf_op jit(solution)/shard_map/ppermute | solution.py:498
  22.1 13.1 %collective-permute-start.2 = (f32[392,128]{1,0:T(8,128)S(1)}, f32[392,128]{1,0:T(8,128)S(1)}, u32[]{:S(2)}, u32[]{:S(2)}) collective-permute-start(f32[392,128]{1,0:T(8,128)S(1)} %pad_maximum_fusion.11), channel_id=1, source_target_pairs={{0,16},{1,17},{2,18},{3,19},{4,20},{5,21},{6,22},{7,23},{8,24},{9,... | collective-permute-start | bytes 602120 | tf_op jit(solution)/shard_map/ppermute | solution.py:498
  34.0 5.8 %collective-permute-start.5 = (f32[392,128]{1,0:T(8,128)S(1)}, f32[392,128]{1,0:T(8,128)S(1)}, u32[]{:S(2)}, u32[]{:S(2)}) collective-permute-start(f32[392,128]{1,0:T(8,128)S(1)} %pad_maximum_fusion.12), channel_id=1, source_target_pairs={{0,4},{1,9},{2,6},{3,11},{4,0},{5,13},{6,2},{7,15},{8,12},{9,1},{1... | collective-permute-start | bytes 602120 | tf_op jit(solution)/shard_map/ppermute | solution.py:498
  35.2 10.0 %collective-permute-start.4 = (f32[384,128]{1,0:T(8,128)S(1)}, f32[384,128]{1,0:T(8,128)S(1)}, u32[]{:S(2)}, u32[]{:S(2)}) collective-permute-start(f32[384,128]{1,0:T(8,128)S(1)} %slice_add_fusion.25.mine_ref), channel_id=1, source_target_pairs={{0,8},{1,5},{2,10},{3,7},{4,12},{5,1},{6,14},{7,3},{8,0},{9,13},{1... | collective-permute-start | bytes 589832 | tf_op jit(solution)/shard_map/ppermute | solution.py:498
  39.8 8.5 %collective-permute-start.7 = (f32[392,128]{1,0:T(8,128)S(1)}, f32[392,128]{1,0:T(8,128)S(1)}, u32[]{:S(2)}, u32[]{:S(2)}) collective-permute-start(f32[392,128]{1,0:T(8,128)S(1)} %pad_maximum_fusion.13), channel_id=1, source_target_pairs={{0,16},{1,17},{2,18},{3,19},{4,20},{5,21},{6,22},{7,23},{8,24},{9,... | collective-permute-start | bytes 602120 | tf_op jit(solution)/shard_map/ppermute | solution.py:498
  45.2 7.8 %collective-permute-start.6 = (f32[768,128]{1,0:T(8,128)S(1)}, f32[768,128]{1,0:T(8,128)S(1)}, u32[]{:S(2)}, u32[]{:S(2)}) collective-permute-start(f32[768,128]{1,0:T(8,128)S(1)} %pad_maximum_fusion), channel_id=1, source_target_pairs={{0,4},{1,9},{2,6},{3,11},{4,0},{5,13},{6,2},{7,15},{8,12},{9,1},{1... | collective-permute-start | bytes 1179656 | tf_op jit(solution)/shard_map/ppermute | solution.py:498
  48.3 6.9 %collective-permute-start.8 = (f32[384,128]{1,0:T(8,128)S(1)}, f32[384,128]{1,0:T(8,128)S(1)}, u32[]{:S(2)}, u32[]{:S(2)}) collective-permute-start(f32[384,128]{1,0:T(8,128)S(1)} %slice_add_fusion.24.mine_ref), channel_id=1, source_target_pairs={{0,4},{1,9},{2,6},{3,11},{4,0},{5,13},{6,2},{7,15},{8,12},{9,1},{1... | collective-permute-start | bytes 589832 | tf_op jit(solution)/shard_map/ppermute | solution.py:498
  54.2 2.1 %collective-permute-start.9 = (f32[520,128]{1,0:T(8,128)S(1)}, f32[520,128]{1,0:T(8,128)S(1)}, u32[]{:S(2)}, u32[]{:S(2)}) collective-permute-start(f32[520,128]{1,0:T(8,128)S(1)} %get-tuple-element.121), channel_id=1, source_target_pairs={{0,1},{1,0},{2,3},{3,2},{4,5},{5,4},{6,7},{7,6},{8,9},{9,8},{10,11... | collective-permute-start | bytes 798728 | tf_op jit(solution)/shard_map/ppermute | solution.py:501
  55.2 7.8 %collective-permute-start.11 = (f32[768,128]{1,0:T(8,128)S(1)}, f32[768,128]{1,0:T(8,128)S(1)}, u32[]{:S(2)}, u32[]{:S(2)}) collective-permute-start(f32[768,128]{1,0:T(8,128)S(1)} %pad_maximum_fusion.1), channel_id=1, source_target_pairs={{0,8},{1,5},{2,10},{3,7},{4,12},{5,1},{6,14},{7,3},{8,0},{9,13},{1... | collective-permute-start | bytes 1179656 | tf_op jit(solution)/shard_map/ppermute | solution.py:498
  56.4 8.4 %collective-permute-start.10 = (f32[520,128]{1,0:T(8,128)S(1)}, f32[520,128]{1,0:T(8,128)S(1)}, u32[]{:S(2)}, u32[]{:S(2)}) collective-permute-start(f32[520,128]{1,0:T(8,128)S(1)} %pad_maximum_fusion.6), channel_id=1, source_target_pairs={{0,2},{1,3},{2,0},{3,1},{4,6},{5,7},{6,4},{7,5},{8,10},{9,11},{10,... | collective-permute-start | bytes 798728 | tf_op jit(solution)/shard_map/ppermute | solution.py:501
  64.2 1.8 collective-permute-start.13
  64.9 2.6 %collective-permute-start.12 = (f32[512,128]{1,0:T(8,128)S(1)}, f32[512,128]{1,0:T(8,128)S(1)}, u32[]{:S(2)}, u32[]{:S(2)}) collective-permute-start(f32[512,128]{1,0:T(8,128)S(1)} %slice_add_fusion.12.refs_2_), channel_id=1, source_target_pairs={{0,1},{1,0},{2,3},{3,2},{4,5},{5,4},{6,7},{7,6},{8,9},{9,8},{10,11... | collective-permute-start | bytes 786440 | tf_op jit(solution)/shard_map/ppermute | solution.py:501
  66.0 8.9 %collective-permute-start.15 = (f32[520,128]{1,0:T(8,128)S(1)}, f32[520,128]{1,0:T(8,128)S(1)}, u32[]{:S(2)}, u32[]{:S(2)}) collective-permute-start(f32[520,128]{1,0:T(8,128)S(1)} %pad_maximum_fusion.7), channel_id=1, source_target_pairs={{0,2},{1,3},{2,0},{3,1},{4,6},{5,7},{6,4},{7,5},{8,10},{9,11},{10,... | collective-permute-start | bytes 798728 | tf_op jit(solution)/shard_map/ppermute | solution.py:501
  68.9 7.9 %collective-permute-start.14 = (f32[776,128]{1,0:T(8,128)S(1)}, f32[776,128]{1,0:T(8,128)S(1)}, u32[]{:S(2)}, u32[]{:S(2)}) collective-permute-start(f32[776,128]{1,0:T(8,128)S(1)} %get-tuple-element.136), channel_id=1, source_target_pairs={{0,4},{1,9},{2,6},{3,11},{4,0},{5,13},{6,2},{7,15},{8,12},{9,1},{1... | collective-permute-start | bytes 1191944 | tf_op jit(solution)/shard_map/ppermute | solution.py:498
  75.1 1.8 %collective-permute-start.17 = (f32[512,128]{1,0:T(8,128)S(1)}, f32[512,128]{1,0:T(8,128)S(1)}, u32[]{:S(2)}, u32[]{:S(2)}) collective-permute-start(f32[512,128]{1,0:T(8,128)S(1)} %slice_add_fusion.10.refs_2_), channel_id=1, source_target_pairs={{0,1},{1,0},{2,3},{3,2},{4,5},{5,4},{6,7},{7,6},{8,9},{9,8},{10,11... | collective-permute-start | bytes 786440 | tf_op jit(solution)/shard_map/ppermute | solution.py:501
  76.9 5.8 %collective-permute-start.16 = (f32[392,128]{1,0:T(8,128)S(1)}, f32[392,128]{1,0:T(8,128)S(1)}, u32[]{:S(2)}, u32[]{:S(2)}) collective-permute-start(f32[392,128]{1,0:T(8,128)S(1)} %pad_maximum_fusion.14), channel_id=1, source_target_pairs={{0,8},{1,5},{2,10},{3,7},{4,12},{5,1},{6,14},{7,3},{8,0},{9,13},{1... | collective-permute-start | bytes 602120 | tf_op jit(solution)/shard_map/ppermute | solution.py:498
  78.4 13.5 %collective-permute-start.19 = (f32[776,128]{1,0:T(8,128)S(1)}, f32[776,128]{1,0:T(8,128)S(1)}, u32[]{:S(2)}, u32[]{:S(2)}) collective-permute-start(f32[776,128]{1,0:T(8,128)S(1)} %get-tuple-element.140), channel_id=1, source_target_pairs={{0,8},{1,5},{2,10},{3,7},{4,12},{5,1},{6,14},{7,3},{8,0},{9,13},{1... | collective-permute-start | bytes 1191944 | tf_op jit(solution)/shard_map/ppermute | solution.py:498
  82.7 9.9 %collective-permute-start.18 = (f32[392,128]{1,0:T(8,128)S(1)}, f32[392,128]{1,0:T(8,128)S(1)}, u32[]{:S(2)}, u32[]{:S(2)}) collective-permute-start(f32[392,128]{1,0:T(8,128)S(1)} %pad_maximum_fusion.15), channel_id=1, source_target_pairs={{0,16},{1,17},{2,18},{3,19},{4,20},{5,21},{6,22},{7,23},{8,24},{9,... | collective-permute-start | bytes 602120 | tf_op jit(solution)/shard_map/ppermute | solution.py:498
  91.9 5.8 %collective-permute-start.21 = (f32[392,128]{1,0:T(8,128)S(1)}, f32[392,128]{1,0:T(8,128)S(1)}, u32[]{:S(2)}, u32[]{:S(2)}) collective-permute-start(f32[392,128]{1,0:T(8,128)S(1)} %pad_maximum_fusion.16), channel_id=1, source_target_pairs={{0,4},{1,9},{2,6},{3,11},{4,0},{5,13},{6,2},{7,15},{8,12},{9,1},{1... | collective-permute-start | bytes 602120 | tf_op jit(solution)/shard_map/ppermute | solution.py:498
  92.6 11.1 %collective-permute-start.20 = (f32[384,128]{1,0:T(8,128)S(1)}, f32[384,128]{1,0:T(8,128)S(1)}, u32[]{:S(2)}, u32[]{:S(2)}) collective-permute-start(f32[384,128]{1,0:T(8,128)S(1)} %slice_add_fusion.23.mine_ref), channel_id=1, source_target_pairs={{0,8},{1,5},{2,10},{3,7},{4,12},{5,1},{6,14},{7,3},{8,0},{9,13},{1... | collective-permute-start | bytes 589832 | tf_op jit(solution)/shard_map/ppermute | solution.py:498
  97.8 8.3 %collective-permute-start.23 = (f32[392,128]{1,0:T(8,128)S(1)}, f32[392,128]{1,0:T(8,128)S(1)}, u32[]{:S(2)}, u32[]{:S(2)}) collective-permute-start(f32[392,128]{1,0:T(8,128)S(1)} %pad_maximum_fusion.17), channel_id=1, source_target_pairs={{0,16},{1,17},{2,18},{3,19},{4,20},{5,21},{6,22},{7,23},{8,24},{9,... | collective-permute-start | bytes 602120 | tf_op jit(solution)/shard_map/ppermute | solution.py:498
  103.8 7.8 %collective-permute-start.22 = (f32[768,128]{1,0:T(8,128)S(1)}, f32[768,128]{1,0:T(8,128)S(1)}, u32[]{:S(2)}, u32[]{:S(2)}) collective-permute-start(f32[768,128]{1,0:T(8,128)S(1)} %pad_maximum_fusion.2), channel_id=1, source_target_pairs={{0,4},{1,9},{2,6},{3,11},{4,0},{5,13},{6,2},{7,15},{8,12},{9,1},{1... | collective-permute-start | bytes 1179656 | tf_op jit(solution)/shard_map/ppermute | solution.py:498
  106.1 7.6 %collective-permute-start.25 = (f32[384,128]{1,0:T(8,128)S(1)}, f32[384,128]{1,0:T(8,128)S(1)}, u32[]{:S(2)}, u32[]{:S(2)}) collective-permute-start(f32[384,128]{1,0:T(8,128)S(1)} %slice_add_fusion.22.mine_ref), channel_id=1, source_target_pairs={{0,4},{1,9},{2,6},{3,11},{4,0},{5,13},{6,2},{7,15},{8,12},{9,1},{1... | collective-permute-start | bytes 589832 | tf_op jit(solution)/shard_map/ppermute | solution.py:498
  112.7 2.4 %collective-permute-start.24 = (f32[520,128]{1,0:T(8,128)S(1)}, f32[520,128]{1,0:T(8,128)S(1)}, u32[]{:S(2)}, u32[]{:S(2)}) collective-permute-start(f32[520,128]{1,0:T(8,128)S(1)} %get-tuple-element.154), channel_id=1, source_target_pairs={{0,1},{1,0},{2,3},{3,2},{4,5},{5,4},{6,7},{7,6},{8,9},{9,8},{10,11... | collective-permute-start | bytes 798728 | tf_op jit(solution)/shard_map/ppermute | solution.py:501
  113.7 7.8 %collective-permute-start.27 = (f32[768,128]{1,0:T(8,128)S(1)}, f32[768,128]{1,0:T(8,128)S(1)}, u32[]{:S(2)}, u32[]{:S(2)}) collective-permute-start(f32[768,128]{1,0:T(8,128)S(1)} %pad_maximum_fusion.3), channel_id=1, source_target_pairs={{0,8},{1,5},{2,10},{3,7},{4,12},{5,1},{6,14},{7,3},{8,0},{9,13},{1... | collective-permute-start | bytes 1179656 | tf_op jit(solution)/shard_map/ppermute | solution.py:498
  115.2 9.1 %collective-permute-start.26 = (f32[520,128]{1,0:T(8,128)S(1)}, f32[520,128]{1,0:T(8,128)S(1)}, u32[]{:S(2)}, u32[]{:S(2)}) collective-permute-start(f32[520,128]{1,0:T(8,128)S(1)} %pad_maximum_fusion.8), channel_id=1, source_target_pairs={{0,2},{1,3},{2,0},{3,1},{4,6},{5,7},{6,4},{7,5},{8,10},{9,11},{10,... | collective-permute-start | bytes 798728 | tf_op jit(solution)/shard_map/ppermute | solution.py:501
  122.7 2.7 %collective-permute-start.29 = (f32[520,128]{1,0:T(8,128)S(1)}, f32[520,128]{1,0:T(8,128)S(1)}, u32[]{:S(2)}, u32[]{:S(2)}) collective-permute-start(f32[520,128]{1,0:T(8,128)S(1)} %get-tuple-element.165), channel_id=1, source_target_pairs={{0,1},{1,0},{2,3},{3,2},{4,5},{5,4},{6,7},{7,6},{8,9},{9,8},{10,11... | collective-permute-start | bytes 798728 | tf_op jit(solution)/shard_map/ppermute | solution.py:501
  124.3 3.0 %collective-permute-start.28 = (f32[512,128]{1,0:T(8,128)S(1)}, f32[512,128]{1,0:T(8,128)S(1)}, u32[]{:S(2)}, u32[]{:S(2)}) collective-permute-start(f32[512,128]{1,0:T(8,128)S(1)} %slice_add_fusion.8.refs_2_), channel_id=1, source_target_pairs={{0,1},{1,0},{2,3},{3,2},{4,5},{5,4},{6,7},{7,6},{8,9},{9,8},{10,11... | collective-permute-start | bytes 786440 | tf_op jit(solution)/shard_map/ppermute | solution.py:501
  125.5 8.9 %collective-permute-start.31 = (f32[520,128]{1,0:T(8,128)S(1)}, f32[520,128]{1,0:T(8,128)S(1)}, u32[]{:S(2)}, u32[]{:S(2)}) collective-permute-start(f32[520,128]{1,0:T(8,128)S(1)} %pad_maximum_fusion.9), channel_id=1, source_target_pairs={{0,2},{1,3},{2,0},{3,1},{4,6},{5,7},{6,4},{7,5},{8,10},{9,11},{10,... | collective-permute-start | bytes 798728 | tf_op jit(solution)/shard_map/ppermute | solution.py:501
  128.8 7.8 %collective-permute-start.30 = (f32[776,128]{1,0:T(8,128)S(1)}, f32[776,128]{1,0:T(8,128)S(1)}, u32[]{:S(2)}, u32[]{:S(2)}) collective-permute-start(f32[776,128]{1,0:T(8,128)S(1)} %get-tuple-element.172), channel_id=1, source_target_pairs={{0,4},{1,9},{2,6},{3,11},{4,0},{5,13},{6,2},{7,15},{8,12},{9,1},{1... | collective-permute-start | bytes 1191944 | tf_op jit(solution)/shard_map/ppermute | solution.py:498
  134.4 2.4 %collective-permute-start.33 = (f32[512,128]{1,0:T(8,128)S(1)}, f32[512,128]{1,0:T(8,128)S(1)}, u32[]{:S(2)}, u32[]{:S(2)}) collective-permute-start(f32[512,128]{1,0:T(8,128)S(1)} %slice_add_fusion.6.refs_2_), channel_id=1, source_target_pairs={{0,1},{1,0},{2,3},{3,2},{4,5},{5,4},{6,7},{7,6},{8,9},{9,8},{10,11... | collective-permute-start | bytes 786440 | tf_op jit(solution)/shard_map/ppermute | solution.py:501
  136.7 5.8 %collective-permute-start.32 = (f32[392,128]{1,0:T(8,128)S(1)}, f32[392,128]{1,0:T(8,128)S(1)}, u32[]{:S(2)}, u32[]{:S(2)}) collective-permute-start(f32[392,128]{1,0:T(8,128)S(1)} %pad_maximum_fusion.18), channel_id=1, source_target_pairs={{0,8},{1,5},{2,10},{3,7},{4,12},{5,1},{6,14},{7,3},{8,0},{9,13},{1... | collective-permute-start | bytes 602120 | tf_op jit(solution)/shard_map/ppermute | solution.py:498
  138.4 11.4 %collective-permute-start.35 = (f32[776,128]{1,0:T(8,128)S(1)}, f32[776,128]{1,0:T(8,128)S(1)}, u32[]{:S(2)}, u32[]{:S(2)}) collective-permute-start(f32[776,128]{1,0:T(8,128)S(1)} %get-tuple-element.178), channel_id=1, source_target_pairs={{0,8},{1,5},{2,10},{3,7},{4,12},{5,1},{6,14},{7,3},{8,0},{9,13},{1... | collective-permute-start | bytes 1191944 | tf_op jit(solution)/shard_map/ppermute | solution.py:498
  142.6 10.5 %collective-permute-start.34 = (f32[392,128]{1,0:T(8,128)S(1)}, f32[392,128]{1,0:T(8,128)S(1)}, u32[]{:S(2)}, u32[]{:S(2)}) collective-permute-start(f32[392,128]{1,0:T(8,128)S(1)} %pad_maximum_fusion.19), channel_id=1, source_target_pairs={{0,16},{1,17},{2,18},{3,19},{4,20},{5,21},{6,22},{7,23},{8,24},{9,... | collective-permute-start | bytes 602120 | tf_op jit(solution)/shard_map/ppermute | solution.py:498
  149.9 7.7 %collective-permute-start.36 = (f32[392,128]{1,0:T(8,128)S(1)}, f32[392,128]{1,0:T(8,128)S(1)}, u32[]{:S(2)}, u32[]{:S(2)}) collective-permute-start(f32[392,128]{1,0:T(8,128)S(1)} %pad_maximum_fusion.20), channel_id=1, source_target_pairs={{0,4},{1,9},{2,6},{3,11},{4,0},{5,13},{6,2},{7,15},{8,12},{9,1},{1... | collective-permute-start | bytes 602120 | tf_op jit(solution)/shard_map/ppermute | solution.py:498
  153.1 7.9 %collective-permute-start.38 = (f32[384,128]{1,0:T(8,128)S(1)}, f32[384,128]{1,0:T(8,128)S(1)}, u32[]{:S(2)}, u32[]{:S(2)}) collective-permute-start(f32[384,128]{1,0:T(8,128)S(1)} %slice_add_fusion.21.mine_ref), channel_id=1, source_target_pairs={{0,8},{1,5},{2,10},{3,7},{4,12},{5,1},{6,14},{7,3},{8,0},{9,13},{1... | collective-permute-start | bytes 589832 | tf_op jit(solution)/shard_map/ppermute | solution.py:498
  157.7 8.9 %collective-permute-start.37 = (f32[392,128]{1,0:T(8,128)S(1)}, f32[392,128]{1,0:T(8,128)S(1)}, u32[]{:S(2)}, u32[]{:S(2)}) collective-permute-start(f32[392,128]{1,0:T(8,128)S(1)} %pad_maximum_fusion.21), channel_id=1, source_target_pairs={{0,16},{1,17},{2,18},{3,19},{4,20},{5,21},{6,22},{7,23},{8,24},{9,... | collective-permute-start | bytes 602120 | tf_op jit(solution)/shard_map/ppermute | solution.py:498
  166.6 7.8 %collective-permute-start.40 = (f32[384,128]{1,0:T(8,128)S(1)}, f32[384,128]{1,0:T(8,128)S(1)}, u32[]{:S(2)}, u32[]{:S(2)}) collective-permute-start(f32[384,128]{1,0:T(8,128)S(1)} %slice_add_fusion.20.refs_6_), channel_id=1, source_target_pairs={{0,4},{1,9},{2,6},{3,11},{4,0},{5,13},{6,2},{7,15},{8,12},{9,1},{1... | collective-permute-start | bytes 589832 | tf_op jit(solution)/shard_map/ppermute | solution.py:498
  166.9 13.1 %collective-permute-start.39 = (f32[768,128]{1,0:T(8,128)S(1)}, f32[768,128]{1,0:T(8,128)S(1)}, u32[]{:S(2)}, u32[]{:S(2)}) collective-permute-start(f32[768,128]{1,0:T(8,128)S(1)} %pad_maximum_fusion.4), channel_id=1, source_target_pairs={{0,4},{1,9},{2,6},{3,11},{4,0},{5,13},{6,2},{7,15},{8,12},{9,1},{1... | collective-permute-start | bytes 1179656 | tf_op jit(solution)/shard_map/ppermute | solution.py:498
  174.5 7.8 %collective-permute-start.41 = (f32[768,128]{1,0:T(8,128)S(1)}, f32[768,128]{1,0:T(8,128)S(1)}, u32[]{:S(2)}, u32[]{:S(2)}) collective-permute-start(f32[768,128]{1,0:T(8,128)S(1)} %pad_maximum_fusion.5), channel_id=1, source_target_pairs={{0,8},{1,5},{2,10},{3,7},{4,12},{5,1},{6,14},{7,3},{8,0},{9,13},{1... | collective-permute-start | bytes 1179656 | tf_op jit(solution)/shard_map/ppermute | solution.py:498

commit v22 on v21

--- a/solution.py
+++ b/solution.py
@@ -204,39 +204,34 @@
     back_pairs(dense_ref, turned_ref, keep_ref, units)
 
 
-def fore_pairs(dense_ref, units, wide_ref, add_ref, out_ref, start):
-    depth = wide_ref.shape[0] // len(units)
+def fore_pairs(dense_ref, units, flat_ref, add_ref, out_ref, start):
+    depth = flat_ref.shape[1] // len(units)
     runs = [(unit * depth, i * depth, depth) for i, unit in enumerate(units)]
     if units[1] == units[0] + 1:
         runs = [(units[0] * depth, 0, 2 * depth)]
-    low = low_lanes((TILE, TILE))
-    step = 4
-    pairs = out_ref.shape[0] // TILE
-    for pair in range(0, pairs, step):
-        rows = slice((start + pair) * PAIR, (start + pair + step) * PAIR)
+    for pair in range(out_ref.shape[0] // TILE):
         product = sum(
-            jnp.dot(
-                dense_ref[rows, cell : cell + size],
-                wide_ref[row : row + size, :],
+            lax.dot_general(
+                flat_ref[:, place : place + size],
+                dense_ref[rows_of(start + pair, PAIR), cell : cell + size],
+                (((1,), (1,)), ((), ())),
                 preferred_element_type=jnp.float32,
             )
-            for cell, row, size in runs
+            for cell, place, size in runs
         )
-        for i in range(step):
-            even, odd = product[rows_of(2 * i), :], product[rows_of(2 * i + 1), :]
-            value = jnp.where(low, even, odd)
-            if add_ref is not None:
-                value = value + add_ref[rows_of(start + pair + i), :]
-            out_ref[rows_of(pair + i), :] = value
-
-
-def fore_vector(parts, wide_ref, raw_ref, scales):
-    low = low_lanes((TILE, TILE))
+        value = jnp.concatenate([product[:, :TILE], product[:, TILE:]], axis=0).T
+        if add_ref is not None:
+            value = value + add_ref[rows_of(start + pair), :]
+        out_ref[rows_of(pair), :] = value
+
+
+def fore_vector(parts, flat_ref, raw_ref, scales):
+    half = flat_ref.shape[0]
     sums = []
     for pair, value, squares in next_vector(parts, raw_ref, *scales):
-        other = turned(value)
-        wide_ref[rows_of(2 * pair), :] = jnp.where(low, value, other).astype(wide_ref.dtype)
-        wide_ref[rows_of(2 * pair + 1), :] = jnp.where(low, other, value).astype(wide_ref.dtype)
+        flat = value.T.astype(flat_ref.dtype)
+        flat_ref[:, rows_of(2 * pair)] = flat[:half]
+        flat_ref[:, rows_of(2 * pair + 1)] = flat[half:]
         if squares is not None:
             sums.append(squares)
     return sums[0] + sums[1]
@@ -244,24 +239,24 @@
 
 def fore_own_kernel(first, units, dense_ref, inner_ref, mine_ref, scale_ref, *refs):
     past_ref, past_scale_ref = (None, None) if first else refs[:2]
-    part_ref, sum_ref, raw_ref, wide_ref = refs[-4:]
+    part_ref, sum_ref, raw_ref, flat_ref = refs[-4:]
     parts = [(inner_ref, 1), (mine_ref, 1)]
-    sum_ref[...] = fore_vector(parts, wide_ref, raw_ref, (scale_ref, past_ref, past_scale_ref))
-    fore_pairs(dense_ref, units, wide_ref, None, part_ref, 0)
+    sum_ref[...] = fore_vector(parts, flat_ref, raw_ref, (scale_ref, past_ref, past_scale_ref))
+    fore_pairs(dense_ref, units, flat_ref, None, part_ref, 0)
 
 
 def fore_send_kernel(first, units, dense_ref, outer_ref, part_ref, sum_ref, scale_ref, *refs):
     past_ref, past_scale_ref = (None, None) if first else refs[:2]
-    send_ref, wide_ref, raw_ref = refs[-3:]
-    squares = fore_vector([(outer_ref, 2)], wide_ref, raw_ref, (scale_ref, past_ref, past_scale_ref))
+    send_ref, flat_ref, raw_ref = refs[-3:]
+    squares = fore_vector([(outer_ref, 2)], flat_ref, raw_ref, (scale_ref, past_ref, past_scale_ref))
     row = squares_row([squares, sum_ref[...]])
     send_ref[-NORM_ROWS:, :] = jnp.broadcast_to(row, (NORM_ROWS, TILE))
-    fore_pairs(dense_ref, units, wide_ref, part_ref, send_ref, 0)
-
-
-def fore_keep_kernel(units, dense_ref, wide_ref, part_ref, keep_ref):
+    fore_pairs(dense_ref, units, flat_ref, part_ref, send_ref, 0)
+
+
+def fore_keep_kernel(units, dense_ref, flat_ref, part_ref, keep_ref):
     start = keep_ref.shape[0] // TILE
-    fore_pairs(dense_ref, units, wide_ref, part_ref, keep_ref, start)
+    fore_pairs(dense_ref, units, flat_ref, part_ref, keep_ref, start)
 
 
 def product_call(body, dense, operands, shapes, scratch=()):
@@ -303,7 +298,7 @@
         dense,
         operands,
         [float_rows(rows // 2), float_rows(NORM_ROWS), float_rows(cells // 4)],
-        [pltpu.VMEM((cells // 2, TILE), dense.dtype)],
+        [pltpu.VMEM((TILE // 2, cells // 2), dense.dtype)],
     )
 
 
@@ -311,18 +306,18 @@
     rows, cells = dense.shape[0], CB_DEV * TILE
     shapes = [
         float_rows(rows // 4 + NORM_ROWS),
-        jax.ShapeDtypeStruct((cells // 2, TILE), dense.dtype),
+        jax.ShapeDtypeStruct((TILE // 2, cells // 2), dense.dtype),
         float_rows(cells // 4),
     ]
-    send, wide, raw = product_call(
+    send, flat, raw = product_call(
         functools.partial(fore_send_kernel, first, order[:2]), dense, operands, shapes
     )
 
-    def keep(wide):
+    def keep(flat):
         body = functools.partial(fore_keep_kernel, order[:2])
-        return product_call(body, dense, [wide, operands[1]], [float_rows(rows // 4)])[0]
-
-    return send, (keep, wide), raw
+        return product_call(body, dense, [flat, operands[1]], [float_rows(rows // 4)])[0]
+
+    return send, (keep, flat), raw
 
 
 def rotation(norms):

time: 184 us -> 183 us (level)
  waiting for transfers between devices: 100 us -> 92.8 us
  starting transfers between devices: 40.2 us -> 43.7 us
  Pallas kernels: 39.5 us -> 42.6 us
    ppermute x30, waiting for transfers between devices: 90.6 us -> 81.8 us  [swap_rows(): return lax.ppermute(value, ('rows', 'cols'), pairs)]
    ppermute x30, starting transfers between devices: 33.8 us -> 37.9 us  [swap_rows(): return lax.ppermute(value, ('rows', 'cols'), pairs)]
    pallas_call x24, Pallas kernels: 32.2 us -> 34.8 us  [product_call(): pl.pallas_call(body, in_specs=[WHOLE] * (1 + len(operands)), out_specs=[W...]
  transfers between devices with their start and end apart: 42 -> 42, of which waited for: 32 -> 32; matrix products, arithmetic and copies ran while one was open for 1% -> 1% of each run, Pallas kernels for 18% -> 19%
where the time goes in v22:
time: 183 us
  waiting for transfers between devices  92.8 us (51%)
  starting transfers between devices  43.7 us (24%)
  Pallas kernels  42.6 us (23%)
    ppermute x30, waiting for transfers between devices, swap_rows(): return lax.ppermute(value, ('rows', 'cols'), pairs)  81.8 us
    ppermute x30, starting transfers between devices, swap_rows(): return lax.ppermute(value, ('rows', 'cols'), pairs)  37.9 us
    pallas_call x24, Pallas kernels, product_call(): pl.pallas_call(body, in_specs=[WHOLE] * (1 + len(operands)), out_specs=[W...  34.8 us
    ppermute x12, waiting for transfers between devices, swap_cols(): lax.ppermute(value, 'cols', [(i, i ^ 1 << level) for i in range(col_count)])  11 us
    ppermute x12, starting transfers between devices, swap_cols(): lax.ppermute(value, 'cols', [(i, i ^ 1 << level) for i in range(col_count)])  5.82 us
    pallas_call x1, Pallas kernels, fill_dense(): pl.pallas_call(fill_kernel, in_specs=[SCALARS] * 2 + [pl.BlockSpec(memory...  4.5 us
  transfers between devices with their start and end apart: 42, of which 32 were waited for; matrix products, arithmetic and copies ran while one was open for 1% of the time, Pallas kernels for 19%

profile of v22, /device:TPU:0, one launch (start us, length us, event | category | flops | bytes accessed | tf_op | source)
XLA Modules:
  0.0 182.7 jit_solution(13340806166016005347)
XLA Ops:
  0.7 4.5 %shard_map.67 = (bf16[2048,3200]{1,0:T(8,128)(2,1)S(1)}, f32[1024,128]{1,0:T(8,128)S(1)}, f32[1024,128]{1,0:T(8,128)S(1)}) custom-call(s32[24]{0:T(128)S(1)} %fusion.place_ref, s32[1]{0:T(128)} %bitcast.1.flip_ref, s32[16,16]{1,0:T(8,128)} %pattern_in.1, s32[16]{0:T(128)} %bitcast.5, f32[2048,128]{1,0:T(8,128)} %delays_in.1, bf16[16,16,128,128]{3,2,1,0:T(8,128)(2,1)} %tiles_in.1), custom_call_target="tpu_custom_call" | custom-call | bytes 8388608 | tf_op jit(solution)/shard_map/pallas_call | solution.py:112
  5.2 1.4 shard_map.68
  6.6 2.5 %collective-permute-start = (f32[776,128]{1,0:T(8,128)S(1)}, f32[776,128]{1,0:T(8,128)S(1)}, u32[]{:S(2)}, u32[]{:S(2)}) collective-permute-start(f32[776,128]{1,0:T(8,128)S(1)} %get-tuple-element.102), channel_id=1, source_target_pairs={{0,4},{1,9},{2,6},{3,11},{4,0},{5,13},{6,2},{7,15},{8,12},{9,1},{1... | collective-permute-start | bytes 1191944 | tf_op jit(solution)/shard_map/ppermute | solution.py:493
  11.8 3.1 %collective-permute-done = f32[776,128]{1,0:T(8,128)S(1)} collective-permute-done((f32[776,128]{1,0:T(8,128)S(1)}, f32[776,128]{1,0:T(8,128)S(1)}, u32[]{:S(2)}, u32[]{:S(2)}) %collective-permute-start) | collective-permute-done | bytes 397344 | tf_op jit(solution)/shard_map/ppermute | solution.py:493
  15.0 3.2 %collective-permute-start.1 = (f32[392,128]{1,0:T(8,128)S(1)}, f32[392,128]{1,0:T(8,128)S(1)}, u32[]{:S(2)}, u32[]{:S(2)}) collective-permute-start(f32[392,128]{1,0:T(8,128)S(1)} %pad_maximum_fusion.10), channel_id=1, source_target_pairs={{0,8},{1,5},{2,10},{3,7},{4,12},{5,1},{6,14},{7,3},{8,0},{9,13},{1... | collective-permute-start | bytes 602120 | tf_op jit(solution)/shard_map/ppermute | solution.py:493
  19.6 2.3 %collective-permute-done.1 = f32[392,128]{1,0:T(8,128)S(1)} collective-permute-done((f32[392,128]{1,0:T(8,128)S(1)}, f32[392,128]{1,0:T(8,128)S(1)}, u32[]{:S(2)}, u32[]{:S(2)}) %collective-permute-start.1) | collective-permute-done | bytes 200736 | tf_op jit(solution)/shard_map/ppermute | solution.py:493
  22.0 3.1 %collective-permute-start.2 = (f32[392,128]{1,0:T(8,128)S(1)}, f32[392,128]{1,0:T(8,128)S(1)}, u32[]{:S(2)}, u32[]{:S(2)}) collective-permute-start(f32[392,128]{1,0:T(8,128)S(1)} %pad_maximum_fusion.11), channel_id=1, source_target_pairs={{0,16},{1,17},{2,18},{3,19},{4,20},{5,21},{6,22},{7,23},{8,24},{9,... | collective-permute-start | bytes 602120 | tf_op jit(solution)/shard_map/ppermute | solution.py:493
  25.1 8.4 %collective-permute-done.3 = f32[776,128]{1,0:T(8,128)S(1)} collective-permute-done((f32[776,128]{1,0:T(8,128)S(1)}, f32[776,128]{1,0:T(8,128)S(1)}, u32[]{:S(2)}, u32[]{:S(2)}) %collective-permute-start.3) | collective-permute-done | bytes 397344 | tf_op jit(solution)/shard_map/ppermute | solution.py:493
  33.8 2.3 %collective-permute-start.4 = (f32[384,128]{1,0:T(8,128)S(1)}, f32[384,128]{1,0:T(8,128)S(1)}, u32[]{:S(2)}, u32[]{:S(2)}) collective-permute-start(f32[384,128]{1,0:T(8,128)S(1)} %slice_add_fusion.25.mine_ref), channel_id=1, source_target_pairs={{0,8},{1,5},{2,10},{3,7},{4,12},{5,1},{6,14},{7,3},{8,0},{9,13},{1... | collective-permute-start | bytes 589832 | tf_op jit(solution)/shard_map/ppermute | solution.py:493
  36.1 3.4 %collective-permute-done.5 = f32[392,128]{1,0:T(8,128)S(1)} collective-permute-done((f32[392,128]{1,0:T(8,128)S(1)}, f32[392,128]{1,0:T(8,128)S(1)}, u32[]{:S(2)}, u32[]{:S(2)}) %collective-permute-start.5) | collective-permute-done | bytes 200736 | tf_op jit(solution)/shard_map/ppermute | solution.py:493
  39.6 4.1 %collective-permute-done.4.inner_ref = f32[384,128]{1,0:T(8,128)S(1)} collective-permute-done((f32[384,128]{1,0:T(8,128)S(1)}, f32[384,128]{1,0:T(8,128)S(1)}, u32[]{:S(2)}, u32[]{:S(2)}) %collective-permute-start.4) | collective-permute-done | bytes 196640 | tf_op jit(solution)/shard_map/ppermute | solution.py:493
  44.8 3.2 %collective-permute-done.7 = f32[392,128]{1,0:T(8,128)S(1)} collective-permute-done((f32[392,128]{1,0:T(8,128)S(1)}, f32[392,128]{1,0:T(8,128)S(1)}, u32[]{:S(2)}, u32[]{:S(2)}) %collective-permute-start.7) | collective-permute-done | bytes 200736 | tf_op jit(solution)/shard_map/ppermute | solution.py:493
  48.5 2.2 %shard_map.72 = (f32[1024,128]{1,0:T(8,128)S(1)}, f32[8,128]{1,0:T(8,128)S(1)}, f32[768,128]{1,0:T(8,128)S(1)}) custom-call(bf16[2048,3200]{1,0:T(8,128)(2,1)S(1)} %get-tuple-element.99.refs_0_.dense_ref, f32[384,128]{1,0:T(8,128)S(1)} %collective-permute-done.4.inner_ref, f32[384,128]{1,0:T(8,128)S(1)} %slice_add_fusion.25.mine_ref, ...), custom_call_target="tpu_custom_call" | custom-call | flops 1677721600 | bytes 6553600 | tf_op jit(solution)/shard_map/pallas_call | solution.py:263
  55.2 2.4 %collective-permute-start.10 = (f32[520,128]{1,0:T(8,128)S(1)}, f32[520,128]{1,0:T(8,128)S(1)}, u32[]{:S(2)}, u32[]{:S(2)}) collective-permute-start(f32[520,128]{1,0:T(8,128)S(1)} %pad_maximum_fusion.6), channel_id=1, source_target_pairs={{0,2},{1,3},{2,0},{3,1},{4,6},{5,7},{6,4},{7,5},{8,10},{9,11},{10,... | collective-permute-start | bytes 798728 | tf_op jit(solution)/shard_map/ppermute | solution.py:496
  57.6 2.2 %shard_map.75 = (f32[1024,128]{1,0:T(8,128)S(1)}, f32[8,128]{1,0:T(8,128)S(1)}, f32[768,128]{1,0:T(8,128)S(1)}) custom-call(bf16[2048,3200]{1,0:T(8,128)(2,1)S(1)} %get-tuple-element.99.refs_0_.dense_ref, f32[384,128]{1,0:T(8,128)S(1)} %collective-permute-done.8.inner_ref, f32[384,128]{1,0:T(8,128)S(1)} %slice_add_fusion.24.mine_ref, ...), custom_call_target="tpu_custom_call" | custom-call | flops 1677721600 | bytes 6553600 | tf_op jit(solution)/shard_map/pallas_call | solution.py:263
  59.8 1.8 %collective-permute-done.11.outer_ref = f32[768,128]{1,0:T(8,128)S(1)} collective-permute-done((f32[768,128]{1,0:T(8,128)S(1)}, f32[768,128]{1,0:T(8,128)S(1)}, u32[]{:S(2)}, u32[]{:S(2)}) %collective-permute-start.11) | collective-permute-done | bytes 393248 | tf_op jit(solution)/shard_map/ppermute | solution.py:493
  62.9 1.6 collective-permute-done.10
  66.0 2.3 %collective-permute-start.15 = (f32[520,128]{1,0:T(8,128)S(1)}, f32[520,128]{1,0:T(8,128)S(1)}, u32[]{:S(2)}, u32[]{:S(2)}) collective-permute-start(f32[520,128]{1,0:T(8,128)S(1)} %pad_maximum_fusion.7), channel_id=1, source_target_pairs={{0,2},{1,3},{2,0},{3,1},{4,6},{5,7},{6,4},{7,5},{8,10},{9,11},{10,... | collective-permute-start | bytes 798728 | tf_op jit(solution)/shard_map/ppermute | solution.py:496
  68.4 1.4 shard_map.78
  71.7 3.7 %collective-permute-done.15 = f32[520,128]{1,0:T(8,128)S(1)} collective-permute-done((f32[520,128]{1,0:T(8,128)S(1)}, f32[520,128]{1,0:T(8,128)S(1)}, u32[]{:S(2)}, u32[]{:S(2)}) %collective-permute-start.15) | collective-permute-done | bytes 266272 | tf_op jit(solution)/shard_map/ppermute | solution.py:496
  75.4 2.2 %collective-permute-done.14 = f32[776,128]{1,0:T(8,128)S(1)} collective-permute-done((f32[776,128]{1,0:T(8,128)S(1)}, f32[776,128]{1,0:T(8,128)S(1)}, u32[]{:S(2)}, u32[]{:S(2)}) %collective-permute-start.14) | collective-permute-done | bytes 397344 | tf_op jit(solution)/shard_map/ppermute | solution.py:493
  77.9 1.6 shard_map.80
  79.5 2.1 %collective-permute-start.19 = (f32[776,128]{1,0:T(8,128)S(1)}, f32[776,128]{1,0:T(8,128)S(1)}, u32[]{:S(2)}, u32[]{:S(2)}) collective-permute-start(f32[776,128]{1,0:T(8,128)S(1)} %get-tuple-element.140), channel_id=1, source_target_pairs={{0,8},{1,5},{2,10},{3,7},{4,12},{5,1},{6,14},{7,3},{8,0},{9,13},{1... | collective-permute-start | bytes 1191944 | tf_op jit(solution)/shard_map/ppermute | solution.py:493
  83.6 1.6 collective-permute-start.18
  85.3 7.5 %collective-permute-done.19 = f32[776,128]{1,0:T(8,128)S(1)} collective-permute-done((f32[776,128]{1,0:T(8,128)S(1)}, f32[776,128]{1,0:T(8,128)S(1)}, u32[]{:S(2)}, u32[]{:S(2)}) %collective-permute-start.19) | collective-permute-done | bytes 397344 | tf_op jit(solution)/shard_map/ppermute | solution.py:493
  93.5 4.0 %collective-permute-start.20 = (f32[384,128]{1,0:T(8,128)S(1)}, f32[384,128]{1,0:T(8,128)S(1)}, u32[]{:S(2)}, u32[]{:S(2)}) collective-permute-start(f32[384,128]{1,0:T(8,128)S(1)} %slice_add_fusion.23.mine_ref), channel_id=1, source_target_pairs={{0,8},{1,5},{2,10},{3,7},{4,12},{5,1},{6,14},{7,3},{8,0},{9,13},{1... | collective-permute-start | bytes 589832 | tf_op jit(solution)/shard_map/ppermute | solution.py:493
  98.7 2.1 %collective-permute-start.23 = (f32[392,128]{1,0:T(8,128)S(1)}, f32[392,128]{1,0:T(8,128)S(1)}, u32[]{:S(2)}, u32[]{:S(2)}) collective-permute-start(f32[392,128]{1,0:T(8,128)S(1)} %pad_maximum_fusion.17), channel_id=1, source_target_pairs={{0,16},{1,17},{2,18},{3,19},{4,20},{5,21},{6,22},{7,23},{8,24},{9,... | collective-permute-start | bytes 602120 | tf_op jit(solution)/shard_map/ppermute | solution.py:493
  100.8 5.6 %collective-permute-done.20.inner_ref = f32[384,128]{1,0:T(8,128)S(1)} collective-permute-done((f32[384,128]{1,0:T(8,128)S(1)}, f32[384,128]{1,0:T(8,128)S(1)}, u32[]{:S(2)}, u32[]{:S(2)}) %collective-permute-start.20) | collective-permute-done | bytes 196640 | tf_op jit(solution)/shard_map/ppermute | solution.py:493
  107.2 1.4 collective-permute-start.25
  108.6 2.2 %shard_map.82 = (f32[1024,128]{1,0:T(8,128)S(1)}, f32[8,128]{1,0:T(8,128)S(1)}, f32[768,128]{1,0:T(8,128)S(1)}) custom-call(bf16[2048,3200]{1,0:T(8,128)(2,1)S(1)} %get-tuple-element.99.refs_0_.dense_ref, f32[384,128]{1,0:T(8,128)S(1)} %collective-permute-done.20.inner_ref, f32[384,128]{1,0:T(8,128)S(1)} %slice_add_fusion.23.mine_ref, ...), custom_call_target="tpu_custom_call" | custom-call | flops 1677721600 | bytes 6553600 | tf_op jit(solution)/shard_map/pallas_call | solution.py:263
  110.8 3.5 %collective-permute-done.22.outer_ref = f32[768,128]{1,0:T(8,128)S(1)} collective-permute-done((f32[768,128]{1,0:T(8,128)S(1)}, f32[768,128]{1,0:T(8,128)S(1)}, u32[]{:S(2)}, u32[]{:S(2)}) %collective-permute-start.22) | collective-permute-done | bytes 393248 | tf_op jit(solution)/shard_map/ppermute | solution.py:493
  117.8 2.2 %shard_map.85 = (f32[1024,128]{1,0:T(8,128)S(1)}, f32[8,128]{1,0:T(8,128)S(1)}, f32[768,128]{1,0:T(8,128)S(1)}) custom-call(bf16[2048,3200]{1,0:T(8,128)(2,1)S(1)} %get-tuple-element.99.refs_0_.dense_ref, f32[384,128]{1,0:T(8,128)S(1)} %collective-permute-done.25.inner_ref, f32[384,128]{1,0:T(8,128)S(1)} %slice_add_fusion.22.mine_ref, ...), custom_call_target="tpu_custom_call" | custom-call | flops 1677721600 | bytes 6553600 | tf_op jit(solution)/shard_map/pallas_call | solution.py:263
  120.0 4.2 %collective-permute-done.27.outer_ref = f32[768,128]{1,0:T(8,128)S(1)} collective-permute-done((f32[768,128]{1,0:T(8,128)S(1)}, f32[768,128]{1,0:T(8,128)S(1)}, u32[]{:S(2)}, u32[]{:S(2)}) %collective-permute-start.27) | collective-permute-done | bytes 393248 | tf_op jit(solution)/shard_map/ppermute | solution.py:493
  128.0 1.5 shard_map.88
  132.1 4.4 %collective-permute-done.31 = f32[520,128]{1,0:T(8,128)S(1)} collective-permute-done((f32[520,128]{1,0:T(8,128)S(1)}, f32[520,128]{1,0:T(8,128)S(1)}, u32[]{:S(2)}, u32[]{:S(2)}) %collective-permute-start.31) | collective-permute-done | bytes 266272 | tf_op jit(solution)/shard_map/ppermute | solution.py:496
  138.1 1.5 shard_map.90
  139.7 1.4 collective-permute-start.35
  143.8 5.8 %collective-permute-done.35 = f32[776,128]{1,0:T(8,128)S(1)} collective-permute-done((f32[776,128]{1,0:T(8,128)S(1)}, f32[776,128]{1,0:T(8,128)S(1)}, u32[]{:S(2)}, u32[]{:S(2)}) %collective-permute-start.35) | collective-permute-done | bytes 397344 | tf_op jit(solution)/shard_map/ppermute | solution.py:493
  149.7 1.4 collective-permute-start.36
  151.1 1.7 collective-permute-done.34
  152.9 3.0 %collective-permute-start.38 = (f32[384,128]{1,0:T(8,128)S(1)}, f32[384,128]{1,0:T(8,128)S(1)}, u32[]{:S(2)}, u32[]{:S(2)}) collective-permute-start(f32[384,128]{1,0:T(8,128)S(1)} %slice_add_fusion.21.mine_ref), channel_id=1, source_target_pairs={{0,8},{1,5},{2,10},{3,7},{4,12},{5,1},{6,14},{7,3},{8,0},{9,13},{1... | collective-permute-start | bytes 589832 | tf_op jit(solution)/shard_map/ppermute | solution.py:493
  155.9 1.5 collective-permute-done.36
  157.5 1.6 collective-permute-start.37
  159.8 6.6 %collective-permute-done.37 = f32[392,128]{1,0:T(8,128)S(1)} collective-permute-done((f32[392,128]{1,0:T(8,128)S(1)}, f32[392,128]{1,0:T(8,128)S(1)}, u32[]{:S(2)}, u32[]{:S(2)}) %collective-permute-start.37) | collective-permute-done | bytes 200736 | tf_op jit(solution)/shard_map/ppermute | solution.py:493
  166.4 1.4 collective-permute-start.40
  168.5 5.0 %collective-permute-done.40.refs_5_ = f32[384,128]{1,0:T(8,128)S(1)} collective-permute-done((f32[384,128]{1,0:T(8,128)S(1)}, f32[384,128]{1,0:T(8,128)S(1)}, u32[]{:S(2)}, u32[]{:S(2)}) %collective-permute-start.40) | collective-permute-done | bytes 196640 | tf_op jit(solution)/shard_map/ppermute | solution.py:493
  173.6 1.8 shard_map.92
  175.9 4.7 %collective-permute-done.39.outer_ref = f32[768,128]{1,0:T(8,128)S(1)} collective-permute-done((f32[768,128]{1,0:T(8,128)S(1)}, f32[768,128]{1,0:T(8,128)S(1)}, u32[]{:S(2)}, u32[]{:S(2)}) %collective-permute-start.39) | collective-permute-done | bytes 393248 | tf_op jit(solution)/shard_map/ppermute | solution.py:493
  (146 shorter events, 38.5 us)
Async XLA Ops:
  6.6 8.3 %collective-permute-start = (f32[776,128]{1,0:T(8,128)S(1)}, f32[776,128]{1,0:T(8,128)S(1)}, u32[]{:S(2)}, u32[]{:S(2)}) collective-permute-start(f32[776,128]{1,0:T(8,128)S(1)} %get-tuple-element.102), channel_id=1, source_target_pairs={{0,4},{1,9},{2,6},{3,11},{4,0},{5,13},{6,2},{7,15},{8,12},{9,1},{1... | collective-permute-start | bytes 1191944 | tf_op jit(solution)/shard_map/ppermute | solution.py:493
  15.0 6.9 %collective-permute-start.1 = (f32[392,128]{1,0:T(8,128)S(1)}, f32[392,128]{1,0:T(8,128)S(1)}, u32[]{:S(2)}, u32[]{:S(2)}) collective-permute-start(f32[392,128]{1,0:T(8,128)S(1)} %pad_maximum_fusion.10), channel_id=1, source_target_pairs={{0,8},{1,5},{2,10},{3,7},{4,12},{5,1},{6,14},{7,3},{8,0},{9,13},{1... | collective-permute-start | bytes 602120 | tf_op jit(solution)/shard_map/ppermute | solution.py:493
  19.5 14.0 %collective-permute-start.3 = (f32[776,128]{1,0:T(8,128)S(1)}, f32[776,128]{1,0:T(8,128)S(1)}, u32[]{:S(2)}, u32[]{:S(2)}) collective-permute-start(f32[776,128]{1,0:T(8,128)S(1)} %get-tuple-element.106), channel_id=1, source_target_pairs={{0,8},{1,5},{2,10},{3,7},{4,12},{5,1},{6,14},{7,3},{8,0},{9,13},{1... | collective-permute-start | bytes 1191944 | tf_op jit(solution)/shard_map/ppermute | solution.py:493
  22.0 11.8 %collective-permute-start.2 = (f32[392,128]{1,0:T(8,128)S(1)}, f32[392,128]{1,0:T(8,128)S(1)}, u32[]{:S(2)}, u32[]{:S(2)}) collective-permute-start(f32[392,128]{1,0:T(8,128)S(1)} %pad_maximum_fusion.11), channel_id=1, source_target_pairs={{0,16},{1,17},{2,18},{3,19},{4,20},{5,21},{6,22},{7,23},{8,24},{9,... | collective-permute-start | bytes 602120 | tf_op jit(solution)/shard_map/ppermute | solution.py:493
  33.7 5.8 %collective-permute-start.5 = (f32[392,128]{1,0:T(8,128)S(1)}, f32[392,128]{1,0:T(8,128)S(1)}, u32[]{:S(2)}, u32[]{:S(2)}) collective-permute-start(f32[392,128]{1,0:T(8,128)S(1)} %pad_maximum_fusion.12), channel_id=1, source_target_pairs={{0,4},{1,9},{2,6},{3,11},{4,0},{5,13},{6,2},{7,15},{8,12},{9,1},{1... | collective-permute-start | bytes 602120 | tf_op jit(solution)/shard_map/ppermute | solution.py:493
  33.8 9.9 %collective-permute-start.4 = (f32[384,128]{1,0:T(8,128)S(1)}, f32[384,128]{1,0:T(8,128)S(1)}, u32[]{:S(2)}, u32[]{:S(2)}) collective-permute-start(f32[384,128]{1,0:T(8,128)S(1)} %slice_add_fusion.25.mine_ref), channel_id=1, source_target_pairs={{0,8},{1,5},{2,10},{3,7},{4,12},{5,1},{6,14},{7,3},{8,0},{9,13},{1... | collective-permute-start | bytes 589832 | tf_op jit(solution)/shard_map/ppermute | solution.py:493
  39.5 8.5 %collective-permute-start.7 = (f32[392,128]{1,0:T(8,128)S(1)}, f32[392,128]{1,0:T(8,128)S(1)}, u32[]{:S(2)}, u32[]{:S(2)}) collective-permute-start(f32[392,128]{1,0:T(8,128)S(1)} %pad_maximum_fusion.13), channel_id=1, source_target_pairs={{0,16},{1,17},{2,18},{3,19},{4,20},{5,21},{6,22},{7,23},{8,24},{9,... | collective-permute-start | bytes 602120 | tf_op jit(solution)/shard_map/ppermute | solution.py:493
  43.7 7.8 %collective-permute-start.6 = (f32[768,128]{1,0:T(8,128)S(1)}, f32[768,128]{1,0:T(8,128)S(1)}, u32[]{:S(2)}, u32[]{:S(2)}) collective-permute-start(f32[768,128]{1,0:T(8,128)S(1)} %pad_maximum_fusion), channel_id=1, source_target_pairs={{0,4},{1,9},{2,6},{3,11},{4,0},{5,13},{6,2},{7,15},{8,12},{9,1},{1... | collective-permute-start | bytes 1179656 | tf_op jit(solution)/shard_map/ppermute | solution.py:493
  48.0 5.7 %collective-permute-start.8 = (f32[384,128]{1,0:T(8,128)S(1)}, f32[384,128]{1,0:T(8,128)S(1)}, u32[]{:S(2)}, u32[]{:S(2)}) collective-permute-start(f32[384,128]{1,0:T(8,128)S(1)} %slice_add_fusion.24.mine_ref), channel_id=1, source_target_pairs={{0,4},{1,9},{2,6},{3,11},{4,0},{5,13},{6,2},{7,15},{8,12},{9,1},{1... | collective-permute-start | bytes 589832 | tf_op jit(solution)/shard_map/ppermute | solution.py:493
  52.8 2.3 %collective-permute-start.9 = (f32[520,128]{1,0:T(8,128)S(1)}, f32[520,128]{1,0:T(8,128)S(1)}, u32[]{:S(2)}, u32[]{:S(2)}) collective-permute-start(f32[520,128]{1,0:T(8,128)S(1)} %get-tuple-element.121), channel_id=1, source_target_pairs={{0,1},{1,0},{2,3},{3,2},{4,5},{5,4},{6,7},{7,6},{8,9},{9,8},{10,11... | collective-permute-start | bytes 798728 | tf_op jit(solution)/shard_map/ppermute | solution.py:496
  53.8 7.8 %collective-permute-start.11 = (f32[768,128]{1,0:T(8,128)S(1)}, f32[768,128]{1,0:T(8,128)S(1)}, u32[]{:S(2)}, u32[]{:S(2)}) collective-permute-start(f32[768,128]{1,0:T(8,128)S(1)} %pad_maximum_fusion.1), channel_id=1, source_target_pairs={{0,8},{1,5},{2,10},{3,7},{4,12},{5,1},{6,14},{7,3},{8,0},{9,13},{1... | collective-permute-start | bytes 1179656 | tf_op jit(solution)/shard_map/ppermute | solution.py:493
  55.2 9.3 %collective-permute-start.10 = (f32[520,128]{1,0:T(8,128)S(1)}, f32[520,128]{1,0:T(8,128)S(1)}, u32[]{:S(2)}, u32[]{:S(2)}) collective-permute-start(f32[520,128]{1,0:T(8,128)S(1)} %pad_maximum_fusion.6), channel_id=1, source_target_pairs={{0,2},{1,3},{2,0},{3,1},{4,6},{5,7},{6,4},{7,5},{8,10},{9,11},{10,... | collective-permute-start | bytes 798728 | tf_op jit(solution)/shard_map/ppermute | solution.py:496
  62.9 3.1 %collective-permute-start.13 = (f32[520,128]{1,0:T(8,128)S(1)}, f32[520,128]{1,0:T(8,128)S(1)}, u32[]{:S(2)}, u32[]{:S(2)}) collective-permute-start(f32[520,128]{1,0:T(8,128)S(1)} %get-tuple-element.129), channel_id=1, source_target_pairs={{0,1},{1,0},{2,3},{3,2},{4,5},{5,4},{6,7},{7,6},{8,9},{9,8},{10,11... | collective-permute-start | bytes 798728 | tf_op jit(solution)/shard_map/ppermute | solution.py:496
  64.6 3.8 %collective-permute-start.12 = (f32[512,128]{1,0:T(8,128)S(1)}, f32[512,128]{1,0:T(8,128)S(1)}, u32[]{:S(2)}, u32[]{:S(2)}) collective-permute-start(f32[512,128]{1,0:T(8,128)S(1)} %slice_add_fusion.12.refs_2_), channel_id=1, source_target_pairs={{0,1},{1,0},{2,3},{3,2},{4,5},{5,4},{6,7},{7,6},{8,9},{9,8},{10,11... | collective-permute-start | bytes 786440 | tf_op jit(solution)/shard_map/ppermute | solution.py:496
  66.0 9.3 %collective-permute-start.15 = (f32[520,128]{1,0:T(8,128)S(1)}, f32[520,128]{1,0:T(8,128)S(1)}, u32[]{:S(2)}, u32[]{:S(2)}) collective-permute-start(f32[520,128]{1,0:T(8,128)S(1)} %pad_maximum_fusion.7), channel_id=1, source_target_pairs={{0,2},{1,3},{2,0},{3,1},{4,6},{5,7},{6,4},{7,5},{8,10},{9,11},{10,... | collective-permute-start | bytes 798728 | tf_op jit(solution)/shard_map/ppermute | solution.py:496
  69.8 7.9 %collective-permute-start.14 = (f32[776,128]{1,0:T(8,128)S(1)}, f32[776,128]{1,0:T(8,128)S(1)}, u32[]{:S(2)}, u32[]{:S(2)}) collective-permute-start(f32[776,128]{1,0:T(8,128)S(1)} %get-tuple-element.136), channel_id=1, source_target_pairs={{0,4},{1,9},{2,6},{3,11},{4,0},{5,13},{6,2},{7,15},{8,12},{9,1},{1... | collective-permute-start | bytes 1191944 | tf_op jit(solution)/shard_map/ppermute | solution.py:493
  75.3 2.5 %collective-permute-start.17 = (f32[512,128]{1,0:T(8,128)S(1)}, f32[512,128]{1,0:T(8,128)S(1)}, u32[]{:S(2)}, u32[]{:S(2)}) collective-permute-start(f32[512,128]{1,0:T(8,128)S(1)} %slice_add_fusion.10.refs_2_), channel_id=1, source_target_pairs={{0,1},{1,0},{2,3},{3,2},{4,5},{5,4},{6,7},{7,6},{8,9},{9,8},{10,11... | collective-permute-start | bytes 786440 | tf_op jit(solution)/shard_map/ppermute | solution.py:496
  77.8 5.8 %collective-permute-start.16 = (f32[392,128]{1,0:T(8,128)S(1)}, f32[392,128]{1,0:T(8,128)S(1)}, u32[]{:S(2)}, u32[]{:S(2)}) collective-permute-start(f32[392,128]{1,0:T(8,128)S(1)} %pad_maximum_fusion.14), channel_id=1, source_target_pairs={{0,8},{1,5},{2,10},{3,7},{4,12},{5,1},{6,14},{7,3},{8,0},{9,13},{1... | collective-permute-start | bytes 602120 | tf_op jit(solution)/shard_map/ppermute | solution.py:493
  79.5 13.3 %collective-permute-start.19 = (f32[776,128]{1,0:T(8,128)S(1)}, f32[776,128]{1,0:T(8,128)S(1)}, u32[]{:S(2)}, u32[]{:S(2)}) collective-permute-start(f32[776,128]{1,0:T(8,128)S(1)} %get-tuple-element.140), channel_id=1, source_target_pairs={{0,8},{1,5},{2,10},{3,7},{4,12},{5,1},{6,14},{7,3},{8,0},{9,13},{1... | collective-permute-start | bytes 1191944 | tf_op jit(solution)/shard_map/ppermute | solution.py:493
  83.6 9.8 %collective-permute-start.18 = (f32[392,128]{1,0:T(8,128)S(1)}, f32[392,128]{1,0:T(8,128)S(1)}, u32[]{:S(2)}, u32[]{:S(2)}) collective-permute-start(f32[392,128]{1,0:T(8,128)S(1)} %pad_maximum_fusion.15), channel_id=1, source_target_pairs={{0,16},{1,17},{2,18},{3,19},{4,20},{5,21},{6,22},{7,23},{8,24},{9,... | collective-permute-start | bytes 602120 | tf_op jit(solution)/shard_map/ppermute | solution.py:493
  92.9 5.8 %collective-permute-start.21 = (f32[392,128]{1,0:T(8,128)S(1)}, f32[392,128]{1,0:T(8,128)S(1)}, u32[]{:S(2)}, u32[]{:S(2)}) collective-permute-start(f32[392,128]{1,0:T(8,128)S(1)} %pad_maximum_fusion.16), channel_id=1, source_target_pairs={{0,4},{1,9},{2,6},{3,11},{4,0},{5,13},{6,2},{7,15},{8,12},{9,1},{1... | collective-permute-start | bytes 602120 | tf_op jit(solution)/shard_map/ppermute | solution.py:493
  93.5 12.9 %collective-permute-start.20 = (f32[384,128]{1,0:T(8,128)S(1)}, f32[384,128]{1,0:T(8,128)S(1)}, u32[]{:S(2)}, u32[]{:S(2)}) collective-permute-start(f32[384,128]{1,0:T(8,128)S(1)} %slice_add_fusion.23.mine_ref), channel_id=1, source_target_pairs={{0,8},{1,5},{2,10},{3,7},{4,12},{5,1},{6,14},{7,3},{8,0},{9,13},{1... | collective-permute-start | bytes 589832 | tf_op jit(solution)/shard_map/ppermute | solution.py:493
  98.7 8.5 %collective-permute-start.23 = (f32[392,128]{1,0:T(8,128)S(1)}, f32[392,128]{1,0:T(8,128)S(1)}, u32[]{:S(2)}, u32[]{:S(2)}) collective-permute-start(f32[392,128]{1,0:T(8,128)S(1)} %pad_maximum_fusion.17), channel_id=1, source_target_pairs={{0,16},{1,17},{2,18},{3,19},{4,20},{5,21},{6,22},{7,23},{8,24},{9,... | collective-permute-start | bytes 602120 | tf_op jit(solution)/shard_map/ppermute | solution.py:493
  106.4 7.8 %collective-permute-start.22 = (f32[768,128]{1,0:T(8,128)S(1)}, f32[768,128]{1,0:T(8,128)S(1)}, u32[]{:S(2)}, u32[]{:S(2)}) collective-permute-start(f32[768,128]{1,0:T(8,128)S(1)} %pad_maximum_fusion.2), channel_id=1, source_target_pairs={{0,4},{1,9},{2,6},{3,11},{4,0},{5,13},{6,2},{7,15},{8,12},{9,1},{1... | collective-permute-start | bytes 1179656 | tf_op jit(solution)/shard_map/ppermute | solution.py:493
  107.2 9.1 %collective-permute-start.25 = (f32[384,128]{1,0:T(8,128)S(1)}, f32[384,128]{1,0:T(8,128)S(1)}, u32[]{:S(2)}, u32[]{:S(2)}) collective-permute-start(f32[384,128]{1,0:T(8,128)S(1)} %slice_add_fusion.22.mine_ref), channel_id=1, source_target_pairs={{0,4},{1,9},{2,6},{3,11},{4,0},{5,13},{6,2},{7,15},{8,12},{9,1},{1... | collective-permute-start | bytes 589832 | tf_op jit(solution)/shard_map/ppermute | solution.py:493
  115.5 2.1 %collective-permute-start.24 = (f32[520,128]{1,0:T(8,128)S(1)}, f32[520,128]{1,0:T(8,128)S(1)}, u32[]{:S(2)}, u32[]{:S(2)}) collective-permute-start(f32[520,128]{1,0:T(8,128)S(1)} %get-tuple-element.154), channel_id=1, source_target_pairs={{0,1},{1,0},{2,3},{3,2},{4,5},{5,4},{6,7},{7,6},{8,9},{9,8},{10,11... | collective-permute-start | bytes 798728 | tf_op jit(solution)/shard_map/ppermute | solution.py:496
  116.4 7.8 %collective-permute-start.27 = (f32[768,128]{1,0:T(8,128)S(1)}, f32[768,128]{1,0:T(8,128)S(1)}, u32[]{:S(2)}, u32[]{:S(2)}) collective-permute-start(f32[768,128]{1,0:T(8,128)S(1)} %pad_maximum_fusion.3), channel_id=1, source_target_pairs={{0,8},{1,5},{2,10},{3,7},{4,12},{5,1},{6,14},{7,3},{8,0},{9,13},{1... | collective-permute-start | bytes 1179656 | tf_op jit(solution)/shard_map/ppermute | solution.py:493
  117.7 8.5 %collective-permute-start.26 = (f32[520,128]{1,0:T(8,128)S(1)}, f32[520,128]{1,0:T(8,128)S(1)}, u32[]{:S(2)}, u32[]{:S(2)}) collective-permute-start(f32[520,128]{1,0:T(8,128)S(1)} %pad_maximum_fusion.8), channel_id=1, source_target_pairs={{0,2},{1,3},{2,0},{3,1},{4,6},{5,7},{6,4},{7,5},{8,10},{9,11},{10,... | collective-permute-start | bytes 798728 | tf_op jit(solution)/shard_map/ppermute | solution.py:496
  125.5 2.0 %collective-permute-start.29 = (f32[520,128]{1,0:T(8,128)S(1)}, f32[520,128]{1,0:T(8,128)S(1)}, u32[]{:S(2)}, u32[]{:S(2)}) collective-permute-start(f32[520,128]{1,0:T(8,128)S(1)} %get-tuple-element.165), channel_id=1, source_target_pairs={{0,1},{1,0},{2,3},{3,2},{4,5},{5,4},{6,7},{7,6},{8,9},{9,8},{10,11... | collective-permute-start | bytes 798728 | tf_op jit(solution)/shard_map/ppermute | solution.py:496
  126.3 1.7 collective-permute-start.28
  127.6 8.9 %collective-permute-start.31 = (f32[520,128]{1,0:T(8,128)S(1)}, f32[520,128]{1,0:T(8,128)S(1)}, u32[]{:S(2)}, u32[]{:S(2)}) collective-permute-start(f32[520,128]{1,0:T(8,128)S(1)} %pad_maximum_fusion.9), channel_id=1, source_target_pairs={{0,2},{1,3},{2,0},{3,1},{4,6},{5,7},{6,4},{7,5},{8,10},{9,11},{10,... | collective-permute-start | bytes 798728 | tf_op jit(solution)/shard_map/ppermute | solution.py:496
  129.5 7.8 %collective-permute-start.30 = (f32[776,128]{1,0:T(8,128)S(1)}, f32[776,128]{1,0:T(8,128)S(1)}, u32[]{:S(2)}, u32[]{:S(2)}) collective-permute-start(f32[776,128]{1,0:T(8,128)S(1)} %get-tuple-element.172), channel_id=1, source_target_pairs={{0,4},{1,9},{2,6},{3,11},{4,0},{5,13},{6,2},{7,15},{8,12},{9,1},{1... | collective-permute-start | bytes 1191944 | tf_op jit(solution)/shard_map/ppermute | solution.py:493
  136.5 1.6 collective-permute-start.33
  137.4 5.8 %collective-permute-start.32 = (f32[392,128]{1,0:T(8,128)S(1)}, f32[392,128]{1,0:T(8,128)S(1)}, u32[]{:S(2)}, u32[]{:S(2)}) collective-permute-start(f32[392,128]{1,0:T(8,128)S(1)} %pad_maximum_fusion.18), channel_id=1, source_target_pairs={{0,8},{1,5},{2,10},{3,7},{4,12},{5,1},{6,14},{7,3},{8,0},{9,13},{1... | collective-permute-start | bytes 602120 | tf_op jit(solution)/shard_map/ppermute | solution.py:493
  139.7 10.0 %collective-permute-start.35 = (f32[776,128]{1,0:T(8,128)S(1)}, f32[776,128]{1,0:T(8,128)S(1)}, u32[]{:S(2)}, u32[]{:S(2)}) collective-permute-start(f32[776,128]{1,0:T(8,128)S(1)} %get-tuple-element.178), channel_id=1, source_target_pairs={{0,8},{1,5},{2,10},{3,7},{4,12},{5,1},{6,14},{7,3},{8,0},{9,13},{1... | collective-permute-start | bytes 1191944 | tf_op jit(solution)/shard_map/ppermute | solution.py:493
  143.3 9.6 %collective-permute-start.34 = (f32[392,128]{1,0:T(8,128)S(1)}, f32[392,128]{1,0:T(8,128)S(1)}, u32[]{:S(2)}, u32[]{:S(2)}) collective-permute-start(f32[392,128]{1,0:T(8,128)S(1)} %pad_maximum_fusion.19), channel_id=1, source_target_pairs={{0,16},{1,17},{2,18},{3,19},{4,20},{5,21},{6,22},{7,23},{8,24},{9,... | collective-permute-start | bytes 602120 | tf_op jit(solution)/shard_map/ppermute | solution.py:493
  149.7 7.7 %collective-permute-start.36 = (f32[392,128]{1,0:T(8,128)S(1)}, f32[392,128]{1,0:T(8,128)S(1)}, u32[]{:S(2)}, u32[]{:S(2)}) collective-permute-start(f32[392,128]{1,0:T(8,128)S(1)} %pad_maximum_fusion.20), channel_id=1, source_target_pairs={{0,4},{1,9},{2,6},{3,11},{4,0},{5,13},{6,2},{7,15},{8,12},{9,1},{1... | collective-permute-start | bytes 602120 | tf_op jit(solution)/shard_map/ppermute | solution.py:493
  152.9 6.9 %collective-permute-start.38 = (f32[384,128]{1,0:T(8,128)S(1)}, f32[384,128]{1,0:T(8,128)S(1)}, u32[]{:S(2)}, u32[]{:S(2)}) collective-permute-start(f32[384,128]{1,0:T(8,128)S(1)} %slice_add_fusion.21.mine_ref), channel_id=1, source_target_pairs={{0,8},{1,5},{2,10},{3,7},{4,12},{5,1},{6,14},{7,3},{8,0},{9,13},{1... | collective-permute-start | bytes 589832 | tf_op jit(solution)/shard_map/ppermute | solution.py:493
  157.5 8.9 %collective-permute-start.37 = (f32[392,128]{1,0:T(8,128)S(1)}, f32[392,128]{1,0:T(8,128)S(1)}, u32[]{:S(2)}, u32[]{:S(2)}) collective-permute-start(f32[392,128]{1,0:T(8,128)S(1)} %pad_maximum_fusion.21), channel_id=1, source_target_pairs={{0,16},{1,17},{2,18},{3,19},{4,20},{5,21},{6,22},{7,23},{8,24},{9,... | collective-permute-start | bytes 602120 | tf_op jit(solution)/shard_map/ppermute | solution.py:493
  166.4 7.0 %collective-permute-start.40 = (f32[384,128]{1,0:T(8,128)S(1)}, f32[384,128]{1,0:T(8,128)S(1)}, u32[]{:S(2)}, u32[]{:S(2)}) collective-permute-start(f32[384,128]{1,0:T(8,128)S(1)} %slice_add_fusion.20.refs_6_), channel_id=1, source_target_pairs={{0,4},{1,9},{2,6},{3,11},{4,0},{5,13},{6,2},{7,15},{8,12},{9,1},{1... | collective-permute-start | bytes 589832 | tf_op jit(solution)/shard_map/ppermute | solution.py:493
  167.9 12.7 %collective-permute-start.39 = (f32[768,128]{1,0:T(8,128)S(1)}, f32[768,128]{1,0:T(8,128)S(1)}, u32[]{:S(2)}, u32[]{:S(2)}) collective-permute-start(f32[768,128]{1,0:T(8,128)S(1)} %pad_maximum_fusion.4), channel_id=1, source_target_pairs={{0,4},{1,9},{2,6},{3,11},{4,0},{5,13},{6,2},{7,15},{8,12},{9,1},{1... | collective-permute-start | bytes 1179656 | tf_op jit(solution)/shard_map/ppermute | solution.py:493
  173.5 7.8 %collective-permute-start.41 = (f32[768,128]{1,0:T(8,128)S(1)}, f32[768,128]{1,0:T(8,128)S(1)}, u32[]{:S(2)}, u32[]{:S(2)}) collective-permute-start(f32[768,128]{1,0:T(8,128)S(1)} %pad_maximum_fusion.5), channel_id=1, source_target_pairs={{0,8},{1,5},{2,10},{3,7},{4,12},{5,1},{6,14},{7,3},{8,0},{9,13},{1... | collective-permute-start | bytes 1179656 | tf_op jit(solution)/shard_map/ppermute | solution.py:493

commit v23 on v21

--- a/solution.py
+++ b/solution.py
@@ -61,39 +61,18 @@
 
     for position in range(row_blocks):
         fetch(position, 0).start()
-    for copy in small[:2]:
-        copy.wait()
-    for position in range(row_blocks):
-
-        @pl.when(counts_ref[position ^ flip] > half)
-        def _():
-            fetch(position, 1).start()
-
     @pl.loop(0, row_blocks)
     def _(position):
         rows = pl.ds(pl.multiple_of(position * TILE, TILE), TILE)
         dense_ref[rows, :] = jnp.zeros((TILE, dense_ref.shape[1]), dense_ref.dtype)
 
-    @pl.loop(0, row_blocks)
-    def _(position):
-        rows = pl.ds(pl.multiple_of(position * TILE, TILE), TILE)
-        block = position ^ flip
-        count = counts_ref[block]
-
-        def place(tile):
-            column = jnp.where(tile < count, place_ref[pattern_ref[block, tile]], CB_DEV)
-            lanes = pl.ds(pl.multiple_of(column * TILE, TILE), TILE)
-            dense_ref[rows, lanes] = tiles_ref[position, tile]
-
-        fetch(position, 0).wait()
-        for tile in range(half):
-            place(tile)
-
-        @pl.when(count > half)
+    for copy in small[:2]:
+        copy.wait()
+    for position in range(row_blocks):
+
+        @pl.when(counts_ref[position ^ flip] > half)
         def _():
-            fetch(position, 1).wait()
-            for tile in range(half, 2 * half):
-                place(tile)
+            fetch(position, 1).start()
 
     small[2].wait()
     low = low_lanes((TILE, TILE))
@@ -103,6 +82,27 @@
         odd = delays_ref[pl.ds(pl.multiple_of(source + TILE, TILE), TILE), :]
         even_left_ref[rows_of(pair), :] = jnp.where(low, even, turned(odd))
         odd_left_ref[rows_of(pair), :] = jnp.where(low, turned(even), odd)
+
+    @pl.loop(0, row_blocks)
+    def _(position):
+        rows = pl.ds(pl.multiple_of(position * TILE, TILE), TILE)
+        block = position ^ flip
+        count = counts_ref[block]
+
+        def place(tile):
+            column = jnp.where(tile < count, place_ref[pattern_ref[block, tile]], CB_DEV)
+            lanes = pl.ds(pl.multiple_of(column * TILE, TILE), TILE)
+            dense_ref[rows, lanes] = tiles_ref[position, tile]
+
+        fetch(position, 0).wait()
+        for tile in range(half):
+            place(tile)
+
+        @pl.when(count > half)
+        def _():
+            fetch(position, 1).wait()
+            for tile in range(half, 2 * half):
+                place(tile)
 
 
 def fill_dense(kernel, pattern, counts, places, flip, delays):

time: 184 us -> 182 us (0.989)
  starting transfers between devices: 40.2 us -> 37.4 us
  transfers between devices with their start and end apart: 42 -> 42, of which waited for: 32 -> 33; matrix products, arithmetic and copies ran while one was open for 1% -> 1% of each run, Pallas kernels for 18% -> 18%
where the time goes in v23:
time: 182 us; the launch traced here: 181 us
  waiting for transfers between devices  101 us (55%)
  Pallas kernels  38.9 us (21%)
  starting transfers between devices  37.4 us (21%)
    ppermute x30, waiting for transfers between devices, swap_rows(): return lax.ppermute(value, ('rows', 'cols'), pairs)  91.9 us
    pallas_call x24, Pallas kernels, product_call(): pl.pallas_call(body, in_specs=[WHOLE] * (1 + len(operands)), out_specs=[W...  32.2 us
    ppermute x30, starting transfers between devices, swap_rows(): return lax.ppermute(value, ('rows', 'cols'), pairs)  32.1 us
    ppermute x12, waiting for transfers between devices, swap_cols(): lax.ppermute(value, 'cols', [(i, i ^ 1 << level) for i in range(col_count)])  8.85 us
    ppermute x12, starting transfers between devices, swap_cols(): lax.ppermute(value, 'cols', [(i, i ^ 1 << level) for i in range(col_count)])  5.34 us
  transfers between devices with their start and end apart: 42, of which 33 were waited for; matrix products, arithmetic and copies ran while one was open for 1% of the time, Pallas kernels for 18%

profile of v23, /device:TPU:0, one launch (start us, length us, event | category | flops | bytes accessed | tf_op | source)
XLA Modules:
  0.0 180.9 jit_solution(17283253728830512511)
XLA Ops:
  0.7 3.5 %shard_map.67 = (bf16[2048,3200]{1,0:T(8,128)(2,1)S(1)}, f32[1024,128]{1,0:T(8,128)S(1)}, f32[1024,128]{1,0:T(8,128)S(1)}) custom-call(s32[24]{0:T(128)S(1)} %fusion.place_ref, s32[1]{0:T(128)} %bitcast.1.flip_ref, s32[16,16]{1,0:T(8,128)} %pattern_in.1, s32[16]{0:T(128)} %bitcast.5, f32[2048,128]{1,0:T(8,128)} %delays_in.1, bf16[16,16,128,128]{3,2,1,0:T(8,128)(2,1)} %tiles_in.1), custom_call_target="tpu_custom_call" | custom-call | bytes 8388608 | tf_op jit(solution)/shard_map/pallas_call | solution.py:112
  4.1 1.4 shard_map.68
  5.5 3.0 %collective-permute-start = (f32[776,128]{1,0:T(8,128)S(1)}, f32[776,128]{1,0:T(8,128)S(1)}, u32[]{:S(2)}, u32[]{:S(2)}) collective-permute-start(f32[776,128]{1,0:T(8,128)S(1)} %get-tuple-element.102), channel_id=1, source_target_pairs={{0,4},{1,9},{2,6},{3,11},{4,0},{5,13},{6,2},{7,15},{8,12},{9,1},{1... | collective-permute-start | bytes 1191944 | tf_op jit(solution)/shard_map/ppermute | solution.py:498
  9.8 1.4 shard_map.70
  11.2 3.1 %collective-permute-done = f32[776,128]{1,0:T(8,128)S(1)} collective-permute-done((f32[776,128]{1,0:T(8,128)S(1)}, f32[776,128]{1,0:T(8,128)S(1)}, u32[]{:S(2)}, u32[]{:S(2)}) %collective-permute-start) | collective-permute-done | bytes 397344 | tf_op jit(solution)/shard_map/ppermute | solution.py:498
  14.5 3.0 %collective-permute-start.1 = (f32[392,128]{1,0:T(8,128)S(1)}, f32[392,128]{1,0:T(8,128)S(1)}, u32[]{:S(2)}, u32[]{:S(2)}) collective-permute-start(f32[392,128]{1,0:T(8,128)S(1)} %pad_maximum_fusion.10), channel_id=1, source_target_pairs={{0,8},{1,5},{2,10},{3,7},{4,12},{5,1},{6,14},{7,3},{8,0},{9,13},{1... | collective-permute-start | bytes 602120 | tf_op jit(solution)/shard_map/ppermute | solution.py:498
  18.8 2.3 %collective-permute-done.1 = f32[392,128]{1,0:T(8,128)S(1)} collective-permute-done((f32[392,128]{1,0:T(8,128)S(1)}, f32[392,128]{1,0:T(8,128)S(1)}, u32[]{:S(2)}, u32[]{:S(2)}) %collective-permute-start.1) | collective-permute-done | bytes 200736 | tf_op jit(solution)/shard_map/ppermute | solution.py:498
  21.2 2.3 %collective-permute-start.2 = (f32[392,128]{1,0:T(8,128)S(1)}, f32[392,128]{1,0:T(8,128)S(1)}, u32[]{:S(2)}, u32[]{:S(2)}) collective-permute-start(f32[392,128]{1,0:T(8,128)S(1)} %pad_maximum_fusion.11), channel_id=1, source_target_pairs={{0,16},{1,17},{2,18},{3,19},{4,20},{5,21},{6,22},{7,23},{8,24},{9,... | collective-permute-start | bytes 602120 | tf_op jit(solution)/shard_map/ppermute | solution.py:498
  23.5 9.3 %collective-permute-done.3 = f32[776,128]{1,0:T(8,128)S(1)} collective-permute-done((f32[776,128]{1,0:T(8,128)S(1)}, f32[776,128]{1,0:T(8,128)S(1)}, u32[]{:S(2)}, u32[]{:S(2)}) %collective-permute-start.3) | collective-permute-done | bytes 397344 | tf_op jit(solution)/shard_map/ppermute | solution.py:498
  33.5 1.4 collective-permute-start.4
  34.9 3.7 %collective-permute-done.5 = f32[392,128]{1,0:T(8,128)S(1)} collective-permute-done((f32[392,128]{1,0:T(8,128)S(1)}, f32[392,128]{1,0:T(8,128)S(1)}, u32[]{:S(2)}, u32[]{:S(2)}) %collective-permute-start.5) | collective-permute-done | bytes 200736 | tf_op jit(solution)/shard_map/ppermute | solution.py:498
  38.8 4.7 %collective-permute-done.4.inner_ref = f32[384,128]{1,0:T(8,128)S(1)} collective-permute-done((f32[384,128]{1,0:T(8,128)S(1)}, f32[384,128]{1,0:T(8,128)S(1)}, u32[]{:S(2)}, u32[]{:S(2)}) %collective-permute-start.4) | collective-permute-done | bytes 196640 | tf_op jit(solution)/shard_map/ppermute | solution.py:498
  43.5 1.8 %collective-permute-start.6 = (f32[768,128]{1,0:T(8,128)S(1)}, f32[768,128]{1,0:T(8,128)S(1)}, u32[]{:S(2)}, u32[]{:S(2)}) collective-permute-start(f32[768,128]{1,0:T(8,128)S(1)} %pad_maximum_fusion), channel_id=1, source_target_pairs={{0,4},{1,9},{2,6},{3,11},{4,0},{5,13},{6,2},{7,15},{8,12},{9,1},{1... | collective-permute-start | bytes 1179656 | tf_op jit(solution)/shard_map/ppermute | solution.py:498
  45.4 1.8 collective-permute-done.7
  47.8 1.9 %shard_map.72 = (f32[1024,128]{1,0:T(8,128)S(1)}, f32[8,128]{1,0:T(8,128)S(1)}, f32[768,128]{1,0:T(8,128)S(1)}) custom-call(bf16[2048,3200]{1,0:T(8,128)(2,1)S(1)} %get-tuple-element.99.refs_0_.dense_ref, f32[384,128]{1,0:T(8,128)S(1)} %collective-permute-done.4.inner_ref, f32[384,128]{1,0:T(8,128)S(1)} %slice_add_fusion.25.mine_ref, ...), custom_call_target="tpu_custom_call" | custom-call | flops 1677721600 | bytes 6553600 | tf_op jit(solution)/shard_map/pallas_call | solution.py:268
  49.7 1.7 collective-permute-done.6.outer_ref
  54.7 2.0 %collective-permute-start.10 = (f32[520,128]{1,0:T(8,128)S(1)}, f32[520,128]{1,0:T(8,128)S(1)}, u32[]{:S(2)}, u32[]{:S(2)}) collective-permute-start(f32[520,128]{1,0:T(8,128)S(1)} %pad_maximum_fusion.6), channel_id=1, source_target_pairs={{0,2},{1,3},{2,0},{3,1},{4,6},{5,7},{6,4},{7,5},{8,10},{9,11},{10,... | collective-permute-start | bytes 798728 | tf_op jit(solution)/shard_map/ppermute | solution.py:501
  56.7 1.9 %shard_map.75 = (f32[1024,128]{1,0:T(8,128)S(1)}, f32[8,128]{1,0:T(8,128)S(1)}, f32[768,128]{1,0:T(8,128)S(1)}) custom-call(bf16[2048,3200]{1,0:T(8,128)(2,1)S(1)} %get-tuple-element.99.refs_0_.dense_ref, f32[384,128]{1,0:T(8,128)S(1)} %collective-permute-done.8.inner_ref, f32[384,128]{1,0:T(8,128)S(1)} %slice_add_fusion.24.mine_ref, ...), custom_call_target="tpu_custom_call" | custom-call | flops 1677721600 | bytes 6553600 | tf_op jit(solution)/shard_map/pallas_call | solution.py:268
  58.6 2.8 %collective-permute-done.11.outer_ref = f32[768,128]{1,0:T(8,128)S(1)} collective-permute-done((f32[768,128]{1,0:T(8,128)S(1)}, f32[768,128]{1,0:T(8,128)S(1)}, u32[]{:S(2)}, u32[]{:S(2)}) %collective-permute-start.11) | collective-permute-done | bytes 393248 | tf_op jit(solution)/shard_map/ppermute | solution.py:498
  65.0 2.0 %collective-permute-start.15 = (f32[520,128]{1,0:T(8,128)S(1)}, f32[520,128]{1,0:T(8,128)S(1)}, u32[]{:S(2)}, u32[]{:S(2)}) collective-permute-start(f32[520,128]{1,0:T(8,128)S(1)} %pad_maximum_fusion.7), channel_id=1, source_target_pairs={{0,2},{1,3},{2,0},{3,1},{4,6},{5,7},{6,4},{7,5},{8,10},{9,11},{10,... | collective-permute-start | bytes 798728 | tf_op jit(solution)/shard_map/ppermute | solution.py:501
  67.0 1.4 shard_map.78
  68.5 1.3 collective-permute-start.14
  71.1 2.9 %collective-permute-done.15 = f32[520,128]{1,0:T(8,128)S(1)} collective-permute-done((f32[520,128]{1,0:T(8,128)S(1)}, f32[520,128]{1,0:T(8,128)S(1)}, u32[]{:S(2)}, u32[]{:S(2)}) %collective-permute-start.15) | collective-permute-done | bytes 266272 | tf_op jit(solution)/shard_map/ppermute | solution.py:501
  74.1 2.3 %collective-permute-done.14 = f32[776,128]{1,0:T(8,128)S(1)} collective-permute-done((f32[776,128]{1,0:T(8,128)S(1)}, f32[776,128]{1,0:T(8,128)S(1)}, u32[]{:S(2)}, u32[]{:S(2)}) %collective-permute-start.14) | collective-permute-done | bytes 397344 | tf_op jit(solution)/shard_map/ppermute | solution.py:498
  76.7 1.4 shard_map.80
  78.2 1.9 %collective-permute-start.19 = (f32[776,128]{1,0:T(8,128)S(1)}, f32[776,128]{1,0:T(8,128)S(1)}, u32[]{:S(2)}, u32[]{:S(2)}) collective-permute-start(f32[776,128]{1,0:T(8,128)S(1)} %get-tuple-element.140), channel_id=1, source_target_pairs={{0,8},{1,5},{2,10},{3,7},{4,12},{5,1},{6,14},{7,3},{8,0},{9,13},{1... | collective-permute-start | bytes 1191944 | tf_op jit(solution)/shard_map/ppermute | solution.py:498
  82.4 8.8 %collective-permute-done.19 = f32[776,128]{1,0:T(8,128)S(1)} collective-permute-done((f32[776,128]{1,0:T(8,128)S(1)}, f32[776,128]{1,0:T(8,128)S(1)}, u32[]{:S(2)}, u32[]{:S(2)}) %collective-permute-start.19) | collective-permute-done | bytes 397344 | tf_op jit(solution)/shard_map/ppermute | solution.py:498
  91.2 1.7 collective-permute-start.21
  94.0 3.0 %collective-permute-done.21 = f32[392,128]{1,0:T(8,128)S(1)} collective-permute-done((f32[392,128]{1,0:T(8,128)S(1)}, f32[392,128]{1,0:T(8,128)S(1)}, u32[]{:S(2)}, u32[]{:S(2)}) %collective-permute-start.21) | collective-permute-done | bytes 200736 | tf_op jit(solution)/shard_map/ppermute | solution.py:498
  97.2 7.9 %collective-permute-done.20.inner_ref = f32[384,128]{1,0:T(8,128)S(1)} collective-permute-done((f32[384,128]{1,0:T(8,128)S(1)}, f32[384,128]{1,0:T(8,128)S(1)}, u32[]{:S(2)}, u32[]{:S(2)}) %collective-permute-start.20) | collective-permute-done | bytes 196640 | tf_op jit(solution)/shard_map/ppermute | solution.py:498
  105.2 2.1 %collective-permute-start.25 = (f32[384,128]{1,0:T(8,128)S(1)}, f32[384,128]{1,0:T(8,128)S(1)}, u32[]{:S(2)}, u32[]{:S(2)}) collective-permute-start(f32[384,128]{1,0:T(8,128)S(1)} %slice_add_fusion.22.mine_ref), channel_id=1, source_target_pairs={{0,4},{1,9},{2,6},{3,11},{4,0},{5,13},{6,2},{7,15},{8,12},{9,1},{1... | collective-permute-start | bytes 589832 | tf_op jit(solution)/shard_map/ppermute | solution.py:498
  107.3 1.9 %shard_map.82 = (f32[1024,128]{1,0:T(8,128)S(1)}, f32[8,128]{1,0:T(8,128)S(1)}, f32[768,128]{1,0:T(8,128)S(1)}) custom-call(bf16[2048,3200]{1,0:T(8,128)(2,1)S(1)} %get-tuple-element.99.refs_0_.dense_ref, f32[384,128]{1,0:T(8,128)S(1)} %collective-permute-done.20.inner_ref, f32[384,128]{1,0:T(8,128)S(1)} %slice_add_fusion.23.mine_ref, ...), custom_call_target="tpu_custom_call" | custom-call | flops 1677721600 | bytes 6553600 | tf_op jit(solution)/shard_map/pallas_call | solution.py:268
  109.2 3.8 %collective-permute-done.22.outer_ref = f32[768,128]{1,0:T(8,128)S(1)} collective-permute-done((f32[768,128]{1,0:T(8,128)S(1)}, f32[768,128]{1,0:T(8,128)S(1)}, u32[]{:S(2)}, u32[]{:S(2)}) %collective-permute-start.22) | collective-permute-done | bytes 393248 | tf_op jit(solution)/shard_map/ppermute | solution.py:498
  116.3 1.9 %shard_map.85 = (f32[1024,128]{1,0:T(8,128)S(1)}, f32[8,128]{1,0:T(8,128)S(1)}, f32[768,128]{1,0:T(8,128)S(1)}) custom-call(bf16[2048,3200]{1,0:T(8,128)(2,1)S(1)} %get-tuple-element.99.refs_0_.dense_ref, f32[384,128]{1,0:T(8,128)S(1)} %collective-permute-done.25.inner_ref, f32[384,128]{1,0:T(8,128)S(1)} %slice_add_fusion.22.mine_ref, ...), custom_call_target="tpu_custom_call" | custom-call | flops 1677721600 | bytes 6553600 | tf_op jit(solution)/shard_map/pallas_call | solution.py:268
  118.2 4.7 %collective-permute-done.27.outer_ref = f32[768,128]{1,0:T(8,128)S(1)} collective-permute-done((f32[768,128]{1,0:T(8,128)S(1)}, f32[768,128]{1,0:T(8,128)S(1)}, u32[]{:S(2)}, u32[]{:S(2)}) %collective-permute-start.27) | collective-permute-done | bytes 393248 | tf_op jit(solution)/shard_map/ppermute | solution.py:498
  126.0 1.5 shard_map.88
  128.4 1.3 shard_map.89
  129.6 4.6 %collective-permute-done.31 = f32[520,128]{1,0:T(8,128)S(1)} collective-permute-done((f32[520,128]{1,0:T(8,128)S(1)}, f32[520,128]{1,0:T(8,128)S(1)}, u32[]{:S(2)}, u32[]{:S(2)}) %collective-permute-start.31) | collective-permute-done | bytes 266272 | tf_op jit(solution)/shard_map/ppermute | solution.py:501
  135.9 1.5 shard_map.90
  137.4 1.6 collective-permute-start.35
  141.8 5.9 %collective-permute-done.35 = f32[776,128]{1,0:T(8,128)S(1)} collective-permute-done((f32[776,128]{1,0:T(8,128)S(1)}, f32[776,128]{1,0:T(8,128)S(1)}, u32[]{:S(2)}, u32[]{:S(2)}) %collective-permute-start.35) | collective-permute-done | bytes 397344 | tf_op jit(solution)/shard_map/ppermute | solution.py:498
  148.8 2.0 %collective-permute-done.34 = f32[392,128]{1,0:T(8,128)S(1)} collective-permute-done((f32[392,128]{1,0:T(8,128)S(1)}, f32[392,128]{1,0:T(8,128)S(1)}, u32[]{:S(2)}, u32[]{:S(2)}) %collective-permute-start.34) | collective-permute-done | bytes 200736 | tf_op jit(solution)/shard_map/ppermute | solution.py:498
  150.9 3.0 %collective-permute-start.38 = (f32[384,128]{1,0:T(8,128)S(1)}, f32[384,128]{1,0:T(8,128)S(1)}, u32[]{:S(2)}, u32[]{:S(2)}) collective-permute-start(f32[384,128]{1,0:T(8,128)S(1)} %slice_add_fusion.21.mine_ref), channel_id=1, source_target_pairs={{0,8},{1,5},{2,10},{3,7},{4,12},{5,1},{6,14},{7,3},{8,0},{9,13},{1... | collective-permute-start | bytes 589832 | tf_op jit(solution)/shard_map/ppermute | solution.py:498
  153.9 1.7 collective-permute-done.36
  157.7 6.8 %collective-permute-done.37 = f32[392,128]{1,0:T(8,128)S(1)} collective-permute-done((f32[392,128]{1,0:T(8,128)S(1)}, f32[392,128]{1,0:T(8,128)S(1)}, u32[]{:S(2)}, u32[]{:S(2)}) %collective-permute-start.37) | collective-permute-done | bytes 200736 | tf_op jit(solution)/shard_map/ppermute | solution.py:498
  166.6 5.0 %collective-permute-done.40.refs_5_ = f32[384,128]{1,0:T(8,128)S(1)} collective-permute-done((f32[384,128]{1,0:T(8,128)S(1)}, f32[384,128]{1,0:T(8,128)S(1)}, u32[]{:S(2)}, u32[]{:S(2)}) %collective-permute-start.40) | collective-permute-done | bytes 196640 | tf_op jit(solution)/shard_map/ppermute | solution.py:498
  171.8 1.8 shard_map.92
  174.1 4.6 %collective-permute-done.39.outer_ref = f32[768,128]{1,0:T(8,128)S(1)} collective-permute-done((f32[768,128]{1,0:T(8,128)S(1)}, f32[768,128]{1,0:T(8,128)S(1)}, u32[]{:S(2)}, u32[]{:S(2)}) %collective-permute-start.39) | collective-permute-done | bytes 393248 | tf_op jit(solution)/shard_map/ppermute | solution.py:498
  (146 shorter events, 36.0 us)
Async XLA Ops:
  5.5 8.8 %collective-permute-start = (f32[776,128]{1,0:T(8,128)S(1)}, f32[776,128]{1,0:T(8,128)S(1)}, u32[]{:S(2)}, u32[]{:S(2)}) collective-permute-start(f32[776,128]{1,0:T(8,128)S(1)} %get-tuple-element.102), channel_id=1, source_target_pairs={{0,4},{1,9},{2,6},{3,11},{4,0},{5,13},{6,2},{7,15},{8,12},{9,1},{1... | collective-permute-start | bytes 1191944 | tf_op jit(solution)/shard_map/ppermute | solution.py:498
  14.5 6.7 %collective-permute-start.1 = (f32[392,128]{1,0:T(8,128)S(1)}, f32[392,128]{1,0:T(8,128)S(1)}, u32[]{:S(2)}, u32[]{:S(2)}) collective-permute-start(f32[392,128]{1,0:T(8,128)S(1)} %pad_maximum_fusion.10), channel_id=1, source_target_pairs={{0,8},{1,5},{2,10},{3,7},{4,12},{5,1},{6,14},{7,3},{8,0},{9,13},{1... | collective-permute-start | bytes 602120 | tf_op jit(solution)/shard_map/ppermute | solution.py:498
  18.7 14.0 %collective-permute-start.3 = (f32[776,128]{1,0:T(8,128)S(1)}, f32[776,128]{1,0:T(8,128)S(1)}, u32[]{:S(2)}, u32[]{:S(2)}) collective-permute-start(f32[776,128]{1,0:T(8,128)S(1)} %get-tuple-element.106), channel_id=1, source_target_pairs={{0,8},{1,5},{2,10},{3,7},{4,12},{5,1},{6,14},{7,3},{8,0},{9,13},{1... | collective-permute-start | bytes 1191944 | tf_op jit(solution)/shard_map/ppermute | solution.py:498
  21.2 12.3 %collective-permute-start.2 = (f32[392,128]{1,0:T(8,128)S(1)}, f32[392,128]{1,0:T(8,128)S(1)}, u32[]{:S(2)}, u32[]{:S(2)}) collective-permute-start(f32[392,128]{1,0:T(8,128)S(1)} %pad_maximum_fusion.11), channel_id=1, source_target_pairs={{0,16},{1,17},{2,18},{3,19},{4,20},{5,21},{6,22},{7,23},{8,24},{9,... | collective-permute-start | bytes 602120 | tf_op jit(solution)/shard_map/ppermute | solution.py:498
  32.9 5.8 %collective-permute-start.5 = (f32[392,128]{1,0:T(8,128)S(1)}, f32[392,128]{1,0:T(8,128)S(1)}, u32[]{:S(2)}, u32[]{:S(2)}) collective-permute-start(f32[392,128]{1,0:T(8,128)S(1)} %pad_maximum_fusion.12), channel_id=1, source_target_pairs={{0,4},{1,9},{2,6},{3,11},{4,0},{5,13},{6,2},{7,15},{8,12},{9,1},{1... | collective-permute-start | bytes 602120 | tf_op jit(solution)/shard_map/ppermute | solution.py:498
  33.5 10.0 %collective-permute-start.4 = (f32[384,128]{1,0:T(8,128)S(1)}, f32[384,128]{1,0:T(8,128)S(1)}, u32[]{:S(2)}, u32[]{:S(2)}) collective-permute-start(f32[384,128]{1,0:T(8,128)S(1)} %slice_add_fusion.25.mine_ref), channel_id=1, source_target_pairs={{0,8},{1,5},{2,10},{3,7},{4,12},{5,1},{6,14},{7,3},{8,0},{9,13},{1... | collective-permute-start | bytes 589832 | tf_op jit(solution)/shard_map/ppermute | solution.py:498
  38.7 8.5 %collective-permute-start.7 = (f32[392,128]{1,0:T(8,128)S(1)}, f32[392,128]{1,0:T(8,128)S(1)}, u32[]{:S(2)}, u32[]{:S(2)}) collective-permute-start(f32[392,128]{1,0:T(8,128)S(1)} %pad_maximum_fusion.13), channel_id=1, source_target_pairs={{0,16},{1,17},{2,18},{3,19},{4,20},{5,21},{6,22},{7,23},{8,24},{9,... | collective-permute-start | bytes 602120 | tf_op jit(solution)/shard_map/ppermute | solution.py:498
  43.5 7.8 %collective-permute-start.6 = (f32[768,128]{1,0:T(8,128)S(1)}, f32[768,128]{1,0:T(8,128)S(1)}, u32[]{:S(2)}, u32[]{:S(2)}) collective-permute-start(f32[768,128]{1,0:T(8,128)S(1)} %pad_maximum_fusion), channel_id=1, source_target_pairs={{0,4},{1,9},{2,6},{3,11},{4,0},{5,13},{6,2},{7,15},{8,12},{9,1},{1... | collective-permute-start | bytes 1179656 | tf_op jit(solution)/shard_map/ppermute | solution.py:498
  47.2 6.3 %collective-permute-start.8 = (f32[384,128]{1,0:T(8,128)S(1)}, f32[384,128]{1,0:T(8,128)S(1)}, u32[]{:S(2)}, u32[]{:S(2)}) collective-permute-start(f32[384,128]{1,0:T(8,128)S(1)} %slice_add_fusion.24.mine_ref), channel_id=1, source_target_pairs={{0,4},{1,9},{2,6},{3,11},{4,0},{5,13},{6,2},{7,15},{8,12},{9,1},{1... | collective-permute-start | bytes 589832 | tf_op jit(solution)/shard_map/ppermute | solution.py:498
  52.5 2.1 %collective-permute-start.9 = (f32[520,128]{1,0:T(8,128)S(1)}, f32[520,128]{1,0:T(8,128)S(1)}, u32[]{:S(2)}, u32[]{:S(2)}) collective-permute-start(f32[520,128]{1,0:T(8,128)S(1)} %get-tuple-element.121), channel_id=1, source_target_pairs={{0,1},{1,0},{2,3},{3,2},{4,5},{5,4},{6,7},{7,6},{8,9},{9,8},{10,11... | collective-permute-start | bytes 798728 | tf_op jit(solution)/shard_map/ppermute | solution.py:501
  53.5 7.8 %collective-permute-start.11 = (f32[768,128]{1,0:T(8,128)S(1)}, f32[768,128]{1,0:T(8,128)S(1)}, u32[]{:S(2)}, u32[]{:S(2)}) collective-permute-start(f32[768,128]{1,0:T(8,128)S(1)} %pad_maximum_fusion.1), channel_id=1, source_target_pairs={{0,8},{1,5},{2,10},{3,7},{4,12},{5,1},{6,14},{7,3},{8,0},{9,13},{1... | collective-permute-start | bytes 1179656 | tf_op jit(solution)/shard_map/ppermute | solution.py:498
  54.7 8.9 %collective-permute-start.10 = (f32[520,128]{1,0:T(8,128)S(1)}, f32[520,128]{1,0:T(8,128)S(1)}, u32[]{:S(2)}, u32[]{:S(2)}) collective-permute-start(f32[520,128]{1,0:T(8,128)S(1)} %pad_maximum_fusion.6), channel_id=1, source_target_pairs={{0,2},{1,3},{2,0},{3,1},{4,6},{5,7},{6,4},{7,5},{8,10},{9,11},{10,... | collective-permute-start | bytes 798728 | tf_op jit(solution)/shard_map/ppermute | solution.py:501
  62.5 2.5 %collective-permute-start.13 = (f32[520,128]{1,0:T(8,128)S(1)}, f32[520,128]{1,0:T(8,128)S(1)}, u32[]{:S(2)}, u32[]{:S(2)}) collective-permute-start(f32[520,128]{1,0:T(8,128)S(1)} %get-tuple-element.129), channel_id=1, source_target_pairs={{0,1},{1,0},{2,3},{3,2},{4,5},{5,4},{6,7},{7,6},{8,9},{9,8},{10,11... | collective-permute-start | bytes 798728 | tf_op jit(solution)/shard_map/ppermute | solution.py:501
  63.6 3.4 %collective-permute-start.12 = (f32[512,128]{1,0:T(8,128)S(1)}, f32[512,128]{1,0:T(8,128)S(1)}, u32[]{:S(2)}, u32[]{:S(2)}) collective-permute-start(f32[512,128]{1,0:T(8,128)S(1)} %slice_add_fusion.12.refs_2_), channel_id=1, source_target_pairs={{0,1},{1,0},{2,3},{3,2},{4,5},{5,4},{6,7},{7,6},{8,9},{9,8},{10,11... | collective-permute-start | bytes 786440 | tf_op jit(solution)/shard_map/ppermute | solution.py:501
  65.0 8.9 %collective-permute-start.15 = (f32[520,128]{1,0:T(8,128)S(1)}, f32[520,128]{1,0:T(8,128)S(1)}, u32[]{:S(2)}, u32[]{:S(2)}) collective-permute-start(f32[520,128]{1,0:T(8,128)S(1)} %pad_maximum_fusion.7), channel_id=1, source_target_pairs={{0,2},{1,3},{2,0},{3,1},{4,6},{5,7},{6,4},{7,5},{8,10},{9,11},{10,... | collective-permute-start | bytes 798728 | tf_op jit(solution)/shard_map/ppermute | solution.py:501
  68.5 7.9 %collective-permute-start.14 = (f32[776,128]{1,0:T(8,128)S(1)}, f32[776,128]{1,0:T(8,128)S(1)}, u32[]{:S(2)}, u32[]{:S(2)}) collective-permute-start(f32[776,128]{1,0:T(8,128)S(1)} %get-tuple-element.136), channel_id=1, source_target_pairs={{0,4},{1,9},{2,6},{3,11},{4,0},{5,13},{6,2},{7,15},{8,12},{9,1},{1... | collective-permute-start | bytes 1191944 | tf_op jit(solution)/shard_map/ppermute | solution.py:498
  74.0 2.6 %collective-permute-start.17 = (f32[512,128]{1,0:T(8,128)S(1)}, f32[512,128]{1,0:T(8,128)S(1)}, u32[]{:S(2)}, u32[]{:S(2)}) collective-permute-start(f32[512,128]{1,0:T(8,128)S(1)} %slice_add_fusion.10.refs_2_), channel_id=1, source_target_pairs={{0,1},{1,0},{2,3},{3,2},{4,5},{5,4},{6,7},{7,6},{8,9},{9,8},{10,11... | collective-permute-start | bytes 786440 | tf_op jit(solution)/shard_map/ppermute | solution.py:501
  76.5 5.8 %collective-permute-start.16 = (f32[392,128]{1,0:T(8,128)S(1)}, f32[392,128]{1,0:T(8,128)S(1)}, u32[]{:S(2)}, u32[]{:S(2)}) collective-permute-start(f32[392,128]{1,0:T(8,128)S(1)} %pad_maximum_fusion.14), channel_id=1, source_target_pairs={{0,8},{1,5},{2,10},{3,7},{4,12},{5,1},{6,14},{7,3},{8,0},{9,13},{1... | collective-permute-start | bytes 602120 | tf_op jit(solution)/shard_map/ppermute | solution.py:498
  78.2 13.0 %collective-permute-start.19 = (f32[776,128]{1,0:T(8,128)S(1)}, f32[776,128]{1,0:T(8,128)S(1)}, u32[]{:S(2)}, u32[]{:S(2)}) collective-permute-start(f32[776,128]{1,0:T(8,128)S(1)} %get-tuple-element.140), channel_id=1, source_target_pairs={{0,8},{1,5},{2,10},{3,7},{4,12},{5,1},{6,14},{7,3},{8,0},{9,13},{1... | collective-permute-start | bytes 1191944 | tf_op jit(solution)/shard_map/ppermute | solution.py:498
  82.3 10.6 %collective-permute-start.18 = (f32[392,128]{1,0:T(8,128)S(1)}, f32[392,128]{1,0:T(8,128)S(1)}, u32[]{:S(2)}, u32[]{:S(2)}) collective-permute-start(f32[392,128]{1,0:T(8,128)S(1)} %pad_maximum_fusion.15), channel_id=1, source_target_pairs={{0,16},{1,17},{2,18},{3,19},{4,20},{5,21},{6,22},{7,23},{8,24},{9,... | collective-permute-start | bytes 602120 | tf_op jit(solution)/shard_map/ppermute | solution.py:498
  91.2 5.8 %collective-permute-start.21 = (f32[392,128]{1,0:T(8,128)S(1)}, f32[392,128]{1,0:T(8,128)S(1)}, u32[]{:S(2)}, u32[]{:S(2)}) collective-permute-start(f32[392,128]{1,0:T(8,128)S(1)} %pad_maximum_fusion.16), channel_id=1, source_target_pairs={{0,4},{1,9},{2,6},{3,11},{4,0},{5,13},{6,2},{7,15},{8,12},{9,1},{1... | collective-permute-start | bytes 602120 | tf_op jit(solution)/shard_map/ppermute | solution.py:498
  92.9 12.1 %collective-permute-start.20 = (f32[384,128]{1,0:T(8,128)S(1)}, f32[384,128]{1,0:T(8,128)S(1)}, u32[]{:S(2)}, u32[]{:S(2)}) collective-permute-start(f32[384,128]{1,0:T(8,128)S(1)} %slice_add_fusion.23.mine_ref), channel_id=1, source_target_pairs={{0,8},{1,5},{2,10},{3,7},{4,12},{5,1},{6,14},{7,3},{8,0},{9,13},{1... | collective-permute-start | bytes 589832 | tf_op jit(solution)/shard_map/ppermute | solution.py:498
  97.1 8.1 %collective-permute-start.23 = (f32[392,128]{1,0:T(8,128)S(1)}, f32[392,128]{1,0:T(8,128)S(1)}, u32[]{:S(2)}, u32[]{:S(2)}) collective-permute-start(f32[392,128]{1,0:T(8,128)S(1)} %pad_maximum_fusion.17), channel_id=1, source_target_pairs={{0,16},{1,17},{2,18},{3,19},{4,20},{5,21},{6,22},{7,23},{8,24},{9,... | collective-permute-start | bytes 602120 | tf_op jit(solution)/shard_map/ppermute | solution.py:498
  105.1 7.8 %collective-permute-start.22 = (f32[768,128]{1,0:T(8,128)S(1)}, f32[768,128]{1,0:T(8,128)S(1)}, u32[]{:S(2)}, u32[]{:S(2)}) collective-permute-start(f32[768,128]{1,0:T(8,128)S(1)} %pad_maximum_fusion.2), channel_id=1, source_target_pairs={{0,4},{1,9},{2,6},{3,11},{4,0},{5,13},{6,2},{7,15},{8,12},{9,1},{1... | collective-permute-start | bytes 1179656 | tf_op jit(solution)/shard_map/ppermute | solution.py:498
  105.2 9.8 %collective-permute-start.25 = (f32[384,128]{1,0:T(8,128)S(1)}, f32[384,128]{1,0:T(8,128)S(1)}, u32[]{:S(2)}, u32[]{:S(2)}) collective-permute-start(f32[384,128]{1,0:T(8,128)S(1)} %slice_add_fusion.22.mine_ref), channel_id=1, source_target_pairs={{0,4},{1,9},{2,6},{3,11},{4,0},{5,13},{6,2},{7,15},{8,12},{9,1},{1... | collective-permute-start | bytes 589832 | tf_op jit(solution)/shard_map/ppermute | solution.py:498
  114.0 2.1 %collective-permute-start.24 = (f32[520,128]{1,0:T(8,128)S(1)}, f32[520,128]{1,0:T(8,128)S(1)}, u32[]{:S(2)}, u32[]{:S(2)}) collective-permute-start(f32[520,128]{1,0:T(8,128)S(1)} %get-tuple-element.154), channel_id=1, source_target_pairs={{0,1},{1,0},{2,3},{3,2},{4,5},{5,4},{6,7},{7,6},{8,9},{9,8},{10,11... | collective-permute-start | bytes 798728 | tf_op jit(solution)/shard_map/ppermute | solution.py:501
  115.1 7.8 %collective-permute-start.27 = (f32[768,128]{1,0:T(8,128)S(1)}, f32[768,128]{1,0:T(8,128)S(1)}, u32[]{:S(2)}, u32[]{:S(2)}) collective-permute-start(f32[768,128]{1,0:T(8,128)S(1)} %pad_maximum_fusion.3), channel_id=1, source_target_pairs={{0,8},{1,5},{2,10},{3,7},{4,12},{5,1},{6,14},{7,3},{8,0},{9,13},{1... | collective-permute-start | bytes 1179656 | tf_op jit(solution)/shard_map/ppermute | solution.py:498
  116.2 8.0 %collective-permute-start.26 = (f32[520,128]{1,0:T(8,128)S(1)}, f32[520,128]{1,0:T(8,128)S(1)}, u32[]{:S(2)}, u32[]{:S(2)}) collective-permute-start(f32[520,128]{1,0:T(8,128)S(1)} %pad_maximum_fusion.8), channel_id=1, source_target_pairs={{0,2},{1,3},{2,0},{3,1},{4,6},{5,7},{6,4},{7,5},{8,10},{9,11},{10,... | collective-permute-start | bytes 798728 | tf_op jit(solution)/shard_map/ppermute | solution.py:501
  124.0 1.7 collective-permute-start.29
  124.2 1.7 collective-permute-start.28
  125.8 8.5 %collective-permute-start.31 = (f32[520,128]{1,0:T(8,128)S(1)}, f32[520,128]{1,0:T(8,128)S(1)}, u32[]{:S(2)}, u32[]{:S(2)}) collective-permute-start(f32[520,128]{1,0:T(8,128)S(1)} %pad_maximum_fusion.9), channel_id=1, source_target_pairs={{0,2},{1,3},{2,0},{3,1},{4,6},{5,7},{6,4},{7,5},{8,10},{9,11},{10,... | collective-permute-start | bytes 798728 | tf_op jit(solution)/shard_map/ppermute | solution.py:501
  127.5 7.8 %collective-permute-start.30 = (f32[776,128]{1,0:T(8,128)S(1)}, f32[776,128]{1,0:T(8,128)S(1)}, u32[]{:S(2)}, u32[]{:S(2)}) collective-permute-start(f32[776,128]{1,0:T(8,128)S(1)} %get-tuple-element.172), channel_id=1, source_target_pairs={{0,4},{1,9},{2,6},{3,11},{4,0},{5,13},{6,2},{7,15},{8,12},{9,1},{1... | collective-permute-start | bytes 1191944 | tf_op jit(solution)/shard_map/ppermute | solution.py:498
  134.3 1.6 collective-permute-start.33
  135.4 5.8 %collective-permute-start.32 = (f32[392,128]{1,0:T(8,128)S(1)}, f32[392,128]{1,0:T(8,128)S(1)}, u32[]{:S(2)}, u32[]{:S(2)}) collective-permute-start(f32[392,128]{1,0:T(8,128)S(1)} %pad_maximum_fusion.18), channel_id=1, source_target_pairs={{0,8},{1,5},{2,10},{3,7},{4,12},{5,1},{6,14},{7,3},{8,0},{9,13},{1... | collective-permute-start | bytes 602120 | tf_op jit(solution)/shard_map/ppermute | solution.py:498
  137.4 10.3 %collective-permute-start.35 = (f32[776,128]{1,0:T(8,128)S(1)}, f32[776,128]{1,0:T(8,128)S(1)}, u32[]{:S(2)}, u32[]{:S(2)}) collective-permute-start(f32[776,128]{1,0:T(8,128)S(1)} %get-tuple-element.178), channel_id=1, source_target_pairs={{0,8},{1,5},{2,10},{3,7},{4,12},{5,1},{6,14},{7,3},{8,0},{9,13},{1... | collective-permute-start | bytes 1191944 | tf_op jit(solution)/shard_map/ppermute | solution.py:498
  141.3 9.6 %collective-permute-start.34 = (f32[392,128]{1,0:T(8,128)S(1)}, f32[392,128]{1,0:T(8,128)S(1)}, u32[]{:S(2)}, u32[]{:S(2)}) collective-permute-start(f32[392,128]{1,0:T(8,128)S(1)} %pad_maximum_fusion.19), channel_id=1, source_target_pairs={{0,16},{1,17},{2,18},{3,19},{4,20},{5,21},{6,22},{7,23},{8,24},{9,... | collective-permute-start | bytes 602120 | tf_op jit(solution)/shard_map/ppermute | solution.py:498
  147.8 7.8 %collective-permute-start.36 = (f32[392,128]{1,0:T(8,128)S(1)}, f32[392,128]{1,0:T(8,128)S(1)}, u32[]{:S(2)}, u32[]{:S(2)}) collective-permute-start(f32[392,128]{1,0:T(8,128)S(1)} %pad_maximum_fusion.20), channel_id=1, source_target_pairs={{0,4},{1,9},{2,6},{3,11},{4,0},{5,13},{6,2},{7,15},{8,12},{9,1},{1... | collective-permute-start | bytes 602120 | tf_op jit(solution)/shard_map/ppermute | solution.py:498
  150.9 6.8 %collective-permute-start.38 = (f32[384,128]{1,0:T(8,128)S(1)}, f32[384,128]{1,0:T(8,128)S(1)}, u32[]{:S(2)}, u32[]{:S(2)}) collective-permute-start(f32[384,128]{1,0:T(8,128)S(1)} %slice_add_fusion.21.mine_ref), channel_id=1, source_target_pairs={{0,8},{1,5},{2,10},{3,7},{4,12},{5,1},{6,14},{7,3},{8,0},{9,13},{1... | collective-permute-start | bytes 589832 | tf_op jit(solution)/shard_map/ppermute | solution.py:498
  155.6 8.9 %collective-permute-start.37 = (f32[392,128]{1,0:T(8,128)S(1)}, f32[392,128]{1,0:T(8,128)S(1)}, u32[]{:S(2)}, u32[]{:S(2)}) collective-permute-start(f32[392,128]{1,0:T(8,128)S(1)} %pad_maximum_fusion.21), channel_id=1, source_target_pairs={{0,16},{1,17},{2,18},{3,19},{4,20},{5,21},{6,22},{7,23},{8,24},{9,... | collective-permute-start | bytes 602120 | tf_op jit(solution)/shard_map/ppermute | solution.py:498
  164.5 7.1 %collective-permute-start.40 = (f32[384,128]{1,0:T(8,128)S(1)}, f32[384,128]{1,0:T(8,128)S(1)}, u32[]{:S(2)}, u32[]{:S(2)}) collective-permute-start(f32[384,128]{1,0:T(8,128)S(1)} %slice_add_fusion.20.refs_6_), channel_id=1, source_target_pairs={{0,4},{1,9},{2,6},{3,11},{4,0},{5,13},{6,2},{7,15},{8,12},{9,1},{1... | collective-permute-start | bytes 589832 | tf_op jit(solution)/shard_map/ppermute | solution.py:498
  165.5 13.2 %collective-permute-start.39 = (f32[768,128]{1,0:T(8,128)S(1)}, f32[768,128]{1,0:T(8,128)S(1)}, u32[]{:S(2)}, u32[]{:S(2)}) collective-permute-start(f32[768,128]{1,0:T(8,128)S(1)} %pad_maximum_fusion.4), channel_id=1, source_target_pairs={{0,4},{1,9},{2,6},{3,11},{4,0},{5,13},{6,2},{7,15},{8,12},{9,1},{1... | collective-permute-start | bytes 1179656 | tf_op jit(solution)/shard_map/ppermute | solution.py:498
  171.7 7.8 %collective-permute-start.41 = (f32[768,128]{1,0:T(8,128)S(1)}, f32[768,128]{1,0:T(8,128)S(1)}, u32[]{:S(2)}, u32[]{:S(2)}) collective-permute-start(f32[768,128]{1,0:T(8,128)S(1)} %pad_maximum_fusion.5), channel_id=1, source_target_pairs={{0,8},{1,5},{2,10},{3,7},{4,12},{5,1},{6,14},{7,3},{8,0},{9,13},{1... | collective-permute-start | bytes 1179656 | tf_op jit(solution)/shard_map/ppermute | solution.py:498

commit v24 on v23

--- a/solution.py
+++ b/solution.py
@@ -13,6 +13,7 @@
 PAIR = 2 * TILE
 UNITS = 4
 NORM_ROWS = 8
+FETCHES = 4
 UNIT_ORDERS = ((0, 1, 2, 3), (0, 2, 1, 3))
 BEHIND = 0
 
@@ -41,7 +42,7 @@
     flip = flip_ref[0]
     row_blocks = tiles_in.shape[0]
     small = [
-        pltpu.make_async_copy(source, target, arrived.at[2 * row_blocks + i])
+        pltpu.make_async_copy(source, target, arrived.at[FETCHES * row_blocks + i])
         for i, (source, target) in enumerate(
             [(pattern_in, pattern_ref), (counts_in, counts_ref), (delays_in, delays_ref)]
         )
@@ -49,14 +50,14 @@
     for copy in small:
         copy.start()
 
-    half = tiles_in.shape[1] // 2
-
-    def fetch(position, upper):
-        slots = pl.ds(upper * half, half)
+    size = tiles_in.shape[1] // FETCHES
+
+    def fetch(position, part):
+        slots = pl.ds(part * size, size)
         return pltpu.make_async_copy(
             tiles_in.at[position ^ flip, slots],
             tiles_ref.at[position, slots],
-            arrived.at[upper * row_blocks + position],
+            arrived.at[part * row_blocks + position],
         )
 
     for position in range(row_blocks):
@@ -69,10 +70,11 @@
     for copy in small[:2]:
         copy.wait()
     for position in range(row_blocks):
-
-        @pl.when(counts_ref[position ^ flip] > half)
-        def _():
-            fetch(position, 1).start()
+        for part in range(1, FETCHES):
+
+            @pl.when(counts_ref[position ^ flip] > part * size)
+            def _():
+                fetch(position, part).start()
 
     small[2].wait()
     low = low_lanes((TILE, TILE))
@@ -94,15 +96,13 @@
             lanes = pl.ds(pl.multiple_of(column * TILE, TILE), TILE)
             dense_ref[rows, lanes] = tiles_ref[position, tile]
 
-        fetch(position, 0).wait()
-        for tile in range(half):
-            place(tile)
-
-        @pl.when(count > half)
-        def _():
-            fetch(position, 1).wait()
-            for tile in range(half, 2 * half):
-                place(tile)
+        for part in range(FETCHES):
+
+            @pl.when(count > part * size)
+            def _():
+                fetch(position, part).wait()
+                for tile in range(part * size, (part + 1) * size):
+                    place(tile)
 
 
 def fill_dense(kernel, pattern, counts, places, flip, delays):
@@ -119,7 +119,7 @@
             pltpu.SMEM((row_blocks,), jnp.int32),
             pltpu.VMEM(delays.shape, delays.dtype),
             pltpu.VMEM(kernel.shape, kernel.dtype),
-            pltpu.SemaphoreType.DMA((2 * row_blocks + 3,)),
+            pltpu.SemaphoreType.DMA((FETCHES * row_blocks + 3,)),
         ],
         compiler_params=pltpu.CompilerParams(vmem_limit_bytes=16 * 1024 * 1024),
         cost_estimate=pl.CostEstimate(

time: 182 us -> 182 us (level)
  waiting for transfers between devices: 101 us -> 87.2 us
  starting transfers between devices: 37.4 us -> 50.7 us
    ppermute x30, waiting for transfers between devices: 91.9 us -> 78.5 us  [swap_rows(): return lax.ppermute(value, ('rows', 'cols'), pairs)]
    ppermute x30, starting transfers between devices: 32.1 us -> 44.6 us  [swap_rows(): return lax.ppermute(value, ('rows', 'cols'), pairs)]
  transfers between devices with their start and end apart: 42 -> 42, of which waited for: 33 -> 31; matrix products, arithmetic and copies ran while one was open for 1% -> 1% of each run, Pallas kernels for 18% -> 18%
where the time goes in v24:
time: 182 us
  waiting for transfers between devices  87.2 us (48%)
  starting transfers between devices  50.7 us (28%)
  Pallas kernels  40.2 us (22%)
    ppermute x30, waiting for transfers between devices, swap_rows(): return lax.ppermute(value, ('rows', 'cols'), pairs)  78.5 us
    ppermute x30, starting transfers between devices, swap_rows(): return lax.ppermute(value, ('rows', 'cols'), pairs)  44.6 us
    pallas_call x24, Pallas kernels, product_call(): pl.pallas_call(body, in_specs=[WHOLE] * (1 + len(operands)), out_specs=[W...  32.2 us
    ppermute x12, waiting for transfers between devices, swap_cols(): lax.ppermute(value, 'cols', [(i, i ^ 1 << level) for i in range(col_count)])  8.75 us
    ppermute x12, starting transfers between devices, swap_cols(): lax.ppermute(value, 'cols', [(i, i ^ 1 << level) for i in range(col_count)])  6.03 us
    pallas_call x1, Pallas kernels, fill_dense(): pl.pallas_call(fill_kernel, in_specs=[SCALARS] * 2 + [pl.BlockSpec(memory...  4.76 us
  transfers between devices with their start and end apart: 42, of which 31 were waited for; matrix products, arithmetic and copies ran while one was open for 1% of the time, Pallas kernels for 18%

profile of v24, /device:TPU:0, one launch (start us, length us, event | category | flops | bytes accessed | tf_op | source)
XLA Modules:
  0.0 181.7 jit_solution(7761713075881664324)
XLA Ops:
  0.7 4.8 %shard_map.67 = (bf16[2048,3200]{1,0:T(8,128)(2,1)S(1)}, f32[1024,128]{1,0:T(8,128)S(1)}, f32[1024,128]{1,0:T(8,128)S(1)}) custom-call(s32[24]{0:T(128)S(1)} %fusion.place_ref, s32[1]{0:T(128)} %bitcast.1.flip_ref, s32[16,16]{1,0:T(8,128)} %pattern_in.1, s32[16]{0:T(128)} %bitcast.5, f32[2048,128]{1,0:T(8,128)} %delays_in.1, bf16[16,16,128,128]{3,2,1,0:T(8,128)(2,1)} %tiles_in.1), custom_call_target="tpu_custom_call" | custom-call | bytes 8388608 | tf_op jit(solution)/shard_map/pallas_call | solution.py:112
  6.8 3.0 %collective-permute-start = (f32[776,128]{1,0:T(8,128)S(1)}, f32[776,128]{1,0:T(8,128)S(1)}, u32[]{:S(2)}, u32[]{:S(2)}) collective-permute-start(f32[776,128]{1,0:T(8,128)S(1)} %get-tuple-element.102), channel_id=1, source_target_pairs={{0,4},{1,9},{2,6},{3,11},{4,0},{5,13},{6,2},{7,15},{8,12},{9,1},{1... | collective-permute-start | bytes 1191944 | tf_op jit(solution)/shard_map/ppermute | solution.py:498
  12.5 3.1 %collective-permute-done = f32[776,128]{1,0:T(8,128)S(1)} collective-permute-done((f32[776,128]{1,0:T(8,128)S(1)}, f32[776,128]{1,0:T(8,128)S(1)}, u32[]{:S(2)}, u32[]{:S(2)}) %collective-permute-start) | collective-permute-done | bytes 397344 | tf_op jit(solution)/shard_map/ppermute | solution.py:498
  15.7 1.8 collective-permute-start.1
  19.2 2.3 %collective-permute-done.1 = f32[392,128]{1,0:T(8,128)S(1)} collective-permute-done((f32[392,128]{1,0:T(8,128)S(1)}, f32[392,128]{1,0:T(8,128)S(1)}, u32[]{:S(2)}, u32[]{:S(2)}) %collective-permute-start.1) | collective-permute-done | bytes 200736 | tf_op jit(solution)/shard_map/ppermute | solution.py:498
  21.6 2.4 %collective-permute-start.2 = (f32[392,128]{1,0:T(8,128)S(1)}, f32[392,128]{1,0:T(8,128)S(1)}, u32[]{:S(2)}, u32[]{:S(2)}) collective-permute-start(f32[392,128]{1,0:T(8,128)S(1)} %pad_maximum_fusion.11), channel_id=1, source_target_pairs={{0,16},{1,17},{2,18},{3,19},{4,20},{5,21},{6,22},{7,23},{8,24},{9,... | collective-permute-start | bytes 602120 | tf_op jit(solution)/shard_map/ppermute | solution.py:498
  24.0 8.4 %collective-permute-done.3 = f32[776,128]{1,0:T(8,128)S(1)} collective-permute-done((f32[776,128]{1,0:T(8,128)S(1)}, f32[776,128]{1,0:T(8,128)S(1)}, u32[]{:S(2)}, u32[]{:S(2)}) %collective-permute-start.3) | collective-permute-done | bytes 397344 | tf_op jit(solution)/shard_map/ppermute | solution.py:498
  32.5 1.8 collective-permute-start.5
  34.3 1.4 collective-permute-start.4
  35.7 2.5 %collective-permute-done.5 = f32[392,128]{1,0:T(8,128)S(1)} collective-permute-done((f32[392,128]{1,0:T(8,128)S(1)}, f32[392,128]{1,0:T(8,128)S(1)}, u32[]{:S(2)}, u32[]{:S(2)}) %collective-permute-start.5) | collective-permute-done | bytes 200736 | tf_op jit(solution)/shard_map/ppermute | solution.py:498
  39.1 5.1 %collective-permute-done.4.inner_ref = f32[384,128]{1,0:T(8,128)S(1)} collective-permute-done((f32[384,128]{1,0:T(8,128)S(1)}, f32[384,128]{1,0:T(8,128)S(1)}, u32[]{:S(2)}, u32[]{:S(2)}) %collective-permute-start.4) | collective-permute-done | bytes 196640 | tf_op jit(solution)/shard_map/ppermute | solution.py:498
  44.7 2.1 %collective-permute-done.7 = f32[392,128]{1,0:T(8,128)S(1)} collective-permute-done((f32[392,128]{1,0:T(8,128)S(1)}, f32[392,128]{1,0:T(8,128)S(1)}, u32[]{:S(2)}, u32[]{:S(2)}) %collective-permute-start.7) | collective-permute-done | bytes 200736 | tf_op jit(solution)/shard_map/ppermute | solution.py:498
  46.8 1.8 collective-permute-start.8
  48.6 1.9 %shard_map.72 = (f32[1024,128]{1,0:T(8,128)S(1)}, f32[8,128]{1,0:T(8,128)S(1)}, f32[768,128]{1,0:T(8,128)S(1)}) custom-call(bf16[2048,3200]{1,0:T(8,128)(2,1)S(1)} %get-tuple-element.99.refs_0_.dense_ref, f32[384,128]{1,0:T(8,128)S(1)} %collective-permute-done.4.inner_ref, f32[384,128]{1,0:T(8,128)S(1)} %slice_add_fusion.25.mine_ref, ...), custom_call_target="tpu_custom_call" | custom-call | flops 1677721600 | bytes 6553600 | tf_op jit(solution)/shard_map/pallas_call | solution.py:268
  50.5 1.6 collective-permute-done.6.outer_ref
  55.3 1.7 collective-permute-start.10
  57.0 1.9 %shard_map.75 = (f32[1024,128]{1,0:T(8,128)S(1)}, f32[8,128]{1,0:T(8,128)S(1)}, f32[768,128]{1,0:T(8,128)S(1)}) custom-call(bf16[2048,3200]{1,0:T(8,128)(2,1)S(1)} %get-tuple-element.99.refs_0_.dense_ref, f32[384,128]{1,0:T(8,128)S(1)} %collective-permute-done.8.inner_ref, f32[384,128]{1,0:T(8,128)S(1)} %slice_add_fusion.24.mine_ref, ...), custom_call_target="tpu_custom_call" | custom-call | flops 1677721600 | bytes 6553600 | tf_op jit(solution)/shard_map/pallas_call | solution.py:268
  58.9 3.1 %collective-permute-done.11.outer_ref = f32[768,128]{1,0:T(8,128)S(1)} collective-permute-done((f32[768,128]{1,0:T(8,128)S(1)}, f32[768,128]{1,0:T(8,128)S(1)}, u32[]{:S(2)}, u32[]{:S(2)}) %collective-permute-start.11) | collective-permute-done | bytes 393248 | tf_op jit(solution)/shard_map/ppermute | solution.py:498
  64.9 1.7 collective-permute-start.15
  66.6 1.4 shard_map.78
  70.7 2.8 %collective-permute-done.15 = f32[520,128]{1,0:T(8,128)S(1)} collective-permute-done((f32[520,128]{1,0:T(8,128)S(1)}, f32[520,128]{1,0:T(8,128)S(1)}, u32[]{:S(2)}, u32[]{:S(2)}) %collective-permute-start.15) | collective-permute-done | bytes 266272 | tf_op jit(solution)/shard_map/ppermute | solution.py:501
  73.6 2.3 %collective-permute-done.14 = f32[776,128]{1,0:T(8,128)S(1)} collective-permute-done((f32[776,128]{1,0:T(8,128)S(1)}, f32[776,128]{1,0:T(8,128)S(1)}, u32[]{:S(2)}, u32[]{:S(2)}) %collective-permute-start.14) | collective-permute-done | bytes 397344 | tf_op jit(solution)/shard_map/ppermute | solution.py:498
  76.7 1.4 shard_map.80
  78.1 1.7 collective-permute-start.19
  82.1 2.8 %collective-permute-start.18 = (f32[392,128]{1,0:T(8,128)S(1)}, f32[392,128]{1,0:T(8,128)S(1)}, u32[]{:S(2)}, u32[]{:S(2)}) collective-permute-start(f32[392,128]{1,0:T(8,128)S(1)} %pad_maximum_fusion.15), channel_id=1, source_target_pairs={{0,16},{1,17},{2,18},{3,19},{4,20},{5,21},{6,22},{7,23},{8,24},{9,... | collective-permute-start | bytes 602120 | tf_op jit(solution)/shard_map/ppermute | solution.py:498
  84.9 6.2 %collective-permute-done.19 = f32[776,128]{1,0:T(8,128)S(1)} collective-permute-done((f32[776,128]{1,0:T(8,128)S(1)}, f32[776,128]{1,0:T(8,128)S(1)}, u32[]{:S(2)}, u32[]{:S(2)}) %collective-permute-start.19) | collective-permute-done | bytes 397344 | tf_op jit(solution)/shard_map/ppermute | solution.py:498
  91.1 1.7 collective-permute-start.21
  92.8 3.8 %collective-permute-start.20 = (f32[384,128]{1,0:T(8,128)S(1)}, f32[384,128]{1,0:T(8,128)S(1)}, u32[]{:S(2)}, u32[]{:S(2)}) collective-permute-start(f32[384,128]{1,0:T(8,128)S(1)} %slice_add_fusion.23.mine_ref), channel_id=1, source_target_pairs={{0,8},{1,5},{2,10},{3,7},{4,12},{5,1},{6,14},{7,3},{8,0},{9,13},{1... | collective-permute-start | bytes 589832 | tf_op jit(solution)/shard_map/ppermute | solution.py:498
  97.0 3.0 %collective-permute-start.23 = (f32[392,128]{1,0:T(8,128)S(1)}, f32[392,128]{1,0:T(8,128)S(1)}, u32[]{:S(2)}, u32[]{:S(2)}) collective-permute-start(f32[392,128]{1,0:T(8,128)S(1)} %pad_maximum_fusion.17), channel_id=1, source_target_pairs={{0,16},{1,17},{2,18},{3,19},{4,20},{5,21},{6,22},{7,23},{8,24},{9,... | collective-permute-start | bytes 602120 | tf_op jit(solution)/shard_map/ppermute | solution.py:498
  100.0 3.1 %collective-permute-done.20.inner_ref = f32[384,128]{1,0:T(8,128)S(1)} collective-permute-done((f32[384,128]{1,0:T(8,128)S(1)}, f32[384,128]{1,0:T(8,128)S(1)}, u32[]{:S(2)}, u32[]{:S(2)}) %collective-permute-start.20) | collective-permute-done | bytes 196640 | tf_op jit(solution)/shard_map/ppermute | solution.py:498
  103.2 2.9 %collective-permute-start.22 = (f32[768,128]{1,0:T(8,128)S(1)}, f32[768,128]{1,0:T(8,128)S(1)}, u32[]{:S(2)}, u32[]{:S(2)}) collective-permute-start(f32[768,128]{1,0:T(8,128)S(1)} %pad_maximum_fusion.2), channel_id=1, source_target_pairs={{0,4},{1,9},{2,6},{3,11},{4,0},{5,13},{6,2},{7,15},{8,12},{9,1},{1... | collective-permute-start | bytes 1179656 | tf_op jit(solution)/shard_map/ppermute | solution.py:498
  107.3 1.9 %shard_map.82 = (f32[1024,128]{1,0:T(8,128)S(1)}, f32[8,128]{1,0:T(8,128)S(1)}, f32[768,128]{1,0:T(8,128)S(1)}) custom-call(bf16[2048,3200]{1,0:T(8,128)(2,1)S(1)} %get-tuple-element.99.refs_0_.dense_ref, f32[384,128]{1,0:T(8,128)S(1)} %collective-permute-done.20.inner_ref, f32[384,128]{1,0:T(8,128)S(1)} %slice_add_fusion.23.mine_ref, ...), custom_call_target="tpu_custom_call" | custom-call | flops 1677721600 | bytes 6553600 | tf_op jit(solution)/shard_map/pallas_call | solution.py:268
  109.2 2.6 %collective-permute-done.22.outer_ref = f32[768,128]{1,0:T(8,128)S(1)} collective-permute-done((f32[768,128]{1,0:T(8,128)S(1)}, f32[768,128]{1,0:T(8,128)S(1)}, u32[]{:S(2)}, u32[]{:S(2)}) %collective-permute-start.22) | collective-permute-done | bytes 393248 | tf_op jit(solution)/shard_map/ppermute | solution.py:498
  116.0 1.9 %shard_map.85 = (f32[1024,128]{1,0:T(8,128)S(1)}, f32[8,128]{1,0:T(8,128)S(1)}, f32[768,128]{1,0:T(8,128)S(1)}) custom-call(bf16[2048,3200]{1,0:T(8,128)(2,1)S(1)} %get-tuple-element.99.refs_0_.dense_ref, f32[384,128]{1,0:T(8,128)S(1)} %collective-permute-done.25.inner_ref, f32[384,128]{1,0:T(8,128)S(1)} %slice_add_fusion.22.mine_ref, ...), custom_call_target="tpu_custom_call" | custom-call | flops 1677721600 | bytes 6553600 | tf_op jit(solution)/shard_map/pallas_call | solution.py:268
  117.9 3.9 %collective-permute-done.27.outer_ref = f32[768,128]{1,0:T(8,128)S(1)} collective-permute-done((f32[768,128]{1,0:T(8,128)S(1)}, f32[768,128]{1,0:T(8,128)S(1)}, u32[]{:S(2)}, u32[]{:S(2)}) %collective-permute-start.27) | collective-permute-done | bytes 393248 | tf_op jit(solution)/shard_map/ppermute | solution.py:498
  126.4 1.5 shard_map.88
  129.7 4.5 %collective-permute-done.31 = f32[520,128]{1,0:T(8,128)S(1)} collective-permute-done((f32[520,128]{1,0:T(8,128)S(1)}, f32[520,128]{1,0:T(8,128)S(1)}, u32[]{:S(2)}, u32[]{:S(2)}) %collective-permute-start.31) | collective-permute-done | bytes 266272 | tf_op jit(solution)/shard_map/ppermute | solution.py:501
  135.9 1.5 shard_map.90
  137.4 2.0 %collective-permute-start.35 = (f32[776,128]{1,0:T(8,128)S(1)}, f32[776,128]{1,0:T(8,128)S(1)}, u32[]{:S(2)}, u32[]{:S(2)}) collective-permute-start(f32[776,128]{1,0:T(8,128)S(1)} %get-tuple-element.178), channel_id=1, source_target_pairs={{0,8},{1,5},{2,10},{3,7},{4,12},{5,1},{6,14},{7,3},{8,0},{9,13},{1... | collective-permute-start | bytes 1191944 | tf_op jit(solution)/shard_map/ppermute | solution.py:498
  143.0 7.4 %collective-permute-done.35 = f32[776,128]{1,0:T(8,128)S(1)} collective-permute-done((f32[776,128]{1,0:T(8,128)S(1)}, f32[776,128]{1,0:T(8,128)S(1)}, u32[]{:S(2)}, u32[]{:S(2)}) %collective-permute-start.35) | collective-permute-done | bytes 397344 | tf_op jit(solution)/shard_map/ppermute | solution.py:498
  151.2 3.5 %collective-permute-start.38 = (f32[384,128]{1,0:T(8,128)S(1)}, f32[384,128]{1,0:T(8,128)S(1)}, u32[]{:S(2)}, u32[]{:S(2)}) collective-permute-start(f32[384,128]{1,0:T(8,128)S(1)} %slice_add_fusion.21.mine_ref), channel_id=1, source_target_pairs={{0,8},{1,5},{2,10},{3,7},{4,12},{5,1},{6,14},{7,3},{8,0},{9,13},{1... | collective-permute-start | bytes 589832 | tf_op jit(solution)/shard_map/ppermute | solution.py:498
  154.8 1.5 collective-permute-done.36
  156.4 1.6 collective-permute-start.37
  158.0 2.3 %collective-permute-done.38.inner_ref = f32[384,128]{1,0:T(8,128)S(1)} collective-permute-done((f32[384,128]{1,0:T(8,128)S(1)}, f32[384,128]{1,0:T(8,128)S(1)}, u32[]{:S(2)}, u32[]{:S(2)}) %collective-permute-start.38) | collective-permute-done | bytes 196640 | tf_op jit(solution)/shard_map/ppermute | solution.py:498
  160.3 4.8 %collective-permute-done.37 = f32[392,128]{1,0:T(8,128)S(1)} collective-permute-done((f32[392,128]{1,0:T(8,128)S(1)}, f32[392,128]{1,0:T(8,128)S(1)}, u32[]{:S(2)}, u32[]{:S(2)}) %collective-permute-start.37) | collective-permute-done | bytes 200736 | tf_op jit(solution)/shard_map/ppermute | solution.py:498
  167.2 5.2 %collective-permute-done.40.refs_5_ = f32[384,128]{1,0:T(8,128)S(1)} collective-permute-done((f32[384,128]{1,0:T(8,128)S(1)}, f32[384,128]{1,0:T(8,128)S(1)}, u32[]{:S(2)}, u32[]{:S(2)}) %collective-permute-start.40) | collective-permute-done | bytes 196640 | tf_op jit(solution)/shard_map/ppermute | solution.py:498
  172.6 1.8 shard_map.92
  174.8 4.4 %collective-permute-done.39.outer_ref = f32[768,128]{1,0:T(8,128)S(1)} collective-permute-done((f32[768,128]{1,0:T(8,128)S(1)}, f32[768,128]{1,0:T(8,128)S(1)}, u32[]{:S(2)}, u32[]{:S(2)}) %collective-permute-start.39) | collective-permute-done | bytes 393248 | tf_op jit(solution)/shard_map/ppermute | solution.py:498
  (146 shorter events, 42.4 us)
Async XLA Ops:
  6.8 8.8 %collective-permute-start = (f32[776,128]{1,0:T(8,128)S(1)}, f32[776,128]{1,0:T(8,128)S(1)}, u32[]{:S(2)}, u32[]{:S(2)}) collective-permute-start(f32[776,128]{1,0:T(8,128)S(1)} %get-tuple-element.102), channel_id=1, source_target_pairs={{0,4},{1,9},{2,6},{3,11},{4,0},{5,13},{6,2},{7,15},{8,12},{9,1},{1... | collective-permute-start | bytes 1191944 | tf_op jit(solution)/shard_map/ppermute | solution.py:498
  15.7 5.8 %collective-permute-start.1 = (f32[392,128]{1,0:T(8,128)S(1)}, f32[392,128]{1,0:T(8,128)S(1)}, u32[]{:S(2)}, u32[]{:S(2)}) collective-permute-start(f32[392,128]{1,0:T(8,128)S(1)} %pad_maximum_fusion.10), channel_id=1, source_target_pairs={{0,8},{1,5},{2,10},{3,7},{4,12},{5,1},{6,14},{7,3},{8,0},{9,13},{1... | collective-permute-start | bytes 602120 | tf_op jit(solution)/shard_map/ppermute | solution.py:498
  18.8 13.6 %collective-permute-start.3 = (f32[776,128]{1,0:T(8,128)S(1)}, f32[776,128]{1,0:T(8,128)S(1)}, u32[]{:S(2)}, u32[]{:S(2)}) collective-permute-start(f32[776,128]{1,0:T(8,128)S(1)} %get-tuple-element.106), channel_id=1, source_target_pairs={{0,8},{1,5},{2,10},{3,7},{4,12},{5,1},{6,14},{7,3},{8,0},{9,13},{1... | collective-permute-start | bytes 1191944 | tf_op jit(solution)/shard_map/ppermute | solution.py:498
  21.6 12.7 %collective-permute-start.2 = (f32[392,128]{1,0:T(8,128)S(1)}, f32[392,128]{1,0:T(8,128)S(1)}, u32[]{:S(2)}, u32[]{:S(2)}) collective-permute-start(f32[392,128]{1,0:T(8,128)S(1)} %pad_maximum_fusion.11), channel_id=1, source_target_pairs={{0,16},{1,17},{2,18},{3,19},{4,20},{5,21},{6,22},{7,23},{8,24},{9,... | collective-permute-start | bytes 602120 | tf_op jit(solution)/shard_map/ppermute | solution.py:498
  32.5 5.8 %collective-permute-start.5 = (f32[392,128]{1,0:T(8,128)S(1)}, f32[392,128]{1,0:T(8,128)S(1)}, u32[]{:S(2)}, u32[]{:S(2)}) collective-permute-start(f32[392,128]{1,0:T(8,128)S(1)} %pad_maximum_fusion.12), channel_id=1, source_target_pairs={{0,4},{1,9},{2,6},{3,11},{4,0},{5,13},{6,2},{7,15},{8,12},{9,1},{1... | collective-permute-start | bytes 602120 | tf_op jit(solution)/shard_map/ppermute | solution.py:498
  34.3 9.9 %collective-permute-start.4 = (f32[384,128]{1,0:T(8,128)S(1)}, f32[384,128]{1,0:T(8,128)S(1)}, u32[]{:S(2)}, u32[]{:S(2)}) collective-permute-start(f32[384,128]{1,0:T(8,128)S(1)} %slice_add_fusion.25.mine_ref), channel_id=1, source_target_pairs={{0,8},{1,5},{2,10},{3,7},{4,12},{5,1},{6,14},{7,3},{8,0},{9,13},{1... | collective-permute-start | bytes 589832 | tf_op jit(solution)/shard_map/ppermute | solution.py:498
  38.3 8.5 %collective-permute-start.7 = (f32[392,128]{1,0:T(8,128)S(1)}, f32[392,128]{1,0:T(8,128)S(1)}, u32[]{:S(2)}, u32[]{:S(2)}) collective-permute-start(f32[392,128]{1,0:T(8,128)S(1)} %pad_maximum_fusion.13), channel_id=1, source_target_pairs={{0,16},{1,17},{2,18},{3,19},{4,20},{5,21},{6,22},{7,23},{8,24},{9,... | collective-permute-start | bytes 602120 | tf_op jit(solution)/shard_map/ppermute | solution.py:498
  44.2 7.8 %collective-permute-start.6 = (f32[768,128]{1,0:T(8,128)S(1)}, f32[768,128]{1,0:T(8,128)S(1)}, u32[]{:S(2)}, u32[]{:S(2)}) collective-permute-start(f32[768,128]{1,0:T(8,128)S(1)} %pad_maximum_fusion), channel_id=1, source_target_pairs={{0,4},{1,9},{2,6},{3,11},{4,0},{5,13},{6,2},{7,15},{8,12},{9,1},{1... | collective-permute-start | bytes 1179656 | tf_op jit(solution)/shard_map/ppermute | solution.py:498
  46.8 7.3 %collective-permute-start.8 = (f32[384,128]{1,0:T(8,128)S(1)}, f32[384,128]{1,0:T(8,128)S(1)}, u32[]{:S(2)}, u32[]{:S(2)}) collective-permute-start(f32[384,128]{1,0:T(8,128)S(1)} %slice_add_fusion.24.mine_ref), channel_id=1, source_target_pairs={{0,4},{1,9},{2,6},{3,11},{4,0},{5,13},{6,2},{7,15},{8,12},{9,1},{1... | collective-permute-start | bytes 589832 | tf_op jit(solution)/shard_map/ppermute | solution.py:498
  53.2 2.1 %collective-permute-start.9 = (f32[520,128]{1,0:T(8,128)S(1)}, f32[520,128]{1,0:T(8,128)S(1)}, u32[]{:S(2)}, u32[]{:S(2)}) collective-permute-start(f32[520,128]{1,0:T(8,128)S(1)} %get-tuple-element.121), channel_id=1, source_target_pairs={{0,1},{1,0},{2,3},{3,2},{4,5},{5,4},{6,7},{7,6},{8,9},{9,8},{10,11... | collective-permute-start | bytes 798728 | tf_op jit(solution)/shard_map/ppermute | solution.py:501
  54.2 7.8 %collective-permute-start.11 = (f32[768,128]{1,0:T(8,128)S(1)}, f32[768,128]{1,0:T(8,128)S(1)}, u32[]{:S(2)}, u32[]{:S(2)}) collective-permute-start(f32[768,128]{1,0:T(8,128)S(1)} %pad_maximum_fusion.1), channel_id=1, source_target_pairs={{0,8},{1,5},{2,10},{3,7},{4,12},{5,1},{6,14},{7,3},{8,0},{9,13},{1... | collective-permute-start | bytes 1179656 | tf_op jit(solution)/shard_map/ppermute | solution.py:498
  55.3 8.1 %collective-permute-start.10 = (f32[520,128]{1,0:T(8,128)S(1)}, f32[520,128]{1,0:T(8,128)S(1)}, u32[]{:S(2)}, u32[]{:S(2)}) collective-permute-start(f32[520,128]{1,0:T(8,128)S(1)} %pad_maximum_fusion.6), channel_id=1, source_target_pairs={{0,2},{1,3},{2,0},{3,1},{4,6},{5,7},{6,4},{7,5},{8,10},{9,11},{10,... | collective-permute-start | bytes 798728 | tf_op jit(solution)/shard_map/ppermute | solution.py:501
  63.1 1.7 collective-permute-start.13
  63.5 3.1 %collective-permute-start.12 = (f32[512,128]{1,0:T(8,128)S(1)}, f32[512,128]{1,0:T(8,128)S(1)}, u32[]{:S(2)}, u32[]{:S(2)}) collective-permute-start(f32[512,128]{1,0:T(8,128)S(1)} %slice_add_fusion.12.refs_2_), channel_id=1, source_target_pairs={{0,1},{1,0},{2,3},{3,2},{4,5},{5,4},{6,7},{7,6},{8,9},{9,8},{10,11... | collective-permute-start | bytes 786440 | tf_op jit(solution)/shard_map/ppermute | solution.py:501
  64.9 8.6 %collective-permute-start.15 = (f32[520,128]{1,0:T(8,128)S(1)}, f32[520,128]{1,0:T(8,128)S(1)}, u32[]{:S(2)}, u32[]{:S(2)}) collective-permute-start(f32[520,128]{1,0:T(8,128)S(1)} %pad_maximum_fusion.7), channel_id=1, source_target_pairs={{0,2},{1,3},{2,0},{3,1},{4,6},{5,7},{6,4},{7,5},{8,10},{9,11},{10,... | collective-permute-start | bytes 798728 | tf_op jit(solution)/shard_map/ppermute | solution.py:501
  68.0 7.9 %collective-permute-start.14 = (f32[776,128]{1,0:T(8,128)S(1)}, f32[776,128]{1,0:T(8,128)S(1)}, u32[]{:S(2)}, u32[]{:S(2)}) collective-permute-start(f32[776,128]{1,0:T(8,128)S(1)} %get-tuple-element.136), channel_id=1, source_target_pairs={{0,4},{1,9},{2,6},{3,11},{4,0},{5,13},{6,2},{7,15},{8,12},{9,1},{1... | collective-permute-start | bytes 1191944 | tf_op jit(solution)/shard_map/ppermute | solution.py:498
  73.5 3.2 %collective-permute-start.17 = (f32[512,128]{1,0:T(8,128)S(1)}, f32[512,128]{1,0:T(8,128)S(1)}, u32[]{:S(2)}, u32[]{:S(2)}) collective-permute-start(f32[512,128]{1,0:T(8,128)S(1)} %slice_add_fusion.10.refs_2_), channel_id=1, source_target_pairs={{0,1},{1,0},{2,3},{3,2},{4,5},{5,4},{6,7},{7,6},{8,9},{9,8},{10,11... | collective-permute-start | bytes 786440 | tf_op jit(solution)/shard_map/ppermute | solution.py:501
  76.0 6.0 %collective-permute-start.16 = (f32[392,128]{1,0:T(8,128)S(1)}, f32[392,128]{1,0:T(8,128)S(1)}, u32[]{:S(2)}, u32[]{:S(2)}) collective-permute-start(f32[392,128]{1,0:T(8,128)S(1)} %pad_maximum_fusion.14), channel_id=1, source_target_pairs={{0,8},{1,5},{2,10},{3,7},{4,12},{5,1},{6,14},{7,3},{8,0},{9,13},{1... | collective-permute-start | bytes 602120 | tf_op jit(solution)/shard_map/ppermute | solution.py:498
  78.1 12.9 %collective-permute-start.19 = (f32[776,128]{1,0:T(8,128)S(1)}, f32[776,128]{1,0:T(8,128)S(1)}, u32[]{:S(2)}, u32[]{:S(2)}) collective-permute-start(f32[776,128]{1,0:T(8,128)S(1)} %get-tuple-element.140), channel_id=1, source_target_pairs={{0,8},{1,5},{2,10},{3,7},{4,12},{5,1},{6,14},{7,3},{8,0},{9,13},{1... | collective-permute-start | bytes 1191944 | tf_op jit(solution)/shard_map/ppermute | solution.py:498
  82.1 10.8 %collective-permute-start.18 = (f32[392,128]{1,0:T(8,128)S(1)}, f32[392,128]{1,0:T(8,128)S(1)}, u32[]{:S(2)}, u32[]{:S(2)}) collective-permute-start(f32[392,128]{1,0:T(8,128)S(1)} %pad_maximum_fusion.15), channel_id=1, source_target_pairs={{0,16},{1,17},{2,18},{3,19},{4,20},{5,21},{6,22},{7,23},{8,24},{9,... | collective-permute-start | bytes 602120 | tf_op jit(solution)/shard_map/ppermute | solution.py:498
  91.1 5.8 %collective-permute-start.21 = (f32[392,128]{1,0:T(8,128)S(1)}, f32[392,128]{1,0:T(8,128)S(1)}, u32[]{:S(2)}, u32[]{:S(2)}) collective-permute-start(f32[392,128]{1,0:T(8,128)S(1)} %pad_maximum_fusion.16), channel_id=1, source_target_pairs={{0,4},{1,9},{2,6},{3,11},{4,0},{5,13},{6,2},{7,15},{8,12},{9,1},{1... | collective-permute-start | bytes 602120 | tf_op jit(solution)/shard_map/ppermute | solution.py:498
  92.8 10.3 %collective-permute-start.20 = (f32[384,128]{1,0:T(8,128)S(1)}, f32[384,128]{1,0:T(8,128)S(1)}, u32[]{:S(2)}, u32[]{:S(2)}) collective-permute-start(f32[384,128]{1,0:T(8,128)S(1)} %slice_add_fusion.23.mine_ref), channel_id=1, source_target_pairs={{0,8},{1,5},{2,10},{3,7},{4,12},{5,1},{6,14},{7,3},{8,0},{9,13},{1... | collective-permute-start | bytes 589832 | tf_op jit(solution)/shard_map/ppermute | solution.py:498
  97.0 9.1 %collective-permute-start.23 = (f32[392,128]{1,0:T(8,128)S(1)}, f32[392,128]{1,0:T(8,128)S(1)}, u32[]{:S(2)}, u32[]{:S(2)}) collective-permute-start(f32[392,128]{1,0:T(8,128)S(1)} %pad_maximum_fusion.17), channel_id=1, source_target_pairs={{0,16},{1,17},{2,18},{3,19},{4,20},{5,21},{6,22},{7,23},{8,24},{9,... | collective-permute-start | bytes 602120 | tf_op jit(solution)/shard_map/ppermute | solution.py:498
  103.2 8.7 %collective-permute-start.22 = (f32[768,128]{1,0:T(8,128)S(1)}, f32[768,128]{1,0:T(8,128)S(1)}, u32[]{:S(2)}, u32[]{:S(2)}) collective-permute-start(f32[768,128]{1,0:T(8,128)S(1)} %pad_maximum_fusion.2), channel_id=1, source_target_pairs={{0,4},{1,9},{2,6},{3,11},{4,0},{5,13},{6,2},{7,15},{8,12},{9,1},{1... | collective-permute-start | bytes 1179656 | tf_op jit(solution)/shard_map/ppermute | solution.py:498
  106.1 7.8 %collective-permute-start.25 = (f32[384,128]{1,0:T(8,128)S(1)}, f32[384,128]{1,0:T(8,128)S(1)}, u32[]{:S(2)}, u32[]{:S(2)}) collective-permute-start(f32[384,128]{1,0:T(8,128)S(1)} %slice_add_fusion.22.mine_ref), channel_id=1, source_target_pairs={{0,4},{1,9},{2,6},{3,11},{4,0},{5,13},{6,2},{7,15},{8,12},{9,1},{1... | collective-permute-start | bytes 589832 | tf_op jit(solution)/shard_map/ppermute | solution.py:498
  112.9 2.1 %collective-permute-start.24 = (f32[520,128]{1,0:T(8,128)S(1)}, f32[520,128]{1,0:T(8,128)S(1)}, u32[]{:S(2)}, u32[]{:S(2)}) collective-permute-start(f32[520,128]{1,0:T(8,128)S(1)} %get-tuple-element.154), channel_id=1, source_target_pairs={{0,1},{1,0},{2,3},{3,2},{4,5},{5,4},{6,7},{7,6},{8,9},{9,8},{10,11... | collective-permute-start | bytes 798728 | tf_op jit(solution)/shard_map/ppermute | solution.py:501
  114.0 7.8 %collective-permute-start.27 = (f32[768,128]{1,0:T(8,128)S(1)}, f32[768,128]{1,0:T(8,128)S(1)}, u32[]{:S(2)}, u32[]{:S(2)}) collective-permute-start(f32[768,128]{1,0:T(8,128)S(1)} %pad_maximum_fusion.3), channel_id=1, source_target_pairs={{0,8},{1,5},{2,10},{3,7},{4,12},{5,1},{6,14},{7,3},{8,0},{9,13},{1... | collective-permute-start | bytes 1179656 | tf_op jit(solution)/shard_map/ppermute | solution.py:498
  115.2 9.0 %collective-permute-start.26 = (f32[520,128]{1,0:T(8,128)S(1)}, f32[520,128]{1,0:T(8,128)S(1)}, u32[]{:S(2)}, u32[]{:S(2)}) collective-permute-start(f32[520,128]{1,0:T(8,128)S(1)} %pad_maximum_fusion.8), channel_id=1, source_target_pairs={{0,2},{1,3},{2,0},{3,1},{4,6},{5,7},{6,4},{7,5},{8,10},{9,11},{10,... | collective-permute-start | bytes 798728 | tf_op jit(solution)/shard_map/ppermute | solution.py:501
  122.9 2.5 %collective-permute-start.29 = (f32[520,128]{1,0:T(8,128)S(1)}, f32[520,128]{1,0:T(8,128)S(1)}, u32[]{:S(2)}, u32[]{:S(2)}) collective-permute-start(f32[520,128]{1,0:T(8,128)S(1)} %get-tuple-element.165), channel_id=1, source_target_pairs={{0,1},{1,0},{2,3},{3,2},{4,5},{5,4},{6,7},{7,6},{8,9},{9,8},{10,11... | collective-permute-start | bytes 798728 | tf_op jit(solution)/shard_map/ppermute | solution.py:501
  124.2 2.1 %collective-permute-start.28 = (f32[512,128]{1,0:T(8,128)S(1)}, f32[512,128]{1,0:T(8,128)S(1)}, u32[]{:S(2)}, u32[]{:S(2)}) collective-permute-start(f32[512,128]{1,0:T(8,128)S(1)} %slice_add_fusion.8.refs_2_), channel_id=1, source_target_pairs={{0,1},{1,0},{2,3},{3,2},{4,5},{5,4},{6,7},{7,6},{8,9},{9,8},{10,11... | collective-permute-start | bytes 786440 | tf_op jit(solution)/shard_map/ppermute | solution.py:501
  125.5 8.7 %collective-permute-start.31 = (f32[520,128]{1,0:T(8,128)S(1)}, f32[520,128]{1,0:T(8,128)S(1)}, u32[]{:S(2)}, u32[]{:S(2)}) collective-permute-start(f32[520,128]{1,0:T(8,128)S(1)} %pad_maximum_fusion.9), channel_id=1, source_target_pairs={{0,2},{1,3},{2,0},{3,1},{4,6},{5,7},{6,4},{7,5},{8,10},{9,11},{10,... | collective-permute-start | bytes 798728 | tf_op jit(solution)/shard_map/ppermute | solution.py:501
  127.9 7.8 %collective-permute-start.30 = (f32[776,128]{1,0:T(8,128)S(1)}, f32[776,128]{1,0:T(8,128)S(1)}, u32[]{:S(2)}, u32[]{:S(2)}) collective-permute-start(f32[776,128]{1,0:T(8,128)S(1)} %get-tuple-element.172), channel_id=1, source_target_pairs={{0,4},{1,9},{2,6},{3,11},{4,0},{5,13},{6,2},{7,15},{8,12},{9,1},{1... | collective-permute-start | bytes 1191944 | tf_op jit(solution)/shard_map/ppermute | solution.py:498
  134.3 1.6 collective-permute-start.33
  135.8 5.8 %collective-permute-start.32 = (f32[392,128]{1,0:T(8,128)S(1)}, f32[392,128]{1,0:T(8,128)S(1)}, u32[]{:S(2)}, u32[]{:S(2)}) collective-permute-start(f32[392,128]{1,0:T(8,128)S(1)} %pad_maximum_fusion.18), channel_id=1, source_target_pairs={{0,8},{1,5},{2,10},{3,7},{4,12},{5,1},{6,14},{7,3},{8,0},{9,13},{1... | collective-permute-start | bytes 602120 | tf_op jit(solution)/shard_map/ppermute | solution.py:498
  137.4 13.0 %collective-permute-start.35 = (f32[776,128]{1,0:T(8,128)S(1)}, f32[776,128]{1,0:T(8,128)S(1)}, u32[]{:S(2)}, u32[]{:S(2)}) collective-permute-start(f32[776,128]{1,0:T(8,128)S(1)} %get-tuple-element.178), channel_id=1, source_target_pairs={{0,8},{1,5},{2,10},{3,7},{4,12},{5,1},{6,14},{7,3},{8,0},{9,13},{1... | collective-permute-start | bytes 1191944 | tf_op jit(solution)/shard_map/ppermute | solution.py:498
  141.6 9.6 %collective-permute-start.34 = (f32[392,128]{1,0:T(8,128)S(1)}, f32[392,128]{1,0:T(8,128)S(1)}, u32[]{:S(2)}, u32[]{:S(2)}) collective-permute-start(f32[392,128]{1,0:T(8,128)S(1)} %pad_maximum_fusion.19), channel_id=1, source_target_pairs={{0,16},{1,17},{2,18},{3,19},{4,20},{5,21},{6,22},{7,23},{8,24},{9,... | collective-permute-start | bytes 602120 | tf_op jit(solution)/shard_map/ppermute | solution.py:498
  150.5 5.8 %collective-permute-start.36 = (f32[392,128]{1,0:T(8,128)S(1)}, f32[392,128]{1,0:T(8,128)S(1)}, u32[]{:S(2)}, u32[]{:S(2)}) collective-permute-start(f32[392,128]{1,0:T(8,128)S(1)} %pad_maximum_fusion.20), channel_id=1, source_target_pairs={{0,4},{1,9},{2,6},{3,11},{4,0},{5,13},{6,2},{7,15},{8,12},{9,1},{1... | collective-permute-start | bytes 602120 | tf_op jit(solution)/shard_map/ppermute | solution.py:498
  151.2 9.0 %collective-permute-start.38 = (f32[384,128]{1,0:T(8,128)S(1)}, f32[384,128]{1,0:T(8,128)S(1)}, u32[]{:S(2)}, u32[]{:S(2)}) collective-permute-start(f32[384,128]{1,0:T(8,128)S(1)} %slice_add_fusion.21.mine_ref), channel_id=1, source_target_pairs={{0,8},{1,5},{2,10},{3,7},{4,12},{5,1},{6,14},{7,3},{8,0},{9,13},{1... | collective-permute-start | bytes 589832 | tf_op jit(solution)/shard_map/ppermute | solution.py:498
  156.4 8.7 %collective-permute-start.37 = (f32[392,128]{1,0:T(8,128)S(1)}, f32[392,128]{1,0:T(8,128)S(1)}, u32[]{:S(2)}, u32[]{:S(2)}) collective-permute-start(f32[392,128]{1,0:T(8,128)S(1)} %pad_maximum_fusion.21), channel_id=1, source_target_pairs={{0,16},{1,17},{2,18},{3,19},{4,20},{5,21},{6,22},{7,23},{8,24},{9,... | collective-permute-start | bytes 602120 | tf_op jit(solution)/shard_map/ppermute | solution.py:498
  165.1 7.3 %collective-permute-start.40 = (f32[384,128]{1,0:T(8,128)S(1)}, f32[384,128]{1,0:T(8,128)S(1)}, u32[]{:S(2)}, u32[]{:S(2)}) collective-permute-start(f32[384,128]{1,0:T(8,128)S(1)} %slice_add_fusion.20.refs_6_), channel_id=1, source_target_pairs={{0,4},{1,9},{2,6},{3,11},{4,0},{5,13},{6,2},{7,15},{8,12},{9,1},{1... | collective-permute-start | bytes 589832 | tf_op jit(solution)/shard_map/ppermute | solution.py:498
  166.0 13.2 %collective-permute-start.39 = (f32[768,128]{1,0:T(8,128)S(1)}, f32[768,128]{1,0:T(8,128)S(1)}, u32[]{:S(2)}, u32[]{:S(2)}) collective-permute-start(f32[768,128]{1,0:T(8,128)S(1)} %pad_maximum_fusion.4), channel_id=1, source_target_pairs={{0,4},{1,9},{2,6},{3,11},{4,0},{5,13},{6,2},{7,15},{8,12},{9,1},{1... | collective-permute-start | bytes 1179656 | tf_op jit(solution)/shard_map/ppermute | solution.py:498
  172.5 7.8 %collective-permute-start.41 = (f32[768,128]{1,0:T(8,128)S(1)}, f32[768,128]{1,0:T(8,128)S(1)}, u32[]{:S(2)}, u32[]{:S(2)}) collective-permute-start(f32[768,128]{1,0:T(8,128)S(1)} %pad_maximum_fusion.5), channel_id=1, source_target_pairs={{0,8},{1,5},{2,10},{3,7},{4,12},{5,1},{6,14},{7,3},{8,0},{9,13},{1... | collective-permute-start | bytes 1179656 | tf_op jit(solution)/shard_map/ppermute | solution.py:498

commit v25 on v23

--- a/solution.py
+++ b/solution.py
@@ -555,7 +555,8 @@
         for iteration in range(ITERS):
             outer, *own = totals
             pasts = [[right, norms[-2]] for right in rights[-1]] if rights else [[], []]
-            own = [tied(own[0], ahead), own[1]]
+            if second:
+                own = [tied(own[0], ahead), own[1]]
             part, squares, own_right = fore_own_product(
                 order, dense, [*own, norms[-1], *pasts[1]], not rights
             )

time: 182 us -> 181 us (level)
  waiting for transfers between devices: 101 us -> 86.9 us
  starting transfers between devices: 37.4 us -> 49.4 us
    ppermute x30, waiting for transfers between devices: 91.9 us -> 75.5 us  [swap_rows(): return lax.ppermute(value, ('rows', 'cols'), pairs)]
    ppermute x30, starting transfers between devices: 32.1 us -> 44.6 us  [swap_rows(): return lax.ppermute(value, ('rows', 'cols'), pairs)]
    ppermute x12, waiting for transfers between devices: 8.85 us -> 11.4 us  [swap_cols(): lax.ppermute(value, 'cols', [(i, i ^ 1 << level) for i in range(col_count)])]
  transfers between devices with their start and end apart: 42 -> 42, of which waited for: 33 -> 32; matrix products, arithmetic and copies ran while one was open for 1% -> 1% of each run, Pallas kernels for 18% -> 18%
where the time goes in v25:
time: 181 us; the launch traced here: 180 us
  waiting for transfers between devices  86.9 us (48%)
  starting transfers between devices  49.4 us (27%)
  Pallas kernels  40.4 us (22%)
    ppermute x30, waiting for transfers between devices, swap_rows(): return lax.ppermute(value, ('rows', 'cols'), pairs)  75.5 us
    ppermute x30, starting transfers between devices, swap_rows(): return lax.ppermute(value, ('rows', 'cols'), pairs)  44.6 us
    pallas_call x24, Pallas kernels, product_call(): pl.pallas_call(body, in_specs=[WHOLE] * (1 + len(operands)), out_specs=[W...  32.2 us
    ppermute x12, waiting for transfers between devices, swap_cols(): lax.ppermute(value, 'cols', [(i, i ^ 1 << level) for i in range(col_count)])  11.4 us
    pallas_call x1, Pallas kernels, fill_dense(): pl.pallas_call(fill_kernel, in_specs=[SCALARS] * 2 + [pl.BlockSpec(memory...  4.95 us
    ppermute x12, starting transfers between devices, swap_cols(): lax.ppermute(value, 'cols', [(i, i ^ 1 << level) for i in range(col_count)])  4.86 us
  transfers between devices with their start and end apart: 42, of which 32 were waited for; matrix products, arithmetic and copies ran while one was open for 1% of the time, Pallas kernels for 18%

profile of v25, /device:TPU:0, one launch (start us, length us, event | category | flops | bytes accessed | tf_op | source)
XLA Modules:
  0.0 180.3 jit_solution(6198024792362536082)
XLA Ops:
  0.7 5.0 %shard_map.67 = (bf16[2048,3200]{1,0:T(8,128)(2,1)S(1)}, f32[1024,128]{1,0:T(8,128)S(1)}, f32[1024,128]{1,0:T(8,128)S(1)}) custom-call(s32[24]{0:T(128)S(1)} %fusion.place_ref, s32[1]{0:T(128)} %bitcast.1.flip_ref, s32[16,16]{1,0:T(8,128)} %pattern_in.1, s32[16]{0:T(128)} %bitcast.5, f32[2048,128]{1,0:T(8,128)} %delays_in.1, bf16[16,16,128,128]{3,2,1,0:T(8,128)(2,1)} %tiles_in.1), custom_call_target="tpu_custom_call" | custom-call | bytes 8388608 | tf_op jit(solution)/shard_map/pallas_call | solution.py:112
  7.0 2.8 %collective-permute-start = (f32[776,128]{1,0:T(8,128)S(1)}, f32[776,128]{1,0:T(8,128)S(1)}, u32[]{:S(2)}, u32[]{:S(2)}) collective-permute-start(f32[776,128]{1,0:T(8,128)S(1)} %get-tuple-element.100), channel_id=1, source_target_pairs={{0,4},{1,9},{2,6},{3,11},{4,0},{5,13},{6,2},{7,15},{8,12},{9,1},{1... | collective-permute-start | bytes 1191944 | tf_op jit(solution)/shard_map/ppermute | solution.py:498
  12.5 3.1 %collective-permute-done = f32[776,128]{1,0:T(8,128)S(1)} collective-permute-done((f32[776,128]{1,0:T(8,128)S(1)}, f32[776,128]{1,0:T(8,128)S(1)}, u32[]{:S(2)}, u32[]{:S(2)}) %collective-permute-start) | collective-permute-done | bytes 397344 | tf_op jit(solution)/shard_map/ppermute | solution.py:498
  19.2 2.3 %collective-permute-done.1 = f32[392,128]{1,0:T(8,128)S(1)} collective-permute-done((f32[392,128]{1,0:T(8,128)S(1)}, f32[392,128]{1,0:T(8,128)S(1)}, u32[]{:S(2)}, u32[]{:S(2)}) %collective-permute-start.1) | collective-permute-done | bytes 200736 | tf_op jit(solution)/shard_map/ppermute | solution.py:498
  21.6 3.3 %collective-permute-start.2 = (f32[392,128]{1,0:T(8,128)S(1)}, f32[392,128]{1,0:T(8,128)S(1)}, u32[]{:S(2)}, u32[]{:S(2)}) collective-permute-start(f32[392,128]{1,0:T(8,128)S(1)} %pad_maximum_fusion.11), channel_id=1, source_target_pairs={{0,16},{1,17},{2,18},{3,19},{4,20},{5,21},{6,22},{7,23},{8,24},{9,... | collective-permute-start | bytes 602120 | tf_op jit(solution)/shard_map/ppermute | solution.py:498
  24.9 6.1 %collective-permute-done.3 = f32[776,128]{1,0:T(8,128)S(1)} collective-permute-done((f32[776,128]{1,0:T(8,128)S(1)}, f32[776,128]{1,0:T(8,128)S(1)}, u32[]{:S(2)}, u32[]{:S(2)}) %collective-permute-start.3) | collective-permute-done | bytes 397344 | tf_op jit(solution)/shard_map/ppermute | solution.py:498
  31.1 2.7 %collective-permute-start.5 = (f32[392,128]{1,0:T(8,128)S(1)}, f32[392,128]{1,0:T(8,128)S(1)}, u32[]{:S(2)}, u32[]{:S(2)}) collective-permute-start(f32[392,128]{1,0:T(8,128)S(1)} %pad_maximum_fusion.12), channel_id=1, source_target_pairs={{0,4},{1,9},{2,6},{3,11},{4,0},{5,13},{6,2},{7,15},{8,12},{9,1},{1... | collective-permute-start | bytes 602120 | tf_op jit(solution)/shard_map/ppermute | solution.py:498
  33.8 1.9 %collective-permute-start.4 = (f32[384,128]{1,0:T(8,128)S(1)}, f32[384,128]{1,0:T(8,128)S(1)}, u32[]{:S(2)}, u32[]{:S(2)}) collective-permute-start(f32[384,128]{1,0:T(8,128)S(1)} %slice_add_fusion.25.mine_ref), channel_id=1, source_target_pairs={{0,8},{1,5},{2,10},{3,7},{4,12},{5,1},{6,14},{7,3},{8,0},{9,13},{1... | collective-permute-start | bytes 589832 | tf_op jit(solution)/shard_map/ppermute | solution.py:498
  35.7 1.8 collective-permute-done.5
  37.6 1.8 collective-permute-start.7
  39.4 3.8 %collective-permute-done.4.inner_ref = f32[384,128]{1,0:T(8,128)S(1)} collective-permute-done((f32[384,128]{1,0:T(8,128)S(1)}, f32[384,128]{1,0:T(8,128)S(1)}, u32[]{:S(2)}, u32[]{:S(2)}) %collective-permute-start.4) | collective-permute-done | bytes 196640 | tf_op jit(solution)/shard_map/ppermute | solution.py:498
  43.2 1.9 %collective-permute-start.6 = (f32[768,128]{1,0:T(8,128)S(1)}, f32[768,128]{1,0:T(8,128)S(1)}, u32[]{:S(2)}, u32[]{:S(2)}) collective-permute-start(f32[768,128]{1,0:T(8,128)S(1)} %pad_maximum_fusion), channel_id=1, source_target_pairs={{0,4},{1,9},{2,6},{3,11},{4,0},{5,13},{6,2},{7,15},{8,12},{9,1},{1... | collective-permute-start | bytes 1179656 | tf_op jit(solution)/shard_map/ppermute | solution.py:498
  45.0 1.9 %shard_map.72 = (f32[1024,128]{1,0:T(8,128)S(1)}, f32[8,128]{1,0:T(8,128)S(1)}, f32[768,128]{1,0:T(8,128)S(1)}) custom-call(bf16[2048,3200]{1,0:T(8,128)(2,1)S(1)} %get-tuple-element.97.refs_0_.dense_ref, f32[384,128]{1,0:T(8,128)S(1)} %collective-permute-done.4.inner_ref, f32[384,128]{1,0:T(8,128)S(1)} %slice_add_fusion.25.mine_ref, ...), custom_call_target="tpu_custom_call" | custom-call | flops 1677721600 | bytes 6553600 | tf_op jit(solution)/shard_map/pallas_call | solution.py:268
  47.0 1.4 collective-permute-start.8
  48.4 2.6 %collective-permute-done.6.outer_ref = f32[768,128]{1,0:T(8,128)S(1)} collective-permute-done((f32[768,128]{1,0:T(8,128)S(1)}, f32[768,128]{1,0:T(8,128)S(1)}, u32[]{:S(2)}, u32[]{:S(2)}) %collective-permute-start.6) | collective-permute-done | bytes 393248 | tf_op jit(solution)/shard_map/ppermute | solution.py:498
  54.7 1.8 collective-permute-start.10
  56.5 1.9 %shard_map.75 = (f32[1024,128]{1,0:T(8,128)S(1)}, f32[8,128]{1,0:T(8,128)S(1)}, f32[768,128]{1,0:T(8,128)S(1)}) custom-call(bf16[2048,3200]{1,0:T(8,128)(2,1)S(1)} %get-tuple-element.97.refs_0_.dense_ref, f32[384,128]{1,0:T(8,128)S(1)} %collective-permute-done.8.inner_ref, f32[384,128]{1,0:T(8,128)S(1)} %slice_add_fusion.24.mine_ref, ...), custom_call_target="tpu_custom_call" | custom-call | flops 1677721600 | bytes 6553600 | tf_op jit(solution)/shard_map/pallas_call | solution.py:268
  58.4 2.6 %collective-permute-done.11.outer_ref = f32[768,128]{1,0:T(8,128)S(1)} collective-permute-done((f32[768,128]{1,0:T(8,128)S(1)}, f32[768,128]{1,0:T(8,128)S(1)}, u32[]{:S(2)}, u32[]{:S(2)}) %collective-permute-start.11) | collective-permute-done | bytes 393248 | tf_op jit(solution)/shard_map/ppermute | solution.py:498
  62.2 1.6 collective-permute-done.10
  65.0 1.4 collective-permute-start.15
  66.4 1.4 shard_map.78
  70.2 3.6 %collective-permute-done.15 = f32[520,128]{1,0:T(8,128)S(1)} collective-permute-done((f32[520,128]{1,0:T(8,128)S(1)}, f32[520,128]{1,0:T(8,128)S(1)}, u32[]{:S(2)}, u32[]{:S(2)}) %collective-permute-start.15) | collective-permute-done | bytes 266272 | tf_op jit(solution)/shard_map/ppermute | solution.py:501
  73.9 1.8 collective-permute-done.14
  76.6 1.4 shard_map.80
  82.3 7.0 %collective-permute-done.19 = f32[776,128]{1,0:T(8,128)S(1)} collective-permute-done((f32[776,128]{1,0:T(8,128)S(1)}, f32[776,128]{1,0:T(8,128)S(1)}, u32[]{:S(2)}, u32[]{:S(2)}) %collective-permute-start.19) | collective-permute-done | bytes 397344 | tf_op jit(solution)/shard_map/ppermute | solution.py:498
  89.4 2.2 %collective-permute-start.21 = (f32[392,128]{1,0:T(8,128)S(1)}, f32[392,128]{1,0:T(8,128)S(1)}, u32[]{:S(2)}, u32[]{:S(2)}) collective-permute-start(f32[392,128]{1,0:T(8,128)S(1)} %pad_maximum_fusion.16), channel_id=1, source_target_pairs={{0,4},{1,9},{2,6},{3,11},{4,0},{5,13},{6,2},{7,15},{8,12},{9,1},{1... | collective-permute-start | bytes 602120 | tf_op jit(solution)/shard_map/ppermute | solution.py:498
  93.1 3.3 %collective-permute-done.21 = f32[392,128]{1,0:T(8,128)S(1)} collective-permute-done((f32[392,128]{1,0:T(8,128)S(1)}, f32[392,128]{1,0:T(8,128)S(1)}, u32[]{:S(2)}, u32[]{:S(2)}) %collective-permute-start.21) | collective-permute-done | bytes 200736 | tf_op jit(solution)/shard_map/ppermute | solution.py:498
  97.7 2.6 %collective-permute-done.20.inner_ref = f32[384,128]{1,0:T(8,128)S(1)} collective-permute-done((f32[384,128]{1,0:T(8,128)S(1)}, f32[384,128]{1,0:T(8,128)S(1)}, u32[]{:S(2)}, u32[]{:S(2)}) %collective-permute-start.20) | collective-permute-done | bytes 196640 | tf_op jit(solution)/shard_map/ppermute | solution.py:498
  100.4 1.7 collective-permute-start.22
  102.1 1.9 %shard_map.82 = (f32[1024,128]{1,0:T(8,128)S(1)}, f32[8,128]{1,0:T(8,128)S(1)}, f32[768,128]{1,0:T(8,128)S(1)}) custom-call(bf16[2048,3200]{1,0:T(8,128)(2,1)S(1)} %get-tuple-element.97.refs_0_.dense_ref, f32[384,128]{1,0:T(8,128)S(1)} %collective-permute-done.20.inner_ref, f32[384,128]{1,0:T(8,128)S(1)} %slice_add_fusion.23.mine_ref, ...), custom_call_target="tpu_custom_call" | custom-call | flops 1677721600 | bytes 6553600 | tf_op jit(solution)/shard_map/pallas_call | solution.py:268
  105.3 3.0 %collective-permute-done.22.outer_ref = f32[768,128]{1,0:T(8,128)S(1)} collective-permute-done((f32[768,128]{1,0:T(8,128)S(1)}, f32[768,128]{1,0:T(8,128)S(1)}, u32[]{:S(2)}, u32[]{:S(2)}) %collective-permute-start.22) | collective-permute-done | bytes 393248 | tf_op jit(solution)/shard_map/ppermute | solution.py:498
  110.4 2.3 %collective-permute-start.27 = (f32[768,128]{1,0:T(8,128)S(1)}, f32[768,128]{1,0:T(8,128)S(1)}, u32[]{:S(2)}, u32[]{:S(2)}) collective-permute-start(f32[768,128]{1,0:T(8,128)S(1)} %pad_maximum_fusion.3), channel_id=1, source_target_pairs={{0,8},{1,5},{2,10},{3,7},{4,12},{5,1},{6,14},{7,3},{8,0},{9,13},{1... | collective-permute-start | bytes 1179656 | tf_op jit(solution)/shard_map/ppermute | solution.py:498
  114.5 1.9 %shard_map.85 = (f32[1024,128]{1,0:T(8,128)S(1)}, f32[8,128]{1,0:T(8,128)S(1)}, f32[768,128]{1,0:T(8,128)S(1)}) custom-call(bf16[2048,3200]{1,0:T(8,128)(2,1)S(1)} %get-tuple-element.97.refs_0_.dense_ref, f32[384,128]{1,0:T(8,128)S(1)} %collective-permute-done.25.inner_ref, f32[384,128]{1,0:T(8,128)S(1)} %slice_add_fusion.22.mine_ref, ...), custom_call_target="tpu_custom_call" | custom-call | flops 1677721600 | bytes 6553600 | tf_op jit(solution)/shard_map/pallas_call | solution.py:268
  116.4 2.0 %collective-permute-done.27.outer_ref = f32[768,128]{1,0:T(8,128)S(1)} collective-permute-done((f32[768,128]{1,0:T(8,128)S(1)}, f32[768,128]{1,0:T(8,128)S(1)}, u32[]{:S(2)}, u32[]{:S(2)}) %collective-permute-start.27) | collective-permute-done | bytes 393248 | tf_op jit(solution)/shard_map/ppermute | solution.py:498
  122.4 1.5 shard_map.88
  126.0 4.9 %collective-permute-done.31 = f32[520,128]{1,0:T(8,128)S(1)} collective-permute-done((f32[520,128]{1,0:T(8,128)S(1)}, f32[520,128]{1,0:T(8,128)S(1)}, u32[]{:S(2)}, u32[]{:S(2)}) %collective-permute-start.31) | collective-permute-done | bytes 266272 | tf_op jit(solution)/shard_map/ppermute | solution.py:501
  131.9 1.7 collective-permute-start.32
  133.6 1.5 shard_map.90
  137.7 3.1 %collective-permute-start.34 = (f32[392,128]{1,0:T(8,128)S(1)}, f32[392,128]{1,0:T(8,128)S(1)}, u32[]{:S(2)}, u32[]{:S(2)}) collective-permute-start(f32[392,128]{1,0:T(8,128)S(1)} %pad_maximum_fusion.19), channel_id=1, source_target_pairs={{0,16},{1,17},{2,18},{3,19},{4,20},{5,21},{6,22},{7,23},{8,24},{9,... | collective-permute-start | bytes 602120 | tf_op jit(solution)/shard_map/ppermute | solution.py:498
  140.8 7.6 %collective-permute-done.35 = f32[776,128]{1,0:T(8,128)S(1)} collective-permute-done((f32[776,128]{1,0:T(8,128)S(1)}, f32[776,128]{1,0:T(8,128)S(1)}, u32[]{:S(2)}, u32[]{:S(2)}) %collective-permute-start.35) | collective-permute-done | bytes 397344 | tf_op jit(solution)/shard_map/ppermute | solution.py:498
  149.7 2.8 %collective-permute-start.38 = (f32[384,128]{1,0:T(8,128)S(1)}, f32[384,128]{1,0:T(8,128)S(1)}, u32[]{:S(2)}, u32[]{:S(2)}) collective-permute-start(f32[384,128]{1,0:T(8,128)S(1)} %slice_add_fusion.21.mine_ref), channel_id=1, source_target_pairs={{0,8},{1,5},{2,10},{3,7},{4,12},{5,1},{6,14},{7,3},{8,0},{9,13},{1... | collective-permute-start | bytes 589832 | tf_op jit(solution)/shard_map/ppermute | solution.py:498
  152.5 1.7 collective-permute-done.36
  155.3 1.8 collective-permute-done.38.inner_ref
  157.1 6.1 %collective-permute-done.37 = f32[392,128]{1,0:T(8,128)S(1)} collective-permute-done((f32[392,128]{1,0:T(8,128)S(1)}, f32[392,128]{1,0:T(8,128)S(1)}, u32[]{:S(2)}, u32[]{:S(2)}) %collective-permute-start.37) | collective-permute-done | bytes 200736 | tf_op jit(solution)/shard_map/ppermute | solution.py:498
  165.3 5.8 %collective-permute-done.40.refs_5_ = f32[384,128]{1,0:T(8,128)S(1)} collective-permute-done((f32[384,128]{1,0:T(8,128)S(1)}, f32[384,128]{1,0:T(8,128)S(1)}, u32[]{:S(2)}, u32[]{:S(2)}) %collective-permute-start.40) | collective-permute-done | bytes 196640 | tf_op jit(solution)/shard_map/ppermute | solution.py:498
  171.2 1.8 shard_map.92
  173.5 1.8 %collective-permute-done.39.outer_ref = f32[768,128]{1,0:T(8,128)S(1)} collective-permute-done((f32[768,128]{1,0:T(8,128)S(1)}, f32[768,128]{1,0:T(8,128)S(1)}, u32[]{:S(2)}, u32[]{:S(2)}) %collective-permute-start.39) | collective-permute-done | bytes 393248 | tf_op jit(solution)/shard_map/ppermute | solution.py:498
  175.7 3.3 %collective-permute-done.41.outer_ref = f32[768,128]{1,0:T(8,128)S(1)} collective-permute-done((f32[768,128]{1,0:T(8,128)S(1)}, f32[768,128]{1,0:T(8,128)S(1)}, u32[]{:S(2)}, u32[]{:S(2)}) %collective-permute-start.41) | collective-permute-done | bytes 393248 | tf_op jit(solution)/shard_map/ppermute | solution.py:498
  (146 shorter events, 45.7 us)
Async XLA Ops:
  7.0 8.6 %collective-permute-start = (f32[776,128]{1,0:T(8,128)S(1)}, f32[776,128]{1,0:T(8,128)S(1)}, u32[]{:S(2)}, u32[]{:S(2)}) collective-permute-start(f32[776,128]{1,0:T(8,128)S(1)} %get-tuple-element.100), channel_id=1, source_target_pairs={{0,4},{1,9},{2,6},{3,11},{4,0},{5,13},{6,2},{7,15},{8,12},{9,1},{1... | collective-permute-start | bytes 1191944 | tf_op jit(solution)/shard_map/ppermute | solution.py:498
  15.7 5.8 %collective-permute-start.1 = (f32[392,128]{1,0:T(8,128)S(1)}, f32[392,128]{1,0:T(8,128)S(1)}, u32[]{:S(2)}, u32[]{:S(2)}) collective-permute-start(f32[392,128]{1,0:T(8,128)S(1)} %pad_maximum_fusion.10), channel_id=1, source_target_pairs={{0,8},{1,5},{2,10},{3,7},{4,12},{5,1},{6,14},{7,3},{8,0},{9,13},{1... | collective-permute-start | bytes 602120 | tf_op jit(solution)/shard_map/ppermute | solution.py:498
  17.9 13.1 %collective-permute-start.3 = (f32[776,128]{1,0:T(8,128)S(1)}, f32[776,128]{1,0:T(8,128)S(1)}, u32[]{:S(2)}, u32[]{:S(2)}) collective-permute-start(f32[776,128]{1,0:T(8,128)S(1)} %get-tuple-element.104), channel_id=1, source_target_pairs={{0,8},{1,5},{2,10},{3,7},{4,12},{5,1},{6,14},{7,3},{8,0},{9,13},{1... | collective-permute-start | bytes 1191944 | tf_op jit(solution)/shard_map/ppermute | solution.py:498
  21.6 12.2 %collective-permute-start.2 = (f32[392,128]{1,0:T(8,128)S(1)}, f32[392,128]{1,0:T(8,128)S(1)}, u32[]{:S(2)}, u32[]{:S(2)}) collective-permute-start(f32[392,128]{1,0:T(8,128)S(1)} %pad_maximum_fusion.11), channel_id=1, source_target_pairs={{0,16},{1,17},{2,18},{3,19},{4,20},{5,21},{6,22},{7,23},{8,24},{9,... | collective-permute-start | bytes 602120 | tf_op jit(solution)/shard_map/ppermute | solution.py:498
  31.1 6.4 %collective-permute-start.5 = (f32[392,128]{1,0:T(8,128)S(1)}, f32[392,128]{1,0:T(8,128)S(1)}, u32[]{:S(2)}, u32[]{:S(2)}) collective-permute-start(f32[392,128]{1,0:T(8,128)S(1)} %pad_maximum_fusion.12), channel_id=1, source_target_pairs={{0,4},{1,9},{2,6},{3,11},{4,0},{5,13},{6,2},{7,15},{8,12},{9,1},{1... | collective-permute-start | bytes 602120 | tf_op jit(solution)/shard_map/ppermute | solution.py:498
  33.8 9.3 %collective-permute-start.4 = (f32[384,128]{1,0:T(8,128)S(1)}, f32[384,128]{1,0:T(8,128)S(1)}, u32[]{:S(2)}, u32[]{:S(2)}) collective-permute-start(f32[384,128]{1,0:T(8,128)S(1)} %slice_add_fusion.25.mine_ref), channel_id=1, source_target_pairs={{0,8},{1,5},{2,10},{3,7},{4,12},{5,1},{6,14},{7,3},{8,0},{9,13},{1... | collective-permute-start | bytes 589832 | tf_op jit(solution)/shard_map/ppermute | solution.py:498
  37.6 9.4 %collective-permute-start.7 = (f32[392,128]{1,0:T(8,128)S(1)}, f32[392,128]{1,0:T(8,128)S(1)}, u32[]{:S(2)}, u32[]{:S(2)}) collective-permute-start(f32[392,128]{1,0:T(8,128)S(1)} %pad_maximum_fusion.13), channel_id=1, source_target_pairs={{0,16},{1,17},{2,18},{3,19},{4,20},{5,21},{6,22},{7,23},{8,24},{9,... | collective-permute-start | bytes 602120 | tf_op jit(solution)/shard_map/ppermute | solution.py:498
  43.2 7.8 %collective-permute-start.6 = (f32[768,128]{1,0:T(8,128)S(1)}, f32[768,128]{1,0:T(8,128)S(1)}, u32[]{:S(2)}, u32[]{:S(2)}) collective-permute-start(f32[768,128]{1,0:T(8,128)S(1)} %pad_maximum_fusion), channel_id=1, source_target_pairs={{0,4},{1,9},{2,6},{3,11},{4,0},{5,13},{6,2},{7,15},{8,12},{9,1},{1... | collective-permute-start | bytes 1179656 | tf_op jit(solution)/shard_map/ppermute | solution.py:498
  47.0 6.1 %collective-permute-start.8 = (f32[384,128]{1,0:T(8,128)S(1)}, f32[384,128]{1,0:T(8,128)S(1)}, u32[]{:S(2)}, u32[]{:S(2)}) collective-permute-start(f32[384,128]{1,0:T(8,128)S(1)} %slice_add_fusion.24.mine_ref), channel_id=1, source_target_pairs={{0,4},{1,9},{2,6},{3,11},{4,0},{5,13},{6,2},{7,15},{8,12},{9,1},{1... | collective-permute-start | bytes 589832 | tf_op jit(solution)/shard_map/ppermute | solution.py:498
  52.1 2.5 %collective-permute-start.9 = (f32[520,128]{1,0:T(8,128)S(1)}, f32[520,128]{1,0:T(8,128)S(1)}, u32[]{:S(2)}, u32[]{:S(2)}) collective-permute-start(f32[520,128]{1,0:T(8,128)S(1)} %get-tuple-element.118), channel_id=1, source_target_pairs={{0,1},{1,0},{2,3},{3,2},{4,5},{5,4},{6,7},{7,6},{8,9},{9,8},{10,11... | collective-permute-start | bytes 798728 | tf_op jit(solution)/shard_map/ppermute | solution.py:501
  53.1 7.8 %collective-permute-start.11 = (f32[768,128]{1,0:T(8,128)S(1)}, f32[768,128]{1,0:T(8,128)S(1)}, u32[]{:S(2)}, u32[]{:S(2)}) collective-permute-start(f32[768,128]{1,0:T(8,128)S(1)} %pad_maximum_fusion.1), channel_id=1, source_target_pairs={{0,8},{1,5},{2,10},{3,7},{4,12},{5,1},{6,14},{7,3},{8,0},{9,13},{1... | collective-permute-start | bytes 1179656 | tf_op jit(solution)/shard_map/ppermute | solution.py:498
  54.7 9.0 %collective-permute-start.10 = (f32[520,128]{1,0:T(8,128)S(1)}, f32[520,128]{1,0:T(8,128)S(1)}, u32[]{:S(2)}, u32[]{:S(2)}) collective-permute-start(f32[520,128]{1,0:T(8,128)S(1)} %pad_maximum_fusion.6), channel_id=1, source_target_pairs={{0,2},{1,3},{2,0},{3,1},{4,6},{5,7},{6,4},{7,5},{8,10},{9,11},{10,... | collective-permute-start | bytes 798728 | tf_op jit(solution)/shard_map/ppermute | solution.py:501
  62.1 2.8 %collective-permute-start.13 = (f32[520,128]{1,0:T(8,128)S(1)}, f32[520,128]{1,0:T(8,128)S(1)}, u32[]{:S(2)}, u32[]{:S(2)}) collective-permute-start(f32[520,128]{1,0:T(8,128)S(1)} %get-tuple-element.126), channel_id=1, source_target_pairs={{0,1},{1,0},{2,3},{3,2},{4,5},{5,4},{6,7},{7,6},{8,9},{9,8},{10,11... | collective-permute-start | bytes 798728 | tf_op jit(solution)/shard_map/ppermute | solution.py:501
  63.8 2.6 %collective-permute-start.12 = (f32[512,128]{1,0:T(8,128)S(1)}, f32[512,128]{1,0:T(8,128)S(1)}, u32[]{:S(2)}, u32[]{:S(2)}) collective-permute-start(f32[512,128]{1,0:T(8,128)S(1)} %slice_add_fusion.12.refs_2_), channel_id=1, source_target_pairs={{0,1},{1,0},{2,3},{3,2},{4,5},{5,4},{6,7},{7,6},{8,9},{9,8},{10,11... | collective-permute-start | bytes 786440 | tf_op jit(solution)/shard_map/ppermute | solution.py:501
  65.0 8.9 %collective-permute-start.15 = (f32[520,128]{1,0:T(8,128)S(1)}, f32[520,128]{1,0:T(8,128)S(1)}, u32[]{:S(2)}, u32[]{:S(2)}) collective-permute-start(f32[520,128]{1,0:T(8,128)S(1)} %pad_maximum_fusion.7), channel_id=1, source_target_pairs={{0,2},{1,3},{2,0},{3,1},{4,6},{5,7},{6,4},{7,5},{8,10},{9,11},{10,... | collective-permute-start | bytes 798728 | tf_op jit(solution)/shard_map/ppermute | solution.py:501
  67.8 7.9 %collective-permute-start.14 = (f32[776,128]{1,0:T(8,128)S(1)}, f32[776,128]{1,0:T(8,128)S(1)}, u32[]{:S(2)}, u32[]{:S(2)}) collective-permute-start(f32[776,128]{1,0:T(8,128)S(1)} %get-tuple-element.133), channel_id=1, source_target_pairs={{0,4},{1,9},{2,6},{3,11},{4,0},{5,13},{6,2},{7,15},{8,12},{9,1},{1... | collective-permute-start | bytes 1191944 | tf_op jit(solution)/shard_map/ppermute | solution.py:498
  73.8 2.8 %collective-permute-start.17 = (f32[512,128]{1,0:T(8,128)S(1)}, f32[512,128]{1,0:T(8,128)S(1)}, u32[]{:S(2)}, u32[]{:S(2)}) collective-permute-start(f32[512,128]{1,0:T(8,128)S(1)} %slice_add_fusion.10.refs_2_), channel_id=1, source_target_pairs={{0,1},{1,0},{2,3},{3,2},{4,5},{5,4},{6,7},{7,6},{8,9},{9,8},{10,11... | collective-permute-start | bytes 786440 | tf_op jit(solution)/shard_map/ppermute | solution.py:501
  75.8 5.8 %collective-permute-start.16 = (f32[392,128]{1,0:T(8,128)S(1)}, f32[392,128]{1,0:T(8,128)S(1)}, u32[]{:S(2)}, u32[]{:S(2)}) collective-permute-start(f32[392,128]{1,0:T(8,128)S(1)} %pad_maximum_fusion.14), channel_id=1, source_target_pairs={{0,8},{1,5},{2,10},{3,7},{4,12},{5,1},{6,14},{7,3},{8,0},{9,13},{1... | collective-permute-start | bytes 602120 | tf_op jit(solution)/shard_map/ppermute | solution.py:498
  78.0 11.3 %collective-permute-start.19 = (f32[776,128]{1,0:T(8,128)S(1)}, f32[776,128]{1,0:T(8,128)S(1)}, u32[]{:S(2)}, u32[]{:S(2)}) collective-permute-start(f32[776,128]{1,0:T(8,128)S(1)} %get-tuple-element.137), channel_id=1, source_target_pairs={{0,8},{1,5},{2,10},{3,7},{4,12},{5,1},{6,14},{7,3},{8,0},{9,13},{1... | collective-permute-start | bytes 1191944 | tf_op jit(solution)/shard_map/ppermute | solution.py:498
  81.7 10.6 %collective-permute-start.18 = (f32[392,128]{1,0:T(8,128)S(1)}, f32[392,128]{1,0:T(8,128)S(1)}, u32[]{:S(2)}, u32[]{:S(2)}) collective-permute-start(f32[392,128]{1,0:T(8,128)S(1)} %pad_maximum_fusion.15), channel_id=1, source_target_pairs={{0,16},{1,17},{2,18},{3,19},{4,20},{5,21},{6,22},{7,23},{8,24},{9,... | collective-permute-start | bytes 602120 | tf_op jit(solution)/shard_map/ppermute | solution.py:498
  89.4 7.0 %collective-permute-start.21 = (f32[392,128]{1,0:T(8,128)S(1)}, f32[392,128]{1,0:T(8,128)S(1)}, u32[]{:S(2)}, u32[]{:S(2)}) collective-permute-start(f32[392,128]{1,0:T(8,128)S(1)} %pad_maximum_fusion.16), channel_id=1, source_target_pairs={{0,4},{1,9},{2,6},{3,11},{4,0},{5,13},{6,2},{7,15},{8,12},{9,1},{1... | collective-permute-start | bytes 602120 | tf_op jit(solution)/shard_map/ppermute | solution.py:498
  92.2 8.1 %collective-permute-start.20 = (f32[384,128]{1,0:T(8,128)S(1)}, f32[384,128]{1,0:T(8,128)S(1)}, u32[]{:S(2)}, u32[]{:S(2)}) collective-permute-start(f32[384,128]{1,0:T(8,128)S(1)} %slice_add_fusion.23.mine_ref), channel_id=1, source_target_pairs={{0,8},{1,5},{2,10},{3,7},{4,12},{5,1},{6,14},{7,3},{8,0},{9,13},{1... | collective-permute-start | bytes 589832 | tf_op jit(solution)/shard_map/ppermute | solution.py:498
  96.5 7.9 %collective-permute-start.23 = (f32[392,128]{1,0:T(8,128)S(1)}, f32[392,128]{1,0:T(8,128)S(1)}, u32[]{:S(2)}, u32[]{:S(2)}) collective-permute-start(f32[392,128]{1,0:T(8,128)S(1)} %pad_maximum_fusion.17), channel_id=1, source_target_pairs={{0,16},{1,17},{2,18},{3,19},{4,20},{5,21},{6,22},{7,23},{8,24},{9,... | collective-permute-start | bytes 602120 | tf_op jit(solution)/shard_map/ppermute | solution.py:498
  100.4 7.8 %collective-permute-start.22 = (f32[768,128]{1,0:T(8,128)S(1)}, f32[768,128]{1,0:T(8,128)S(1)}, u32[]{:S(2)}, u32[]{:S(2)}) collective-permute-start(f32[768,128]{1,0:T(8,128)S(1)} %pad_maximum_fusion.2), channel_id=1, source_target_pairs={{0,4},{1,9},{2,6},{3,11},{4,0},{5,13},{6,2},{7,15},{8,12},{9,1},{1... | collective-permute-start | bytes 1179656 | tf_op jit(solution)/shard_map/ppermute | solution.py:498
  104.4 5.9 %collective-permute-start.25 = (f32[384,128]{1,0:T(8,128)S(1)}, f32[384,128]{1,0:T(8,128)S(1)}, u32[]{:S(2)}, u32[]{:S(2)}) collective-permute-start(f32[384,128]{1,0:T(8,128)S(1)} %slice_add_fusion.22.mine_ref), channel_id=1, source_target_pairs={{0,4},{1,9},{2,6},{3,11},{4,0},{5,13},{6,2},{7,15},{8,12},{9,1},{1... | collective-permute-start | bytes 589832 | tf_op jit(solution)/shard_map/ppermute | solution.py:498
  109.4 4.3 %collective-permute-start.24 = (f32[520,128]{1,0:T(8,128)S(1)}, f32[520,128]{1,0:T(8,128)S(1)}, u32[]{:S(2)}, u32[]{:S(2)}) collective-permute-start(f32[520,128]{1,0:T(8,128)S(1)} %get-tuple-element.150), channel_id=1, source_target_pairs={{0,1},{1,0},{2,3},{3,2},{4,5},{5,4},{6,7},{7,6},{8,9},{9,8},{10,11... | collective-permute-start | bytes 798728 | tf_op jit(solution)/shard_map/ppermute | solution.py:501
  110.4 8.0 %collective-permute-start.27 = (f32[768,128]{1,0:T(8,128)S(1)}, f32[768,128]{1,0:T(8,128)S(1)}, u32[]{:S(2)}, u32[]{:S(2)}) collective-permute-start(f32[768,128]{1,0:T(8,128)S(1)} %pad_maximum_fusion.3), channel_id=1, source_target_pairs={{0,8},{1,5},{2,10},{3,7},{4,12},{5,1},{6,14},{7,3},{8,0},{9,13},{1... | collective-permute-start | bytes 1179656 | tf_op jit(solution)/shard_map/ppermute | solution.py:498
  113.7 7.1 %collective-permute-start.26 = (f32[520,128]{1,0:T(8,128)S(1)}, f32[520,128]{1,0:T(8,128)S(1)}, u32[]{:S(2)}, u32[]{:S(2)}) collective-permute-start(f32[520,128]{1,0:T(8,128)S(1)} %pad_maximum_fusion.8), channel_id=1, source_target_pairs={{0,2},{1,3},{2,0},{3,1},{4,6},{5,7},{6,4},{7,5},{8,10},{9,11},{10,... | collective-permute-start | bytes 798728 | tf_op jit(solution)/shard_map/ppermute | solution.py:501
  119.5 2.4 %collective-permute-start.29 = (f32[520,128]{1,0:T(8,128)S(1)}, f32[520,128]{1,0:T(8,128)S(1)}, u32[]{:S(2)}, u32[]{:S(2)}) collective-permute-start(f32[520,128]{1,0:T(8,128)S(1)} %get-tuple-element.161), channel_id=1, source_target_pairs={{0,1},{1,0},{2,3},{3,2},{4,5},{5,4},{6,7},{7,6},{8,9},{9,8},{10,11... | collective-permute-start | bytes 798728 | tf_op jit(solution)/shard_map/ppermute | solution.py:501
  120.8 1.6 collective-permute-start.28
  122.0 8.9 %collective-permute-start.31 = (f32[520,128]{1,0:T(8,128)S(1)}, f32[520,128]{1,0:T(8,128)S(1)}, u32[]{:S(2)}, u32[]{:S(2)}) collective-permute-start(f32[520,128]{1,0:T(8,128)S(1)} %pad_maximum_fusion.9), channel_id=1, source_target_pairs={{0,2},{1,3},{2,0},{3,1},{4,6},{5,7},{6,4},{7,5},{8,10},{9,11},{10,... | collective-permute-start | bytes 798728 | tf_op jit(solution)/shard_map/ppermute | solution.py:501
  124.0 7.8 %collective-permute-start.30 = (f32[776,128]{1,0:T(8,128)S(1)}, f32[776,128]{1,0:T(8,128)S(1)}, u32[]{:S(2)}, u32[]{:S(2)}) collective-permute-start(f32[776,128]{1,0:T(8,128)S(1)} %get-tuple-element.168), channel_id=1, source_target_pairs={{0,4},{1,9},{2,6},{3,11},{4,0},{5,13},{6,2},{7,15},{8,12},{9,1},{1... | collective-permute-start | bytes 1191944 | tf_op jit(solution)/shard_map/ppermute | solution.py:498
  130.9 2.7 %collective-permute-start.33 = (f32[512,128]{1,0:T(8,128)S(1)}, f32[512,128]{1,0:T(8,128)S(1)}, u32[]{:S(2)}, u32[]{:S(2)}) collective-permute-start(f32[512,128]{1,0:T(8,128)S(1)} %slice_add_fusion.6.refs_2_), channel_id=1, source_target_pairs={{0,1},{1,0},{2,3},{3,2},{4,5},{5,4},{6,7},{7,6},{8,9},{9,8},{10,11... | collective-permute-start | bytes 786440 | tf_op jit(solution)/shard_map/ppermute | solution.py:501
  131.9 5.8 %collective-permute-start.32 = (f32[392,128]{1,0:T(8,128)S(1)}, f32[392,128]{1,0:T(8,128)S(1)}, u32[]{:S(2)}, u32[]{:S(2)}) collective-permute-start(f32[392,128]{1,0:T(8,128)S(1)} %pad_maximum_fusion.18), channel_id=1, source_target_pairs={{0,8},{1,5},{2,10},{3,7},{4,12},{5,1},{6,14},{7,3},{8,0},{9,13},{1... | collective-permute-start | bytes 602120 | tf_op jit(solution)/shard_map/ppermute | solution.py:498
  135.1 13.2 %collective-permute-start.35 = (f32[776,128]{1,0:T(8,128)S(1)}, f32[776,128]{1,0:T(8,128)S(1)}, u32[]{:S(2)}, u32[]{:S(2)}) collective-permute-start(f32[776,128]{1,0:T(8,128)S(1)} %get-tuple-element.174), channel_id=1, source_target_pairs={{0,8},{1,5},{2,10},{3,7},{4,12},{5,1},{6,14},{7,3},{8,0},{9,13},{1... | collective-permute-start | bytes 1191944 | tf_op jit(solution)/shard_map/ppermute | solution.py:498
  137.7 12.0 %collective-permute-start.34 = (f32[392,128]{1,0:T(8,128)S(1)}, f32[392,128]{1,0:T(8,128)S(1)}, u32[]{:S(2)}, u32[]{:S(2)}) collective-permute-start(f32[392,128]{1,0:T(8,128)S(1)} %pad_maximum_fusion.19), channel_id=1, source_target_pairs={{0,16},{1,17},{2,18},{3,19},{4,20},{5,21},{6,22},{7,23},{8,24},{9,... | collective-permute-start | bytes 602120 | tf_op jit(solution)/shard_map/ppermute | solution.py:498
  148.4 5.8 %collective-permute-start.36 = (f32[392,128]{1,0:T(8,128)S(1)}, f32[392,128]{1,0:T(8,128)S(1)}, u32[]{:S(2)}, u32[]{:S(2)}) collective-permute-start(f32[392,128]{1,0:T(8,128)S(1)} %pad_maximum_fusion.20), channel_id=1, source_target_pairs={{0,4},{1,9},{2,6},{3,11},{4,0},{5,13},{6,2},{7,15},{8,12},{9,1},{1... | collective-permute-start | bytes 602120 | tf_op jit(solution)/shard_map/ppermute | solution.py:498
  149.7 7.3 %collective-permute-start.38 = (f32[384,128]{1,0:T(8,128)S(1)}, f32[384,128]{1,0:T(8,128)S(1)}, u32[]{:S(2)}, u32[]{:S(2)}) collective-permute-start(f32[384,128]{1,0:T(8,128)S(1)} %slice_add_fusion.21.mine_ref), channel_id=1, source_target_pairs={{0,8},{1,5},{2,10},{3,7},{4,12},{5,1},{6,14},{7,3},{8,0},{9,13},{1... | collective-permute-start | bytes 589832 | tf_op jit(solution)/shard_map/ppermute | solution.py:498
  154.3 8.9 %collective-permute-start.37 = (f32[392,128]{1,0:T(8,128)S(1)}, f32[392,128]{1,0:T(8,128)S(1)}, u32[]{:S(2)}, u32[]{:S(2)}) collective-permute-start(f32[392,128]{1,0:T(8,128)S(1)} %pad_maximum_fusion.21), channel_id=1, source_target_pairs={{0,16},{1,17},{2,18},{3,19},{4,20},{5,21},{6,22},{7,23},{8,24},{9,... | collective-permute-start | bytes 602120 | tf_op jit(solution)/shard_map/ppermute | solution.py:498
  163.2 7.9 %collective-permute-start.40 = (f32[384,128]{1,0:T(8,128)S(1)}, f32[384,128]{1,0:T(8,128)S(1)}, u32[]{:S(2)}, u32[]{:S(2)}) collective-permute-start(f32[384,128]{1,0:T(8,128)S(1)} %slice_add_fusion.20.refs_6_), channel_id=1, source_target_pairs={{0,4},{1,9},{2,6},{3,11},{4,0},{5,13},{6,2},{7,15},{8,12},{9,1},{1... | collective-permute-start | bytes 589832 | tf_op jit(solution)/shard_map/ppermute | solution.py:498
  164.5 10.8 %collective-permute-start.39 = (f32[768,128]{1,0:T(8,128)S(1)}, f32[768,128]{1,0:T(8,128)S(1)}, u32[]{:S(2)}, u32[]{:S(2)}) collective-permute-start(f32[768,128]{1,0:T(8,128)S(1)} %pad_maximum_fusion.4), channel_id=1, source_target_pairs={{0,4},{1,9},{2,6},{3,11},{4,0},{5,13},{6,2},{7,15},{8,12},{9,1},{1... | collective-permute-start | bytes 1179656 | tf_op jit(solution)/shard_map/ppermute | solution.py:498
  171.1 7.8 %collective-permute-start.41 = (f32[768,128]{1,0:T(8,128)S(1)}, f32[768,128]{1,0:T(8,128)S(1)}, u32[]{:S(2)}, u32[]{:S(2)}) collective-permute-start(f32[768,128]{1,0:T(8,128)S(1)} %pad_maximum_fusion.5), channel_id=1, source_target_pairs={{0,8},{1,5},{2,10},{3,7},{4,12},{5,1},{6,14},{7,3},{8,0},{9,13},{1... | collective-permute-start | bytes 1179656 | tf_op jit(solution)/shard_map/ppermute | solution.py:498
